TPU v7x, 32 devices: a whole 2x2x4 slice. The times are simulated.
32 devices in a mesh: slab: 8 (over z, core), obs: 4 (over y, x).
Axes of the slice: x: 2, y: 2, z: 4, core: 2. Of those that a mesh axis runs over, the one named last changes fastest.
Arguments:
- innovation: float32 [32, 75, 256], P('obs'), may hold values from -6 to 6
- obs_precision: float32 [32, 75, 256], P('obs'), may hold values from 0.5 to 4
- seeds: int32 [4], replicated, may hold values from 0 to 999999
- col_sd: float32 [32, 128], P(('slab', 'obs')), may hold values from 0.3 to 3
- vert_factor: float32 [75, 75], replicated, may hold values from -0.75 to 0.75
- h_values: bfloat16 [8, 4, 32, 128, 256], P('slab', 'obs'), may hold values from -0.125 to 0.125
- block_obs: int32 [8, 4, 32], P('slab', 'obs'), may hold values from 0 to 7, as said below
- block_col: int32 [8, 4, 32], P('slab', 'obs'), may hold values from 0 to 3
- entry_count: int32 [8, 4], P('slab', 'obs'), may hold values from 5 to 32, as said below
Outputs:
- analysis_increment: float32 [32, 4, 75, 128], P(('slab', 'obs'))
- residual: float32 [32, 4, 75, 128], P(('slab', 'obs'))
Inputs may be any that keep to these rules, and one draw needn't show every extreme that they name: For each slab s and obs index o, the first entry_count[s, o] slots name distinct pairs (block_obs, block_col); later slots are unused. `entry_count`: 32 is reached in every draw.
All inputs are finite; a program needn't handle non-finite values.
Results may differ from a plain program's by a relative error of at most 0.02.
Values may be sent and summed in bfloat16 or wider, within the bound.
No kernel may reach another device: no remote copies, remote signals or barrier semaphores. Data moves between devices by JAX's collectives and lax.ppermute only.
A program may use at most 64 MiB of HBM per device.

v0:
```python
import jax
import jax.numpy as jnp
from jax import lax
from jax.sharding import PartitionSpec as P

ITERS = 2


def perturbed(innovation, precision, seeds, first_block):
    blocks = innovation.shape[0]
    levels = innovation.shape[1]
    width = innovation.shape[2]
    block_index = (first_block + jnp.arange(blocks, dtype=jnp.int32))[:, None, None]
    level_index = jnp.arange(levels, dtype=jnp.int32)[None, :, None]
    profile_index = jnp.arange(width, dtype=jnp.int32)[None, None, :]
    flat_index = (block_index * levels + level_index) * width + profile_index
    hashed = (seeds[None, :, None, None] % 32749 + 7919 * (flat_index[:, None] % 32749)) % 32749
    hashed = (hashed * hashed + 12345) % 32749
    hashed = (hashed * hashed + 2719) % 32749
    noise = hashed.astype(jnp.float32) / 32749.0 - 0.5
    spread = lax.rsqrt(precision)[:, None]
    return innovation[:, None] + 3.4 * noise * spread


def vertical(matrix, field):
    return jnp.einsum("kl,cmlp->cmkp", matrix, field, precision=lax.Precision.HIGHEST)


def vertical_adj(matrix, field):
    return jnp.einsum("lk,cmlp->cmkp", matrix, field, precision=lax.Precision.HIGHEST)


def member_sum(left, right):
    return jnp.sum(left * right, axis=(0, 2, 3))


def squares(residual):
    return lax.psum(member_sum(residual, residual), ("slab", "obs"))


def per_device(
    innovation,
    obs_precision,
    seeds,
    col_sd,
    vert_factor,
    h_values,
    block_obs,
    block_col,
    entry_count,
):
    h_block = h_values.reshape(h_values.shape[2:])
    obs_ids = block_obs.reshape(-1)
    col_ids = block_col.reshape(-1)
    used = entry_count.reshape(())
    slots = h_block.shape[0]
    live = (jnp.arange(slots, dtype=jnp.int32) < used).astype(jnp.float32)
    blocks = innovation.shape[0]
    obs_pick = (obs_ids[:, None] == jnp.arange(blocks, dtype=jnp.int32)[None, :]).astype(
        jnp.float32
    ) * live[:, None]
    colblocks = col_sd.shape[0]
    sigma = col_sd[:, None, None, :]

    def adjoint(weighted):
        pieces = jnp.take(weighted, obs_ids, axis=0)
        contrib = jnp.einsum("nmlp,ncp->nmlc", pieces, h_block, preferred_element_type=jnp.float32)
        targets = jnp.arange(colblocks * lax.axis_size("obs"), dtype=jnp.int32)
        col_pick = (col_ids[None, :] == targets[:, None]).astype(jnp.float32) * live[None, :]
        summed = lax.psum_scatter(
            jnp.einsum("kn,nmlc->kmlc", col_pick, contrib, precision=lax.Precision.HIGHEST).astype(
                jnp.bfloat16
            ),
            "obs",
            scatter_dimension=0,
            tiled=True,
        ).astype(jnp.float32)
        return vertical_adj(vert_factor, sigma * summed)

    target = perturbed(innovation, obs_precision, seeds, lax.axis_index("obs") * blocks)
    weighted0 = (obs_precision[:, None] * target).astype(jnp.bfloat16)
    rhs = adjoint(weighted0)
    solution = jnp.zeros_like(rhs)
    residual = rhs
    direction = rhs
    norm_now = squares(residual)
    for sweep in range(ITERS):
        moved = (sigma * vertical(vert_factor, direction)).astype(jnp.bfloat16)
        slab_field = lax.all_gather(moved, "obs", axis=0, tiled=True)
        forward_pieces = jnp.take(slab_field, col_ids, axis=0)
        product = jnp.einsum(
            "nmlc,ncp->nmlp", forward_pieces, h_block, preferred_element_type=jnp.float32
        )
        partial_value = jnp.einsum(
            "nb,nmlp->bmlp", obs_pick, product, precision=lax.Precision.HIGHEST
        )
        total = lax.psum(partial_value.astype(jnp.bfloat16), "slab").astype(jnp.float32)
        scaled = obs_precision[:, None] * total
        first_slab = (lax.axis_index("slab") == 0).astype(jnp.float32)
        energy = jnp.sum(total * scaled, axis=(0, 2, 3)) * first_slab
        weighted, energy = (scaled.astype(jnp.bfloat16), energy)
        sums_pair = lax.psum((member_sum(direction, direction), energy), ("slab", "obs"))
        image = direction + adjoint(weighted)
        curvature = sums_pair[0] + sums_pair[1]
        alpha = (norm_now / curvature)[None, :, None, None]
        solution = solution + alpha * direction
        residual = residual - alpha * image
        norm_next = squares(residual)
        direction = residual + (norm_next / norm_now)[None, :, None, None] * direction
        norm_now = norm_next
    analysis_increment = sigma * vertical(vert_factor, solution)
    return (analysis_increment, residual)


def solution(mesh):
    return jax.shard_map(
        per_device,
        mesh=mesh,
        in_specs=(
            P("obs", None, None),
            P("obs", None, None),
            P(),
            P(("slab", "obs"), None),
            P(),
            P("slab", "obs", None, None, None),
            P("slab", "obs", None),
            P("slab", "obs", None),
            P("slab", "obs"),
        ),
        out_specs=(P(("slab", "obs"), None, None, None), P(("slab", "obs"), None, None, None)),
        check_vma=False,
    )
```

profile of v0, /device:TPU:0, one launch (start us, length us, event | category | flops | bytes accessed | tf_op | source)
XLA Modules:
  0.0 445.4 jit_solution(4450624589326286802)
XLA Ops:
  11.0 6.7 %fusion.34 = bf16[8,4,75,256]{3,0,2,1:T(8,128)(2,1)S(1)} fusion(f32[8,75,256]{2,0,1:T(8,128)S(1)} %rsqrt_multiply_fusion, s32[8,75,256]{2,0,1:T(8,128)S(1)} %fusion.72, s32[4]{0:T(128)S(1)} %and_select_fusion, f32[8,75,256]{2,0,1:T(8,128)} %param.13, f32[8,75,256]{2,0,1:T(8,128)} %param.14), kind=kLoop, calls=%fused_computation.49 | loop fusion | flops 18432000 | bytes 3686416 | tf_op jit(solution)/shard_map/convert_element_type | solution.py:81
  18.9 6.6 %gather_fusion = bf16[32,4,75,256]{3,1,2,0:T(4,128)(2,1)} fusion(bf16[8,4,75,256]{3,1,2,0:T(4,128)(2,1)S(1)} %copy.30, s32[1024]{0:T(1024)S(1)} %pad_clamp_fusion.1), kind=kCustom, calls=%fused_computation.clone | custom fusion | bytes 9830528 | tf_op jit(solution)/shard_map/jit(_take)/gather | solution.py:66
  25.5 4.6 %broadcast_select_fusion.2 = bf16[32,4,75,256]{3,1,2,0:T(4,128)(2,1)S(1)} fusion(bf16[32,4,75,256]{3,1,2,0:T(4,128)(2,1)} %gather_fusion, pred[32]{0:T(512)(128)(4,1)S(1)} %compare_and_fusion.1), kind=kLoop, calls=%fused_computation.23 | loop fusion | flops 2457600 | bytes 9830432 | tf_op jit(solution)/shard_map/jit(_take)/select_n | solution.py:66
  31.8 5.1 %fusion.49 = bf16[4,4,75,128]{3,0,2,1:T(4,128)(2,1)S(1)} fusion(f32[32,4,75,128]{3,2,1,0:T(8,128)S(1)} %fusion.8, f32[32]{0:T(128)S(1)} %compare_convert_fusion, s32[32]{0:T(128)S(1)} %bitcast.159), kind=kOutput, calls=%fused_computation.63 | convolution fusion | flops 59136256 | bytes 5222656 | tf_op jit(solution)/shard_map/kn,nmlc->kmlc/dot_general | solution.py:71
  38.4 45.5 %all-reduce.14.cloned.1.call-done = bf16[4,4,75,128]{3,1,2,0:T(4,128)(2,1)} async-done(((bf16[4,4,75,128]{3,1,2,0:T(4,128)(2,1)}), bf16[4,4,75,128]{3,1,2,0:T(4,128)(2,1)}) %all-reduce.14.cloned.1.call-update) | async-done | bytes 307216
  83.9 1.6 multiply_bitcast_fusion.2
  86.8 9.7 %all_gather.6 = bf16[4,4,75,128]{3,1,2,0:T(4,128)(2,1)S(1)} all-gather(bf16[1,4,75,128]{3,1,2,0:T(4,128)(2,1)S(1)} %copy.36), channel_id=1, replica_groups=mesh['slab'=8,'obs'=4] {'obs'}, dimensions={0}, use_global_device_ids=true | all-gather | bytes 384000 | tf_op jit(solution)/shard_map/all_gather | solution.py:89
  96.4 4.0 gather_fusion.1
  100.4 2.9 broadcast_select_fusion.4
  104.8 11.1 %fusion.43 = bf16[8,4,75,256]{3,0,2,1:T(8,128)(2,1)} fusion(f32[32,4,75,256]{3,2,1,0:T(8,128)S(1)} %fusion.18, f32[32]{0:T(128)S(1)} %compare_convert_fusion, s32[32]{0:T(128)S(1)} %bitcast.162), kind=kOutput, calls=%fused_computation.61 | convolution fusion | flops 236544512 | bytes 11059456 | tf_op jit(solution)/shard_map/nb,nmlp->bmlp/dot_general | solution.py:94
  116.0 59.7 %all-reduce.10.cloned.1.call-done = bf16[8,4,75,256]{3,0,2,1:T(8,128)(2,1)} async-done(((bf16[8,4,75,256]{3,0,2,1:T(8,128)(2,1)}), bf16[8,4,75,256]{3,0,2,1:T(8,128)(2,1)}) %all-reduce.10.cloned.1.call-update) | async-done | bytes 1228816 | tf_op jit(solution)/shard_map/psum | solution.py:97
  175.7 2.3 fusion.20
  178.5 6.7 %gather_fusion.2 = bf16[32,4,75,256]{3,1,2,0:T(4,128)(2,1)} fusion(bf16[8,4,75,256]{3,1,2,0:T(4,128)(2,1)S(1)} %copy.39, s32[1024]{0:T(1024)S(1)} %pad_clamp_fusion.1), kind=kCustom, calls=%fused_computation.2.clone | custom fusion | bytes 9830528 | tf_op jit(solution)/shard_map/jit(_take)/gather | solution.py:66
  185.2 4.6 %broadcast_select_fusion.1 = bf16[32,4,75,256]{3,1,2,0:T(4,128)(2,1)S(1)} fusion(bf16[32,4,75,256]{3,1,2,0:T(4,128)(2,1)} %gather_fusion.2, pred[32]{0:T(512)(128)(4,1)S(1)} %compare_and_fusion.1), kind=kLoop, calls=%fused_computation.22 | loop fusion | flops 2457600 | bytes 9830432 | tf_op jit(solution)/shard_map/jit(_take)/select_n | solution.py:66
  191.4 5.1 %fusion.52 = bf16[4,4,75,128]{3,0,2,1:T(4,128)(2,1)S(1)} fusion(f32[32,4,75,128]{3,2,1,0:T(8,128)S(1)} %fusion.6, f32[32]{0:T(128)S(1)} %compare_convert_fusion, s32[32]{0:T(128)S(1)} %bitcast.160), kind=kOutput, calls=%fused_computation.64 | convolution fusion | flops 59136256 | bytes 5222656 | tf_op jit(solution)/shard_map/kn,nmlc->kmlc/dot_general | solution.py:71
  197.4 39.5 %all-reduce.3 = (f32[4]{0:T(128)S(1)}, f32[4]{0:T(128)S(1)}) all-reduce(f32[4]{0:T(128)S(1)} %copy-done.18, f32[4]{0:T(128)S(1)} %broadcast_multiply_fusion), channel_id=1, replica_groups=mesh['slab'=8,'obs'=4] {'slab','obs'}, use_global_device_ids=true, to_apply=%region_2.4 | all-reduce | flops 8 | bytes 64 | tf_op jit(solution)/shard_map/psum | solution.py:38
  236.9 3.1 all-reduce.16.cloned.1.call-done
  240.1 1.6 multiply_bitcast_fusion.1
  242.1 39.5 %psum.55 = f32[4]{0:T(128)S(1)} all-reduce(f32[4]{0:T(128)S(1)} %get-tuple-element.18), channel_id=1, replica_groups=mesh['slab'=8,'obs'=4] {'slab','obs'}, use_global_device_ids=true, to_apply=%region_8.11 | all-reduce | flops 4 | bytes 32 | tf_op jit(solution)/shard_map/psum | solution.py:38
  282.6 10.8 %all_gather.7 = bf16[4,4,75,128]{3,1,2,0:T(4,128)(2,1)S(1)} all-gather(bf16[1,4,75,128]{3,1,2,0:T(4,128)(2,1)S(1)} %copy.45), channel_id=1, replica_groups=mesh['slab'=8,'obs'=4] {'obs'}, dimensions={0}, use_global_device_ids=true | all-gather | bytes 384000 | tf_op jit(solution)/shard_map/all_gather | solution.py:89
  293.4 4.0 gather_fusion.3
  297.3 2.9 broadcast_select_fusion.3
  301.8 11.3 %fusion.46 = bf16[8,4,75,256]{3,0,2,1:T(8,128)(2,1)} fusion(f32[32,4,75,256]{3,2,1,0:T(8,128)S(1)} %fusion.16, f32[32]{0:T(128)S(1)} %compare_convert_fusion, s32[32]{0:T(128)S(1)} %bitcast.163), kind=kOutput, calls=%fused_computation.62 | convolution fusion | flops 236544512 | bytes 11059456 | tf_op jit(solution)/shard_map/nb,nmlp->bmlp/dot_general | solution.py:94
  313.9 57.9 %all-reduce.12.cloned.1.call-done = bf16[8,4,75,256]{3,0,2,1:T(8,128)(2,1)} async-done(((bf16[8,4,75,256]{3,0,2,1:T(8,128)(2,1)}), bf16[8,4,75,256]{3,0,2,1:T(8,128)(2,1)}) %all-reduce.12.cloned.1.call-update) | async-done | bytes 1228816 | tf_op jit(solution)/shard_map/psum | solution.py:97
  371.8 2.4 multiply_convert_fusion
  374.7 6.5 %gather_fusion.4 = bf16[32,4,75,256]{3,1,2,0:T(4,128)(2,1)} fusion(bf16[8,4,75,256]{3,1,2,0:T(4,128)(2,1)S(1)} %copy.48, s32[1024]{0:T(1024)S(1)} %pad_clamp_fusion.1), kind=kCustom, calls=%fused_computation.3.clone | custom fusion | bytes 9830528 | tf_op jit(solution)/shard_map/jit(_take)/gather | solution.py:66
  381.2 4.6 %broadcast_select_fusion = bf16[32,4,75,256]{3,1,2,0:T(4,128)(2,1)S(1)} fusion(bf16[32,4,75,256]{3,1,2,0:T(4,128)(2,1)} %gather_fusion.4, pred[32]{0:T(512)(128)(4,1)S(1)} %copy-done.9), kind=kLoop, calls=%fused_computation.21 | loop fusion | flops 2457600 | bytes 9830432 | tf_op jit(solution)/shard_map/jit(_take)/select_n | solution.py:66
  385.8 1.5 fusion.4
  387.4 5.1 %fusion.55 = bf16[4,4,75,128]{3,0,2,1:T(4,128)(2,1)S(1)} fusion(f32[32,4,75,128]{3,2,1,0:T(8,128)S(1)} %fusion.4, f32[32]{0:T(128)S(1)} %compare_convert_fusion, s32[32]{0:T(128)S(1)} %bitcast.161), kind=kOutput, calls=%fused_computation.65 | convolution fusion | flops 59136256 | bytes 5222656 | tf_op jit(solution)/shard_map/kn,nmlc->kmlc/dot_general | solution.py:71
  393.4 39.5 %psum.59 = f32[4]{0:T(128)S(1)} all-reduce(f32[4]{0:T(128)S(1)} %multiply_add_fusion), channel_id=1, replica_groups=mesh['slab'=8,'obs'=4] {'slab','obs'}, use_global_device_ids=true, to_apply=%region_10.13 | all-reduce | flops 4 | bytes 32 | tf_op jit(solution)/shard_map/psum | solution.py:102
  434.1 2.0 all-reduce.18.cloned.1.call-done
  436.1 1.6 multiply_bitcast_fusion
  (95 shorter events, 20.5 us)
Async XLA Ops:
  7.2 23.0 %copy-start = (bf16[1,1,32,128,256]{4,3,2,1,0:T(8,128)(2,1)S(1)}, bf16[1,1,32,128,256]{4,3,2,1,0:T(8,128)(2,1)}, u32[]{:S(2)}) copy-start(bf16[1,1,32,128,256]{4,3,2,1,0:T(8,128)(2,1)} %param.18) | copy-start | bytes 6291460
  7.2 76.7 %all-reduce.14.cloned.1.call-start = ((), (), s32[]{:S(2)}) async-start(), calls=%async_computation.2 | async-start | bytes 614400
  8.7 176.5 %copy-start.8 = (pred[32]{0:T(512)(128)(4,1)}, pred[32]{0:T(512)(128)(4,1)S(1)}, u32[]{:S(2)}) copy-start(pred[32]{0:T(512)(128)(4,1)S(1)} %compare_and_fusion.1) | copy-start | bytes 100
  30.2 1.5 copy-start.7
  31.7 6.1 %copy-start.22 = (u32[32]{0:T(128)S(1)}, u32[32]{0:T(128)}, u32[]{:S(2)}) copy-start(u32[32]{0:T(128)} %constant.91) | copy-start | bytes 388
  31.7 52.1 %copy-start.6 = (f32[1,128]{1,0:T(1,128)S(1)}, f32[1,128]{1,0:T(1,128)}, u32[]{:S(2)}) copy-start(f32[1,128]{1,0:T(1,128)} %param.16) | copy-start | bytes 1540
  31.7 53.7 %copy-start.5 = (f32[75,75]{1,0:T(8,128)S(1)}, f32[75,75]{1,0:T(8,128)}, u32[]{:S(2)}) copy-start(f32[75,75]{1,0:T(8,128)} %param.17) | copy-start | bytes 67504
  37.7 138.0 %all-reduce.10.cloned.1.call-start = ((), (), s32[]{:S(2)}) async-start(), calls=%async_computation | async-start | bytes 2457600 | tf_op jit(solution)/shard_map/psum | solution.py:97
  38.4 62.0 %copy-start.12 = (pred[32]{0:T(512)(128)(4,1)}, pred[32]{0:T(512)(128)(4,1)S(1)}, u32[]{:S(2)}) copy-start(pred[32]{0:T(512)(128)(4,1)S(1)} %compare_and_fusion) | copy-start | bytes 100
  103.3 1.5 copy-start.10
  104.8 70.9 %copy-start.1 = (f32[8,75,256]{2,0,1:T(8,128)S(1)}, f32[8,75,256]{2,0,1:T(8,128)}, u32[]{:S(2)}) copy-start(f32[8,75,256]{2,0,1:T(8,128)} %param.14) | copy-start | bytes 1843204
  116.0 124.1 %all-reduce.16.cloned.1.call-start = ((), (), s32[]{:S(2)}) async-start(), calls=%async_computation.3 | async-start | bytes 614400
  191.4 6.0 %copy-start.19 = (f32[4]{0:T(128)S(1)}, f32[4]{0:T(128)}, u32[]{:S(2)}) copy-start(f32[4]{0:T(128)} %get-tuple-element.14) | copy-start | bytes 52
  191.4 6.0 %copy-start.18 = (f32[4]{0:T(128)S(1)}, f32[4]{0:T(128)}, u32[]{:S(2)}) copy-start(f32[4]{0:T(128)} %get-tuple-element.16) | copy-start | bytes 52
  197.3 174.5 %all-reduce.12.cloned.1.call-start = ((), (), s32[]{:S(2)}) async-start(), calls=%async_computation.1 | async-start | bytes 2457600 | tf_op jit(solution)/shard_map/psum | solution.py:97
  236.9 5.2 %copy-start.16 = (f32[4]{0:T(128)}, f32[4]{0:T(128)S(1)}, u32[]{:S(2)}) copy-start(f32[4]{0:T(128)S(1)} %add_divide_fusion) | copy-start | bytes 52
  242.1 71.0 %copy-start.3 = (f32[1,4,75,128]{3,2,1,0:T(8,128)}, f32[1,4,75,128]{3,2,1,0:T(8,128)S(1)}, u32[]{:S(2)}) copy-start(f32[1,4,75,128]{3,2,1,0:T(8,128)S(1)} %get-tuple-element.19) | copy-start | bytes 460804
  281.6 0.5 copy-start.20
  293.4 4.0 copy-start.13
  300.2 1.5 copy-start.11
  301.8 70.1 %copy-start.2 = (f32[8,75,256]{2,0,1:T(8,128)S(1)}, f32[8,75,256]{2,0,1:T(8,128)}, u32[]{:S(2)}) copy-start(f32[8,75,256]{2,0,1:T(8,128)} %param.14) | copy-start | bytes 1843204
  313.1 123.0 %all-reduce.18.cloned.1.call-start = ((), (), s32[]{:S(2)}) async-start(), calls=%async_computation.4 | async-start | bytes 614400
  374.7 6.5 %copy-start.9 = (pred[32]{0:T(512)(128)(4,1)S(1)}, pred[32]{0:T(512)(128)(4,1)}, u32[]{:S(2)}) copy-start(pred[32]{0:T(512)(128)(4,1)} %copy-done.8) | copy-start | bytes 100
  387.4 6.0 %copy-start.14 = (f32[4]{0:T(128)S(1)}, f32[4]{0:T(128)}, u32[]{:S(2)}) copy-start(f32[4]{0:T(128)} %multiply_reduce_fusion) | copy-start | bytes 52
  387.4 6.0 %copy-start.15 = (f32[4]{0:T(128)S(1)}, f32[4]{0:T(128)}, u32[]{:S(2)}) copy-start(f32[4]{0:T(128)} %get-tuple-element.13) | copy-start | bytes 52
  387.4 45.5 %copy-start.21 = (f32[4]{0:T(128)S(1)}, f32[4]{0:T(128)}, u32[]{:S(2)}) copy-start(f32[4]{0:T(128)} %copy-done.20) | copy-start | bytes 52
  387.4 45.5 %copy-start.4 = (f32[1,4,75,128]{3,2,1,0:T(8,128)S(1)}, f32[1,4,75,128]{3,2,1,0:T(8,128)}, u32[]{:S(2)}) copy-start(f32[1,4,75,128]{3,2,1,0:T(8,128)} %copy-done.3) | copy-start | bytes 460804
  387.4 45.5 %copy-start.17 = (f32[4]{0:T(128)S(1)}, f32[4]{0:T(128)}, u32[]{:S(2)}) copy-start(f32[4]{0:T(128)} %copy-done.16) | copy-start | bytes 52
Sparse Core Ops, SparseCore 0:
  37.8 45.9 all-reduce.13
  116.1 59.5 all-reduce.9
  197.5 42.5 all-reduce.15
  313.2 58.5 all-reduce.11
  393.5 42.5 all-reduce.17
where the time goes:
time: 450 us; the launch traced here: 445 us
  waiting for transfers between devices  168 us (37%)
  blocking collectives  139 us (31%)
  matrix products  48.1 us (11%)
  other arithmetic  40.3 us (9%)
  local copies, waits for them, and re-layouts  34.4 us (8%)
  between operations  15.1 us (3%)
    psum x2, waiting for transfers between devices, per_device(): lax.psum(partial_value.astype(jnp.bfloat16), 'slab').astype(jnp.float32)  118 us
    psum x2, blocking collectives, squares(): return lax.psum(member_sum(residual, residual), ('slab', 'obs'))  79 us
    unnamed x8, waiting for transfers between devices  50.7 us
    psum x1, blocking collectives, per_device(): lax.psum((member_sum(direction, direction), energy), ('slab', 'obs'))  39.5 us
    dot_general x2, matrix products, per_device(): jnp.einsum('nb,nmlp->bmlp', obs_pick, product, precision=lax.Precision.HI...  22.4 us
    all_gather x2, blocking collectives, per_device(): slab_field = lax.all_gather(moved, 'obs', axis=0, tiled=True)  20.5 us
    gather x3, local copies, waits for them, and re-layouts, adjoint(): pieces = jnp.take(weighted, obs_ids, axis=0)  19.8 us
    dot_general x3, matrix products, adjoint(): jnp.einsum('kn,nmlc->kmlc', col_pick, contrib, precision=lax.Precision.HI...  15.2 us
  transfers between devices with their start and end apart: 5, of which 5 were waited for; matrix products, arithmetic and copies ran while one was open for 1% of the time, Pallas kernels for 0%

commit v1 on v0

v1 whole, which is shorter than its diff:
```python
import functools

import jax
import jax.numpy as jnp
from jax import lax
from jax.experimental import pallas as pl
from jax.experimental.pallas import tpu as pltpu
from jax.sharding import PartitionSpec as P

ITERS = 2
GROUPS = 1
LANES = 128
PIECES = 3
PRIME = 32749
VMEM = pl.BlockSpec(memory_space=pltpu.VMEM)
SMEM = pl.BlockSpec(memory_space=pltpu.SMEM)
F32 = jnp.float32
BF16 = jnp.bfloat16
NT = (((1,), (1,)), ((), ()))


def call(kernel, outs, scratch, flops, *args, scalars=0):
    nbytes = sum(a.size * a.dtype.itemsize for a in (*args, *outs))
    return pl.pallas_call(
        kernel,
        out_shape=outs,
        in_specs=[SMEM] * scalars + [VMEM] * (len(args) - scalars),
        out_specs=[VMEM] * len(outs),
        scratch_shapes=scratch,
        compiler_params=pltpu.CompilerParams(vmem_limit_bytes=40 * 1024 * 1024),
        cost_estimate=pl.CostEstimate(flops=flops, bytes_accessed=nbytes, transcendentals=0),
    )(*args)


def struct(shape, dtype):
    return jax.ShapeDtypeStruct(shape, dtype)


def place():
    slab = lax.axis_index("slab")
    return slab // 2, slab % 2, lax.axis_index("obs")


def total(x):
    return jnp.sum(jnp.sum(x, axis=0, keepdims=True), axis=1, keepdims=True)


def with_scalars(body, values):
    rows = lax.broadcasted_iota(jnp.int32, body.shape, 0)
    lanes = lax.broadcasted_iota(jnp.int32, body.shape, 1)
    line = jnp.zeros(body.shape, F32)
    for q, value in enumerate(values):
        rest = value
        for piece in range(PIECES):
            part = rest.astype(BF16).astype(F32)
            rest = rest - part
            line = jnp.where(lanes == q * PIECES + piece, part, line)
    return jnp.where(rows == body.shape[0] - 1, line, body)


def read_scalars(refs, member, count):
    rows = refs[0].shape[1]
    tail = refs[0][member, rows - 16 : rows, 0:LANES].astype(F32)
    for ref in refs[1:]:
        tail = tail + ref[member, rows - 16 : rows, 0:LANES].astype(F32)
    sub = lax.broadcasted_iota(jnp.int32, tail.shape, 0)
    lanes = lax.broadcasted_iota(jnp.int32, tail.shape, 1)
    found = []
    for q in range(count):
        mine = (sub == 15) & (lanes >= q * PIECES) & (lanes < (q + 1) * PIECES)
        found.append(total(jnp.where(mine, tail, 0.0)))
    return found


def remainder(x, factor):
    return x - (x.astype(F32) * factor).astype(jnp.int32) * PRIME


def start_kernel(
    dims, seeds, ids, cols, count, innov, prec, h, own, partner, *rest
):
    chips, n_obs, lev, halves, groups = dims
    outs, (scratch, acc) = rest[:-2], rest[-2:]
    z, core, obs = place()
    blocks, width, profiles = innov.shape[0], own.shape[3], innov.shape[2]
    colblocks = own.shape[1]
    members = seeds.shape[0]
    levp = scratch.shape[1]

    own[...] = jnp.zeros_like(own)
    partner[...] = jnp.zeros_like(partner)

    def put(n, carry):
        b, k = ids[n], cols[n]
        for half in range(halves):
            piece = b * halves + half
            tile = h[n, :, half * width : (half + 1) * width]

            @pl.when(piece % 2 == core)
            def _():
                own[piece // 2, k] = tile

            @pl.when(piece % 2 != core)
            def _():
                partner[piece // 2, k] = tile

        return carry

    lax.fori_loop(0, count[0], put, 0)

    scratch[...] = jnp.zeros_like(scratch)
    shape = (lev, profiles)
    spot = lax.broadcasted_iota(jnp.int32, shape, 0) * profiles + lax.broadcasted_iota(
        jnp.int32, shape, 1
    )
    first = True
    for source in range(2):
        for zz in range(chips):
            piece = 2 * zz + (core if source == 0 else 1 - core)
            b = piece // halves
            flat = spot + (obs * blocks + b) * (lev * profiles)
            base = remainder(7919 * remainder(flat, 1.0 / PRIME), 1.0 / PRIME)
            p = prec[b]
            gain = 3.4 * p * lax.rsqrt(p)
            offset = p * innov[b] - 0.5 * gain
            gain = gain * (1.0 / PRIME)
            for m in range(members):
                k0 = base + lax.rem(seeds[m], PRIME)
                k0 = jnp.where(k0 >= PRIME, k0 - PRIME, k0)
                k1 = remainder(k0 * k0 + 12345, 1.0 / PRIME)
                k2 = remainder(k1 * k1 + 2719, 1.0 / PRIME)
                k2 = jnp.where(k2 < 0, k2 + PRIME, k2)
                k2 = jnp.where(k2 >= PRIME, k2 - PRIME, k2)
                scratch[m, 0:lev, :] = offset + gain * k2.astype(F32)
            if halves == 1:
                w = scratch[...]
            else:
                w = scratch[:, :, pl.ds(pl.multiple_of((piece % halves) * width, LANES), width)]
            w = w.astype(BF16).reshape(members * levp, width)
            tiles = (own if source == 0 else partner)[zz].reshape(colblocks * LANES, width)
            part = lax.dot_general(w, tiles, NT, preferred_element_type=F32)
            for k in range(colblocks):
                piece_k = part[:, k * LANES : (k + 1) * LANES]
                acc[k] = piece_k if first else acc[k] + piece_k
            first = False

    share = members // groups
    for i in range(n_obs):
        value = acc[obs ^ i].astype(BF16).reshape(members, levp, LANES)
        for g in range(groups):
            outs[g * n_obs + i][...] = value[g * share : (g + 1) * share]


def precision_kernel(halves, prec, out):
    z, core, unused = place()
    piece = 2 * z + core
    lev = prec.shape[1]
    width = out.shape[1]
    out[...] = jnp.zeros_like(out)
    if halves == 1:
        out[0:lev, :] = prec[piece]
    else:
        out[0:lev, :] = prec[
            piece // halves, :, pl.ds(pl.multiple_of((piece % halves) * width, LANES), width)
        ]


def dot(a, b):
    return jnp.dot(a, b, preferred_element_type=F32, precision=lax.Precision.HIGHEST)


def first_kernel(parts, *refs):
    pieces, (sd, vert, vert_t), (residual, moved) = refs[:parts], refs[parts : parts + 3], refs[-2:]
    for m in range(residual.shape[0]):
        t = pieces[0][m].astype(F32)
        for ref in pieces[1:]:
            t = t + ref[m].astype(F32)
        r = dot(vert_t[...], sd[...] * t)
        residual[m] = r
        x = sd[...] * dot(vert[...], r)
        moved[m] = with_scalars(x, [total(r * r)]).astype(BF16)


def forward_kernel(dims, *refs):
    chips, n_obs = dims
    xs = refs[: 2 * n_obs]
    own, partner = refs[2 * n_obs : 2 * n_obs + 2]
    outs, panel = refs[-1 - chips : -1], refs[-1]
    z, core, obs = place()
    members, levp, unused = xs[0].shape
    colblocks, width = own.shape[1], own.shape[3]
    rows = members * levp
    for source in range(2):
        for i in range(n_obs):
            at = pl.multiple_of((source * colblocks + (obs ^ i)) * LANES, LANES)
            panel[:, pl.ds(at, LANES)] = xs[source * n_obs + i][...].reshape(rows, LANES)
    scalars = [read_scalars(xs, m, 2) for m in range(members)]
    half = colblocks * LANES
    for i in range(chips):
        zz = z ^ i
        y = jnp.dot(panel[:, 0:half], own[zz].reshape(half, width), preferred_element_type=F32)
        y = y + jnp.dot(
            panel[:, half : 2 * half], partner[zz].reshape(half, width), preferred_element_type=F32
        )
        y = y.reshape(members, levp, width)
        for m in range(members):
            outs[i][m] = with_scalars(y[m], scalars[m]).astype(outs[i].dtype)


def weigh_kernel(chips, later, *refs):
    ys, prec = refs[:chips], refs[chips]
    image, weighted, state = refs[-3:]
    p = prec[...]
    for m in range(image.shape[0]):
        y = ys[0][m]
        for ref in ys[1:]:
            y = y + ref[m].astype(F32)
        norm, cross = read_scalars(ys, m, 2)
        if later:
            old_image, old = refs[chips + 1 : chips + 3]
            old_norm, old_square = old[m, 0:1, 0:1], old[m, 1:2, 0:1]
            beta = norm / old_norm
            square = norm + 2.0 * beta * cross + beta * beta * old_square
            y = y + beta * old_image[m]
        else:
            beta = jnp.zeros_like(norm)
            square = norm
        scaled = p * y
        image[m] = y
        weighted[m] = with_scalars(scaled, [total(scaled * y)]).astype(BF16)
        sub = lax.broadcasted_iota(jnp.int32, (8, LANES), 0)
        state[m] = jnp.where(sub == 0, norm, jnp.where(sub == 1, square, beta))


def adjoint_kernel(dims, *refs):
    chips, n_obs = dims
    ws, own, partner = refs[:chips], refs[chips], refs[chips + 1]
    outs, acc = refs[-1 - 2 * n_obs : -1], refs[-1]
    z, core, obs = place()
    members, levp, width = ws[0].shape
    colblocks = own.shape[1]
    rows = members * levp
    energies = [read_scalars(ws, m, 1) for m in range(members)]
    for source in range(2):
        tiles = own if source == 0 else partner
        for i in range(chips):
            part = lax.dot_general(
                ws[i][...].reshape(rows, width),
                tiles[z ^ i].reshape(colblocks * LANES, width),
                NT,
                preferred_element_type=F32,
            )
            for k in range(colblocks):
                piece = part[:, k * LANES : (k + 1) * LANES]
                at = source * colblocks + k
                acc[at] = piece if i == 0 else acc[at] + piece
    for source in range(2):
        for i in range(n_obs):
            value = acc[source * colblocks + (obs ^ i)].reshape(members, levp, LANES)
            out = outs[source * n_obs + i]
            for m in range(members):
                out[m] = with_scalars(value[m], energies[m]).astype(BF16)


def update_kernel(parts, later, last, lev, *refs):
    pieces, (sd, vert, vert_t, state, residual) = refs[:parts], refs[parts : parts + 5]
    more = refs[parts + 5 :]
    old_direction = old_solution = None
    if later:
        old_direction, old_solution = more[:2]
        more = more[2:]
    for m in range(residual.shape[0]):
        t = pieces[0][m].astype(F32)
        for ref in pieces[1:]:
            t = t + ref[m].astype(F32)
        (energy,) = read_scalars(pieces, m, 1)
        norm, square, beta = state[m, 0:1, 0:1], state[m, 1:2, 0:1], state[m, 2:3, 0:1]
        alpha = norm / (square + energy)
        r = residual[m]
        d = r + beta * old_direction[m] if later else r
        q = d + dot(vert_t[...], sd[...] * t)
        solution = alpha * d
        if later:
            solution = old_solution[m] + solution
        r = r - alpha * q
        if last:
            increment_out, residual_out = more
            increment = sd[...] * dot(vert[...], solution)
            increment_out[0, m] = increment[0:lev]
            residual_out[0, m] = r[0:lev]
        else:
            residual_out, direction_out, solution_out, moved = more
            residual_out[m] = r
            direction_out[m] = d
            solution_out[m] = solution
            x = sd[...] * dot(vert[...], r)
            moved[m] = with_scalars(x, [total(r * r), total(r * d)]).astype(BF16)


def per_device(
    n_slab,
    n_obs,
    innovation,
    obs_precision,
    seeds,
    col_sd,
    vert_factor,
    h_values,
    block_obs,
    block_col,
    entry_count,
):
    blocks, lev, profiles = innovation.shape
    members = seeds.shape[0]
    groups, share = GROUPS, members // GROUPS
    chips = n_slab // 2
    halves = n_slab // blocks
    width = profiles // halves
    colblocks = n_obs
    assert halves * blocks == n_slab and width % LANES == 0 and col_sd.shape[0] == 1
    assert chips & (chips - 1) == 0 and n_obs & (n_obs - 1) == 0
    levp = (lev + 1 + 15) // 16 * 16
    rows = share * levp
    field = (share, levp, LANES)
    panel = (share, levp, width)
    pad = ((0, levp - lev), (0, levp - lev))
    vert = jnp.pad(vert_factor, pad)
    vert_t = jnp.pad(vert_factor.T, pad)
    h_block = h_values.reshape(h_values.shape[2:])
    product = 2 * n_slab * width * colblocks * LANES * rows
    small = 24 * rows * levp * LANES

    def across(x, i):
        return lax.ppermute(x, "slab", [(s, s ^ (2 * i)) for s in range(n_slab)])

    def beside(x, c, i):
        pairs = [
            (s * n_obs + o, (s ^ c) * n_obs + (o ^ i)) for s in range(n_slab) for o in range(n_obs)
        ]
        return lax.ppermute(x, ("slab", "obs"), pairs)

    def spread(outs):
        return [
            x if at == 0 else beside(x, at // n_obs, at % n_obs) for at, x in enumerate(outs)
        ]

    dense = struct((chips, colblocks, LANES, width), BF16)
    own, for_partner, *partials = call(
        functools.partial(start_kernel, (chips, n_obs, lev, halves, groups)),
        [dense, dense] + [struct(field, BF16)] * (groups * n_obs),
        [
            pltpu.VMEM((members, levp, profiles), F32),
            pltpu.VMEM((colblocks, members * levp, LANES), F32),
        ],
        product * groups,
        seeds,
        block_obs.reshape(-1),
        block_col.reshape(-1),
        entry_count.reshape(-1),
        innovation,
        obs_precision,
        h_block,
        scalars=4,
    )
    arrived = [spread(partials[g * n_obs : (g + 1) * n_obs]) for g in range(groups)]
    partner = beside(for_partner, 1, 0)
    (precision,) = call(
        functools.partial(precision_kernel, halves),
        [struct((levp, width), F32)],
        [],
        0,
        obs_precision,
    )
    state = [None] * groups
    direction = [None] * groups
    total_step = [None] * groups
    image = [None] * groups
    residual, moved, outputs = [], [], []
    for g in range(groups):
        r, x = call(
            functools.partial(first_kernel, n_obs),
            [struct(field, F32), struct(field, BF16)],
            [],
            small,
            *arrived[g],
            col_sd,
            vert,
            vert_t,
        )
        residual.append(r)
        moved.append(x)
    for sweep in range(ITERS):
        later, last = sweep > 0, sweep == ITERS - 1
        for g in range(groups):
            columns = spread([moved[g]] * (2 * n_obs))
            ys = call(
                functools.partial(forward_kernel, (chips, n_obs)),
                [struct(panel, F32)] + [struct(panel, BF16)] * (chips - 1),
                [pltpu.VMEM((rows, 2 * colblocks * LANES), BF16)],
                product,
                *columns,
                own,
                partner,
            )
            ys = [y if i == 0 else across(y, i) for i, y in enumerate(ys)]
            image[g], weighted, state[g] = call(
                functools.partial(weigh_kernel, chips, later),
                [struct(panel, F32), struct(panel, BF16), struct((share, 8, LANES), F32)],
                [],
                0,
                *ys,
                precision,
                *([image[g], state[g]] if later else []),
            )
            ws = [weighted if i == 0 else across(weighted, i) for i in range(chips)]
            ps = call(
                functools.partial(adjoint_kernel, (chips, n_obs)),
                [struct(field, BF16)] * (2 * n_obs),
                [pltpu.VMEM((2 * colblocks, rows, LANES), F32)],
                product,
                *ws,
                own,
                partner,
            )
            if last:
                outs = [struct((1, share, lev, LANES), F32)] * 2
            else:
                outs = [struct(field, F32)] * 3 + [struct(field, BF16)]
            results = call(
                functools.partial(update_kernel, 2 * n_obs, later, last, lev),
                outs,
                [],
                small,
                *spread(ps),
                col_sd,
                vert,
                vert_t,
                state[g],
                residual[g],
                *([direction[g], total_step[g]] if later else []),
            )
            if last:
                outputs.append(results)
            else:
                residual[g], direction[g], total_step[g], moved[g] = results
    if groups == 1:
        return tuple(outputs[0])
    return tuple(jnp.concatenate(parts, axis=1) for parts in zip(*outputs))


def solution(mesh):
    return jax.shard_map(
        functools.partial(per_device, mesh.shape["slab"], mesh.shape["obs"]),
        mesh=mesh,
        in_specs=(
            P("obs", None, None),
            P("obs", None, None),
            P(),
            P(("slab", "obs"), None),
            P(),
            P("slab", "obs", None, None, None),
            P("slab", "obs", None),
            P("slab", "obs", None),
            P("slab", "obs"),
        ),
        out_specs=(P(("slab", "obs"), None, None, None), P(("slab", "obs"), None, None, None)),
        check_vma=False,
    )
```

time: 450 us -> 138 us (0.31); the launches traced: 445 us -> 139 us
  blocking collectives: 139 us -> 0 us
  waiting for transfers between devices: 168 us -> 68.4 us
  starting transfers between devices: 0.21 us -> 53.2 us
  matrix products: 48.1 us -> 0 us
  other arithmetic: 40.3 us -> 0 us
  local copies, waits for them, and re-layouts: 34.4 us -> 4.15 us
  between operations: 15.1 us -> 1.62 us
  Pallas kernels: 0 us -> 11.5 us
    psum x3 -> x0, blocking collectives: 119 us -> none  [the longest x2 79 us: squares(): return lax.psum(member_sum(residual, residual), ('slab', 'obs'))]
    psum x2 -> x0, waiting for transfers between devices: 118 us -> none  [per_device(): lax.psum(partial_value.astype(jnp.bfloat16), 'slab').astype(jnp.float32)]
    ppermute x0 -> x44, waiting for transfers between devices: none -> 68.4 us  [the longest x12 45.7 us: across(): return lax.ppermute(x, 'slab', [(s, s ^ 2 * i) for s in range(n_slab)])]
    ppermute x0 -> x44, starting transfers between devices: none -> 53.2 us  [the longest x32 34.4 us: beside(): return lax.ppermute(x, ('slab', 'obs'), pairs)]
    unnamed x8 -> x0, waiting for transfers between devices: 50.7 us -> none
    dot_general x16 -> x0, matrix products: 48.1 us -> none  [the longest x2 22.4 us: per_device(): jnp.einsum('nb,nmlp->bmlp', obs_pick, product, precision=lax.Precision.HI...]
    gather x5 -> x0, local copies, waits for them, and re-layouts: 27.7 us -> none  [the longest x3 19.8 us: adjoint(): pieces = jnp.take(weighted, obs_ids, axis=0)]
    select_n x8 -> x0, other arithmetic: 21.1 us -> none  [the longest x4 14.7 us: adjoint(): pieces = jnp.take(weighted, obs_ids, axis=0)]
  transfers between devices with their start and end apart: 5 -> 44, of which waited for: 5 -> 27; matrix products, arithmetic and copies ran while one was open for 1% -> 0% of each run, Pallas kernels for 0% -> 0%
where the time goes in v1:
time: 138 us; the launch traced here: 139 us
  waiting for transfers between devices  68.4 us (50%)
  starting transfers between devices  53.2 us (39%)
  Pallas kernels  11.5 us (8%)
  local copies, waits for them, and re-layouts  4.15 us (3%)
  between operations  1.62 us (1%)
    ppermute x12, waiting for transfers between devices, across(): return lax.ppermute(x, 'slab', [(s, s ^ 2 * i) for s in range(n_slab)])  45.7 us
    ppermute x32, starting transfers between devices, beside(): return lax.ppermute(x, ('slab', 'obs'), pairs)  34.4 us
    ppermute x32, waiting for transfers between devices, beside(): return lax.ppermute(x, ('slab', 'obs'), pairs)  22.6 us
    ppermute x12, starting transfers between devices, across(): return lax.ppermute(x, 'slab', [(s, s ^ 2 * i) for s in range(n_slab)])  18.8 us
    pallas_call x11, Pallas kernels, call(): pl.pallas_call(kernel, out_shape=outs, in_specs=[SMEM] * scalars + [VMEM]...  11.5 us
  transfers between devices with their start and end apart: 44, of which 27 were waited for; matrix products, arithmetic and copies ran while one was open for 0% of the time, Pallas kernels for 0%

profile of v1, /device:TPU:0, one launch (start us, length us, event | category | flops | bytes accessed | tf_op | source)
XLA Modules:
  0.0 138.8 jit_solution(8049174074841113583)
XLA Ops:
  4.1 4.6 %shard_map.104 = (bf16[4,4,128,256]{3,2,1,0:T(8,128)(2,1)S(1)}, bf16[4,4,128,256]{3,2,1,0:T(8,128)(2,1)}, bf16[4,80,128]{2,1,0:T(8,128)(2,1)S(1)}, bf16[4,80,128...) custom-call(s32[4]{0:T(128)S(1)} %copy-done.2, s32[32]{0:T(128)S(1)} %bitcast.7, ...), custom_call_target="tpu_custom_call" | custom-call | flops 671088640 | bytes 5751060 | tf_op jit(solution)/shard_map/pallas_call | solution.py:24
  9.0 2.6 %collective-permute-start = (bf16[4,80,128]{2,1,0:T(8,128)(2,1)S(1)}, bf16[4,80,128]{2,1,0:T(8,128)(2,1)S(1)}, u32[]{:S(2)}, u32[]{:S(2)}) collective-permute-start(bf16[4,80,128]{2,1,0:T(8,128)(2,1)S(1)} %get-tuple-element.44), channel_id=1, source_target_pairs={{0,1},{1,0},{2,3},{3,2},{4,5},{5,4},{6,7},{7,6},{8,9},{9,8},{10,11... | collective-permute-start | bytes 245768 | tf_op jit(solution)/shard_map/ppermute | solution.py:340
  11.6 2.0 %collective-permute-start.1 = (bf16[4,80,128]{2,1,0:T(8,128)(2,1)S(1)}, bf16[4,80,128]{2,1,0:T(8,128)(2,1)S(1)}, u32[]{:S(2)}, u32[]{:S(2)}) collective-permute-start(bf16[4,80,128]{2,1,0:T(8,128)(2,1)S(1)} %get-tuple-element.45), channel_id=1, source_target_pairs={{0,2},{1,3},{2,0},{3,1},{4,6},{5,7},{6,4},{7,5},{8,10},{9,11},{10,... | collective-permute-start | bytes 245768 | tf_op jit(solution)/shard_map/ppermute | solution.py:340
  14.7 2.6 %collective-permute-done.1.refs_2_ = bf16[4,80,128]{2,1,0:T(8,128)(2,1)S(1)} collective-permute-done((bf16[4,80,128]{2,1,0:T(8,128)(2,1)S(1)}, bf16[4,80,128]{2,1,0:T(8,128)(2,1)S(1)}, u32[]{:S(2)}, u32[]{:S(2)}) %collective-permute-start.1) | collective-permute-done | bytes 81952 | tf_op jit(solution)/shard_map/ppermute | solution.py:340
  17.2 1.8 %collective-permute-done.2.refs_3_ = bf16[4,80,128]{2,1,0:T(8,128)(2,1)S(1)} collective-permute-done((bf16[4,80,128]{2,1,0:T(8,128)(2,1)S(1)}, bf16[4,80,128]{2,1,0:T(8,128)(2,1)S(1)}, u32[]{:S(2)}, u32[]{:S(2)}) %collective-permute-start.2) | collective-permute-done | bytes 81952 | tf_op jit(solution)/shard_map/ppermute | solution.py:340
  23.0 1.5 %collective-permute-done.9.refs_7_ = bf16[4,80,128]{2,1,0:T(8,128)(2,1)S(1)} collective-permute-done((bf16[4,80,128]{2,1,0:T(8,128)(2,1)S(1)}, bf16[4,80,128]{2,1,0:T(8,128)(2,1)S(1)}, u32[]{:S(2)}, u32[]{:S(2)}) %collective-permute-start.9) | collective-permute-done | bytes 81952 | tf_op jit(solution)/shard_map/ppermute | solution.py:340
  28.0 2.3 %collective-permute-done.5.refs_3_ = bf16[4,80,128]{2,1,0:T(8,128)(2,1)S(1)} collective-permute-done((bf16[4,80,128]{2,1,0:T(8,128)(2,1)S(1)}, bf16[4,80,128]{2,1,0:T(8,128)(2,1)S(1)}, u32[]{:S(2)}, u32[]{:S(2)}) %collective-permute-start.5) | collective-permute-done | bytes 81952 | tf_op jit(solution)/shard_map/ppermute | solution.py:340
  32.2 1.5 %collective-permute-start.11 = (bf16[4,80,256]{2,1,0:T(8,128)(2,1)S(1)}, bf16[4,80,256]{2,1,0:T(8,128)(2,1)S(1)}, u32[]{:S(2)}, u32[]{:S(2)}) collective-permute-start(bf16[4,80,256]{2,1,0:T(8,128)(2,1)S(1)} %get-tuple-element.51), channel_id=1, source_target_pairs={{0,8},{4,12},{8,0},{12,4},{16,24},{20,28},{24,16},{28,20},{1,9},{5... | collective-permute-start | bytes 491528 | tf_op jit(solution)/shard_map/ppermute | solution.py:334
  33.7 2.6 %collective-permute-start.12 = (bf16[4,80,256]{2,1,0:T(8,128)(2,1)S(1)}, bf16[4,80,256]{2,1,0:T(8,128)(2,1)S(1)}, u32[]{:S(2)}, u32[]{:S(2)}) collective-permute-start(bf16[4,80,256]{2,1,0:T(8,128)(2,1)S(1)} %get-tuple-element.52), channel_id=1, source_target_pairs={{0,16},{4,20},{8,24},{12,28},{16,0},{20,4},{24,8},{28,12},{1,17},{... | collective-permute-start | bytes 491528 | tf_op jit(solution)/shard_map/ppermute | solution.py:334
  37.2 3.0 %collective-permute-done.11.refs_1_ = bf16[4,80,256]{2,1,0:T(8,128)(2,1)S(1)} collective-permute-done((bf16[4,80,256]{2,1,0:T(8,128)(2,1)S(1)}, bf16[4,80,256]{2,1,0:T(8,128)(2,1)S(1)}, u32[]{:S(2)}, u32[]{:S(2)}) %collective-permute-start.11) | collective-permute-done | bytes 163872 | tf_op jit(solution)/shard_map/ppermute | solution.py:334
  40.2 8.3 %collective-permute-done.12.refs_2_ = bf16[4,80,256]{2,1,0:T(8,128)(2,1)S(1)} collective-permute-done((bf16[4,80,256]{2,1,0:T(8,128)(2,1)S(1)}, bf16[4,80,256]{2,1,0:T(8,128)(2,1)S(1)}, u32[]{:S(2)}, u32[]{:S(2)}) %collective-permute-start.12) | collective-permute-done | bytes 163872 | tf_op jit(solution)/shard_map/ppermute | solution.py:334
  48.7 3.0 %collective-permute-start.16 = (bf16[4,80,256]{2,1,0:T(8,128)(2,1)S(1)}, bf16[4,80,256]{2,1,0:T(8,128)(2,1)S(1)}, u32[]{:S(2)}, u32[]{:S(2)}) collective-permute-start(bf16[4,80,256]{2,1,0:T(8,128)(2,1)S(1)} %get-tuple-element.54.refs_0_), channel_id=1, source_target_pairs={{0,24},{4,28},{8,16},{12,20},{16,8},{20,12},{24,0},{28,4},{1,25},{... | collective-permute-start | bytes 491528 | tf_op jit(solution)/shard_map/ppermute | solution.py:334
  51.6 1.5 %collective-permute-start.15 = (bf16[4,80,256]{2,1,0:T(8,128)(2,1)S(1)}, bf16[4,80,256]{2,1,0:T(8,128)(2,1)S(1)}, u32[]{:S(2)}, u32[]{:S(2)}) collective-permute-start(bf16[4,80,256]{2,1,0:T(8,128)(2,1)S(1)} %get-tuple-element.54.refs_0_), channel_id=1, source_target_pairs={{0,16},{4,20},{8,24},{12,28},{16,0},{20,4},{24,8},{28,12},{1,17},{... | collective-permute-start | bytes 491528 | tf_op jit(solution)/shard_map/ppermute | solution.py:334
  53.6 3.0 %collective-permute-done.16.refs_3_ = bf16[4,80,256]{2,1,0:T(8,128)(2,1)S(1)} collective-permute-done((bf16[4,80,256]{2,1,0:T(8,128)(2,1)S(1)}, bf16[4,80,256]{2,1,0:T(8,128)(2,1)S(1)}, u32[]{:S(2)}, u32[]{:S(2)}) %collective-permute-start.16) | collective-permute-done | bytes 163872 | tf_op jit(solution)/shard_map/ppermute | solution.py:334
  56.6 8.6 %collective-permute-done.15.refs_2_ = bf16[4,80,256]{2,1,0:T(8,128)(2,1)S(1)} collective-permute-done((bf16[4,80,256]{2,1,0:T(8,128)(2,1)S(1)}, bf16[4,80,256]{2,1,0:T(8,128)(2,1)S(1)}, u32[]{:S(2)}, u32[]{:S(2)}) %collective-permute-start.15) | collective-permute-done | bytes 163872 | tf_op jit(solution)/shard_map/ppermute | solution.py:334
  66.2 2.0 %collective-permute-start.17 = (bf16[4,80,128]{2,1,0:T(8,128)(2,1)S(1)}, bf16[4,80,128]{2,1,0:T(8,128)(2,1)S(1)}, u32[]{:S(2)}, u32[]{:S(2)}) collective-permute-start(bf16[4,80,128]{2,1,0:T(8,128)(2,1)S(1)} %get-tuple-element.56), channel_id=1, source_target_pairs={{0,1},{1,0},{2,3},{3,2},{4,5},{5,4},{6,7},{7,6},{8,9},{9,8},{10,11... | collective-permute-start | bytes 245768 | tf_op jit(solution)/shard_map/ppermute | solution.py:340
  69.9 1.9 %collective-permute-start.21 = (bf16[4,80,128]{2,1,0:T(8,128)(2,1)S(1)}, bf16[4,80,128]{2,1,0:T(8,128)(2,1)S(1)}, u32[]{:S(2)}, u32[]{:S(2)}) collective-permute-start(bf16[4,80,128]{2,1,0:T(8,128)(2,1)S(1)} %get-tuple-element.60), channel_id=1, source_target_pairs={{0,5},{1,4},{2,7},{3,6},{4,1},{5,0},{6,3},{7,2},{8,13},{9,12},{10,... | collective-permute-start | bytes 245768 | tf_op jit(solution)/shard_map/ppermute | solution.py:340
  74.6 1.7 %collective-permute-done.22.refs_6_ = bf16[4,80,128]{2,1,0:T(8,128)(2,1)S(1)} collective-permute-done((bf16[4,80,128]{2,1,0:T(8,128)(2,1)S(1)}, bf16[4,80,128]{2,1,0:T(8,128)(2,1)S(1)}, u32[]{:S(2)}, u32[]{:S(2)}) %collective-permute-start.22) | collective-permute-done | bytes 81952 | tf_op jit(solution)/shard_map/ppermute | solution.py:340
  76.3 1.7 %collective-permute-done.23.refs_7_ = bf16[4,80,128]{2,1,0:T(8,128)(2,1)S(1)} collective-permute-done((bf16[4,80,128]{2,1,0:T(8,128)(2,1)S(1)}, bf16[4,80,128]{2,1,0:T(8,128)(2,1)S(1)}, u32[]{:S(2)}, u32[]{:S(2)}) %collective-permute-start.23) | collective-permute-done | bytes 81952 | tf_op jit(solution)/shard_map/ppermute | solution.py:340
  78.7 2.1 %collective-permute-start.30 = (bf16[4,80,128]{2,1,0:T(8,128)(2,1)S(1)}, bf16[4,80,128]{2,1,0:T(8,128)(2,1)S(1)}, u32[]{:S(2)}, u32[]{:S(2)}) collective-permute-start(bf16[4,80,128]{2,1,0:T(8,128)(2,1)S(1)} %get-tuple-element.65.refs_0_), channel_id=1, source_target_pairs={{0,7},{1,6},{2,5},{3,4},{4,3},{5,2},{6,1},{7,0},{8,15},{9,14},{10,... | collective-permute-start | bytes 245768 | tf_op jit(solution)/shard_map/ppermute | solution.py:340
  82.1 2.7 %collective-permute-start.26 = (bf16[4,80,128]{2,1,0:T(8,128)(2,1)S(1)}, bf16[4,80,128]{2,1,0:T(8,128)(2,1)S(1)}, u32[]{:S(2)}, u32[]{:S(2)}) collective-permute-start(bf16[4,80,128]{2,1,0:T(8,128)(2,1)S(1)} %get-tuple-element.65.refs_0_), channel_id=1, source_target_pairs={{0,3},{1,2},{2,1},{3,0},{4,7},{5,6},{6,5},{7,4},{8,11},{9,10},{10,... | collective-permute-start | bytes 245768 | tf_op jit(solution)/shard_map/ppermute | solution.py:340
  85.9 1.9 %collective-permute-start.24 = (bf16[4,80,128]{2,1,0:T(8,128)(2,1)S(1)}, bf16[4,80,128]{2,1,0:T(8,128)(2,1)S(1)}, u32[]{:S(2)}, u32[]{:S(2)}) collective-permute-start(bf16[4,80,128]{2,1,0:T(8,128)(2,1)S(1)} %get-tuple-element.65.refs_0_), channel_id=1, source_target_pairs={{0,1},{1,0},{2,3},{3,2},{4,5},{5,4},{6,7},{7,6},{8,9},{9,8},{10,11... | collective-permute-start | bytes 245768 | tf_op jit(solution)/shard_map/ppermute | solution.py:340
  91.8 3.4 %collective-permute-start.32 = (bf16[4,80,256]{2,1,0:T(8,128)(2,1)S(1)}, bf16[4,80,256]{2,1,0:T(8,128)(2,1)S(1)}, u32[]{:S(2)}, u32[]{:S(2)}) collective-permute-start(bf16[4,80,256]{2,1,0:T(8,128)(2,1)S(1)} %get-tuple-element.68), channel_id=1, source_target_pairs={{0,16},{4,20},{8,24},{12,28},{16,0},{20,4},{24,8},{28,12},{1,17},{... | collective-permute-start | bytes 491528 | tf_op jit(solution)/shard_map/ppermute | solution.py:334
  96.1 4.3 %collective-permute-done.31.refs_1_ = bf16[4,80,256]{2,1,0:T(8,128)(2,1)S(1)} collective-permute-done((bf16[4,80,256]{2,1,0:T(8,128)(2,1)S(1)}, bf16[4,80,256]{2,1,0:T(8,128)(2,1)S(1)}, u32[]{:S(2)}, u32[]{:S(2)}) %collective-permute-start.31) | collective-permute-done | bytes 163872 | tf_op jit(solution)/shard_map/ppermute | solution.py:334
  100.4 6.9 %collective-permute-done.32.refs_2_ = bf16[4,80,256]{2,1,0:T(8,128)(2,1)S(1)} collective-permute-done((bf16[4,80,256]{2,1,0:T(8,128)(2,1)S(1)}, bf16[4,80,256]{2,1,0:T(8,128)(2,1)S(1)}, u32[]{:S(2)}, u32[]{:S(2)}) %collective-permute-start.32) | collective-permute-done | bytes 163872 | tf_op jit(solution)/shard_map/ppermute | solution.py:334
  108.2 2.4 %collective-permute-start.36 = (bf16[4,80,256]{2,1,0:T(8,128)(2,1)S(1)}, bf16[4,80,256]{2,1,0:T(8,128)(2,1)S(1)}, u32[]{:S(2)}, u32[]{:S(2)}) collective-permute-start(bf16[4,80,256]{2,1,0:T(8,128)(2,1)S(1)} %get-tuple-element.71.refs_0_), channel_id=1, source_target_pairs={{0,24},{4,28},{8,16},{12,20},{16,8},{20,12},{24,0},{28,4},{1,25},{... | collective-permute-start | bytes 491528 | tf_op jit(solution)/shard_map/ppermute | solution.py:334
  110.6 1.9 %collective-permute-start.35 = (bf16[4,80,256]{2,1,0:T(8,128)(2,1)S(1)}, bf16[4,80,256]{2,1,0:T(8,128)(2,1)S(1)}, u32[]{:S(2)}, u32[]{:S(2)}) collective-permute-start(bf16[4,80,256]{2,1,0:T(8,128)(2,1)S(1)} %get-tuple-element.71.refs_0_), channel_id=1, source_target_pairs={{0,16},{4,20},{8,24},{12,28},{16,0},{20,4},{24,8},{28,12},{1,17},{... | collective-permute-start | bytes 491528 | tf_op jit(solution)/shard_map/ppermute | solution.py:334
  112.6 3.9 %collective-permute-done.36.refs_3_ = bf16[4,80,256]{2,1,0:T(8,128)(2,1)S(1)} collective-permute-done((bf16[4,80,256]{2,1,0:T(8,128)(2,1)S(1)}, bf16[4,80,256]{2,1,0:T(8,128)(2,1)S(1)}, u32[]{:S(2)}, u32[]{:S(2)}) %collective-permute-start.36) | collective-permute-done | bytes 163872 | tf_op jit(solution)/shard_map/ppermute | solution.py:334
  116.5 7.9 %collective-permute-done.35.refs_2_ = bf16[4,80,256]{2,1,0:T(8,128)(2,1)S(1)} collective-permute-done((bf16[4,80,256]{2,1,0:T(8,128)(2,1)S(1)}, bf16[4,80,256]{2,1,0:T(8,128)(2,1)S(1)}, u32[]{:S(2)}, u32[]{:S(2)}) %collective-permute-start.35) | collective-permute-done | bytes 163872 | tf_op jit(solution)/shard_map/ppermute | solution.py:334
  125.9 1.6 %collective-permute-start.38 = (bf16[4,80,128]{2,1,0:T(8,128)(2,1)S(1)}, bf16[4,80,128]{2,1,0:T(8,128)(2,1)S(1)}, u32[]{:S(2)}, u32[]{:S(2)}) collective-permute-start(bf16[4,80,128]{2,1,0:T(8,128)(2,1)S(1)} %get-tuple-element.74), channel_id=1, source_target_pairs={{0,2},{1,3},{2,0},{3,1},{4,6},{5,7},{6,4},{7,5},{8,10},{9,11},{10,... | collective-permute-start | bytes 245768 | tf_op jit(solution)/shard_map/ppermute | solution.py:340
  130.9 1.5 %collective-permute-start.43 = (bf16[4,80,128]{2,1,0:T(8,128)(2,1)S(1)}, bf16[4,80,128]{2,1,0:T(8,128)(2,1)S(1)}, u32[]{:S(2)}, u32[]{:S(2)}) collective-permute-start(bf16[4,80,128]{2,1,0:T(8,128)(2,1)S(1)} %get-tuple-element.79), channel_id=1, source_target_pairs={{0,7},{1,6},{2,5},{3,4},{4,3},{5,2},{6,1},{7,0},{8,15},{9,14},{10,... | collective-permute-start | bytes 245768 | tf_op jit(solution)/shard_map/ppermute | solution.py:340
  133.7 3.1 %collective-permute-done.42.refs_6_ = bf16[4,80,128]{2,1,0:T(8,128)(2,1)S(1)} collective-permute-done((bf16[4,80,128]{2,1,0:T(8,128)(2,1)S(1)}, bf16[4,80,128]{2,1,0:T(8,128)(2,1)S(1)}, u32[]{:S(2)}, u32[]{:S(2)}) %collective-permute-start.42) | collective-permute-done | bytes 81952 | tf_op jit(solution)/shard_map/ppermute | solution.py:340
  (86 shorter events, 37.6 us)
Async XLA Ops:
  8.7 22.6 %collective-permute-start.10 = (bf16[4,4,128,256]{3,2,1,0:T(8,128)(2,1)}, bf16[4,4,128,256]{3,2,1,0:T(8,128)(2,1)S(1)}, u32[]{:S(2)}, u32[]{:S(2)}) collective-permute-start(bf16[4,4,128,256]{3,2,1,0:T(8,128)(2,1)} %get-tuple-element.49), channel_id=1, source_target_pairs={{0,4},{1,5},{2,6},{3,7},{4,0},{5,1},{6,2},{7,3},{8,12},{9,13},{10,... | collective-permute-start | bytes 3145736 | tf_op jit(solution)/shard_map/ppermute | solution.py:340
  9.0 5.7 %collective-permute-start = (bf16[4,80,128]{2,1,0:T(8,128)(2,1)S(1)}, bf16[4,80,128]{2,1,0:T(8,128)(2,1)S(1)}, u32[]{:S(2)}, u32[]{:S(2)}) collective-permute-start(bf16[4,80,128]{2,1,0:T(8,128)(2,1)S(1)} %get-tuple-element.44), channel_id=1, source_target_pairs={{0,1},{1,0},{2,3},{3,2},{4,5},{5,4},{6,7},{7,6},{8,9},{9,8},{10,11... | collective-permute-start | bytes 245768 | tf_op jit(solution)/shard_map/ppermute | solution.py:340
  11.6 5.6 %collective-permute-start.1 = (bf16[4,80,128]{2,1,0:T(8,128)(2,1)S(1)}, bf16[4,80,128]{2,1,0:T(8,128)(2,1)S(1)}, u32[]{:S(2)}, u32[]{:S(2)}) collective-permute-start(bf16[4,80,128]{2,1,0:T(8,128)(2,1)S(1)} %get-tuple-element.45), channel_id=1, source_target_pairs={{0,2},{1,3},{2,0},{3,1},{4,6},{5,7},{6,4},{7,5},{8,10},{9,11},{10,... | collective-permute-start | bytes 245768 | tf_op jit(solution)/shard_map/ppermute | solution.py:340
  13.7 5.3 %collective-permute-start.2 = (bf16[4,80,128]{2,1,0:T(8,128)(2,1)S(1)}, bf16[4,80,128]{2,1,0:T(8,128)(2,1)S(1)}, u32[]{:S(2)}, u32[]{:S(2)}) collective-permute-start(bf16[4,80,128]{2,1,0:T(8,128)(2,1)S(1)} %get-tuple-element.46), channel_id=1, source_target_pairs={{0,3},{1,2},{2,1},{3,0},{4,7},{5,6},{6,5},{7,4},{8,11},{9,10},{10,... | collective-permute-start | bytes 245768 | tf_op jit(solution)/shard_map/ppermute | solution.py:340
  19.6 6.0 %collective-permute-start.8 = (bf16[4,80,128]{2,1,0:T(8,128)(2,1)S(1)}, bf16[4,80,128]{2,1,0:T(8,128)(2,1)S(1)}, u32[]{:S(2)}, u32[]{:S(2)}) collective-permute-start(bf16[4,80,128]{2,1,0:T(8,128)(2,1)S(1)} %get-tuple-element.47.refs_0_), channel_id=1, source_target_pairs={{0,6},{1,7},{2,4},{3,5},{4,2},{5,3},{6,0},{7,1},{8,14},{9,15},{10,... | collective-permute-start | bytes 245768 | tf_op jit(solution)/shard_map/ppermute | solution.py:340
  21.1 5.7 %collective-permute-start.7 = (bf16[4,80,128]{2,1,0:T(8,128)(2,1)S(1)}, bf16[4,80,128]{2,1,0:T(8,128)(2,1)S(1)}, u32[]{:S(2)}, u32[]{:S(2)}) collective-permute-start(bf16[4,80,128]{2,1,0:T(8,128)(2,1)S(1)} %get-tuple-element.47.refs_0_), channel_id=1, source_target_pairs={{0,5},{1,4},{2,7},{3,6},{4,1},{5,0},{6,3},{7,2},{8,13},{9,12},{10,... | collective-permute-start | bytes 245768 | tf_op jit(solution)/shard_map/ppermute | solution.py:340
  21.5 6.5 %collective-permute-start.6 = (bf16[4,80,128]{2,1,0:T(8,128)(2,1)S(1)}, bf16[4,80,128]{2,1,0:T(8,128)(2,1)S(1)}, u32[]{:S(2)}, u32[]{:S(2)}) collective-permute-start(bf16[4,80,128]{2,1,0:T(8,128)(2,1)S(1)} %get-tuple-element.47.refs_0_), channel_id=1, source_target_pairs={{0,4},{1,5},{2,6},{3,7},{4,0},{5,1},{6,2},{7,3},{8,12},{9,13},{10,... | collective-permute-start | bytes 245768 | tf_op jit(solution)/shard_map/ppermute | solution.py:340
  24.5 5.8 %collective-permute-start.5 = (bf16[4,80,128]{2,1,0:T(8,128)(2,1)S(1)}, bf16[4,80,128]{2,1,0:T(8,128)(2,1)S(1)}, u32[]{:S(2)}, u32[]{:S(2)}) collective-permute-start(bf16[4,80,128]{2,1,0:T(8,128)(2,1)S(1)} %get-tuple-element.47.refs_0_), channel_id=1, source_target_pairs={{0,3},{1,2},{2,1},{3,0},{4,7},{5,6},{6,5},{7,4},{8,11},{9,10},{10,... | collective-permute-start | bytes 245768 | tf_op jit(solution)/shard_map/ppermute | solution.py:340
  25.6 5.3 %collective-permute-start.4 = (bf16[4,80,128]{2,1,0:T(8,128)(2,1)S(1)}, bf16[4,80,128]{2,1,0:T(8,128)(2,1)S(1)}, u32[]{:S(2)}, u32[]{:S(2)}) collective-permute-start(bf16[4,80,128]{2,1,0:T(8,128)(2,1)S(1)} %get-tuple-element.47.refs_0_), channel_id=1, source_target_pairs={{0,2},{1,3},{2,0},{3,1},{4,6},{5,7},{6,4},{7,5},{8,10},{9,11},{10,... | collective-permute-start | bytes 245768 | tf_op jit(solution)/shard_map/ppermute | solution.py:340
  32.2 7.9 %collective-permute-start.11 = (bf16[4,80,256]{2,1,0:T(8,128)(2,1)S(1)}, bf16[4,80,256]{2,1,0:T(8,128)(2,1)S(1)}, u32[]{:S(2)}, u32[]{:S(2)}) collective-permute-start(bf16[4,80,256]{2,1,0:T(8,128)(2,1)S(1)} %get-tuple-element.51), channel_id=1, source_target_pairs={{0,8},{4,12},{8,0},{12,4},{16,24},{20,28},{24,16},{28,20},{1,9},{5... | collective-permute-start | bytes 491528 | tf_op jit(solution)/shard_map/ppermute | solution.py:334
  33.7 14.7 %collective-permute-start.12 = (bf16[4,80,256]{2,1,0:T(8,128)(2,1)S(1)}, bf16[4,80,256]{2,1,0:T(8,128)(2,1)S(1)}, u32[]{:S(2)}, u32[]{:S(2)}) collective-permute-start(bf16[4,80,256]{2,1,0:T(8,128)(2,1)S(1)} %get-tuple-element.52), channel_id=1, source_target_pairs={{0,16},{4,20},{8,24},{12,28},{16,0},{20,4},{24,8},{28,12},{1,17},{... | collective-permute-start | bytes 491528 | tf_op jit(solution)/shard_map/ppermute | solution.py:334
  36.3 12.2 %collective-permute-start.13 = (bf16[4,80,256]{2,1,0:T(8,128)(2,1)S(1)}, bf16[4,80,256]{2,1,0:T(8,128)(2,1)S(1)}, u32[]{:S(2)}, u32[]{:S(2)}) collective-permute-start(bf16[4,80,256]{2,1,0:T(8,128)(2,1)S(1)} %get-tuple-element.53), channel_id=1, source_target_pairs={{0,24},{4,28},{8,16},{12,20},{16,8},{20,12},{24,0},{28,4},{1,25},{... | collective-permute-start | bytes 491528 | tf_op jit(solution)/shard_map/ppermute | solution.py:334
  48.7 7.9 %collective-permute-start.16 = (bf16[4,80,256]{2,1,0:T(8,128)(2,1)S(1)}, bf16[4,80,256]{2,1,0:T(8,128)(2,1)S(1)}, u32[]{:S(2)}, u32[]{:S(2)}) collective-permute-start(bf16[4,80,256]{2,1,0:T(8,128)(2,1)S(1)} %get-tuple-element.54.refs_0_), channel_id=1, source_target_pairs={{0,24},{4,28},{8,16},{12,20},{16,8},{20,12},{24,0},{28,4},{1,25},{... | collective-permute-start | bytes 491528 | tf_op jit(solution)/shard_map/ppermute | solution.py:334
  51.6 13.5 %collective-permute-start.15 = (bf16[4,80,256]{2,1,0:T(8,128)(2,1)S(1)}, bf16[4,80,256]{2,1,0:T(8,128)(2,1)S(1)}, u32[]{:S(2)}, u32[]{:S(2)}) collective-permute-start(bf16[4,80,256]{2,1,0:T(8,128)(2,1)S(1)} %get-tuple-element.54.refs_0_), channel_id=1, source_target_pairs={{0,16},{4,20},{8,24},{12,28},{16,0},{20,4},{24,8},{28,12},{1,17},{... | collective-permute-start | bytes 491528 | tf_op jit(solution)/shard_map/ppermute | solution.py:334
  53.2 12.0 %collective-permute-start.14 = (bf16[4,80,256]{2,1,0:T(8,128)(2,1)S(1)}, bf16[4,80,256]{2,1,0:T(8,128)(2,1)S(1)}, u32[]{:S(2)}, u32[]{:S(2)}) collective-permute-start(bf16[4,80,256]{2,1,0:T(8,128)(2,1)S(1)} %get-tuple-element.54.refs_0_), channel_id=1, source_target_pairs={{0,8},{4,12},{8,0},{12,4},{16,24},{20,28},{24,16},{28,20},{1,9},{5... | collective-permute-start | bytes 491528 | tf_op jit(solution)/shard_map/ppermute | solution.py:334
  66.2 5.6 %collective-permute-start.17 = (bf16[4,80,128]{2,1,0:T(8,128)(2,1)S(1)}, bf16[4,80,128]{2,1,0:T(8,128)(2,1)S(1)}, u32[]{:S(2)}, u32[]{:S(2)}) collective-permute-start(bf16[4,80,128]{2,1,0:T(8,128)(2,1)S(1)} %get-tuple-element.56), channel_id=1, source_target_pairs={{0,1},{1,0},{2,3},{3,2},{4,5},{5,4},{6,7},{7,6},{8,9},{9,8},{10,11... | collective-permute-start | bytes 245768 | tf_op jit(solution)/shard_map/ppermute | solution.py:340
  68.5 6.0 %collective-permute-start.19 = (bf16[4,80,128]{2,1,0:T(8,128)(2,1)S(1)}, bf16[4,80,128]{2,1,0:T(8,128)(2,1)S(1)}, u32[]{:S(2)}, u32[]{:S(2)}) collective-permute-start(bf16[4,80,128]{2,1,0:T(8,128)(2,1)S(1)} %get-tuple-element.58), channel_id=1, source_target_pairs={{0,3},{1,2},{2,1},{3,0},{4,7},{5,6},{6,5},{7,4},{8,11},{9,10},{10,... | collective-permute-start | bytes 245768 | tf_op jit(solution)/shard_map/ppermute | solution.py:340
  78.7 6.0 %collective-permute-start.30 = (bf16[4,80,128]{2,1,0:T(8,128)(2,1)S(1)}, bf16[4,80,128]{2,1,0:T(8,128)(2,1)S(1)}, u32[]{:S(2)}, u32[]{:S(2)}) collective-permute-start(bf16[4,80,128]{2,1,0:T(8,128)(2,1)S(1)} %get-tuple-element.65.refs_0_), channel_id=1, source_target_pairs={{0,7},{1,6},{2,5},{3,4},{4,3},{5,2},{6,1},{7,0},{8,15},{9,14},{10,... | collective-permute-start | bytes 245768 | tf_op jit(solution)/shard_map/ppermute | solution.py:340
  80.8 5.1 %collective-permute-start.29 = (bf16[4,80,128]{2,1,0:T(8,128)(2,1)S(1)}, bf16[4,80,128]{2,1,0:T(8,128)(2,1)S(1)}, u32[]{:S(2)}, u32[]{:S(2)}) collective-permute-start(bf16[4,80,128]{2,1,0:T(8,128)(2,1)S(1)} %get-tuple-element.65.refs_0_), channel_id=1, source_target_pairs={{0,6},{1,7},{2,4},{3,5},{4,2},{5,3},{6,0},{7,1},{8,14},{9,15},{10,... | collective-permute-start | bytes 245768 | tf_op jit(solution)/shard_map/ppermute | solution.py:340
  81.5 6.3 %collective-permute-start.28 = (bf16[4,80,128]{2,1,0:T(8,128)(2,1)S(1)}, bf16[4,80,128]{2,1,0:T(8,128)(2,1)S(1)}, u32[]{:S(2)}, u32[]{:S(2)}) collective-permute-start(bf16[4,80,128]{2,1,0:T(8,128)(2,1)S(1)} %get-tuple-element.65.refs_0_), channel_id=1, source_target_pairs={{0,5},{1,4},{2,7},{3,6},{4,1},{5,0},{6,3},{7,2},{8,13},{9,12},{10,... | collective-permute-start | bytes 245768 | tf_op jit(solution)/shard_map/ppermute | solution.py:340
  82.0 5.8 %collective-permute-start.27 = (bf16[4,80,128]{2,1,0:T(8,128)(2,1)S(1)}, bf16[4,80,128]{2,1,0:T(8,128)(2,1)S(1)}, u32[]{:S(2)}, u32[]{:S(2)}) collective-permute-start(bf16[4,80,128]{2,1,0:T(8,128)(2,1)S(1)} %get-tuple-element.65.refs_0_), channel_id=1, source_target_pairs={{0,4},{1,5},{2,6},{3,7},{4,0},{5,1},{6,2},{7,3},{8,12},{9,13},{10,... | collective-permute-start | bytes 245768 | tf_op jit(solution)/shard_map/ppermute | solution.py:340
  82.1 7.0 %collective-permute-start.26 = (bf16[4,80,128]{2,1,0:T(8,128)(2,1)S(1)}, bf16[4,80,128]{2,1,0:T(8,128)(2,1)S(1)}, u32[]{:S(2)}, u32[]{:S(2)}) collective-permute-start(bf16[4,80,128]{2,1,0:T(8,128)(2,1)S(1)} %get-tuple-element.65.refs_0_), channel_id=1, source_target_pairs={{0,3},{1,2},{2,1},{3,0},{4,7},{5,6},{6,5},{7,4},{8,11},{9,10},{10,... | collective-permute-start | bytes 245768 | tf_op jit(solution)/shard_map/ppermute | solution.py:340
  84.7 5.8 %collective-permute-start.25 = (bf16[4,80,128]{2,1,0:T(8,128)(2,1)S(1)}, bf16[4,80,128]{2,1,0:T(8,128)(2,1)S(1)}, u32[]{:S(2)}, u32[]{:S(2)}) collective-permute-start(bf16[4,80,128]{2,1,0:T(8,128)(2,1)S(1)} %get-tuple-element.65.refs_0_), channel_id=1, source_target_pairs={{0,2},{1,3},{2,0},{3,1},{4,6},{5,7},{6,4},{7,5},{8,10},{9,11},{10,... | collective-permute-start | bytes 245768 | tf_op jit(solution)/shard_map/ppermute | solution.py:340
  91.6 8.7 %collective-permute-start.31 = (bf16[4,80,256]{2,1,0:T(8,128)(2,1)S(1)}, bf16[4,80,256]{2,1,0:T(8,128)(2,1)S(1)}, u32[]{:S(2)}, u32[]{:S(2)}) collective-permute-start(bf16[4,80,256]{2,1,0:T(8,128)(2,1)S(1)} %get-tuple-element.67), channel_id=1, source_target_pairs={{0,8},{4,12},{8,0},{12,4},{16,24},{20,28},{24,16},{28,20},{1,9},{5... | collective-permute-start | bytes 491528 | tf_op jit(solution)/shard_map/ppermute | solution.py:334
  91.8 15.5 %collective-permute-start.32 = (bf16[4,80,256]{2,1,0:T(8,128)(2,1)S(1)}, bf16[4,80,256]{2,1,0:T(8,128)(2,1)S(1)}, u32[]{:S(2)}, u32[]{:S(2)}) collective-permute-start(bf16[4,80,256]{2,1,0:T(8,128)(2,1)S(1)} %get-tuple-element.68), channel_id=1, source_target_pairs={{0,16},{4,20},{8,24},{12,28},{16,0},{20,4},{24,8},{28,12},{1,17},{... | collective-permute-start | bytes 491528 | tf_op jit(solution)/shard_map/ppermute | solution.py:334
  95.1 12.1 %collective-permute-start.33 = (bf16[4,80,256]{2,1,0:T(8,128)(2,1)S(1)}, bf16[4,80,256]{2,1,0:T(8,128)(2,1)S(1)}, u32[]{:S(2)}, u32[]{:S(2)}) collective-permute-start(bf16[4,80,256]{2,1,0:T(8,128)(2,1)S(1)} %get-tuple-element.69), channel_id=1, source_target_pairs={{0,24},{4,28},{8,16},{12,20},{16,8},{20,12},{24,0},{28,4},{1,25},{... | collective-permute-start | bytes 491528 | tf_op jit(solution)/shard_map/ppermute | solution.py:334
  108.2 8.3 %collective-permute-start.36 = (bf16[4,80,256]{2,1,0:T(8,128)(2,1)S(1)}, bf16[4,80,256]{2,1,0:T(8,128)(2,1)S(1)}, u32[]{:S(2)}, u32[]{:S(2)}) collective-permute-start(bf16[4,80,256]{2,1,0:T(8,128)(2,1)S(1)} %get-tuple-element.71.refs_0_), channel_id=1, source_target_pairs={{0,24},{4,28},{8,16},{12,20},{16,8},{20,12},{24,0},{28,4},{1,25},{... | collective-permute-start | bytes 491528 | tf_op jit(solution)/shard_map/ppermute | solution.py:334
  110.6 13.8 %collective-permute-start.35 = (bf16[4,80,256]{2,1,0:T(8,128)(2,1)S(1)}, bf16[4,80,256]{2,1,0:T(8,128)(2,1)S(1)}, u32[]{:S(2)}, u32[]{:S(2)}) collective-permute-start(bf16[4,80,256]{2,1,0:T(8,128)(2,1)S(1)} %get-tuple-element.71.refs_0_), channel_id=1, source_target_pairs={{0,16},{4,20},{8,24},{12,28},{16,0},{20,4},{24,8},{28,12},{1,17},{... | collective-permute-start | bytes 491528 | tf_op jit(solution)/shard_map/ppermute | solution.py:334
  112.5 11.8 %collective-permute-start.34 = (bf16[4,80,256]{2,1,0:T(8,128)(2,1)S(1)}, bf16[4,80,256]{2,1,0:T(8,128)(2,1)S(1)}, u32[]{:S(2)}, u32[]{:S(2)}) collective-permute-start(bf16[4,80,256]{2,1,0:T(8,128)(2,1)S(1)} %get-tuple-element.71.refs_0_), channel_id=1, source_target_pairs={{0,8},{4,12},{8,0},{12,4},{16,24},{20,28},{24,16},{28,20},{1,9},{5... | collective-permute-start | bytes 491528 | tf_op jit(solution)/shard_map/ppermute | solution.py:334
  127.5 6.1 %collective-permute-start.39 = (bf16[4,80,128]{2,1,0:T(8,128)(2,1)S(1)}, bf16[4,80,128]{2,1,0:T(8,128)(2,1)S(1)}, u32[]{:S(2)}, u32[]{:S(2)}) collective-permute-start(bf16[4,80,128]{2,1,0:T(8,128)(2,1)S(1)} %get-tuple-element.75), channel_id=1, source_target_pairs={{0,3},{1,2},{2,1},{3,0},{4,7},{5,6},{6,5},{7,4},{8,11},{9,10},{10,... | collective-permute-start | bytes 245768 | tf_op jit(solution)/shard_map/ppermute | solution.py:340
  129.9 6.9 %collective-permute-start.42 = (bf16[4,80,128]{2,1,0:T(8,128)(2,1)S(1)}, bf16[4,80,128]{2,1,0:T(8,128)(2,1)S(1)}, u32[]{:S(2)}, u32[]{:S(2)}) collective-permute-start(bf16[4,80,128]{2,1,0:T(8,128)(2,1)S(1)} %get-tuple-element.78), channel_id=1, source_target_pairs={{0,6},{1,7},{2,4},{3,5},{4,2},{5,3},{6,0},{7,1},{8,14},{9,15},{10,... | collective-permute-start | bytes 245768 | tf_op jit(solution)/shard_map/ppermute | solution.py:340
  130.9 5.8 %collective-permute-start.43 = (bf16[4,80,128]{2,1,0:T(8,128)(2,1)S(1)}, bf16[4,80,128]{2,1,0:T(8,128)(2,1)S(1)}, u32[]{:S(2)}, u32[]{:S(2)}) collective-permute-start(bf16[4,80,128]{2,1,0:T(8,128)(2,1)S(1)} %get-tuple-element.79), channel_id=1, source_target_pairs={{0,7},{1,6},{2,5},{3,4},{4,3},{5,2},{6,1},{7,0},{8,15},{9,14},{10,... | collective-permute-start | bytes 245768 | tf_op jit(solution)/shard_map/ppermute | solution.py:340
  (18 other events, 96.5 us)

commit v2 on v1

v2 whole, which is shorter than its diff:
```python
import functools

import jax
import jax.numpy as jnp
from jax import lax
from jax.experimental import pallas as pl
from jax.experimental.pallas import tpu as pltpu
from jax.sharding import PartitionSpec as P

ITERS = 2
GROUPS = 1
PLANE_SUM = "permute"
PLANE_GATHER = "permute"
LINE_SUM = "permute"
LINE_GATHER = "permute"
LANES = 128
PIECES = 3
PRIME = 32749
VMEM = pl.BlockSpec(memory_space=pltpu.VMEM)
SMEM = pl.BlockSpec(memory_space=pltpu.SMEM)
F32 = jnp.float32
BF16 = jnp.bfloat16
NT = (((1,), (1,)), ((), ()))


def call(kernel, outs, scratch, flops, *args, scalars=0):
    nbytes = sum(a.size * a.dtype.itemsize for a in (*args, *outs))
    return pl.pallas_call(
        kernel,
        out_shape=outs,
        in_specs=[SMEM] * scalars + [VMEM] * (len(args) - scalars),
        out_specs=[VMEM] * len(outs),
        scratch_shapes=scratch,
        compiler_params=pltpu.CompilerParams(vmem_limit_bytes=40 * 1024 * 1024),
        cost_estimate=pl.CostEstimate(flops=flops, bytes_accessed=nbytes, transcendentals=0),
    )(*args)


def struct(shape, dtype):
    return jax.ShapeDtypeStruct(shape, dtype)


def place():
    slab = lax.axis_index("slab")
    return slab // 2, slab % 2, lax.axis_index("obs")


def views(refs, count, me):
    if len(refs) == 1:
        return [refs[0].at[me ^ i] for i in range(count)]
    return refs


def total(x):
    return jnp.sum(jnp.sum(x, axis=0, keepdims=True), axis=1, keepdims=True)


def with_scalars(body, values):
    rows = lax.broadcasted_iota(jnp.int32, body.shape, 0)
    lanes = lax.broadcasted_iota(jnp.int32, body.shape, 1)
    line = jnp.zeros(body.shape, F32)
    for q, value in enumerate(values):
        rest = value
        for piece in range(PIECES):
            part = rest.astype(BF16).astype(F32)
            rest = rest - part
            line = jnp.where(lanes == q * PIECES + piece, part, line)
    return jnp.where(rows == body.shape[0] - 1, line, body)


def read_scalars(refs, member, count):
    rows = refs[0].shape[1]
    tail = refs[0][member, rows - 16 : rows, 0:LANES].astype(F32)
    for ref in refs[1:]:
        tail = tail + ref[member, rows - 16 : rows, 0:LANES].astype(F32)
    sub = lax.broadcasted_iota(jnp.int32, tail.shape, 0)
    lanes = lax.broadcasted_iota(jnp.int32, tail.shape, 1)
    found = []
    for q in range(count):
        mine = (sub == 15) & (lanes >= q * PIECES) & (lanes < (q + 1) * PIECES)
        found.append(total(jnp.where(mine, tail, 0.0)))
    return found


def remainder(x, factor):
    return x - (x.astype(F32) * factor).astype(jnp.int32) * PRIME


def start_kernel(dims, seeds, ids, cols, count, innov, prec, h, own, partner, *rest):
    chips, n_obs, halves, groups = dims
    outs, (scratch, acc) = rest[:-2], rest[-2:]
    z, core, obs = place()
    lev, blocks, profiles = innov.shape
    colblocks, width = own.shape[1], own.shape[3]
    members = seeds.shape[0]
    levp = scratch.shape[2] // blocks
    strips = profiles // LANES

    own[...] = jnp.zeros_like(own)
    partner[...] = jnp.zeros_like(partner)

    def put(n, carry):
        b, k = ids[n], cols[n]
        for half in range(halves):
            piece = b * halves + half
            tile = h[n, :, half * width : (half + 1) * width]

            @pl.when(piece % 2 == core)
            def _():
                own[piece // 2, k] = tile

            @pl.when(piece % 2 != core)
            def _():
                partner[piece // 2, k] = tile

        return carry

    lax.fori_loop(0, count[0], put, 0)

    scratch[:, :, lev * blocks :, :] = jnp.zeros(
        (members, strips, (levp - lev) * blocks, LANES), F32
    )
    shape = (blocks, profiles)
    spot = (
        lax.broadcasted_iota(jnp.int32, shape, 0) + obs * blocks
    ) * (lev * profiles) + lax.broadcasted_iota(jnp.int32, shape, 1)
    starts = [lax.rem(seeds[m], PRIME) for m in range(members)]

    def draw(level, carry):
        base = remainder(7919 * remainder(spot + level * profiles, 1.0 / PRIME), 1.0 / PRIME)
        p = prec[level]
        gain = 3.4 * p * lax.rsqrt(p)
        offset = p * innov[level] - 0.5 * gain
        gain = gain * (1.0 / PRIME)
        at = pl.multiple_of(level * blocks, blocks)
        for m in range(members):
            k0 = base + starts[m]
            k0 = jnp.where(k0 >= PRIME, k0 - PRIME, k0)
            k1 = remainder(k0 * k0 + 12345, 1.0 / PRIME)
            k2 = remainder(k1 * k1 + 2719, 1.0 / PRIME)
            k2 = jnp.where(k2 < 0, k2 + PRIME, k2)
            k2 = jnp.where(k2 >= PRIME, k2 - PRIME, k2)
            w = offset + gain * k2.astype(F32)
            for t in range(strips):
                scratch[m, t, pl.ds(at, blocks), :] = w[:, t * LANES : (t + 1) * LANES]
        return carry

    lax.fori_loop(0, lev, draw, 0, unroll=3)

    for source in range(2):
        for zz in range(chips):
            piece = 2 * zz + (core if source == 0 else 1 - core)
            rows = pl.ds(piece // halves, levp, stride=blocks)
            strip = (piece % halves) * (width // LANES)
            w = [
                jnp.concatenate(
                    [scratch[m, strip + t, rows, :].astype(BF16) for t in range(width // LANES)],
                    axis=1,
                )
                for m in range(members)
            ]
            w = jnp.concatenate(w, axis=0)
            tiles = (own if source == 0 else partner)[zz].reshape(colblocks * LANES, width)
            part = lax.dot_general(w, tiles, NT, preferred_element_type=F32)
            for k in range(colblocks):
                piece_k = part[:, k * LANES : (k + 1) * LANES]
                acc[k] = piece_k if source + zz == 0 else acc[k] + piece_k

    share = members // groups
    for g in range(groups):
        for i, out in enumerate(views(outs[g::groups], n_obs, obs)):
            value = acc[obs ^ i].astype(BF16).reshape(members, levp, LANES)
            out[...] = value[g * share : (g + 1) * share]


def precision_kernel(halves, prec, out):
    z, core, unused = place()
    piece = 2 * z + core
    lev, blocks, unused = prec.shape
    width = out.shape[1]
    block = lax.broadcasted_iota(jnp.int32, (lev, blocks, width), 1)
    if halves == 1:
        mine = prec[...]
    else:
        mine = prec[:, :, pl.ds(pl.multiple_of((piece % halves) * width, LANES), width)]
    out[...] = jnp.zeros_like(out)
    out[0:lev, :] = jnp.sum(jnp.where(block == piece // halves, mine, 0.0), axis=1)


def dot(a, b):
    return jnp.dot(a, b, preferred_element_type=F32, precision=lax.Precision.HIGHEST)


def first_kernel(n_obs, *refs):
    (sd, vert, vert_t, residual, moved), pieces = refs[-5:], refs[:-5]
    pieces = views(pieces, n_obs, lax.axis_index("obs"))
    for m in range(residual.shape[0]):
        t = pieces[0][m].astype(F32)
        for ref in pieces[1:]:
            t = t + ref[m].astype(F32)
        r = dot(vert_t[...], sd[...] * t)
        residual[m] = r
        x = sd[...] * dot(vert[...], r)
        put_columns(moved, m, with_scalars(x, [total(r * r)]).astype(BF16))


def put_columns(moved, m, x):
    if len(moved.shape) == 3:
        moved[m] = x
    else:
        for i in range(moved.shape[0]):
            moved[i, m] = x


def forward_kernel(dims, *refs):
    chips, n_obs, n_columns, n_outs = dims
    z, core, obs = place()
    xs = []
    for source in range(2):
        xs += views(refs[source * n_columns : (source + 1) * n_columns], n_obs, obs)
    own, partner = refs[2 * n_columns : 2 * n_columns + 2]
    panel = refs[-1]
    outs = views(refs[-1 - n_outs : -1], chips, z)
    members, levp, unused = xs[0].shape
    colblocks, width = own.shape[1], own.shape[3]
    rows = members * levp
    for source in range(2):
        for i in range(n_obs):
            at = pl.multiple_of((source * colblocks + (obs ^ i)) * LANES, LANES)
            panel[:, pl.ds(at, LANES)] = xs[source * n_obs + i][...].reshape(rows, LANES)
    scalars = [read_scalars(xs, m, 2) for m in range(members)]
    half = colblocks * LANES
    for i in range(chips):
        zz = z ^ i
        y = jnp.dot(panel[:, 0:half], own[zz].reshape(half, width), preferred_element_type=F32)
        y = y + jnp.dot(
            panel[:, half : 2 * half], partner[zz].reshape(half, width), preferred_element_type=F32
        )
        y = y.reshape(members, levp, width)
        for m in range(members):
            outs[i][m] = with_scalars(y[m], scalars[m]).astype(outs[i].dtype)


def weigh_kernel(chips, later, n_ys, *refs):
    ys, prec = views(refs[:n_ys], chips, place()[0]), refs[n_ys]
    image, weighted, state = refs[-3:]
    p = prec[...]
    for m in range(image.shape[0]):
        y = ys[0][m].astype(F32)
        for ref in ys[1:]:
            y = y + ref[m].astype(F32)
        norm, cross = read_scalars(ys, m, 2)
        if later:
            old_image, old = refs[n_ys + 1 : n_ys + 3]
            old_norm, old_square = old[m, 0:1, 0:1], old[m, 1:2, 0:1]
            beta = norm / old_norm
            square = norm + 2.0 * beta * cross + beta * beta * old_square
            y = y + beta * old_image[m]
        else:
            beta = jnp.zeros_like(norm)
            square = norm
        scaled = p * y
        image[m] = y
        put_columns(weighted, m, with_scalars(scaled, [total(scaled * y)]).astype(BF16))
        sub = lax.broadcasted_iota(jnp.int32, (8, LANES), 0)
        state[m] = jnp.where(sub == 0, norm, jnp.where(sub == 1, square, beta))


def adjoint_kernel(dims, *refs):
    chips, n_obs, n_ws, n_outs, added = dims
    z, core, obs = place()
    ws, tiles = views(refs[:n_ws], chips, z), refs[n_ws]
    acc = refs[-1]
    outs = refs[-1 - n_outs : -1]
    members, levp, width = ws[0].shape
    colblocks = tiles.shape[1]
    rows = members * levp
    for i in range(chips):
        part = lax.dot_general(
            ws[i][...].reshape(rows, width),
            tiles[z ^ i].reshape(colblocks * LANES, width),
            NT,
            preferred_element_type=F32,
        )
        for k in range(colblocks):
            piece = part[:, k * LANES : (k + 1) * LANES]
            acc[k] = piece if i == 0 else acc[k] + piece
    if added:
        more = refs[n_ws + 1]
        outs = views(outs, n_obs, obs)
    for m in range(members):
        (energy,) = read_scalars(ws, m, 1)
        if added:
            energy = energy + read_scalars([more.at[0]], m, 1)[0]
        for i in range(n_obs):
            if added:
                value = acc[obs ^ i].reshape(members, levp, LANES)[m]
                value = value + more[obs ^ i, m].astype(F32)
                outs[i][m] = with_scalars(value, [energy]).astype(BF16)
            else:
                value = acc[i].reshape(members, levp, LANES)[m]
                outs[0][i, m] = with_scalars(value, [energy]).astype(BF16)


def update_kernel(n_obs, n_pieces, later, last, lev, *refs):
    pieces = views(refs[:n_pieces], n_obs, lax.axis_index("obs"))
    sd, vert, vert_t, state, residual = refs[n_pieces : n_pieces + 5]
    more = refs[n_pieces + 5 :]
    old_direction = old_solution = None
    if later:
        old_direction, old_solution = more[:2]
        more = more[2:]
    for m in range(residual.shape[0]):
        t = pieces[0][m].astype(F32)
        for ref in pieces[1:]:
            t = t + ref[m].astype(F32)
        (energy,) = read_scalars(pieces, m, 1)
        norm, square, beta = state[m, 0:1, 0:1], state[m, 1:2, 0:1], state[m, 2:3, 0:1]
        alpha = norm / (square + energy)
        r = residual[m]
        d = r + beta * old_direction[m] if later else r
        q = d + dot(vert_t[...], sd[...] * t)
        solution = alpha * d
        if later:
            solution = old_solution[m] + solution
        r = r - alpha * q
        if last:
            increment_out, residual_out = more
            increment = sd[...] * dot(vert[...], solution)
            increment_out[:, m, :] = increment[0:lev]
            residual_out[:, m, :] = r[0:lev]
        else:
            residual_out, direction_out, solution_out, moved = more
            residual_out[m] = r
            direction_out[m] = d
            solution_out[m] = solution
            x = sd[...] * dot(vert[...], r)
            put_columns(moved, m, with_scalars(x, [total(r * r), total(r * d)]).astype(BF16))


def per_device(
    n_slab,
    n_obs,
    innovation,
    obs_precision,
    seeds,
    col_sd,
    vert_factor,
    h_values,
    block_obs,
    block_col,
    entry_count,
):
    blocks, lev, profiles = innovation.shape
    members = seeds.shape[0]
    groups, share = GROUPS, members // GROUPS
    chips = n_slab // 2
    halves = n_slab // blocks
    width = profiles // halves
    colblocks = n_obs
    assert halves * blocks == n_slab and width % LANES == 0 and col_sd.shape[0] == 1
    assert chips & (chips - 1) == 0 and n_obs & (n_obs - 1) == 0
    levp = (lev + 1 + 15) // 16 * 16
    rows = share * levp
    field = (share, levp, LANES)
    panel = (share, levp, width)
    pad = ((0, levp - lev), (0, levp - lev))
    vert = jnp.pad(vert_factor, pad)
    vert_t = jnp.pad(vert_factor.T, pad)
    h_block = h_values.reshape(h_values.shape[2:])
    innovation = jnp.transpose(innovation, (1, 0, 2))
    obs_precision = jnp.transpose(obs_precision, (1, 0, 2))
    product = n_slab * width * colblocks * LANES * rows
    small = 24 * rows * levp * LANES
    cores = [[s for s in range(n_slab) if s % 2 == c] for c in range(2)]

    def along(x, i):
        return lax.ppermute(x, "slab", [(s, s ^ (2 * i)) for s in range(n_slab)])

    def plane(x, i):
        return lax.ppermute(x, "obs", [(o, o ^ i) for o in range(n_obs)])

    def swap(x):
        return lax.ppermute(x, "slab", [(s, s ^ 1) for s in range(n_slab)])

    def spread(mode, outs, move):
        if mode == "permute":
            return [x if i == 0 else move(x, i) for i, x in enumerate(outs)]
        if move is plane:
            return [lax.all_to_all(outs[0], "obs", 0, 0, tiled=True)]
        return [lax.all_to_all(outs[0], "slab", 0, 0, axis_index_groups=cores, tiled=True)]

    def copies(mode, x, count):
        return [x] * count if mode == "permute" else [x]

    def shapes(mode, shape, dtype, count):
        return [struct(shape, dtype)] * count if mode == "permute" else [struct((count, *shape), dtype)]

    dense = struct((chips, colblocks, LANES, width), BF16)
    partial_shapes = shapes(PLANE_SUM, field, BF16, n_obs)
    n_parts = len(partial_shapes)
    own, for_partner, *partials = call(
        functools.partial(start_kernel, (chips, n_obs, halves, groups)),
        [dense, dense] + [x for x in partial_shapes for g in range(groups)],
        [
            pltpu.VMEM((members, profiles // LANES, levp * blocks, LANES), F32),
            pltpu.VMEM((colblocks, members * levp, LANES), F32),
        ],
        2 * product * groups,
        seeds,
        block_obs.reshape(-1),
        block_col.reshape(-1),
        entry_count.reshape(-1),
        innovation,
        obs_precision,
        h_block,
        scalars=4,
    )
    arrived = [spread(PLANE_SUM, partials[g::groups], plane) for g in range(groups)]
    partner = swap(for_partner)
    (precision,) = call(
        functools.partial(precision_kernel, halves),
        [struct((levp, width), F32)],
        [],
        0,
        obs_precision,
    )
    state = [None] * groups
    direction = [None] * groups
    total_step = [None] * groups
    image = [None] * groups
    residual, moved, outputs = [], [], []
    (moved_shape,) = shapes(PLANE_GATHER, field, BF16, n_obs)[:1]
    (weighted_shape,) = shapes(LINE_GATHER, panel, BF16, chips)[:1]
    for g in range(groups):
        r, x = call(
            functools.partial(first_kernel, n_obs),
            [struct(field, F32), moved_shape],
            [],
            small,
            *arrived[g],
            col_sd,
            vert,
            vert_t,
        )
        residual.append(r)
        moved.append(x)
    for sweep in range(ITERS):
        later, last = sweep > 0, sweep == ITERS - 1
        for g in range(groups):
            columns = spread(PLANE_GATHER, copies(PLANE_GATHER, moved[g], n_obs), plane)
            others = [swap(x) for x in columns]
            image_shapes = shapes(LINE_SUM, panel, BF16, chips)
            if len(image_shapes) > 1:
                image_shapes[0] = struct(panel, F32)
            ys = call(
                functools.partial(
                    forward_kernel, (chips, n_obs, len(columns), len(image_shapes))
                ),
                image_shapes,
                [pltpu.VMEM((rows, 2 * colblocks * LANES), BF16)],
                2 * product,
                *columns,
                *others,
                own,
                partner,
            )
            ys = spread(LINE_SUM, ys, along)
            image[g], weighted, state[g] = call(
                functools.partial(weigh_kernel, chips, later, len(ys)),
                [struct(panel, F32), weighted_shape, struct((share, 8, LANES), F32)],
                [],
                0,
                *ys,
                precision,
                *([image[g], state[g]] if later else []),
            )
            ws = spread(LINE_GATHER, copies(LINE_GATHER, weighted, chips), along)
            acc = [pltpu.VMEM((colblocks, rows, LANES), F32)]
            (theirs,) = call(
                functools.partial(adjoint_kernel, (chips, n_obs, len(ws), 1, False)),
                [struct((n_obs, *field), BF16)],
                acc,
                product,
                *ws,
                partner,
            )
            ps = call(
                functools.partial(adjoint_kernel, (chips, n_obs, len(ws), n_parts, True)),
                partial_shapes,
                acc,
                product,
                *ws,
                own,
                swap(theirs),
            )
            ps = spread(PLANE_SUM, ps, plane)
            if last:
                outs = [struct((lev, share, LANES), F32)] * 2
            else:
                outs = [struct(field, F32)] * 3 + [moved_shape]
            results = call(
                functools.partial(update_kernel, n_obs, len(ps), later, last, lev),
                outs,
                [],
                small,
                *ps,
                col_sd,
                vert,
                vert_t,
                state[g],
                residual[g],
                *([direction[g], total_step[g]] if later else []),
            )
            if last:
                outputs.append(results)
            else:
                residual[g], direction[g], total_step[g], moved[g] = results
    outputs = [x[0] if groups == 1 else jnp.concatenate(x, axis=1) for x in zip(*outputs)]
    return tuple(jnp.transpose(x, (1, 0, 2))[None] for x in outputs)


def solution(mesh):
    return jax.shard_map(
        functools.partial(per_device, mesh.shape["slab"], mesh.shape["obs"]),
        mesh=mesh,
        in_specs=(
            P("obs", None, None),
            P("obs", None, None),
            P(),
            P(("slab", "obs"), None),
            P(),
            P("slab", "obs", None, None, None),
            P("slab", "obs", None),
            P("slab", "obs", None),
            P("slab", "obs"),
        ),
        out_specs=(P(("slab", "obs"), None, None, None), P(("slab", "obs"), None, None, None)),
        check_vma=False,
    )
```

time: 138 us -> 132 us (0.957)
  starting transfers between devices: 53.2 us -> 38.4 us
  waiting for transfers between devices: 68.4 us -> 71.8 us
  Pallas kernels: 11.5 us -> 13.9 us
  local copies, waits for them, and re-layouts: 4.15 us -> 5.82 us
    ppermute x44 -> x38, starting transfers between devices: 53.2 us -> 38.4 us  [the longest x15 18.9 us: plane(): return lax.ppermute(x, 'obs', [(o, o ^ i) for o in range(n_obs)])]
    ppermute x44 -> x38, waiting for transfers between devices: 68.4 us -> 71.8 us  [the longest x12 47.3 us: along(): return lax.ppermute(x, 'slab', [(s, s ^ 2 * i) for s in range(n_slab)])]
    unnamed x15 -> x19, local copies, waits for them, and re-layouts: 2.69 us -> 5.8 us
    pallas_call x11 -> x13, Pallas kernels: 11.5 us -> 13.9 us  [call(): pl.pallas_call(kernel, out_shape=outs, in_specs=[SMEM] * scalars + [VMEM]...]
    pallas_call x2 -> x0, local copies, waits for them, and re-layouts: 1.45 us -> none  [call(): pl.pallas_call(kernel, out_shape=outs, in_specs=[SMEM] * scalars + [VMEM]...]
  transfers between devices with their start and end apart: 44 -> 38, of which waited for: 27 -> 28; matrix products, arithmetic and copies ran while one was open for 0% -> 0% of each run, Pallas kernels for 0% -> 1%
where the time goes in v2:
time: 132 us; the launch traced here: 131 us
  waiting for transfers between devices  71.8 us (54%)
  starting transfers between devices  38.4 us (29%)
  Pallas kernels  13.9 us (11%)
  local copies, waits for them, and re-layouts  5.82 us (4%)
  between operations  1.45 us (1%)
    ppermute x12, waiting for transfers between devices, along(): return lax.ppermute(x, 'slab', [(s, s ^ 2 * i) for s in range(n_slab)])  47.3 us
    ppermute x15, waiting for transfers between devices, plane(): return lax.ppermute(x, 'obs', [(o, o ^ i) for o in range(n_obs)])  19 us
    ppermute x15, starting transfers between devices, plane(): return lax.ppermute(x, 'obs', [(o, o ^ i) for o in range(n_obs)])  18.9 us
    ppermute x12, starting transfers between devices, along(): return lax.ppermute(x, 'slab', [(s, s ^ 2 * i) for s in range(n_slab)])  18.4 us
    pallas_call x13, Pallas kernels, call(): pl.pallas_call(kernel, out_shape=outs, in_specs=[SMEM] * scalars + [VMEM]...  13.9 us
    unnamed x19, local copies, waits for them, and re-layouts  5.8 us
    ppermute x11, waiting for transfers between devices, swap(): return lax.ppermute(x, 'slab', [(s, s ^ 1) for s in range(n_slab)])  5.48 us
  transfers between devices with their start and end apart: 38, of which 28 were waited for; matrix products, arithmetic and copies ran while one was open for 0% of the time, Pallas kernels for 1%

profile of v2, /device:TPU:0, one launch (start us, length us, event | category | flops | bytes accessed | tf_op | source)
XLA Modules:
  0.0 131.4 jit_solution(8657528626413451401)
XLA Ops:
  2.4 1.6 %copy-done.2 = bf16[1,1,32,128,256]{4,3,2,1,0:T(8,128)(2,1)S(1)} copy-done((bf16[1,1,32,128,256]{4,3,2,1,0:T(8,128)(2,1)S(1)}, bf16[1,1,32,128,256]{4,3,2,1,0:T(8,128)(2,1)}, u32[]{:S(2)}) %copy-start.2) | copy-done | bytes 2097176
  7.0 5.8 %shard_map.104 = (bf16[4,4,128,256]{3,2,1,0:T(8,128)(2,1)S(1)}, bf16[4,4,128,256]{3,2,1,0:T(8,128)(2,1)}, bf16[4,80,128]{2,1,0:T(8,128)(2,1)S(1)}, bf16[4,80,128...) custom-call(s32[4]{0:T(128)S(1)} %copy-done.5, s32[32]{0:T(128)S(1)} %bitcast.18, ...), custom_call_target="tpu_custom_call" | custom-call | flops 671088640 | bytes 5751060 | tf_op jit(solution)/shard_map/pallas_call | solution.py:28
  13.3 3.2 %collective-permute-start = (bf16[4,80,128]{2,1,0:T(8,128)(2,1)S(1)}, bf16[4,80,128]{2,1,0:T(8,128)(2,1)S(1)}, u32[]{:S(2)}, u32[]{:S(2)}) collective-permute-start(bf16[4,80,128]{2,1,0:T(8,128)(2,1)S(1)} %get-tuple-element.38), channel_id=1, source_target_pairs={{0,1},{1,0},{2,3},{3,2},{4,5},{5,4},{6,7},{7,6},{8,9},{9,8},{10,11... | collective-permute-start | bytes 245768 | tf_op jit(solution)/shard_map/ppermute | solution.py:381
  16.5 1.4 %collective-permute-start.1 = (bf16[4,80,128]{2,1,0:T(8,128)(2,1)S(1)}, bf16[4,80,128]{2,1,0:T(8,128)(2,1)S(1)}, u32[]{:S(2)}, u32[]{:S(2)}) collective-permute-start(bf16[4,80,128]{2,1,0:T(8,128)(2,1)S(1)} %get-tuple-element.39), channel_id=1, source_target_pairs={{0,2},{1,3},{2,0},{3,1},{4,6},{5,7},{6,4},{7,5},{8,10},{9,11},{10,... | collective-permute-start | bytes 245768 | tf_op jit(solution)/shard_map/ppermute | solution.py:381
  18.2 1.5 %collective-permute-done.refs_1_ = bf16[4,80,128]{2,1,0:T(8,128)(2,1)S(1)} collective-permute-done((bf16[4,80,128]{2,1,0:T(8,128)(2,1)S(1)}, bf16[4,80,128]{2,1,0:T(8,128)(2,1)S(1)}, u32[]{:S(2)}, u32[]{:S(2)}) %collective-permute-start) | collective-permute-done | bytes 81952 | tf_op jit(solution)/shard_map/ppermute | solution.py:381
  19.6 2.3 %collective-permute-done.1.refs_2_ = bf16[4,80,128]{2,1,0:T(8,128)(2,1)S(1)} collective-permute-done((bf16[4,80,128]{2,1,0:T(8,128)(2,1)S(1)}, bf16[4,80,128]{2,1,0:T(8,128)(2,1)S(1)}, u32[]{:S(2)}, u32[]{:S(2)}) %collective-permute-start.1) | collective-permute-done | bytes 81952 | tf_op jit(solution)/shard_map/ppermute | solution.py:381
  25.6 1.7 %collective-permute-start.3 = (bf16[4,80,128]{2,1,0:T(8,128)(2,1)S(1)}, bf16[4,80,128]{2,1,0:T(8,128)(2,1)S(1)}, u32[]{:S(2)}, u32[]{:S(2)}) collective-permute-start(bf16[4,80,128]{2,1,0:T(8,128)(2,1)S(1)} %get-tuple-element.41.refs_0_), channel_id=1, source_target_pairs={{0,1},{1,0},{2,3},{3,2},{4,5},{5,4},{6,7},{7,6},{8,9},{9,8},{10,11... | collective-permute-start | bytes 245768 | tf_op jit(solution)/shard_map/ppermute | solution.py:381
  27.3 2.3 %collective-permute-done.5.refs_3_ = bf16[4,80,128]{2,1,0:T(8,128)(2,1)S(1)} collective-permute-done((bf16[4,80,128]{2,1,0:T(8,128)(2,1)S(1)}, bf16[4,80,128]{2,1,0:T(8,128)(2,1)S(1)}, u32[]{:S(2)}, u32[]{:S(2)}) %collective-permute-start.5) | collective-permute-done | bytes 81952 | tf_op jit(solution)/shard_map/ppermute | solution.py:381
  32.5 1.9 %collective-permute-start.11 = (bf16[4,80,256]{2,1,0:T(8,128)(2,1)S(1)}, bf16[4,80,256]{2,1,0:T(8,128)(2,1)S(1)}, u32[]{:S(2)}, u32[]{:S(2)}) collective-permute-start(bf16[4,80,256]{2,1,0:T(8,128)(2,1)S(1)} %get-tuple-element.45), channel_id=1, source_target_pairs={{0,8},{4,12},{8,0},{12,4},{16,24},{20,28},{24,16},{28,20},{1,9},{5... | collective-permute-start | bytes 491528 | tf_op jit(solution)/shard_map/ppermute | solution.py:378
  34.4 2.6 %collective-permute-start.12 = (bf16[4,80,256]{2,1,0:T(8,128)(2,1)S(1)}, bf16[4,80,256]{2,1,0:T(8,128)(2,1)S(1)}, u32[]{:S(2)}, u32[]{:S(2)}) collective-permute-start(bf16[4,80,256]{2,1,0:T(8,128)(2,1)S(1)} %get-tuple-element.46), channel_id=1, source_target_pairs={{0,16},{4,20},{8,24},{12,28},{16,0},{20,4},{24,8},{28,12},{1,17},{... | collective-permute-start | bytes 491528 | tf_op jit(solution)/shard_map/ppermute | solution.py:378
  37.2 4.7 %collective-permute-done.11.refs_1_ = bf16[4,80,256]{2,1,0:T(8,128)(2,1)S(1)} collective-permute-done((bf16[4,80,256]{2,1,0:T(8,128)(2,1)S(1)}, bf16[4,80,256]{2,1,0:T(8,128)(2,1)S(1)}, u32[]{:S(2)}, u32[]{:S(2)}) %collective-permute-start.11) | collective-permute-done | bytes 163872 | tf_op jit(solution)/shard_map/ppermute | solution.py:378
  41.8 7.6 %collective-permute-done.12.refs_2_ = bf16[4,80,256]{2,1,0:T(8,128)(2,1)S(1)} collective-permute-done((bf16[4,80,256]{2,1,0:T(8,128)(2,1)S(1)}, bf16[4,80,256]{2,1,0:T(8,128)(2,1)S(1)}, u32[]{:S(2)}, u32[]{:S(2)}) %collective-permute-start.12) | collective-permute-done | bytes 163872 | tf_op jit(solution)/shard_map/ppermute | solution.py:378
  49.6 2.2 %collective-permute-start.16 = (bf16[4,80,256]{2,1,0:T(8,128)(2,1)S(1)}, bf16[4,80,256]{2,1,0:T(8,128)(2,1)S(1)}, u32[]{:S(2)}, u32[]{:S(2)}) collective-permute-start(bf16[4,80,256]{2,1,0:T(8,128)(2,1)S(1)} %get-tuple-element.48.refs_0_), channel_id=1, source_target_pairs={{0,24},{4,28},{8,16},{12,20},{16,8},{20,12},{24,0},{28,4},{1,25},{... | collective-permute-start | bytes 491528 | tf_op jit(solution)/shard_map/ppermute | solution.py:378
  51.8 2.4 %collective-permute-start.15 = (bf16[4,80,256]{2,1,0:T(8,128)(2,1)S(1)}, bf16[4,80,256]{2,1,0:T(8,128)(2,1)S(1)}, u32[]{:S(2)}, u32[]{:S(2)}) collective-permute-start(bf16[4,80,256]{2,1,0:T(8,128)(2,1)S(1)} %get-tuple-element.48.refs_0_), channel_id=1, source_target_pairs={{0,16},{4,20},{8,24},{12,28},{16,0},{20,4},{24,8},{28,12},{1,17},{... | collective-permute-start | bytes 491528 | tf_op jit(solution)/shard_map/ppermute | solution.py:378
  54.2 3.2 %collective-permute-done.16.refs_3_ = bf16[4,80,256]{2,1,0:T(8,128)(2,1)S(1)} collective-permute-done((bf16[4,80,256]{2,1,0:T(8,128)(2,1)S(1)}, bf16[4,80,256]{2,1,0:T(8,128)(2,1)S(1)}, u32[]{:S(2)}, u32[]{:S(2)}) %collective-permute-start.16) | collective-permute-done | bytes 163872 | tf_op jit(solution)/shard_map/ppermute | solution.py:378
  57.4 9.0 %collective-permute-done.15.refs_2_ = bf16[4,80,256]{2,1,0:T(8,128)(2,1)S(1)} collective-permute-done((bf16[4,80,256]{2,1,0:T(8,128)(2,1)S(1)}, bf16[4,80,256]{2,1,0:T(8,128)(2,1)S(1)}, u32[]{:S(2)}, u32[]{:S(2)}) %collective-permute-start.15) | collective-permute-done | bytes 163872 | tf_op jit(solution)/shard_map/ppermute | solution.py:378
  67.0 1.6 %collective-permute-done.17.refs_5_ = bf16[4,4,80,128]{3,2,1,0:T(8,128)(2,1)S(1)} collective-permute-done((bf16[4,4,80,128]{3,2,1,0:T(8,128)(2,1)S(1)}, bf16[4,4,80,128]{3,2,1,0:T(8,128)(2,1)S(1)}, u32[]{:S(2)}, u32[]{:S(2)}) %collective-permute-start.17) | collective-permute-done | bytes 327712 | tf_op jit(solution)/shard_map/ppermute | solution.py:384
  71.2 1.7 %collective-permute-start.20 = (bf16[4,80,128]{2,1,0:T(8,128)(2,1)S(1)}, bf16[4,80,128]{2,1,0:T(8,128)(2,1)S(1)}, u32[]{:S(2)}, u32[]{:S(2)}) collective-permute-start(bf16[4,80,128]{2,1,0:T(8,128)(2,1)S(1)} %get-tuple-element.52), channel_id=1, source_target_pairs={{0,3},{1,2},{2,1},{3,0},{4,7},{5,6},{6,5},{7,4},{8,11},{9,10},{10,... | collective-permute-start | bytes 245768 | tf_op jit(solution)/shard_map/ppermute | solution.py:381
  73.8 2.9 %collective-permute-done.19.refs_2_ = bf16[4,80,128]{2,1,0:T(8,128)(2,1)S(1)} collective-permute-done((bf16[4,80,128]{2,1,0:T(8,128)(2,1)S(1)}, bf16[4,80,128]{2,1,0:T(8,128)(2,1)S(1)}, u32[]{:S(2)}, u32[]{:S(2)}) %collective-permute-start.19) | collective-permute-done | bytes 81952 | tf_op jit(solution)/shard_map/ppermute | solution.py:381
  77.3 1.5 %collective-permute-start.23 = (bf16[4,80,128]{2,1,0:T(8,128)(2,1)S(1)}, bf16[4,80,128]{2,1,0:T(8,128)(2,1)S(1)}, u32[]{:S(2)}, u32[]{:S(2)}) collective-permute-start(bf16[4,80,128]{2,1,0:T(8,128)(2,1)S(1)} %get-tuple-element.55.refs_0_), channel_id=1, source_target_pairs={{0,3},{1,2},{2,1},{3,0},{4,7},{5,6},{6,5},{7,4},{8,11},{9,10},{10,... | collective-permute-start | bytes 245768 | tf_op jit(solution)/shard_map/ppermute | solution.py:381
  80.9 1.9 %collective-permute-done.23.refs_3_ = bf16[4,80,128]{2,1,0:T(8,128)(2,1)S(1)} collective-permute-done((bf16[4,80,128]{2,1,0:T(8,128)(2,1)S(1)}, bf16[4,80,128]{2,1,0:T(8,128)(2,1)S(1)}, u32[]{:S(2)}, u32[]{:S(2)}) %collective-permute-start.23) | collective-permute-done | bytes 81952 | tf_op jit(solution)/shard_map/ppermute | solution.py:381
  86.6 3.0 %collective-permute-start.29 = (bf16[4,80,256]{2,1,0:T(8,128)(2,1)S(1)}, bf16[4,80,256]{2,1,0:T(8,128)(2,1)S(1)}, u32[]{:S(2)}, u32[]{:S(2)}) collective-permute-start(bf16[4,80,256]{2,1,0:T(8,128)(2,1)S(1)} %get-tuple-element.58), channel_id=1, source_target_pairs={{0,16},{4,20},{8,24},{12,28},{16,0},{20,4},{24,8},{28,12},{1,17},{... | collective-permute-start | bytes 491528 | tf_op jit(solution)/shard_map/ppermute | solution.py:378
  89.6 1.4 %collective-permute-start.30 = (bf16[4,80,256]{2,1,0:T(8,128)(2,1)S(1)}, bf16[4,80,256]{2,1,0:T(8,128)(2,1)S(1)}, u32[]{:S(2)}, u32[]{:S(2)}) collective-permute-start(bf16[4,80,256]{2,1,0:T(8,128)(2,1)S(1)} %get-tuple-element.59), channel_id=1, source_target_pairs={{0,24},{4,28},{8,16},{12,20},{16,8},{20,12},{24,0},{28,4},{1,25},{... | collective-permute-start | bytes 491528 | tf_op jit(solution)/shard_map/ppermute | solution.py:378
  91.0 4.9 %collective-permute-done.28.refs_1_ = bf16[4,80,256]{2,1,0:T(8,128)(2,1)S(1)} collective-permute-done((bf16[4,80,256]{2,1,0:T(8,128)(2,1)S(1)}, bf16[4,80,256]{2,1,0:T(8,128)(2,1)S(1)}, u32[]{:S(2)}, u32[]{:S(2)}) %collective-permute-start.28) | collective-permute-done | bytes 163872 | tf_op jit(solution)/shard_map/ppermute | solution.py:378
  95.8 5.8 %collective-permute-done.29.refs_2_ = bf16[4,80,256]{2,1,0:T(8,128)(2,1)S(1)} collective-permute-done((bf16[4,80,256]{2,1,0:T(8,128)(2,1)S(1)}, bf16[4,80,256]{2,1,0:T(8,128)(2,1)S(1)}, u32[]{:S(2)}, u32[]{:S(2)}) %collective-permute-start.29) | collective-permute-done | bytes 163872 | tf_op jit(solution)/shard_map/ppermute | solution.py:378
  102.6 2.4 %collective-permute-start.33 = (bf16[4,80,256]{2,1,0:T(8,128)(2,1)S(1)}, bf16[4,80,256]{2,1,0:T(8,128)(2,1)S(1)}, u32[]{:S(2)}, u32[]{:S(2)}) collective-permute-start(bf16[4,80,256]{2,1,0:T(8,128)(2,1)S(1)} %get-tuple-element.61.refs_0_), channel_id=1, source_target_pairs={{0,24},{4,28},{8,16},{12,20},{16,8},{20,12},{24,0},{28,4},{1,25},{... | collective-permute-start | bytes 491528 | tf_op jit(solution)/shard_map/ppermute | solution.py:378
  105.0 2.3 %collective-permute-start.32 = (bf16[4,80,256]{2,1,0:T(8,128)(2,1)S(1)}, bf16[4,80,256]{2,1,0:T(8,128)(2,1)S(1)}, u32[]{:S(2)}, u32[]{:S(2)}) collective-permute-start(bf16[4,80,256]{2,1,0:T(8,128)(2,1)S(1)} %get-tuple-element.61.refs_0_), channel_id=1, source_target_pairs={{0,16},{4,20},{8,24},{12,28},{16,0},{20,4},{24,8},{28,12},{1,17},{... | collective-permute-start | bytes 491528 | tf_op jit(solution)/shard_map/ppermute | solution.py:378
  107.4 2.8 %collective-permute-done.33.refs_3_ = bf16[4,80,256]{2,1,0:T(8,128)(2,1)S(1)} collective-permute-done((bf16[4,80,256]{2,1,0:T(8,128)(2,1)S(1)}, bf16[4,80,256]{2,1,0:T(8,128)(2,1)S(1)}, u32[]{:S(2)}, u32[]{:S(2)}) %collective-permute-start.33) | collective-permute-done | bytes 163872 | tf_op jit(solution)/shard_map/ppermute | solution.py:378
  110.2 9.4 %collective-permute-done.32.refs_2_ = bf16[4,80,256]{2,1,0:T(8,128)(2,1)S(1)} collective-permute-done((bf16[4,80,256]{2,1,0:T(8,128)(2,1)S(1)}, bf16[4,80,256]{2,1,0:T(8,128)(2,1)S(1)}, u32[]{:S(2)}, u32[]{:S(2)}) %collective-permute-start.32) | collective-permute-done | bytes 163872 | tf_op jit(solution)/shard_map/ppermute | solution.py:378
  120.2 1.6 %collective-permute-done.34.refs_5_ = bf16[4,4,80,128]{3,2,1,0:T(8,128)(2,1)S(1)} collective-permute-done((bf16[4,4,80,128]{3,2,1,0:T(8,128)(2,1)S(1)}, bf16[4,4,80,128]{3,2,1,0:T(8,128)(2,1)S(1)}, u32[]{:S(2)}, u32[]{:S(2)}) %collective-permute-start.34) | collective-permute-done | bytes 327712 | tf_op jit(solution)/shard_map/ppermute | solution.py:384
  127.0 1.9 %collective-permute-done.36.refs_2_ = bf16[4,80,128]{2,1,0:T(8,128)(2,1)S(1)} collective-permute-done((bf16[4,80,128]{2,1,0:T(8,128)(2,1)S(1)}, bf16[4,80,128]{2,1,0:T(8,128)(2,1)S(1)}, u32[]{:S(2)}, u32[]{:S(2)}) %collective-permute-start.36) | collective-permute-done | bytes 81952 | tf_op jit(solution)/shard_map/ppermute | solution.py:381
  130.1 1.3 shard_map.116
  (78 shorter events, 30.3 us)
Async XLA Ops:
  12.8 18.6 %collective-permute-start.10 = (bf16[4,4,128,256]{3,2,1,0:T(8,128)(2,1)}, bf16[4,4,128,256]{3,2,1,0:T(8,128)(2,1)S(1)}, u32[]{:S(2)}, u32[]{:S(2)}) collective-permute-start(bf16[4,4,128,256]{3,2,1,0:T(8,128)(2,1)} %get-tuple-element.43), channel_id=1, source_target_pairs={{0,4},{4,0},{8,12},{12,8},{16,20},{20,16},{24,28},{28,24},{1,5},{5... | collective-permute-start | bytes 3145736 | tf_op jit(solution)/shard_map/ppermute | solution.py:384
  13.3 6.3 %collective-permute-start = (bf16[4,80,128]{2,1,0:T(8,128)(2,1)S(1)}, bf16[4,80,128]{2,1,0:T(8,128)(2,1)S(1)}, u32[]{:S(2)}, u32[]{:S(2)}) collective-permute-start(bf16[4,80,128]{2,1,0:T(8,128)(2,1)S(1)} %get-tuple-element.38), channel_id=1, source_target_pairs={{0,1},{1,0},{2,3},{3,2},{4,5},{5,4},{6,7},{7,6},{8,9},{9,8},{10,11... | collective-permute-start | bytes 245768 | tf_op jit(solution)/shard_map/ppermute | solution.py:381
  16.5 5.5 %collective-permute-start.1 = (bf16[4,80,128]{2,1,0:T(8,128)(2,1)S(1)}, bf16[4,80,128]{2,1,0:T(8,128)(2,1)S(1)}, u32[]{:S(2)}, u32[]{:S(2)}) collective-permute-start(bf16[4,80,128]{2,1,0:T(8,128)(2,1)S(1)} %get-tuple-element.39), channel_id=1, source_target_pairs={{0,2},{1,3},{2,0},{3,1},{4,6},{5,7},{6,4},{7,5},{8,10},{9,11},{10,... | collective-permute-start | bytes 245768 | tf_op jit(solution)/shard_map/ppermute | solution.py:381
  17.9 5.3 %collective-permute-start.2 = (bf16[4,80,128]{2,1,0:T(8,128)(2,1)S(1)}, bf16[4,80,128]{2,1,0:T(8,128)(2,1)S(1)}, u32[]{:S(2)}, u32[]{:S(2)}) collective-permute-start(bf16[4,80,128]{2,1,0:T(8,128)(2,1)S(1)} %get-tuple-element.40), channel_id=1, source_target_pairs={{0,3},{1,2},{2,1},{3,0},{4,7},{5,6},{6,5},{7,4},{8,11},{9,10},{10,... | collective-permute-start | bytes 245768 | tf_op jit(solution)/shard_map/ppermute | solution.py:381
  23.8 5.9 %collective-permute-start.5 = (bf16[4,80,128]{2,1,0:T(8,128)(2,1)S(1)}, bf16[4,80,128]{2,1,0:T(8,128)(2,1)S(1)}, u32[]{:S(2)}, u32[]{:S(2)}) collective-permute-start(bf16[4,80,128]{2,1,0:T(8,128)(2,1)S(1)} %get-tuple-element.41.refs_0_), channel_id=1, source_target_pairs={{0,3},{1,2},{2,1},{3,0},{4,7},{5,6},{6,5},{7,4},{8,11},{9,10},{10,... | collective-permute-start | bytes 245768 | tf_op jit(solution)/shard_map/ppermute | solution.py:381
  24.6 5.3 %collective-permute-start.4 = (bf16[4,80,128]{2,1,0:T(8,128)(2,1)S(1)}, bf16[4,80,128]{2,1,0:T(8,128)(2,1)S(1)}, u32[]{:S(2)}, u32[]{:S(2)}) collective-permute-start(bf16[4,80,128]{2,1,0:T(8,128)(2,1)S(1)} %get-tuple-element.41.refs_0_), channel_id=1, source_target_pairs={{0,2},{1,3},{2,0},{3,1},{4,6},{5,7},{6,4},{7,5},{8,10},{9,11},{10,... | collective-permute-start | bytes 245768 | tf_op jit(solution)/shard_map/ppermute | solution.py:381
  25.6 4.6 %collective-permute-start.3 = (bf16[4,80,128]{2,1,0:T(8,128)(2,1)S(1)}, bf16[4,80,128]{2,1,0:T(8,128)(2,1)S(1)}, u32[]{:S(2)}, u32[]{:S(2)}) collective-permute-start(bf16[4,80,128]{2,1,0:T(8,128)(2,1)S(1)} %get-tuple-element.41.refs_0_), channel_id=1, source_target_pairs={{0,1},{1,0},{2,3},{3,2},{4,5},{5,4},{6,7},{7,6},{8,9},{9,8},{10,11... | collective-permute-start | bytes 245768 | tf_op jit(solution)/shard_map/ppermute | solution.py:381
  27.3 3.2 %collective-permute-start.6 = (bf16[4,80,128]{2,1,0:T(8,128)(2,1)S(1)}, bf16[4,80,128]{2,1,0:T(8,128)(2,1)S(1)}, u32[]{:S(2)}, u32[]{:S(2)}) collective-permute-start(bf16[4,80,128]{2,1,0:T(8,128)(2,1)S(1)} %get-tuple-element.41.refs_0_), channel_id=1, source_target_pairs={{0,4},{4,0},{8,12},{12,8},{16,20},{20,16},{24,28},{28,24},{1,5},{5... | collective-permute-start | bytes 245768 | tf_op jit(solution)/shard_map/ppermute | solution.py:384
  32.5 9.3 %collective-permute-start.11 = (bf16[4,80,256]{2,1,0:T(8,128)(2,1)S(1)}, bf16[4,80,256]{2,1,0:T(8,128)(2,1)S(1)}, u32[]{:S(2)}, u32[]{:S(2)}) collective-permute-start(bf16[4,80,256]{2,1,0:T(8,128)(2,1)S(1)} %get-tuple-element.45), channel_id=1, source_target_pairs={{0,8},{4,12},{8,0},{12,4},{16,24},{20,28},{24,16},{28,20},{1,9},{5... | collective-permute-start | bytes 491528 | tf_op jit(solution)/shard_map/ppermute | solution.py:378
  34.4 15.0 %collective-permute-start.12 = (bf16[4,80,256]{2,1,0:T(8,128)(2,1)S(1)}, bf16[4,80,256]{2,1,0:T(8,128)(2,1)S(1)}, u32[]{:S(2)}, u32[]{:S(2)}) collective-permute-start(bf16[4,80,256]{2,1,0:T(8,128)(2,1)S(1)} %get-tuple-element.46), channel_id=1, source_target_pairs={{0,16},{4,20},{8,24},{12,28},{16,0},{20,4},{24,8},{28,12},{1,17},{... | collective-permute-start | bytes 491528 | tf_op jit(solution)/shard_map/ppermute | solution.py:378
  37.0 12.4 %collective-permute-start.13 = (bf16[4,80,256]{2,1,0:T(8,128)(2,1)S(1)}, bf16[4,80,256]{2,1,0:T(8,128)(2,1)S(1)}, u32[]{:S(2)}, u32[]{:S(2)}) collective-permute-start(bf16[4,80,256]{2,1,0:T(8,128)(2,1)S(1)} %get-tuple-element.47), channel_id=1, source_target_pairs={{0,24},{4,28},{8,16},{12,20},{16,8},{20,12},{24,0},{28,4},{1,25},{... | collective-permute-start | bytes 491528 | tf_op jit(solution)/shard_map/ppermute | solution.py:378
  49.6 7.8 %collective-permute-start.16 = (bf16[4,80,256]{2,1,0:T(8,128)(2,1)S(1)}, bf16[4,80,256]{2,1,0:T(8,128)(2,1)S(1)}, u32[]{:S(2)}, u32[]{:S(2)}) collective-permute-start(bf16[4,80,256]{2,1,0:T(8,128)(2,1)S(1)} %get-tuple-element.48.refs_0_), channel_id=1, source_target_pairs={{0,24},{4,28},{8,16},{12,20},{16,8},{20,12},{24,0},{28,4},{1,25},{... | collective-permute-start | bytes 491528 | tf_op jit(solution)/shard_map/ppermute | solution.py:378
  51.8 14.6 %collective-permute-start.15 = (bf16[4,80,256]{2,1,0:T(8,128)(2,1)S(1)}, bf16[4,80,256]{2,1,0:T(8,128)(2,1)S(1)}, u32[]{:S(2)}, u32[]{:S(2)}) collective-permute-start(bf16[4,80,256]{2,1,0:T(8,128)(2,1)S(1)} %get-tuple-element.48.refs_0_), channel_id=1, source_target_pairs={{0,16},{4,20},{8,24},{12,28},{16,0},{20,4},{24,8},{28,12},{1,17},{... | collective-permute-start | bytes 491528 | tf_op jit(solution)/shard_map/ppermute | solution.py:378
  54.1 12.3 %collective-permute-start.14 = (bf16[4,80,256]{2,1,0:T(8,128)(2,1)S(1)}, bf16[4,80,256]{2,1,0:T(8,128)(2,1)S(1)}, u32[]{:S(2)}, u32[]{:S(2)}) collective-permute-start(bf16[4,80,256]{2,1,0:T(8,128)(2,1)S(1)} %get-tuple-element.48.refs_0_), channel_id=1, source_target_pairs={{0,8},{4,12},{8,0},{12,4},{16,24},{20,28},{24,16},{28,20},{1,9},{5... | collective-permute-start | bytes 491528 | tf_op jit(solution)/shard_map/ppermute | solution.py:378
  67.0 1.7 %collective-permute-start.17 = (bf16[4,4,80,128]{3,2,1,0:T(8,128)(2,1)S(1)}, bf16[4,4,80,128]{3,2,1,0:T(8,128)(2,1)S(1)}, u32[]{:S(2)}, u32[]{:S(2)}) collective-permute-start(bf16[4,4,80,128]{3,2,1,0:T(8,128)(2,1)S(1)} %shard_map.109), channel_id=1, source_target_pairs={{0,4},{4,0},{8,12},{12,8},{16,20},{20,16},{24,28},{28,24},{1,5},{5... | collective-permute-start | bytes 983048 | tf_op jit(solution)/shard_map/ppermute | solution.py:384
  69.3 4.5 %collective-permute-start.18 = (bf16[4,80,128]{2,1,0:T(8,128)(2,1)S(1)}, bf16[4,80,128]{2,1,0:T(8,128)(2,1)S(1)}, u32[]{:S(2)}, u32[]{:S(2)}) collective-permute-start(bf16[4,80,128]{2,1,0:T(8,128)(2,1)S(1)} %get-tuple-element.50), channel_id=1, source_target_pairs={{0,1},{1,0},{2,3},{3,2},{4,5},{5,4},{6,7},{7,6},{8,9},{9,8},{10,11... | collective-permute-start | bytes 245768 | tf_op jit(solution)/shard_map/ppermute | solution.py:381
  70.5 6.2 %collective-permute-start.19 = (bf16[4,80,128]{2,1,0:T(8,128)(2,1)S(1)}, bf16[4,80,128]{2,1,0:T(8,128)(2,1)S(1)}, u32[]{:S(2)}, u32[]{:S(2)}) collective-permute-start(bf16[4,80,128]{2,1,0:T(8,128)(2,1)S(1)} %get-tuple-element.51), channel_id=1, source_target_pairs={{0,2},{1,3},{2,0},{3,1},{4,6},{5,7},{6,4},{7,5},{8,10},{9,11},{10,... | collective-permute-start | bytes 245768 | tf_op jit(solution)/shard_map/ppermute | solution.py:381
  71.2 5.6 %collective-permute-start.20 = (bf16[4,80,128]{2,1,0:T(8,128)(2,1)S(1)}, bf16[4,80,128]{2,1,0:T(8,128)(2,1)S(1)}, u32[]{:S(2)}, u32[]{:S(2)}) collective-permute-start(bf16[4,80,128]{2,1,0:T(8,128)(2,1)S(1)} %get-tuple-element.52), channel_id=1, source_target_pairs={{0,3},{1,2},{2,1},{3,0},{4,7},{5,6},{6,5},{7,4},{8,11},{9,10},{10,... | collective-permute-start | bytes 245768 | tf_op jit(solution)/shard_map/ppermute | solution.py:381
  77.3 5.4 %collective-permute-start.23 = (bf16[4,80,128]{2,1,0:T(8,128)(2,1)S(1)}, bf16[4,80,128]{2,1,0:T(8,128)(2,1)S(1)}, u32[]{:S(2)}, u32[]{:S(2)}) collective-permute-start(bf16[4,80,128]{2,1,0:T(8,128)(2,1)S(1)} %get-tuple-element.55.refs_0_), channel_id=1, source_target_pairs={{0,3},{1,2},{2,1},{3,0},{4,7},{5,6},{6,5},{7,4},{8,11},{9,10},{10,... | collective-permute-start | bytes 245768 | tf_op jit(solution)/shard_map/ppermute | solution.py:381
  78.9 4.8 %collective-permute-start.22 = (bf16[4,80,128]{2,1,0:T(8,128)(2,1)S(1)}, bf16[4,80,128]{2,1,0:T(8,128)(2,1)S(1)}, u32[]{:S(2)}, u32[]{:S(2)}) collective-permute-start(bf16[4,80,128]{2,1,0:T(8,128)(2,1)S(1)} %get-tuple-element.55.refs_0_), channel_id=1, source_target_pairs={{0,2},{1,3},{2,0},{3,1},{4,6},{5,7},{6,4},{7,5},{8,10},{9,11},{10,... | collective-permute-start | bytes 245768 | tf_op jit(solution)/shard_map/ppermute | solution.py:381
  79.8 4.4 %collective-permute-start.21 = (bf16[4,80,128]{2,1,0:T(8,128)(2,1)S(1)}, bf16[4,80,128]{2,1,0:T(8,128)(2,1)S(1)}, u32[]{:S(2)}, u32[]{:S(2)}) collective-permute-start(bf16[4,80,128]{2,1,0:T(8,128)(2,1)S(1)} %get-tuple-element.55.refs_0_), channel_id=1, source_target_pairs={{0,1},{1,0},{2,3},{3,2},{4,5},{5,4},{6,7},{7,6},{8,9},{9,8},{10,11... | collective-permute-start | bytes 245768 | tf_op jit(solution)/shard_map/ppermute | solution.py:381
  80.9 3.3 %collective-permute-start.24 = (bf16[4,80,128]{2,1,0:T(8,128)(2,1)S(1)}, bf16[4,80,128]{2,1,0:T(8,128)(2,1)S(1)}, u32[]{:S(2)}, u32[]{:S(2)}) collective-permute-start(bf16[4,80,128]{2,1,0:T(8,128)(2,1)S(1)} %get-tuple-element.55.refs_0_), channel_id=1, source_target_pairs={{0,4},{4,0},{8,12},{12,8},{16,20},{20,16},{24,28},{28,24},{1,5},{5... | collective-permute-start | bytes 245768 | tf_op jit(solution)/shard_map/ppermute | solution.py:384
  86.5 9.3 %collective-permute-start.28 = (bf16[4,80,256]{2,1,0:T(8,128)(2,1)S(1)}, bf16[4,80,256]{2,1,0:T(8,128)(2,1)S(1)}, u32[]{:S(2)}, u32[]{:S(2)}) collective-permute-start(bf16[4,80,256]{2,1,0:T(8,128)(2,1)S(1)} %get-tuple-element.57), channel_id=1, source_target_pairs={{0,8},{4,12},{8,0},{12,4},{16,24},{20,28},{24,16},{28,20},{1,9},{5... | collective-permute-start | bytes 491528 | tf_op jit(solution)/shard_map/ppermute | solution.py:378
  86.6 15.1 %collective-permute-start.29 = (bf16[4,80,256]{2,1,0:T(8,128)(2,1)S(1)}, bf16[4,80,256]{2,1,0:T(8,128)(2,1)S(1)}, u32[]{:S(2)}, u32[]{:S(2)}) collective-permute-start(bf16[4,80,256]{2,1,0:T(8,128)(2,1)S(1)} %get-tuple-element.58), channel_id=1, source_target_pairs={{0,16},{4,20},{8,24},{12,28},{16,0},{20,4},{24,8},{28,12},{1,17},{... | collective-permute-start | bytes 491528 | tf_op jit(solution)/shard_map/ppermute | solution.py:378
  89.6 12.1 %collective-permute-start.30 = (bf16[4,80,256]{2,1,0:T(8,128)(2,1)S(1)}, bf16[4,80,256]{2,1,0:T(8,128)(2,1)S(1)}, u32[]{:S(2)}, u32[]{:S(2)}) collective-permute-start(bf16[4,80,256]{2,1,0:T(8,128)(2,1)S(1)} %get-tuple-element.59), channel_id=1, source_target_pairs={{0,24},{4,28},{8,16},{12,20},{16,8},{20,12},{24,0},{28,4},{1,25},{... | collective-permute-start | bytes 491528 | tf_op jit(solution)/shard_map/ppermute | solution.py:378
  102.6 7.6 %collective-permute-start.33 = (bf16[4,80,256]{2,1,0:T(8,128)(2,1)S(1)}, bf16[4,80,256]{2,1,0:T(8,128)(2,1)S(1)}, u32[]{:S(2)}, u32[]{:S(2)}) collective-permute-start(bf16[4,80,256]{2,1,0:T(8,128)(2,1)S(1)} %get-tuple-element.61.refs_0_), channel_id=1, source_target_pairs={{0,24},{4,28},{8,16},{12,20},{16,8},{20,12},{24,0},{28,4},{1,25},{... | collective-permute-start | bytes 491528 | tf_op jit(solution)/shard_map/ppermute | solution.py:378
  105.0 14.6 %collective-permute-start.32 = (bf16[4,80,256]{2,1,0:T(8,128)(2,1)S(1)}, bf16[4,80,256]{2,1,0:T(8,128)(2,1)S(1)}, u32[]{:S(2)}, u32[]{:S(2)}) collective-permute-start(bf16[4,80,256]{2,1,0:T(8,128)(2,1)S(1)} %get-tuple-element.61.refs_0_), channel_id=1, source_target_pairs={{0,16},{4,20},{8,24},{12,28},{16,0},{20,4},{24,8},{28,12},{1,17},{... | collective-permute-start | bytes 491528 | tf_op jit(solution)/shard_map/ppermute | solution.py:378
  107.4 12.2 %collective-permute-start.31 = (bf16[4,80,256]{2,1,0:T(8,128)(2,1)S(1)}, bf16[4,80,256]{2,1,0:T(8,128)(2,1)S(1)}, u32[]{:S(2)}, u32[]{:S(2)}) collective-permute-start(bf16[4,80,256]{2,1,0:T(8,128)(2,1)S(1)} %get-tuple-element.61.refs_0_), channel_id=1, source_target_pairs={{0,8},{4,12},{8,0},{12,4},{16,24},{20,28},{24,16},{28,20},{1,9},{5... | collective-permute-start | bytes 491528 | tf_op jit(solution)/shard_map/ppermute | solution.py:378
  120.1 1.7 %collective-permute-start.34 = (bf16[4,4,80,128]{3,2,1,0:T(8,128)(2,1)S(1)}, bf16[4,4,80,128]{3,2,1,0:T(8,128)(2,1)S(1)}, u32[]{:S(2)}, u32[]{:S(2)}) collective-permute-start(bf16[4,4,80,128]{3,2,1,0:T(8,128)(2,1)S(1)} %shard_map.114), channel_id=1, source_target_pairs={{0,4},{4,0},{8,12},{12,8},{16,20},{20,16},{24,28},{28,24},{1,5},{5... | collective-permute-start | bytes 983048 | tf_op jit(solution)/shard_map/ppermute | solution.py:384
  122.5 4.5 %collective-permute-start.35 = (bf16[4,80,128]{2,1,0:T(8,128)(2,1)S(1)}, bf16[4,80,128]{2,1,0:T(8,128)(2,1)S(1)}, u32[]{:S(2)}, u32[]{:S(2)}) collective-permute-start(bf16[4,80,128]{2,1,0:T(8,128)(2,1)S(1)} %get-tuple-element.63), channel_id=1, source_target_pairs={{0,1},{1,0},{2,3},{3,2},{4,5},{5,4},{6,7},{7,6},{8,9},{9,8},{10,11... | collective-permute-start | bytes 245768 | tf_op jit(solution)/shard_map/ppermute | solution.py:381
  123.6 5.3 %collective-permute-start.36 = (bf16[4,80,128]{2,1,0:T(8,128)(2,1)S(1)}, bf16[4,80,128]{2,1,0:T(8,128)(2,1)S(1)}, u32[]{:S(2)}, u32[]{:S(2)}) collective-permute-start(bf16[4,80,128]{2,1,0:T(8,128)(2,1)S(1)} %get-tuple-element.64), channel_id=1, source_target_pairs={{0,2},{1,3},{2,0},{3,1},{4,6},{5,7},{6,4},{7,5},{8,10},{9,11},{10,... | collective-permute-start | bytes 245768 | tf_op jit(solution)/shard_map/ppermute | solution.py:381
  124.8 5.3 %collective-permute-start.37 = (bf16[4,80,128]{2,1,0:T(8,128)(2,1)S(1)}, bf16[4,80,128]{2,1,0:T(8,128)(2,1)S(1)}, u32[]{:S(2)}, u32[]{:S(2)}) collective-permute-start(bf16[4,80,128]{2,1,0:T(8,128)(2,1)S(1)} %get-tuple-element.65), channel_id=1, source_target_pairs={{0,3},{1,2},{2,1},{3,0},{4,7},{5,6},{6,5},{7,4},{8,11},{9,10},{10,... | collective-permute-start | bytes 245768 | tf_op jit(solution)/shard_map/ppermute | solution.py:381
  (15 other events, 71.3 us)

commit v3 on v2

--- a/solution.py
+++ b/solution.py
@@ -9,29 +9,29 @@
 
 ITERS = 2
 GROUPS = 1
-PLANE_SUM = "permute"
-PLANE_GATHER = "permute"
-LINE_SUM = "permute"
+PLANE_SUM = "whole"
+PLANE_GATHER = "whole"
+LINE_SUM = "whole"
 LINE_GATHER = "permute"
 LANES = 128
 PIECES = 3
 PRIME = 32749
 VMEM = pl.BlockSpec(memory_space=pltpu.VMEM)
-SMEM = pl.BlockSpec(memory_space=pltpu.SMEM)
+HBM = pl.BlockSpec(memory_space=pltpu.HBM)
 F32 = jnp.float32
 BF16 = jnp.bfloat16
 NT = (((1,), (1,)), ((), ()))
 
 
-def call(kernel, outs, scratch, flops, *args, scalars=0):
+def call(kernel, outs, scratch, flops, *args, space=VMEM, limit=40):
     nbytes = sum(a.size * a.dtype.itemsize for a in (*args, *outs))
     return pl.pallas_call(
         kernel,
         out_shape=outs,
-        in_specs=[SMEM] * scalars + [VMEM] * (len(args) - scalars),
+        in_specs=[space] * len(args),
         out_specs=[VMEM] * len(outs),
         scratch_shapes=scratch,
-        compiler_params=pltpu.CompilerParams(vmem_limit_bytes=40 * 1024 * 1024),
+        compiler_params=pltpu.CompilerParams(vmem_limit_bytes=limit * 1024 * 1024),
         cost_estimate=pl.CostEstimate(flops=flops, bytes_accessed=nbytes, transcendentals=0),
     )(*args)
 
@@ -86,53 +86,61 @@
     return x - (x.astype(F32) * factor).astype(jnp.int32) * PRIME
 
 
-def start_kernel(dims, seeds, ids, cols, count, innov, prec, h, own, partner, *rest):
+def start_kernel(dims, seeds_in, ids_in, cols_in, count_in, innov_in, prec_in, h, own, partner, *rest):
     chips, n_obs, halves, groups = dims
-    outs, (scratch, acc) = rest[:-2], rest[-2:]
+    outs = rest[:-11]
+    seeds, ids, cols, count, innov, prec, hashed, scratch, acc, sems, h_sems = rest[-11:]
     z, core, obs = place()
-    lev, blocks, profiles = innov.shape
+    blocks, lev, profiles = innov.shape
     colblocks, width = own.shape[1], own.shape[3]
-    members = seeds.shape[0]
-    levp = scratch.shape[2] // blocks
-    strips = profiles // LANES
-
+    members, levp = scratch.shape[0], scratch.shape[1]
+
+    pairs = [(seeds_in, seeds), (ids_in, ids), (cols_in, cols), (count_in, count)]
+    small = [pltpu.make_async_copy(x, y, sems.at[i]) for i, (x, y) in enumerate(pairs)]
+    for copy in small:
+        copy.start()
+    large = []
+    for b in range(blocks):
+        at = len(pairs) + 2 * b
+        large.append(pltpu.make_async_copy(innov_in.at[:, b, :], innov.at[b], sems.at[at]))
+        large.append(pltpu.make_async_copy(prec_in.at[:, b, :], prec.at[b], sems.at[at + 1]))
+    for copy in large:
+        copy.start()
     own[...] = jnp.zeros_like(own)
     partner[...] = jnp.zeros_like(partner)
+    scratch[...] = jnp.zeros_like(scratch)
+    for copy in small:
+        copy.wait()
+
+    def tile_copy(n, half, target):
+        lanes = pl.ds(half * width, width)
+        return pltpu.make_async_copy(h.at[n, :, lanes], target, h_sems.at[n * halves + half])
 
     def put(n, carry):
-        b, k = ids[n], cols[n]
         for half in range(halves):
-            piece = b * halves + half
-            tile = h[n, :, half * width : (half + 1) * width]
+            piece, k = ids[0, 0, n] * halves + half, cols[0, 0, n]
 
             @pl.when(piece % 2 == core)
             def _():
-                own[piece // 2, k] = tile
+                tile_copy(n, half, own.at[piece // 2, k]).start()
 
             @pl.when(piece % 2 != core)
             def _():
-                partner[piece // 2, k] = tile
+                tile_copy(n, half, partner.at[piece // 2, k]).start()
 
         return carry
 
-    lax.fori_loop(0, count[0], put, 0)
-
-    scratch[:, :, lev * blocks :, :] = jnp.zeros(
-        (members, strips, (levp - lev) * blocks, LANES), F32
-    )
-    shape = (blocks, profiles)
-    spot = (
-        lax.broadcasted_iota(jnp.int32, shape, 0) + obs * blocks
-    ) * (lev * profiles) + lax.broadcasted_iota(jnp.int32, shape, 1)
+    lax.fori_loop(0, count[0, 0], put, 0)
+
     starts = [lax.rem(seeds[m], PRIME) for m in range(members)]
-
-    def draw(level, carry):
-        base = remainder(7919 * remainder(spot + level * profiles, 1.0 / PRIME), 1.0 / PRIME)
-        p = prec[level]
-        gain = 3.4 * p * lax.rsqrt(p)
-        offset = p * innov[level] - 0.5 * gain
-        gain = gain * (1.0 / PRIME)
-        at = pl.multiple_of(level * blocks, blocks)
+    order = [(source, zz) for source in range(2) for zz in range(chips)]
+    shape = (levp, width)
+    spot = lax.broadcasted_iota(jnp.int32, shape, 0) * profiles
+    spot = spot + lax.broadcasted_iota(jnp.int32, shape, 1)
+    for at, (source, zz) in enumerate(order):
+        piece = 2 * zz + (core if source == 0 else 1 - core)
+        first = (obs * blocks + piece // halves) * (lev * profiles) + (piece % halves) * width
+        base = remainder(7919 * remainder(spot + first, 1.0 / PRIME), 1.0 / PRIME)
         for m in range(members):
             k0 = base + starts[m]
             k0 = jnp.where(k0 >= PRIME, k0 - PRIME, k0)
@@ -140,31 +148,37 @@
             k2 = remainder(k1 * k1 + 2719, 1.0 / PRIME)
             k2 = jnp.where(k2 < 0, k2 + PRIME, k2)
             k2 = jnp.where(k2 >= PRIME, k2 - PRIME, k2)
-            w = offset + gain * k2.astype(F32)
-            for t in range(strips):
-                scratch[m, t, pl.ds(at, blocks), :] = w[:, t * LANES : (t + 1) * LANES]
+            hashed[at, m] = k2.astype(F32)
+
+    for copy in large:
+        copy.wait()
+
+    def arrive(n, carry):
+        for half in range(halves):
+            tile_copy(n, half, own.at[0, 0]).wait()
         return carry
 
-    lax.fori_loop(0, lev, draw, 0, unroll=3)
-
-    for source in range(2):
-        for zz in range(chips):
-            piece = 2 * zz + (core if source == 0 else 1 - core)
-            rows = pl.ds(piece // halves, levp, stride=blocks)
-            strip = (piece % halves) * (width // LANES)
-            w = [
-                jnp.concatenate(
-                    [scratch[m, strip + t, rows, :].astype(BF16) for t in range(width // LANES)],
-                    axis=1,
-                )
-                for m in range(members)
-            ]
-            w = jnp.concatenate(w, axis=0)
-            tiles = (own if source == 0 else partner)[zz].reshape(colblocks * LANES, width)
-            part = lax.dot_general(w, tiles, NT, preferred_element_type=F32)
-            for k in range(colblocks):
-                piece_k = part[:, k * LANES : (k + 1) * LANES]
-                acc[k] = piece_k if source + zz == 0 else acc[k] + piece_k
+    lax.fori_loop(0, count[0, 0], arrive, 0)
+
+    for at, (source, zz) in enumerate(order):
+        piece = 2 * zz + (core if source == 0 else 1 - core)
+        b = piece // halves
+        if halves == 1:
+            p, d = prec[b], innov[b]
+        else:
+            lanes = pl.ds(pl.multiple_of((piece % halves) * width, LANES), width)
+            p, d = prec[b, :, lanes], innov[b, :, lanes]
+        gain = 3.4 * p * lax.rsqrt(p)
+        offset = p * d - 0.5 * gain
+        gain = gain * (1.0 / PRIME)
+        for m in range(members):
+            scratch[m, 0:lev, :] = offset + gain * hashed[at, m, 0:lev, :]
+        w = scratch[...].astype(BF16).reshape(members * levp, width)
+        tiles = (own if source == 0 else partner)[zz].reshape(colblocks * LANES, width)
+        part = lax.dot_general(w, tiles, NT, preferred_element_type=F32)
+        for k in range(colblocks):
+            piece_k = part[:, k * LANES : (k + 1) * LANES]
+            acc[k] = piece_k if at == 0 else acc[k] + piece_k
 
     share = members // groups
     for g in range(groups):
@@ -403,18 +417,28 @@
         functools.partial(start_kernel, (chips, n_obs, halves, groups)),
         [dense, dense] + [x for x in partial_shapes for g in range(groups)],
         [
-            pltpu.VMEM((members, profiles // LANES, levp * blocks, LANES), F32),
+            pltpu.SMEM(seeds.shape, jnp.int32),
+            pltpu.SMEM(block_obs.shape, jnp.int32),
+            pltpu.SMEM(block_col.shape, jnp.int32),
+            pltpu.SMEM(entry_count.shape, jnp.int32),
+            pltpu.VMEM((blocks, lev, profiles), F32),
+            pltpu.VMEM((blocks, lev, profiles), F32),
+            pltpu.VMEM((n_slab, members, levp, width), F32),
+            pltpu.VMEM((members, levp, width), F32),
             pltpu.VMEM((colblocks, members * levp, LANES), F32),
+            pltpu.SemaphoreType.DMA((4 + 2 * blocks,)),
+            pltpu.SemaphoreType.DMA((h_block.shape[0] * halves,)),
         ],
         2 * product * groups,
         seeds,
-        block_obs.reshape(-1),
-        block_col.reshape(-1),
-        entry_count.reshape(-1),
+        block_obs,
+        block_col,
+        entry_count,
         innovation,
         obs_precision,
         h_block,
-        scalars=4,
+        space=HBM,
+        limit=60,
     )
     arrived = [spread(PLANE_SUM, partials[g::groups], plane) for g in range(groups)]
     partner = swap(for_partner)

time: 132 us -> 146 us (1.11)
  blocking collectives: 0 us -> 57.7 us
  waiting for transfers between devices: 71.8 us -> 51.2 us
  starting transfers between devices: 38.4 us -> 19 us
  local copies, waits for them, and re-layouts: 5.82 us -> 0.78 us
    all_to_all x0 -> x5, blocking collectives: none -> 57.7 us  [the longest x4 36.7 us: spread(): return [lax.all_to_all(outs[0], 'obs', 0, 0, tiled=True)]]
    ppermute x12 -> x6, waiting for transfers between devices: 47.3 us -> 20.8 us  [along(): return lax.ppermute(x, 'slab', [(s, s ^ 2 * i) for s in range(n_slab)])]
    all_to_all x0 -> x2, waiting for transfers between devices: none -> 24 us  [the longest x1 17.4 us: spread(): lax.all_to_all(outs[0], 'slab', 0, 0, axis_index_groups=cores, tiled=True)]
    ppermute x15 -> x0, waiting for transfers between devices: 19 us -> none  [plane(): return lax.ppermute(x, 'obs', [(o, o ^ i) for o in range(n_obs)])]
    ppermute x15 -> x0, starting transfers between devices: 18.9 us -> none  [plane(): return lax.ppermute(x, 'obs', [(o, o ^ i) for o in range(n_obs)])]
    ppermute x12 -> x6, starting transfers between devices: 18.4 us -> 8.84 us  [along(): return lax.ppermute(x, 'slab', [(s, s ^ 2 * i) for s in range(n_slab)])]
    all_to_all x0 -> x2, starting transfers between devices: none -> 8.99 us  [the longest x1 4.65 us: spread(): lax.all_to_all(outs[0], 'slab', 0, 0, axis_index_groups=cores, tiled=True)]
    unnamed x19 -> x13, local copies, waits for them, and re-layouts: 5.8 us -> 0.76 us
  transfers between devices with their start and end apart: 38 -> 13, of which waited for: 28 -> 10; matrix products, arithmetic and copies ran while one was open for 0% -> 0% of each run, Pallas kernels for 1% -> 1%
where the time goes in v3:
time: 146 us; the launch traced here: 145 us
  blocking collectives  57.7 us (40%)
  waiting for transfers between devices  51.2 us (35%)
  starting transfers between devices  19 us (13%)
  Pallas kernels  14.9 us (10%)
    all_to_all x4, blocking collectives, spread(): return [lax.all_to_all(outs[0], 'obs', 0, 0, tiled=True)]  36.7 us
    all_to_all x1, blocking collectives, spread(): lax.all_to_all(outs[0], 'slab', 0, 0, axis_index_groups=cores, tiled=True)  21 us
    ppermute x6, waiting for transfers between devices, along(): return lax.ppermute(x, 'slab', [(s, s ^ 2 * i) for s in range(n_slab)])  20.8 us
    all_to_all x1, waiting for transfers between devices, spread(): lax.all_to_all(outs[0], 'slab', 0, 0, axis_index_groups=cores, tiled=True)  17.4 us
    pallas_call x13, Pallas kernels, call(): pl.pallas_call(kernel, out_shape=outs, in_specs=[space] * len(args), out_...  14.9 us
    ppermute x6, starting transfers between devices, along(): return lax.ppermute(x, 'slab', [(s, s ^ 2 * i) for s in range(n_slab)])  8.84 us
    all_to_all x1, waiting for transfers between devices, spread(): return [lax.all_to_all(outs[0], 'obs', 0, 0, tiled=True)]  6.59 us
    ppermute x5, waiting for transfers between devices, swap(): return lax.ppermute(x, 'slab', [(s, s ^ 1) for s in range(n_slab)])  6.47 us
  transfers between devices with their start and end apart: 13, of which 10 were waited for; matrix products, arithmetic and copies ran while one was open for 0% of the time, Pallas kernels for 1%

profile of v3, /device:TPU:0, one launch (start us, length us, event | category | flops | bytes accessed | tf_op | source)
XLA Modules:
  0.0 145.1 jit_solution(2618140249744041457)
XLA Ops:
  1.3 5.8 %shard_map.104 = (bf16[4,4,128,256]{3,2,1,0:T(8,128)(2,1)}, bf16[4,4,128,256]{3,2,1,0:T(8,128)(2,1)}, bf16[4,4,80,128]{3,2,1,0:T(8,128)(2,1)}) custom-call(s32[4]{0:T(128)} %seeds_in.1, s32[1,1,32]{2,1,0:T(1,128)} %ids_in.1, s32[1,1,32]{2,1,0:T(1,128)} %cols_in.1, s32[1,1]{1,0:T(1,128)S(6)} %copy.12.count_in, f32[75,8,256]{2,1,0:T(8,128)} %bitcast.13, ...), custom_call_target="tpu_custom_call" | custom-call | flops 671088640 | bytes 5751060 | tf_op jit(solution)/shard_map/pallas_call | solution.py:28
  7.1 1.0 collective-permute-start.1
  8.2 4.3 %all-to-all-start = ((bf16[4,4,80,128]{3,2,1,0:T(8,128)(2,1)}), bf16[4,4,80,128]{3,2,1,0:T(8,128)(2,1)S(1)}, u32[]{:S(2)}, u32[]{:S(2)}) async-start(bf16[4,4,80,128]{3,2,1,0:T(8,128)(2,1)} %get-tuple-element.18), calls=%async_computation | async-start | bytes 655360 | tf_op jit(solution)/shard_map/all_to_all | solution.py:404
  12.6 6.6 %all-to-all-done.refs_0_ = bf16[4,4,80,128]{3,2,1,0:T(8,128)(2,1)S(1)} async-done(((bf16[4,4,80,128]{3,2,1,0:T(8,128)(2,1)}), bf16[4,4,80,128]{3,2,1,0:T(8,128)(2,1)S(1)}, u32[]{:S(2)}, u32[]{:S(2)}) %all-to-all-start) | async-done | bytes 327712 | tf_op jit(solution)/shard_map/all_to_all | solution.py:404
  19.2 0.6 shard_map.105
  19.8 0.6 copy-done.2
  20.5 9.0 %all_to_all.35.refs_0_ = bf16[4,4,80,128]{3,2,1,0:T(8,128)(2,1)S(1)} all-to-all(bf16[4,4,80,128]{3,2,1,0:T(8,128)(2,1)S(1)} %get-tuple-element.19), channel_id=1, replica_groups=mesh['slab'=8,'obs'=4] {'obs'}, dimensions={0} | all-to-all | bytes 655360 | tf_op jit(solution)/shard_map/all_to_all | solution.py:404
  29.4 1.6 %collective-permute-done.refs_1_ = bf16[4,4,80,128]{3,2,1,0:T(8,128)(2,1)S(1)} collective-permute-done((bf16[4,4,80,128]{3,2,1,0:T(8,128)(2,1)S(1)}, bf16[4,4,80,128]{3,2,1,0:T(8,128)(2,1)S(1)}, u32[]{:S(2)}, u32[]{:S(2)}) %collective-permute-start) | collective-permute-done | bytes 327712 | tf_op jit(solution)/shard_map/ppermute | solution.py:398
  31.0 1.9 %shard_map.106 = bf16[4,4,80,256]{3,2,1,0:T(8,128)(2,1)} custom-call(bf16[4,4,80,128]{3,2,1,0:T(8,128)(2,1)S(1)} %all_to_all.35.refs_0_, bf16[4,4,80,128]{3,2,1,0:T(8,128)(2,1)S(1)} %collective-permute-done.refs_1_, bf16[4,4,128,256]{3,2,1,0:T(8,128)(2,1)S(1)} %copy-done, bf16[4,4,128,256]{3,2,1,0:T(8,128)(2,1)S(1)} %collective-permute-done.1.refs_3_.refs_4_), custom_call_target="tpu_custom_call" | custom-call | flops 671088640 | bytes 3407872 | tf_op jit(solution)/shard_map/pallas_call | solution.py:28
  33.0 4.7 %all-to-all-start.2 = ((bf16[4,4,80,256]{3,2,1,0:T(8,128)(2,1)}), bf16[4,4,80,256]{3,2,1,0:T(8,128)(2,1)S(1)}, u32[]{:S(2)}, u32[]{:S(2)}) async-start(bf16[4,4,80,256]{3,2,1,0:T(8,128)(2,1)} %shard_map.106), calls=%async_computation.2 | async-start | bytes 1310720 | tf_op jit(solution)/shard_map/all_to_all | solution.py:405
  37.8 17.4 %all-to-all-done.2.refs_0_ = bf16[4,4,80,256]{3,2,1,0:T(8,128)(2,1)S(1)} async-done(((bf16[4,4,80,256]{3,2,1,0:T(8,128)(2,1)}), bf16[4,4,80,256]{3,2,1,0:T(8,128)(2,1)S(1)}, u32[]{:S(2)}, u32[]{:S(2)}) %all-to-all-start.2) | async-done | bytes 655392 | tf_op jit(solution)/shard_map/all_to_all | solution.py:405
  55.4 1.5 %collective-permute-start.4 = (bf16[4,80,256]{2,1,0:T(8,128)(2,1)S(1)}, bf16[4,80,256]{2,1,0:T(8,128)(2,1)S(1)}, u32[]{:S(2)}, u32[]{:S(2)}) collective-permute-start(bf16[4,80,256]{2,1,0:T(8,128)(2,1)S(1)} %get-tuple-element.22.refs_0_), channel_id=1, source_target_pairs={{0,24},{4,28},{8,16},{12,20},{16,8},{20,12},{24,0},{28,4},{1,25},{... | collective-permute-start | bytes 491528 | tf_op jit(solution)/shard_map/ppermute | solution.py:392
  57.0 2.9 %collective-permute-start.2 = (bf16[4,80,256]{2,1,0:T(8,128)(2,1)S(1)}, bf16[4,80,256]{2,1,0:T(8,128)(2,1)S(1)}, u32[]{:S(2)}, u32[]{:S(2)}) collective-permute-start(bf16[4,80,256]{2,1,0:T(8,128)(2,1)S(1)} %get-tuple-element.22.refs_0_), channel_id=1, source_target_pairs={{0,8},{4,12},{8,0},{12,4},{16,24},{20,28},{24,16},{28,20},{1,9},{5... | collective-permute-start | bytes 491528 | tf_op jit(solution)/shard_map/ppermute | solution.py:392
  59.9 4.6 %collective-permute-done.4.refs_3_ = bf16[4,80,256]{2,1,0:T(8,128)(2,1)S(1)} collective-permute-done((bf16[4,80,256]{2,1,0:T(8,128)(2,1)S(1)}, bf16[4,80,256]{2,1,0:T(8,128)(2,1)S(1)}, u32[]{:S(2)}, u32[]{:S(2)}) %collective-permute-start.4) | collective-permute-done | bytes 163872 | tf_op jit(solution)/shard_map/ppermute | solution.py:392
  64.5 5.1 %collective-permute-done.3.refs_2_ = bf16[4,80,256]{2,1,0:T(8,128)(2,1)S(1)} collective-permute-done((bf16[4,80,256]{2,1,0:T(8,128)(2,1)S(1)}, bf16[4,80,256]{2,1,0:T(8,128)(2,1)S(1)}, u32[]{:S(2)}, u32[]{:S(2)}) %collective-permute-start.3) | collective-permute-done | bytes 163872 | tf_op jit(solution)/shard_map/ppermute | solution.py:392
  70.2 1.6 %collective-permute-done.5.refs_5_ = bf16[4,4,80,128]{3,2,1,0:T(8,128)(2,1)S(1)} collective-permute-done((bf16[4,4,80,128]{3,2,1,0:T(8,128)(2,1)S(1)}, bf16[4,4,80,128]{3,2,1,0:T(8,128)(2,1)S(1)}, u32[]{:S(2)}, u32[]{:S(2)}) %collective-permute-start.5) | collective-permute-done | bytes 327712 | tf_op jit(solution)/shard_map/ppermute | solution.py:398
  71.8 0.6 shard_map.110
  72.4 9.5 %all_to_all.36.refs_0_ = bf16[4,4,80,128]{3,2,1,0:T(8,128)(2,1)S(1)} all-to-all(bf16[4,4,80,128]{3,2,1,0:T(8,128)(2,1)S(1)} %shard_map.110), channel_id=1, replica_groups=mesh['slab'=8,'obs'=4] {'obs'}, dimensions={0} | all-to-all | bytes 655360 | tf_op jit(solution)/shard_map/all_to_all | solution.py:404
  82.0 0.6 shard_map.111
  82.6 8.6 %all_to_all.37.refs_0_ = bf16[4,4,80,128]{3,2,1,0:T(8,128)(2,1)S(1)} all-to-all(bf16[4,4,80,128]{3,2,1,0:T(8,128)(2,1)S(1)} %get-tuple-element.25), channel_id=1, replica_groups=mesh['slab'=8,'obs'=4] {'obs'}, dimensions={0} | all-to-all | bytes 655360 | tf_op jit(solution)/shard_map/all_to_all | solution.py:404
  91.2 1.6 %collective-permute-done.6.refs_1_ = bf16[4,4,80,128]{3,2,1,0:T(8,128)(2,1)S(1)} collective-permute-done((bf16[4,4,80,128]{3,2,1,0:T(8,128)(2,1)S(1)}, bf16[4,4,80,128]{3,2,1,0:T(8,128)(2,1)S(1)}, u32[]{:S(2)}, u32[]{:S(2)}) %collective-permute-start.6) | collective-permute-done | bytes 327712 | tf_op jit(solution)/shard_map/ppermute | solution.py:398
  92.8 1.1 shard_map.112
  93.9 21.0 %all_to_all.38.refs_0_ = bf16[4,4,80,256]{3,2,1,0:T(8,128)(2,1)S(1)} all-to-all(bf16[4,4,80,256]{3,2,1,0:T(8,128)(2,1)S(1)} %shard_map.112), channel_id=1, replica_groups={{0,8,16,24},{4,12,20,28},{1,9,17,25},{5,13,21,29},{2,10,18,26},{6,14,22..., dimensions={0} | all-to-all | bytes 1310720 | tf_op jit(solution)/shard_map/all_to_all | solution.py:405
  114.9 0.9 shard_map.113
  115.9 1.5 %collective-permute-start.9 = (bf16[4,80,256]{2,1,0:T(8,128)(2,1)S(1)}, bf16[4,80,256]{2,1,0:T(8,128)(2,1)S(1)}, u32[]{:S(2)}, u32[]{:S(2)}) collective-permute-start(bf16[4,80,256]{2,1,0:T(8,128)(2,1)S(1)} %get-tuple-element.27.refs_0_), channel_id=1, source_target_pairs={{0,24},{4,28},{8,16},{12,20},{16,8},{20,12},{24,0},{28,4},{1,25},{... | collective-permute-start | bytes 491528 | tf_op jit(solution)/shard_map/ppermute | solution.py:392
  117.5 2.7 %collective-permute-start.7 = (bf16[4,80,256]{2,1,0:T(8,128)(2,1)S(1)}, bf16[4,80,256]{2,1,0:T(8,128)(2,1)S(1)}, u32[]{:S(2)}, u32[]{:S(2)}) collective-permute-start(bf16[4,80,256]{2,1,0:T(8,128)(2,1)S(1)} %get-tuple-element.27.refs_0_), channel_id=1, source_target_pairs={{0,8},{4,12},{8,0},{12,4},{16,24},{20,28},{24,16},{28,20},{1,9},{5... | collective-permute-start | bytes 491528 | tf_op jit(solution)/shard_map/ppermute | solution.py:392
  120.3 4.6 %collective-permute-done.9.refs_3_ = bf16[4,80,256]{2,1,0:T(8,128)(2,1)S(1)} collective-permute-done((bf16[4,80,256]{2,1,0:T(8,128)(2,1)S(1)}, bf16[4,80,256]{2,1,0:T(8,128)(2,1)S(1)}, u32[]{:S(2)}, u32[]{:S(2)}) %collective-permute-start.9) | collective-permute-done | bytes 163872 | tf_op jit(solution)/shard_map/ppermute | solution.py:392
  124.8 6.6 %collective-permute-done.8.refs_2_ = bf16[4,80,256]{2,1,0:T(8,128)(2,1)S(1)} collective-permute-done((bf16[4,80,256]{2,1,0:T(8,128)(2,1)S(1)}, bf16[4,80,256]{2,1,0:T(8,128)(2,1)S(1)}, u32[]{:S(2)}, u32[]{:S(2)}) %collective-permute-start.8) | collective-permute-done | bytes 163872 | tf_op jit(solution)/shard_map/ppermute | solution.py:392
  132.0 1.6 %collective-permute-done.10.refs_5_ = bf16[4,4,80,128]{3,2,1,0:T(8,128)(2,1)S(1)} collective-permute-done((bf16[4,4,80,128]{3,2,1,0:T(8,128)(2,1)S(1)}, bf16[4,4,80,128]{3,2,1,0:T(8,128)(2,1)S(1)}, u32[]{:S(2)}, u32[]{:S(2)}) %collective-permute-start.10) | collective-permute-done | bytes 327712 | tf_op jit(solution)/shard_map/ppermute | solution.py:398
  133.6 0.6 shard_map.115
  134.2 9.5 %all_to_all.39.refs_0_ = bf16[4,4,80,128]{3,2,1,0:T(8,128)(2,1)S(1)} all-to-all(bf16[4,4,80,128]{3,2,1,0:T(8,128)(2,1)S(1)} %shard_map.115), channel_id=1, replica_groups=mesh['slab'=8,'obs'=4] {'obs'}, dimensions={0} | all-to-all | bytes 655360 | tf_op jit(solution)/shard_map/all_to_all | solution.py:404
  143.8 1.3 shard_map.116
  (27 shorter events, 2.0 us)
Async XLA Ops:
  0.6 11.9 %copy-start.5 = (f32[75,75]{1,0:T(8,128)S(1)}, f32[75,75]{1,0:T(8,128)}, u32[]{:S(2)}) copy-start(f32[75,75]{1,0:T(8,128)} %param.13) | copy-start | bytes 67504
  1.3 17.9 %copy-start.4 = (f32[1,128]{1,0:T(1,128)S(1)}, f32[1,128]{1,0:T(1,128)}, u32[]{:S(2)}) copy-start(f32[1,128]{1,0:T(1,128)} %refs_1_.5) | copy-start | bytes 1540
  7.1 23.9 %copy-start = (bf16[4,4,128,256]{3,2,1,0:T(8,128)(2,1)S(1)}, bf16[4,4,128,256]{3,2,1,0:T(8,128)(2,1)}, u32[]{:S(2)}) copy-start(bf16[4,4,128,256]{3,2,1,0:T(8,128)(2,1)} %get-tuple-element.20.refs_2_.refs_4_) | copy-start | bytes 3145732
  7.1 23.9 %collective-permute-start.1 = (bf16[4,4,128,256]{3,2,1,0:T(8,128)(2,1)}, bf16[4,4,128,256]{3,2,1,0:T(8,128)(2,1)S(1)}, u32[]{:S(2)}, u32[]{:S(2)}) collective-permute-start(bf16[4,4,128,256]{3,2,1,0:T(8,128)(2,1)} %get-tuple-element.21), channel_id=1, source_target_pairs={{0,4},{4,0},{8,12},{12,8},{16,20},{20,16},{24,28},{28,24},{1,5},{5... | collective-permute-start | bytes 3145736 | tf_op jit(solution)/shard_map/ppermute | solution.py:398
  8.2 11.1 %all-to-all-start = ((bf16[4,4,80,128]{3,2,1,0:T(8,128)(2,1)}), bf16[4,4,80,128]{3,2,1,0:T(8,128)(2,1)S(1)}, u32[]{:S(2)}, u32[]{:S(2)}) async-start(bf16[4,4,80,128]{3,2,1,0:T(8,128)(2,1)} %get-tuple-element.18), calls=%async_computation | async-start | bytes 655360 | tf_op jit(solution)/shard_map/all_to_all | solution.py:404
  19.8 0.7 copy-start.2
  29.4 1.6 %collective-permute-start = (bf16[4,4,80,128]{3,2,1,0:T(8,128)(2,1)S(1)}, bf16[4,4,80,128]{3,2,1,0:T(8,128)(2,1)S(1)}, u32[]{:S(2)}, u32[]{:S(2)}) collective-permute-start(bf16[4,4,80,128]{3,2,1,0:T(8,128)(2,1)S(1)} %all_to_all.35.refs_0_), channel_id=1, source_target_pairs={{0,4},{4,0},{8,12},{12,8},{16,20},{20,16},{24,28},{28,24},{1,5},{5... | collective-permute-start | bytes 983048 | tf_op jit(solution)/shard_map/ppermute | solution.py:398
  31.0 6.6 %copy-start.1 = (f32[8,75,256]{2,0,1:T(8,128)S(1)}, f32[8,75,256]{2,0,1:T(8,128)}, u32[]{:S(2)}) copy-start(f32[8,75,256]{2,0,1:T(8,128)} %param.10) | copy-start | bytes 1843204
  33.0 22.2 %all-to-all-start.2 = ((bf16[4,4,80,256]{3,2,1,0:T(8,128)(2,1)}), bf16[4,4,80,256]{3,2,1,0:T(8,128)(2,1)S(1)}, u32[]{:S(2)}, u32[]{:S(2)}) async-start(bf16[4,4,80,256]{3,2,1,0:T(8,128)(2,1)} %shard_map.106), calls=%async_computation.2 | async-start | bytes 1310720 | tf_op jit(solution)/shard_map/all_to_all | solution.py:405
  55.4 26.5 %copy-start.3 = (f32[4,80,128]{2,1,0:T(8,128)S(1)}, f32[4,80,128]{2,1,0:T(8,128)}, u32[]{:S(2)}) copy-start(f32[4,80,128]{2,1,0:T(8,128)} %copy-done.2) | copy-start | bytes 491524
  55.4 9.0 %collective-permute-start.4 = (bf16[4,80,256]{2,1,0:T(8,128)(2,1)S(1)}, bf16[4,80,256]{2,1,0:T(8,128)(2,1)S(1)}, u32[]{:S(2)}, u32[]{:S(2)}) collective-permute-start(bf16[4,80,256]{2,1,0:T(8,128)(2,1)S(1)} %get-tuple-element.22.refs_0_), channel_id=1, source_target_pairs={{0,24},{4,28},{8,16},{12,20},{16,8},{20,12},{24,0},{28,4},{1,25},{... | collective-permute-start | bytes 491528 | tf_op jit(solution)/shard_map/ppermute | solution.py:392
  57.0 12.6 %collective-permute-start.3 = (bf16[4,80,256]{2,1,0:T(8,128)(2,1)S(1)}, bf16[4,80,256]{2,1,0:T(8,128)(2,1)S(1)}, u32[]{:S(2)}, u32[]{:S(2)}) collective-permute-start(bf16[4,80,256]{2,1,0:T(8,128)(2,1)S(1)} %get-tuple-element.22.refs_0_), channel_id=1, source_target_pairs={{0,16},{4,20},{8,24},{12,28},{16,0},{20,4},{24,8},{28,12},{1,17},{... | collective-permute-start | bytes 491528 | tf_op jit(solution)/shard_map/ppermute | solution.py:392
  57.0 12.6 %collective-permute-start.2 = (bf16[4,80,256]{2,1,0:T(8,128)(2,1)S(1)}, bf16[4,80,256]{2,1,0:T(8,128)(2,1)S(1)}, u32[]{:S(2)}, u32[]{:S(2)}) collective-permute-start(bf16[4,80,256]{2,1,0:T(8,128)(2,1)S(1)} %get-tuple-element.22.refs_0_), channel_id=1, source_target_pairs={{0,8},{4,12},{8,0},{12,4},{16,24},{20,28},{24,16},{28,20},{1,9},{5... | collective-permute-start | bytes 491528 | tf_op jit(solution)/shard_map/ppermute | solution.py:392
  70.1 1.7 %collective-permute-start.5 = (bf16[4,4,80,128]{3,2,1,0:T(8,128)(2,1)S(1)}, bf16[4,4,80,128]{3,2,1,0:T(8,128)(2,1)S(1)}, u32[]{:S(2)}, u32[]{:S(2)}) collective-permute-start(bf16[4,4,80,128]{3,2,1,0:T(8,128)(2,1)S(1)} %shard_map.109), channel_id=1, source_target_pairs={{0,4},{4,0},{8,12},{12,8},{16,20},{20,16},{24,28},{28,24},{1,5},{5... | collective-permute-start | bytes 983048 | tf_op jit(solution)/shard_map/ppermute | solution.py:398
  91.2 1.6 %collective-permute-start.6 = (bf16[4,4,80,128]{3,2,1,0:T(8,128)(2,1)S(1)}, bf16[4,4,80,128]{3,2,1,0:T(8,128)(2,1)S(1)}, u32[]{:S(2)}, u32[]{:S(2)}) collective-permute-start(bf16[4,4,80,128]{3,2,1,0:T(8,128)(2,1)S(1)} %all_to_all.37.refs_0_), channel_id=1, source_target_pairs={{0,4},{4,0},{8,12},{12,8},{16,20},{20,16},{24,28},{28,24},{1,5},{5... | collective-permute-start | bytes 983048 | tf_op jit(solution)/shard_map/ppermute | solution.py:398
  115.9 8.9 %collective-permute-start.9 = (bf16[4,80,256]{2,1,0:T(8,128)(2,1)S(1)}, bf16[4,80,256]{2,1,0:T(8,128)(2,1)S(1)}, u32[]{:S(2)}, u32[]{:S(2)}) collective-permute-start(bf16[4,80,256]{2,1,0:T(8,128)(2,1)S(1)} %get-tuple-element.27.refs_0_), channel_id=1, source_target_pairs={{0,24},{4,28},{8,16},{12,20},{16,8},{20,12},{24,0},{28,4},{1,25},{... | collective-permute-start | bytes 491528 | tf_op jit(solution)/shard_map/ppermute | solution.py:392
  117.3 14.0 %collective-permute-start.8 = (bf16[4,80,256]{2,1,0:T(8,128)(2,1)S(1)}, bf16[4,80,256]{2,1,0:T(8,128)(2,1)S(1)}, u32[]{:S(2)}, u32[]{:S(2)}) collective-permute-start(bf16[4,80,256]{2,1,0:T(8,128)(2,1)S(1)} %get-tuple-element.27.refs_0_), channel_id=1, source_target_pairs={{0,16},{4,20},{8,24},{12,28},{16,0},{20,4},{24,8},{28,12},{1,17},{... | collective-permute-start | bytes 491528 | tf_op jit(solution)/shard_map/ppermute | solution.py:392
  117.5 13.8 %collective-permute-start.7 = (bf16[4,80,256]{2,1,0:T(8,128)(2,1)S(1)}, bf16[4,80,256]{2,1,0:T(8,128)(2,1)S(1)}, u32[]{:S(2)}, u32[]{:S(2)}) collective-permute-start(bf16[4,80,256]{2,1,0:T(8,128)(2,1)S(1)} %get-tuple-element.27.refs_0_), channel_id=1, source_target_pairs={{0,8},{4,12},{8,0},{12,4},{16,24},{20,28},{24,16},{28,20},{1,9},{5... | collective-permute-start | bytes 491528 | tf_op jit(solution)/shard_map/ppermute | solution.py:392
  131.9 1.7 %collective-permute-start.10 = (bf16[4,4,80,128]{3,2,1,0:T(8,128)(2,1)S(1)}, bf16[4,4,80,128]{3,2,1,0:T(8,128)(2,1)S(1)}, u32[]{:S(2)}, u32[]{:S(2)}) collective-permute-start(bf16[4,4,80,128]{3,2,1,0:T(8,128)(2,1)S(1)} %shard_map.114), channel_id=1, source_target_pairs={{0,4},{4,0},{8,12},{12,8},{16,20},{20,16},{24,28},{28,24},{1,5},{5... | collective-permute-start | bytes 983048 | tf_op jit(solution)/shard_map/ppermute | solution.py:398

commit v4 on v3

--- a/solution.py
+++ b/solution.py
@@ -8,10 +8,10 @@
 from jax.sharding import PartitionSpec as P
 
 ITERS = 2
-GROUPS = 1
-PLANE_SUM = "whole"
-PLANE_GATHER = "whole"
-LINE_SUM = "whole"
+GROUPS = 2
+PLANE_SUM = "permute"
+PLANE_GATHER = "permute"
+LINE_SUM = "permute"
 LINE_GATHER = "permute"
 LANES = 128
 PIECES = 3

time: 146 us -> 134 us (0.918)
  starting transfers between devices: 19 us -> 84.9 us
  blocking collectives: 57.7 us -> 0 us
  waiting for transfers between devices: 51.2 us -> 26.7 us
  local copies, waits for them, and re-layouts: 0.78 us -> 2.91 us
  Pallas kernels: 14.9 us -> 16.9 us
    all_to_all x5 -> x0, blocking collectives: 57.7 us -> none  [the longest x4 36.7 us: spread(): return [lax.all_to_all(outs[0], 'obs', 0, 0, tiled=True)]]
    ppermute x0 -> x30, starting transfers between devices: none -> 37.1 us  [plane(): return lax.ppermute(x, 'obs', [(o, o ^ i) for o in range(n_obs)])]
    ppermute x6 -> x24, starting transfers between devices: 8.84 us -> 44.7 us  [along(): return lax.ppermute(x, 'slab', [(s, s ^ 2 * i) for s in range(n_slab)])]
    all_to_all x2 -> x0, waiting for transfers between devices: 24 us -> none  [the longest x1 17.4 us: spread(): lax.all_to_all(outs[0], 'slab', 0, 0, axis_index_groups=cores, tiled=True)]
    ppermute x0 -> x30, waiting for transfers between devices: none -> 10 us  [plane(): return lax.ppermute(x, 'obs', [(o, o ^ i) for o in range(n_obs)])]
    all_to_all x2 -> x0, starting transfers between devices: 8.99 us -> none  [the longest x1 4.65 us: spread(): lax.all_to_all(outs[0], 'slab', 0, 0, axis_index_groups=cores, tiled=True)]
    ppermute x5 -> x21, waiting for transfers between devices: 6.47 us -> 0.06 us  [swap(): return lax.ppermute(x, 'slab', [(s, s ^ 1) for s in range(n_slab)])]
    ppermute x6 -> x24, waiting for transfers between devices: 20.8 us -> 16.7 us  [along(): return lax.ppermute(x, 'slab', [(s, s ^ 2 * i) for s in range(n_slab)])]
  transfers between devices with their start and end apart: 13 -> 75, of which waited for: 10 -> 16; matrix products, arithmetic and copies ran while one was open for 0% -> 0% of each run, Pallas kernels for 1% -> 8%
where the time goes in v4:
time: 134 us
  starting transfers between devices  84.9 us (63%)
  waiting for transfers between devices  26.7 us (20%)
  Pallas kernels  16.9 us (13%)
  local copies, waits for them, and re-layouts  2.91 us (2%)
  between operations  1.61 us (1%)
    ppermute x24, starting transfers between devices, along(): return lax.ppermute(x, 'slab', [(s, s ^ 2 * i) for s in range(n_slab)])  44.7 us
    ppermute x30, starting transfers between devices, plane(): return lax.ppermute(x, 'obs', [(o, o ^ i) for o in range(n_obs)])  37.1 us
    pallas_call x24, Pallas kernels, call(): pl.pallas_call(kernel, out_shape=outs, in_specs=[space] * len(args), out_...  16.9 us
    ppermute x24, waiting for transfers between devices, along(): return lax.ppermute(x, 'slab', [(s, s ^ 2 * i) for s in range(n_slab)])  16.7 us
    ppermute x30, waiting for transfers between devices, plane(): return lax.ppermute(x, 'obs', [(o, o ^ i) for o in range(n_obs)])  10 us
    ppermute x21, starting transfers between devices, swap(): return lax.ppermute(x, 'slab', [(s, s ^ 1) for s in range(n_slab)])  3.1 us
    unnamed x15, local copies, waits for them, and re-layouts  2.89 us
  transfers between devices with their start and end apart: 75, of which 16 were waited for; matrix products, arithmetic and copies ran while one was open for 0% of the time, Pallas kernels for 8%

profile of v4, /device:TPU:0, one launch (start us, length us, event | category | flops | bytes accessed | tf_op | source)
XLA Modules:
  0.0 133.9 jit_solution(8986072758595601587)
XLA Ops:
  1.3 5.8 %shard_map.104 = (bf16[4,4,128,256]{3,2,1,0:T(8,128)(2,1)}, bf16[4,4,128,256]{3,2,1,0:T(8,128)(2,1)}, bf16[2,80,128]{2,1,0:T(8,128)(2,1)}, bf16[2,80,128]{2,1,0:...) custom-call(s32[4]{0:T(128)} %seeds_in.1, ...), custom_call_target="tpu_custom_call" | custom-call | flops 671088640 | bytes 5751060 | tf_op jit(solution)/shard_map/pallas_call | solution.py:28
  7.6 2.9 %collective-permute-start = (bf16[2,80,128]{2,1,0:T(8,128)(2,1)}, bf16[2,80,128]{2,1,0:T(8,128)(2,1)S(1)}, u32[]{:S(2)}, u32[]{:S(2)}) collective-permute-start(bf16[2,80,128]{2,1,0:T(8,128)(2,1)} %get-tuple-element.71), channel_id=1, source_target_pairs={{0,1},{1,0},{2,3},{3,2},{4,5},{5,4},{6,7},{7,6},{8,9},{9,8},{10,11... | collective-permute-start | bytes 122888 | tf_op jit(solution)/shard_map/ppermute | solution.py:395
  10.5 1.5 %collective-permute-start.1 = (bf16[2,80,128]{2,1,0:T(8,128)(2,1)}, bf16[2,80,128]{2,1,0:T(8,128)(2,1)S(1)}, u32[]{:S(2)}, u32[]{:S(2)}) collective-permute-start(bf16[2,80,128]{2,1,0:T(8,128)(2,1)} %get-tuple-element.72), channel_id=1, source_target_pairs={{0,2},{1,3},{2,0},{3,1},{4,6},{5,7},{6,4},{7,5},{8,10},{9,11},{10,... | collective-permute-start | bytes 122888 | tf_op jit(solution)/shard_map/ppermute | solution.py:395
  12.0 2.0 %collective-permute-start.38 = (bf16[2,80,128]{2,1,0:T(8,128)(2,1)}, bf16[2,80,128]{2,1,0:T(8,128)(2,1)S(1)}, u32[]{:S(2)}, u32[]{:S(2)}) collective-permute-start(bf16[2,80,128]{2,1,0:T(8,128)(2,1)} %get-tuple-element.105), channel_id=1, source_target_pairs={{0,1},{1,0},{2,3},{3,2},{4,5},{5,4},{6,7},{7,6},{8,9},{9,8},{10,11... | collective-permute-start | bytes 122888 | tf_op jit(solution)/shard_map/ppermute | solution.py:395
  14.0 1.5 %collective-permute-start.39 = (bf16[2,80,128]{2,1,0:T(8,128)(2,1)}, bf16[2,80,128]{2,1,0:T(8,128)(2,1)S(1)}, u32[]{:S(2)}, u32[]{:S(2)}) collective-permute-start(bf16[2,80,128]{2,1,0:T(8,128)(2,1)} %get-tuple-element.106), channel_id=1, source_target_pairs={{0,2},{1,3},{2,0},{3,1},{4,6},{5,7},{6,4},{7,5},{8,10},{9,11},{10,... | collective-permute-start | bytes 122888 | tf_op jit(solution)/shard_map/ppermute | solution.py:395
  20.4 1.5 %collective-permute-start.5 = (bf16[2,80,128]{2,1,0:T(8,128)(2,1)S(1)}, bf16[2,80,128]{2,1,0:T(8,128)(2,1)S(1)}, u32[]{:S(2)}, u32[]{:S(2)}) collective-permute-start(bf16[2,80,128]{2,1,0:T(8,128)(2,1)S(1)} %get-tuple-element.74.refs_0_), channel_id=1, source_target_pairs={{0,3},{1,2},{2,1},{3,0},{4,7},{5,6},{6,5},{7,4},{8,11},{9,10},{10,... | collective-permute-start | bytes 122888 | tf_op jit(solution)/shard_map/ppermute | solution.py:395
  25.3 1.5 %collective-permute-start.43 = (bf16[2,80,128]{2,1,0:T(8,128)(2,1)S(1)}, bf16[2,80,128]{2,1,0:T(8,128)(2,1)S(1)}, u32[]{:S(2)}, u32[]{:S(2)}) collective-permute-start(bf16[2,80,128]{2,1,0:T(8,128)(2,1)S(1)} %get-tuple-element.108.refs_0_), channel_id=1, source_target_pairs={{0,3},{1,2},{2,1},{3,0},{4,7},{5,6},{6,5},{7,4},{8,11},{9,10},{10,... | collective-permute-start | bytes 122888 | tf_op jit(solution)/shard_map/ppermute | solution.py:395
  28.4 1.9 %collective-permute-done.43.refs_3_ = bf16[2,80,128]{2,1,0:T(8,128)(2,1)S(1)} collective-permute-done((bf16[2,80,128]{2,1,0:T(8,128)(2,1)S(1)}, bf16[2,80,128]{2,1,0:T(8,128)(2,1)S(1)}, u32[]{:S(2)}, u32[]{:S(2)}) %collective-permute-start.43) | collective-permute-done | bytes 40992 | tf_op jit(solution)/shard_map/ppermute | solution.py:395
  34.5 2.5 %collective-permute-start.12 = (bf16[2,80,256]{2,1,0:T(8,128)(2,1)S(1)}, bf16[2,80,256]{2,1,0:T(8,128)(2,1)S(1)}, u32[]{:S(2)}, u32[]{:S(2)}) collective-permute-start(bf16[2,80,256]{2,1,0:T(8,128)(2,1)S(1)} %get-tuple-element.79), channel_id=1, source_target_pairs={{0,16},{4,20},{8,24},{12,28},{16,0},{20,4},{24,8},{28,12},{1,17},{... | collective-permute-start | bytes 245768 | tf_op jit(solution)/shard_map/ppermute | solution.py:392
  38.8 3.5 %collective-permute-start.49 = (bf16[2,80,256]{2,1,0:T(8,128)(2,1)S(1)}, bf16[2,80,256]{2,1,0:T(8,128)(2,1)S(1)}, u32[]{:S(2)}, u32[]{:S(2)}) collective-permute-start(bf16[2,80,256]{2,1,0:T(8,128)(2,1)S(1)} %get-tuple-element.111), channel_id=1, source_target_pairs={{0,16},{4,20},{8,24},{12,28},{16,0},{20,4},{24,8},{28,12},{1,17},{... | collective-permute-start | bytes 245768 | tf_op jit(solution)/shard_map/ppermute | solution.py:392
  42.8 1.7 %collective-permute-done.12.refs_2_ = bf16[2,80,256]{2,1,0:T(8,128)(2,1)S(1)} collective-permute-done((bf16[2,80,256]{2,1,0:T(8,128)(2,1)S(1)}, bf16[2,80,256]{2,1,0:T(8,128)(2,1)S(1)}, u32[]{:S(2)}, u32[]{:S(2)}) %collective-permute-start.12) | collective-permute-done | bytes 81952 | tf_op jit(solution)/shard_map/ppermute | solution.py:392
  44.7 6.2 %collective-permute-start.14 = (bf16[2,80,256]{2,1,0:T(8,128)(2,1)S(1)}, bf16[2,80,256]{2,1,0:T(8,128)(2,1)S(1)}, u32[]{:S(2)}, u32[]{:S(2)}) collective-permute-start(bf16[2,80,256]{2,1,0:T(8,128)(2,1)S(1)} %get-tuple-element.81.refs_0_), channel_id=1, source_target_pairs={{0,8},{4,12},{8,0},{12,4},{16,24},{20,28},{24,16},{28,20},{1,9},{5... | collective-permute-start | bytes 245768 | tf_op jit(solution)/shard_map/ppermute | solution.py:392
  50.9 2.1 %collective-permute-start.15 = (bf16[2,80,256]{2,1,0:T(8,128)(2,1)S(1)}, bf16[2,80,256]{2,1,0:T(8,128)(2,1)S(1)}, u32[]{:S(2)}, u32[]{:S(2)}) collective-permute-start(bf16[2,80,256]{2,1,0:T(8,128)(2,1)S(1)} %get-tuple-element.81.refs_0_), channel_id=1, source_target_pairs={{0,16},{4,20},{8,24},{12,28},{16,0},{20,4},{24,8},{28,12},{1,17},{... | collective-permute-start | bytes 245768 | tf_op jit(solution)/shard_map/ppermute | solution.py:392
  55.2 2.4 %collective-permute-start.52 = (bf16[2,80,256]{2,1,0:T(8,128)(2,1)S(1)}, bf16[2,80,256]{2,1,0:T(8,128)(2,1)S(1)}, u32[]{:S(2)}, u32[]{:S(2)}) collective-permute-start(bf16[2,80,256]{2,1,0:T(8,128)(2,1)S(1)} %get-tuple-element.113.refs_0_), channel_id=1, source_target_pairs={{0,16},{4,20},{8,24},{12,28},{16,0},{20,4},{24,8},{28,12},{1,17},{... | collective-permute-start | bytes 245768 | tf_op jit(solution)/shard_map/ppermute | solution.py:392
  59.0 2.1 %collective-permute-done.16.refs_3_ = bf16[2,80,256]{2,1,0:T(8,128)(2,1)S(1)} collective-permute-done((bf16[2,80,256]{2,1,0:T(8,128)(2,1)S(1)}, bf16[2,80,256]{2,1,0:T(8,128)(2,1)S(1)}, u32[]{:S(2)}, u32[]{:S(2)}) %collective-permute-start.16) | collective-permute-done | bytes 81952 | tf_op jit(solution)/shard_map/ppermute | solution.py:392
  61.7 4.0 %collective-permute-done.52.refs_2_ = bf16[2,80,256]{2,1,0:T(8,128)(2,1)S(1)} collective-permute-done((bf16[2,80,256]{2,1,0:T(8,128)(2,1)S(1)}, bf16[2,80,256]{2,1,0:T(8,128)(2,1)S(1)}, u32[]{:S(2)}, u32[]{:S(2)}) %collective-permute-start.52) | collective-permute-done | bytes 81952 | tf_op jit(solution)/shard_map/ppermute | solution.py:392
  69.0 1.4 %collective-permute-start.20 = (bf16[2,80,128]{2,1,0:T(8,128)(2,1)S(1)}, bf16[2,80,128]{2,1,0:T(8,128)(2,1)S(1)}, u32[]{:S(2)}, u32[]{:S(2)}) collective-permute-start(bf16[2,80,128]{2,1,0:T(8,128)(2,1)S(1)} %get-tuple-element.85), channel_id=1, source_target_pairs={{0,3},{1,2},{2,1},{3,0},{4,7},{5,6},{6,5},{7,4},{8,11},{9,10},{10,... | collective-permute-start | bytes 122888 | tf_op jit(solution)/shard_map/ppermute | solution.py:395
  83.8 2.2 %collective-permute-done.60.refs_3_ = bf16[2,80,128]{2,1,0:T(8,128)(2,1)S(1)} collective-permute-done((bf16[2,80,128]{2,1,0:T(8,128)(2,1)S(1)}, bf16[2,80,128]{2,1,0:T(8,128)(2,1)S(1)}, u32[]{:S(2)}, u32[]{:S(2)}) %collective-permute-start.60) | collective-permute-done | bytes 40992 | tf_op jit(solution)/shard_map/ppermute | solution.py:395
  87.2 1.5 %collective-permute-start.28 = (bf16[2,80,256]{2,1,0:T(8,128)(2,1)S(1)}, bf16[2,80,256]{2,1,0:T(8,128)(2,1)S(1)}, u32[]{:S(2)}, u32[]{:S(2)}) collective-permute-start(bf16[2,80,256]{2,1,0:T(8,128)(2,1)S(1)} %get-tuple-element.90), channel_id=1, source_target_pairs={{0,8},{4,12},{8,0},{12,4},{16,24},{20,28},{24,16},{28,20},{1,9},{5... | collective-permute-start | bytes 245768 | tf_op jit(solution)/shard_map/ppermute | solution.py:392
  88.7 1.7 %collective-permute-start.29 = (bf16[2,80,256]{2,1,0:T(8,128)(2,1)S(1)}, bf16[2,80,256]{2,1,0:T(8,128)(2,1)S(1)}, u32[]{:S(2)}, u32[]{:S(2)}) collective-permute-start(bf16[2,80,256]{2,1,0:T(8,128)(2,1)S(1)} %get-tuple-element.91), channel_id=1, source_target_pairs={{0,16},{4,20},{8,24},{12,28},{16,0},{20,4},{24,8},{28,12},{1,17},{... | collective-permute-start | bytes 245768 | tf_op jit(solution)/shard_map/ppermute | solution.py:392
  92.9 2.6 %collective-permute-start.66 = (bf16[2,80,256]{2,1,0:T(8,128)(2,1)S(1)}, bf16[2,80,256]{2,1,0:T(8,128)(2,1)S(1)}, u32[]{:S(2)}, u32[]{:S(2)}) collective-permute-start(bf16[2,80,256]{2,1,0:T(8,128)(2,1)S(1)} %get-tuple-element.123), channel_id=1, source_target_pairs={{0,16},{4,20},{8,24},{12,28},{16,0},{20,4},{24,8},{28,12},{1,17},{... | collective-permute-start | bytes 245768 | tf_op jit(solution)/shard_map/ppermute | solution.py:392
  96.7 1.4 %collective-permute-done.29.refs_2_ = bf16[2,80,256]{2,1,0:T(8,128)(2,1)S(1)} collective-permute-done((bf16[2,80,256]{2,1,0:T(8,128)(2,1)S(1)}, bf16[2,80,256]{2,1,0:T(8,128)(2,1)S(1)}, u32[]{:S(2)}, u32[]{:S(2)}) %collective-permute-start.29) | collective-permute-done | bytes 81952 | tf_op jit(solution)/shard_map/ppermute | solution.py:392
  99.0 5.8 %collective-permute-start.31 = (bf16[2,80,256]{2,1,0:T(8,128)(2,1)S(1)}, bf16[2,80,256]{2,1,0:T(8,128)(2,1)S(1)}, u32[]{:S(2)}, u32[]{:S(2)}) collective-permute-start(bf16[2,80,256]{2,1,0:T(8,128)(2,1)S(1)} %get-tuple-element.94.refs_0_), channel_id=1, source_target_pairs={{0,8},{4,12},{8,0},{12,4},{16,24},{20,28},{24,16},{28,20},{1,9},{5... | collective-permute-start | bytes 245768 | tf_op jit(solution)/shard_map/ppermute | solution.py:392
  105.8 1.5 %collective-permute-start.33 = (bf16[2,80,256]{2,1,0:T(8,128)(2,1)S(1)}, bf16[2,80,256]{2,1,0:T(8,128)(2,1)S(1)}, u32[]{:S(2)}, u32[]{:S(2)}) collective-permute-start(bf16[2,80,256]{2,1,0:T(8,128)(2,1)S(1)} %get-tuple-element.94.refs_0_), channel_id=1, source_target_pairs={{0,24},{4,28},{8,16},{12,20},{16,8},{20,12},{24,0},{28,4},{1,25},{... | collective-permute-start | bytes 245768 | tf_op jit(solution)/shard_map/ppermute | solution.py:392
  109.1 1.9 %collective-permute-start.69 = (bf16[2,80,256]{2,1,0:T(8,128)(2,1)S(1)}, bf16[2,80,256]{2,1,0:T(8,128)(2,1)S(1)}, u32[]{:S(2)}, u32[]{:S(2)}) collective-permute-start(bf16[2,80,256]{2,1,0:T(8,128)(2,1)S(1)} %get-tuple-element.126.refs_0_), channel_id=1, source_target_pairs={{0,16},{4,20},{8,24},{12,28},{16,0},{20,4},{24,8},{28,12},{1,17},{... | collective-permute-start | bytes 245768 | tf_op jit(solution)/shard_map/ppermute | solution.py:392
  111.0 1.5 %collective-permute-start.70 = (bf16[2,80,256]{2,1,0:T(8,128)(2,1)S(1)}, bf16[2,80,256]{2,1,0:T(8,128)(2,1)S(1)}, u32[]{:S(2)}, u32[]{:S(2)}) collective-permute-start(bf16[2,80,256]{2,1,0:T(8,128)(2,1)S(1)} %get-tuple-element.126.refs_0_), channel_id=1, source_target_pairs={{0,24},{4,28},{8,16},{12,20},{16,8},{20,12},{24,0},{28,4},{1,25},{... | collective-permute-start | bytes 245768 | tf_op jit(solution)/shard_map/ppermute | solution.py:392
  112.4 2.0 %collective-permute-done.32.refs_2_ = bf16[2,80,256]{2,1,0:T(8,128)(2,1)S(1)} collective-permute-done((bf16[2,80,256]{2,1,0:T(8,128)(2,1)S(1)}, bf16[2,80,256]{2,1,0:T(8,128)(2,1)S(1)}, u32[]{:S(2)}, u32[]{:S(2)}) %collective-permute-start.32) | collective-permute-done | bytes 81952 | tf_op jit(solution)/shard_map/ppermute | solution.py:392
  115.0 5.4 %collective-permute-done.69.refs_2_ = bf16[2,80,256]{2,1,0:T(8,128)(2,1)S(1)} collective-permute-done((bf16[2,80,256]{2,1,0:T(8,128)(2,1)S(1)}, bf16[2,80,256]{2,1,0:T(8,128)(2,1)S(1)}, u32[]{:S(2)}, u32[]{:S(2)}) %collective-permute-start.69) | collective-permute-done | bytes 81952 | tf_op jit(solution)/shard_map/ppermute | solution.py:392
  123.6 1.5 %collective-permute-start.37 = (bf16[2,80,128]{2,1,0:T(8,128)(2,1)S(1)}, bf16[2,80,128]{2,1,0:T(8,128)(2,1)S(1)}, u32[]{:S(2)}, u32[]{:S(2)}) collective-permute-start(bf16[2,80,128]{2,1,0:T(8,128)(2,1)S(1)} %get-tuple-element.98), channel_id=1, source_target_pairs={{0,3},{1,2},{2,1},{3,0},{4,7},{5,6},{6,5},{7,4},{8,11},{9,10},{10,... | collective-permute-start | bytes 122888 | tf_op jit(solution)/shard_map/ppermute | solution.py:395
  127.7 1.5 %collective-permute-start.74 = (bf16[2,80,128]{2,1,0:T(8,128)(2,1)S(1)}, bf16[2,80,128]{2,1,0:T(8,128)(2,1)S(1)}, u32[]{:S(2)}, u32[]{:S(2)}) collective-permute-start(bf16[2,80,128]{2,1,0:T(8,128)(2,1)S(1)} %get-tuple-element.130), channel_id=1, source_target_pairs={{0,3},{1,2},{2,1},{3,0},{4,7},{5,6},{6,5},{7,4},{8,11},{9,10},{10,... | collective-permute-start | bytes 122888 | tf_op jit(solution)/shard_map/ppermute | solution.py:395
  129.7 1.5 %collective-permute-done.73.refs_2_ = bf16[2,80,128]{2,1,0:T(8,128)(2,1)S(1)} collective-permute-done((bf16[2,80,128]{2,1,0:T(8,128)(2,1)S(1)}, bf16[2,80,128]{2,1,0:T(8,128)(2,1)S(1)}, u32[]{:S(2)}, u32[]{:S(2)}) %collective-permute-start.73) | collective-permute-done | bytes 40992 | tf_op jit(solution)/shard_map/ppermute | solution.py:395
  131.2 1.5 %collective-permute-done.74.refs_3_ = bf16[2,80,128]{2,1,0:T(8,128)(2,1)S(1)} collective-permute-done((bf16[2,80,128]{2,1,0:T(8,128)(2,1)S(1)}, bf16[2,80,128]{2,1,0:T(8,128)(2,1)S(1)}, u32[]{:S(2)}, u32[]{:S(2)}) %collective-permute-start.74) | collective-permute-done | bytes 40992 | tf_op jit(solution)/shard_map/ppermute | solution.py:395
  (160 shorter events, 54.5 us)
Async XLA Ops:
  7.1 24.2 %collective-permute-start.10 = (bf16[4,4,128,256]{3,2,1,0:T(8,128)(2,1)}, bf16[4,4,128,256]{3,2,1,0:T(8,128)(2,1)S(1)}, u32[]{:S(2)}, u32[]{:S(2)}) collective-permute-start(bf16[4,4,128,256]{3,2,1,0:T(8,128)(2,1)} %get-tuple-element.76), channel_id=1, source_target_pairs={{0,4},{4,0},{8,12},{12,8},{16,20},{20,16},{24,28},{28,24},{1,5},{5... | collective-permute-start | bytes 3145736 | tf_op jit(solution)/shard_map/ppermute | solution.py:398
  12.0 7.5 %collective-permute-start.38 = (bf16[2,80,128]{2,1,0:T(8,128)(2,1)}, bf16[2,80,128]{2,1,0:T(8,128)(2,1)S(1)}, u32[]{:S(2)}, u32[]{:S(2)}) collective-permute-start(bf16[2,80,128]{2,1,0:T(8,128)(2,1)} %get-tuple-element.105), channel_id=1, source_target_pairs={{0,1},{1,0},{2,3},{3,2},{4,5},{5,4},{6,7},{7,6},{8,9},{9,8},{10,11... | collective-permute-start | bytes 122888 | tf_op jit(solution)/shard_map/ppermute | solution.py:395
  30.2 6.8 %collective-permute-start.45 = (bf16[2,80,128]{2,1,0:T(8,128)(2,1)S(1)}, bf16[2,80,128]{2,1,0:T(8,128)(2,1)S(1)}, u32[]{:S(2)}, u32[]{:S(2)}) collective-permute-start(bf16[2,80,128]{2,1,0:T(8,128)(2,1)S(1)} %collective-permute-done.41.refs_1_), channel_id=1, source_target_pairs={{0,4},{4,0},{8,12},{12,8},{16,20},{20,16},{24,28},{28,24},{1,5},{5... | collective-permute-start | bytes 122888 | tf_op jit(solution)/shard_map/ppermute | solution.py:398
  30.7 6.8 %collective-permute-start.46 = (bf16[2,80,128]{2,1,0:T(8,128)(2,1)S(1)}, bf16[2,80,128]{2,1,0:T(8,128)(2,1)S(1)}, u32[]{:S(2)}, u32[]{:S(2)}) collective-permute-start(bf16[2,80,128]{2,1,0:T(8,128)(2,1)S(1)} %collective-permute-done.42.refs_2_), channel_id=1, source_target_pairs={{0,4},{4,0},{8,12},{12,8},{16,20},{20,16},{24,28},{28,24},{1,5},{5... | collective-permute-start | bytes 122888 | tf_op jit(solution)/shard_map/ppermute | solution.py:398
  30.8 6.7 %collective-permute-start.47 = (bf16[2,80,128]{2,1,0:T(8,128)(2,1)S(1)}, bf16[2,80,128]{2,1,0:T(8,128)(2,1)S(1)}, u32[]{:S(2)}, u32[]{:S(2)}) collective-permute-start(bf16[2,80,128]{2,1,0:T(8,128)(2,1)S(1)} %collective-permute-done.43.refs_3_), channel_id=1, source_target_pairs={{0,4},{4,0},{8,12},{12,8},{16,20},{20,16},{24,28},{28,24},{1,5},{5... | collective-permute-start | bytes 122888 | tf_op jit(solution)/shard_map/ppermute | solution.py:398
  33.1 9.3 %collective-permute-start.11 = (bf16[2,80,256]{2,1,0:T(8,128)(2,1)S(1)}, bf16[2,80,256]{2,1,0:T(8,128)(2,1)S(1)}, u32[]{:S(2)}, u32[]{:S(2)}) collective-permute-start(bf16[2,80,256]{2,1,0:T(8,128)(2,1)S(1)} %get-tuple-element.78), channel_id=1, source_target_pairs={{0,8},{4,12},{8,0},{12,4},{16,24},{20,28},{24,16},{28,20},{1,9},{5... | collective-permute-start | bytes 245768 | tf_op jit(solution)/shard_map/ppermute | solution.py:392
  34.5 10.1 %collective-permute-start.12 = (bf16[2,80,256]{2,1,0:T(8,128)(2,1)S(1)}, bf16[2,80,256]{2,1,0:T(8,128)(2,1)S(1)}, u32[]{:S(2)}, u32[]{:S(2)}) collective-permute-start(bf16[2,80,256]{2,1,0:T(8,128)(2,1)S(1)} %get-tuple-element.79), channel_id=1, source_target_pairs={{0,16},{4,20},{8,24},{12,28},{16,0},{20,4},{24,8},{28,12},{1,17},{... | collective-permute-start | bytes 245768 | tf_op jit(solution)/shard_map/ppermute | solution.py:392
  37.0 7.5 %collective-permute-start.13 = (bf16[2,80,256]{2,1,0:T(8,128)(2,1)S(1)}, bf16[2,80,256]{2,1,0:T(8,128)(2,1)S(1)}, u32[]{:S(2)}, u32[]{:S(2)}) collective-permute-start(bf16[2,80,256]{2,1,0:T(8,128)(2,1)S(1)} %get-tuple-element.80), channel_id=1, source_target_pairs={{0,24},{4,28},{8,16},{12,20},{16,8},{20,12},{24,0},{28,4},{1,25},{... | collective-permute-start | bytes 245768 | tf_op jit(solution)/shard_map/ppermute | solution.py:392
  38.1 14.9 %collective-permute-start.48 = (bf16[2,80,256]{2,1,0:T(8,128)(2,1)S(1)}, bf16[2,80,256]{2,1,0:T(8,128)(2,1)S(1)}, u32[]{:S(2)}, u32[]{:S(2)}) collective-permute-start(bf16[2,80,256]{2,1,0:T(8,128)(2,1)S(1)} %get-tuple-element.110), channel_id=1, source_target_pairs={{0,8},{4,12},{8,0},{12,4},{16,24},{20,28},{24,16},{28,20},{1,9},{5... | collective-permute-start | bytes 245768 | tf_op jit(solution)/shard_map/ppermute | solution.py:392
  38.8 15.6 %collective-permute-start.49 = (bf16[2,80,256]{2,1,0:T(8,128)(2,1)S(1)}, bf16[2,80,256]{2,1,0:T(8,128)(2,1)S(1)}, u32[]{:S(2)}, u32[]{:S(2)}) collective-permute-start(bf16[2,80,256]{2,1,0:T(8,128)(2,1)S(1)} %get-tuple-element.111), channel_id=1, source_target_pairs={{0,16},{4,20},{8,24},{12,28},{16,0},{20,4},{24,8},{28,12},{1,17},{... | collective-permute-start | bytes 245768 | tf_op jit(solution)/shard_map/ppermute | solution.py:392
  42.3 12.1 %collective-permute-start.50 = (bf16[2,80,256]{2,1,0:T(8,128)(2,1)S(1)}, bf16[2,80,256]{2,1,0:T(8,128)(2,1)S(1)}, u32[]{:S(2)}, u32[]{:S(2)}) collective-permute-start(bf16[2,80,256]{2,1,0:T(8,128)(2,1)S(1)} %get-tuple-element.112), channel_id=1, source_target_pairs={{0,24},{4,28},{8,16},{12,20},{16,8},{20,12},{24,0},{28,4},{1,25},{... | collective-permute-start | bytes 245768 | tf_op jit(solution)/shard_map/ppermute | solution.py:392
  44.7 12.9 %collective-permute-start.14 = (bf16[2,80,256]{2,1,0:T(8,128)(2,1)S(1)}, bf16[2,80,256]{2,1,0:T(8,128)(2,1)S(1)}, u32[]{:S(2)}, u32[]{:S(2)}) collective-permute-start(bf16[2,80,256]{2,1,0:T(8,128)(2,1)S(1)} %get-tuple-element.81.refs_0_), channel_id=1, source_target_pairs={{0,8},{4,12},{8,0},{12,4},{16,24},{20,28},{24,16},{28,20},{1,9},{5... | collective-permute-start | bytes 245768 | tf_op jit(solution)/shard_map/ppermute | solution.py:392
  50.9 8.2 %collective-permute-start.15 = (bf16[2,80,256]{2,1,0:T(8,128)(2,1)S(1)}, bf16[2,80,256]{2,1,0:T(8,128)(2,1)S(1)}, u32[]{:S(2)}, u32[]{:S(2)}) collective-permute-start(bf16[2,80,256]{2,1,0:T(8,128)(2,1)S(1)} %get-tuple-element.81.refs_0_), channel_id=1, source_target_pairs={{0,16},{4,20},{8,24},{12,28},{16,0},{20,4},{24,8},{28,12},{1,17},{... | collective-permute-start | bytes 245768 | tf_op jit(solution)/shard_map/ppermute | solution.py:392
  53.0 8.1 %collective-permute-start.16 = (bf16[2,80,256]{2,1,0:T(8,128)(2,1)S(1)}, bf16[2,80,256]{2,1,0:T(8,128)(2,1)S(1)}, u32[]{:S(2)}, u32[]{:S(2)}) collective-permute-start(bf16[2,80,256]{2,1,0:T(8,128)(2,1)S(1)} %get-tuple-element.81.refs_0_), channel_id=1, source_target_pairs={{0,24},{4,28},{8,16},{12,20},{16,8},{20,12},{24,0},{28,4},{1,25},{... | collective-permute-start | bytes 245768 | tf_op jit(solution)/shard_map/ppermute | solution.py:392
  54.6 7.1 %collective-permute-start.51 = (bf16[2,80,256]{2,1,0:T(8,128)(2,1)S(1)}, bf16[2,80,256]{2,1,0:T(8,128)(2,1)S(1)}, u32[]{:S(2)}, u32[]{:S(2)}) collective-permute-start(bf16[2,80,256]{2,1,0:T(8,128)(2,1)S(1)} %get-tuple-element.113.refs_0_), channel_id=1, source_target_pairs={{0,8},{4,12},{8,0},{12,4},{16,24},{20,28},{24,16},{28,20},{1,9},{5... | collective-permute-start | bytes 245768 | tf_op jit(solution)/shard_map/ppermute | solution.py:392
  55.2 10.5 %collective-permute-start.52 = (bf16[2,80,256]{2,1,0:T(8,128)(2,1)S(1)}, bf16[2,80,256]{2,1,0:T(8,128)(2,1)S(1)}, u32[]{:S(2)}, u32[]{:S(2)}) collective-permute-start(bf16[2,80,256]{2,1,0:T(8,128)(2,1)S(1)} %get-tuple-element.113.refs_0_), channel_id=1, source_target_pairs={{0,16},{4,20},{8,24},{12,28},{16,0},{20,4},{24,8},{28,12},{1,17},{... | collective-permute-start | bytes 245768 | tf_op jit(solution)/shard_map/ppermute | solution.py:392
  57.6 8.1 %collective-permute-start.53 = (bf16[2,80,256]{2,1,0:T(8,128)(2,1)S(1)}, bf16[2,80,256]{2,1,0:T(8,128)(2,1)S(1)}, u32[]{:S(2)}, u32[]{:S(2)}) collective-permute-start(bf16[2,80,256]{2,1,0:T(8,128)(2,1)S(1)} %get-tuple-element.113.refs_0_), channel_id=1, source_target_pairs={{0,24},{4,28},{8,16},{12,20},{16,8},{20,12},{24,0},{28,4},{1,25},{... | collective-permute-start | bytes 245768 | tf_op jit(solution)/shard_map/ppermute | solution.py:392
  67.7 6.8 %collective-permute-start.19 = (bf16[2,80,128]{2,1,0:T(8,128)(2,1)S(1)}, bf16[2,80,128]{2,1,0:T(8,128)(2,1)S(1)}, u32[]{:S(2)}, u32[]{:S(2)}) collective-permute-start(bf16[2,80,128]{2,1,0:T(8,128)(2,1)S(1)} %get-tuple-element.84), channel_id=1, source_target_pairs={{0,2},{1,3},{2,0},{3,1},{4,6},{5,7},{6,4},{7,5},{8,10},{9,11},{10,... | collective-permute-start | bytes 122888 | tf_op jit(solution)/shard_map/ppermute | solution.py:395
  71.8 6.7 %collective-permute-start.56 = (bf16[2,80,128]{2,1,0:T(8,128)(2,1)S(1)}, bf16[2,80,128]{2,1,0:T(8,128)(2,1)S(1)}, u32[]{:S(2)}, u32[]{:S(2)}) collective-permute-start(bf16[2,80,128]{2,1,0:T(8,128)(2,1)S(1)} %get-tuple-element.116), channel_id=1, source_target_pairs={{0,2},{1,3},{2,0},{3,1},{4,6},{5,7},{6,4},{7,5},{8,10},{9,11},{10,... | collective-permute-start | bytes 122888 | tf_op jit(solution)/shard_map/ppermute | solution.py:395
  87.2 8.3 %collective-permute-start.28 = (bf16[2,80,256]{2,1,0:T(8,128)(2,1)S(1)}, bf16[2,80,256]{2,1,0:T(8,128)(2,1)S(1)}, u32[]{:S(2)}, u32[]{:S(2)}) collective-permute-start(bf16[2,80,256]{2,1,0:T(8,128)(2,1)S(1)} %get-tuple-element.90), channel_id=1, source_target_pairs={{0,8},{4,12},{8,0},{12,4},{16,24},{20,28},{24,16},{28,20},{1,9},{5... | collective-permute-start | bytes 245768 | tf_op jit(solution)/shard_map/ppermute | solution.py:392
  88.7 9.4 %collective-permute-start.29 = (bf16[2,80,256]{2,1,0:T(8,128)(2,1)S(1)}, bf16[2,80,256]{2,1,0:T(8,128)(2,1)S(1)}, u32[]{:S(2)}, u32[]{:S(2)}) collective-permute-start(bf16[2,80,256]{2,1,0:T(8,128)(2,1)S(1)} %get-tuple-element.91), channel_id=1, source_target_pairs={{0,16},{4,20},{8,24},{12,28},{16,0},{20,4},{24,8},{28,12},{1,17},{... | collective-permute-start | bytes 245768 | tf_op jit(solution)/shard_map/ppermute | solution.py:392
  90.4 7.7 %collective-permute-start.30 = (bf16[2,80,256]{2,1,0:T(8,128)(2,1)S(1)}, bf16[2,80,256]{2,1,0:T(8,128)(2,1)S(1)}, u32[]{:S(2)}, u32[]{:S(2)}) collective-permute-start(bf16[2,80,256]{2,1,0:T(8,128)(2,1)S(1)} %get-tuple-element.92), channel_id=1, source_target_pairs={{0,24},{4,28},{8,16},{12,20},{16,8},{20,12},{24,0},{28,4},{1,25},{... | collective-permute-start | bytes 245768 | tf_op jit(solution)/shard_map/ppermute | solution.py:392
  92.3 13.5 %collective-permute-start.65 = (bf16[2,80,256]{2,1,0:T(8,128)(2,1)S(1)}, bf16[2,80,256]{2,1,0:T(8,128)(2,1)S(1)}, u32[]{:S(2)}, u32[]{:S(2)}) collective-permute-start(bf16[2,80,256]{2,1,0:T(8,128)(2,1)S(1)} %get-tuple-element.122), channel_id=1, source_target_pairs={{0,8},{4,12},{8,0},{12,4},{16,24},{20,28},{24,16},{28,20},{1,9},{5... | collective-permute-start | bytes 245768 | tf_op jit(solution)/shard_map/ppermute | solution.py:392
  92.9 14.4 %collective-permute-start.66 = (bf16[2,80,256]{2,1,0:T(8,128)(2,1)S(1)}, bf16[2,80,256]{2,1,0:T(8,128)(2,1)S(1)}, u32[]{:S(2)}, u32[]{:S(2)}) collective-permute-start(bf16[2,80,256]{2,1,0:T(8,128)(2,1)S(1)} %get-tuple-element.123), channel_id=1, source_target_pairs={{0,16},{4,20},{8,24},{12,28},{16,0},{20,4},{24,8},{28,12},{1,17},{... | collective-permute-start | bytes 245768 | tf_op jit(solution)/shard_map/ppermute | solution.py:392
  95.5 11.8 %collective-permute-start.67 = (bf16[2,80,256]{2,1,0:T(8,128)(2,1)S(1)}, bf16[2,80,256]{2,1,0:T(8,128)(2,1)S(1)}, u32[]{:S(2)}, u32[]{:S(2)}) collective-permute-start(bf16[2,80,256]{2,1,0:T(8,128)(2,1)S(1)} %get-tuple-element.124), channel_id=1, source_target_pairs={{0,24},{4,28},{8,16},{12,20},{16,8},{20,12},{24,0},{28,4},{1,25},{... | collective-permute-start | bytes 245768 | tf_op jit(solution)/shard_map/ppermute | solution.py:392
  99.0 12.0 %collective-permute-start.31 = (bf16[2,80,256]{2,1,0:T(8,128)(2,1)S(1)}, bf16[2,80,256]{2,1,0:T(8,128)(2,1)S(1)}, u32[]{:S(2)}, u32[]{:S(2)}) collective-permute-start(bf16[2,80,256]{2,1,0:T(8,128)(2,1)S(1)} %get-tuple-element.94.refs_0_), channel_id=1, source_target_pairs={{0,8},{4,12},{8,0},{12,4},{16,24},{20,28},{24,16},{28,20},{1,9},{5... | collective-permute-start | bytes 245768 | tf_op jit(solution)/shard_map/ppermute | solution.py:392
  104.8 9.6 %collective-permute-start.32 = (bf16[2,80,256]{2,1,0:T(8,128)(2,1)S(1)}, bf16[2,80,256]{2,1,0:T(8,128)(2,1)S(1)}, u32[]{:S(2)}, u32[]{:S(2)}) collective-permute-start(bf16[2,80,256]{2,1,0:T(8,128)(2,1)S(1)} %get-tuple-element.94.refs_0_), channel_id=1, source_target_pairs={{0,16},{4,20},{8,24},{12,28},{16,0},{20,4},{24,8},{28,12},{1,17},{... | collective-permute-start | bytes 245768 | tf_op jit(solution)/shard_map/ppermute | solution.py:392
  105.8 8.7 %collective-permute-start.33 = (bf16[2,80,256]{2,1,0:T(8,128)(2,1)S(1)}, bf16[2,80,256]{2,1,0:T(8,128)(2,1)S(1)}, u32[]{:S(2)}, u32[]{:S(2)}) collective-permute-start(bf16[2,80,256]{2,1,0:T(8,128)(2,1)S(1)} %get-tuple-element.94.refs_0_), channel_id=1, source_target_pairs={{0,24},{4,28},{8,16},{12,20},{16,8},{20,12},{24,0},{28,4},{1,25},{... | collective-permute-start | bytes 245768 | tf_op jit(solution)/shard_map/ppermute | solution.py:392
  108.1 7.0 %collective-permute-start.68 = (bf16[2,80,256]{2,1,0:T(8,128)(2,1)S(1)}, bf16[2,80,256]{2,1,0:T(8,128)(2,1)S(1)}, u32[]{:S(2)}, u32[]{:S(2)}) collective-permute-start(bf16[2,80,256]{2,1,0:T(8,128)(2,1)S(1)} %get-tuple-element.126.refs_0_), channel_id=1, source_target_pairs={{0,8},{4,12},{8,0},{12,4},{16,24},{20,28},{24,16},{28,20},{1,9},{5... | collective-permute-start | bytes 245768 | tf_op jit(solution)/shard_map/ppermute | solution.py:392
  109.1 11.3 %collective-permute-start.69 = (bf16[2,80,256]{2,1,0:T(8,128)(2,1)S(1)}, bf16[2,80,256]{2,1,0:T(8,128)(2,1)S(1)}, u32[]{:S(2)}, u32[]{:S(2)}) collective-permute-start(bf16[2,80,256]{2,1,0:T(8,128)(2,1)S(1)} %get-tuple-element.126.refs_0_), channel_id=1, source_target_pairs={{0,16},{4,20},{8,24},{12,28},{16,0},{20,4},{24,8},{28,12},{1,17},{... | collective-permute-start | bytes 245768 | tf_op jit(solution)/shard_map/ppermute | solution.py:392
  111.0 9.4 %collective-permute-start.70 = (bf16[2,80,256]{2,1,0:T(8,128)(2,1)S(1)}, bf16[2,80,256]{2,1,0:T(8,128)(2,1)S(1)}, u32[]{:S(2)}, u32[]{:S(2)}) collective-permute-start(bf16[2,80,256]{2,1,0:T(8,128)(2,1)S(1)} %get-tuple-element.126.refs_0_), channel_id=1, source_target_pairs={{0,24},{4,28},{8,16},{12,20},{16,8},{20,12},{24,0},{28,4},{1,25},{... | collective-permute-start | bytes 245768 | tf_op jit(solution)/shard_map/ppermute | solution.py:392
  122.8 6.5 %collective-permute-start.36 = (bf16[2,80,128]{2,1,0:T(8,128)(2,1)S(1)}, bf16[2,80,128]{2,1,0:T(8,128)(2,1)S(1)}, u32[]{:S(2)}, u32[]{:S(2)}) collective-permute-start(bf16[2,80,128]{2,1,0:T(8,128)(2,1)S(1)} %get-tuple-element.97), channel_id=1, source_target_pairs={{0,2},{1,3},{2,0},{3,1},{4,6},{5,7},{6,4},{7,5},{8,10},{9,11},{10,... | collective-permute-start | bytes 122888 | tf_op jit(solution)/shard_map/ppermute | solution.py:395
  (50 other events, 275.2 us)

commit v5 on v3

v5 whole, which is shorter than its diff:
```python
import functools

import jax
import jax.numpy as jnp
from jax import lax
from jax.experimental import pallas as pl
from jax.experimental.pallas import tpu as pltpu
from jax.sharding import PartitionSpec as P

ITERS = 2
GROUPS = 1
LANES = 128
PIECES = 3
PRIME = 32749
VMEM = pl.BlockSpec(memory_space=pltpu.VMEM)
HBM = pl.BlockSpec(memory_space=pltpu.HBM)
F32 = jnp.float32
BF16 = jnp.bfloat16
NT = (((1,), (1,)), ((), ()))


def call(kernel, outs, scratch, flops, *args, space=VMEM, limit=40):
    nbytes = sum(a.size * a.dtype.itemsize for a in (*args, *outs))
    return pl.pallas_call(
        kernel,
        out_shape=outs,
        in_specs=[space] * len(args),
        out_specs=[VMEM] * len(outs),
        scratch_shapes=scratch,
        compiler_params=pltpu.CompilerParams(vmem_limit_bytes=limit * 1024 * 1024),
        cost_estimate=pl.CostEstimate(flops=flops, bytes_accessed=nbytes, transcendentals=0),
    )(*args)


def struct(shape, dtype):
    return jax.ShapeDtypeStruct(shape, dtype)


def place():
    slab = lax.axis_index("slab")
    return slab // 2, slab % 2, lax.axis_index("obs")


def add(parts):
    value = parts[0].astype(F32)
    for part in parts[1:]:
        value = value + part.astype(F32)
    return value


def split(x):
    high = x.astype(BF16)
    return high, (x - high.astype(F32)).astype(BF16)


def dot(a, b):
    (a, a_rest), (b, b_rest) = split(a), split(b)
    one = functools.partial(jnp.dot, preferred_element_type=F32)
    return one(a, b) + (one(a, b_rest) + one(a_rest, b))


def total(x):
    return jnp.sum(jnp.sum(x, axis=0, keepdims=True), axis=1, keepdims=True)


def with_scalars(body, values):
    rows = lax.broadcasted_iota(jnp.int32, body.shape, 0)
    lanes = lax.broadcasted_iota(jnp.int32, body.shape, 1)
    line = jnp.zeros(body.shape, F32)
    for q, value in enumerate(values):
        rest = value
        for piece in range(PIECES):
            part = rest.astype(BF16).astype(F32)
            rest = rest - part
            line = jnp.where(lanes == q * PIECES + piece, part, line)
    return jnp.where(rows == body.shape[0] - 1, line, body)


def read_scalars(refs, member, count):
    rows = refs[0].shape[1]
    tail = add([ref[member, rows - 16 : rows, 0:LANES] for ref in refs])
    sub = lax.broadcasted_iota(jnp.int32, tail.shape, 0)
    lanes = lax.broadcasted_iota(jnp.int32, tail.shape, 1)
    found = []
    for q in range(count):
        mine = (sub == 15) & (lanes >= q * PIECES) & (lanes < (q + 1) * PIECES)
        found.append(total(jnp.where(mine, tail, 0.0)))
    return found


def remainder(x, factor):
    return x - (x.astype(F32) * factor).astype(jnp.int32) * PRIME


def start_kernel(
    dims, seeds_in, ids_in, cols_in, count_in, sd_in, innov_in, prec_in, h, own, partner, *rest
):
    chips, halves, groups = dims
    outs = rest[:-12]
    seeds, ids, cols, count, sd, innov, prec, hashed, scratch, acc, sems, h_sems = rest[-12:]
    z, core, obs = place()
    blocks, lev, profiles = innov.shape
    colblocks, width = own.shape[1], own.shape[3]
    members, levp = scratch.shape[0], scratch.shape[1]

    pairs = [(seeds_in, seeds), (ids_in, ids), (cols_in, cols), (count_in, count), (sd_in, sd)]
    small = [pltpu.make_async_copy(x, y, sems.at[i]) for i, (x, y) in enumerate(pairs)]
    for copy in small:
        copy.start()
    large = []
    for b in range(blocks):
        at = len(pairs) + 2 * b
        large.append(pltpu.make_async_copy(innov_in.at[:, b, :], innov.at[b], sems.at[at]))
        large.append(pltpu.make_async_copy(prec_in.at[:, b, :], prec.at[b], sems.at[at + 1]))
    for copy in large:
        copy.start()
    own[...] = jnp.zeros_like(own)
    partner[...] = jnp.zeros_like(partner)
    scratch[...] = jnp.zeros_like(scratch)
    for copy in small:
        copy.wait()

    def tile_copy(n, half, target):
        lanes = pl.ds(half * width, width)
        return pltpu.make_async_copy(h.at[n, :, lanes], target, h_sems.at[n * halves + half])

    def put(n, carry):
        for half in range(halves):
            piece, k = ids[0, 0, n] * halves + half, cols[0, 0, n]

            @pl.when(piece % 2 == core)
            def _():
                tile_copy(n, half, own.at[piece // 2, k]).start()

            @pl.when(piece % 2 != core)
            def _():
                tile_copy(n, half, partner.at[piece // 2, k]).start()

        return carry

    lax.fori_loop(0, count[0, 0], put, 0)

    starts = [lax.rem(seeds[m], PRIME) for m in range(members)]
    order = [(source, zz) for source in range(2) for zz in range(chips)]
    shape = (levp, width)
    spot = lax.broadcasted_iota(jnp.int32, shape, 0) * profiles
    spot = spot + lax.broadcasted_iota(jnp.int32, shape, 1)
    for at, (source, zz) in enumerate(order):
        piece = 2 * zz + (core if source == 0 else 1 - core)
        first = (obs * blocks + piece // halves) * (lev * profiles) + (piece % halves) * width
        base = remainder(7919 * remainder(spot + first, 1.0 / PRIME), 1.0 / PRIME)
        for m in range(members):
            k0 = base + starts[m]
            k0 = jnp.where(k0 >= PRIME, k0 - PRIME, k0)
            k1 = remainder(k0 * k0 + 12345, 1.0 / PRIME)
            k2 = remainder(k1 * k1 + 2719, 1.0 / PRIME)
            k2 = jnp.where(k2 < 0, k2 + PRIME, k2)
            k2 = jnp.where(k2 >= PRIME, k2 - PRIME, k2)
            hashed[at, m] = k2.astype(F32)

    for copy in large:
        copy.wait()

    def arrive(n, carry):
        for half in range(halves):
            tile_copy(n, half, own.at[0, 0]).wait()
        return carry

    lax.fori_loop(0, count[0, 0], arrive, 0)

    for at, (source, zz) in enumerate(order):
        piece = 2 * zz + (core if source == 0 else 1 - core)
        b = piece // halves
        if halves == 1:
            p, d = prec[b], innov[b]
        else:
            lanes = pl.ds(pl.multiple_of((piece % halves) * width, LANES), width)
            p, d = prec[b, :, lanes], innov[b, :, lanes]
        gain = 3.4 * p * lax.rsqrt(p)
        offset = p * d - 0.5 * gain
        gain = gain * (1.0 / PRIME)
        for m in range(members):
            scratch[m, 0:lev, :] = offset + gain * hashed[at, m, 0:lev, :]
        w = scratch[...].astype(BF16).reshape(members * levp, width)
        tiles = (own if source == 0 else partner)[zz].reshape(colblocks * LANES, width)
        part = lax.dot_general(w, tiles, NT, preferred_element_type=F32)
        if at == 0:
            acc[...] = part
        else:
            acc[...] += part

    share = members // groups
    half = colblocks * LANES // 2
    for g in range(groups):
        for m in range(share):
            first = (g * share + m) * levp
            value = acc[first : first + levp, :]
            if m == 0:
                value = with_columns(value, jnp.concatenate([sd[...]] * colblocks, axis=1), obs)
            outs[2 * g][m] = value[:, :half].astype(BF16)
            outs[2 * g + 1][m] = value[:, half:].astype(BF16)


def with_columns(body, line, obs):
    rows = lax.broadcasted_iota(jnp.int32, body.shape, 0)
    mine = lax.broadcasted_iota(jnp.int32, body.shape, 1) // LANES == obs
    rest = line
    for piece in range(PIECES):
        part = rest.astype(BF16).astype(F32)
        rest = rest - part
        body = jnp.where((rows == body.shape[0] - 1 - PIECES + piece) & mine, part, body)
    return body


def read_columns(body):
    tail = body[body.shape[0] - 8 :]
    sub = lax.broadcasted_iota(jnp.int32, tail.shape, 0)
    mine = (sub >= 7 - PIECES) & (sub < 7)
    return jnp.sum(jnp.where(mine, tail, 0.0), axis=0, keepdims=True)


def precision_kernel(halves, prec, out):
    z, core, unused = place()
    piece = 2 * z + core
    lev, blocks, unused = prec.shape
    width = out.shape[1]
    block = lax.broadcasted_iota(jnp.int32, (lev, blocks, width), 1)
    if halves == 1:
        mine = prec[...]
    else:
        mine = prec[:, :, pl.ds(pl.multiple_of((piece % halves) * width, LANES), width)]
    out[...] = jnp.zeros_like(out)
    out[0:lev, :] = jnp.sum(jnp.where(block == piece // halves, mine, 0.0), axis=1)


def joined(refs, m):
    one, two = refs[: len(refs) // 2], refs[len(refs) // 2 :]
    return jnp.concatenate([add([x[m] for x in one]), add([x[m] for x in two])], axis=1)


def first_kernel(parts, *refs):
    pieces = refs[:parts]
    vert, vert_t, sd_out, residual, moved = refs[parts:]
    for m in range(residual.shape[0]):
        t = joined(pieces, m)
        if m == 0:
            sd = read_columns(t)
            sd_out[...] = sd
        r = dot(vert_t[...], sd * t)
        residual[m] = r
        x = sd * dot(vert[...], r)
        moved[m] = with_scalars(x, [total(r * r)]).astype(BF16)


def add_kernel(scalars, *refs):
    parts, out = refs[:-1], refs[-1]
    for m in range(out.shape[0]):
        value = add([x[m] for x in parts])
        if scalars:
            value = with_scalars(value, read_scalars(parts, m, scalars))
        out[m] = value.astype(BF16)


def add_halves_kernel(scalars, one, one_more, two, two_more, one_out, two_out):
    add_kernel(scalars, one, one_more, one_out)
    add_kernel(0, two, two_more, two_out)


def forward_kernel(mine, other, own, partner, *outs):
    z, core, obs = place()
    members, levp, lanes = mine.shape
    chips, width = own.shape[0], own.shape[3]
    rows = members * levp
    scalars = [read_scalars([mine, other], m, 2) for m in range(members)]
    order = [i for i in range(chips) if i % 2] + [i for i in range(chips) if i % 2 == 0]
    for i in order:
        zz = z ^ i
        y = jnp.dot(
            mine[...].reshape(rows, lanes),
            own[zz].reshape(lanes, width),
            preferred_element_type=F32,
        )
        y = y + jnp.dot(
            other[...].reshape(rows, lanes),
            partner[zz].reshape(lanes, width),
            preferred_element_type=F32,
        )
        y = y.reshape(members, levp, width)
        for m in range(members):
            outs[i][m] = with_scalars(y[m], scalars[m]).astype(outs[i].dtype)


def weigh_kernel(later, n_ys, *refs):
    ys, prec = refs[:n_ys], refs[n_ys]
    image, weighted, state = refs[-3:]
    p = prec[...]
    for m in range(image.shape[0]):
        y = add([x[m] for x in ys])
        norm, cross = read_scalars(ys, m, 2)
        if later:
            old_image, old = refs[n_ys + 1 : n_ys + 3]
            old_norm, old_square = old[m, 0:1, 0:1], old[m, 1:2, 0:1]
            beta = norm / old_norm
            square = norm + 2.0 * beta * cross + beta * beta * old_square
            y = y + beta * old_image[m]
        else:
            beta = jnp.zeros_like(norm)
            square = norm
        scaled = p * y
        image[m] = y
        weighted[m] = with_scalars(scaled, [total(scaled * y)]).astype(BF16)
        sub = lax.broadcasted_iota(jnp.int32, (8, LANES), 0)
        state[m] = jnp.where(sub == 0, norm, jnp.where(sub == 1, square, beta))


def adjoint_kernel(chips, kind, *refs):
    z, core, obs = place()
    ws, tiles = refs[:chips], refs[chips]
    members, levp, width = ws[0].shape
    lanes = tiles.shape[1] * LANES
    rows = members * levp
    acc = None
    for i in range(chips):
        part = lax.dot_general(
            ws[i][...].reshape(rows, width),
            tiles[z ^ i].reshape(lanes, width),
            NT,
            preferred_element_type=F32,
        )
        acc = part if i == 0 else acc + part
    acc = acc.reshape(members, levp, lanes)
    if kind == "theirs":
        (out,) = refs[chips + 1 :]
        for m in range(members):
            out[m] = with_scalars(acc[m], read_scalars(ws, m, 1)).astype(BF16)
        return
    more = refs[chips + 1]
    for m in range(members):
        (energy,) = read_scalars(ws, m, 1)
        energy = energy + read_scalars([more], m, 1)[0]
        value = acc[m] + more[m].astype(F32)
        if kind == "halves":
            one, two = refs[chips + 2 :]
            one[m] = with_scalars(value[:, : lanes // 2], [energy]).astype(BF16)
            two[m] = value[:, lanes // 2 :].astype(BF16)
        else:
            outs, scratch = refs[chips + 2 : -1], refs[-1]
            scratch[m] = value
            for i, out in enumerate(outs):
                lane = pl.ds(pl.multiple_of((obs ^ i) * LANES, LANES), LANES)
                out[m] = with_scalars(scratch[m, :, lane], [energy]).astype(BF16)


def update_kernel(parts, later, *refs):
    pieces, refs = refs[:parts], refs[parts:]
    sd, vert, vert_t, state, residual = refs[:5]
    if later:
        old_direction, old_solution, residual_out, solution_out, moved, direction_out = refs[5:]
    else:
        residual_out, solution_out, moved = refs[5:]
    obs = lax.axis_index("obs")
    mine = pl.ds(pl.multiple_of(obs * LANES, LANES), LANES)
    for m in range(residual.shape[0]):
        t = joined(pieces, m)
        (energy,) = read_scalars(pieces[: parts // 2], m, 1)
        norm, square, beta = state[m, 0:1, 0:1], state[m, 1:2, 0:1], state[m, 2:3, 0:1]
        alpha = norm / (square + energy)
        r = residual[m]
        if later:
            d = r + beta * old_direction[m]
            direction_out[m] = d
            step = direction_out[m, :, mine]
            solution_out[m] = old_solution[m] + alpha * step
        else:
            d = r
            solution_out[m] = alpha * residual[m, :, mine]
        r = r - alpha * (d + dot(vert_t[...], sd[...] * t))
        residual_out[m] = r
        x = sd[...] * dot(vert[...], r)
        moved[m] = with_scalars(x, [total(r * r), total(r * d)]).astype(BF16)


def last_kernel(parts, later, lev, *refs):
    pieces, refs = refs[:parts], refs[parts:]
    sd, vert, vert_t, state, residual = refs[:5]
    increment_out, residual_out = refs[-2:]
    obs = lax.axis_index("obs")
    mine = pl.ds(pl.multiple_of(obs * LANES, LANES), LANES)
    for m in range(residual.shape[0]):
        t = add([x[m] for x in pieces])
        (energy,) = read_scalars(pieces, m, 1)
        norm, square, beta = state[m, 0:1, 0:1], state[m, 1:2, 0:1], state[m, 2:3, 0:1]
        alpha = norm / (square + energy)
        d = r = residual[m, :, mine]
        if later:
            old_direction, old_solution = refs[5:7]
            d = r + beta * old_direction[m, :, mine]
        solution = alpha * d
        if later:
            solution = old_solution[m] + solution
        r = r - alpha * (d + dot(vert_t[...], sd[...] * t))
        increment = sd[...] * dot(vert[...], solution)
        increment_out[:, m, :] = increment[0:lev]
        residual_out[:, m, :] = r[0:lev]


def per_device(
    n_slab,
    n_obs,
    innovation,
    obs_precision,
    seeds,
    col_sd,
    vert_factor,
    h_values,
    block_obs,
    block_col,
    entry_count,
):
    blocks, lev, profiles = innovation.shape
    members = seeds.shape[0]
    groups, share = GROUPS, members // GROUPS
    chips = n_slab // 2
    halves = n_slab // blocks
    width = profiles // halves
    colblocks = n_obs
    assert halves * blocks == n_slab and width % LANES == 0 and col_sd.shape[0] == 1
    assert chips & (chips - 1) == 0 and n_obs & (n_obs - 1) == 0
    levp = (lev + 1 + 15) // 16 * 16
    rows = share * levp
    lanes = colblocks * LANES
    field = (share, levp, LANES)
    half_field = (share, levp, lanes // 2)
    slab_field = (share, levp, lanes)
    panel = (share, levp, width)
    pad = ((0, levp - lev), (0, levp - lev))
    vert = jnp.pad(vert_factor, pad)
    vert_t = jnp.pad(vert_factor.T, pad)
    h_block = h_values.reshape(h_values.shape[2:])
    innovation = jnp.transpose(innovation, (1, 0, 2))
    obs_precision = jnp.transpose(obs_precision, (1, 0, 2))
    product = n_slab * width * lanes * rows
    small = 12 * rows * levp * LANES
    line_bits = [1 << k for k in range(chips.bit_length() - 1)]
    plane_bits = [1 << k for k in range(n_obs.bit_length() - 1)]

    def along(x, i):
        return lax.ppermute(x, "slab", [(s, s ^ (2 * i)) for s in range(n_slab)])

    def plane(x, i):
        return lax.ppermute(x, "obs", [(o, o ^ i) for o in range(n_obs)])

    def swap(x):
        return lax.ppermute(x, "slab", [(s, s ^ 1) for s in range(n_slab)])

    def plane_sum(one, two, scalars):
        for step, bit in enumerate(plane_bits):
            far = plane_bits[len(plane_bits) - 1 - step]
            parts = [one, plane(one, bit), two, plane(two, far)]
            if step < len(plane_bits) - 1:
                one, two = call(
                    functools.partial(add_halves_kernel, scalars),
                    [struct(half_field, BF16)] * 2,
                    [],
                    0,
                    *parts,
                )
        return parts

    def line_sum(ys):
        parts = {i: [y] for i, y in enumerate(ys)}
        for bit in line_bits:
            sent = [i for i in parts if i & bit]
            for i in sorted(sent, reverse=True):
                y = parts.pop(i)
                if len(y) > 1:
                    y = call(
                        functools.partial(add_kernel, 2), [struct(panel, BF16)], [], 0, *y
                    )
                parts[i ^ bit].append(along(y[0], bit))
        return parts[0]

    def line_gather(w):
        held = {0: w}
        for bit in reversed(line_bits):
            held.update({i ^ bit: along(x, bit) for i, x in held.items()})
        return [held[i] for i in range(chips)]

    dense = struct((chips, colblocks, LANES, width), BF16)
    own, for_partner, *partials = call(
        functools.partial(start_kernel, (chips, halves, groups)),
        [dense, dense] + [struct(half_field, BF16)] * (2 * groups),
        [
            pltpu.SMEM(seeds.shape, jnp.int32),
            pltpu.SMEM(block_obs.shape, jnp.int32),
            pltpu.SMEM(block_col.shape, jnp.int32),
            pltpu.SMEM(entry_count.shape, jnp.int32),
            pltpu.VMEM(col_sd.shape, F32),
            pltpu.VMEM((blocks, lev, profiles), F32),
            pltpu.VMEM((blocks, lev, profiles), F32),
            pltpu.VMEM((n_slab, members, levp, width), F32),
            pltpu.VMEM((members, levp, width), F32),
            pltpu.VMEM((members * levp, lanes), F32),
            pltpu.SemaphoreType.DMA((5 + 2 * blocks,)),
            pltpu.SemaphoreType.DMA((h_block.shape[0] * halves,)),
        ],
        2 * product * groups,
        seeds,
        block_obs,
        block_col,
        entry_count,
        col_sd,
        innovation,
        obs_precision,
        h_block,
        space=HBM,
        limit=60,
    )
    arrived = [plane_sum(*partials[2 * g : 2 * g + 2], 0) for g in range(groups)]
    partner = swap(for_partner)
    (precision,) = call(
        functools.partial(precision_kernel, halves),
        [struct((levp, width), F32)],
        [],
        0,
        obs_precision,
    )
    state = [None] * groups
    direction = [None] * groups
    total_step = [None] * groups
    image = [None] * groups
    residual, moved, slab_sd, outputs = [], [], [], []
    for g in range(groups):
        sd, r, x = call(
            functools.partial(first_kernel, len(arrived[g])),
            [struct((1, lanes), F32), struct(slab_field, F32), struct(slab_field, BF16)],
            [],
            small * colblocks,
            *arrived[g],
            vert,
            vert_t,
        )
        slab_sd.append(sd)
        residual.append(r)
        moved.append(x)
    for sweep in range(ITERS):
        later, last = sweep > 0, sweep == ITERS - 1
        for g in range(groups):
            ys = call(
                forward_kernel,
                [struct(panel, BF16 if i % 2 else F32) for i in range(chips)],
                [],
                2 * product,
                moved[g],
                swap(moved[g]),
                own,
                partner,
            )
            ys = line_sum(ys)
            image[g], weighted, state[g] = call(
                functools.partial(weigh_kernel, later, len(ys)),
                [struct(panel, F32), struct(panel, BF16), struct((share, 8, LANES), F32)],
                [],
                0,
                *ys,
                precision,
                *([image[g], state[g]] if later else []),
            )
            ws = line_gather(weighted)
            (theirs,) = call(
                functools.partial(adjoint_kernel, chips, "theirs"),
                [struct(slab_field, BF16)],
                [],
                product,
                *ws,
                partner,
            )
            theirs = swap(theirs)
            old = [direction[g], total_step[g]] if later else []
            known = [vert, vert_t, state[g], residual[g], *old]
            if last:
                ps = call(
                    functools.partial(adjoint_kernel, chips, "columns"),
                    [struct(field, BF16)] * n_obs,
                    [pltpu.VMEM(slab_field, F32)],
                    product,
                    *ws,
                    own,
                    theirs,
                )
                ps = [x if i == 0 else plane(x, i) for i, x in enumerate(ps)]
                outputs.append(
                    call(
                        functools.partial(last_kernel, len(ps), later, lev),
                        [struct((lev, share, LANES), F32)] * 2,
                        [],
                        small,
                        *ps,
                        col_sd,
                        *known,
                    )
                )
                continue
            ps = call(
                functools.partial(adjoint_kernel, chips, "halves"),
                [struct(half_field, BF16)] * 2,
                [],
                product,
                *ws,
                own,
                theirs,
            )
            ps = plane_sum(*ps, 1)
            outs = [struct(slab_field, F32), struct(field, F32), struct(slab_field, BF16)]
            if later:
                outs.append(struct(slab_field, F32))
            r, total_step[g], moved[g], *d = call(
                functools.partial(update_kernel, len(ps), later),
                outs,
                [],
                small * colblocks,
                *ps,
                slab_sd[g],
                *known,
            )
            direction[g] = d[0] if later else residual[g]
            residual[g] = r
    outputs = [x[0] if groups == 1 else jnp.concatenate(x, axis=1) for x in zip(*outputs)]
    return tuple(jnp.transpose(x, (1, 0, 2))[None] for x in outputs)


def solution(mesh):
    return jax.shard_map(
        functools.partial(per_device, mesh.shape["slab"], mesh.shape["obs"]),
        mesh=mesh,
        in_specs=(
            P("obs", None, None),
            P("obs", None, None),
            P(),
            P(("slab", "obs"), None),
            P(),
            P("slab", "obs", None, None, None),
            P("slab", "obs", None),
            P("slab", "obs", None),
            P("slab", "obs"),
        ),
        out_specs=(P(("slab", "obs"), None, None, None), P(("slab", "obs"), None, None, None)),
        check_vma=False,
    )
```

time: 146 us -> 127 us (0.87)
  blocking collectives: 57.7 us -> 0 us
  waiting for transfers between devices: 51.2 us -> 79.3 us
  starting transfers between devices: 19 us -> 27.5 us
  local copies, waits for them, and re-layouts: 0.78 us -> 3.19 us
    all_to_all x5 -> x0, blocking collectives: 57.7 us -> none  [the longest x4 36.7 us: spread(): return [lax.all_to_all(outs[0], 'obs', 0, 0, tiled=True)]]
    ppermute x6 -> x12, waiting for transfers between devices: 20.8 us -> 49 us  [along(): return lax.ppermute(x, 'slab', [(s, s ^ 2 * i) for s in range(n_slab)])]
    all_to_all x2 -> x0, waiting for transfers between devices: 24 us -> none  [the longest x1 17.4 us: spread(): lax.all_to_all(outs[0], 'slab', 0, 0, axis_index_groups=cores, tiled=True)]
    ppermute x0 -> x11, waiting for transfers between devices: none -> 23.9 us  [plane(): return lax.ppermute(x, 'obs', [(o, o ^ i) for o in range(n_obs)])]
    ppermute x0 -> x11, starting transfers between devices: none -> 12.3 us  [plane(): return lax.ppermute(x, 'obs', [(o, o ^ i) for o in range(n_obs)])]
    all_to_all x2 -> x0, starting transfers between devices: 8.99 us -> none  [the longest x1 4.65 us: spread(): lax.all_to_all(outs[0], 'slab', 0, 0, axis_index_groups=cores, tiled=True)]
    ppermute x6 -> x12, starting transfers between devices: 8.84 us -> 14 us  [along(): return lax.ppermute(x, 'slab', [(s, s ^ 2 * i) for s in range(n_slab)])]
    unnamed x13 -> x15, local copies, waits for them, and re-layouts: 0.76 us -> 3.17 us
  transfers between devices with their start and end apart: 13 -> 28, of which waited for: 10 -> 27; matrix products, arithmetic and copies ran while one was open for 0% -> 0% of each run, Pallas kernels for 1% -> 1%
where the time goes in v5:
time: 127 us
  waiting for transfers between devices  79.3 us (62%)
  starting transfers between devices  27.5 us (22%)
  Pallas kernels  15 us (12%)
  local copies, waits for them, and re-layouts  3.19 us (3%)
  between operations  1.47 us (1%)
    ppermute x12, waiting for transfers between devices, along(): return lax.ppermute(x, 'slab', [(s, s ^ 2 * i) for s in range(n_slab)])  49 us
    ppermute x11, waiting for transfers between devices, plane(): return lax.ppermute(x, 'obs', [(o, o ^ i) for o in range(n_obs)])  23.9 us
    pallas_call x17, Pallas kernels, call(): pl.pallas_call(kernel, out_shape=outs, in_specs=[space] * len(args), out_...  15 us
    ppermute x12, starting transfers between devices, along(): return lax.ppermute(x, 'slab', [(s, s ^ 2 * i) for s in range(n_slab)])  14 us
    ppermute x11, starting transfers between devices, plane(): return lax.ppermute(x, 'obs', [(o, o ^ i) for o in range(n_obs)])  12.3 us
    ppermute x5, waiting for transfers between devices, swap(): return lax.ppermute(x, 'slab', [(s, s ^ 1) for s in range(n_slab)])  6.47 us
    unnamed x15, local copies, waits for them, and re-layouts  3.17 us
  transfers between devices with their start and end apart: 28, of which 27 were waited for; matrix products, arithmetic and copies ran while one was open for 0% of the time, Pallas kernels for 1%

profile of v5, /device:TPU:0, one launch (start us, length us, event | category | flops | bytes accessed | tf_op | source)
XLA Modules:
  0.0 126.5 jit_solution(16548755084044899665)
XLA Ops:
  1.3 5.7 %shard_map.104 = (bf16[4,4,128,256]{3,2,1,0:T(8,128)(2,1)}, bf16[4,4,128,256]{3,2,1,0:T(8,128)(2,1)}, bf16[4,80,256]{2,1,0:T(8,128)(2,1)}, bf16[4,80,256]{2,1,0:T(8,128)(2,1)}) custom-call(s32[4]{0:T(128)} %seeds_in.1, s32[1,1,32]{2,1,0:T(1,128)} %ids_in.1, s32[1,1,32]{2,1,0:T(1,128)} %cols_in.1, s32[1,1]{1,0:T(1,128)S(6)} %copy.12.count_in, ...), custom_call_target="tpu_custom_call" | custom-call | flops 671088640 | bytes 5751572 | tf_op jit(solution)/shard_map/pallas_call | solution.py:24
  8.0 2.3 %collective-permute-start = (bf16[4,80,256]{2,1,0:T(8,128)(2,1)}, bf16[4,80,256]{2,1,0:T(8,128)(2,1)S(1)}, u32[]{:S(2)}, u32[]{:S(2)}) collective-permute-start(bf16[4,80,256]{2,1,0:T(8,128)(2,1)} %get-tuple-element.37.one), channel_id=1, source_target_pairs={{0,1},{1,0},{2,3},{3,2},{4,5},{5,4},{6,7},{7,6},{8,9},{9,8},{10,11... | collective-permute-start | bytes 491528 | tf_op jit(solution)/shard_map/ppermute | solution.py:451
  10.3 1.5 %collective-permute-start.1 = (bf16[4,80,256]{2,1,0:T(8,128)(2,1)}, bf16[4,80,256]{2,1,0:T(8,128)(2,1)S(1)}, u32[]{:S(2)}, u32[]{:S(2)}) collective-permute-start(bf16[4,80,256]{2,1,0:T(8,128)(2,1)} %get-tuple-element.38.two), channel_id=1, source_target_pairs={{0,2},{1,3},{2,0},{3,1},{4,6},{5,7},{6,4},{7,5},{8,10},{9,11},{10,... | collective-permute-start | bytes 491528 | tf_op jit(solution)/shard_map/ppermute | solution.py:451
  11.8 3.3 %collective-permute-done.one_more = bf16[4,80,256]{2,1,0:T(8,128)(2,1)S(1)} collective-permute-done((bf16[4,80,256]{2,1,0:T(8,128)(2,1)}, bf16[4,80,256]{2,1,0:T(8,128)(2,1)S(1)}, u32[]{:S(2)}, u32[]{:S(2)}) %collective-permute-start) | collective-permute-done | bytes 163872 | tf_op jit(solution)/shard_map/ppermute | solution.py:451
  18.5 1.6 %collective-permute-start.2 = (bf16[4,80,256]{2,1,0:T(8,128)(2,1)S(1)}, bf16[4,80,256]{2,1,0:T(8,128)(2,1)S(1)}, u32[]{:S(2)}, u32[]{:S(2)}) collective-permute-start(bf16[4,80,256]{2,1,0:T(8,128)(2,1)S(1)} %get-tuple-element.39.refs_0_), channel_id=1, source_target_pairs={{0,2},{1,3},{2,0},{3,1},{4,6},{5,7},{6,4},{7,5},{8,10},{9,11},{10,... | collective-permute-start | bytes 491528 | tf_op jit(solution)/shard_map/ppermute | solution.py:451
  20.6 3.2 %collective-permute-done.2.refs_1_ = bf16[4,80,256]{2,1,0:T(8,128)(2,1)S(1)} collective-permute-done((bf16[4,80,256]{2,1,0:T(8,128)(2,1)S(1)}, bf16[4,80,256]{2,1,0:T(8,128)(2,1)S(1)}, u32[]{:S(2)}, u32[]{:S(2)}) %collective-permute-start.2) | collective-permute-done | bytes 163872 | tf_op jit(solution)/shard_map/ppermute | solution.py:451
  23.8 1.5 %collective-permute-done.3.refs_3_ = bf16[4,80,256]{2,1,0:T(8,128)(2,1)S(1)} collective-permute-done((bf16[4,80,256]{2,1,0:T(8,128)(2,1)S(1)}, bf16[4,80,256]{2,1,0:T(8,128)(2,1)S(1)}, u32[]{:S(2)}, u32[]{:S(2)}) %collective-permute-start.3) | collective-permute-done | bytes 163872 | tf_op jit(solution)/shard_map/ppermute | solution.py:451
  26.7 1.6 %collective-permute-done.4.other = bf16[4,80,512]{2,1,0:T(8,128)(2,1)S(1)} collective-permute-done((bf16[4,80,512]{2,1,0:T(8,128)(2,1)S(1)}, bf16[4,80,512]{2,1,0:T(8,128)(2,1)S(1)}, u32[]{:S(2)}, u32[]{:S(2)}) %collective-permute-start.4) | collective-permute-done | bytes 327712 | tf_op jit(solution)/shard_map/ppermute | solution.py:454
  30.4 2.1 %collective-permute-start.7 = (bf16[4,80,256]{2,1,0:T(8,128)(2,1)S(1)}, bf16[4,80,256]{2,1,0:T(8,128)(2,1)S(1)}, u32[]{:S(2)}, u32[]{:S(2)}) collective-permute-start(bf16[4,80,256]{2,1,0:T(8,128)(2,1)S(1)} %get-tuple-element.47), channel_id=1, source_target_pairs={{0,8},{4,12},{8,0},{12,4},{16,24},{20,28},{24,16},{28,20},{1,9},{5... | collective-permute-start | bytes 491528 | tf_op jit(solution)/shard_map/ppermute | solution.py:448
  32.6 4.9 %collective-permute-done.7.refs_1_ = bf16[4,80,256]{2,1,0:T(8,128)(2,1)S(1)} collective-permute-done((bf16[4,80,256]{2,1,0:T(8,128)(2,1)S(1)}, bf16[4,80,256]{2,1,0:T(8,128)(2,1)S(1)}, u32[]{:S(2)}, u32[]{:S(2)}) %collective-permute-start.7) | collective-permute-done | bytes 163872 | tf_op jit(solution)/shard_map/ppermute | solution.py:448
  37.6 2.6 %collective-permute-start.8 = (bf16[4,80,256]{2,1,0:T(8,128)(2,1)S(1)}, bf16[4,80,256]{2,1,0:T(8,128)(2,1)S(1)}, u32[]{:S(2)}, u32[]{:S(2)}) collective-permute-start(bf16[4,80,256]{2,1,0:T(8,128)(2,1)S(1)} %shard_map.108), channel_id=1, source_target_pairs={{0,16},{4,20},{8,24},{12,28},{16,0},{20,4},{24,8},{28,12},{1,17},{... | collective-permute-start | bytes 491528 | tf_op jit(solution)/shard_map/ppermute | solution.py:448
  41.8 5.6 %collective-permute-done.8.refs_2_ = bf16[4,80,256]{2,1,0:T(8,128)(2,1)S(1)} collective-permute-done((bf16[4,80,256]{2,1,0:T(8,128)(2,1)S(1)}, bf16[4,80,256]{2,1,0:T(8,128)(2,1)S(1)}, u32[]{:S(2)}, u32[]{:S(2)}) %collective-permute-start.8) | collective-permute-done | bytes 163872 | tf_op jit(solution)/shard_map/ppermute | solution.py:448
  47.6 3.5 %collective-permute-start.9 = (bf16[4,80,256]{2,1,0:T(8,128)(2,1)S(1)}, bf16[4,80,256]{2,1,0:T(8,128)(2,1)S(1)}, u32[]{:S(2)}, u32[]{:S(2)}) collective-permute-start(bf16[4,80,256]{2,1,0:T(8,128)(2,1)S(1)} %get-tuple-element.48.refs_0_), channel_id=1, source_target_pairs={{0,8},{4,12},{8,0},{12,4},{16,24},{20,28},{24,16},{28,20},{1,9},{5... | collective-permute-start | bytes 491528 | tf_op jit(solution)/shard_map/ppermute | solution.py:448
  51.1 5.8 %collective-permute-done.10.refs_2_ = bf16[4,80,256]{2,1,0:T(8,128)(2,1)S(1)} collective-permute-done((bf16[4,80,256]{2,1,0:T(8,128)(2,1)S(1)}, bf16[4,80,256]{2,1,0:T(8,128)(2,1)S(1)}, u32[]{:S(2)}, u32[]{:S(2)}) %collective-permute-start.10) | collective-permute-done | bytes 163872 | tf_op jit(solution)/shard_map/ppermute | solution.py:448
  57.0 5.2 %collective-permute-done.11.refs_3_ = bf16[4,80,256]{2,1,0:T(8,128)(2,1)S(1)} collective-permute-done((bf16[4,80,256]{2,1,0:T(8,128)(2,1)S(1)}, bf16[4,80,256]{2,1,0:T(8,128)(2,1)S(1)}, u32[]{:S(2)}, u32[]{:S(2)}) %collective-permute-start.11) | collective-permute-done | bytes 163872 | tf_op jit(solution)/shard_map/ppermute | solution.py:448
  62.8 1.6 %collective-permute-done.12.refs_5_ = bf16[4,80,512]{2,1,0:T(8,128)(2,1)S(1)} collective-permute-done((bf16[4,80,512]{2,1,0:T(8,128)(2,1)S(1)}, bf16[4,80,512]{2,1,0:T(8,128)(2,1)S(1)}, u32[]{:S(2)}, u32[]{:S(2)}) %collective-permute-start.12) | collective-permute-done | bytes 327712 | tf_op jit(solution)/shard_map/ppermute | solution.py:454
  65.8 5.5 %collective-permute-done.13.one_more = bf16[4,80,256]{2,1,0:T(8,128)(2,1)S(1)} collective-permute-done((bf16[4,80,256]{2,1,0:T(8,128)(2,1)S(1)}, bf16[4,80,256]{2,1,0:T(8,128)(2,1)S(1)}, u32[]{:S(2)}, u32[]{:S(2)}) %collective-permute-start.13) | collective-permute-done | bytes 163872 | tf_op jit(solution)/shard_map/ppermute | solution.py:451
  71.9 1.6 %collective-permute-start.16 = (bf16[4,80,256]{2,1,0:T(8,128)(2,1)S(1)}, bf16[4,80,256]{2,1,0:T(8,128)(2,1)S(1)}, u32[]{:S(2)}, u32[]{:S(2)}) collective-permute-start(bf16[4,80,256]{2,1,0:T(8,128)(2,1)S(1)} %get-tuple-element.52.refs_2_), channel_id=1, source_target_pairs={{0,1},{1,0},{2,3},{3,2},{4,5},{5,4},{6,7},{7,6},{8,9},{9,8},{10,11... | collective-permute-start | bytes 491528 | tf_op jit(solution)/shard_map/ppermute | solution.py:451
  73.5 3.4 %collective-permute-done.15.refs_1_ = bf16[4,80,256]{2,1,0:T(8,128)(2,1)S(1)} collective-permute-done((bf16[4,80,256]{2,1,0:T(8,128)(2,1)S(1)}, bf16[4,80,256]{2,1,0:T(8,128)(2,1)S(1)}, u32[]{:S(2)}, u32[]{:S(2)}) %collective-permute-start.15) | collective-permute-done | bytes 163872 | tf_op jit(solution)/shard_map/ppermute | solution.py:451
  78.6 1.6 %collective-permute-done.17.other = bf16[4,80,512]{2,1,0:T(8,128)(2,1)S(1)} collective-permute-done((bf16[4,80,512]{2,1,0:T(8,128)(2,1)S(1)}, bf16[4,80,512]{2,1,0:T(8,128)(2,1)S(1)}, u32[]{:S(2)}, u32[]{:S(2)}) %collective-permute-start.17) | collective-permute-done | bytes 327712 | tf_op jit(solution)/shard_map/ppermute | solution.py:454
  81.2 2.0 %collective-permute-start.18 = (bf16[4,80,256]{2,1,0:T(8,128)(2,1)S(1)}, bf16[4,80,256]{2,1,0:T(8,128)(2,1)S(1)}, u32[]{:S(2)}, u32[]{:S(2)}) collective-permute-start(bf16[4,80,256]{2,1,0:T(8,128)(2,1)S(1)} %get-tuple-element.58), channel_id=1, source_target_pairs={{0,8},{4,12},{8,0},{12,4},{16,24},{20,28},{24,16},{28,20},{1,9},{5... | collective-permute-start | bytes 491528 | tf_op jit(solution)/shard_map/ppermute | solution.py:448
  83.2 5.0 %collective-permute-done.19.refs_1_ = bf16[4,80,256]{2,1,0:T(8,128)(2,1)S(1)} collective-permute-done((bf16[4,80,256]{2,1,0:T(8,128)(2,1)S(1)}, bf16[4,80,256]{2,1,0:T(8,128)(2,1)S(1)}, u32[]{:S(2)}, u32[]{:S(2)}) %collective-permute-start.19) | collective-permute-done | bytes 163872 | tf_op jit(solution)/shard_map/ppermute | solution.py:448
  89.2 2.4 %collective-permute-done.18.refs_1_ = bf16[4,80,256]{2,1,0:T(8,128)(2,1)S(1)} collective-permute-done((bf16[4,80,256]{2,1,0:T(8,128)(2,1)S(1)}, bf16[4,80,256]{2,1,0:T(8,128)(2,1)S(1)}, u32[]{:S(2)}, u32[]{:S(2)}) %collective-permute-start.18) | collective-permute-done | bytes 163872 | tf_op jit(solution)/shard_map/ppermute | solution.py:448
  91.6 5.8 %collective-permute-done.20.refs_2_ = bf16[4,80,256]{2,1,0:T(8,128)(2,1)S(1)} collective-permute-done((bf16[4,80,256]{2,1,0:T(8,128)(2,1)S(1)}, bf16[4,80,256]{2,1,0:T(8,128)(2,1)S(1)}, u32[]{:S(2)}, u32[]{:S(2)}) %collective-permute-start.20) | collective-permute-done | bytes 163872 | tf_op jit(solution)/shard_map/ppermute | solution.py:448
  98.3 2.6 %collective-permute-start.21 = (bf16[4,80,256]{2,1,0:T(8,128)(2,1)S(1)}, bf16[4,80,256]{2,1,0:T(8,128)(2,1)S(1)}, u32[]{:S(2)}, u32[]{:S(2)}) collective-permute-start(bf16[4,80,256]{2,1,0:T(8,128)(2,1)S(1)} %get-tuple-element.62.refs_0_), channel_id=1, source_target_pairs={{0,8},{4,12},{8,0},{12,4},{16,24},{20,28},{24,16},{28,20},{1,9},{5... | collective-permute-start | bytes 491528 | tf_op jit(solution)/shard_map/ppermute | solution.py:448
  100.9 6.8 %collective-permute-done.22.refs_2_ = bf16[4,80,256]{2,1,0:T(8,128)(2,1)S(1)} collective-permute-done((bf16[4,80,256]{2,1,0:T(8,128)(2,1)S(1)}, bf16[4,80,256]{2,1,0:T(8,128)(2,1)S(1)}, u32[]{:S(2)}, u32[]{:S(2)}) %collective-permute-start.22) | collective-permute-done | bytes 163872 | tf_op jit(solution)/shard_map/ppermute | solution.py:448
  107.9 5.9 %collective-permute-done.23.refs_3_ = bf16[4,80,256]{2,1,0:T(8,128)(2,1)S(1)} collective-permute-done((bf16[4,80,256]{2,1,0:T(8,128)(2,1)S(1)}, bf16[4,80,256]{2,1,0:T(8,128)(2,1)S(1)}, u32[]{:S(2)}, u32[]{:S(2)}) %collective-permute-start.23) | collective-permute-done | bytes 163872 | tf_op jit(solution)/shard_map/ppermute | solution.py:448
  114.4 1.6 %collective-permute-done.24.refs_5_ = bf16[4,80,512]{2,1,0:T(8,128)(2,1)S(1)} collective-permute-done((bf16[4,80,512]{2,1,0:T(8,128)(2,1)S(1)}, bf16[4,80,512]{2,1,0:T(8,128)(2,1)S(1)}, u32[]{:S(2)}, u32[]{:S(2)}) %collective-permute-start.24) | collective-permute-done | bytes 327712 | tf_op jit(solution)/shard_map/ppermute | solution.py:454
  116.7 1.7 %collective-permute-start.25 = (bf16[4,80,128]{2,1,0:T(8,128)(2,1)S(1)}, bf16[4,80,128]{2,1,0:T(8,128)(2,1)S(1)}, u32[]{:S(2)}, u32[]{:S(2)}) collective-permute-start(bf16[4,80,128]{2,1,0:T(8,128)(2,1)S(1)} %get-tuple-element.64), channel_id=1, source_target_pairs={{0,1},{1,0},{2,3},{3,2},{4,5},{5,4},{6,7},{7,6},{8,9},{9,8},{10,11... | collective-permute-start | bytes 245768 | tf_op jit(solution)/shard_map/ppermute | solution.py:451
  118.4 1.5 %collective-permute-start.26 = (bf16[4,80,128]{2,1,0:T(8,128)(2,1)S(1)}, bf16[4,80,128]{2,1,0:T(8,128)(2,1)S(1)}, u32[]{:S(2)}, u32[]{:S(2)}) collective-permute-start(bf16[4,80,128]{2,1,0:T(8,128)(2,1)S(1)} %get-tuple-element.65), channel_id=1, source_target_pairs={{0,2},{1,3},{2,0},{3,1},{4,6},{5,7},{6,4},{7,5},{8,10},{9,11},{10,... | collective-permute-start | bytes 245768 | tf_op jit(solution)/shard_map/ppermute | solution.py:451
  121.2 2.5 %collective-permute-done.26.refs_2_ = bf16[4,80,128]{2,1,0:T(8,128)(2,1)S(1)} collective-permute-done((bf16[4,80,128]{2,1,0:T(8,128)(2,1)S(1)}, bf16[4,80,128]{2,1,0:T(8,128)(2,1)S(1)}, u32[]{:S(2)}, u32[]{:S(2)}) %collective-permute-start.26) | collective-permute-done | bytes 81952 | tf_op jit(solution)/shard_map/ppermute | solution.py:451
  123.7 1.6 %collective-permute-done.27.refs_3_ = bf16[4,80,128]{2,1,0:T(8,128)(2,1)S(1)} collective-permute-done((bf16[4,80,128]{2,1,0:T(8,128)(2,1)S(1)}, bf16[4,80,128]{2,1,0:T(8,128)(2,1)S(1)}, u32[]{:S(2)}, u32[]{:S(2)}) %collective-permute-start.27) | collective-permute-done | bytes 81952 | tf_op jit(solution)/shard_map/ppermute | solution.py:451
  (58 shorter events, 21.5 us)
Async XLA Ops:
  0.6 19.9 %copy-start.6 = (f32[75,75]{1,0:T(8,128)S(1)}, f32[75,75]{1,0:T(8,128)}, u32[]{:S(2)}) copy-start(f32[75,75]{1,0:T(8,128)} %param.13) | copy-start | bytes 67504
  7.0 21.3 %collective-permute-start.5 = (bf16[4,4,128,256]{3,2,1,0:T(8,128)(2,1)}, bf16[4,4,128,256]{3,2,1,0:T(8,128)(2,1)S(1)}, u32[]{:S(2)}, u32[]{:S(2)}) collective-permute-start(bf16[4,4,128,256]{3,2,1,0:T(8,128)(2,1)} %get-tuple-element.43), channel_id=1, source_target_pairs={{0,4},{4,0},{8,12},{12,8},{16,20},{20,16},{24,28},{28,24},{1,5},{5... | collective-permute-start | bytes 3145736 | tf_op jit(solution)/shard_map/ppermute | solution.py:454
  8.0 7.1 %collective-permute-start = (bf16[4,80,256]{2,1,0:T(8,128)(2,1)}, bf16[4,80,256]{2,1,0:T(8,128)(2,1)S(1)}, u32[]{:S(2)}, u32[]{:S(2)}) collective-permute-start(bf16[4,80,256]{2,1,0:T(8,128)(2,1)} %get-tuple-element.37.one), channel_id=1, source_target_pairs={{0,1},{1,0},{2,3},{3,2},{4,5},{5,4},{6,7},{7,6},{8,9},{9,8},{10,11... | collective-permute-start | bytes 491528 | tf_op jit(solution)/shard_map/ppermute | solution.py:451
  10.3 6.2 %collective-permute-start.1 = (bf16[4,80,256]{2,1,0:T(8,128)(2,1)}, bf16[4,80,256]{2,1,0:T(8,128)(2,1)S(1)}, u32[]{:S(2)}, u32[]{:S(2)}) collective-permute-start(bf16[4,80,256]{2,1,0:T(8,128)(2,1)} %get-tuple-element.38.two), channel_id=1, source_target_pairs={{0,2},{1,3},{2,0},{3,1},{4,6},{5,7},{6,4},{7,5},{8,10},{9,11},{10,... | collective-permute-start | bytes 491528 | tf_op jit(solution)/shard_map/ppermute | solution.py:451
  18.5 5.4 %collective-permute-start.2 = (bf16[4,80,256]{2,1,0:T(8,128)(2,1)S(1)}, bf16[4,80,256]{2,1,0:T(8,128)(2,1)S(1)}, u32[]{:S(2)}, u32[]{:S(2)}) collective-permute-start(bf16[4,80,256]{2,1,0:T(8,128)(2,1)S(1)} %get-tuple-element.39.refs_0_), channel_id=1, source_target_pairs={{0,2},{1,3},{2,0},{3,1},{4,6},{5,7},{6,4},{7,5},{8,10},{9,11},{10,... | collective-permute-start | bytes 491528 | tf_op jit(solution)/shard_map/ppermute | solution.py:451
  20.0 5.3 %collective-permute-start.3 = (bf16[4,80,256]{2,1,0:T(8,128)(2,1)S(1)}, bf16[4,80,256]{2,1,0:T(8,128)(2,1)S(1)}, u32[]{:S(2)}, u32[]{:S(2)}) collective-permute-start(bf16[4,80,256]{2,1,0:T(8,128)(2,1)S(1)} %get-tuple-element.40.refs_2_), channel_id=1, source_target_pairs={{0,1},{1,0},{2,3},{3,2},{4,5},{5,4},{6,7},{7,6},{8,9},{9,8},{10,11... | collective-permute-start | bytes 491528 | tf_op jit(solution)/shard_map/ppermute | solution.py:451
  20.6 19.6 %copy-start.2 = (f32[8,75,256]{2,0,1:T(8,128)S(1)}, f32[8,75,256]{2,0,1:T(8,128)}, u32[]{:S(2)}) copy-start(f32[8,75,256]{2,0,1:T(8,128)} %param.10) | copy-start | bytes 1843204
  26.6 1.7 %collective-permute-start.4 = (bf16[4,80,512]{2,1,0:T(8,128)(2,1)S(1)}, bf16[4,80,512]{2,1,0:T(8,128)(2,1)S(1)}, u32[]{:S(2)}, u32[]{:S(2)}) collective-permute-start(bf16[4,80,512]{2,1,0:T(8,128)(2,1)S(1)} %get-tuple-element.41.mine), channel_id=1, source_target_pairs={{0,4},{4,0},{8,12},{12,8},{16,20},{20,16},{24,28},{28,24},{1,5},{5... | collective-permute-start | bytes 983048 | tf_op jit(solution)/shard_map/ppermute | solution.py:454
  30.3 34.0 %copy-start.1 = (bf16[4,4,128,256]{3,2,1,0:T(8,128)(2,1)S(1)}, bf16[4,4,128,256]{3,2,1,0:T(8,128)(2,1)}, u32[]{:S(2)}) copy-start(bf16[4,4,128,256]{3,2,1,0:T(8,128)(2,1)} %get-tuple-element.42.own.refs_4_) | copy-start | bytes 3145732
  30.4 7.1 %collective-permute-start.7 = (bf16[4,80,256]{2,1,0:T(8,128)(2,1)S(1)}, bf16[4,80,256]{2,1,0:T(8,128)(2,1)S(1)}, u32[]{:S(2)}, u32[]{:S(2)}) collective-permute-start(bf16[4,80,256]{2,1,0:T(8,128)(2,1)S(1)} %get-tuple-element.47), channel_id=1, source_target_pairs={{0,8},{4,12},{8,0},{12,4},{16,24},{20,28},{24,16},{28,20},{1,9},{5... | collective-permute-start | bytes 491528 | tf_op jit(solution)/shard_map/ppermute | solution.py:448
  32.5 9.3 %collective-permute-start.6 = (bf16[4,80,256]{2,1,0:T(8,128)(2,1)S(1)}, bf16[4,80,256]{2,1,0:T(8,128)(2,1)S(1)}, u32[]{:S(2)}, u32[]{:S(2)}) collective-permute-start(bf16[4,80,256]{2,1,0:T(8,128)(2,1)S(1)} %get-tuple-element.45), channel_id=1, source_target_pairs={{0,8},{4,12},{8,0},{12,4},{16,24},{20,28},{24,16},{28,20},{1,9},{5... | collective-permute-start | bytes 491528 | tf_op jit(solution)/shard_map/ppermute | solution.py:448
  37.6 9.8 %collective-permute-start.8 = (bf16[4,80,256]{2,1,0:T(8,128)(2,1)S(1)}, bf16[4,80,256]{2,1,0:T(8,128)(2,1)S(1)}, u32[]{:S(2)}, u32[]{:S(2)}) collective-permute-start(bf16[4,80,256]{2,1,0:T(8,128)(2,1)S(1)} %shard_map.108), channel_id=1, source_target_pairs={{0,16},{4,20},{8,24},{12,28},{16,0},{20,4},{24,8},{28,12},{1,17},{... | collective-permute-start | bytes 491528 | tf_op jit(solution)/shard_map/ppermute | solution.py:448
  47.5 9.3 %collective-permute-start.10 = (bf16[4,80,256]{2,1,0:T(8,128)(2,1)S(1)}, bf16[4,80,256]{2,1,0:T(8,128)(2,1)S(1)}, u32[]{:S(2)}, u32[]{:S(2)}) collective-permute-start(bf16[4,80,256]{2,1,0:T(8,128)(2,1)S(1)} %get-tuple-element.48.refs_0_), channel_id=1, source_target_pairs={{0,16},{4,20},{8,24},{12,28},{16,0},{20,4},{24,8},{28,12},{1,17},{... | collective-permute-start | bytes 491528 | tf_op jit(solution)/shard_map/ppermute | solution.py:448
  47.6 9.4 %collective-permute-start.9 = (bf16[4,80,256]{2,1,0:T(8,128)(2,1)S(1)}, bf16[4,80,256]{2,1,0:T(8,128)(2,1)S(1)}, u32[]{:S(2)}, u32[]{:S(2)}) collective-permute-start(bf16[4,80,256]{2,1,0:T(8,128)(2,1)S(1)} %get-tuple-element.48.refs_0_), channel_id=1, source_target_pairs={{0,8},{4,12},{8,0},{12,4},{16,24},{20,28},{24,16},{28,20},{1,9},{5... | collective-permute-start | bytes 491528 | tf_op jit(solution)/shard_map/ppermute | solution.py:448
  56.8 5.3 %collective-permute-start.11 = (bf16[4,80,256]{2,1,0:T(8,128)(2,1)S(1)}, bf16[4,80,256]{2,1,0:T(8,128)(2,1)S(1)}, u32[]{:S(2)}, u32[]{:S(2)}) collective-permute-start(bf16[4,80,256]{2,1,0:T(8,128)(2,1)S(1)} %collective-permute-done.10.refs_2_), channel_id=1, source_target_pairs={{0,8},{4,12},{8,0},{12,4},{16,24},{20,28},{24,16},{28,20},{1,9},{5... | collective-permute-start | bytes 491528 | tf_op jit(solution)/shard_map/ppermute | solution.py:448
  62.7 1.7 %collective-permute-start.12 = (bf16[4,80,512]{2,1,0:T(8,128)(2,1)S(1)}, bf16[4,80,512]{2,1,0:T(8,128)(2,1)S(1)}, u32[]{:S(2)}, u32[]{:S(2)}) collective-permute-start(bf16[4,80,512]{2,1,0:T(8,128)(2,1)S(1)} %shard_map.111), channel_id=1, source_target_pairs={{0,4},{4,0},{8,12},{12,8},{16,20},{20,16},{24,28},{28,24},{1,5},{5... | collective-permute-start | bytes 983048 | tf_op jit(solution)/shard_map/ppermute | solution.py:454
  64.9 6.3 %collective-permute-start.13 = (bf16[4,80,256]{2,1,0:T(8,128)(2,1)S(1)}, bf16[4,80,256]{2,1,0:T(8,128)(2,1)S(1)}, u32[]{:S(2)}, u32[]{:S(2)}) collective-permute-start(bf16[4,80,256]{2,1,0:T(8,128)(2,1)S(1)} %get-tuple-element.49.one), channel_id=1, source_target_pairs={{0,1},{1,0},{2,3},{3,2},{4,5},{5,4},{6,7},{7,6},{8,9},{9,8},{10,11... | collective-permute-start | bytes 491528 | tf_op jit(solution)/shard_map/ppermute | solution.py:451
  65.5 6.0 %collective-permute-start.14 = (bf16[4,80,256]{2,1,0:T(8,128)(2,1)S(1)}, bf16[4,80,256]{2,1,0:T(8,128)(2,1)S(1)}, u32[]{:S(2)}, u32[]{:S(2)}) collective-permute-start(bf16[4,80,256]{2,1,0:T(8,128)(2,1)S(1)} %get-tuple-element.50.two), channel_id=1, source_target_pairs={{0,2},{1,3},{2,0},{3,1},{4,6},{5,7},{6,4},{7,5},{8,10},{9,11},{10,... | collective-permute-start | bytes 491528 | tf_op jit(solution)/shard_map/ppermute | solution.py:451
  71.5 5.4 %collective-permute-start.15 = (bf16[4,80,256]{2,1,0:T(8,128)(2,1)S(1)}, bf16[4,80,256]{2,1,0:T(8,128)(2,1)S(1)}, u32[]{:S(2)}, u32[]{:S(2)}) collective-permute-start(bf16[4,80,256]{2,1,0:T(8,128)(2,1)S(1)} %get-tuple-element.51.refs_0_), channel_id=1, source_target_pairs={{0,2},{1,3},{2,0},{3,1},{4,6},{5,7},{6,4},{7,5},{8,10},{9,11},{10,... | collective-permute-start | bytes 491528 | tf_op jit(solution)/shard_map/ppermute | solution.py:451
  71.9 5.3 %collective-permute-start.16 = (bf16[4,80,256]{2,1,0:T(8,128)(2,1)S(1)}, bf16[4,80,256]{2,1,0:T(8,128)(2,1)S(1)}, u32[]{:S(2)}, u32[]{:S(2)}) collective-permute-start(bf16[4,80,256]{2,1,0:T(8,128)(2,1)S(1)} %get-tuple-element.52.refs_2_), channel_id=1, source_target_pairs={{0,1},{1,0},{2,3},{3,2},{4,5},{5,4},{6,7},{7,6},{8,9},{9,8},{10,11... | collective-permute-start | bytes 491528 | tf_op jit(solution)/shard_map/ppermute | solution.py:451
  78.6 1.7 %collective-permute-start.17 = (bf16[4,80,512]{2,1,0:T(8,128)(2,1)S(1)}, bf16[4,80,512]{2,1,0:T(8,128)(2,1)S(1)}, u32[]{:S(2)}, u32[]{:S(2)}) collective-permute-start(bf16[4,80,512]{2,1,0:T(8,128)(2,1)S(1)} %get-tuple-element.56.mine), channel_id=1, source_target_pairs={{0,4},{4,0},{8,12},{12,8},{16,20},{20,16},{24,28},{28,24},{1,5},{5... | collective-permute-start | bytes 983048 | tf_op jit(solution)/shard_map/ppermute | solution.py:454
  81.1 7.1 %collective-permute-start.19 = (bf16[4,80,256]{2,1,0:T(8,128)(2,1)S(1)}, bf16[4,80,256]{2,1,0:T(8,128)(2,1)S(1)}, u32[]{:S(2)}, u32[]{:S(2)}) collective-permute-start(bf16[4,80,256]{2,1,0:T(8,128)(2,1)S(1)} %get-tuple-element.60), channel_id=1, source_target_pairs={{0,8},{4,12},{8,0},{12,4},{16,24},{20,28},{24,16},{28,20},{1,9},{5... | collective-permute-start | bytes 491528 | tf_op jit(solution)/shard_map/ppermute | solution.py:448
  81.2 10.4 %collective-permute-start.18 = (bf16[4,80,256]{2,1,0:T(8,128)(2,1)S(1)}, bf16[4,80,256]{2,1,0:T(8,128)(2,1)S(1)}, u32[]{:S(2)}, u32[]{:S(2)}) collective-permute-start(bf16[4,80,256]{2,1,0:T(8,128)(2,1)S(1)} %get-tuple-element.58), channel_id=1, source_target_pairs={{0,8},{4,12},{8,0},{12,4},{16,24},{20,28},{24,16},{28,20},{1,9},{5... | collective-permute-start | bytes 491528 | tf_op jit(solution)/shard_map/ppermute | solution.py:448
  88.3 9.1 %collective-permute-start.20 = (bf16[4,80,256]{2,1,0:T(8,128)(2,1)S(1)}, bf16[4,80,256]{2,1,0:T(8,128)(2,1)S(1)}, u32[]{:S(2)}, u32[]{:S(2)}) collective-permute-start(bf16[4,80,256]{2,1,0:T(8,128)(2,1)S(1)} %shard_map.116), channel_id=1, source_target_pairs={{0,16},{4,20},{8,24},{12,28},{16,0},{20,4},{24,8},{28,12},{1,17},{... | collective-permute-start | bytes 491528 | tf_op jit(solution)/shard_map/ppermute | solution.py:448
  98.3 27.0 %copy-start.5 = (f32[1,128]{1,0:T(1,128)S(1)}, f32[1,128]{1,0:T(1,128)}, u32[]{:S(2)}) copy-start(f32[1,128]{1,0:T(1,128)} %refs_4_.1) | copy-start | bytes 1540
  98.3 9.4 %collective-permute-start.22 = (bf16[4,80,256]{2,1,0:T(8,128)(2,1)S(1)}, bf16[4,80,256]{2,1,0:T(8,128)(2,1)S(1)}, u32[]{:S(2)}, u32[]{:S(2)}) collective-permute-start(bf16[4,80,256]{2,1,0:T(8,128)(2,1)S(1)} %get-tuple-element.62.refs_0_), channel_id=1, source_target_pairs={{0,16},{4,20},{8,24},{12,28},{16,0},{20,4},{24,8},{28,12},{1,17},{... | collective-permute-start | bytes 491528 | tf_op jit(solution)/shard_map/ppermute | solution.py:448
  98.3 9.6 %collective-permute-start.21 = (bf16[4,80,256]{2,1,0:T(8,128)(2,1)S(1)}, bf16[4,80,256]{2,1,0:T(8,128)(2,1)S(1)}, u32[]{:S(2)}, u32[]{:S(2)}) collective-permute-start(bf16[4,80,256]{2,1,0:T(8,128)(2,1)S(1)} %get-tuple-element.62.refs_0_), channel_id=1, source_target_pairs={{0,8},{4,12},{8,0},{12,4},{16,24},{20,28},{24,16},{28,20},{1,9},{5... | collective-permute-start | bytes 491528 | tf_op jit(solution)/shard_map/ppermute | solution.py:448
  107.7 6.1 %collective-permute-start.23 = (bf16[4,80,256]{2,1,0:T(8,128)(2,1)S(1)}, bf16[4,80,256]{2,1,0:T(8,128)(2,1)S(1)}, u32[]{:S(2)}, u32[]{:S(2)}) collective-permute-start(bf16[4,80,256]{2,1,0:T(8,128)(2,1)S(1)} %collective-permute-done.22.refs_2_), channel_id=1, source_target_pairs={{0,8},{4,12},{8,0},{12,4},{16,24},{20,28},{24,16},{28,20},{1,9},{5... | collective-permute-start | bytes 491528 | tf_op jit(solution)/shard_map/ppermute | solution.py:448
  114.3 1.7 %collective-permute-start.24 = (bf16[4,80,512]{2,1,0:T(8,128)(2,1)S(1)}, bf16[4,80,512]{2,1,0:T(8,128)(2,1)S(1)}, u32[]{:S(2)}, u32[]{:S(2)}) collective-permute-start(bf16[4,80,512]{2,1,0:T(8,128)(2,1)S(1)} %shard_map.118), channel_id=1, source_target_pairs={{0,4},{4,0},{8,12},{12,8},{16,20},{20,16},{24,28},{28,24},{1,5},{5... | collective-permute-start | bytes 983048 | tf_op jit(solution)/shard_map/ppermute | solution.py:454
  116.7 4.5 %collective-permute-start.25 = (bf16[4,80,128]{2,1,0:T(8,128)(2,1)S(1)}, bf16[4,80,128]{2,1,0:T(8,128)(2,1)S(1)}, u32[]{:S(2)}, u32[]{:S(2)}) collective-permute-start(bf16[4,80,128]{2,1,0:T(8,128)(2,1)S(1)} %get-tuple-element.64), channel_id=1, source_target_pairs={{0,1},{1,0},{2,3},{3,2},{4,5},{5,4},{6,7},{7,6},{8,9},{9,8},{10,11... | collective-permute-start | bytes 245768 | tf_op jit(solution)/shard_map/ppermute | solution.py:451
  118.4 5.3 %collective-permute-start.26 = (bf16[4,80,128]{2,1,0:T(8,128)(2,1)S(1)}, bf16[4,80,128]{2,1,0:T(8,128)(2,1)S(1)}, u32[]{:S(2)}, u32[]{:S(2)}) collective-permute-start(bf16[4,80,128]{2,1,0:T(8,128)(2,1)S(1)} %get-tuple-element.65), channel_id=1, source_target_pairs={{0,2},{1,3},{2,0},{3,1},{4,6},{5,7},{6,4},{7,5},{8,10},{9,11},{10,... | collective-permute-start | bytes 245768 | tf_op jit(solution)/shard_map/ppermute | solution.py:451
  119.9 5.3 %collective-permute-start.27 = (bf16[4,80,128]{2,1,0:T(8,128)(2,1)S(1)}, bf16[4,80,128]{2,1,0:T(8,128)(2,1)S(1)}, u32[]{:S(2)}, u32[]{:S(2)}) collective-permute-start(bf16[4,80,128]{2,1,0:T(8,128)(2,1)S(1)} %get-tuple-element.66), channel_id=1, source_target_pairs={{0,3},{1,2},{2,1},{3,0},{4,7},{5,6},{6,5},{7,4},{8,11},{9,10},{10,... | collective-permute-start | bytes 245768 | tf_op jit(solution)/shard_map/ppermute | solution.py:451
  (3 other events, 3.1 us)

commit v6 on v5

--- a/solution.py
+++ b/solution.py
@@ -8,7 +8,7 @@
 from jax.sharding import PartitionSpec as P
 
 ITERS = 2
-GROUPS = 1
+GROUPS = 2
 LANES = 128
 PIECES = 3
 PRIME = 32749
@@ -19,17 +19,33 @@
 NT = (((1,), (1,)), ((), ()))
 
 
-def call(kernel, outs, scratch, flops, *args, space=VMEM, limit=40):
-    nbytes = sum(a.size * a.dtype.itemsize for a in (*args, *outs))
-    return pl.pallas_call(
-        kernel,
-        out_shape=outs,
-        in_specs=[space] * len(args),
-        out_specs=[VMEM] * len(outs),
-        scratch_shapes=scratch,
-        compiler_params=pltpu.CompilerParams(vmem_limit_bytes=limit * 1024 * 1024),
-        cost_estimate=pl.CostEstimate(flops=flops, bytes_accessed=nbytes, transcendentals=0),
-    )(*args)
+class Caller:
+    def __init__(self):
+        self.previous = None
+
+    def __call__(self, kernel, outs, scratch, flops, *args, space=VMEM, limit=40):
+        nbytes = sum(a.size * a.dtype.itemsize for a in (*args, *outs))
+        count = len(args)
+        specs = [space] * count
+        body = kernel
+        if self.previous is not None:
+            args = (*args, self.previous)
+            specs = specs + [pl.BlockSpec(memory_space=pl.ANY)]
+
+            def body(*refs):
+                kernel(*refs[:count], *refs[count + 1 :])
+
+        results = pl.pallas_call(
+            body,
+            out_shape=outs,
+            in_specs=specs,
+            out_specs=[VMEM] * len(outs),
+            scratch_shapes=scratch,
+            compiler_params=pltpu.CompilerParams(vmem_limit_bytes=limit * 1024 * 1024),
+            cost_estimate=pl.CostEstimate(flops=flops, bytes_accessed=nbytes, transcendentals=0),
+        )(*args)
+        self.previous = results[-1]
+        return results
 
 
 def struct(shape, dtype):
@@ -272,8 +288,7 @@
     chips, width = own.shape[0], own.shape[3]
     rows = members * levp
     scalars = [read_scalars([mine, other], m, 2) for m in range(members)]
-    order = [i for i in range(chips) if i % 2] + [i for i in range(chips) if i % 2 == 0]
-    for i in order:
+    for i in reversed(range(chips)):
         zz = z ^ i
         y = jnp.dot(
             mine[...].reshape(rows, lanes),
@@ -380,10 +395,13 @@
         moved[m] = with_scalars(x, [total(r * r), total(r * d)]).astype(BF16)
 
 
-def last_kernel(parts, later, lev, *refs):
+def last_kernel(parts, later, lev, first, *refs):
     pieces, refs = refs[:parts], refs[parts:]
     sd, vert, vert_t, state, residual = refs[:5]
     increment_out, residual_out = refs[-2:]
+    if first:
+        increment_out[:, 0:first, :] = refs[-4][...]
+        residual_out[:, 0:first, :] = refs[-3][...]
     obs = lax.axis_index("obs")
     mine = pl.ds(pl.multiple_of(obs * LANES, LANES), LANES)
     for m in range(residual.shape[0]):
@@ -400,8 +418,8 @@
             solution = old_solution[m] + solution
         r = r - alpha * (d + dot(vert_t[...], sd[...] * t))
         increment = sd[...] * dot(vert[...], solution)
-        increment_out[:, m, :] = increment[0:lev]
-        residual_out[:, m, :] = r[0:lev]
+        increment_out[:, first + m, :] = increment[0:lev]
+        residual_out[:, first + m, :] = r[0:lev]
 
 
 def per_device(
@@ -441,7 +459,6 @@
     obs_precision = jnp.transpose(obs_precision, (1, 0, 2))
     product = n_slab * width * lanes * rows
     small = 12 * rows * levp * LANES
-    line_bits = [1 << k for k in range(chips.bit_length() - 1)]
     plane_bits = [1 << k for k in range(n_obs.bit_length() - 1)]
 
     def along(x, i):
@@ -458,6 +475,7 @@
             far = plane_bits[len(plane_bits) - 1 - step]
             parts = [one, plane(one, bit), two, plane(two, far)]
             if step < len(plane_bits) - 1:
+                yield
                 one, two = call(
                     functools.partial(add_halves_kernel, scalars),
                     [struct(half_field, BF16)] * 2,
@@ -465,27 +483,16 @@
                     0,
                     *parts,
                 )
+        yield
         return parts
 
     def line_sum(ys):
-        parts = {i: [y] for i, y in enumerate(ys)}
-        for bit in line_bits:
-            sent = [i for i in parts if i & bit]
-            for i in sorted(sent, reverse=True):
-                y = parts.pop(i)
-                if len(y) > 1:
-                    y = call(
-                        functools.partial(add_kernel, 2), [struct(panel, BF16)], [], 0, *y
-                    )
-                parts[i ^ bit].append(along(y[0], bit))
-        return parts[0]
+        return [y if i == 0 else along(y, i) for i, y in enumerate(ys)]
 
     def line_gather(w):
-        held = {0: w}
-        for bit in reversed(line_bits):
-            held.update({i ^ bit: along(x, bit) for i, x in held.items()})
-        return [held[i] for i in range(chips)]
-
+        return [w if i == 0 else along(w, i) for i in range(chips)]
+
+    call = Caller()
     dense = struct((chips, colblocks, LANES, width), BF16)
     own, for_partner, *partials = call(
         functools.partial(start_kernel, (chips, halves, groups)),
@@ -516,57 +523,55 @@
         space=HBM,
         limit=60,
     )
-    arrived = [plane_sum(*partials[2 * g : 2 * g + 2], 0) for g in range(groups)]
     partner = swap(for_partner)
-    (precision,) = call(
+    (precision,) = Caller()(
         functools.partial(precision_kernel, halves),
         [struct((levp, width), F32)],
         [],
         0,
         obs_precision,
     )
-    state = [None] * groups
-    direction = [None] * groups
-    total_step = [None] * groups
-    image = [None] * groups
-    residual, moved, slab_sd, outputs = [], [], [], []
-    for g in range(groups):
-        sd, r, x = call(
-            functools.partial(first_kernel, len(arrived[g])),
+    outputs = []
+
+    def group(partials):
+        ps = yield from plane_sum(*partials, 0)
+        slab_sd, residual, moved = call(
+            functools.partial(first_kernel, len(ps)),
             [struct((1, lanes), F32), struct(slab_field, F32), struct(slab_field, BF16)],
             [],
             small * colblocks,
-            *arrived[g],
+            *ps,
             vert,
             vert_t,
         )
-        slab_sd.append(sd)
-        residual.append(r)
-        moved.append(x)
-    for sweep in range(ITERS):
-        later, last = sweep > 0, sweep == ITERS - 1
-        for g in range(groups):
+        direction = total_step = image = state = None
+        for sweep in range(ITERS):
+            later, last = sweep > 0, sweep == ITERS - 1
+            other = swap(moved)
+            yield
             ys = call(
                 forward_kernel,
-                [struct(panel, BF16 if i % 2 else F32) for i in range(chips)],
+                [struct(panel, BF16 if i else F32) for i in range(chips)],
                 [],
                 2 * product,
-                moved[g],
-                swap(moved[g]),
+                moved,
+                other,
                 own,
                 partner,
             )
             ys = line_sum(ys)
-            image[g], weighted, state[g] = call(
+            yield
+            image, weighted, state = call(
                 functools.partial(weigh_kernel, later, len(ys)),
                 [struct(panel, F32), struct(panel, BF16), struct((share, 8, LANES), F32)],
                 [],
                 0,
                 *ys,
                 precision,
-                *([image[g], state[g]] if later else []),
+                *([image, state] if later else []),
             )
             ws = line_gather(weighted)
+            yield
             (theirs,) = call(
                 functools.partial(adjoint_kernel, chips, "theirs"),
                 [struct(slab_field, BF16)],
@@ -576,8 +581,10 @@
                 partner,
             )
             theirs = swap(theirs)
-            old = [direction[g], total_step[g]] if later else []
-            known = [vert, vert_t, state[g], residual[g], *old]
+            known = [vert, vert_t, state, residual]
+            if later:
+                known += [direction, total_step]
+            yield
             if last:
                 ps = call(
                     functools.partial(adjoint_kernel, chips, "columns"),
@@ -589,18 +596,22 @@
                     theirs,
                 )
                 ps = [x if i == 0 else plane(x, i) for i, x in enumerate(ps)]
+                yield
+                before = outputs[-1] if outputs else []
+                done = before[0].shape[1] if before else 0
                 outputs.append(
                     call(
-                        functools.partial(last_kernel, len(ps), later, lev),
-                        [struct((lev, share, LANES), F32)] * 2,
+                        functools.partial(last_kernel, len(ps), later, lev, done),
+                        [struct((lev, done + share, LANES), F32)] * 2,
                         [],
                         small,
                         *ps,
                         col_sd,
                         *known,
+                        *before,
                     )
                 )
-                continue
+                return
             ps = call(
                 functools.partial(adjoint_kernel, chips, "halves"),
                 [struct(half_field, BF16)] * 2,
@@ -610,23 +621,36 @@
                 own,
                 theirs,
             )
-            ps = plane_sum(*ps, 1)
+            ps = yield from plane_sum(*ps, 1)
             outs = [struct(slab_field, F32), struct(field, F32), struct(slab_field, BF16)]
             if later:
                 outs.append(struct(slab_field, F32))
-            r, total_step[g], moved[g], *d = call(
+            r, total_step, moved, *d = call(
                 functools.partial(update_kernel, len(ps), later),
                 outs,
                 [],
                 small * colblocks,
                 *ps,
-                slab_sd[g],
+                slab_sd,
                 *known,
             )
-            direction[g] = d[0] if later else residual[g]
-            residual[g] = r
-    outputs = [x[0] if groups == 1 else jnp.concatenate(x, axis=1) for x in zip(*outputs)]
-    return tuple(jnp.transpose(x, (1, 0, 2))[None] for x in outputs)
+            direction, residual = (d[0] if later else residual), r
+
+    steps = [group(partials[2 * g : 2 * g + 2]) for g in range(groups)]
+    for g in range(groups):
+        next(steps[g])
+    if groups == 2:
+        adds = len(plane_bits) - 1
+        order = [0] * adds + [0, 0] + [1] * adds + [0, 1]
+        for sweep in range(ITERS - 1):
+            order += [1, 0, 0, 1] + [0] * adds + [0]
+            order += [0, 1, 1, 0] + [1] * adds + [1]
+        order += [1, 0, 0, 1, 0, 1, 1, 1]
+    else:
+        order = [g for g in range(groups) for step in range(ITERS * (6 + len(plane_bits)))]
+    for g in order:
+        next(steps[g], None)
+    return tuple(jnp.transpose(x, (1, 0, 2))[None] for x in outputs[-1])
 
 
 def solution(mesh):

time: 127 us -> 140 us (1.10)
  starting transfers between devices: 27.5 us -> 61.6 us
  waiting for transfers between devices: 79.3 us -> 53.6 us
  Pallas kernels: 15 us -> 19.2 us
    ppermute x12 -> x24, starting transfers between devices: 14 us -> 35.5 us  [along(): return lax.ppermute(x, 'slab', [(s, s ^ 2 * i) for s in range(n_slab)])]
    ppermute x12 -> x24, waiting for transfers between devices: 49 us -> 30.2 us  [along(): return lax.ppermute(x, 'slab', [(s, s ^ 2 * i) for s in range(n_slab)])]
    ppermute x11 -> x22, starting transfers between devices: 12.3 us -> 25 us  [plane(): return lax.ppermute(x, 'obs', [(o, o ^ i) for o in range(n_obs)])]
    ppermute x5 -> x9, waiting for transfers between devices: 6.47 us -> 1.92 us  [swap(): return lax.ppermute(x, 'slab', [(s, s ^ 1) for s in range(n_slab)])]
    pallas_call x17 -> x28, Pallas kernels: 15 us -> 19.2 us  [__call__(): pl.pallas_call(body, out_shape=outs, in_specs=specs, out_specs=[VMEM] * l...]
    ppermute x11 -> x22, waiting for transfers between devices: 23.9 us -> 21.5 us  [plane(): return lax.ppermute(x, 'obs', [(o, o ^ i) for o in range(n_obs)])]
    unnamed x15 -> x21, local copies, waits for them, and re-layouts: 3.17 us -> 4.01 us
  transfers between devices with their start and end apart: 28 -> 55, of which waited for: 27 -> 27; matrix products, arithmetic and copies ran while one was open for 0% -> 0% of each run, Pallas kernels for 1% -> 5%
where the time goes in v6:
time: 140 us
  starting transfers between devices  61.6 us (44%)
  waiting for transfers between devices  53.6 us (38%)
  Pallas kernels  19.2 us (14%)
  local copies, waits for them, and re-layouts  4.02 us (3%)
  between operations  1.62 us (1%)
    ppermute x24, starting transfers between devices, along(): return lax.ppermute(x, 'slab', [(s, s ^ 2 * i) for s in range(n_slab)])  35.5 us
    ppermute x24, waiting for transfers between devices, along(): return lax.ppermute(x, 'slab', [(s, s ^ 2 * i) for s in range(n_slab)])  30.2 us
    ppermute x22, starting transfers between devices, plane(): return lax.ppermute(x, 'obs', [(o, o ^ i) for o in range(n_obs)])  25 us
    ppermute x22, waiting for transfers between devices, plane(): return lax.ppermute(x, 'obs', [(o, o ^ i) for o in range(n_obs)])  21.5 us
    pallas_call x28, Pallas kernels, __call__(): pl.pallas_call(body, out_shape=outs, in_specs=specs, out_specs=[VMEM] * l...  19.2 us
    unnamed x21, local copies, waits for them, and re-layouts  4.01 us
  transfers between devices with their start and end apart: 55, of which 27 were waited for; matrix products, arithmetic and copies ran while one was open for 0% of the time, Pallas kernels for 5%

profile of v6, /device:TPU:0, one launch (start us, length us, event | category | flops | bytes accessed | tf_op | source)
XLA Modules:
  0.0 140.0 jit_solution(11497013415115201431)
XLA Ops:
  1.3 6.3 %shard_map.104 = (bf16[4,4,128,256]{3,2,1,0:T(8,128)(2,1)}, bf16[4,4,128,256]{3,2,1,0:T(8,128)(2,1)}, bf16[2,80,256]{2,1,0:T(8,128)(2,1)}, bf16[2,80,256]{2,1,0:...) custom-call(s32[4]{0:T(128)} %seeds_in.1, s32[1,1,32]{2,1,0:T(1,128)} %ids_in.1, ...), custom_call_target="tpu_custom_call" | custom-call | flops 671088640 | bytes 5751572 | tf_op jit(solution)/shard_map/pallas_call | solution.py:38
  8.1 2.6 %collective-permute-start.2 = (bf16[2,80,256]{2,1,0:T(8,128)(2,1)}, bf16[2,80,256]{2,1,0:T(8,128)(2,1)S(1)}, u32[]{:S(2)}, u32[]{:S(2)}) collective-permute-start(bf16[2,80,256]{2,1,0:T(8,128)(2,1)} %get-tuple-element.72.refs_0_), channel_id=1, source_target_pairs={{0,1},{1,0},{2,3},{3,2},{4,5},{5,4},{6,7},{7,6},{8,9},{9,8},{10,11... | collective-permute-start | bytes 245768 | tf_op jit(solution)/shard_map/ppermute | solution.py:468
  12.2 1.7 %collective-permute-done.2.refs_1_ = bf16[2,80,256]{2,1,0:T(8,128)(2,1)S(1)} collective-permute-done((bf16[2,80,256]{2,1,0:T(8,128)(2,1)}, bf16[2,80,256]{2,1,0:T(8,128)(2,1)S(1)}, u32[]{:S(2)}, u32[]{:S(2)}) %collective-permute-start.2) | collective-permute-done | bytes 81952 | tf_op jit(solution)/shard_map/ppermute | solution.py:468
  18.1 1.6 %collective-permute-start.4 = (bf16[2,80,256]{2,1,0:T(8,128)(2,1)S(1)}, bf16[2,80,256]{2,1,0:T(8,128)(2,1)S(1)}, u32[]{:S(2)}, u32[]{:S(2)}) collective-permute-start(bf16[2,80,256]{2,1,0:T(8,128)(2,1)S(1)} %get-tuple-element.74.refs_0_), channel_id=1, source_target_pairs={{0,2},{1,3},{2,0},{3,1},{4,6},{5,7},{6,4},{7,5},{8,10},{9,11},{10,... | collective-permute-start | bytes 245768 | tf_op jit(solution)/shard_map/ppermute | solution.py:468
  20.4 2.3 %collective-permute-done.4.refs_1_ = bf16[2,80,256]{2,1,0:T(8,128)(2,1)S(1)} collective-permute-done((bf16[2,80,256]{2,1,0:T(8,128)(2,1)S(1)}, bf16[2,80,256]{2,1,0:T(8,128)(2,1)S(1)}, u32[]{:S(2)}, u32[]{:S(2)}) %collective-permute-start.4) | collective-permute-done | bytes 81952 | tf_op jit(solution)/shard_map/ppermute | solution.py:468
  28.1 1.6 %collective-permute-start.10 = (bf16[2,80,256]{2,1,0:T(8,128)(2,1)S(1)}, bf16[2,80,256]{2,1,0:T(8,128)(2,1)S(1)}, u32[]{:S(2)}, u32[]{:S(2)}) collective-permute-start(bf16[2,80,256]{2,1,0:T(8,128)(2,1)S(1)} %get-tuple-element.83), channel_id=1, source_target_pairs={{0,8},{4,12},{8,0},{12,4},{16,24},{20,28},{24,16},{28,20},{1,9},{5... | collective-permute-start | bytes 245768 | tf_op jit(solution)/shard_map/ppermute | solution.py:465
  29.7 2.6 %collective-permute-start.11 = (bf16[2,80,256]{2,1,0:T(8,128)(2,1)S(1)}, bf16[2,80,256]{2,1,0:T(8,128)(2,1)S(1)}, u32[]{:S(2)}, u32[]{:S(2)}) collective-permute-start(bf16[2,80,256]{2,1,0:T(8,128)(2,1)S(1)} %get-tuple-element.84), channel_id=1, source_target_pairs={{0,16},{4,20},{8,24},{12,28},{16,0},{20,4},{24,8},{28,12},{1,17},{... | collective-permute-start | bytes 245768 | tf_op jit(solution)/shard_map/ppermute | solution.py:465
  35.6 3.6 %collective-permute-done.11.refs_2_ = bf16[2,80,256]{2,1,0:T(8,128)(2,1)S(1)} collective-permute-done((bf16[2,80,256]{2,1,0:T(8,128)(2,1)S(1)}, bf16[2,80,256]{2,1,0:T(8,128)(2,1)S(1)}, u32[]{:S(2)}, u32[]{:S(2)}) %collective-permute-start.11) | collective-permute-done | bytes 81952 | tf_op jit(solution)/shard_map/ppermute | solution.py:465
  40.1 2.7 %collective-permute-start.19 = (bf16[2,80,256]{2,1,0:T(8,128)(2,1)S(1)}, bf16[2,80,256]{2,1,0:T(8,128)(2,1)S(1)}, u32[]{:S(2)}, u32[]{:S(2)}) collective-permute-start(bf16[2,80,256]{2,1,0:T(8,128)(2,1)S(1)} %get-tuple-element.91.refs_0_), channel_id=1, source_target_pairs={{0,24},{4,28},{8,16},{12,20},{16,8},{20,12},{24,0},{28,4},{1,25},{... | collective-permute-start | bytes 245768 | tf_op jit(solution)/shard_map/ppermute | solution.py:465
  45.1 2.2 %collective-permute-done.19.refs_3_ = bf16[2,80,256]{2,1,0:T(8,128)(2,1)S(1)} collective-permute-done((bf16[2,80,256]{2,1,0:T(8,128)(2,1)S(1)}, bf16[2,80,256]{2,1,0:T(8,128)(2,1)S(1)}, u32[]{:S(2)}, u32[]{:S(2)}) %collective-permute-start.19) | collective-permute-done | bytes 81952 | tf_op jit(solution)/shard_map/ppermute | solution.py:465
  47.3 3.9 %collective-permute-done.18.refs_2_ = bf16[2,80,256]{2,1,0:T(8,128)(2,1)S(1)} collective-permute-done((bf16[2,80,256]{2,1,0:T(8,128)(2,1)S(1)}, bf16[2,80,256]{2,1,0:T(8,128)(2,1)S(1)}, u32[]{:S(2)}, u32[]{:S(2)}) %collective-permute-start.18) | collective-permute-done | bytes 81952 | tf_op jit(solution)/shard_map/ppermute | solution.py:465
  51.8 2.5 %collective-permute-start.16 = (bf16[2,80,256]{2,1,0:T(8,128)(2,1)S(1)}, bf16[2,80,256]{2,1,0:T(8,128)(2,1)S(1)}, u32[]{:S(2)}, u32[]{:S(2)}) collective-permute-start(bf16[2,80,256]{2,1,0:T(8,128)(2,1)S(1)} %get-tuple-element.90.refs_5_), channel_id=1, source_target_pairs={{0,24},{4,28},{8,16},{12,20},{16,8},{20,12},{24,0},{28,4},{1,25},{... | collective-permute-start | bytes 245768 | tf_op jit(solution)/shard_map/ppermute | solution.py:465
  54.3 2.0 %collective-permute-start.15 = (bf16[2,80,256]{2,1,0:T(8,128)(2,1)S(1)}, bf16[2,80,256]{2,1,0:T(8,128)(2,1)S(1)}, u32[]{:S(2)}, u32[]{:S(2)}) collective-permute-start(bf16[2,80,256]{2,1,0:T(8,128)(2,1)S(1)} %get-tuple-element.89), channel_id=1, source_target_pairs={{0,16},{4,20},{8,24},{12,28},{16,0},{20,4},{24,8},{28,12},{1,17},{... | collective-permute-start | bytes 245768 | tf_op jit(solution)/shard_map/ppermute | solution.py:465
  59.2 2.7 %collective-permute-done.14.refs_1_ = bf16[2,80,256]{2,1,0:T(8,128)(2,1)S(1)} collective-permute-done((bf16[2,80,256]{2,1,0:T(8,128)(2,1)S(1)}, bf16[2,80,256]{2,1,0:T(8,128)(2,1)S(1)}, u32[]{:S(2)}, u32[]{:S(2)}) %collective-permute-start.14) | collective-permute-done | bytes 81952 | tf_op jit(solution)/shard_map/ppermute | solution.py:465
  64.7 2.4 %collective-permute-done.26.refs_1_ = bf16[2,80,256]{2,1,0:T(8,128)(2,1)S(1)} collective-permute-done((bf16[2,80,256]{2,1,0:T(8,128)(2,1)S(1)}, bf16[2,80,256]{2,1,0:T(8,128)(2,1)S(1)}, u32[]{:S(2)}, u32[]{:S(2)}) %collective-permute-start.26) | collective-permute-done | bytes 81952 | tf_op jit(solution)/shard_map/ppermute | solution.py:468
  69.1 2.5 %collective-permute-start.23 = (bf16[2,80,256]{2,1,0:T(8,128)(2,1)S(1)}, bf16[2,80,256]{2,1,0:T(8,128)(2,1)S(1)}, u32[]{:S(2)}, u32[]{:S(2)}) collective-permute-start(bf16[2,80,256]{2,1,0:T(8,128)(2,1)S(1)} %get-tuple-element.93.refs_0_), channel_id=1, source_target_pairs={{0,24},{4,28},{8,16},{12,20},{16,8},{20,12},{24,0},{28,4},{1,25},{... | collective-permute-start | bytes 245768 | tf_op jit(solution)/shard_map/ppermute | solution.py:465
  71.6 1.9 %collective-permute-start.21 = (bf16[2,80,256]{2,1,0:T(8,128)(2,1)S(1)}, bf16[2,80,256]{2,1,0:T(8,128)(2,1)S(1)}, u32[]{:S(2)}, u32[]{:S(2)}) collective-permute-start(bf16[2,80,256]{2,1,0:T(8,128)(2,1)S(1)} %get-tuple-element.93.refs_0_), channel_id=1, source_target_pairs={{0,8},{4,12},{8,0},{12,4},{16,24},{20,28},{24,16},{28,20},{1,9},{5... | collective-permute-start | bytes 245768 | tf_op jit(solution)/shard_map/ppermute | solution.py:465
  74.1 2.2 %collective-permute-done.23.refs_3_ = bf16[2,80,256]{2,1,0:T(8,128)(2,1)S(1)} collective-permute-done((bf16[2,80,256]{2,1,0:T(8,128)(2,1)S(1)}, bf16[2,80,256]{2,1,0:T(8,128)(2,1)S(1)}, u32[]{:S(2)}, u32[]{:S(2)}) %collective-permute-start.23) | collective-permute-done | bytes 81952 | tf_op jit(solution)/shard_map/ppermute | solution.py:465
  76.3 3.0 %collective-permute-done.22.refs_2_ = bf16[2,80,256]{2,1,0:T(8,128)(2,1)S(1)} collective-permute-done((bf16[2,80,256]{2,1,0:T(8,128)(2,1)S(1)}, bf16[2,80,256]{2,1,0:T(8,128)(2,1)S(1)}, u32[]{:S(2)}, u32[]{:S(2)}) %collective-permute-start.22) | collective-permute-done | bytes 81952 | tf_op jit(solution)/shard_map/ppermute | solution.py:465
  79.9 2.5 %collective-permute-start.34 = (bf16[2,80,256]{2,1,0:T(8,128)(2,1)S(1)}, bf16[2,80,256]{2,1,0:T(8,128)(2,1)S(1)}, u32[]{:S(2)}, u32[]{:S(2)}) collective-permute-start(bf16[2,80,256]{2,1,0:T(8,128)(2,1)S(1)} %get-tuple-element.101.refs_5_), channel_id=1, source_target_pairs={{0,24},{4,28},{8,16},{12,20},{16,8},{20,12},{24,0},{28,4},{1,25},{... | collective-permute-start | bytes 245768 | tf_op jit(solution)/shard_map/ppermute | solution.py:465
  82.4 1.9 %collective-permute-start.33 = (bf16[2,80,256]{2,1,0:T(8,128)(2,1)S(1)}, bf16[2,80,256]{2,1,0:T(8,128)(2,1)S(1)}, u32[]{:S(2)}, u32[]{:S(2)}) collective-permute-start(bf16[2,80,256]{2,1,0:T(8,128)(2,1)S(1)} %get-tuple-element.106), channel_id=1, source_target_pairs={{0,16},{4,20},{8,24},{12,28},{16,0},{20,4},{24,8},{28,12},{1,17},{... | collective-permute-start | bytes 245768 | tf_op jit(solution)/shard_map/ppermute | solution.py:465
  86.7 3.4 %collective-permute-done.32.refs_1_ = bf16[2,80,256]{2,1,0:T(8,128)(2,1)S(1)} collective-permute-done((bf16[2,80,256]{2,1,0:T(8,128)(2,1)S(1)}, bf16[2,80,256]{2,1,0:T(8,128)(2,1)S(1)}, u32[]{:S(2)}, u32[]{:S(2)}) %collective-permute-start.32) | collective-permute-done | bytes 81952 | tf_op jit(solution)/shard_map/ppermute | solution.py:465
  92.8 2.7 %collective-permute-done.35.refs_1_ = bf16[2,80,256]{2,1,0:T(8,128)(2,1)S(1)} collective-permute-done((bf16[2,80,256]{2,1,0:T(8,128)(2,1)S(1)}, bf16[2,80,256]{2,1,0:T(8,128)(2,1)S(1)}, u32[]{:S(2)}, u32[]{:S(2)}) %collective-permute-start.35) | collective-permute-done | bytes 81952 | tf_op jit(solution)/shard_map/ppermute | solution.py:468
  97.2 1.8 %collective-permute-start.43 = (bf16[2,80,256]{2,1,0:T(8,128)(2,1)S(1)}, bf16[2,80,256]{2,1,0:T(8,128)(2,1)S(1)}, u32[]{:S(2)}, u32[]{:S(2)}) collective-permute-start(bf16[2,80,256]{2,1,0:T(8,128)(2,1)S(1)} %get-tuple-element.119.refs_0_), channel_id=1, source_target_pairs={{0,24},{4,28},{8,16},{12,20},{16,8},{20,12},{24,0},{28,4},{1,25},{... | collective-permute-start | bytes 245768 | tf_op jit(solution)/shard_map/ppermute | solution.py:465
  99.4 2.3 %collective-permute-start.41 = (bf16[2,80,256]{2,1,0:T(8,128)(2,1)S(1)}, bf16[2,80,256]{2,1,0:T(8,128)(2,1)S(1)}, u32[]{:S(2)}, u32[]{:S(2)}) collective-permute-start(bf16[2,80,256]{2,1,0:T(8,128)(2,1)S(1)} %get-tuple-element.119.refs_0_), channel_id=1, source_target_pairs={{0,8},{4,12},{8,0},{12,4},{16,24},{20,28},{24,16},{28,20},{1,9},{5... | collective-permute-start | bytes 245768 | tf_op jit(solution)/shard_map/ppermute | solution.py:465
  102.2 2.2 %collective-permute-done.43.refs_3_ = bf16[2,80,256]{2,1,0:T(8,128)(2,1)S(1)} collective-permute-done((bf16[2,80,256]{2,1,0:T(8,128)(2,1)S(1)}, bf16[2,80,256]{2,1,0:T(8,128)(2,1)S(1)}, u32[]{:S(2)}, u32[]{:S(2)}) %collective-permute-start.43) | collective-permute-done | bytes 81952 | tf_op jit(solution)/shard_map/ppermute | solution.py:465
  104.4 3.0 %collective-permute-done.42.refs_2_ = bf16[2,80,256]{2,1,0:T(8,128)(2,1)S(1)} collective-permute-done((bf16[2,80,256]{2,1,0:T(8,128)(2,1)S(1)}, bf16[2,80,256]{2,1,0:T(8,128)(2,1)S(1)}, u32[]{:S(2)}, u32[]{:S(2)}) %collective-permute-start.42) | collective-permute-done | bytes 81952 | tf_op jit(solution)/shard_map/ppermute | solution.py:465
  108.1 2.9 %collective-permute-start.39 = (bf16[2,80,256]{2,1,0:T(8,128)(2,1)S(1)}, bf16[2,80,256]{2,1,0:T(8,128)(2,1)S(1)}, u32[]{:S(2)}, u32[]{:S(2)}) collective-permute-start(bf16[2,80,256]{2,1,0:T(8,128)(2,1)S(1)} %get-tuple-element.116), channel_id=1, source_target_pairs={{0,16},{4,20},{8,24},{12,28},{16,0},{20,4},{24,8},{28,12},{1,17},{... | collective-permute-start | bytes 245768 | tf_op jit(solution)/shard_map/ppermute | solution.py:465
  114.2 3.6 %collective-permute-done.39.refs_2_ = bf16[2,80,256]{2,1,0:T(8,128)(2,1)S(1)} collective-permute-done((bf16[2,80,256]{2,1,0:T(8,128)(2,1)S(1)}, bf16[2,80,256]{2,1,0:T(8,128)(2,1)S(1)}, u32[]{:S(2)}, u32[]{:S(2)}) %collective-permute-start.39) | collective-permute-done | bytes 81952 | tf_op jit(solution)/shard_map/ppermute | solution.py:465
  118.7 2.4 %collective-permute-start.47 = (bf16[2,80,256]{2,1,0:T(8,128)(2,1)S(1)}, bf16[2,80,256]{2,1,0:T(8,128)(2,1)S(1)}, u32[]{:S(2)}, u32[]{:S(2)}) collective-permute-start(bf16[2,80,256]{2,1,0:T(8,128)(2,1)S(1)} %get-tuple-element.121.refs_0_), channel_id=1, source_target_pairs={{0,24},{4,28},{8,16},{12,20},{16,8},{20,12},{24,0},{28,4},{1,25},{... | collective-permute-start | bytes 245768 | tf_op jit(solution)/shard_map/ppermute | solution.py:465
  127.1 2.0 %collective-permute-done.50.refs_3_ = bf16[2,80,128]{2,1,0:T(8,128)(2,1)S(1)} collective-permute-done((bf16[2,80,128]{2,1,0:T(8,128)(2,1)S(1)}, bf16[2,80,128]{2,1,0:T(8,128)(2,1)S(1)}, u32[]{:S(2)}, u32[]{:S(2)}) %collective-permute-start.50) | collective-permute-done | bytes 40992 | tf_op jit(solution)/shard_map/ppermute | solution.py:468
  137.1 1.8 %collective-permute-done.54.refs_3_ = bf16[2,80,128]{2,1,0:T(8,128)(2,1)S(1)} collective-permute-done((bf16[2,80,128]{2,1,0:T(8,128)(2,1)S(1)}, bf16[2,80,128]{2,1,0:T(8,128)(2,1)S(1)}, u32[]{:S(2)}, u32[]{:S(2)}) %collective-permute-start.54) | collective-permute-done | bytes 40992 | tf_op jit(solution)/shard_map/ppermute | solution.py:468
  (129 shorter events, 55.5 us)
Async XLA Ops:
  7.6 18.7 %collective-permute-start.7 = (bf16[4,4,128,256]{3,2,1,0:T(8,128)(2,1)}, bf16[4,4,128,256]{3,2,1,0:T(8,128)(2,1)S(1)}, u32[]{:S(2)}, u32[]{:S(2)}) collective-permute-start(bf16[4,4,128,256]{3,2,1,0:T(8,128)(2,1)} %get-tuple-element.78), channel_id=1, source_target_pairs={{0,4},{4,0},{8,12},{12,8},{16,20},{20,16},{24,28},{28,24},{1,5},{5... | collective-permute-start | bytes 3145736 | tf_op jit(solution)/shard_map/ppermute | solution.py:471
  8.1 5.9 %collective-permute-start.2 = (bf16[2,80,256]{2,1,0:T(8,128)(2,1)}, bf16[2,80,256]{2,1,0:T(8,128)(2,1)S(1)}, u32[]{:S(2)}, u32[]{:S(2)}) collective-permute-start(bf16[2,80,256]{2,1,0:T(8,128)(2,1)} %get-tuple-element.72.refs_0_), channel_id=1, source_target_pairs={{0,1},{1,0},{2,3},{3,2},{4,5},{5,4},{6,7},{7,6},{8,9},{9,8},{10,11... | collective-permute-start | bytes 245768 | tf_op jit(solution)/shard_map/ppermute | solution.py:468
  24.9 7.6 %collective-permute-start = (bf16[2,80,256]{2,1,0:T(8,128)(2,1)}, bf16[2,80,256]{2,1,0:T(8,128)(2,1)S(1)}, u32[]{:S(2)}, u32[]{:S(2)}) collective-permute-start(bf16[2,80,256]{2,1,0:T(8,128)(2,1)} %get-tuple-element.70.refs_0_), channel_id=1, source_target_pairs={{0,1},{1,0},{2,3},{3,2},{4,5},{5,4},{6,7},{7,6},{8,9},{9,8},{10,11... | collective-permute-start | bytes 245768 | tf_op jit(solution)/shard_map/ppermute | solution.py:468
  25.5 7.0 %collective-permute-start.1 = (bf16[2,80,256]{2,1,0:T(8,128)(2,1)}, bf16[2,80,256]{2,1,0:T(8,128)(2,1)S(1)}, u32[]{:S(2)}, u32[]{:S(2)}) collective-permute-start(bf16[2,80,256]{2,1,0:T(8,128)(2,1)} %get-tuple-element.71.refs_4_.refs_2_), channel_id=1, source_target_pairs={{0,2},{1,3},{2,0},{3,1},{4,6},{5,7},{6,4},{7,5},{8,10},{9,11},{10,... | collective-permute-start | bytes 245768 | tf_op jit(solution)/shard_map/ppermute | solution.py:468
  28.1 7.5 %collective-permute-start.10 = (bf16[2,80,256]{2,1,0:T(8,128)(2,1)S(1)}, bf16[2,80,256]{2,1,0:T(8,128)(2,1)S(1)}, u32[]{:S(2)}, u32[]{:S(2)}) collective-permute-start(bf16[2,80,256]{2,1,0:T(8,128)(2,1)S(1)} %get-tuple-element.83), channel_id=1, source_target_pairs={{0,8},{4,12},{8,0},{12,4},{16,24},{20,28},{24,16},{28,20},{1,9},{5... | collective-permute-start | bytes 245768 | tf_op jit(solution)/shard_map/ppermute | solution.py:465
  29.7 9.5 %collective-permute-start.11 = (bf16[2,80,256]{2,1,0:T(8,128)(2,1)S(1)}, bf16[2,80,256]{2,1,0:T(8,128)(2,1)S(1)}, u32[]{:S(2)}, u32[]{:S(2)}) collective-permute-start(bf16[2,80,256]{2,1,0:T(8,128)(2,1)S(1)} %get-tuple-element.84), channel_id=1, source_target_pairs={{0,16},{4,20},{8,24},{12,28},{16,0},{20,4},{24,8},{28,12},{1,17},{... | collective-permute-start | bytes 245768 | tf_op jit(solution)/shard_map/ppermute | solution.py:465
  32.3 6.9 %collective-permute-start.12 = (bf16[2,80,256]{2,1,0:T(8,128)(2,1)S(1)}, bf16[2,80,256]{2,1,0:T(8,128)(2,1)S(1)}, u32[]{:S(2)}, u32[]{:S(2)}) collective-permute-start(bf16[2,80,256]{2,1,0:T(8,128)(2,1)S(1)} %get-tuple-element.79.refs_4_), channel_id=1, source_target_pairs={{0,24},{4,28},{8,16},{12,20},{16,8},{20,12},{24,0},{28,4},{1,25},{... | collective-permute-start | bytes 245768 | tf_op jit(solution)/shard_map/ppermute | solution.py:465
  32.6 6.7 %collective-permute-start.8 = (bf16[2,80,256]{2,1,0:T(8,128)(2,1)S(1)}, bf16[2,80,256]{2,1,0:T(8,128)(2,1)S(1)}, u32[]{:S(2)}, u32[]{:S(2)}) collective-permute-start(bf16[2,80,256]{2,1,0:T(8,128)(2,1)S(1)} %get-tuple-element.80.refs_0_), channel_id=1, source_target_pairs={{0,2},{1,3},{2,0},{3,1},{4,6},{5,7},{6,4},{7,5},{8,10},{9,11},{10,... | collective-permute-start | bytes 245768 | tf_op jit(solution)/shard_map/ppermute | solution.py:468
  33.9 5.4 %collective-permute-start.9 = (bf16[2,80,256]{2,1,0:T(8,128)(2,1)S(1)}, bf16[2,80,256]{2,1,0:T(8,128)(2,1)S(1)}, u32[]{:S(2)}, u32[]{:S(2)}) collective-permute-start(bf16[2,80,256]{2,1,0:T(8,128)(2,1)S(1)} %get-tuple-element.81.refs_5_.refs_2_), channel_id=1, source_target_pairs={{0,1},{1,0},{2,3},{3,2},{4,5},{5,4},{6,7},{7,6},{8,9},{9,8},{10,11... | collective-permute-start | bytes 245768 | tf_op jit(solution)/shard_map/ppermute | solution.py:468
  40.1 7.2 %collective-permute-start.19 = (bf16[2,80,256]{2,1,0:T(8,128)(2,1)S(1)}, bf16[2,80,256]{2,1,0:T(8,128)(2,1)S(1)}, u32[]{:S(2)}, u32[]{:S(2)}) collective-permute-start(bf16[2,80,256]{2,1,0:T(8,128)(2,1)S(1)} %get-tuple-element.91.refs_0_), channel_id=1, source_target_pairs={{0,24},{4,28},{8,16},{12,20},{16,8},{20,12},{24,0},{28,4},{1,25},{... | collective-permute-start | bytes 245768 | tf_op jit(solution)/shard_map/ppermute | solution.py:465
  42.8 8.5 %collective-permute-start.18 = (bf16[2,80,256]{2,1,0:T(8,128)(2,1)S(1)}, bf16[2,80,256]{2,1,0:T(8,128)(2,1)S(1)}, u32[]{:S(2)}, u32[]{:S(2)}) collective-permute-start(bf16[2,80,256]{2,1,0:T(8,128)(2,1)S(1)} %get-tuple-element.91.refs_0_), channel_id=1, source_target_pairs={{0,16},{4,20},{8,24},{12,28},{16,0},{20,4},{24,8},{28,12},{1,17},{... | collective-permute-start | bytes 245768 | tf_op jit(solution)/shard_map/ppermute | solution.py:465
  43.2 8.0 %collective-permute-start.17 = (bf16[2,80,256]{2,1,0:T(8,128)(2,1)S(1)}, bf16[2,80,256]{2,1,0:T(8,128)(2,1)S(1)}, u32[]{:S(2)}, u32[]{:S(2)}) collective-permute-start(bf16[2,80,256]{2,1,0:T(8,128)(2,1)S(1)} %get-tuple-element.91.refs_0_), channel_id=1, source_target_pairs={{0,8},{4,12},{8,0},{12,4},{16,24},{20,28},{24,16},{28,20},{1,9},{5... | collective-permute-start | bytes 245768 | tf_op jit(solution)/shard_map/ppermute | solution.py:465
  51.8 10.2 %collective-permute-start.16 = (bf16[2,80,256]{2,1,0:T(8,128)(2,1)S(1)}, bf16[2,80,256]{2,1,0:T(8,128)(2,1)S(1)}, u32[]{:S(2)}, u32[]{:S(2)}) collective-permute-start(bf16[2,80,256]{2,1,0:T(8,128)(2,1)S(1)} %get-tuple-element.90.refs_5_), channel_id=1, source_target_pairs={{0,24},{4,28},{8,16},{12,20},{16,8},{20,12},{24,0},{28,4},{1,25},{... | collective-permute-start | bytes 245768 | tf_op jit(solution)/shard_map/ppermute | solution.py:465
  54.3 7.7 %collective-permute-start.14 = (bf16[2,80,256]{2,1,0:T(8,128)(2,1)S(1)}, bf16[2,80,256]{2,1,0:T(8,128)(2,1)S(1)}, u32[]{:S(2)}, u32[]{:S(2)}) collective-permute-start(bf16[2,80,256]{2,1,0:T(8,128)(2,1)S(1)} %get-tuple-element.88), channel_id=1, source_target_pairs={{0,8},{4,12},{8,0},{12,4},{16,24},{20,28},{24,16},{28,20},{1,9},{5... | collective-permute-start | bytes 245768 | tf_op jit(solution)/shard_map/ppermute | solution.py:465
  54.3 7.7 %collective-permute-start.15 = (bf16[2,80,256]{2,1,0:T(8,128)(2,1)S(1)}, bf16[2,80,256]{2,1,0:T(8,128)(2,1)S(1)}, u32[]{:S(2)}, u32[]{:S(2)}) collective-permute-start(bf16[2,80,256]{2,1,0:T(8,128)(2,1)S(1)} %get-tuple-element.89), channel_id=1, source_target_pairs={{0,16},{4,20},{8,24},{12,28},{16,0},{20,4},{24,8},{28,12},{1,17},{... | collective-permute-start | bytes 245768 | tf_op jit(solution)/shard_map/ppermute | solution.py:465
  69.1 7.2 %collective-permute-start.23 = (bf16[2,80,256]{2,1,0:T(8,128)(2,1)S(1)}, bf16[2,80,256]{2,1,0:T(8,128)(2,1)S(1)}, u32[]{:S(2)}, u32[]{:S(2)}) collective-permute-start(bf16[2,80,256]{2,1,0:T(8,128)(2,1)S(1)} %get-tuple-element.93.refs_0_), channel_id=1, source_target_pairs={{0,24},{4,28},{8,16},{12,20},{16,8},{20,12},{24,0},{28,4},{1,25},{... | collective-permute-start | bytes 245768 | tf_op jit(solution)/shard_map/ppermute | solution.py:465
  71.6 7.6 %collective-permute-start.22 = (bf16[2,80,256]{2,1,0:T(8,128)(2,1)S(1)}, bf16[2,80,256]{2,1,0:T(8,128)(2,1)S(1)}, u32[]{:S(2)}, u32[]{:S(2)}) collective-permute-start(bf16[2,80,256]{2,1,0:T(8,128)(2,1)S(1)} %get-tuple-element.93.refs_0_), channel_id=1, source_target_pairs={{0,16},{4,20},{8,24},{12,28},{16,0},{20,4},{24,8},{28,12},{1,17},{... | collective-permute-start | bytes 245768 | tf_op jit(solution)/shard_map/ppermute | solution.py:465
  71.6 7.6 %collective-permute-start.21 = (bf16[2,80,256]{2,1,0:T(8,128)(2,1)S(1)}, bf16[2,80,256]{2,1,0:T(8,128)(2,1)S(1)}, u32[]{:S(2)}, u32[]{:S(2)}) collective-permute-start(bf16[2,80,256]{2,1,0:T(8,128)(2,1)S(1)} %get-tuple-element.93.refs_0_), channel_id=1, source_target_pairs={{0,8},{4,12},{8,0},{12,4},{16,24},{20,28},{24,16},{28,20},{1,9},{5... | collective-permute-start | bytes 245768 | tf_op jit(solution)/shard_map/ppermute | solution.py:465
  79.9 10.2 %collective-permute-start.34 = (bf16[2,80,256]{2,1,0:T(8,128)(2,1)S(1)}, bf16[2,80,256]{2,1,0:T(8,128)(2,1)S(1)}, u32[]{:S(2)}, u32[]{:S(2)}) collective-permute-start(bf16[2,80,256]{2,1,0:T(8,128)(2,1)S(1)} %get-tuple-element.101.refs_5_), channel_id=1, source_target_pairs={{0,24},{4,28},{8,16},{12,20},{16,8},{20,12},{24,0},{28,4},{1,25},{... | collective-permute-start | bytes 245768 | tf_op jit(solution)/shard_map/ppermute | solution.py:465
  82.4 7.7 %collective-permute-start.32 = (bf16[2,80,256]{2,1,0:T(8,128)(2,1)S(1)}, bf16[2,80,256]{2,1,0:T(8,128)(2,1)S(1)}, u32[]{:S(2)}, u32[]{:S(2)}) collective-permute-start(bf16[2,80,256]{2,1,0:T(8,128)(2,1)S(1)} %get-tuple-element.105), channel_id=1, source_target_pairs={{0,8},{4,12},{8,0},{12,4},{16,24},{20,28},{24,16},{28,20},{1,9},{5... | collective-permute-start | bytes 245768 | tf_op jit(solution)/shard_map/ppermute | solution.py:465
  82.4 7.7 %collective-permute-start.33 = (bf16[2,80,256]{2,1,0:T(8,128)(2,1)S(1)}, bf16[2,80,256]{2,1,0:T(8,128)(2,1)S(1)}, u32[]{:S(2)}, u32[]{:S(2)}) collective-permute-start(bf16[2,80,256]{2,1,0:T(8,128)(2,1)S(1)} %get-tuple-element.106), channel_id=1, source_target_pairs={{0,16},{4,20},{8,24},{12,28},{16,0},{20,4},{24,8},{28,12},{1,17},{... | collective-permute-start | bytes 245768 | tf_op jit(solution)/shard_map/ppermute | solution.py:465
  84.8 6.1 %collective-permute-start.30 = (bf16[2,80,256]{2,1,0:T(8,128)(2,1)S(1)}, bf16[2,80,256]{2,1,0:T(8,128)(2,1)S(1)}, u32[]{:S(2)}, u32[]{:S(2)}) collective-permute-start(bf16[2,80,256]{2,1,0:T(8,128)(2,1)S(1)} %get-tuple-element.102.refs_0_), channel_id=1, source_target_pairs={{0,1},{1,0},{2,3},{3,2},{4,5},{5,4},{6,7},{7,6},{8,9},{9,8},{10,11... | collective-permute-start | bytes 245768 | tf_op jit(solution)/shard_map/ppermute | solution.py:468
  97.2 7.2 %collective-permute-start.43 = (bf16[2,80,256]{2,1,0:T(8,128)(2,1)S(1)}, bf16[2,80,256]{2,1,0:T(8,128)(2,1)S(1)}, u32[]{:S(2)}, u32[]{:S(2)}) collective-permute-start(bf16[2,80,256]{2,1,0:T(8,128)(2,1)S(1)} %get-tuple-element.119.refs_0_), channel_id=1, source_target_pairs={{0,24},{4,28},{8,16},{12,20},{16,8},{20,12},{24,0},{28,4},{1,25},{... | collective-permute-start | bytes 245768 | tf_op jit(solution)/shard_map/ppermute | solution.py:465
  99.0 8.4 %collective-permute-start.42 = (bf16[2,80,256]{2,1,0:T(8,128)(2,1)S(1)}, bf16[2,80,256]{2,1,0:T(8,128)(2,1)S(1)}, u32[]{:S(2)}, u32[]{:S(2)}) collective-permute-start(bf16[2,80,256]{2,1,0:T(8,128)(2,1)S(1)} %get-tuple-element.119.refs_0_), channel_id=1, source_target_pairs={{0,16},{4,20},{8,24},{12,28},{16,0},{20,4},{24,8},{28,12},{1,17},{... | collective-permute-start | bytes 245768 | tf_op jit(solution)/shard_map/ppermute | solution.py:465
  99.4 8.0 %collective-permute-start.41 = (bf16[2,80,256]{2,1,0:T(8,128)(2,1)S(1)}, bf16[2,80,256]{2,1,0:T(8,128)(2,1)S(1)}, u32[]{:S(2)}, u32[]{:S(2)}) collective-permute-start(bf16[2,80,256]{2,1,0:T(8,128)(2,1)S(1)} %get-tuple-element.119.refs_0_), channel_id=1, source_target_pairs={{0,8},{4,12},{8,0},{12,4},{16,24},{20,28},{24,16},{28,20},{1,9},{5... | collective-permute-start | bytes 245768 | tf_op jit(solution)/shard_map/ppermute | solution.py:465
  108.0 6.2 %collective-permute-start.38 = (bf16[2,80,256]{2,1,0:T(8,128)(2,1)S(1)}, bf16[2,80,256]{2,1,0:T(8,128)(2,1)S(1)}, u32[]{:S(2)}, u32[]{:S(2)}) collective-permute-start(bf16[2,80,256]{2,1,0:T(8,128)(2,1)S(1)} %get-tuple-element.115), channel_id=1, source_target_pairs={{0,8},{4,12},{8,0},{12,4},{16,24},{20,28},{24,16},{28,20},{1,9},{5... | collective-permute-start | bytes 245768 | tf_op jit(solution)/shard_map/ppermute | solution.py:465
  108.1 9.8 %collective-permute-start.39 = (bf16[2,80,256]{2,1,0:T(8,128)(2,1)S(1)}, bf16[2,80,256]{2,1,0:T(8,128)(2,1)S(1)}, u32[]{:S(2)}, u32[]{:S(2)}) collective-permute-start(bf16[2,80,256]{2,1,0:T(8,128)(2,1)S(1)} %get-tuple-element.116), channel_id=1, source_target_pairs={{0,16},{4,20},{8,24},{12,28},{16,0},{20,4},{24,8},{28,12},{1,17},{... | collective-permute-start | bytes 245768 | tf_op jit(solution)/shard_map/ppermute | solution.py:465
  111.0 6.9 %collective-permute-start.40 = (bf16[2,80,256]{2,1,0:T(8,128)(2,1)S(1)}, bf16[2,80,256]{2,1,0:T(8,128)(2,1)S(1)}, u32[]{:S(2)}, u32[]{:S(2)}) collective-permute-start(bf16[2,80,256]{2,1,0:T(8,128)(2,1)S(1)} %get-tuple-element.117.refs_5_), channel_id=1, source_target_pairs={{0,24},{4,28},{8,16},{12,20},{16,8},{20,12},{24,0},{28,4},{1,25},{... | collective-permute-start | bytes 245768 | tf_op jit(solution)/shard_map/ppermute | solution.py:465
  113.0 11.2 %collective-permute-start.48 = (bf16[2,80,128]{2,1,0:T(8,128)(2,1)S(1)}, bf16[2,80,128]{2,1,0:T(8,128)(2,1)S(1)}, u32[]{:S(2)}, u32[]{:S(2)}) collective-permute-start(bf16[2,80,128]{2,1,0:T(8,128)(2,1)S(1)} %get-tuple-element.123), channel_id=1, source_target_pairs={{0,1},{1,0},{2,3},{3,2},{4,5},{5,4},{6,7},{7,6},{8,9},{9,8},{10,11... | collective-permute-start | bytes 122888 | tf_op jit(solution)/shard_map/ppermute | solution.py:468
  118.7 10.8 %collective-permute-start.47 = (bf16[2,80,256]{2,1,0:T(8,128)(2,1)S(1)}, bf16[2,80,256]{2,1,0:T(8,128)(2,1)S(1)}, u32[]{:S(2)}, u32[]{:S(2)}) collective-permute-start(bf16[2,80,256]{2,1,0:T(8,128)(2,1)S(1)} %get-tuple-element.121.refs_0_), channel_id=1, source_target_pairs={{0,24},{4,28},{8,16},{12,20},{16,8},{20,12},{24,0},{28,4},{1,25},{... | collective-permute-start | bytes 245768 | tf_op jit(solution)/shard_map/ppermute | solution.py:465
  121.0 8.5 %collective-permute-start.46 = (bf16[2,80,256]{2,1,0:T(8,128)(2,1)S(1)}, bf16[2,80,256]{2,1,0:T(8,128)(2,1)S(1)}, u32[]{:S(2)}, u32[]{:S(2)}) collective-permute-start(bf16[2,80,256]{2,1,0:T(8,128)(2,1)S(1)} %get-tuple-element.121.refs_0_), channel_id=1, source_target_pairs={{0,16},{4,20},{8,24},{12,28},{16,0},{20,4},{24,8},{28,12},{1,17},{... | collective-permute-start | bytes 245768 | tf_op jit(solution)/shard_map/ppermute | solution.py:465
  121.9 7.6 %collective-permute-start.45 = (bf16[2,80,256]{2,1,0:T(8,128)(2,1)S(1)}, bf16[2,80,256]{2,1,0:T(8,128)(2,1)S(1)}, u32[]{:S(2)}, u32[]{:S(2)}) collective-permute-start(bf16[2,80,256]{2,1,0:T(8,128)(2,1)S(1)} %get-tuple-element.121.refs_0_), channel_id=1, source_target_pairs={{0,8},{4,12},{8,0},{12,4},{16,24},{20,28},{24,16},{28,20},{1,9},{5... | collective-permute-start | bytes 245768 | tf_op jit(solution)/shard_map/ppermute | solution.py:465
  (33 other events, 222.6 us)

commit v7 on v5

v7 whole, which is shorter than its diff:
```python
import functools

import jax
import jax.numpy as jnp
from jax import lax
from jax.experimental import pallas as pl
from jax.experimental.pallas import tpu as pltpu
from jax.sharding import PartitionSpec as P

ITERS = 2
LANES = 128
PIECES = 3
PRIME = 32749
VMEM = pl.BlockSpec(memory_space=pltpu.VMEM)
HBM = pl.BlockSpec(memory_space=pltpu.HBM)
F32 = jnp.float32
BF16 = jnp.bfloat16
NT = (((1,), (1,)), ((), ()))


def call(kernel, outs, scratch, flops, *args, space=VMEM, limit=24):
    nbytes = sum(a.size * a.dtype.itemsize for a in (*args, *outs))
    return pl.pallas_call(
        kernel,
        out_shape=outs,
        in_specs=[space] * len(args),
        out_specs=[VMEM] * len(outs),
        scratch_shapes=scratch,
        compiler_params=pltpu.CompilerParams(vmem_limit_bytes=limit * 1024 * 1024),
        cost_estimate=pl.CostEstimate(flops=flops, bytes_accessed=nbytes, transcendentals=0),
    )(*args)


def struct(shape, dtype):
    return jax.ShapeDtypeStruct(shape, dtype)


def place():
    slab = lax.axis_index("slab")
    return slab // 2, slab % 2, lax.axis_index("obs")


def add(parts):
    value = parts[0].astype(F32)
    for part in parts[1:]:
        value = value + part.astype(F32)
    return value


def split(x):
    high = x.astype(BF16)
    return high, (x - high.astype(F32)).astype(BF16)


def dot(a, b):
    (a, a_rest), (b, b_rest) = split(a), split(b)
    one = functools.partial(jnp.dot, preferred_element_type=F32)
    return one(a, b) + (one(a, b_rest) + one(a_rest, b))


def total(x):
    return jnp.sum(jnp.sum(x, axis=0, keepdims=True), axis=1, keepdims=True)


def with_scalars(body, values):
    rows = lax.broadcasted_iota(jnp.int32, body.shape, 0)
    lanes = lax.broadcasted_iota(jnp.int32, body.shape, 1)
    line = jnp.zeros(body.shape, F32)
    for q, value in enumerate(values):
        rest = value
        for piece in range(PIECES):
            part = rest.astype(BF16).astype(F32)
            rest = rest - part
            line = jnp.where(lanes == q * PIECES + piece, part, line)
    return jnp.where(rows == body.shape[0] - 1, line, body)


def read_scalars(refs, count):
    rows = refs[0].shape[0]
    tail = add([ref[rows - 16 : rows, 0:LANES] for ref in refs])
    sub = lax.broadcasted_iota(jnp.int32, tail.shape, 0)
    lanes = lax.broadcasted_iota(jnp.int32, tail.shape, 1)
    found = []
    for q in range(count):
        mine = (sub == 15) & (lanes >= q * PIECES) & (lanes < (q + 1) * PIECES)
        found.append(total(jnp.where(mine, tail, 0.0)))
    return found


def of_member(refs, spans, m):
    return [
        ref.at[m - first] for ref, (first, count) in zip(refs, spans) if first <= m < first + count
    ]


def remainder(x, factor):
    return x - (x.astype(F32) * factor).astype(jnp.int32) * PRIME


def start_kernel(
    dims, seeds_in, ids_in, cols_in, count_in, sd_in, innov_in, prec_in, h, own, partner, *rest
):
    chips, halves = dims
    outs = rest[:-12]
    seeds, ids, cols, count, sd, innov, prec, hashed, scratch, acc, sems, h_sems = rest[-12:]
    z, core, obs = place()
    blocks, lev, profiles = innov.shape
    colblocks, width = own.shape[1], own.shape[3]
    members, levp = scratch.shape[1], scratch.shape[2]

    pairs = [(seeds_in, seeds), (ids_in, ids), (cols_in, cols), (count_in, count), (sd_in, sd)]
    small = [pltpu.make_async_copy(x, y, sems.at[i]) for i, (x, y) in enumerate(pairs)]
    for copy in small:
        copy.start()
    large = []
    for b in range(blocks):
        at = len(pairs) + 2 * b
        large.append(pltpu.make_async_copy(innov_in.at[:, b, :], innov.at[b], sems.at[at]))
        large.append(pltpu.make_async_copy(prec_in.at[:, b, :], prec.at[b], sems.at[at + 1]))
    for copy in large:
        copy.start()
    own[...] = jnp.zeros_like(own)
    partner[...] = jnp.zeros_like(partner)
    scratch[...] = jnp.zeros_like(scratch)
    for copy in small:
        copy.wait()

    def tile_copy(n, half, target):
        lanes = pl.ds(half * width, width)
        return pltpu.make_async_copy(h.at[n, :, lanes], target, h_sems.at[n * halves + half])

    def put(n, carry):
        for half in range(halves):
            piece, k = ids[0, 0, n] * halves + half, cols[0, 0, n]

            @pl.when(piece % 2 == core)
            def _():
                tile_copy(n, half, own.at[piece // 2, k]).start()

            @pl.when(piece % 2 != core)
            def _():
                tile_copy(n, half, partner.at[piece // 2, k]).start()

        return carry

    lax.fori_loop(0, count[0, 0], put, 0)

    starts = [lax.rem(seeds[m], PRIME) - PRIME for m in range(members)]
    order = [(source, zz) for source in range(2) for zz in range(chips)]
    shape = (levp, width)
    spot = lax.broadcasted_iota(jnp.int32, shape, 0) * profiles
    spot = spot + lax.broadcasted_iota(jnp.int32, shape, 1)
    low = (1.0 - 2.0**-21) / PRIME

    def piece_at(at):
        source, zz = order[at]
        return 2 * zz + (core if source == 0 else 1 - core)

    def draw(at):
        piece = piece_at(at)
        first = (obs * blocks + piece // halves) * (lev * profiles) + (piece % halves) * width
        base = remainder(7919 * remainder(spot + first, 1.0 / PRIME), 1.0 / PRIME)
        for m in range(members):
            k0 = base + starts[m]
            k1 = remainder(k0 * k0 + 12345, 1.0 / PRIME)
            k2 = remainder(k1 * k1 + 2719, low)
            k2 = jnp.where(k2 >= PRIME, k2 - PRIME, k2)
            hashed[at, m] = k2.astype(F32)

    def adjoint(at):
        source, zz = order[at]
        piece = piece_at(at)
        b = piece // halves
        if halves == 1:
            p, d = prec[b], innov[b]
        else:
            lanes = pl.ds(pl.multiple_of((piece % halves) * width, LANES), width)
            p, d = prec[b, :, lanes], innov[b, :, lanes]
        gain = 3.4 * p * lax.rsqrt(p)
        offset = p * d - 0.5 * gain
        gain = gain * (1.0 / PRIME)
        for m in range(members):
            scratch[at % 2, m, 0:lev, :] = offset + gain * hashed[at, m, 0:lev, :]
        w = scratch[at % 2].astype(BF16).reshape(members * levp, width)
        tiles = (own if source == 0 else partner)[zz].reshape(colblocks * LANES, width)
        part = lax.dot_general(w, tiles, NT, preferred_element_type=F32)
        if at == 0:
            acc[...] = part
        else:
            acc[...] += part

    early = len(order) // 2
    for at in range(early):
        draw(at)
    for copy in large:
        copy.wait()

    def arrive(n, carry):
        for half in range(halves):
            tile_copy(n, half, own.at[0, 0]).wait()
        return carry

    lax.fori_loop(0, count[0, 0], arrive, 0)

    for at in range(len(order)):
        if at + early < len(order):
            draw(at + early)
        adjoint(at)

    half = colblocks * LANES // 2
    for m in range(members):
        value = acc[m * levp : (m + 1) * levp, :]
        if m == 0:
            value = with_columns(value, jnp.concatenate([sd[...]] * colblocks, axis=1), obs)
        outs[0][m] = value[:, :half].astype(BF16)
        outs[1][m] = value[:, half:].astype(BF16)


def with_columns(body, line, obs):
    rows = lax.broadcasted_iota(jnp.int32, body.shape, 0)
    mine = lax.broadcasted_iota(jnp.int32, body.shape, 1) // LANES == obs
    rest = line
    for piece in range(PIECES):
        part = rest.astype(BF16).astype(F32)
        rest = rest - part
        body = jnp.where((rows == body.shape[0] - 1 - PIECES + piece) & mine, part, body)
    return body


def read_columns(body):
    tail = body[body.shape[0] - 8 :]
    sub = lax.broadcasted_iota(jnp.int32, tail.shape, 0)
    mine = (sub >= 7 - PIECES) & (sub < 7)
    return jnp.sum(jnp.where(mine, tail, 0.0), axis=0, keepdims=True)


def precision_kernel(halves, prec, out):
    z, core, unused = place()
    piece = 2 * z + core
    lev, blocks, unused = prec.shape
    width = out.shape[1]
    block = lax.broadcasted_iota(jnp.int32, (lev, blocks, width), 1)
    if halves == 1:
        mine = prec[...]
    else:
        mine = prec[:, :, pl.ds(pl.multiple_of((piece % halves) * width, LANES), width)]
    out[...] = jnp.zeros_like(out)
    out[0:lev, :] = jnp.sum(jnp.where(block == piece // halves, mine, 0.0), axis=1)


def joined(refs, m):
    one, two = refs[: len(refs) // 2], refs[len(refs) // 2 :]
    return jnp.concatenate([add([x[m] for x in one]), add([x[m] for x in two])], axis=1)


def first_kernel(parts, *refs):
    pieces = refs[:parts]
    vert, vert_t, sd_out, residual, moved = refs[parts:]
    for m in range(residual.shape[0]):
        t = joined(pieces, m)
        if m == 0:
            sd = read_columns(t)
            sd_out[...] = sd
        r = dot(vert_t[...], sd * t)
        residual[m] = r
        x = sd * dot(vert[...], r)
        moved[m] = with_scalars(x, [total(r * r)]).astype(BF16)


def add_kernel(scalars, *refs):
    parts, out = refs[:-1], refs[-1]
    for m in range(out.shape[0]):
        value = add([x[m] for x in parts])
        if scalars:
            value = with_scalars(value, read_scalars([x.at[m] for x in parts], scalars))
        out[m] = value.astype(BF16)


def add_halves_kernel(scalars, one, one_more, two, two_more, one_out, two_out):
    add_kernel(scalars, one, one_more, one_out)
    add_kernel(0, two, two_more, two_out)


def stage_kernel(one, two, one_out, two_out, sems):
    copies = [
        pltpu.make_async_copy(x, y, sems.at[i])
        for i, (x, y) in enumerate([(one, one_out), (two, two_out)])
    ]
    for copy in copies:
        copy.start()
    for copy in copies:
        copy.wait()


def forward_kernel(plan, mine, other, own, partner, *outs):
    z, core, obs = place()
    members, levp, lanes = mine.shape
    chips, width = own.shape[0], own.shape[3]
    rows = members * levp
    scalars = [read_scalars([mine.at[m], other.at[m]], 2) for m in range(members)]
    for i in reversed(range(chips)):
        zz = z ^ i
        y = jnp.dot(
            mine[...].reshape(rows, lanes),
            own[zz].reshape(lanes, width),
            preferred_element_type=F32,
        )
        y = y + jnp.dot(
            other[...].reshape(rows, lanes),
            partner[zz].reshape(lanes, width),
            preferred_element_type=F32,
        )
        y = y.reshape(members, levp, width)
        for out, (chip, first, count) in zip(outs, plan):
            if chip == i:
                for m in range(count):
                    value = with_scalars(y[first + m], scalars[first + m])
                    out[m] = value.astype(out.dtype)


def weigh_kernel(later, spans, *refs):
    ys, refs = refs[: len(spans)], refs[len(spans) :]
    prec = refs[0]
    image, state, weighted, *parts = refs[3 if later else 1 :]
    p = prec[...]
    for m in range(image.shape[0]):
        mine = of_member(ys, spans, m)
        y = add([x[...] for x in mine])
        norm, cross = read_scalars(mine, 2)
        if later:
            old_image, old = refs[1:3]
            old_norm, old_square = old[m, 0:1, 0:1], old[m, 1:2, 0:1]
            beta = norm / old_norm
            square = norm + 2.0 * beta * cross + beta * beta * old_square
            y = y + beta * old_image[m]
        else:
            beta = jnp.zeros_like(norm)
            square = norm
        scaled = p * y
        image[m] = y
        value = with_scalars(scaled, [total(scaled * y)]).astype(BF16)
        weighted[m] = value
        first = 0
        for part in parts:
            if first <= m < first + part.shape[0]:
                part[m - first] = value
            first += part.shape[0]
        sub = lax.broadcasted_iota(jnp.int32, (8, LANES), 0)
        state[m] = jnp.where(sub == 0, norm, jnp.where(sub == 1, square, beta))


def adjoint_kernel(plan, *refs):
    z, core, obs = place()
    ws, tiles, out = refs[: len(plan)], refs[len(plan)], refs[len(plan) + 1]
    members, levp, lanes = out.shape
    width = ws[0].shape[2]
    acc = None
    for i in range(tiles.shape[0]):
        w = [ref[...].reshape(-1, width) for ref, (chip, *span) in zip(ws, plan) if chip == i]
        w = w[0] if len(w) == 1 else jnp.concatenate(w, axis=0)
        part = lax.dot_general(
            w, tiles[z ^ i].reshape(lanes, width), NT, preferred_element_type=F32
        )
        acc = part if i == 0 else acc + part
    acc = acc.reshape(members, levp, lanes)
    spans = [span for chip, *span in plan]
    for m in range(members):
        energy = read_scalars(of_member(ws, spans, m), 1)
        out[m] = with_scalars(acc[m], energy).astype(out.dtype)


def combine_kernel(mine, theirs, one, two):
    half = one.shape[2]
    for m in range(one.shape[0]):
        energy = read_scalars([mine.at[m], theirs.at[m]], 1)
        value = mine[m] + theirs[m].astype(F32)
        one[m] = with_scalars(value[:, :half], energy).astype(BF16)
        two[m] = value[:, half:].astype(BF16)


def combine_columns_kernel(mine, theirs, *outs):
    obs = lax.axis_index("obs")
    for m in range(mine.shape[0]):
        energy = read_scalars([mine.at[m], theirs.at[m]], 1)
        for i, out in enumerate(outs):
            lane = pl.ds(pl.multiple_of((obs ^ i) * LANES, LANES), LANES)
            value = mine[m, :, lane] + theirs[m, :, lane].astype(F32)
            out[m] = with_scalars(value, energy).astype(BF16)


def update_kernel(parts, later, *refs):
    pieces, refs = refs[:parts], refs[parts:]
    sd, vert, vert_t, state, residual = refs[:5]
    if later:
        old_direction, old_solution, residual_out, solution_out, moved, direction_out = refs[5:]
    else:
        residual_out, solution_out, moved = refs[5:]
    obs = lax.axis_index("obs")
    mine = pl.ds(pl.multiple_of(obs * LANES, LANES), LANES)
    for m in range(residual.shape[0]):
        t = joined(pieces, m)
        (energy,) = read_scalars([x.at[m] for x in pieces[: parts // 2]], 1)
        norm, square, beta = state[m, 0:1, 0:1], state[m, 1:2, 0:1], state[m, 2:3, 0:1]
        alpha = norm / (square + energy)
        r = residual[m]
        if later:
            d = r + beta * old_direction[m]
            direction_out[m] = d
            step = direction_out[m, :, mine]
            solution_out[m] = old_solution[m] + alpha * step
        else:
            d = r
            solution_out[m] = alpha * residual[m, :, mine]
        r = r - alpha * (d + dot(vert_t[...], sd[...] * t))
        residual_out[m] = r
        x = sd[...] * dot(vert[...], r)
        moved[m] = with_scalars(x, [total(r * r), total(r * d)]).astype(BF16)


def last_kernel(parts, later, lev, *refs):
    pieces, refs = refs[:parts], refs[parts:]
    sd, vert, vert_t, state, residual = refs[:5]
    increment_out, residual_out = refs[-2:]
    obs = lax.axis_index("obs")
    mine = pl.ds(pl.multiple_of(obs * LANES, LANES), LANES)
    for m in range(residual.shape[0]):
        t = add([x[m] for x in pieces])
        (energy,) = read_scalars([x.at[m] for x in pieces], 1)
        norm, square, beta = state[m, 0:1, 0:1], state[m, 1:2, 0:1], state[m, 2:3, 0:1]
        alpha = norm / (square + energy)
        d = r = residual[m, :, mine]
        if later:
            old_direction, old_solution = refs[5:7]
            d = r + beta * old_direction[m, :, mine]
        solution = alpha * d
        if later:
            solution = old_solution[m] + solution
        r = r - alpha * (d + dot(vert_t[...], sd[...] * t))
        increment = sd[...] * dot(vert[...], solution)
        increment_out[:, m, :] = increment[0:lev]
        residual_out[:, m, :] = r[0:lev]


def per_device(
    n_slab,
    n_obs,
    innovation,
    obs_precision,
    seeds,
    col_sd,
    vert_factor,
    h_values,
    block_obs,
    block_col,
    entry_count,
):
    blocks, lev, profiles = innovation.shape
    members = seeds.shape[0]
    chips = n_slab // 2
    halves = n_slab // blocks
    width = profiles // halves
    colblocks = n_obs
    assert halves * blocks == n_slab and width % LANES == 0 and col_sd.shape[0] == 1
    assert chips & (chips - 1) == 0 and n_obs & (n_obs - 1) == 0
    levp = (lev + 1 + 15) // 16 * 16
    rows = members * levp
    lanes = colblocks * LANES
    field = (members, levp, LANES)
    half_field = (members, levp, lanes // 2)
    slab_field = (members, levp, lanes)
    panel = (members, levp, width)
    some, rest = members // 2, members - members // 2
    via = chips == 4 and some > 0
    if via:
        plan = [(0, 0, members), (1, 0, members)]
        plan += [(i, *span) for i in (2, 3) for span in ((0, some), (some, rest))]
    else:
        plan = [(i, 0, members) for i in range(chips)]
    pad = ((0, levp - lev), (0, levp - lev))
    vert = jnp.pad(vert_factor, pad)
    vert_t = jnp.pad(vert_factor.T, pad)
    h_block = h_values.reshape(h_values.shape[2:])
    innovation = jnp.transpose(innovation, (1, 0, 2))
    obs_precision = jnp.transpose(obs_precision, (1, 0, 2))
    product = n_slab * width * lanes * rows
    small = 12 * rows * levp * LANES
    plane_bits = [1 << k for k in range(n_obs.bit_length() - 1)]

    def along(x, i):
        return lax.ppermute(x, "slab", [(s, s ^ (2 * i)) for s in range(n_slab)])

    def plane(x, i):
        return lax.ppermute(x, "obs", [(o, o ^ i) for o in range(n_obs)])

    def swap(x):
        return lax.ppermute(x, "slab", [(s, s ^ 1) for s in range(n_slab)])

    def plane_sum(one, two, scalars):
        for step, bit in enumerate(plane_bits):
            far = plane_bits[len(plane_bits) - 1 - step]
            one_more, two_more = plane(one, bit), plane(two, far)
            if step == 0 and not scalars:
                one, two = call(
                    stage_kernel,
                    [struct(half_field, BF16)] * 2,
                    [pltpu.SemaphoreType.DMA((2,))],
                    0,
                    one,
                    two,
                    space=HBM,
                )
            parts = [one, one_more, two, two_more]
            if step < len(plane_bits) - 1:
                one, two = call(
                    functools.partial(add_halves_kernel, scalars),
                    [struct(half_field, BF16)] * 2,
                    [],
                    0,
                    *parts,
                )
        return parts

    def line_sum(ys):
        if not via:
            return [y if i == 0 else along(y, i) for i, y in enumerate(ys)], [
                (0, members) for y in ys
            ]
        near, next_, far, far_rest, last_, last_rest = ys
        passed = along(last_, 1)
        far_rest, last_rest, next_ = along(far_rest, 2), along(last_rest, 3), along(next_, 1)
        (far,) = call(
            functools.partial(add_kernel, 2),
            [struct((some, levp, width), BF16)],
            [],
            0,
            far,
            passed,
        )
        spans = [(0, members), (0, members), (0, some), (some, rest), (some, rest)]
        return [near, next_, along(far, 2), far_rest, last_rest], spans

    def line_gather(w, *parts):
        if not via:
            return [w if i == 0 else along(w, i) for i in range(chips)]
        one, two = parts
        far = along(one, 2)
        far_rest, last_rest, next_ = along(two, 2), along(two, 3), along(w, 1)
        return [w, next_, far, far_rest, along(far, 1), last_rest]

    dense = struct((chips, colblocks, LANES, width), BF16)
    own, for_partner, *partials = call(
        functools.partial(start_kernel, (chips, halves)),
        [dense, dense] + [struct(half_field, BF16)] * 2,
        [
            pltpu.SMEM(seeds.shape, jnp.int32),
            pltpu.SMEM(block_obs.shape, jnp.int32),
            pltpu.SMEM(block_col.shape, jnp.int32),
            pltpu.SMEM(entry_count.shape, jnp.int32),
            pltpu.VMEM(col_sd.shape, F32),
            pltpu.VMEM((blocks, lev, profiles), F32),
            pltpu.VMEM((blocks, lev, profiles), F32),
            pltpu.VMEM((n_slab, members, levp, width), F32),
            pltpu.VMEM((2, members, levp, width), F32),
            pltpu.VMEM((rows, lanes), F32),
            pltpu.SemaphoreType.DMA((5 + 2 * blocks,)),
            pltpu.SemaphoreType.DMA((h_block.shape[0] * halves,)),
        ],
        2 * product,
        seeds,
        block_obs,
        block_col,
        entry_count,
        col_sd,
        innovation,
        obs_precision,
        h_block,
        space=HBM,
        limit=60,
    )
    ps = plane_sum(*partials, 0)
    partner = swap(for_partner)
    (precision,) = call(
        functools.partial(precision_kernel, halves),
        [struct((levp, width), F32)],
        [],
        0,
        obs_precision,
    )
    slab_sd, residual, moved = call(
        functools.partial(first_kernel, len(ps)),
        [struct((1, lanes), F32), struct(slab_field, F32), struct(slab_field, BF16)],
        [],
        small * colblocks,
        *ps,
        vert,
        vert_t,
    )
    direction = total_step = image = state = None
    for sweep in range(ITERS):
        later, last = sweep > 0, sweep == ITERS - 1
        ys = call(
            functools.partial(forward_kernel, plan),
            [
                struct((count, levp, width), F32 if at == 0 or (via and at == 2) else BF16)
                for at, (unused, unused, count) in enumerate(plan)
            ],
            [],
            2 * product,
            moved,
            swap(moved),
            own,
            partner,
        )
        ys, spans = line_sum(ys)
        image, state, *weighted = call(
            functools.partial(weigh_kernel, later, spans),
            [struct(panel, F32), struct((members, 8, LANES), F32), struct(panel, BF16)]
            + ([struct((n, levp, width), BF16) for n in (some, rest)] if via else []),
            [],
            0,
            *ys,
            precision,
            *([image, state] if later else []),
        )
        ws = line_gather(*weighted)
        (theirs,) = call(
            functools.partial(adjoint_kernel, plan),
            [struct(slab_field, BF16)],
            [],
            product,
            *ws,
            partner,
        )
        theirs = swap(theirs)
        (mine,) = call(
            functools.partial(adjoint_kernel, plan),
            [struct(slab_field, F32)],
            [],
            product,
            *ws,
            own,
        )
        known = [vert, vert_t, state, residual]
        if later:
            known += [direction, total_step]
        if last:
            ps = call(
                combine_columns_kernel, [struct(field, BF16)] * n_obs, [], 0, mine, theirs
            )
            ps = [x if i == 0 else plane(x, i) for i, x in enumerate(ps)]
            outputs = call(
                functools.partial(last_kernel, len(ps), later, lev),
                [struct((lev, members, LANES), F32)] * 2,
                [],
                small,
                *ps,
                col_sd,
                *known,
            )
            break
        ps = call(combine_kernel, [struct(half_field, BF16)] * 2, [], 0, mine, theirs)
        ps = plane_sum(*ps, 1)
        outs = [struct(slab_field, F32), struct(field, F32), struct(slab_field, BF16)]
        if later:
            outs.append(struct(slab_field, F32))
        r, total_step, moved, *d = call(
            functools.partial(update_kernel, len(ps), later),
            outs,
            [],
            small * colblocks,
            *ps,
            slab_sd,
            *known,
        )
        direction, residual = (d[0] if later else residual), r
    return tuple(jnp.transpose(x, (1, 0, 2))[None] for x in outputs)


def solution(mesh):
    return jax.shard_map(
        functools.partial(per_device, mesh.shape["slab"], mesh.shape["obs"]),
        mesh=mesh,
        in_specs=(
            P("obs", None, None),
            P("obs", None, None),
            P(),
            P(("slab", "obs"), None),
            P(),
            P("slab", "obs", None, None, None),
            P("slab", "obs", None),
            P("slab", "obs", None),
            P("slab", "obs"),
        ),
        out_specs=(P(("slab", "obs"), None, None, None), P(("slab", "obs"), None, None, None)),
        check_vma=False,
    )
```

time: 127 us -> 117 us (0.921)
  waiting for transfers between devices: 79.3 us -> 60.4 us
  starting transfers between devices: 27.5 us -> 37.7 us
    ppermute x12 -> x20, waiting for transfers between devices: 49 us -> 33.9 us  [along(): return lax.ppermute(x, 'slab', [(s, s ^ 2 * i) for s in range(n_slab)])]
    ppermute x12 -> x20, starting transfers between devices: 14 us -> 23.5 us  [along(): return lax.ppermute(x, 'slab', [(s, s ^ 2 * i) for s in range(n_slab)])]
    ppermute x11, waiting for transfers between devices: 23.9 us -> 21.2 us  [plane(): return lax.ppermute(x, 'obs', [(o, o ^ i) for o in range(n_obs)])]
    unnamed x15 -> x13, local copies, waits for them, and re-layouts: 3.17 us -> 1.98 us
    pallas_call x17 -> x20, Pallas kernels: 15 us -> 15.2 us  [call(): pl.pallas_call(kernel, out_shape=outs, in_specs=[space] * len(args), out_...]
  transfers between devices with their start and end apart: 28 -> 36, of which waited for: 27 -> 29; matrix products, arithmetic and copies ran while one was open for 0% -> 0% of each run, Pallas kernels for 1% -> 3%
where the time goes in v7:
time: 117 us
  waiting for transfers between devices  60.4 us (52%)
  starting transfers between devices  37.7 us (32%)
  Pallas kernels  15.2 us (13%)
  local copies, waits for them, and re-layouts  2 us (2%)
  between operations  1.49 us (1%)
    ppermute x20, waiting for transfers between devices, along(): return lax.ppermute(x, 'slab', [(s, s ^ 2 * i) for s in range(n_slab)])  33.9 us
    ppermute x20, starting transfers between devices, along(): return lax.ppermute(x, 'slab', [(s, s ^ 2 * i) for s in range(n_slab)])  23.5 us
    ppermute x11, waiting for transfers between devices, plane(): return lax.ppermute(x, 'obs', [(o, o ^ i) for o in range(n_obs)])  21.2 us
    pallas_call x20, Pallas kernels, call(): pl.pallas_call(kernel, out_shape=outs, in_specs=[space] * len(args), out_...  15.2 us
    ppermute x11, starting transfers between devices, plane(): return lax.ppermute(x, 'obs', [(o, o ^ i) for o in range(n_obs)])  13.4 us
    ppermute x5, waiting for transfers between devices, swap(): return lax.ppermute(x, 'slab', [(s, s ^ 1) for s in range(n_slab)])  5.35 us
  transfers between devices with their start and end apart: 36, of which 29 were waited for; matrix products, arithmetic and copies ran while one was open for 0% of the time, Pallas kernels for 3%

profile of v7, /device:TPU:0, one launch (start us, length us, event | category | flops | bytes accessed | tf_op | source)
XLA Modules:
  0.0 116.8 jit_solution(6284706854347582415)
XLA Ops:
  1.3 5.3 %shard_map.104 = (bf16[4,4,128,256]{3,2,1,0:T(8,128)(2,1)}, bf16[4,4,128,256]{3,2,1,0:T(8,128)(2,1)}, bf16[4,80,256]{2,1,0:T(8,128)(2,1)}, bf16[4,80,256]{2,1,0:T(8,128)(2,1)}) custom-call(s32[4]{0:T(128)} %seeds_in.1, s32[1,1,32]{2,1,0:T(1,128)} %ids_in.1, s32[1,1,32]{2,1,0:T(1,128)} %cols_in.1, s32[1,1]{1,0:T(1,128)S(6)} %copy.12.count_in, ...), custom_call_target="tpu_custom_call" | custom-call | flops 671088640 | bytes 5751572 | tf_op jit(solution)/shard_map/pallas_call | solution.py:23
  7.1 3.1 %collective-permute-start = (bf16[4,80,256]{2,1,0:T(8,128)(2,1)}, bf16[4,80,256]{2,1,0:T(8,128)(2,1)S(1)}, u32[]{:S(2)}, u32[]{:S(2)}) collective-permute-start(bf16[4,80,256]{2,1,0:T(8,128)(2,1)} %get-tuple-element.47.one), channel_id=1, source_target_pairs={{0,1},{1,0},{2,3},{3,2},{4,5},{5,4},{6,7},{7,6},{8,9},{9,8},{10,11... | collective-permute-start | bytes 491528 | tf_op jit(solution)/shard_map/ppermute | solution.py:493
  13.4 1.8 %collective-permute-done.one_more = bf16[4,80,256]{2,1,0:T(8,128)(2,1)S(1)} collective-permute-done((bf16[4,80,256]{2,1,0:T(8,128)(2,1)}, bf16[4,80,256]{2,1,0:T(8,128)(2,1)S(1)}, u32[]{:S(2)}, u32[]{:S(2)}) %collective-permute-start) | collective-permute-done | bytes 163872 | tf_op jit(solution)/shard_map/ppermute | solution.py:493
  15.2 1.5 %collective-permute-done.1.two_more = bf16[4,80,256]{2,1,0:T(8,128)(2,1)S(1)} collective-permute-done((bf16[4,80,256]{2,1,0:T(8,128)(2,1)}, bf16[4,80,256]{2,1,0:T(8,128)(2,1)S(1)}, u32[]{:S(2)}, u32[]{:S(2)}) %collective-permute-start.1) | collective-permute-done | bytes 163872 | tf_op jit(solution)/shard_map/ppermute | solution.py:493
  19.0 3.3 %collective-permute-done.2.refs_1_ = bf16[4,80,256]{2,1,0:T(8,128)(2,1)S(1)} collective-permute-done((bf16[4,80,256]{2,1,0:T(8,128)(2,1)S(1)}, bf16[4,80,256]{2,1,0:T(8,128)(2,1)S(1)}, u32[]{:S(2)}, u32[]{:S(2)}) %collective-permute-start.2) | collective-permute-done | bytes 163872 | tf_op jit(solution)/shard_map/ppermute | solution.py:493
  24.4 1.6 %collective-permute-done.4.other = bf16[4,80,512]{2,1,0:T(8,128)(2,1)S(1)} collective-permute-done((bf16[4,80,512]{2,1,0:T(8,128)(2,1)S(1)}, bf16[4,80,512]{2,1,0:T(8,128)(2,1)S(1)}, u32[]{:S(2)}, u32[]{:S(2)}) %collective-permute-start.4) | collective-permute-done | bytes 327712 | tf_op jit(solution)/shard_map/ppermute | solution.py:496
  26.9 1.7 %collective-permute-start.7 = (bf16[2,80,256]{2,1,0:T(8,128)(2,1)S(1)}, bf16[2,80,256]{2,1,0:T(8,128)(2,1)S(1)}, u32[]{:S(2)}, u32[]{:S(2)}) collective-permute-start(bf16[2,80,256]{2,1,0:T(8,128)(2,1)S(1)} %get-tuple-element.59), channel_id=1, source_target_pairs={{0,8},{4,12},{8,0},{12,4},{16,24},{20,28},{24,16},{28,20},{1,9},{5... | collective-permute-start | bytes 245768 | tf_op jit(solution)/shard_map/ppermute | solution.py:490
  29.0 3.1 %collective-permute-start.9 = (bf16[2,80,256]{2,1,0:T(8,128)(2,1)S(1)}, bf16[2,80,256]{2,1,0:T(8,128)(2,1)S(1)}, u32[]{:S(2)}, u32[]{:S(2)}) collective-permute-start(bf16[2,80,256]{2,1,0:T(8,128)(2,1)S(1)} %get-tuple-element.60), channel_id=1, source_target_pairs={{0,16},{4,20},{8,24},{12,28},{16,0},{20,4},{24,8},{28,12},{1,17},{... | collective-permute-start | bytes 245768 | tf_op jit(solution)/shard_map/ppermute | solution.py:490
  33.1 2.5 %collective-permute-start.8 = (bf16[2,80,256]{2,1,0:T(8,128)(2,1)S(1)}, bf16[2,80,256]{2,1,0:T(8,128)(2,1)S(1)}, u32[]{:S(2)}, u32[]{:S(2)}) collective-permute-start(bf16[2,80,256]{2,1,0:T(8,128)(2,1)S(1)} %shard_map.109), channel_id=1, source_target_pairs={{0,16},{4,20},{8,24},{12,28},{16,0},{20,4},{24,8},{28,12},{1,17},{... | collective-permute-start | bytes 245768 | tf_op jit(solution)/shard_map/ppermute | solution.py:490
  36.7 5.2 %collective-permute-done.10.refs_4_ = bf16[2,80,256]{2,1,0:T(8,128)(2,1)S(1)} collective-permute-done((bf16[2,80,256]{2,1,0:T(8,128)(2,1)S(1)}, bf16[2,80,256]{2,1,0:T(8,128)(2,1)S(1)}, u32[]{:S(2)}, u32[]{:S(2)}) %collective-permute-start.10) | collective-permute-done | bytes 81952 | tf_op jit(solution)/shard_map/ppermute | solution.py:490
  42.0 1.6 %collective-permute-done.8.refs_2_ = bf16[2,80,256]{2,1,0:T(8,128)(2,1)S(1)} collective-permute-done((bf16[2,80,256]{2,1,0:T(8,128)(2,1)S(1)}, bf16[2,80,256]{2,1,0:T(8,128)(2,1)S(1)}, u32[]{:S(2)}, u32[]{:S(2)}) %collective-permute-start.8) | collective-permute-done | bytes 81952 | tf_op jit(solution)/shard_map/ppermute | solution.py:490
  44.7 2.3 %collective-permute-start.11 = (bf16[4,80,256]{2,1,0:T(8,128)(2,1)S(1)}, bf16[4,80,256]{2,1,0:T(8,128)(2,1)S(1)}, u32[]{:S(2)}, u32[]{:S(2)}) collective-permute-start(bf16[4,80,256]{2,1,0:T(8,128)(2,1)S(1)} %get-tuple-element.62.refs_0_), channel_id=1, source_target_pairs={{0,8},{4,12},{8,0},{12,4},{16,24},{20,28},{24,16},{28,20},{1,9},{5... | collective-permute-start | bytes 491528 | tf_op jit(solution)/shard_map/ppermute | solution.py:490
  48.5 3.5 %collective-permute-done.12.refs_2_ = bf16[2,80,256]{2,1,0:T(8,128)(2,1)S(1)} collective-permute-done((bf16[2,80,256]{2,1,0:T(8,128)(2,1)S(1)}, bf16[2,80,256]{2,1,0:T(8,128)(2,1)S(1)}, u32[]{:S(2)}, u32[]{:S(2)}) %collective-permute-start.12) | collective-permute-done | bytes 81952 | tf_op jit(solution)/shard_map/ppermute | solution.py:490
  52.0 3.0 %collective-permute-done.15.refs_5_ = bf16[2,80,256]{2,1,0:T(8,128)(2,1)S(1)} collective-permute-done((bf16[2,80,256]{2,1,0:T(8,128)(2,1)S(1)}, bf16[2,80,256]{2,1,0:T(8,128)(2,1)S(1)}, u32[]{:S(2)}, u32[]{:S(2)}) %collective-permute-start.15) | collective-permute-done | bytes 81952 | tf_op jit(solution)/shard_map/ppermute | solution.py:490
  55.0 1.5 %collective-permute-done.13.refs_3_ = bf16[2,80,256]{2,1,0:T(8,128)(2,1)S(1)} collective-permute-done((bf16[2,80,256]{2,1,0:T(8,128)(2,1)S(1)}, bf16[2,80,256]{2,1,0:T(8,128)(2,1)S(1)}, u32[]{:S(2)}, u32[]{:S(2)}) %collective-permute-start.13) | collective-permute-done | bytes 81952 | tf_op jit(solution)/shard_map/ppermute | solution.py:490
  60.9 4.7 %collective-permute-done.17.one_more = bf16[4,80,256]{2,1,0:T(8,128)(2,1)S(1)} collective-permute-done((bf16[4,80,256]{2,1,0:T(8,128)(2,1)S(1)}, bf16[4,80,256]{2,1,0:T(8,128)(2,1)S(1)}, u32[]{:S(2)}, u32[]{:S(2)}) %collective-permute-start.17) | collective-permute-done | bytes 163872 | tf_op jit(solution)/shard_map/ppermute | solution.py:493
  68.3 3.3 %collective-permute-done.19.refs_1_ = bf16[4,80,256]{2,1,0:T(8,128)(2,1)S(1)} collective-permute-done((bf16[4,80,256]{2,1,0:T(8,128)(2,1)S(1)}, bf16[4,80,256]{2,1,0:T(8,128)(2,1)S(1)}, u32[]{:S(2)}, u32[]{:S(2)}) %collective-permute-start.19) | collective-permute-done | bytes 163872 | tf_op jit(solution)/shard_map/ppermute | solution.py:493
  72.4 1.3 %shard_map.116 = (f32[4,80,512]{2,1,0:T(8,128)S(1)}, f32[4,80,128]{2,1,0:T(8,128)S(1)}, bf16[4,80,512]{2,1,0:T(8,128)(2,1)S(1)}) custom-call(bf16[4,80,256]{2,1,0:T(8,128)(2,1)S(1)} %get-tuple-element.67.refs_0_, bf16[4,80,256]{2,1,0:T(8,128)(2,1)S(1)} %collective-permute-done.19.refs_1_, bf16[4,80,256]{2,1,0:T(8,128)(2,1)S(1)} %get-tuple-element.68.refs_2_, ...), custom_call_target="tpu_custom_call" | custom-call | flops 157286400 | bytes 2527232 | tf_op jit(solution)/shard_map/pallas_call | solution.py:23
  73.8 1.6 %collective-permute-done.21.other = bf16[4,80,512]{2,1,0:T(8,128)(2,1)S(1)} collective-permute-done((bf16[4,80,512]{2,1,0:T(8,128)(2,1)S(1)}, bf16[4,80,512]{2,1,0:T(8,128)(2,1)S(1)}, u32[]{:S(2)}, u32[]{:S(2)}) %collective-permute-start.21) | collective-permute-done | bytes 327712 | tf_op jit(solution)/shard_map/ppermute | solution.py:496
  76.8 1.6 %collective-permute-start.22 = (bf16[4,80,256]{2,1,0:T(8,128)(2,1)S(1)}, bf16[4,80,256]{2,1,0:T(8,128)(2,1)S(1)}, u32[]{:S(2)}, u32[]{:S(2)}) collective-permute-start(bf16[4,80,256]{2,1,0:T(8,128)(2,1)S(1)} %get-tuple-element.74), channel_id=1, source_target_pairs={{0,8},{4,12},{8,0},{12,4},{16,24},{20,28},{24,16},{28,20},{1,9},{5... | collective-permute-start | bytes 491528 | tf_op jit(solution)/shard_map/ppermute | solution.py:490
  78.9 2.3 %collective-permute-start.26 = (bf16[2,80,256]{2,1,0:T(8,128)(2,1)S(1)}, bf16[2,80,256]{2,1,0:T(8,128)(2,1)S(1)}, u32[]{:S(2)}, u32[]{:S(2)}) collective-permute-start(bf16[2,80,256]{2,1,0:T(8,128)(2,1)S(1)} %get-tuple-element.78), channel_id=1, source_target_pairs={{0,24},{4,28},{8,16},{12,20},{16,8},{20,12},{24,0},{28,4},{1,25},{... | collective-permute-start | bytes 245768 | tf_op jit(solution)/shard_map/ppermute | solution.py:490
  82.7 2.2 %collective-permute-done.25.refs_3_ = bf16[2,80,256]{2,1,0:T(8,128)(2,1)S(1)} collective-permute-done((bf16[2,80,256]{2,1,0:T(8,128)(2,1)S(1)}, bf16[2,80,256]{2,1,0:T(8,128)(2,1)S(1)}, u32[]{:S(2)}, u32[]{:S(2)}) %collective-permute-start.25) | collective-permute-done | bytes 81952 | tf_op jit(solution)/shard_map/ppermute | solution.py:490
  84.9 3.6 %collective-permute-done.26.refs_4_ = bf16[2,80,256]{2,1,0:T(8,128)(2,1)S(1)} collective-permute-done((bf16[2,80,256]{2,1,0:T(8,128)(2,1)S(1)}, bf16[2,80,256]{2,1,0:T(8,128)(2,1)S(1)}, u32[]{:S(2)}, u32[]{:S(2)}) %collective-permute-start.26) | collective-permute-done | bytes 81952 | tf_op jit(solution)/shard_map/ppermute | solution.py:490
  88.5 3.5 %collective-permute-done.24.refs_2_ = bf16[2,80,256]{2,1,0:T(8,128)(2,1)S(1)} collective-permute-done((bf16[2,80,256]{2,1,0:T(8,128)(2,1)S(1)}, bf16[2,80,256]{2,1,0:T(8,128)(2,1)S(1)}, u32[]{:S(2)}, u32[]{:S(2)}) %collective-permute-start.24) | collective-permute-done | bytes 81952 | tf_op jit(solution)/shard_map/ppermute | solution.py:490
  92.9 2.3 %collective-permute-start.27 = (bf16[4,80,256]{2,1,0:T(8,128)(2,1)S(1)}, bf16[4,80,256]{2,1,0:T(8,128)(2,1)S(1)}, u32[]{:S(2)}, u32[]{:S(2)}) collective-permute-start(bf16[4,80,256]{2,1,0:T(8,128)(2,1)S(1)} %get-tuple-element.80.refs_0_), channel_id=1, source_target_pairs={{0,8},{4,12},{8,0},{12,4},{16,24},{20,28},{24,16},{28,20},{1,9},{5... | collective-permute-start | bytes 491528 | tf_op jit(solution)/shard_map/ppermute | solution.py:490
  95.2 2.1 %collective-permute-start.31 = (bf16[2,80,256]{2,1,0:T(8,128)(2,1)S(1)}, bf16[2,80,256]{2,1,0:T(8,128)(2,1)S(1)}, u32[]{:S(2)}, u32[]{:S(2)}) collective-permute-start(bf16[2,80,256]{2,1,0:T(8,128)(2,1)S(1)} %get-tuple-element.82), channel_id=1, source_target_pairs={{0,24},{4,28},{8,16},{12,20},{16,8},{20,12},{24,0},{28,4},{1,25},{... | collective-permute-start | bytes 245768 | tf_op jit(solution)/shard_map/ppermute | solution.py:490
  97.3 1.5 %collective-permute-done.28.refs_2_ = bf16[2,80,256]{2,1,0:T(8,128)(2,1)S(1)} collective-permute-done((bf16[2,80,256]{2,1,0:T(8,128)(2,1)S(1)}, bf16[2,80,256]{2,1,0:T(8,128)(2,1)S(1)}, u32[]{:S(2)}, u32[]{:S(2)}) %collective-permute-start.28) | collective-permute-done | bytes 81952 | tf_op jit(solution)/shard_map/ppermute | solution.py:490
  99.6 4.5 %collective-permute-done.31.refs_5_ = bf16[2,80,256]{2,1,0:T(8,128)(2,1)S(1)} collective-permute-done((bf16[2,80,256]{2,1,0:T(8,128)(2,1)S(1)}, bf16[2,80,256]{2,1,0:T(8,128)(2,1)S(1)}, u32[]{:S(2)}, u32[]{:S(2)}) %collective-permute-start.31) | collective-permute-done | bytes 81952 | tf_op jit(solution)/shard_map/ppermute | solution.py:490
  107.4 1.5 %collective-permute-start.33 = (bf16[4,80,128]{2,1,0:T(8,128)(2,1)S(1)}, bf16[4,80,128]{2,1,0:T(8,128)(2,1)S(1)}, u32[]{:S(2)}, u32[]{:S(2)}) collective-permute-start(bf16[4,80,128]{2,1,0:T(8,128)(2,1)S(1)} %get-tuple-element.84), channel_id=1, source_target_pairs={{0,1},{1,0},{2,3},{3,2},{4,5},{5,4},{6,7},{7,6},{8,9},{9,8},{10,11... | collective-permute-start | bytes 245768 | tf_op jit(solution)/shard_map/ppermute | solution.py:493
  108.9 1.4 %collective-permute-start.34 = (bf16[4,80,128]{2,1,0:T(8,128)(2,1)S(1)}, bf16[4,80,128]{2,1,0:T(8,128)(2,1)S(1)}, u32[]{:S(2)}, u32[]{:S(2)}) collective-permute-start(bf16[4,80,128]{2,1,0:T(8,128)(2,1)S(1)} %get-tuple-element.85), channel_id=1, source_target_pairs={{0,2},{1,3},{2,0},{3,1},{4,6},{5,7},{6,4},{7,5},{8,10},{9,11},{10,... | collective-permute-start | bytes 245768 | tf_op jit(solution)/shard_map/ppermute | solution.py:493
  112.0 1.4 %collective-permute-done.34.refs_2_ = bf16[4,80,128]{2,1,0:T(8,128)(2,1)S(1)} collective-permute-done((bf16[4,80,128]{2,1,0:T(8,128)(2,1)S(1)}, bf16[4,80,128]{2,1,0:T(8,128)(2,1)S(1)}, u32[]{:S(2)}, u32[]{:S(2)}) %collective-permute-start.34) | collective-permute-done | bytes 81952 | tf_op jit(solution)/shard_map/ppermute | solution.py:493
  113.4 2.2 %collective-permute-done.35.refs_3_ = bf16[4,80,128]{2,1,0:T(8,128)(2,1)S(1)} collective-permute-done((bf16[4,80,128]{2,1,0:T(8,128)(2,1)S(1)}, bf16[4,80,128]{2,1,0:T(8,128)(2,1)S(1)}, u32[]{:S(2)}, u32[]{:S(2)}) %collective-permute-start.35) | collective-permute-done | bytes 81952 | tf_op jit(solution)/shard_map/ppermute | solution.py:493
  (75 shorter events, 33.5 us)
Async XLA Ops:
  6.6 19.5 %collective-permute-start.5 = (bf16[4,4,128,256]{3,2,1,0:T(8,128)(2,1)}, bf16[4,4,128,256]{3,2,1,0:T(8,128)(2,1)S(1)}, u32[]{:S(2)}, u32[]{:S(2)}) collective-permute-start(bf16[4,4,128,256]{3,2,1,0:T(8,128)(2,1)} %get-tuple-element.55), channel_id=1, source_target_pairs={{0,4},{4,0},{8,12},{12,8},{16,20},{20,16},{24,28},{28,24},{1,5},{5... | collective-permute-start | bytes 3145736 | tf_op jit(solution)/shard_map/ppermute | solution.py:496
  7.1 8.1 %collective-permute-start = (bf16[4,80,256]{2,1,0:T(8,128)(2,1)}, bf16[4,80,256]{2,1,0:T(8,128)(2,1)S(1)}, u32[]{:S(2)}, u32[]{:S(2)}) collective-permute-start(bf16[4,80,256]{2,1,0:T(8,128)(2,1)} %get-tuple-element.47.one), channel_id=1, source_target_pairs={{0,1},{1,0},{2,3},{3,2},{4,5},{5,4},{6,7},{7,6},{8,9},{9,8},{10,11... | collective-permute-start | bytes 491528 | tf_op jit(solution)/shard_map/ppermute | solution.py:493
  10.2 6.5 %collective-permute-start.1 = (bf16[4,80,256]{2,1,0:T(8,128)(2,1)}, bf16[4,80,256]{2,1,0:T(8,128)(2,1)S(1)}, u32[]{:S(2)}, u32[]{:S(2)}) collective-permute-start(bf16[4,80,256]{2,1,0:T(8,128)(2,1)} %get-tuple-element.48.two), channel_id=1, source_target_pairs={{0,2},{1,3},{2,0},{3,1},{4,6},{5,7},{6,4},{7,5},{8,10},{9,11},{10,... | collective-permute-start | bytes 491528 | tf_op jit(solution)/shard_map/ppermute | solution.py:493
  16.7 5.5 %collective-permute-start.2 = (bf16[4,80,256]{2,1,0:T(8,128)(2,1)S(1)}, bf16[4,80,256]{2,1,0:T(8,128)(2,1)S(1)}, u32[]{:S(2)}, u32[]{:S(2)}) collective-permute-start(bf16[4,80,256]{2,1,0:T(8,128)(2,1)S(1)} %get-tuple-element.51.refs_0_), channel_id=1, source_target_pairs={{0,2},{1,3},{2,0},{3,1},{4,6},{5,7},{6,4},{7,5},{8,10},{9,11},{10,... | collective-permute-start | bytes 491528 | tf_op jit(solution)/shard_map/ppermute | solution.py:493
  17.8 5.3 %collective-permute-start.3 = (bf16[4,80,256]{2,1,0:T(8,128)(2,1)S(1)}, bf16[4,80,256]{2,1,0:T(8,128)(2,1)S(1)}, u32[]{:S(2)}, u32[]{:S(2)}) collective-permute-start(bf16[4,80,256]{2,1,0:T(8,128)(2,1)S(1)} %get-tuple-element.52.refs_2_), channel_id=1, source_target_pairs={{0,1},{1,0},{2,3},{3,2},{4,5},{5,4},{6,7},{7,6},{8,9},{9,8},{10,11... | collective-permute-start | bytes 491528 | tf_op jit(solution)/shard_map/ppermute | solution.py:493
  26.9 6.1 %collective-permute-start.7 = (bf16[2,80,256]{2,1,0:T(8,128)(2,1)S(1)}, bf16[2,80,256]{2,1,0:T(8,128)(2,1)S(1)}, u32[]{:S(2)}, u32[]{:S(2)}) collective-permute-start(bf16[2,80,256]{2,1,0:T(8,128)(2,1)S(1)} %get-tuple-element.59), channel_id=1, source_target_pairs={{0,8},{4,12},{8,0},{12,4},{16,24},{20,28},{24,16},{28,20},{1,9},{5... | collective-permute-start | bytes 245768 | tf_op jit(solution)/shard_map/ppermute | solution.py:490
  28.6 13.3 %collective-permute-start.6 = (bf16[4,80,256]{2,1,0:T(8,128)(2,1)S(1)}, bf16[4,80,256]{2,1,0:T(8,128)(2,1)S(1)}, u32[]{:S(2)}, u32[]{:S(2)}) collective-permute-start(bf16[4,80,256]{2,1,0:T(8,128)(2,1)S(1)} %get-tuple-element.57), channel_id=1, source_target_pairs={{0,8},{4,12},{8,0},{12,4},{16,24},{20,28},{24,16},{28,20},{1,9},{5... | collective-permute-start | bytes 491528 | tf_op jit(solution)/shard_map/ppermute | solution.py:490
  29.0 7.8 %collective-permute-start.9 = (bf16[2,80,256]{2,1,0:T(8,128)(2,1)S(1)}, bf16[2,80,256]{2,1,0:T(8,128)(2,1)S(1)}, u32[]{:S(2)}, u32[]{:S(2)}) collective-permute-start(bf16[2,80,256]{2,1,0:T(8,128)(2,1)S(1)} %get-tuple-element.60), channel_id=1, source_target_pairs={{0,16},{4,20},{8,24},{12,28},{16,0},{20,4},{24,8},{28,12},{1,17},{... | collective-permute-start | bytes 245768 | tf_op jit(solution)/shard_map/ppermute | solution.py:490
  32.1 9.8 %collective-permute-start.10 = (bf16[2,80,256]{2,1,0:T(8,128)(2,1)S(1)}, bf16[2,80,256]{2,1,0:T(8,128)(2,1)S(1)}, u32[]{:S(2)}, u32[]{:S(2)}) collective-permute-start(bf16[2,80,256]{2,1,0:T(8,128)(2,1)S(1)} %get-tuple-element.61), channel_id=1, source_target_pairs={{0,24},{4,28},{8,16},{12,20},{16,8},{20,12},{24,0},{28,4},{1,25},{... | collective-permute-start | bytes 245768 | tf_op jit(solution)/shard_map/ppermute | solution.py:490
  33.1 10.5 %collective-permute-start.8 = (bf16[2,80,256]{2,1,0:T(8,128)(2,1)S(1)}, bf16[2,80,256]{2,1,0:T(8,128)(2,1)S(1)}, u32[]{:S(2)}, u32[]{:S(2)}) collective-permute-start(bf16[2,80,256]{2,1,0:T(8,128)(2,1)S(1)} %shard_map.109), channel_id=1, source_target_pairs={{0,16},{4,20},{8,24},{12,28},{16,0},{20,4},{24,8},{28,12},{1,17},{... | collective-permute-start | bytes 245768 | tf_op jit(solution)/shard_map/ppermute | solution.py:490
  43.8 8.2 %collective-permute-start.12 = (bf16[2,80,256]{2,1,0:T(8,128)(2,1)S(1)}, bf16[2,80,256]{2,1,0:T(8,128)(2,1)S(1)}, u32[]{:S(2)}, u32[]{:S(2)}) collective-permute-start(bf16[2,80,256]{2,1,0:T(8,128)(2,1)S(1)} %get-tuple-element.63), channel_id=1, source_target_pairs={{0,16},{4,20},{8,24},{12,28},{16,0},{20,4},{24,8},{28,12},{1,17},{... | collective-permute-start | bytes 245768 | tf_op jit(solution)/shard_map/ppermute | solution.py:490
  44.7 11.8 %collective-permute-start.11 = (bf16[4,80,256]{2,1,0:T(8,128)(2,1)S(1)}, bf16[4,80,256]{2,1,0:T(8,128)(2,1)S(1)}, u32[]{:S(2)}, u32[]{:S(2)}) collective-permute-start(bf16[4,80,256]{2,1,0:T(8,128)(2,1)S(1)} %get-tuple-element.62.refs_0_), channel_id=1, source_target_pairs={{0,8},{4,12},{8,0},{12,4},{16,24},{20,28},{24,16},{28,20},{1,9},{5... | collective-permute-start | bytes 491528 | tf_op jit(solution)/shard_map/ppermute | solution.py:490
  47.1 7.9 %collective-permute-start.15 = (bf16[2,80,256]{2,1,0:T(8,128)(2,1)S(1)}, bf16[2,80,256]{2,1,0:T(8,128)(2,1)S(1)}, u32[]{:S(2)}, u32[]{:S(2)}) collective-permute-start(bf16[2,80,256]{2,1,0:T(8,128)(2,1)S(1)} %get-tuple-element.64), channel_id=1, source_target_pairs={{0,24},{4,28},{8,16},{12,20},{16,8},{20,12},{24,0},{28,4},{1,25},{... | collective-permute-start | bytes 245768 | tf_op jit(solution)/shard_map/ppermute | solution.py:490
  48.2 8.3 %collective-permute-start.13 = (bf16[2,80,256]{2,1,0:T(8,128)(2,1)S(1)}, bf16[2,80,256]{2,1,0:T(8,128)(2,1)S(1)}, u32[]{:S(2)}, u32[]{:S(2)}) collective-permute-start(bf16[2,80,256]{2,1,0:T(8,128)(2,1)S(1)} %get-tuple-element.64), channel_id=1, source_target_pairs={{0,16},{4,20},{8,24},{12,28},{16,0},{20,4},{24,8},{28,12},{1,17},{... | collective-permute-start | bytes 245768 | tf_op jit(solution)/shard_map/ppermute | solution.py:490
  52.0 5.0 %collective-permute-start.14 = (bf16[2,80,256]{2,1,0:T(8,128)(2,1)S(1)}, bf16[2,80,256]{2,1,0:T(8,128)(2,1)S(1)}, u32[]{:S(2)}, u32[]{:S(2)}) collective-permute-start(bf16[2,80,256]{2,1,0:T(8,128)(2,1)S(1)} %collective-permute-done.12.refs_2_), channel_id=1, source_target_pairs={{0,8},{4,12},{8,0},{12,4},{16,24},{20,28},{24,16},{28,20},{1,9},{5... | collective-permute-start | bytes 245768 | tf_op jit(solution)/shard_map/ppermute | solution.py:490
  59.3 6.3 %collective-permute-start.17 = (bf16[4,80,256]{2,1,0:T(8,128)(2,1)S(1)}, bf16[4,80,256]{2,1,0:T(8,128)(2,1)S(1)}, u32[]{:S(2)}, u32[]{:S(2)}) collective-permute-start(bf16[4,80,256]{2,1,0:T(8,128)(2,1)S(1)} %get-tuple-element.65.one), channel_id=1, source_target_pairs={{0,1},{1,0},{2,3},{3,2},{4,5},{5,4},{6,7},{7,6},{8,9},{9,8},{10,11... | collective-permute-start | bytes 491528 | tf_op jit(solution)/shard_map/ppermute | solution.py:493
  60.1 6.0 %collective-permute-start.18 = (bf16[4,80,256]{2,1,0:T(8,128)(2,1)S(1)}, bf16[4,80,256]{2,1,0:T(8,128)(2,1)S(1)}, u32[]{:S(2)}, u32[]{:S(2)}) collective-permute-start(bf16[4,80,256]{2,1,0:T(8,128)(2,1)S(1)} %get-tuple-element.66.two), channel_id=1, source_target_pairs={{0,2},{1,3},{2,0},{3,1},{4,6},{5,7},{6,4},{7,5},{8,10},{9,11},{10,... | collective-permute-start | bytes 491528 | tf_op jit(solution)/shard_map/ppermute | solution.py:493
  66.2 5.4 %collective-permute-start.19 = (bf16[4,80,256]{2,1,0:T(8,128)(2,1)S(1)}, bf16[4,80,256]{2,1,0:T(8,128)(2,1)S(1)}, u32[]{:S(2)}, u32[]{:S(2)}) collective-permute-start(bf16[4,80,256]{2,1,0:T(8,128)(2,1)S(1)} %get-tuple-element.67.refs_0_), channel_id=1, source_target_pairs={{0,2},{1,3},{2,0},{3,1},{4,6},{5,7},{6,4},{7,5},{8,10},{9,11},{10,... | collective-permute-start | bytes 491528 | tf_op jit(solution)/shard_map/ppermute | solution.py:493
  67.1 5.3 %collective-permute-start.20 = (bf16[4,80,256]{2,1,0:T(8,128)(2,1)S(1)}, bf16[4,80,256]{2,1,0:T(8,128)(2,1)S(1)}, u32[]{:S(2)}, u32[]{:S(2)}) collective-permute-start(bf16[4,80,256]{2,1,0:T(8,128)(2,1)S(1)} %get-tuple-element.68.refs_2_), channel_id=1, source_target_pairs={{0,1},{1,0},{2,3},{3,2},{4,5},{5,4},{6,7},{7,6},{8,9},{9,8},{10,11... | collective-permute-start | bytes 491528 | tf_op jit(solution)/shard_map/ppermute | solution.py:493
  76.3 6.2 %collective-permute-start.23 = (bf16[2,80,256]{2,1,0:T(8,128)(2,1)S(1)}, bf16[2,80,256]{2,1,0:T(8,128)(2,1)S(1)}, u32[]{:S(2)}, u32[]{:S(2)}) collective-permute-start(bf16[2,80,256]{2,1,0:T(8,128)(2,1)S(1)} %get-tuple-element.76), channel_id=1, source_target_pairs={{0,8},{4,12},{8,0},{12,4},{16,24},{20,28},{24,16},{28,20},{1,9},{5... | collective-permute-start | bytes 245768 | tf_op jit(solution)/shard_map/ppermute | solution.py:490
  76.8 15.2 %collective-permute-start.22 = (bf16[4,80,256]{2,1,0:T(8,128)(2,1)S(1)}, bf16[4,80,256]{2,1,0:T(8,128)(2,1)S(1)}, u32[]{:S(2)}, u32[]{:S(2)}) collective-permute-start(bf16[4,80,256]{2,1,0:T(8,128)(2,1)S(1)} %get-tuple-element.74), channel_id=1, source_target_pairs={{0,8},{4,12},{8,0},{12,4},{16,24},{20,28},{24,16},{28,20},{1,9},{5... | collective-permute-start | bytes 491528 | tf_op jit(solution)/shard_map/ppermute | solution.py:490
  78.4 6.5 %collective-permute-start.25 = (bf16[2,80,256]{2,1,0:T(8,128)(2,1)S(1)}, bf16[2,80,256]{2,1,0:T(8,128)(2,1)S(1)}, u32[]{:S(2)}, u32[]{:S(2)}) collective-permute-start(bf16[2,80,256]{2,1,0:T(8,128)(2,1)S(1)} %get-tuple-element.77), channel_id=1, source_target_pairs={{0,16},{4,20},{8,24},{12,28},{16,0},{20,4},{24,8},{28,12},{1,17},{... | collective-permute-start | bytes 245768 | tf_op jit(solution)/shard_map/ppermute | solution.py:490
  78.9 9.6 %collective-permute-start.26 = (bf16[2,80,256]{2,1,0:T(8,128)(2,1)S(1)}, bf16[2,80,256]{2,1,0:T(8,128)(2,1)S(1)}, u32[]{:S(2)}, u32[]{:S(2)}) collective-permute-start(bf16[2,80,256]{2,1,0:T(8,128)(2,1)S(1)} %get-tuple-element.78), channel_id=1, source_target_pairs={{0,24},{4,28},{8,16},{12,20},{16,8},{20,12},{24,0},{28,4},{1,25},{... | collective-permute-start | bytes 245768 | tf_op jit(solution)/shard_map/ppermute | solution.py:490
  82.6 9.4 %collective-permute-start.24 = (bf16[2,80,256]{2,1,0:T(8,128)(2,1)S(1)}, bf16[2,80,256]{2,1,0:T(8,128)(2,1)S(1)}, u32[]{:S(2)}, u32[]{:S(2)}) collective-permute-start(bf16[2,80,256]{2,1,0:T(8,128)(2,1)S(1)} %shard_map.118), channel_id=1, source_target_pairs={{0,16},{4,20},{8,24},{12,28},{16,0},{20,4},{24,8},{28,12},{1,17},{... | collective-permute-start | bytes 245768 | tf_op jit(solution)/shard_map/ppermute | solution.py:490
  92.9 5.9 %collective-permute-start.28 = (bf16[2,80,256]{2,1,0:T(8,128)(2,1)S(1)}, bf16[2,80,256]{2,1,0:T(8,128)(2,1)S(1)}, u32[]{:S(2)}, u32[]{:S(2)}) collective-permute-start(bf16[2,80,256]{2,1,0:T(8,128)(2,1)S(1)} %get-tuple-element.81), channel_id=1, source_target_pairs={{0,16},{4,20},{8,24},{12,28},{16,0},{20,4},{24,8},{28,12},{1,17},{... | collective-permute-start | bytes 245768 | tf_op jit(solution)/shard_map/ppermute | solution.py:490
  92.9 12.2 %collective-permute-start.27 = (bf16[4,80,256]{2,1,0:T(8,128)(2,1)S(1)}, bf16[4,80,256]{2,1,0:T(8,128)(2,1)S(1)}, u32[]{:S(2)}, u32[]{:S(2)}) collective-permute-start(bf16[4,80,256]{2,1,0:T(8,128)(2,1)S(1)} %get-tuple-element.80.refs_0_), channel_id=1, source_target_pairs={{0,8},{4,12},{8,0},{12,4},{16,24},{20,28},{24,16},{28,20},{1,9},{5... | collective-permute-start | bytes 491528 | tf_op jit(solution)/shard_map/ppermute | solution.py:490
  95.2 8.9 %collective-permute-start.31 = (bf16[2,80,256]{2,1,0:T(8,128)(2,1)S(1)}, bf16[2,80,256]{2,1,0:T(8,128)(2,1)S(1)}, u32[]{:S(2)}, u32[]{:S(2)}) collective-permute-start(bf16[2,80,256]{2,1,0:T(8,128)(2,1)S(1)} %get-tuple-element.82), channel_id=1, source_target_pairs={{0,24},{4,28},{8,16},{12,20},{16,8},{20,12},{24,0},{28,4},{1,25},{... | collective-permute-start | bytes 245768 | tf_op jit(solution)/shard_map/ppermute | solution.py:490
  97.3 6.9 %collective-permute-start.29 = (bf16[2,80,256]{2,1,0:T(8,128)(2,1)S(1)}, bf16[2,80,256]{2,1,0:T(8,128)(2,1)S(1)}, u32[]{:S(2)}, u32[]{:S(2)}) collective-permute-start(bf16[2,80,256]{2,1,0:T(8,128)(2,1)S(1)} %get-tuple-element.82), channel_id=1, source_target_pairs={{0,16},{4,20},{8,24},{12,28},{16,0},{20,4},{24,8},{28,12},{1,17},{... | collective-permute-start | bytes 245768 | tf_op jit(solution)/shard_map/ppermute | solution.py:490
  98.8 6.3 %collective-permute-start.30 = (bf16[2,80,256]{2,1,0:T(8,128)(2,1)S(1)}, bf16[2,80,256]{2,1,0:T(8,128)(2,1)S(1)}, u32[]{:S(2)}, u32[]{:S(2)}) collective-permute-start(bf16[2,80,256]{2,1,0:T(8,128)(2,1)S(1)} %collective-permute-done.28.refs_2_), channel_id=1, source_target_pairs={{0,8},{4,12},{8,0},{12,4},{16,24},{20,28},{24,16},{28,20},{1,9},{5... | collective-permute-start | bytes 245768 | tf_op jit(solution)/shard_map/ppermute | solution.py:490
  107.4 4.6 %collective-permute-start.33 = (bf16[4,80,128]{2,1,0:T(8,128)(2,1)S(1)}, bf16[4,80,128]{2,1,0:T(8,128)(2,1)S(1)}, u32[]{:S(2)}, u32[]{:S(2)}) collective-permute-start(bf16[4,80,128]{2,1,0:T(8,128)(2,1)S(1)} %get-tuple-element.84), channel_id=1, source_target_pairs={{0,1},{1,0},{2,3},{3,2},{4,5},{5,4},{6,7},{7,6},{8,9},{9,8},{10,11... | collective-permute-start | bytes 245768 | tf_op jit(solution)/shard_map/ppermute | solution.py:493
  108.9 4.5 %collective-permute-start.34 = (bf16[4,80,128]{2,1,0:T(8,128)(2,1)S(1)}, bf16[4,80,128]{2,1,0:T(8,128)(2,1)S(1)}, u32[]{:S(2)}, u32[]{:S(2)}) collective-permute-start(bf16[4,80,128]{2,1,0:T(8,128)(2,1)S(1)} %get-tuple-element.85), channel_id=1, source_target_pairs={{0,2},{1,3},{2,0},{3,1},{4,6},{5,7},{6,4},{7,5},{8,10},{9,11},{10,... | collective-permute-start | bytes 245768 | tf_op jit(solution)/shard_map/ppermute | solution.py:493
  110.3 5.3 %collective-permute-start.35 = (bf16[4,80,128]{2,1,0:T(8,128)(2,1)S(1)}, bf16[4,80,128]{2,1,0:T(8,128)(2,1)S(1)}, u32[]{:S(2)}, u32[]{:S(2)}) collective-permute-start(bf16[4,80,128]{2,1,0:T(8,128)(2,1)S(1)} %get-tuple-element.86), channel_id=1, source_target_pairs={{0,3},{1,2},{2,1},{3,0},{4,7},{5,6},{6,5},{7,4},{8,11},{9,10},{10,... | collective-permute-start | bytes 245768 | tf_op jit(solution)/shard_map/ppermute | solution.py:493
  (10 other events, 74.6 us)

commit v8 on v7

--- a/solution.py
+++ b/solution.py
@@ -47,15 +47,11 @@
     return value
 
 
-def split(x):
+def dot(matrix, x):
     high = x.astype(BF16)
-    return high, (x - high.astype(F32)).astype(BF16)
-
-
-def dot(a, b):
-    (a, a_rest), (b, b_rest) = split(a), split(b)
-    one = functools.partial(jnp.dot, preferred_element_type=F32)
-    return one(a, b) + (one(a, b_rest) + one(a_rest, b))
+    rest = (x - high.astype(F32)).astype(BF16)
+    x = jnp.concatenate([high, rest, high], axis=0)
+    return jnp.dot(matrix, x, preferred_element_type=F32)
 
 
 def total(x):
@@ -89,7 +85,9 @@
 
 def of_member(refs, spans, m):
     return [
-        ref.at[m - first] for ref, (first, count) in zip(refs, spans) if first <= m < first + count
+        ref.at[m - first + skip]
+        for ref, (first, count, skip) in zip(refs, spans)
+        if first <= m < first + count
     ]
 
 
@@ -207,13 +205,20 @@
             draw(at + early)
         adjoint(at)
 
-    half = colblocks * LANES // 2
     for m in range(members):
         value = acc[m * levp : (m + 1) * levp, :]
         if m == 0:
             value = with_columns(value, jnp.concatenate([sd[...]] * colblocks, axis=1), obs)
-        outs[0][m] = value[:, :half].astype(BF16)
-        outs[1][m] = value[:, half:].astype(BF16)
+        put_halves(outs, m, value)
+
+
+def put_halves(outs, m, value):
+    half = value.shape[1] // 2
+    for one, two in zip(outs[::2], outs[1::2]):
+        if 0 <= m < one.shape[0]:
+            one[m] = value[:, :half].astype(BF16)
+            two[m] = value[:, half:].astype(BF16)
+        m -= one.shape[0]
 
 
 def with_columns(body, line, obs):
@@ -248,16 +253,20 @@
     out[0:lev, :] = jnp.sum(jnp.where(block == piece // halves, mine, 0.0), axis=1)
 
 
-def joined(refs, m):
-    one, two = refs[: len(refs) // 2], refs[len(refs) // 2 :]
-    return jnp.concatenate([add([x[m] for x in one]), add([x[m] for x in two])], axis=1)
+def joined(pieces, m):
+    for at in range(0, len(pieces), 4):
+        one, one_more, two, two_more = pieces[at : at + 4]
+        if m < one.shape[0]:
+            halves = [add([one[m], one_more[m]]), add([two[m], two_more[m]])]
+            return jnp.concatenate(halves, axis=1), [one.at[m], one_more.at[m]]
+        m -= one.shape[0]
 
 
 def first_kernel(parts, *refs):
     pieces = refs[:parts]
     vert, vert_t, sd_out, residual, moved = refs[parts:]
     for m in range(residual.shape[0]):
-        t = joined(pieces, m)
+        t, unused = joined(pieces, m)
         if m == 0:
             sd = read_columns(t)
             sd_out[...] = sd
@@ -281,10 +290,11 @@
     add_kernel(0, two, two_more, two_out)
 
 
-def stage_kernel(one, two, one_out, two_out, sems):
+def stage_kernel(*refs):
+    sems = refs[-1]
+    count = len(refs) // 2
     copies = [
-        pltpu.make_async_copy(x, y, sems.at[i])
-        for i, (x, y) in enumerate([(one, one_out), (two, two_out)])
+        pltpu.make_async_copy(refs[i], refs[count + i], sems.at[i]) for i in range(count)
     ]
     for copy in copies:
         copy.start()
@@ -292,7 +302,7 @@
         copy.wait()
 
 
-def forward_kernel(plan, mine, other, own, partner, *outs):
+def forward_kernel(sends, mine, other, own, partner, *outs):
     z, core, obs = place()
     members, levp, lanes = mine.shape
     chips, width = own.shape[0], own.shape[3]
@@ -311,19 +321,22 @@
             preferred_element_type=F32,
         )
         y = y.reshape(members, levp, width)
-        for out, (chip, first, count) in zip(outs, plan):
-            if chip == i:
-                for m in range(count):
-                    value = with_scalars(y[first + m], scalars[first + m])
-                    out[m] = value.astype(out.dtype)
-
-
-def weigh_kernel(later, spans, *refs):
+        for out, parts in zip(outs, sends):
+            at = 0
+            for chip, first, count in parts:
+                for m in range(first, first + count if chip == i else first):
+                    out[at + m - first] = with_scalars(y[m], scalars[m]).astype(out.dtype)
+                at += count
+
+
+def weigh_kernel(later, last, spans, *refs):
     ys, refs = refs[: len(spans)], refs[len(spans) :]
     prec = refs[0]
-    image, state, weighted, *parts = refs[3 if later else 1 :]
+    state, weighted, *parts = refs[3 if later else 1 :]
+    if not last:
+        *parts, image = parts
     p = prec[...]
-    for m in range(image.shape[0]):
+    for m in range(weighted.shape[0]):
         mine = of_member(ys, spans, m)
         y = add([x[...] for x in mine])
         norm, cross = read_scalars(mine, 2)
@@ -337,7 +350,8 @@
             beta = jnp.zeros_like(norm)
             square = norm
         scaled = p * y
-        image[m] = y
+        if not last:
+            image[m] = y
         value = with_scalars(scaled, [total(scaled * y)]).astype(BF16)
         weighted[m] = value
         first = 0
@@ -363,19 +377,16 @@
         )
         acc = part if i == 0 else acc + part
     acc = acc.reshape(members, levp, lanes)
-    spans = [span for chip, *span in plan]
+    spans = [(*span, 0) for chip, *span in plan]
     for m in range(members):
         energy = read_scalars(of_member(ws, spans, m), 1)
         out[m] = with_scalars(acc[m], energy).astype(out.dtype)
 
 
-def combine_kernel(mine, theirs, one, two):
-    half = one.shape[2]
-    for m in range(one.shape[0]):
+def combine_kernel(mine, theirs, *outs):
+    for m in range(mine.shape[0]):
         energy = read_scalars([mine.at[m], theirs.at[m]], 1)
-        value = mine[m] + theirs[m].astype(F32)
-        one[m] = with_scalars(value[:, :half], energy).astype(BF16)
-        two[m] = value[:, half:].astype(BF16)
+        put_halves(outs, m, with_scalars(mine[m] + theirs[m].astype(F32), energy))
 
 
 def combine_columns_kernel(mine, theirs, *outs):
@@ -398,8 +409,8 @@
     obs = lax.axis_index("obs")
     mine = pl.ds(pl.multiple_of(obs * LANES, LANES), LANES)
     for m in range(residual.shape[0]):
-        t = joined(pieces, m)
-        (energy,) = read_scalars([x.at[m] for x in pieces[: parts // 2]], 1)
+        t, places = joined(pieces, m)
+        (energy,) = read_scalars(places, 1)
         norm, square, beta = state[m, 0:1, 0:1], state[m, 1:2, 0:1], state[m, 2:3, 0:1]
         alpha = norm / (square + energy)
         r = residual[m]
@@ -466,19 +477,27 @@
     rows = members * levp
     lanes = colblocks * LANES
     field = (members, levp, LANES)
-    half_field = (members, levp, lanes // 2)
     slab_field = (members, levp, lanes)
     panel = (members, levp, width)
     some, rest = members // 2, members - members // 2
+    half_fields = [
+        struct((n, levp, lanes // 2), BF16) for n in (some, rest) if n for half in range(2)
+    ]
     via = chips == 4 and some > 0
     if via:
         plan = [(0, 0, members), (1, 0, members)]
         plan += [(i, *span) for i in (2, 3) for span in ((0, some), (some, rest))]
+        sends = [[plan[0]], [plan[4], plan[1]], [plan[2]], [plan[3]], [plan[5]]]
     else:
         plan = [(i, 0, members) for i in range(chips)]
+        sends = [[part] for part in plan]
     pad = ((0, levp - lev), (0, levp - lev))
-    vert = jnp.pad(vert_factor, pad)
-    vert_t = jnp.pad(vert_factor.T, pad)
+    high = lax.reduce_precision(vert_factor, 8, 7)
+    low = vert_factor - high
+    vert, vert_t = [
+        jnp.concatenate([jnp.pad(x, pad).astype(BF16) for x in parts], axis=1)
+        for parts in ((high, high, low), (high.T, high.T, low.T))
+    ]
     h_block = h_values.reshape(h_values.shape[2:])
     innovation = jnp.transpose(innovation, (1, 0, 2))
     obs_precision = jnp.transpose(obs_precision, (1, 0, 2))
@@ -495,48 +514,56 @@
     def swap(x):
         return lax.ppermute(x, "slab", [(s, s ^ 1) for s in range(n_slab)])
 
-    def plane_sum(one, two, scalars):
+    def plane_sum(halves, staged):
+        halves = list(halves)
+        moved_halves = [None] * len(halves)
         for step, bit in enumerate(plane_bits):
-            far = plane_bits[len(plane_bits) - 1 - step]
-            one_more, two_more = plane(one, bit), plane(two, far)
-            if step == 0 and not scalars:
-                one, two = call(
+            bits = [bit, plane_bits[len(plane_bits) - 1 - step]]
+            for at in range(0, len(halves), 2):
+                if step > 0:
+                    one, two = halves[at : at + 2]
+                    one_more, two_more = moved_halves[at : at + 2]
+                    halves[at : at + 2] = call(
+                        functools.partial(add_halves_kernel, 0 if staged else 1),
+                        [struct(one.shape, BF16)] * 2,
+                        [],
+                        0,
+                        one,
+                        one_more,
+                        two,
+                        two_more,
+                    )
+                for half in range(2):
+                    moved_halves[at + half] = plane(halves[at + half], bits[half])
+            if step == 0 and staged:
+                halves[:] = call(
                     stage_kernel,
-                    [struct(half_field, BF16)] * 2,
-                    [pltpu.SemaphoreType.DMA((2,))],
+                    [struct(x.shape, BF16) for x in halves],
+                    [pltpu.SemaphoreType.DMA((len(halves),))],
                     0,
-                    one,
-                    two,
+                    *halves,
                     space=HBM,
                 )
-            parts = [one, one_more, two, two_more]
-            if step < len(plane_bits) - 1:
-                one, two = call(
-                    functools.partial(add_halves_kernel, scalars),
-                    [struct(half_field, BF16)] * 2,
-                    [],
-                    0,
-                    *parts,
-                )
-        return parts
+        return [x for pair in zip(halves, moved_halves) for x in pair]
 
     def line_sum(ys):
         if not via:
             return [y if i == 0 else along(y, i) for i, y in enumerate(ys)], [
-                (0, members) for y in ys
+                (0, members, 0) for y in ys
             ]
-        near, next_, far, far_rest, last_, last_rest = ys
-        passed = along(last_, 1)
-        far_rest, last_rest, next_ = along(far_rest, 2), along(last_rest, 3), along(next_, 1)
+        near, next_, far, far_rest, last_rest = ys
+        next_ = along(next_, 1)
+        far_rest, last_rest = along(far_rest, 2), along(last_rest, 3)
         (far,) = call(
             functools.partial(add_kernel, 2),
             [struct((some, levp, width), BF16)],
             [],
             0,
             far,
-            passed,
-        )
-        spans = [(0, members), (0, members), (0, some), (some, rest), (some, rest)]
+            next_,
+        )
+        spans = [(0, members, 0), (0, members, some), (0, some, 0)]
+        spans += [(some, rest, 0), (some, rest, 0)]
         return [near, next_, along(far, 2), far_rest, last_rest], spans
 
     def line_gather(w, *parts):
@@ -550,7 +577,7 @@
     dense = struct((chips, colblocks, LANES, width), BF16)
     own, for_partner, *partials = call(
         functools.partial(start_kernel, (chips, halves)),
-        [dense, dense] + [struct(half_field, BF16)] * 2,
+        [dense, dense] + half_fields,
         [
             pltpu.SMEM(seeds.shape, jnp.int32),
             pltpu.SMEM(block_obs.shape, jnp.int32),
@@ -577,7 +604,7 @@
         space=HBM,
         limit=60,
     )
-    ps = plane_sum(*partials, 0)
+    ps = plane_sum(partials, True)
     partner = swap(for_partner)
     (precision,) = call(
         functools.partial(precision_kernel, halves),
@@ -599,10 +626,13 @@
     for sweep in range(ITERS):
         later, last = sweep > 0, sweep == ITERS - 1
         ys = call(
-            functools.partial(forward_kernel, plan),
+            functools.partial(forward_kernel, sends),
             [
-                struct((count, levp, width), F32 if at == 0 or (via and at == 2) else BF16)
-                for at, (unused, unused, count) in enumerate(plan)
+                struct(
+                    (sum(count for *unused, count in parts), levp, width),
+                    F32 if at == 0 or (via and at == 2) else BF16,
+                )
+                for at, parts in enumerate(sends)
             ],
             [],
             2 * product,
@@ -612,16 +642,19 @@
             partner,
         )
         ys, spans = line_sum(ys)
-        image, state, *weighted = call(
-            functools.partial(weigh_kernel, later, spans),
-            [struct(panel, F32), struct((members, 8, LANES), F32), struct(panel, BF16)]
-            + ([struct((n, levp, width), BF16) for n in (some, rest)] if via else []),
+        state, *weighted = call(
+            functools.partial(weigh_kernel, later, last, spans),
+            [struct((members, 8, LANES), F32), struct(panel, BF16)]
+            + ([struct((n, levp, width), BF16) for n in (some, rest)] if via else [])
+            + ([] if last else [struct(panel, F32)]),
             [],
             0,
             *ys,
             precision,
             *([image, state] if later else []),
         )
+        if not last:
+            *weighted, image = weighted
         ws = line_gather(*weighted)
         (theirs,) = call(
             functools.partial(adjoint_kernel, plan),
@@ -658,8 +691,8 @@
                 *known,
             )
             break
-        ps = call(combine_kernel, [struct(half_field, BF16)] * 2, [], 0, mine, theirs)
-        ps = plane_sum(*ps, 1)
+        ps = call(combine_kernel, half_fields, [], 0, mine, theirs)
+        ps = plane_sum(ps, False)
         outs = [struct(slab_field, F32), struct(field, F32), struct(slab_field, BF16)]
         if later:
             outs.append(struct(slab_field, F32))

time: 117 us -> 119 us (1.017)
  starting transfers between devices: 37.7 us -> 50.9 us
  waiting for transfers between devices: 60.4 us -> 48.3 us
  local copies, waits for them, and re-layouts: 2 us -> 3.78 us
    ppermute x11 -> x19, starting transfers between devices: 13.4 us -> 21.6 us  [plane(): return lax.ppermute(x, 'obs', [(o, o ^ i) for o in range(n_obs)])]
    ppermute x11 -> x19, waiting for transfers between devices: 21.2 us -> 13.5 us  [plane(): return lax.ppermute(x, 'obs', [(o, o ^ i) for o in range(n_obs)])]
    ppermute x20 -> x18, starting transfers between devices: 23.5 us -> 28.5 us  [along(): return lax.ppermute(x, 'slab', [(s, s ^ 2 * i) for s in range(n_slab)])]
    ppermute x20 -> x18, waiting for transfers between devices: 33.9 us -> 29.4 us  [along(): return lax.ppermute(x, 'slab', [(s, s ^ 2 * i) for s in range(n_slab)])]
    unnamed x13 -> x17, local copies, waits for them, and re-layouts: 1.98 us -> 3.66 us
    pallas_call x20 -> x22, Pallas kernels: 15.2 us -> 14.2 us  [call(): pl.pallas_call(kernel, out_shape=outs, in_specs=[space] * len(args), out_...]
  transfers between devices with their start and end apart: 36 -> 42, of which waited for: 29 -> 31; matrix products, arithmetic and copies ran while one was open for 0% -> 0% of each run, Pallas kernels for 3% -> 3%
where the time goes in v8:
time: 119 us
  starting transfers between devices  50.9 us (43%)
  waiting for transfers between devices  48.3 us (41%)
  Pallas kernels  14.2 us (12%)
  local copies, waits for them, and re-layouts  3.78 us (3%)
  between operations  1.55 us (1%)
    ppermute x18, waiting for transfers between devices, along(): return lax.ppermute(x, 'slab', [(s, s ^ 2 * i) for s in range(n_slab)])  29.4 us
    ppermute x18, starting transfers between devices, along(): return lax.ppermute(x, 'slab', [(s, s ^ 2 * i) for s in range(n_slab)])  28.5 us
    ppermute x19, starting transfers between devices, plane(): return lax.ppermute(x, 'obs', [(o, o ^ i) for o in range(n_obs)])  21.6 us
    pallas_call x22, Pallas kernels, call(): pl.pallas_call(kernel, out_shape=outs, in_specs=[space] * len(args), out_...  14.2 us
    ppermute x19, waiting for transfers between devices, plane(): return lax.ppermute(x, 'obs', [(o, o ^ i) for o in range(n_obs)])  13.5 us
    ppermute x5, waiting for transfers between devices, swap(): return lax.ppermute(x, 'slab', [(s, s ^ 1) for s in range(n_slab)])  5.36 us
    unnamed x17, local copies, waits for them, and re-layouts  3.66 us
  transfers between devices with their start and end apart: 42, of which 31 were waited for; matrix products, arithmetic and copies ran while one was open for 0% of the time, Pallas kernels for 3%

profile of v8, /device:TPU:0, one launch (start us, length us, event | category | flops | bytes accessed | tf_op | source)
XLA Modules:
  0.0 118.9 jit_solution(9081131038823907839)
XLA Ops:
  1.3 5.4 %shard_map.104 = (bf16[4,4,128,256]{3,2,1,0:T(8,128)(2,1)}, bf16[4,4,128,256]{3,2,1,0:T(8,128)(2,1)}, bf16[2,80,256]{2,1,0:T(8,128)(2,1)}, bf16[2,80,256]{2,1,0:...) custom-call(s32[4]{0:T(128)} %seeds_in.1, s32[1,1,32]{2,1,0:T(1,128)} %ids_in.1, ...), custom_call_target="tpu_custom_call" | custom-call | flops 671088640 | bytes 5751572 | tf_op jit(solution)/shard_map/pallas_call | solution.py:23
  7.2 3.1 %collective-permute-start = (bf16[2,80,256]{2,1,0:T(8,128)(2,1)}, bf16[2,80,256]{2,1,0:T(8,128)(2,1)S(1)}, u32[]{:S(2)}, u32[]{:S(2)}) collective-permute-start(bf16[2,80,256]{2,1,0:T(8,128)(2,1)} %get-tuple-element.55.refs_0_), channel_id=1, source_target_pairs={{0,1},{1,0},{2,3},{3,2},{4,5},{5,4},{6,7},{7,6},{8,9},{9,8},{10,11... | collective-permute-start | bytes 245768 | tf_op jit(solution)/shard_map/ppermute | solution.py:512
  10.3 1.5 %collective-permute-start.1 = (bf16[2,80,256]{2,1,0:T(8,128)(2,1)}, bf16[2,80,256]{2,1,0:T(8,128)(2,1)S(1)}, u32[]{:S(2)}, u32[]{:S(2)}) collective-permute-start(bf16[2,80,256]{2,1,0:T(8,128)(2,1)} %get-tuple-element.56.refs_1_), channel_id=1, source_target_pairs={{0,2},{1,3},{2,0},{3,1},{4,6},{5,7},{6,4},{7,5},{8,10},{9,11},{10,... | collective-permute-start | bytes 245768 | tf_op jit(solution)/shard_map/ppermute | solution.py:512
  16.8 1.7 %collective-permute-start.6 = (bf16[2,80,256]{2,1,0:T(8,128)(2,1)S(1)}, bf16[2,80,256]{2,1,0:T(8,128)(2,1)S(1)}, u32[]{:S(2)}, u32[]{:S(2)}) collective-permute-start(bf16[2,80,256]{2,1,0:T(8,128)(2,1)S(1)} %get-tuple-element.65.refs_4_), channel_id=1, source_target_pairs={{0,2},{1,3},{2,0},{3,1},{4,6},{5,7},{6,4},{7,5},{8,10},{9,11},{10,... | collective-permute-start | bytes 245768 | tf_op jit(solution)/shard_map/ppermute | solution.py:512
  18.5 1.7 %collective-permute-start.7 = (bf16[2,80,256]{2,1,0:T(8,128)(2,1)S(1)}, bf16[2,80,256]{2,1,0:T(8,128)(2,1)S(1)}, u32[]{:S(2)}, u32[]{:S(2)}) collective-permute-start(bf16[2,80,256]{2,1,0:T(8,128)(2,1)S(1)} %get-tuple-element.66.refs_6_), channel_id=1, source_target_pairs={{0,1},{1,0},{2,3},{3,2},{4,5},{5,4},{6,7},{7,6},{8,9},{9,8},{10,11... | collective-permute-start | bytes 245768 | tf_op jit(solution)/shard_map/ppermute | solution.py:512
  21.3 2.4 %collective-permute-done.7.refs_7_ = bf16[2,80,256]{2,1,0:T(8,128)(2,1)S(1)} collective-permute-done((bf16[2,80,256]{2,1,0:T(8,128)(2,1)S(1)}, bf16[2,80,256]{2,1,0:T(8,128)(2,1)S(1)}, u32[]{:S(2)}, u32[]{:S(2)}) %collective-permute-start.7) | collective-permute-done | bytes 81952 | tf_op jit(solution)/shard_map/ppermute | solution.py:512
  26.4 1.6 %collective-permute-done.8.other = bf16[4,80,512]{2,1,0:T(8,128)(2,1)S(1)} collective-permute-done((bf16[4,80,512]{2,1,0:T(8,128)(2,1)S(1)}, bf16[4,80,512]{2,1,0:T(8,128)(2,1)S(1)}, u32[]{:S(2)}, u32[]{:S(2)}) %collective-permute-start.8) | collective-permute-done | bytes 327712 | tf_op jit(solution)/shard_map/ppermute | solution.py:515
  28.9 1.4 %collective-permute-start.10 = (bf16[6,80,256]{2,1,0:T(8,128)(2,1)S(1)}, bf16[6,80,256]{2,1,0:T(8,128)(2,1)S(1)}, u32[]{:S(2)}, u32[]{:S(2)}) collective-permute-start(bf16[6,80,256]{2,1,0:T(8,128)(2,1)S(1)} %get-tuple-element.71), channel_id=1, source_target_pairs={{0,8},{4,12},{8,0},{12,4},{16,24},{20,28},{24,16},{28,20},{1,9},{5... | collective-permute-start | bytes 737288 | tf_op jit(solution)/shard_map/ppermute | solution.py:509
  30.3 2.3 %collective-permute-start.12 = (bf16[2,80,256]{2,1,0:T(8,128)(2,1)S(1)}, bf16[2,80,256]{2,1,0:T(8,128)(2,1)S(1)}, u32[]{:S(2)}, u32[]{:S(2)}) collective-permute-start(bf16[2,80,256]{2,1,0:T(8,128)(2,1)S(1)} %get-tuple-element.73), channel_id=1, source_target_pairs={{0,16},{4,20},{8,24},{12,28},{16,0},{20,4},{24,8},{28,12},{1,17},{... | collective-permute-start | bytes 245768 | tf_op jit(solution)/shard_map/ppermute | solution.py:509
  33.3 5.4 %collective-permute-done.10.refs_1_ = bf16[6,80,256]{2,1,0:T(8,128)(2,1)S(1)} collective-permute-done((bf16[6,80,256]{2,1,0:T(8,128)(2,1)S(1)}, bf16[6,80,256]{2,1,0:T(8,128)(2,1)S(1)}, u32[]{:S(2)}, u32[]{:S(2)}) %collective-permute-start.10) | collective-permute-done | bytes 245792 | tf_op jit(solution)/shard_map/ppermute | solution.py:509
  38.8 1.8 %collective-permute-start.11 = (bf16[2,80,256]{2,1,0:T(8,128)(2,1)S(1)}, bf16[2,80,256]{2,1,0:T(8,128)(2,1)S(1)}, u32[]{:S(2)}, u32[]{:S(2)}) collective-permute-start(bf16[2,80,256]{2,1,0:T(8,128)(2,1)S(1)} %shard_map.110), channel_id=1, source_target_pairs={{0,16},{4,20},{8,24},{12,28},{16,0},{20,4},{24,8},{28,12},{1,17},{... | collective-permute-start | bytes 245768 | tf_op jit(solution)/shard_map/ppermute | solution.py:509
  41.9 3.5 %collective-permute-done.11.refs_2_ = bf16[2,80,256]{2,1,0:T(8,128)(2,1)S(1)} collective-permute-done((bf16[2,80,256]{2,1,0:T(8,128)(2,1)S(1)}, bf16[2,80,256]{2,1,0:T(8,128)(2,1)S(1)}, u32[]{:S(2)}, u32[]{:S(2)}) %collective-permute-start.11) | collective-permute-done | bytes 81952 | tf_op jit(solution)/shard_map/ppermute | solution.py:509
  46.2 2.6 %collective-permute-start.14 = (bf16[4,80,256]{2,1,0:T(8,128)(2,1)S(1)}, bf16[4,80,256]{2,1,0:T(8,128)(2,1)S(1)}, u32[]{:S(2)}, u32[]{:S(2)}) collective-permute-start(bf16[4,80,256]{2,1,0:T(8,128)(2,1)S(1)} %get-tuple-element.75.refs_0_), channel_id=1, source_target_pairs={{0,8},{4,12},{8,0},{12,4},{16,24},{20,28},{24,16},{28,20},{1,9},{5... | collective-permute-start | bytes 491528 | tf_op jit(solution)/shard_map/ppermute | solution.py:509
  48.8 1.3 %collective-permute-start.18 = (bf16[2,80,256]{2,1,0:T(8,128)(2,1)S(1)}, bf16[2,80,256]{2,1,0:T(8,128)(2,1)S(1)}, u32[]{:S(2)}, u32[]{:S(2)}) collective-permute-start(bf16[2,80,256]{2,1,0:T(8,128)(2,1)S(1)} %get-tuple-element.77), channel_id=1, source_target_pairs={{0,24},{4,28},{8,16},{12,20},{16,8},{20,12},{24,0},{28,4},{1,25},{... | collective-permute-start | bytes 245768 | tf_op jit(solution)/shard_map/ppermute | solution.py:509
  50.3 2.2 %collective-permute-done.15.refs_2_ = bf16[2,80,256]{2,1,0:T(8,128)(2,1)S(1)} collective-permute-done((bf16[2,80,256]{2,1,0:T(8,128)(2,1)S(1)}, bf16[2,80,256]{2,1,0:T(8,128)(2,1)S(1)}, u32[]{:S(2)}, u32[]{:S(2)}) %collective-permute-start.15) | collective-permute-done | bytes 81952 | tf_op jit(solution)/shard_map/ppermute | solution.py:509
  53.7 3.3 %collective-permute-done.18.refs_5_ = bf16[2,80,256]{2,1,0:T(8,128)(2,1)S(1)} collective-permute-done((bf16[2,80,256]{2,1,0:T(8,128)(2,1)S(1)}, bf16[2,80,256]{2,1,0:T(8,128)(2,1)S(1)}, u32[]{:S(2)}, u32[]{:S(2)}) %collective-permute-start.18) | collective-permute-done | bytes 81952 | tf_op jit(solution)/shard_map/ppermute | solution.py:509
  61.1 2.1 %collective-permute-start.21 = (bf16[2,80,256]{2,1,0:T(8,128)(2,1)S(1)}, bf16[2,80,256]{2,1,0:T(8,128)(2,1)S(1)}, u32[]{:S(2)}, u32[]{:S(2)}) collective-permute-start(bf16[2,80,256]{2,1,0:T(8,128)(2,1)S(1)} %get-tuple-element.79.two), channel_id=1, source_target_pairs={{0,2},{1,3},{2,0},{3,1},{4,6},{5,7},{6,4},{7,5},{8,10},{9,11},{10,... | collective-permute-start | bytes 245768 | tf_op jit(solution)/shard_map/ppermute | solution.py:512
  65.9 2.5 %collective-permute-start.22 = (bf16[2,80,256]{2,1,0:T(8,128)(2,1)S(1)}, bf16[2,80,256]{2,1,0:T(8,128)(2,1)S(1)}, u32[]{:S(2)}, u32[]{:S(2)}) collective-permute-start(bf16[2,80,256]{2,1,0:T(8,128)(2,1)S(1)} %get-tuple-element.80.refs_0_), channel_id=1, source_target_pairs={{0,2},{1,3},{2,0},{3,1},{4,6},{5,7},{6,4},{7,5},{8,10},{9,11},{10,... | collective-permute-start | bytes 245768 | tf_op jit(solution)/shard_map/ppermute | solution.py:512
  75.3 1.6 %collective-permute-done.28.other = bf16[4,80,512]{2,1,0:T(8,128)(2,1)S(1)} collective-permute-done((bf16[4,80,512]{2,1,0:T(8,128)(2,1)S(1)}, bf16[4,80,512]{2,1,0:T(8,128)(2,1)S(1)}, u32[]{:S(2)}, u32[]{:S(2)}) %collective-permute-start.28) | collective-permute-done | bytes 327712 | tf_op jit(solution)/shard_map/ppermute | solution.py:515
  78.2 3.3 %collective-permute-start.31 = (bf16[2,80,256]{2,1,0:T(8,128)(2,1)S(1)}, bf16[2,80,256]{2,1,0:T(8,128)(2,1)S(1)}, u32[]{:S(2)}, u32[]{:S(2)}) collective-permute-start(bf16[2,80,256]{2,1,0:T(8,128)(2,1)S(1)} %get-tuple-element.93), channel_id=1, source_target_pairs={{0,16},{4,20},{8,24},{12,28},{16,0},{20,4},{24,8},{28,12},{1,17},{... | collective-permute-start | bytes 245768 | tf_op jit(solution)/shard_map/ppermute | solution.py:509
  82.2 5.4 %collective-permute-done.29.refs_1_ = bf16[6,80,256]{2,1,0:T(8,128)(2,1)S(1)} collective-permute-done((bf16[6,80,256]{2,1,0:T(8,128)(2,1)S(1)}, bf16[6,80,256]{2,1,0:T(8,128)(2,1)S(1)}, u32[]{:S(2)}, u32[]{:S(2)}) %collective-permute-start.29) | collective-permute-done | bytes 245792 | tf_op jit(solution)/shard_map/ppermute | solution.py:509
  87.7 3.0 %collective-permute-start.30 = (bf16[2,80,256]{2,1,0:T(8,128)(2,1)S(1)}, bf16[2,80,256]{2,1,0:T(8,128)(2,1)S(1)}, u32[]{:S(2)}, u32[]{:S(2)}) collective-permute-start(bf16[2,80,256]{2,1,0:T(8,128)(2,1)S(1)} %shard_map.120), channel_id=1, source_target_pairs={{0,16},{4,20},{8,24},{12,28},{16,0},{20,4},{24,8},{28,12},{1,17},{... | collective-permute-start | bytes 245768 | tf_op jit(solution)/shard_map/ppermute | solution.py:509
  90.7 2.9 %collective-permute-done.30.refs_2_ = bf16[2,80,256]{2,1,0:T(8,128)(2,1)S(1)} collective-permute-done((bf16[2,80,256]{2,1,0:T(8,128)(2,1)S(1)}, bf16[2,80,256]{2,1,0:T(8,128)(2,1)S(1)}, u32[]{:S(2)}, u32[]{:S(2)}) %collective-permute-start.30) | collective-permute-done | bytes 81952 | tf_op jit(solution)/shard_map/ppermute | solution.py:509
  93.9 2.5 %collective-permute-start.34 = (bf16[2,80,256]{2,1,0:T(8,128)(2,1)S(1)}, bf16[2,80,256]{2,1,0:T(8,128)(2,1)S(1)}, u32[]{:S(2)}, u32[]{:S(2)}) collective-permute-start(bf16[2,80,256]{2,1,0:T(8,128)(2,1)S(1)} %get-tuple-element.97), channel_id=1, source_target_pairs={{0,16},{4,20},{8,24},{12,28},{16,0},{20,4},{24,8},{28,12},{1,17},{... | collective-permute-start | bytes 245768 | tf_op jit(solution)/shard_map/ppermute | solution.py:509
  96.4 3.5 %collective-permute-start.33 = (bf16[4,80,256]{2,1,0:T(8,128)(2,1)S(1)}, bf16[4,80,256]{2,1,0:T(8,128)(2,1)S(1)}, u32[]{:S(2)}, u32[]{:S(2)}) collective-permute-start(bf16[4,80,256]{2,1,0:T(8,128)(2,1)S(1)} %get-tuple-element.96.refs_0_), channel_id=1, source_target_pairs={{0,8},{4,12},{8,0},{12,4},{16,24},{20,28},{24,16},{28,20},{1,9},{5... | collective-permute-start | bytes 491528 | tf_op jit(solution)/shard_map/ppermute | solution.py:509
  99.9 1.5 %collective-permute-start.35 = (bf16[2,80,256]{2,1,0:T(8,128)(2,1)S(1)}, bf16[2,80,256]{2,1,0:T(8,128)(2,1)S(1)}, u32[]{:S(2)}, u32[]{:S(2)}) collective-permute-start(bf16[2,80,256]{2,1,0:T(8,128)(2,1)S(1)} %get-tuple-element.98), channel_id=1, source_target_pairs={{0,16},{4,20},{8,24},{12,28},{16,0},{20,4},{24,8},{28,12},{1,17},{... | collective-permute-start | bytes 245768 | tf_op jit(solution)/shard_map/ppermute | solution.py:509
  101.3 1.5 %collective-permute-done.34.refs_2_ = bf16[2,80,256]{2,1,0:T(8,128)(2,1)S(1)} collective-permute-done((bf16[2,80,256]{2,1,0:T(8,128)(2,1)S(1)}, bf16[2,80,256]{2,1,0:T(8,128)(2,1)S(1)}, u32[]{:S(2)}, u32[]{:S(2)}) %collective-permute-start.34) | collective-permute-done | bytes 81952 | tf_op jit(solution)/shard_map/ppermute | solution.py:509
  102.8 1.4 %collective-permute-start.36 = (bf16[2,80,256]{2,1,0:T(8,128)(2,1)S(1)}, bf16[2,80,256]{2,1,0:T(8,128)(2,1)S(1)}, u32[]{:S(2)}, u32[]{:S(2)}) collective-permute-start(bf16[2,80,256]{2,1,0:T(8,128)(2,1)S(1)} %collective-permute-done.34.refs_2_), channel_id=1, source_target_pairs={{0,8},{4,12},{8,0},{12,4},{16,24},{20,28},{24,16},{28,20},{1,9},{5... | collective-permute-start | bytes 245768 | tf_op jit(solution)/shard_map/ppermute | solution.py:509
  104.3 1.9 %collective-permute-done.37.refs_5_ = bf16[2,80,256]{2,1,0:T(8,128)(2,1)S(1)} collective-permute-done((bf16[2,80,256]{2,1,0:T(8,128)(2,1)S(1)}, bf16[2,80,256]{2,1,0:T(8,128)(2,1)S(1)}, u32[]{:S(2)}, u32[]{:S(2)}) %collective-permute-start.37) | collective-permute-done | bytes 81952 | tf_op jit(solution)/shard_map/ppermute | solution.py:509
  109.9 2.6 %collective-permute-start.40 = (bf16[4,80,128]{2,1,0:T(8,128)(2,1)S(1)}, bf16[4,80,128]{2,1,0:T(8,128)(2,1)S(1)}, u32[]{:S(2)}, u32[]{:S(2)}) collective-permute-start(bf16[4,80,128]{2,1,0:T(8,128)(2,1)S(1)} %get-tuple-element.101), channel_id=1, source_target_pairs={{0,2},{1,3},{2,0},{3,1},{4,6},{5,7},{6,4},{7,5},{8,10},{9,11},{10,... | collective-permute-start | bytes 245768 | tf_op jit(solution)/shard_map/ppermute | solution.py:512
  114.2 1.7 %collective-permute-done.40.refs_2_ = bf16[4,80,128]{2,1,0:T(8,128)(2,1)S(1)} collective-permute-done((bf16[4,80,128]{2,1,0:T(8,128)(2,1)S(1)}, bf16[4,80,128]{2,1,0:T(8,128)(2,1)S(1)}, u32[]{:S(2)}, u32[]{:S(2)}) %collective-permute-start.40) | collective-permute-done | bytes 81952 | tf_op jit(solution)/shard_map/ppermute | solution.py:512
  116.0 1.8 %collective-permute-done.41.refs_3_ = bf16[4,80,128]{2,1,0:T(8,128)(2,1)S(1)} collective-permute-done((bf16[4,80,128]{2,1,0:T(8,128)(2,1)S(1)}, bf16[4,80,128]{2,1,0:T(8,128)(2,1)S(1)}, u32[]{:S(2)}, u32[]{:S(2)}) %collective-permute-start.41) | collective-permute-done | bytes 81952 | tf_op jit(solution)/shard_map/ppermute | solution.py:512
  (97 shorter events, 37.0 us)
Async XLA Ops:
  6.7 21.3 %collective-permute-start.9 = (bf16[4,4,128,256]{3,2,1,0:T(8,128)(2,1)}, bf16[4,4,128,256]{3,2,1,0:T(8,128)(2,1)S(1)}, u32[]{:S(2)}, u32[]{:S(2)}) collective-permute-start(bf16[4,4,128,256]{3,2,1,0:T(8,128)(2,1)} %get-tuple-element.69), channel_id=1, source_target_pairs={{0,4},{4,0},{8,12},{12,8},{16,20},{20,16},{24,28},{28,24},{1,5},{5... | collective-permute-start | bytes 3145736 | tf_op jit(solution)/shard_map/ppermute | solution.py:515
  7.2 13.0 %collective-permute-start = (bf16[2,80,256]{2,1,0:T(8,128)(2,1)}, bf16[2,80,256]{2,1,0:T(8,128)(2,1)S(1)}, u32[]{:S(2)}, u32[]{:S(2)}) collective-permute-start(bf16[2,80,256]{2,1,0:T(8,128)(2,1)} %get-tuple-element.55.refs_0_), channel_id=1, source_target_pairs={{0,1},{1,0},{2,3},{3,2},{4,5},{5,4},{6,7},{7,6},{8,9},{9,8},{10,11... | collective-permute-start | bytes 245768 | tf_op jit(solution)/shard_map/ppermute | solution.py:512
  10.3 10.0 %collective-permute-start.1 = (bf16[2,80,256]{2,1,0:T(8,128)(2,1)}, bf16[2,80,256]{2,1,0:T(8,128)(2,1)S(1)}, u32[]{:S(2)}, u32[]{:S(2)}) collective-permute-start(bf16[2,80,256]{2,1,0:T(8,128)(2,1)} %get-tuple-element.56.refs_1_), channel_id=1, source_target_pairs={{0,2},{1,3},{2,0},{3,1},{4,6},{5,7},{6,4},{7,5},{8,10},{9,11},{10,... | collective-permute-start | bytes 245768 | tf_op jit(solution)/shard_map/ppermute | solution.py:512
  11.8 4.9 %collective-permute-start.4 = (bf16[2,80,256]{2,1,0:T(8,128)(2,1)}, bf16[2,80,256]{2,1,0:T(8,128)(2,1)S(1)}, u32[]{:S(2)}, u32[]{:S(2)}) collective-permute-start(bf16[2,80,256]{2,1,0:T(8,128)(2,1)} %get-tuple-element.57.refs_2_), channel_id=1, source_target_pairs={{0,1},{1,0},{2,3},{3,2},{4,5},{5,4},{6,7},{7,6},{8,9},{9,8},{10,11... | collective-permute-start | bytes 245768 | tf_op jit(solution)/shard_map/ppermute | solution.py:512
  12.1 4.7 %collective-permute-start.5 = (bf16[2,80,256]{2,1,0:T(8,128)(2,1)}, bf16[2,80,256]{2,1,0:T(8,128)(2,1)S(1)}, u32[]{:S(2)}, u32[]{:S(2)}) collective-permute-start(bf16[2,80,256]{2,1,0:T(8,128)(2,1)} %get-tuple-element.58.refs_3_), channel_id=1, source_target_pairs={{0,2},{1,3},{2,0},{3,1},{4,6},{5,7},{6,4},{7,5},{8,10},{9,11},{10,... | collective-permute-start | bytes 245768 | tf_op jit(solution)/shard_map/ppermute | solution.py:512
  16.8 4.5 %collective-permute-start.6 = (bf16[2,80,256]{2,1,0:T(8,128)(2,1)S(1)}, bf16[2,80,256]{2,1,0:T(8,128)(2,1)S(1)}, u32[]{:S(2)}, u32[]{:S(2)}) collective-permute-start(bf16[2,80,256]{2,1,0:T(8,128)(2,1)S(1)} %get-tuple-element.65.refs_4_), channel_id=1, source_target_pairs={{0,2},{1,3},{2,0},{3,1},{4,6},{5,7},{6,4},{7,5},{8,10},{9,11},{10,... | collective-permute-start | bytes 245768 | tf_op jit(solution)/shard_map/ppermute | solution.py:512
  18.5 5.2 %collective-permute-start.7 = (bf16[2,80,256]{2,1,0:T(8,128)(2,1)S(1)}, bf16[2,80,256]{2,1,0:T(8,128)(2,1)S(1)}, u32[]{:S(2)}, u32[]{:S(2)}) collective-permute-start(bf16[2,80,256]{2,1,0:T(8,128)(2,1)S(1)} %get-tuple-element.66.refs_6_), channel_id=1, source_target_pairs={{0,1},{1,0},{2,3},{3,2},{4,5},{5,4},{6,7},{7,6},{8,9},{9,8},{10,11... | collective-permute-start | bytes 245768 | tf_op jit(solution)/shard_map/ppermute | solution.py:512
  28.9 9.8 %collective-permute-start.10 = (bf16[6,80,256]{2,1,0:T(8,128)(2,1)S(1)}, bf16[6,80,256]{2,1,0:T(8,128)(2,1)S(1)}, u32[]{:S(2)}, u32[]{:S(2)}) collective-permute-start(bf16[6,80,256]{2,1,0:T(8,128)(2,1)S(1)} %get-tuple-element.71), channel_id=1, source_target_pairs={{0,8},{4,12},{8,0},{12,4},{16,24},{20,28},{24,16},{28,20},{1,9},{5... | collective-permute-start | bytes 737288 | tf_op jit(solution)/shard_map/ppermute | solution.py:509
  30.3 10.5 %collective-permute-start.12 = (bf16[2,80,256]{2,1,0:T(8,128)(2,1)S(1)}, bf16[2,80,256]{2,1,0:T(8,128)(2,1)S(1)}, u32[]{:S(2)}, u32[]{:S(2)}) collective-permute-start(bf16[2,80,256]{2,1,0:T(8,128)(2,1)S(1)} %get-tuple-element.73), channel_id=1, source_target_pairs={{0,16},{4,20},{8,24},{12,28},{16,0},{20,4},{24,8},{28,12},{1,17},{... | collective-permute-start | bytes 245768 | tf_op jit(solution)/shard_map/ppermute | solution.py:509
  32.6 9.4 %collective-permute-start.13 = (bf16[2,80,256]{2,1,0:T(8,128)(2,1)S(1)}, bf16[2,80,256]{2,1,0:T(8,128)(2,1)S(1)}, u32[]{:S(2)}, u32[]{:S(2)}) collective-permute-start(bf16[2,80,256]{2,1,0:T(8,128)(2,1)S(1)} %get-tuple-element.74), channel_id=1, source_target_pairs={{0,24},{4,28},{8,16},{12,20},{16,8},{20,12},{24,0},{28,4},{1,25},{... | collective-permute-start | bytes 245768 | tf_op jit(solution)/shard_map/ppermute | solution.py:509
  38.8 6.6 %collective-permute-start.11 = (bf16[2,80,256]{2,1,0:T(8,128)(2,1)S(1)}, bf16[2,80,256]{2,1,0:T(8,128)(2,1)S(1)}, u32[]{:S(2)}, u32[]{:S(2)}) collective-permute-start(bf16[2,80,256]{2,1,0:T(8,128)(2,1)S(1)} %shard_map.110), channel_id=1, source_target_pairs={{0,16},{4,20},{8,24},{12,28},{16,0},{20,4},{24,8},{28,12},{1,17},{... | collective-permute-start | bytes 245768 | tf_op jit(solution)/shard_map/ppermute | solution.py:509
  45.6 6.8 %collective-permute-start.15 = (bf16[2,80,256]{2,1,0:T(8,128)(2,1)S(1)}, bf16[2,80,256]{2,1,0:T(8,128)(2,1)S(1)}, u32[]{:S(2)}, u32[]{:S(2)}) collective-permute-start(bf16[2,80,256]{2,1,0:T(8,128)(2,1)S(1)} %get-tuple-element.76), channel_id=1, source_target_pairs={{0,16},{4,20},{8,24},{12,28},{16,0},{20,4},{24,8},{28,12},{1,17},{... | collective-permute-start | bytes 245768 | tf_op jit(solution)/shard_map/ppermute | solution.py:509
  46.2 11.8 %collective-permute-start.14 = (bf16[4,80,256]{2,1,0:T(8,128)(2,1)S(1)}, bf16[4,80,256]{2,1,0:T(8,128)(2,1)S(1)}, u32[]{:S(2)}, u32[]{:S(2)}) collective-permute-start(bf16[4,80,256]{2,1,0:T(8,128)(2,1)S(1)} %get-tuple-element.75.refs_0_), channel_id=1, source_target_pairs={{0,8},{4,12},{8,0},{12,4},{16,24},{20,28},{24,16},{28,20},{1,9},{5... | collective-permute-start | bytes 491528 | tf_op jit(solution)/shard_map/ppermute | solution.py:509
  48.8 8.1 %collective-permute-start.18 = (bf16[2,80,256]{2,1,0:T(8,128)(2,1)S(1)}, bf16[2,80,256]{2,1,0:T(8,128)(2,1)S(1)}, u32[]{:S(2)}, u32[]{:S(2)}) collective-permute-start(bf16[2,80,256]{2,1,0:T(8,128)(2,1)S(1)} %get-tuple-element.77), channel_id=1, source_target_pairs={{0,24},{4,28},{8,16},{12,20},{16,8},{20,12},{24,0},{28,4},{1,25},{... | collective-permute-start | bytes 245768 | tf_op jit(solution)/shard_map/ppermute | solution.py:509
  50.1 7.9 %collective-permute-start.16 = (bf16[2,80,256]{2,1,0:T(8,128)(2,1)S(1)}, bf16[2,80,256]{2,1,0:T(8,128)(2,1)S(1)}, u32[]{:S(2)}, u32[]{:S(2)}) collective-permute-start(bf16[2,80,256]{2,1,0:T(8,128)(2,1)S(1)} %get-tuple-element.77), channel_id=1, source_target_pairs={{0,16},{4,20},{8,24},{12,28},{16,0},{20,4},{24,8},{28,12},{1,17},{... | collective-permute-start | bytes 245768 | tf_op jit(solution)/shard_map/ppermute | solution.py:509
  52.5 5.7 %collective-permute-start.17 = (bf16[2,80,256]{2,1,0:T(8,128)(2,1)S(1)}, bf16[2,80,256]{2,1,0:T(8,128)(2,1)S(1)}, u32[]{:S(2)}, u32[]{:S(2)}) collective-permute-start(bf16[2,80,256]{2,1,0:T(8,128)(2,1)S(1)} %collective-permute-done.15.refs_2_), channel_id=1, source_target_pairs={{0,8},{4,12},{8,0},{12,4},{16,24},{20,28},{24,16},{28,20},{1,9},{5... | collective-permute-start | bytes 245768 | tf_op jit(solution)/shard_map/ppermute | solution.py:509
  60.5 4.6 %collective-permute-start.20 = (bf16[2,80,256]{2,1,0:T(8,128)(2,1)S(1)}, bf16[2,80,256]{2,1,0:T(8,128)(2,1)S(1)}, u32[]{:S(2)}, u32[]{:S(2)}) collective-permute-start(bf16[2,80,256]{2,1,0:T(8,128)(2,1)S(1)} %get-tuple-element.78.one), channel_id=1, source_target_pairs={{0,1},{1,0},{2,3},{3,2},{4,5},{5,4},{6,7},{7,6},{8,9},{9,8},{10,11... | collective-permute-start | bytes 245768 | tf_op jit(solution)/shard_map/ppermute | solution.py:512
  61.1 4.7 %collective-permute-start.21 = (bf16[2,80,256]{2,1,0:T(8,128)(2,1)S(1)}, bf16[2,80,256]{2,1,0:T(8,128)(2,1)S(1)}, u32[]{:S(2)}, u32[]{:S(2)}) collective-permute-start(bf16[2,80,256]{2,1,0:T(8,128)(2,1)S(1)} %get-tuple-element.79.two), channel_id=1, source_target_pairs={{0,2},{1,3},{2,0},{3,1},{4,6},{5,7},{6,4},{7,5},{8,10},{9,11},{10,... | collective-permute-start | bytes 245768 | tf_op jit(solution)/shard_map/ppermute | solution.py:512
  63.2 6.2 %collective-permute-start.24 = (bf16[2,80,256]{2,1,0:T(8,128)(2,1)S(1)}, bf16[2,80,256]{2,1,0:T(8,128)(2,1)S(1)}, u32[]{:S(2)}, u32[]{:S(2)}) collective-permute-start(bf16[2,80,256]{2,1,0:T(8,128)(2,1)S(1)} %get-tuple-element.82.one), channel_id=1, source_target_pairs={{0,1},{1,0},{2,3},{3,2},{4,5},{5,4},{6,7},{7,6},{8,9},{9,8},{10,11... | collective-permute-start | bytes 245768 | tf_op jit(solution)/shard_map/ppermute | solution.py:512
  64.1 5.3 %collective-permute-start.25 = (bf16[2,80,256]{2,1,0:T(8,128)(2,1)S(1)}, bf16[2,80,256]{2,1,0:T(8,128)(2,1)S(1)}, u32[]{:S(2)}, u32[]{:S(2)}) collective-permute-start(bf16[2,80,256]{2,1,0:T(8,128)(2,1)S(1)} %get-tuple-element.83.two), channel_id=1, source_target_pairs={{0,2},{1,3},{2,0},{3,1},{4,6},{5,7},{6,4},{7,5},{8,10},{9,11},{10,... | collective-permute-start | bytes 245768 | tf_op jit(solution)/shard_map/ppermute | solution.py:512
  65.9 5.8 %collective-permute-start.22 = (bf16[2,80,256]{2,1,0:T(8,128)(2,1)S(1)}, bf16[2,80,256]{2,1,0:T(8,128)(2,1)S(1)}, u32[]{:S(2)}, u32[]{:S(2)}) collective-permute-start(bf16[2,80,256]{2,1,0:T(8,128)(2,1)S(1)} %get-tuple-element.80.refs_0_), channel_id=1, source_target_pairs={{0,2},{1,3},{2,0},{3,1},{4,6},{5,7},{6,4},{7,5},{8,10},{9,11},{10,... | collective-permute-start | bytes 245768 | tf_op jit(solution)/shard_map/ppermute | solution.py:512
  77.8 9.8 %collective-permute-start.29 = (bf16[6,80,256]{2,1,0:T(8,128)(2,1)S(1)}, bf16[6,80,256]{2,1,0:T(8,128)(2,1)S(1)}, u32[]{:S(2)}, u32[]{:S(2)}) collective-permute-start(bf16[6,80,256]{2,1,0:T(8,128)(2,1)S(1)} %get-tuple-element.91), channel_id=1, source_target_pairs={{0,8},{4,12},{8,0},{12,4},{16,24},{20,28},{24,16},{28,20},{1,9},{5... | collective-permute-start | bytes 737288 | tf_op jit(solution)/shard_map/ppermute | solution.py:509
  78.2 12.5 %collective-permute-start.31 = (bf16[2,80,256]{2,1,0:T(8,128)(2,1)S(1)}, bf16[2,80,256]{2,1,0:T(8,128)(2,1)S(1)}, u32[]{:S(2)}, u32[]{:S(2)}) collective-permute-start(bf16[2,80,256]{2,1,0:T(8,128)(2,1)S(1)} %get-tuple-element.93), channel_id=1, source_target_pairs={{0,16},{4,20},{8,24},{12,28},{16,0},{20,4},{24,8},{28,12},{1,17},{... | collective-permute-start | bytes 245768 | tf_op jit(solution)/shard_map/ppermute | solution.py:509
  81.5 9.2 %collective-permute-start.32 = (bf16[2,80,256]{2,1,0:T(8,128)(2,1)S(1)}, bf16[2,80,256]{2,1,0:T(8,128)(2,1)S(1)}, u32[]{:S(2)}, u32[]{:S(2)}) collective-permute-start(bf16[2,80,256]{2,1,0:T(8,128)(2,1)S(1)} %get-tuple-element.94), channel_id=1, source_target_pairs={{0,24},{4,28},{8,16},{12,20},{16,8},{20,12},{24,0},{28,4},{1,25},{... | collective-permute-start | bytes 245768 | tf_op jit(solution)/shard_map/ppermute | solution.py:509
  87.7 5.9 %collective-permute-start.30 = (bf16[2,80,256]{2,1,0:T(8,128)(2,1)S(1)}, bf16[2,80,256]{2,1,0:T(8,128)(2,1)S(1)}, u32[]{:S(2)}, u32[]{:S(2)}) collective-permute-start(bf16[2,80,256]{2,1,0:T(8,128)(2,1)S(1)} %shard_map.120), channel_id=1, source_target_pairs={{0,16},{4,20},{8,24},{12,28},{16,0},{20,4},{24,8},{28,12},{1,17},{... | collective-permute-start | bytes 245768 | tf_op jit(solution)/shard_map/ppermute | solution.py:509
  93.9 8.9 %collective-permute-start.34 = (bf16[2,80,256]{2,1,0:T(8,128)(2,1)S(1)}, bf16[2,80,256]{2,1,0:T(8,128)(2,1)S(1)}, u32[]{:S(2)}, u32[]{:S(2)}) collective-permute-start(bf16[2,80,256]{2,1,0:T(8,128)(2,1)S(1)} %get-tuple-element.97), channel_id=1, source_target_pairs={{0,16},{4,20},{8,24},{12,28},{16,0},{20,4},{24,8},{28,12},{1,17},{... | collective-permute-start | bytes 245768 | tf_op jit(solution)/shard_map/ppermute | solution.py:509
  96.4 10.9 %collective-permute-start.33 = (bf16[4,80,256]{2,1,0:T(8,128)(2,1)S(1)}, bf16[4,80,256]{2,1,0:T(8,128)(2,1)S(1)}, u32[]{:S(2)}, u32[]{:S(2)}) collective-permute-start(bf16[4,80,256]{2,1,0:T(8,128)(2,1)S(1)} %get-tuple-element.96.refs_0_), channel_id=1, source_target_pairs={{0,8},{4,12},{8,0},{12,4},{16,24},{20,28},{24,16},{28,20},{1,9},{5... | collective-permute-start | bytes 491528 | tf_op jit(solution)/shard_map/ppermute | solution.py:509
  99.9 6.2 %collective-permute-start.37 = (bf16[2,80,256]{2,1,0:T(8,128)(2,1)S(1)}, bf16[2,80,256]{2,1,0:T(8,128)(2,1)S(1)}, u32[]{:S(2)}, u32[]{:S(2)}) collective-permute-start(bf16[2,80,256]{2,1,0:T(8,128)(2,1)S(1)} %get-tuple-element.98), channel_id=1, source_target_pairs={{0,24},{4,28},{8,16},{12,20},{16,8},{20,12},{24,0},{28,4},{1,25},{... | collective-permute-start | bytes 245768 | tf_op jit(solution)/shard_map/ppermute | solution.py:509
  99.9 6.2 %collective-permute-start.35 = (bf16[2,80,256]{2,1,0:T(8,128)(2,1)S(1)}, bf16[2,80,256]{2,1,0:T(8,128)(2,1)S(1)}, u32[]{:S(2)}, u32[]{:S(2)}) collective-permute-start(bf16[2,80,256]{2,1,0:T(8,128)(2,1)S(1)} %get-tuple-element.98), channel_id=1, source_target_pairs={{0,16},{4,20},{8,24},{12,28},{16,0},{20,4},{24,8},{28,12},{1,17},{... | collective-permute-start | bytes 245768 | tf_op jit(solution)/shard_map/ppermute | solution.py:509
  109.7 4.6 %collective-permute-start.39 = (bf16[4,80,128]{2,1,0:T(8,128)(2,1)S(1)}, bf16[4,80,128]{2,1,0:T(8,128)(2,1)S(1)}, u32[]{:S(2)}, u32[]{:S(2)}) collective-permute-start(bf16[4,80,128]{2,1,0:T(8,128)(2,1)S(1)} %get-tuple-element.100), channel_id=1, source_target_pairs={{0,1},{1,0},{2,3},{3,2},{4,5},{5,4},{6,7},{7,6},{8,9},{9,8},{10,11... | collective-permute-start | bytes 245768 | tf_op jit(solution)/shard_map/ppermute | solution.py:512
  109.9 6.1 %collective-permute-start.40 = (bf16[4,80,128]{2,1,0:T(8,128)(2,1)S(1)}, bf16[4,80,128]{2,1,0:T(8,128)(2,1)S(1)}, u32[]{:S(2)}, u32[]{:S(2)}) collective-permute-start(bf16[4,80,128]{2,1,0:T(8,128)(2,1)S(1)} %get-tuple-element.101), channel_id=1, source_target_pairs={{0,2},{1,3},{2,0},{3,1},{4,6},{5,7},{6,4},{7,5},{8,10},{9,11},{10,... | collective-permute-start | bytes 245768 | tf_op jit(solution)/shard_map/ppermute | solution.py:512
  112.4 5.3 %collective-permute-start.41 = (bf16[4,80,128]{2,1,0:T(8,128)(2,1)S(1)}, bf16[4,80,128]{2,1,0:T(8,128)(2,1)S(1)}, u32[]{:S(2)}, u32[]{:S(2)}) collective-permute-start(bf16[4,80,128]{2,1,0:T(8,128)(2,1)S(1)} %get-tuple-element.102), channel_id=1, source_target_pairs={{0,3},{1,2},{2,1},{3,0},{4,7},{5,6},{6,5},{7,4},{8,11},{9,10},{10,... | collective-permute-start | bytes 245768 | tf_op jit(solution)/shard_map/ppermute | solution.py:512
  (18 other events, 104.5 us)

commit v9 on v8

--- a/solution.py
+++ b/solution.py
@@ -305,38 +305,31 @@
 def forward_kernel(sends, mine, other, own, partner, *outs):
     z, core, obs = place()
     members, levp, lanes = mine.shape
-    chips, width = own.shape[0], own.shape[3]
-    rows = members * levp
+    width = own.shape[3]
     scalars = [read_scalars([mine.at[m], other.at[m]], 2) for m in range(members)]
-    for i in reversed(range(chips)):
-        zz = z ^ i
-        y = jnp.dot(
-            mine[...].reshape(rows, lanes),
-            own[zz].reshape(lanes, width),
-            preferred_element_type=F32,
-        )
-        y = y + jnp.dot(
-            other[...].reshape(rows, lanes),
-            partner[zz].reshape(lanes, width),
-            preferred_element_type=F32,
-        )
-        y = y.reshape(members, levp, width)
-        for out, parts in zip(outs, sends):
-            at = 0
-            for chip, first, count in parts:
-                for m in range(first, first + count if chip == i else first):
-                    out[at + m - first] = with_scalars(y[m], scalars[m]).astype(out.dtype)
-                at += count
+    for out, (chip, first, count) in zip(outs, sends):
+        zz = z ^ chip
+        y = [
+            jnp.dot(
+                x[first : first + count].reshape(count * levp, lanes),
+                tiles[zz].reshape(lanes, width),
+                preferred_element_type=F32,
+            )
+            for x, tiles in ((mine, own), (other, partner))
+        ]
+        y = (y[0] + y[1]).reshape(count, levp, width)
+        for m in range(count):
+            out[m] = with_scalars(y[m], scalars[first + m]).astype(out.dtype)
 
 
 def weigh_kernel(later, last, spans, *refs):
     ys, refs = refs[: len(spans)], refs[len(spans) :]
     prec = refs[0]
-    state, weighted, *parts = refs[3 if later else 1 :]
+    state, *parts = refs[3 if later else 1 :]
     if not last:
         *parts, image = parts
     p = prec[...]
-    for m in range(weighted.shape[0]):
+    for m in range(state.shape[0]):
         mine = of_member(ys, spans, m)
         y = add([x[...] for x in mine])
         norm, cross = read_scalars(mine, 2)
@@ -353,7 +346,6 @@
         if not last:
             image[m] = y
         value = with_scalars(scaled, [total(scaled * y)]).astype(BF16)
-        weighted[m] = value
         first = 0
         for part in parts:
             if first <= m < first + part.shape[0]:
@@ -370,7 +362,8 @@
     width = ws[0].shape[2]
     acc = None
     for i in range(tiles.shape[0]):
-        w = [ref[...].reshape(-1, width) for ref, (chip, *span) in zip(ws, plan) if chip == i]
+        w = {span[0]: ref for ref, (chip, *span) in zip(ws, plan) if chip == i}
+        w = [w[first][...].reshape(-1, width) for first in sorted(w)]
         w = w[0] if len(w) == 1 else jnp.concatenate(w, axis=0)
         part = lax.dot_general(
             w, tiles[z ^ i].reshape(lanes, width), NT, preferred_element_type=F32
@@ -480,17 +473,15 @@
     slab_field = (members, levp, lanes)
     panel = (members, levp, width)
     some, rest = members // 2, members - members // 2
-    half_fields = [
-        struct((n, levp, lanes // 2), BF16) for n in (some, rest) if n for half in range(2)
-    ]
+    half_fields = [struct((members, levp, lanes // 2), BF16)] * 2
     via = chips == 4 and some > 0
     if via:
-        plan = [(0, 0, members), (1, 0, members)]
-        plan += [(i, *span) for i in (2, 3) for span in ((0, some), (some, rest))]
-        sends = [[plan[0]], [plan[4], plan[1]], [plan[2]], [plan[3]], [plan[5]]]
+        plan = [(i, *span) for i in range(chips) for span in ((0, some), (some, rest))]
+        sends = [plan[6], plan[5], plan[7], *plan[2:4], (0, 0, members), plan[4]]
+        plan = [*plan[0:2], plan[5], plan[7], *plan[2:4], plan[4], plan[6]]
     else:
         plan = [(i, 0, members) for i in range(chips)]
-        sends = [[part] for part in plan]
+        sends = plan
     pad = ((0, levp - lev), (0, levp - lev))
     high = lax.reduce_precision(vert_factor, 8, 7)
     low = vert_factor - high
@@ -546,33 +537,47 @@
                 )
         return [x for pair in zip(halves, moved_halves) for x in pair]
 
-    def line_sum(ys):
+    def line_sum(moved, other):
+        ys = call(
+            functools.partial(forward_kernel, sends),
+            [
+                struct((count, levp, width), F32 if i == 0 or (via and at == 6) else BF16)
+                for at, (i, unused, count) in enumerate(sends)
+            ],
+            [],
+            2 * product,
+            moved,
+            other,
+            own,
+            partner,
+        )
         if not via:
             return [y if i == 0 else along(y, i) for i, y in enumerate(ys)], [
                 (0, members, 0) for y in ys
             ]
-        near, next_, far, far_rest, last_rest = ys
-        next_ = along(next_, 1)
+        passed, far_rest, last_rest, next_some, next_rest, near, far = ys
+        passed = along(passed, 1)
         far_rest, last_rest = along(far_rest, 2), along(last_rest, 3)
+        next_some, next_rest = along(next_some, 1), along(next_rest, 1)
         (far,) = call(
             functools.partial(add_kernel, 2),
             [struct((some, levp, width), BF16)],
             [],
             0,
             far,
-            next_,
+            passed,
         )
-        spans = [(0, members, 0), (0, members, some), (0, some, 0)]
-        spans += [(some, rest, 0), (some, rest, 0)]
-        return [near, next_, along(far, 2), far_rest, last_rest], spans
-
-    def line_gather(w, *parts):
+        ys = [near, far_rest, last_rest, next_some, next_rest, along(far, 2)]
+        spans = [(0, members, 0)] + [(some, rest, 0)] * 2 + [(0, some, 0), (some, rest, 0)]
+        return ys, spans + [(0, some, 0)]
+
+    def line_gather(*parts):
         if not via:
-            return [w if i == 0 else along(w, i) for i in range(chips)]
+            return [parts[0] if i == 0 else along(parts[0], i) for i in range(chips)]
         one, two = parts
         far = along(one, 2)
-        far_rest, last_rest, next_ = along(two, 2), along(two, 3), along(w, 1)
-        return [w, next_, far, far_rest, along(far, 1), last_rest]
+        far_rest, last_rest = along(two, 2), along(two, 3)
+        return [one, two, far_rest, last_rest, along(one, 1), along(two, 1), far, along(far, 1)]
 
     dense = struct((chips, colblocks, LANES, width), BF16)
     own, for_partner, *partials = call(
@@ -625,27 +630,11 @@
     direction = total_step = image = state = None
     for sweep in range(ITERS):
         later, last = sweep > 0, sweep == ITERS - 1
-        ys = call(
-            functools.partial(forward_kernel, sends),
-            [
-                struct(
-                    (sum(count for *unused, count in parts), levp, width),
-                    F32 if at == 0 or (via and at == 2) else BF16,
-                )
-                for at, parts in enumerate(sends)
-            ],
-            [],
-            2 * product,
-            moved,
-            swap(moved),
-            own,
-            partner,
-        )
-        ys, spans = line_sum(ys)
+        ys, spans = line_sum(moved, swap(moved))
         state, *weighted = call(
             functools.partial(weigh_kernel, later, last, spans),
-            [struct((members, 8, LANES), F32), struct(panel, BF16)]
-            + ([struct((n, levp, width), BF16) for n in (some, rest)] if via else [])
+            [struct((members, 8, LANES), F32)]
+            + [struct((n, levp, width), BF16) for n in ((some, rest) if via else (members,))]
             + ([] if last else [struct(panel, F32)]),
             [],
             0,
@@ -680,7 +669,7 @@
             ps = call(
                 combine_columns_kernel, [struct(field, BF16)] * n_obs, [], 0, mine, theirs
             )
-            ps = [x if i == 0 else plane(x, i) for i, x in enumerate(ps)]
+            ps = [ps[0]] + [plane(ps[i], i) for i in reversed(range(1, n_obs))]
             outputs = call(
                 functools.partial(last_kernel, len(ps), later, lev),
                 [struct((lev, members, LANES), F32)] * 2,

time: 119 us -> 114 us (0.958)
  starting transfers between devices: 50.9 us -> 42.6 us
  waiting for transfers between devices: 48.3 us -> 54 us
  local copies, waits for them, and re-layouts: 3.78 us -> 2.1 us
    ppermute x19 -> x11, starting transfers between devices: 21.6 us -> 13.3 us  [plane(): return lax.ppermute(x, 'obs', [(o, o ^ i) for o in range(n_obs)])]
    ppermute x19 -> x11, waiting for transfers between devices: 13.5 us -> 19.9 us  [plane(): return lax.ppermute(x, 'obs', [(o, o ^ i) for o in range(n_obs)])]
    unnamed x17 -> x13, local copies, waits for them, and re-layouts: 3.66 us -> 1.98 us
    ppermute x18 -> x24, waiting for transfers between devices: 29.4 us -> 28.8 us  [along(): return lax.ppermute(x, 'slab', [(s, s ^ 2 * i) for s in range(n_slab)])]
    pallas_call x22 -> x20, Pallas kernels: 14.2 us -> 13.9 us  [call(): pl.pallas_call(kernel, out_shape=outs, in_specs=[space] * len(args), out_...]
    ppermute x18 -> x24, starting transfers between devices: 28.5 us -> 28.4 us  [along(): return lax.ppermute(x, 'slab', [(s, s ^ 2 * i) for s in range(n_slab)])]
  transfers between devices with their start and end apart: 42 -> 40, of which waited for: 31 -> 32; matrix products, arithmetic and copies ran while one was open for 0% -> 0% of each run, Pallas kernels for 3% -> 3%
where the time goes in v9:
time: 114 us
  waiting for transfers between devices  54 us (47%)
  starting transfers between devices  42.6 us (37%)
  Pallas kernels  13.9 us (12%)
  local copies, waits for them, and re-layouts  2.1 us (2%)
  between operations  1.53 us (1%)
    ppermute x24, waiting for transfers between devices, along(): return lax.ppermute(x, 'slab', [(s, s ^ 2 * i) for s in range(n_slab)])  28.8 us
    ppermute x24, starting transfers between devices, along(): return lax.ppermute(x, 'slab', [(s, s ^ 2 * i) for s in range(n_slab)])  28.4 us
    ppermute x11, waiting for transfers between devices, plane(): return lax.ppermute(x, 'obs', [(o, o ^ i) for o in range(n_obs)])  19.9 us
    pallas_call x20, Pallas kernels, call(): pl.pallas_call(kernel, out_shape=outs, in_specs=[space] * len(args), out_...  13.9 us
    ppermute x11, starting transfers between devices, plane(): return lax.ppermute(x, 'obs', [(o, o ^ i) for o in range(n_obs)])  13.3 us
    ppermute x5, waiting for transfers between devices, swap(): return lax.ppermute(x, 'slab', [(s, s ^ 1) for s in range(n_slab)])  5.36 us
  transfers between devices with their start and end apart: 40, of which 32 were waited for; matrix products, arithmetic and copies ran while one was open for 0% of the time, Pallas kernels for 3%

profile of v9, /device:TPU:0, one launch (start us, length us, event | category | flops | bytes accessed | tf_op | source)
XLA Modules:
  0.0 114.2 jit_solution(903168095836230241)
XLA Ops:
  1.3 5.1 %shard_map.104 = (bf16[4,4,128,256]{3,2,1,0:T(8,128)(2,1)}, bf16[4,4,128,256]{3,2,1,0:T(8,128)(2,1)}, bf16[4,80,256]{2,1,0:T(8,128)(2,1)}, bf16[4,80,256]{2,1,0:T(8,128)(2,1)}) custom-call(s32[4]{0:T(128)} %seeds_in.1, s32[1,1,32]{2,1,0:T(1,128)} %ids_in.1, s32[1,1,32]{2,1,0:T(1,128)} %cols_in.1, s32[1,1]{1,0:T(1,128)S(6)} %copy.16.count_in, ...), custom_call_target="tpu_custom_call" | custom-call | flops 671088640 | bytes 5751572 | tf_op jit(solution)/shard_map/pallas_call | solution.py:23
  7.0 2.6 %collective-permute-start = (bf16[4,80,256]{2,1,0:T(8,128)(2,1)}, bf16[4,80,256]{2,1,0:T(8,128)(2,1)S(1)}, u32[]{:S(2)}, u32[]{:S(2)}) collective-permute-start(bf16[4,80,256]{2,1,0:T(8,128)(2,1)} %get-tuple-element.47.refs_0_), channel_id=1, source_target_pairs={{0,1},{1,0},{2,3},{3,2},{4,5},{5,4},{6,7},{7,6},{8,9},{9,8},{10,11... | collective-permute-start | bytes 491528 | tf_op jit(solution)/shard_map/ppermute | solution.py:503
  18.5 3.2 %collective-permute-done.2.refs_1_ = bf16[4,80,256]{2,1,0:T(8,128)(2,1)S(1)} collective-permute-done((bf16[4,80,256]{2,1,0:T(8,128)(2,1)S(1)}, bf16[4,80,256]{2,1,0:T(8,128)(2,1)S(1)}, u32[]{:S(2)}, u32[]{:S(2)}) %collective-permute-start.2) | collective-permute-done | bytes 163872 | tf_op jit(solution)/shard_map/ppermute | solution.py:503
  24.1 1.6 %collective-permute-done.4.other = bf16[4,80,512]{2,1,0:T(8,128)(2,1)S(1)} collective-permute-done((bf16[4,80,512]{2,1,0:T(8,128)(2,1)S(1)}, bf16[4,80,512]{2,1,0:T(8,128)(2,1)S(1)}, u32[]{:S(2)}, u32[]{:S(2)}) %collective-permute-start.4) | collective-permute-done | bytes 327712 | tf_op jit(solution)/shard_map/ppermute | solution.py:506
  26.6 1.7 %collective-permute-start.10 = (bf16[2,80,256]{2,1,0:T(8,128)(2,1)S(1)}, bf16[2,80,256]{2,1,0:T(8,128)(2,1)S(1)}, u32[]{:S(2)}, u32[]{:S(2)}) collective-permute-start(bf16[2,80,256]{2,1,0:T(8,128)(2,1)S(1)} %get-tuple-element.62), channel_id=1, source_target_pairs={{0,8},{4,12},{8,0},{12,4},{16,24},{20,28},{24,16},{28,20},{1,9},{5... | collective-permute-start | bytes 245768 | tf_op jit(solution)/shard_map/ppermute | solution.py:500
  28.3 3.1 %collective-permute-start.6 = (bf16[2,80,256]{2,1,0:T(8,128)(2,1)S(1)}, bf16[2,80,256]{2,1,0:T(8,128)(2,1)S(1)}, u32[]{:S(2)}, u32[]{:S(2)}) collective-permute-start(bf16[2,80,256]{2,1,0:T(8,128)(2,1)S(1)} %get-tuple-element.57), channel_id=1, source_target_pairs={{0,16},{4,20},{8,24},{12,28},{16,0},{20,4},{24,8},{28,12},{1,17},{... | collective-permute-start | bytes 245768 | tf_op jit(solution)/shard_map/ppermute | solution.py:500
  33.5 2.5 %collective-permute-start.11 = (bf16[2,80,256]{2,1,0:T(8,128)(2,1)S(1)}, bf16[2,80,256]{2,1,0:T(8,128)(2,1)S(1)}, u32[]{:S(2)}, u32[]{:S(2)}) collective-permute-start(bf16[2,80,256]{2,1,0:T(8,128)(2,1)S(1)} %shard_map.109), channel_id=1, source_target_pairs={{0,16},{4,20},{8,24},{12,28},{16,0},{20,4},{24,8},{28,12},{1,17},{... | collective-permute-start | bytes 245768 | tf_op jit(solution)/shard_map/ppermute | solution.py:500
  39.9 2.7 %collective-permute-done.11.refs_5_ = bf16[2,80,256]{2,1,0:T(8,128)(2,1)S(1)} collective-permute-done((bf16[2,80,256]{2,1,0:T(8,128)(2,1)S(1)}, bf16[2,80,256]{2,1,0:T(8,128)(2,1)S(1)}, u32[]{:S(2)}, u32[]{:S(2)}) %collective-permute-start.11) | collective-permute-done | bytes 81952 | tf_op jit(solution)/shard_map/ppermute | solution.py:500
  43.9 2.0 %collective-permute-start.14 = (bf16[2,80,256]{2,1,0:T(8,128)(2,1)S(1)}, bf16[2,80,256]{2,1,0:T(8,128)(2,1)S(1)}, u32[]{:S(2)}, u32[]{:S(2)}) collective-permute-start(bf16[2,80,256]{2,1,0:T(8,128)(2,1)S(1)} %get-tuple-element.63.refs_0_), channel_id=1, source_target_pairs={{0,8},{4,12},{8,0},{12,4},{16,24},{20,28},{24,16},{28,20},{1,9},{5... | collective-permute-start | bytes 245768 | tf_op jit(solution)/shard_map/ppermute | solution.py:500
  45.9 1.7 %collective-permute-start.13 = (bf16[2,80,256]{2,1,0:T(8,128)(2,1)S(1)}, bf16[2,80,256]{2,1,0:T(8,128)(2,1)S(1)}, u32[]{:S(2)}, u32[]{:S(2)}) collective-permute-start(bf16[2,80,256]{2,1,0:T(8,128)(2,1)S(1)} %get-tuple-element.64.refs_1_), channel_id=1, source_target_pairs={{0,24},{4,28},{8,16},{12,20},{16,8},{20,12},{24,0},{28,4},{1,25},{... | collective-permute-start | bytes 245768 | tf_op jit(solution)/shard_map/ppermute | solution.py:500
  47.6 1.7 %collective-permute-start.12 = (bf16[2,80,256]{2,1,0:T(8,128)(2,1)S(1)}, bf16[2,80,256]{2,1,0:T(8,128)(2,1)S(1)}, u32[]{:S(2)}, u32[]{:S(2)}) collective-permute-start(bf16[2,80,256]{2,1,0:T(8,128)(2,1)S(1)} %get-tuple-element.64.refs_1_), channel_id=1, source_target_pairs={{0,16},{4,20},{8,24},{12,28},{16,0},{20,4},{24,8},{28,12},{1,17},{... | collective-permute-start | bytes 245768 | tf_op jit(solution)/shard_map/ppermute | solution.py:500
  49.3 1.6 %collective-permute-done.16.refs_6_ = bf16[2,80,256]{2,1,0:T(8,128)(2,1)S(1)} collective-permute-done((bf16[2,80,256]{2,1,0:T(8,128)(2,1)S(1)}, bf16[2,80,256]{2,1,0:T(8,128)(2,1)S(1)}, u32[]{:S(2)}, u32[]{:S(2)}) %collective-permute-start.16) | collective-permute-done | bytes 81952 | tf_op jit(solution)/shard_map/ppermute | solution.py:500
  52.1 1.9 %collective-permute-done.13.refs_3_ = bf16[2,80,256]{2,1,0:T(8,128)(2,1)S(1)} collective-permute-done((bf16[2,80,256]{2,1,0:T(8,128)(2,1)S(1)}, bf16[2,80,256]{2,1,0:T(8,128)(2,1)S(1)}, u32[]{:S(2)}, u32[]{:S(2)}) %collective-permute-start.13) | collective-permute-done | bytes 81952 | tf_op jit(solution)/shard_map/ppermute | solution.py:500
  54.0 2.1 %collective-permute-done.12.refs_2_ = bf16[2,80,256]{2,1,0:T(8,128)(2,1)S(1)} collective-permute-done((bf16[2,80,256]{2,1,0:T(8,128)(2,1)S(1)}, bf16[2,80,256]{2,1,0:T(8,128)(2,1)S(1)}, u32[]{:S(2)}, u32[]{:S(2)}) %collective-permute-start.12) | collective-permute-done | bytes 81952 | tf_op jit(solution)/shard_map/ppermute | solution.py:500
  59.9 5.2 %collective-permute-done.19.one_more = bf16[4,80,256]{2,1,0:T(8,128)(2,1)S(1)} collective-permute-done((bf16[4,80,256]{2,1,0:T(8,128)(2,1)S(1)}, bf16[4,80,256]{2,1,0:T(8,128)(2,1)S(1)}, u32[]{:S(2)}, u32[]{:S(2)}) %collective-permute-start.19) | collective-permute-done | bytes 163872 | tf_op jit(solution)/shard_map/ppermute | solution.py:503
  66.3 1.7 %collective-permute-start.22 = (bf16[4,80,256]{2,1,0:T(8,128)(2,1)S(1)}, bf16[4,80,256]{2,1,0:T(8,128)(2,1)S(1)}, u32[]{:S(2)}, u32[]{:S(2)}) collective-permute-start(bf16[4,80,256]{2,1,0:T(8,128)(2,1)S(1)} %get-tuple-element.68.refs_2_), channel_id=1, source_target_pairs={{0,1},{1,0},{2,3},{3,2},{4,5},{5,4},{6,7},{7,6},{8,9},{9,8},{10,11... | collective-permute-start | bytes 491528 | tf_op jit(solution)/shard_map/ppermute | solution.py:503
  68.0 2.8 %collective-permute-done.21.refs_1_ = bf16[4,80,256]{2,1,0:T(8,128)(2,1)S(1)} collective-permute-done((bf16[4,80,256]{2,1,0:T(8,128)(2,1)S(1)}, bf16[4,80,256]{2,1,0:T(8,128)(2,1)S(1)}, u32[]{:S(2)}, u32[]{:S(2)}) %collective-permute-start.21) | collective-permute-done | bytes 163872 | tf_op jit(solution)/shard_map/ppermute | solution.py:503
  72.8 1.6 %collective-permute-done.23.other = bf16[4,80,512]{2,1,0:T(8,128)(2,1)S(1)} collective-permute-done((bf16[4,80,512]{2,1,0:T(8,128)(2,1)S(1)}, bf16[4,80,512]{2,1,0:T(8,128)(2,1)S(1)}, u32[]{:S(2)}, u32[]{:S(2)}) %collective-permute-start.23) | collective-permute-done | bytes 327712 | tf_op jit(solution)/shard_map/ppermute | solution.py:506
  75.4 2.2 %collective-permute-start.24 = (bf16[2,80,256]{2,1,0:T(8,128)(2,1)S(1)}, bf16[2,80,256]{2,1,0:T(8,128)(2,1)S(1)}, u32[]{:S(2)}, u32[]{:S(2)}) collective-permute-start(bf16[2,80,256]{2,1,0:T(8,128)(2,1)S(1)} %get-tuple-element.74), channel_id=1, source_target_pairs={{0,16},{4,20},{8,24},{12,28},{16,0},{20,4},{24,8},{28,12},{1,17},{... | collective-permute-start | bytes 245768 | tf_op jit(solution)/shard_map/ppermute | solution.py:500
  77.6 2.1 %collective-permute-start.25 = (bf16[2,80,256]{2,1,0:T(8,128)(2,1)S(1)}, bf16[2,80,256]{2,1,0:T(8,128)(2,1)S(1)}, u32[]{:S(2)}, u32[]{:S(2)}) collective-permute-start(bf16[2,80,256]{2,1,0:T(8,128)(2,1)S(1)} %get-tuple-element.75), channel_id=1, source_target_pairs={{0,24},{4,28},{8,16},{12,20},{16,8},{20,12},{24,0},{28,4},{1,25},{... | collective-permute-start | bytes 245768 | tf_op jit(solution)/shard_map/ppermute | solution.py:500
  79.7 2.0 %collective-permute-start.27 = (bf16[2,80,256]{2,1,0:T(8,128)(2,1)S(1)}, bf16[2,80,256]{2,1,0:T(8,128)(2,1)S(1)}, u32[]{:S(2)}, u32[]{:S(2)}) collective-permute-start(bf16[2,80,256]{2,1,0:T(8,128)(2,1)S(1)} %get-tuple-element.77), channel_id=1, source_target_pairs={{0,8},{4,12},{8,0},{12,4},{16,24},{20,28},{24,16},{28,20},{1,9},{5... | collective-permute-start | bytes 245768 | tf_op jit(solution)/shard_map/ppermute | solution.py:500
  82.2 3.0 %collective-permute-done.24.refs_1_ = bf16[2,80,256]{2,1,0:T(8,128)(2,1)S(1)} collective-permute-done((bf16[2,80,256]{2,1,0:T(8,128)(2,1)S(1)}, bf16[2,80,256]{2,1,0:T(8,128)(2,1)S(1)}, u32[]{:S(2)}, u32[]{:S(2)}) %collective-permute-start.24) | collective-permute-done | bytes 81952 | tf_op jit(solution)/shard_map/ppermute | solution.py:500
  85.2 2.1 %collective-permute-done.26.refs_3_ = bf16[2,80,256]{2,1,0:T(8,128)(2,1)S(1)} collective-permute-done((bf16[2,80,256]{2,1,0:T(8,128)(2,1)S(1)}, bf16[2,80,256]{2,1,0:T(8,128)(2,1)S(1)}, u32[]{:S(2)}, u32[]{:S(2)}) %collective-permute-start.26) | collective-permute-done | bytes 81952 | tf_op jit(solution)/shard_map/ppermute | solution.py:500
  87.3 1.7 %collective-permute-done.27.refs_4_ = bf16[2,80,256]{2,1,0:T(8,128)(2,1)S(1)} collective-permute-done((bf16[2,80,256]{2,1,0:T(8,128)(2,1)S(1)}, bf16[2,80,256]{2,1,0:T(8,128)(2,1)S(1)}, u32[]{:S(2)}, u32[]{:S(2)}) %collective-permute-start.27) | collective-permute-done | bytes 81952 | tf_op jit(solution)/shard_map/ppermute | solution.py:500
  90.4 1.8 %collective-permute-start.32 = (bf16[2,80,256]{2,1,0:T(8,128)(2,1)S(1)}, bf16[2,80,256]{2,1,0:T(8,128)(2,1)S(1)}, u32[]{:S(2)}, u32[]{:S(2)}) collective-permute-start(bf16[2,80,256]{2,1,0:T(8,128)(2,1)S(1)} %get-tuple-element.81.refs_0_), channel_id=1, source_target_pairs={{0,8},{4,12},{8,0},{12,4},{16,24},{20,28},{24,16},{28,20},{1,9},{5... | collective-permute-start | bytes 245768 | tf_op jit(solution)/shard_map/ppermute | solution.py:500
  92.4 2.1 %collective-permute-start.31 = (bf16[2,80,256]{2,1,0:T(8,128)(2,1)S(1)}, bf16[2,80,256]{2,1,0:T(8,128)(2,1)S(1)}, u32[]{:S(2)}, u32[]{:S(2)}) collective-permute-start(bf16[2,80,256]{2,1,0:T(8,128)(2,1)S(1)} %get-tuple-element.82.refs_1_), channel_id=1, source_target_pairs={{0,24},{4,28},{8,16},{12,20},{16,8},{20,12},{24,0},{28,4},{1,25},{... | collective-permute-start | bytes 245768 | tf_op jit(solution)/shard_map/ppermute | solution.py:500
  95.7 2.6 %collective-permute-done.34.refs_6_ = bf16[2,80,256]{2,1,0:T(8,128)(2,1)S(1)} collective-permute-done((bf16[2,80,256]{2,1,0:T(8,128)(2,1)S(1)}, bf16[2,80,256]{2,1,0:T(8,128)(2,1)S(1)}, u32[]{:S(2)}, u32[]{:S(2)}) %collective-permute-start.34) | collective-permute-done | bytes 81952 | tf_op jit(solution)/shard_map/ppermute | solution.py:500
  99.4 1.6 %collective-permute-done.31.refs_3_ = bf16[2,80,256]{2,1,0:T(8,128)(2,1)S(1)} collective-permute-done((bf16[2,80,256]{2,1,0:T(8,128)(2,1)S(1)}, bf16[2,80,256]{2,1,0:T(8,128)(2,1)S(1)}, u32[]{:S(2)}, u32[]{:S(2)}) %collective-permute-start.31) | collective-permute-done | bytes 81952 | tf_op jit(solution)/shard_map/ppermute | solution.py:500
  101.0 1.7 %collective-permute-done.30.refs_2_ = bf16[2,80,256]{2,1,0:T(8,128)(2,1)S(1)} collective-permute-done((bf16[2,80,256]{2,1,0:T(8,128)(2,1)S(1)}, bf16[2,80,256]{2,1,0:T(8,128)(2,1)S(1)}, u32[]{:S(2)}, u32[]{:S(2)}) %collective-permute-start.30) | collective-permute-done | bytes 81952 | tf_op jit(solution)/shard_map/ppermute | solution.py:500
  105.9 2.3 %collective-permute-start.37 = (bf16[4,80,128]{2,1,0:T(8,128)(2,1)S(1)}, bf16[4,80,128]{2,1,0:T(8,128)(2,1)S(1)}, u32[]{:S(2)}, u32[]{:S(2)}) collective-permute-start(bf16[4,80,128]{2,1,0:T(8,128)(2,1)S(1)} %get-tuple-element.84), channel_id=1, source_target_pairs={{0,3},{1,2},{2,1},{3,0},{4,7},{5,6},{6,5},{7,4},{8,11},{9,10},{10,... | collective-permute-start | bytes 245768 | tf_op jit(solution)/shard_map/ppermute | solution.py:503
  109.5 2.0 %collective-permute-done.37.refs_1_ = bf16[4,80,128]{2,1,0:T(8,128)(2,1)S(1)} collective-permute-done((bf16[4,80,128]{2,1,0:T(8,128)(2,1)S(1)}, bf16[4,80,128]{2,1,0:T(8,128)(2,1)S(1)}, u32[]{:S(2)}, u32[]{:S(2)}) %collective-permute-start.37) | collective-permute-done | bytes 81952 | tf_op jit(solution)/shard_map/ppermute | solution.py:503
  111.5 1.7 %collective-permute-done.38.refs_2_ = bf16[4,80,128]{2,1,0:T(8,128)(2,1)S(1)} collective-permute-done((bf16[4,80,128]{2,1,0:T(8,128)(2,1)S(1)}, bf16[4,80,128]{2,1,0:T(8,128)(2,1)S(1)}, u32[]{:S(2)}, u32[]{:S(2)}) %collective-permute-start.38) | collective-permute-done | bytes 81952 | tf_op jit(solution)/shard_map/ppermute | solution.py:503
  (87 shorter events, 38.9 us)
Async XLA Ops:
  6.5 19.2 %collective-permute-start.5 = (bf16[4,4,128,256]{3,2,1,0:T(8,128)(2,1)}, bf16[4,4,128,256]{3,2,1,0:T(8,128)(2,1)S(1)}, u32[]{:S(2)}, u32[]{:S(2)}) collective-permute-start(bf16[4,4,128,256]{3,2,1,0:T(8,128)(2,1)} %get-tuple-element.55), channel_id=1, source_target_pairs={{0,4},{4,0},{8,12},{12,8},{16,20},{20,16},{24,28},{28,24},{1,5},{5... | collective-permute-start | bytes 3145736 | tf_op jit(solution)/shard_map/ppermute | solution.py:506
  7.0 7.6 %collective-permute-start = (bf16[4,80,256]{2,1,0:T(8,128)(2,1)}, bf16[4,80,256]{2,1,0:T(8,128)(2,1)S(1)}, u32[]{:S(2)}, u32[]{:S(2)}) collective-permute-start(bf16[4,80,256]{2,1,0:T(8,128)(2,1)} %get-tuple-element.47.refs_0_), channel_id=1, source_target_pairs={{0,1},{1,0},{2,3},{3,2},{4,5},{5,4},{6,7},{7,6},{8,9},{9,8},{10,11... | collective-permute-start | bytes 491528 | tf_op jit(solution)/shard_map/ppermute | solution.py:503
  9.6 6.5 %collective-permute-start.1 = (bf16[4,80,256]{2,1,0:T(8,128)(2,1)}, bf16[4,80,256]{2,1,0:T(8,128)(2,1)S(1)}, u32[]{:S(2)}, u32[]{:S(2)}) collective-permute-start(bf16[4,80,256]{2,1,0:T(8,128)(2,1)} %get-tuple-element.48.refs_1_), channel_id=1, source_target_pairs={{0,2},{1,3},{2,0},{3,1},{4,6},{5,7},{6,4},{7,5},{8,10},{9,11},{10,... | collective-permute-start | bytes 491528 | tf_op jit(solution)/shard_map/ppermute | solution.py:503
  16.2 5.5 %collective-permute-start.2 = (bf16[4,80,256]{2,1,0:T(8,128)(2,1)S(1)}, bf16[4,80,256]{2,1,0:T(8,128)(2,1)S(1)}, u32[]{:S(2)}, u32[]{:S(2)}) collective-permute-start(bf16[4,80,256]{2,1,0:T(8,128)(2,1)S(1)} %get-tuple-element.51.refs_0_), channel_id=1, source_target_pairs={{0,2},{1,3},{2,0},{3,1},{4,6},{5,7},{6,4},{7,5},{8,10},{9,11},{10,... | collective-permute-start | bytes 491528 | tf_op jit(solution)/shard_map/ppermute | solution.py:503
  17.7 5.3 %collective-permute-start.3 = (bf16[4,80,256]{2,1,0:T(8,128)(2,1)S(1)}, bf16[4,80,256]{2,1,0:T(8,128)(2,1)S(1)}, u32[]{:S(2)}, u32[]{:S(2)}) collective-permute-start(bf16[4,80,256]{2,1,0:T(8,128)(2,1)S(1)} %get-tuple-element.52.refs_2_), channel_id=1, source_target_pairs={{0,1},{1,0},{2,3},{3,2},{4,5},{5,4},{6,7},{7,6},{8,9},{9,8},{10,11... | collective-permute-start | bytes 491528 | tf_op jit(solution)/shard_map/ppermute | solution.py:503
  26.6 6.8 %collective-permute-start.10 = (bf16[2,80,256]{2,1,0:T(8,128)(2,1)S(1)}, bf16[2,80,256]{2,1,0:T(8,128)(2,1)S(1)}, u32[]{:S(2)}, u32[]{:S(2)}) collective-permute-start(bf16[2,80,256]{2,1,0:T(8,128)(2,1)S(1)} %get-tuple-element.62), channel_id=1, source_target_pairs={{0,8},{4,12},{8,0},{12,4},{16,24},{20,28},{24,16},{28,20},{1,9},{5... | collective-permute-start | bytes 245768 | tf_op jit(solution)/shard_map/ppermute | solution.py:500
  28.3 9.1 %collective-permute-start.6 = (bf16[2,80,256]{2,1,0:T(8,128)(2,1)S(1)}, bf16[2,80,256]{2,1,0:T(8,128)(2,1)S(1)}, u32[]{:S(2)}, u32[]{:S(2)}) collective-permute-start(bf16[2,80,256]{2,1,0:T(8,128)(2,1)S(1)} %get-tuple-element.57), channel_id=1, source_target_pairs={{0,16},{4,20},{8,24},{12,28},{16,0},{20,4},{24,8},{28,12},{1,17},{... | collective-permute-start | bytes 245768 | tf_op jit(solution)/shard_map/ppermute | solution.py:500
  31.3 7.2 %collective-permute-start.7 = (bf16[2,80,256]{2,1,0:T(8,128)(2,1)S(1)}, bf16[2,80,256]{2,1,0:T(8,128)(2,1)S(1)}, u32[]{:S(2)}, u32[]{:S(2)}) collective-permute-start(bf16[2,80,256]{2,1,0:T(8,128)(2,1)S(1)} %get-tuple-element.58), channel_id=1, source_target_pairs={{0,24},{4,28},{8,16},{12,20},{16,8},{20,12},{24,0},{28,4},{1,25},{... | collective-permute-start | bytes 245768 | tf_op jit(solution)/shard_map/ppermute | solution.py:500
  31.3 7.2 %collective-permute-start.8 = (bf16[2,80,256]{2,1,0:T(8,128)(2,1)S(1)}, bf16[2,80,256]{2,1,0:T(8,128)(2,1)S(1)}, u32[]{:S(2)}, u32[]{:S(2)}) collective-permute-start(bf16[2,80,256]{2,1,0:T(8,128)(2,1)S(1)} %get-tuple-element.59), channel_id=1, source_target_pairs={{0,8},{4,12},{8,0},{12,4},{16,24},{20,28},{24,16},{28,20},{1,9},{5... | collective-permute-start | bytes 245768 | tf_op jit(solution)/shard_map/ppermute | solution.py:500
  31.9 8.0 %collective-permute-start.9 = (bf16[2,80,256]{2,1,0:T(8,128)(2,1)S(1)}, bf16[2,80,256]{2,1,0:T(8,128)(2,1)S(1)}, u32[]{:S(2)}, u32[]{:S(2)}) collective-permute-start(bf16[2,80,256]{2,1,0:T(8,128)(2,1)S(1)} %get-tuple-element.60), channel_id=1, source_target_pairs={{0,8},{4,12},{8,0},{12,4},{16,24},{20,28},{24,16},{28,20},{1,9},{5... | collective-permute-start | bytes 245768 | tf_op jit(solution)/shard_map/ppermute | solution.py:500
  33.5 9.1 %collective-permute-start.11 = (bf16[2,80,256]{2,1,0:T(8,128)(2,1)S(1)}, bf16[2,80,256]{2,1,0:T(8,128)(2,1)S(1)}, u32[]{:S(2)}, u32[]{:S(2)}) collective-permute-start(bf16[2,80,256]{2,1,0:T(8,128)(2,1)S(1)} %shard_map.109), channel_id=1, source_target_pairs={{0,16},{4,20},{8,24},{12,28},{16,0},{20,4},{24,8},{28,12},{1,17},{... | collective-permute-start | bytes 245768 | tf_op jit(solution)/shard_map/ppermute | solution.py:500
  42.8 8.2 %collective-permute-start.16 = (bf16[2,80,256]{2,1,0:T(8,128)(2,1)S(1)}, bf16[2,80,256]{2,1,0:T(8,128)(2,1)S(1)}, u32[]{:S(2)}, u32[]{:S(2)}) collective-permute-start(bf16[2,80,256]{2,1,0:T(8,128)(2,1)S(1)} %get-tuple-element.63.refs_0_), channel_id=1, source_target_pairs={{0,16},{4,20},{8,24},{12,28},{16,0},{20,4},{24,8},{28,12},{1,17},{... | collective-permute-start | bytes 245768 | tf_op jit(solution)/shard_map/ppermute | solution.py:500
  43.9 7.1 %collective-permute-start.14 = (bf16[2,80,256]{2,1,0:T(8,128)(2,1)S(1)}, bf16[2,80,256]{2,1,0:T(8,128)(2,1)S(1)}, u32[]{:S(2)}, u32[]{:S(2)}) collective-permute-start(bf16[2,80,256]{2,1,0:T(8,128)(2,1)S(1)} %get-tuple-element.63.refs_0_), channel_id=1, source_target_pairs={{0,8},{4,12},{8,0},{12,4},{16,24},{20,28},{24,16},{28,20},{1,9},{5... | collective-permute-start | bytes 245768 | tf_op jit(solution)/shard_map/ppermute | solution.py:500
  45.8 6.2 %collective-permute-start.15 = (bf16[2,80,256]{2,1,0:T(8,128)(2,1)S(1)}, bf16[2,80,256]{2,1,0:T(8,128)(2,1)S(1)}, u32[]{:S(2)}, u32[]{:S(2)}) collective-permute-start(bf16[2,80,256]{2,1,0:T(8,128)(2,1)S(1)} %get-tuple-element.64.refs_1_), channel_id=1, source_target_pairs={{0,8},{4,12},{8,0},{12,4},{16,24},{20,28},{24,16},{28,20},{1,9},{5... | collective-permute-start | bytes 245768 | tf_op jit(solution)/shard_map/ppermute | solution.py:500
  45.9 8.1 %collective-permute-start.13 = (bf16[2,80,256]{2,1,0:T(8,128)(2,1)S(1)}, bf16[2,80,256]{2,1,0:T(8,128)(2,1)S(1)}, u32[]{:S(2)}, u32[]{:S(2)}) collective-permute-start(bf16[2,80,256]{2,1,0:T(8,128)(2,1)S(1)} %get-tuple-element.64.refs_1_), channel_id=1, source_target_pairs={{0,24},{4,28},{8,16},{12,20},{16,8},{20,12},{24,0},{28,4},{1,25},{... | collective-permute-start | bytes 245768 | tf_op jit(solution)/shard_map/ppermute | solution.py:500
  47.6 8.5 %collective-permute-start.12 = (bf16[2,80,256]{2,1,0:T(8,128)(2,1)S(1)}, bf16[2,80,256]{2,1,0:T(8,128)(2,1)S(1)}, u32[]{:S(2)}, u32[]{:S(2)}) collective-permute-start(bf16[2,80,256]{2,1,0:T(8,128)(2,1)S(1)} %get-tuple-element.64.refs_1_), channel_id=1, source_target_pairs={{0,16},{4,20},{8,24},{12,28},{16,0},{20,4},{24,8},{28,12},{1,17},{... | collective-permute-start | bytes 245768 | tf_op jit(solution)/shard_map/ppermute | solution.py:500
  50.9 5.5 %collective-permute-start.17 = (bf16[2,80,256]{2,1,0:T(8,128)(2,1)S(1)}, bf16[2,80,256]{2,1,0:T(8,128)(2,1)S(1)}, u32[]{:S(2)}, u32[]{:S(2)}) collective-permute-start(bf16[2,80,256]{2,1,0:T(8,128)(2,1)S(1)} %collective-permute-done.16.refs_6_), channel_id=1, source_target_pairs={{0,8},{4,12},{8,0},{12,4},{16,24},{20,28},{24,16},{28,20},{1,9},{5... | collective-permute-start | bytes 245768 | tf_op jit(solution)/shard_map/ppermute | solution.py:500
  58.8 6.3 %collective-permute-start.19 = (bf16[4,80,256]{2,1,0:T(8,128)(2,1)S(1)}, bf16[4,80,256]{2,1,0:T(8,128)(2,1)S(1)}, u32[]{:S(2)}, u32[]{:S(2)}) collective-permute-start(bf16[4,80,256]{2,1,0:T(8,128)(2,1)S(1)} %get-tuple-element.65.one), channel_id=1, source_target_pairs={{0,1},{1,0},{2,3},{3,2},{4,5},{5,4},{6,7},{7,6},{8,9},{9,8},{10,11... | collective-permute-start | bytes 491528 | tf_op jit(solution)/shard_map/ppermute | solution.py:503
  59.4 6.0 %collective-permute-start.20 = (bf16[4,80,256]{2,1,0:T(8,128)(2,1)S(1)}, bf16[4,80,256]{2,1,0:T(8,128)(2,1)S(1)}, u32[]{:S(2)}, u32[]{:S(2)}) collective-permute-start(bf16[4,80,256]{2,1,0:T(8,128)(2,1)S(1)} %get-tuple-element.66.two), channel_id=1, source_target_pairs={{0,2},{1,3},{2,0},{3,1},{4,6},{5,7},{6,4},{7,5},{8,10},{9,11},{10,... | collective-permute-start | bytes 491528 | tf_op jit(solution)/shard_map/ppermute | solution.py:503
  65.4 5.4 %collective-permute-start.21 = (bf16[4,80,256]{2,1,0:T(8,128)(2,1)S(1)}, bf16[4,80,256]{2,1,0:T(8,128)(2,1)S(1)}, u32[]{:S(2)}, u32[]{:S(2)}) collective-permute-start(bf16[4,80,256]{2,1,0:T(8,128)(2,1)S(1)} %get-tuple-element.67.refs_0_), channel_id=1, source_target_pairs={{0,2},{1,3},{2,0},{3,1},{4,6},{5,7},{6,4},{7,5},{8,10},{9,11},{10,... | collective-permute-start | bytes 491528 | tf_op jit(solution)/shard_map/ppermute | solution.py:503
  75.3 6.5 %collective-permute-start.28 = (bf16[2,80,256]{2,1,0:T(8,128)(2,1)S(1)}, bf16[2,80,256]{2,1,0:T(8,128)(2,1)S(1)}, u32[]{:S(2)}, u32[]{:S(2)}) collective-permute-start(bf16[2,80,256]{2,1,0:T(8,128)(2,1)S(1)} %get-tuple-element.79), channel_id=1, source_target_pairs={{0,8},{4,12},{8,0},{12,4},{16,24},{20,28},{24,16},{28,20},{1,9},{5... | collective-permute-start | bytes 245768 | tf_op jit(solution)/shard_map/ppermute | solution.py:500
  75.4 9.8 %collective-permute-start.24 = (bf16[2,80,256]{2,1,0:T(8,128)(2,1)S(1)}, bf16[2,80,256]{2,1,0:T(8,128)(2,1)S(1)}, u32[]{:S(2)}, u32[]{:S(2)}) collective-permute-start(bf16[2,80,256]{2,1,0:T(8,128)(2,1)S(1)} %get-tuple-element.74), channel_id=1, source_target_pairs={{0,16},{4,20},{8,24},{12,28},{16,0},{20,4},{24,8},{28,12},{1,17},{... | collective-permute-start | bytes 245768 | tf_op jit(solution)/shard_map/ppermute | solution.py:500
  77.6 7.6 %collective-permute-start.25 = (bf16[2,80,256]{2,1,0:T(8,128)(2,1)S(1)}, bf16[2,80,256]{2,1,0:T(8,128)(2,1)S(1)}, u32[]{:S(2)}, u32[]{:S(2)}) collective-permute-start(bf16[2,80,256]{2,1,0:T(8,128)(2,1)S(1)} %get-tuple-element.75), channel_id=1, source_target_pairs={{0,24},{4,28},{8,16},{12,20},{16,8},{20,12},{24,0},{28,4},{1,25},{... | collective-permute-start | bytes 245768 | tf_op jit(solution)/shard_map/ppermute | solution.py:500
  79.7 7.5 %collective-permute-start.26 = (bf16[2,80,256]{2,1,0:T(8,128)(2,1)S(1)}, bf16[2,80,256]{2,1,0:T(8,128)(2,1)S(1)}, u32[]{:S(2)}, u32[]{:S(2)}) collective-permute-start(bf16[2,80,256]{2,1,0:T(8,128)(2,1)S(1)} %get-tuple-element.76), channel_id=1, source_target_pairs={{0,8},{4,12},{8,0},{12,4},{16,24},{20,28},{24,16},{28,20},{1,9},{5... | collective-permute-start | bytes 245768 | tf_op jit(solution)/shard_map/ppermute | solution.py:500
  79.7 9.2 %collective-permute-start.27 = (bf16[2,80,256]{2,1,0:T(8,128)(2,1)S(1)}, bf16[2,80,256]{2,1,0:T(8,128)(2,1)S(1)}, u32[]{:S(2)}, u32[]{:S(2)}) collective-permute-start(bf16[2,80,256]{2,1,0:T(8,128)(2,1)S(1)} %get-tuple-element.77), channel_id=1, source_target_pairs={{0,8},{4,12},{8,0},{12,4},{16,24},{20,28},{24,16},{28,20},{1,9},{5... | collective-permute-start | bytes 245768 | tf_op jit(solution)/shard_map/ppermute | solution.py:500
  81.9 7.8 %collective-permute-start.29 = (bf16[2,80,256]{2,1,0:T(8,128)(2,1)S(1)}, bf16[2,80,256]{2,1,0:T(8,128)(2,1)S(1)}, u32[]{:S(2)}, u32[]{:S(2)}) collective-permute-start(bf16[2,80,256]{2,1,0:T(8,128)(2,1)S(1)} %shard_map.118), channel_id=1, source_target_pairs={{0,16},{4,20},{8,24},{12,28},{16,0},{20,4},{24,8},{28,12},{1,17},{... | collective-permute-start | bytes 245768 | tf_op jit(solution)/shard_map/ppermute | solution.py:500
  89.9 8.4 %collective-permute-start.34 = (bf16[2,80,256]{2,1,0:T(8,128)(2,1)S(1)}, bf16[2,80,256]{2,1,0:T(8,128)(2,1)S(1)}, u32[]{:S(2)}, u32[]{:S(2)}) collective-permute-start(bf16[2,80,256]{2,1,0:T(8,128)(2,1)S(1)} %get-tuple-element.81.refs_0_), channel_id=1, source_target_pairs={{0,16},{4,20},{8,24},{12,28},{16,0},{20,4},{24,8},{28,12},{1,17},{... | collective-permute-start | bytes 245768 | tf_op jit(solution)/shard_map/ppermute | solution.py:500
  90.4 7.9 %collective-permute-start.32 = (bf16[2,80,256]{2,1,0:T(8,128)(2,1)S(1)}, bf16[2,80,256]{2,1,0:T(8,128)(2,1)S(1)}, u32[]{:S(2)}, u32[]{:S(2)}) collective-permute-start(bf16[2,80,256]{2,1,0:T(8,128)(2,1)S(1)} %get-tuple-element.81.refs_0_), channel_id=1, source_target_pairs={{0,8},{4,12},{8,0},{12,4},{16,24},{20,28},{24,16},{28,20},{1,9},{5... | collective-permute-start | bytes 245768 | tf_op jit(solution)/shard_map/ppermute | solution.py:500
  92.2 7.1 %collective-permute-start.33 = (bf16[2,80,256]{2,1,0:T(8,128)(2,1)S(1)}, bf16[2,80,256]{2,1,0:T(8,128)(2,1)S(1)}, u32[]{:S(2)}, u32[]{:S(2)}) collective-permute-start(bf16[2,80,256]{2,1,0:T(8,128)(2,1)S(1)} %get-tuple-element.82.refs_1_), channel_id=1, source_target_pairs={{0,8},{4,12},{8,0},{12,4},{16,24},{20,28},{24,16},{28,20},{1,9},{5... | collective-permute-start | bytes 245768 | tf_op jit(solution)/shard_map/ppermute | solution.py:500
  92.4 8.6 %collective-permute-start.31 = (bf16[2,80,256]{2,1,0:T(8,128)(2,1)S(1)}, bf16[2,80,256]{2,1,0:T(8,128)(2,1)S(1)}, u32[]{:S(2)}, u32[]{:S(2)}) collective-permute-start(bf16[2,80,256]{2,1,0:T(8,128)(2,1)S(1)} %get-tuple-element.82.refs_1_), channel_id=1, source_target_pairs={{0,24},{4,28},{8,16},{12,20},{16,8},{20,12},{24,0},{28,4},{1,25},{... | collective-permute-start | bytes 245768 | tf_op jit(solution)/shard_map/ppermute | solution.py:500
  94.6 8.2 %collective-permute-start.30 = (bf16[2,80,256]{2,1,0:T(8,128)(2,1)S(1)}, bf16[2,80,256]{2,1,0:T(8,128)(2,1)S(1)}, u32[]{:S(2)}, u32[]{:S(2)}) collective-permute-start(bf16[2,80,256]{2,1,0:T(8,128)(2,1)S(1)} %get-tuple-element.82.refs_1_), channel_id=1, source_target_pairs={{0,16},{4,20},{8,24},{12,28},{16,0},{20,4},{24,8},{28,12},{1,17},{... | collective-permute-start | bytes 245768 | tf_op jit(solution)/shard_map/ppermute | solution.py:500
  105.9 5.5 %collective-permute-start.37 = (bf16[4,80,128]{2,1,0:T(8,128)(2,1)S(1)}, bf16[4,80,128]{2,1,0:T(8,128)(2,1)S(1)}, u32[]{:S(2)}, u32[]{:S(2)}) collective-permute-start(bf16[4,80,128]{2,1,0:T(8,128)(2,1)S(1)} %get-tuple-element.84), channel_id=1, source_target_pairs={{0,3},{1,2},{2,1},{3,0},{4,7},{5,6},{6,5},{7,4},{8,11},{9,10},{10,... | collective-permute-start | bytes 245768 | tf_op jit(solution)/shard_map/ppermute | solution.py:503
  (14 other events, 89.4 us)

commit v10 on v9

v10 whole, which is shorter than its diff:
```python
import functools

import jax
import jax.numpy as jnp
from jax import lax
from jax.experimental import pallas as pl
from jax.experimental.pallas import tpu as pltpu
from jax.sharding import PartitionSpec as P

ITERS = 2
LANES = 128
PIECES = 3
PRIME = 32749
VMEM = pl.BlockSpec(memory_space=pltpu.VMEM)
HBM = pl.BlockSpec(memory_space=pltpu.HBM)
F32 = jnp.float32
BF16 = jnp.bfloat16
NT = (((1,), (1,)), ((), ()))


def call(kernel, outs, scratch, flops, *args, space=VMEM, limit=24):
    nbytes = sum(a.size * a.dtype.itemsize for a in (*args, *outs))
    return pl.pallas_call(
        kernel,
        out_shape=outs,
        in_specs=[space] * len(args),
        out_specs=[VMEM] * len(outs),
        scratch_shapes=scratch,
        compiler_params=pltpu.CompilerParams(vmem_limit_bytes=limit * 1024 * 1024),
        cost_estimate=pl.CostEstimate(flops=flops, bytes_accessed=nbytes, transcendentals=0),
    )(*args)


def struct(shape, dtype):
    return jax.ShapeDtypeStruct(shape, dtype)


def place():
    slab = lax.axis_index("slab")
    return slab // 2, slab % 2, lax.axis_index("obs")


def add(parts):
    value = parts[0].astype(F32)
    for part in parts[1:]:
        value = value + part.astype(F32)
    return value


def dot(matrix, x):
    high = x.astype(BF16)
    rest = (x - high.astype(F32)).astype(BF16)
    x = jnp.concatenate([high, rest, high], axis=0)
    return jnp.dot(matrix, x, preferred_element_type=F32)


def total(x):
    return jnp.sum(jnp.sum(x, axis=0, keepdims=True), axis=1, keepdims=True)


def with_scalars(body, values):
    count = body.shape[0]
    tail = body[count - 16 :]
    sub = lax.broadcasted_iota(jnp.int32, tail.shape, 0) - (16 - len(values))
    lanes = lax.broadcasted_iota(jnp.int32, tail.shape, 1)
    line = jnp.zeros(tail.shape, F32)
    for m, member in enumerate(values):
        for q, value in enumerate(member):
            rest = value
            for piece in range(PIECES):
                part = rest.astype(BF16).astype(F32)
                rest = rest - part
                line = jnp.where((sub == m) & (lanes == q * PIECES + piece), part, line)
    return jnp.concatenate([body[: count - 16], jnp.where(sub >= 0, line, tail)], axis=0)


def read_scalars(refs, members, count):
    tail = add([ref[ref.shape[0] - 16 :, 0:LANES] for ref in refs])
    sub = lax.broadcasted_iota(jnp.int32, tail.shape, 0) - (16 - members)
    lanes = lax.broadcasted_iota(jnp.int32, tail.shape, 1)
    return [
        [
            total(
                jnp.where(
                    (sub == m) & (lanes >= q * PIECES) & (lanes < (q + 1) * PIECES), tail, 0.0
                )
            )
            for q in range(count)
        ]
        for m in range(members)
    ]


def by_member(values, shape, lev):
    rows = lax.broadcasted_iota(jnp.int32, shape, 0)
    out = jnp.zeros(shape, F32)
    for m, value in enumerate(values):
        out = jnp.where((rows >= m * lev) & (rows < (m + 1) * lev), value, out)
    return out


def member_sums(x, members, lev):
    lines = jnp.sum(x, axis=1, keepdims=True)
    rows = lax.broadcasted_iota(jnp.int32, lines.shape, 0)
    return [
        jnp.sum(
            jnp.where((rows >= m * lev) & (rows < (m + 1) * lev), lines, 0.0),
            axis=0,
            keepdims=True,
        )
        for m in range(members)
    ]


def remainder(x, factor):
    return x - (x.astype(F32) * factor).astype(jnp.int32) * PRIME


def start_kernel(
    dims, seeds_in, ids_in, cols_in, count_in, sd_in, innov_in, prec_in, h, own, partner, *rest
):
    chips, halves = dims
    outs = rest[:-12]
    seeds, ids, cols, count, sd, innov, prec, hashed, scratch, acc, sems, h_sems = rest[-12:]
    z, core, obs = place()
    blocks, lev, profiles = innov.shape
    colblocks, width = own.shape[1], own.shape[3]
    members, levp = hashed.shape[1], hashed.shape[2]
    rows = acc.shape[0]

    pairs = [(seeds_in, seeds), (ids_in, ids), (cols_in, cols), (count_in, count), (sd_in, sd)]
    small = [pltpu.make_async_copy(x, y, sems.at[i]) for i, (x, y) in enumerate(pairs)]
    for copy in small:
        copy.start()
    large = []
    for b in range(blocks):
        at = len(pairs) + 2 * b
        large.append(pltpu.make_async_copy(innov_in.at[:, b, :], innov.at[b], sems.at[at]))
        large.append(pltpu.make_async_copy(prec_in.at[:, b, :], prec.at[b], sems.at[at + 1]))
    for copy in large:
        copy.start()
    own[...] = jnp.zeros_like(own)
    partner[...] = jnp.zeros_like(partner)
    scratch[...] = jnp.zeros_like(scratch)
    for copy in small:
        copy.wait()

    def tile_copy(n, half, target):
        lanes = pl.ds(half * width, width)
        return pltpu.make_async_copy(h.at[n, :, lanes], target, h_sems.at[n * halves + half])

    def put(n, carry):
        for half in range(halves):
            piece, k = ids[0, 0, n] * halves + half, cols[0, 0, n]

            @pl.when(piece % 2 == core)
            def _():
                tile_copy(n, half, own.at[piece // 2, k]).start()

            @pl.when(piece % 2 != core)
            def _():
                tile_copy(n, half, partner.at[piece // 2, k]).start()

        return carry

    lax.fori_loop(0, count[0, 0], put, 0)

    starts = [lax.rem(seeds[m], PRIME) - PRIME for m in range(members)]
    order = [(source, zz) for source in range(2) for zz in range(chips)]
    shape = (levp, width)
    spot = lax.broadcasted_iota(jnp.int32, shape, 0) * profiles
    spot = spot + lax.broadcasted_iota(jnp.int32, shape, 1)
    low = (1.0 - 2.0**-21) / PRIME

    def piece_at(at):
        source, zz = order[at]
        return 2 * zz + (core if source == 0 else 1 - core)

    def draw(at):
        piece = piece_at(at)
        first = (obs * blocks + piece // halves) * (lev * profiles) + (piece % halves) * width
        base = remainder(7919 * remainder(spot + first, 1.0 / PRIME), 1.0 / PRIME)
        for m in range(members):
            k0 = base + starts[m]
            k1 = remainder(k0 * k0 + 12345, 1.0 / PRIME)
            k2 = remainder(k1 * k1 + 2719, low)
            k2 = jnp.where(k2 >= PRIME, k2 - PRIME, k2)
            hashed[at, m] = k2.astype(F32)

    def adjoint(at):
        source, zz = order[at]
        piece = piece_at(at)
        b = piece // halves
        if halves == 1:
            p, d = prec[b], innov[b]
        else:
            lanes = pl.ds(pl.multiple_of((piece % halves) * width, LANES), width)
            p, d = prec[b, :, lanes], innov[b, :, lanes]
        gain = 3.4 * p * lax.rsqrt(p)
        offset = p * d - 0.5 * gain
        gain = gain * (1.0 / PRIME)
        for m in range(members):
            w = offset + gain * hashed[at, m, 0:lev, :]
            scratch[at % 2, m * lev : (m + 1) * lev, :] = w
        w = scratch[at % 2].astype(BF16)
        tiles = (own if source == 0 else partner)[zz].reshape(colblocks * LANES, width)
        part = lax.dot_general(w, tiles, NT, preferred_element_type=F32)
        if at == 0:
            acc[...] = part
        else:
            acc[...] += part

    early = len(order) // 2
    for at in range(early):
        draw(at)
    for copy in large:
        copy.wait()

    def arrive(n, carry):
        for half in range(halves):
            tile_copy(n, half, own.at[0, 0]).wait()
        return carry

    lax.fori_loop(0, count[0, 0], arrive, 0)

    for at in range(len(order)):
        if at + early < len(order):
            draw(at + early)
        adjoint(at)

    line = jnp.concatenate([sd[...]] * colblocks, axis=1)
    put_halves(outs, with_columns(acc[...], line, obs, members))


def put_halves(outs, value):
    half = value.shape[1] // 2
    outs[0][...] = value[:, :half].astype(BF16)
    outs[1][...] = value[:, half:].astype(BF16)


def with_columns(body, line, obs, members):
    tail = body[body.shape[0] - 16 :]
    sub = lax.broadcasted_iota(jnp.int32, tail.shape, 0)
    mine = lax.broadcasted_iota(jnp.int32, tail.shape, 1) // LANES == obs
    rest = line
    for piece in range(PIECES):
        part = rest.astype(BF16).astype(F32)
        rest = rest - part
        tail = jnp.where((sub == 16 - PIECES + piece) & mine, part, tail)
    return jnp.concatenate([body[: body.shape[0] - 16], tail], axis=0)


def read_columns(body):
    tail = body[body.shape[0] - 16 :]
    sub = lax.broadcasted_iota(jnp.int32, tail.shape, 0)
    return jnp.sum(jnp.where(sub >= 16 - PIECES, tail, 0.0), axis=0, keepdims=True)


def precision_kernel(halves, members, prec, out):
    z, core, unused = place()
    piece = 2 * z + core
    lev, blocks, unused = prec.shape
    width = out.shape[1]
    block = lax.broadcasted_iota(jnp.int32, (lev, blocks, width), 1)
    if halves == 1:
        mine = prec[...]
    else:
        mine = prec[:, :, pl.ds(pl.multiple_of((piece % halves) * width, LANES), width)]
    out[...] = jnp.zeros_like(out)
    mine = jnp.sum(jnp.where(block == piece // halves, mine, 0.0), axis=1)
    for m in range(members):
        out[m * lev : (m + 1) * lev, :] = mine


def joined(pieces):
    one, one_more, two, two_more = [x[...] for x in pieces]
    return jnp.concatenate([add([one, one_more]), add([two, two_more])], axis=1)


def unpack(spread, value):
    count = value.shape[0]
    spread[0:count, :] = value
    spread[count:, :] = jnp.zeros((spread.shape[0] - count, value.shape[1]), F32)


def first_kernel(lev, *refs):
    vert, vert_t, sd_out, residual, moved, spread, packed = refs[4:]
    members, levp, unused = residual.shape
    t = joined(refs[:4])
    sd = read_columns(t)
    sd_out[...] = sd
    unpack(spread, t)
    scalars = []
    for m in range(members):
        at = slice(m * lev, m * lev + levp)
        r = dot(vert_t[...], sd * spread[at, :])
        residual[m] = r
        packed[at, :] = sd * dot(vert[...], r)
        scalars.append([total(r * r)])
    moved[...] = with_scalars(packed[0 : moved.shape[0], :], scalars).astype(BF16)


def add_kernel(members, scalars, *refs):
    parts, out = refs[:-1], refs[-1]
    value = add([x[...] for x in parts])
    if scalars:
        value = with_scalars(value, read_scalars(parts, members, scalars))
    out[...] = value.astype(BF16)


def add_halves_kernel(members, scalars, one, one_more, two, two_more, one_out, two_out):
    add_kernel(members, scalars, one, one_more, one_out)
    add_kernel(members, 0, two, two_more, two_out)


def stage_kernel(*refs):
    sems = refs[-1]
    count = len(refs) // 2
    copies = [
        pltpu.make_async_copy(refs[i], refs[count + i], sems.at[i]) for i in range(count)
    ]
    for copy in copies:
        copy.start()
    for copy in copies:
        copy.wait()


def forward_kernel(sends, members, mine, other, own, partner, *outs):
    z, core, obs = place()
    rows, lanes = mine.shape
    width = own.shape[3]
    scalars = read_scalars([mine, other], members, 2)
    for out, (chip, first, count) in zip(outs, sends):
        zz = z ^ chip
        y = [
            jnp.dot(
                x[first : first + count, :],
                tiles[zz].reshape(lanes, width),
                preferred_element_type=F32,
            )
            for x, tiles in ((mine, own), (other, partner))
        ]
        y = y[0] + y[1]
        if first + count == rows:
            y = with_scalars(y, scalars)
        out[...] = y.astype(out.dtype)


def weigh_kernel(later, last, members, lev, spans, *refs):
    ys, refs = refs[: len(spans)], refs[len(spans) :]
    prec, old_image, old = refs[0], *(refs[1:3] if later else (None, None))
    state, *outs = refs[3 if later else 1 :]
    if not last:
        *outs, image = outs
    rows = prec.shape[0]
    cuts = sorted({first for first, count in spans}) + [rows]
    parts = []
    for low, high in zip(cuts, cuts[1:]):
        held = [
            ref[low - first : high - first, :]
            for ref, (first, count) in zip(ys, spans)
            if first <= low < first + count
        ]
        parts.append(add(held))
    y = parts[0] if len(parts) == 1 else jnp.concatenate(parts, axis=0)
    ends = [ref for ref, (first, count) in zip(ys, spans) if first + count == rows]
    sub = lax.broadcasted_iota(jnp.int32, (8, LANES), 0)
    betas = []
    for m, (norm, cross) in enumerate(read_scalars(ends, members, 2)):
        if later:
            old_norm, old_square = old[m, 0:1, 0:1], old[m, 1:2, 0:1]
            beta = norm / old_norm
            square = norm + 2.0 * beta * cross + beta * beta * old_square
        else:
            beta = jnp.zeros_like(norm)
            square = norm
        betas.append(beta)
        state[m] = jnp.where(sub == 0, norm, jnp.where(sub == 1, square, beta))
    if later:
        y = y + by_member(betas, (rows, 1), lev) * old_image[...]
    if not last:
        image[...] = y
    scaled = prec[...] * y
    energies = [[x] for x in member_sums(scaled * y, members, lev)]
    weighted = with_scalars(scaled, energies).astype(BF16)
    first = 0
    outs[0][...] = weighted
    for out in outs[1:]:
        out[...] = weighted[first : first + out.shape[0]]
        first += out.shape[0]


def adjoint_kernel(plan, members, *refs):
    z, core, obs = place()
    ws, tiles, out = refs[: len(plan)], refs[len(plan)], refs[len(plan) + 1]
    rows, lanes = out.shape
    width = ws[0].shape[1]
    acc = None
    for i in range(tiles.shape[0]):
        w = [ref[...] for ref, (chip, *span) in zip(ws, plan) if chip == i]
        w = w[0] if len(w) == 1 else jnp.concatenate(w, axis=0)
        part = lax.dot_general(
            w, tiles[z ^ i].reshape(lanes, width), NT, preferred_element_type=F32
        )
        acc = part if i == 0 else acc + part
    ends = [ref for ref, (chip, first, count) in zip(ws, plan) if first + count == rows]
    out[...] = with_scalars(acc, read_scalars(ends, members, 1)).astype(out.dtype)


def combine_kernel(members, mine, theirs, *outs):
    value = mine[...] + theirs[...].astype(F32)
    put_halves(outs, with_scalars(value, read_scalars([mine, theirs], members, 1)))


def combine_columns_kernel(members, mine, theirs, *outs):
    obs = lax.axis_index("obs")
    energies = read_scalars([mine, theirs], members, 1)
    for i, out in enumerate(outs):
        lane = pl.ds(pl.multiple_of((obs ^ i) * LANES, LANES), LANES)
        value = mine[:, lane] + theirs[:, lane].astype(F32)
        out[...] = with_scalars(value, energies).astype(BF16)


def update_kernel(later, lev, *refs):
    pieces, refs = refs[:4], refs[4:]
    sd, vert, vert_t, state, residual = refs[:5]
    spread, packed = refs[-2:]
    if later:
        old_direction, old_solution, residual_out, solution_out, moved, direction_out = refs[5:-2]
    else:
        residual_out, solution_out, moved = refs[5:-2]
    members, levp, unused = residual.shape
    obs = lax.axis_index("obs")
    mine = pl.ds(pl.multiple_of(obs * LANES, LANES), LANES)
    unpack(spread, joined(pieces))
    energies = read_scalars(pieces[:2], members, 1)
    scalars = []
    for m in range(members):
        at = slice(m * lev, m * lev + levp)
        norm, square, beta = state[m, 0:1, 0:1], state[m, 1:2, 0:1], state[m, 2:3, 0:1]
        alpha = norm / (square + energies[m][0])
        r = residual[m]
        if later:
            d = r + beta * old_direction[m]
            direction_out[m] = d
            step = direction_out[m, :, mine]
            solution_out[m] = old_solution[m] + alpha * step
        else:
            d = r
            solution_out[m] = alpha * residual[m, :, mine]
        r = r - alpha * (d + dot(vert_t[...], sd[...] * spread[at, :]))
        residual_out[m] = r
        packed[at, :] = sd[...] * dot(vert[...], r)
        scalars.append([total(r * r), total(r * d)])
    moved[...] = with_scalars(packed[0 : moved.shape[0], :], scalars).astype(BF16)


def last_kernel(parts, later, lev, *refs):
    pieces, refs = refs[:parts], refs[parts:]
    sd, vert, vert_t, state, residual = refs[:5]
    increment_out, residual_out, spread = refs[-3:]
    members, levp, unused = residual.shape
    obs = lax.axis_index("obs")
    mine = pl.ds(pl.multiple_of(obs * LANES, LANES), LANES)
    unpack(spread, add([x[...] for x in pieces]))
    energies = read_scalars(pieces, members, 1)
    for m in range(members):
        t = spread[m * lev : m * lev + levp, :]
        norm, square, beta = state[m, 0:1, 0:1], state[m, 1:2, 0:1], state[m, 2:3, 0:1]
        alpha = norm / (square + energies[m][0])
        d = r = residual[m, :, mine]
        if later:
            old_direction, old_solution = refs[5:7]
            d = r + beta * old_direction[m, :, mine]
        solution = alpha * d
        if later:
            solution = old_solution[m] + solution
        r = r - alpha * (d + dot(vert_t[...], sd[...] * t))
        increment = sd[...] * dot(vert[...], solution)
        increment_out[:, m, :] = increment[0:lev]
        residual_out[:, m, :] = r[0:lev]


def per_device(
    n_slab,
    n_obs,
    innovation,
    obs_precision,
    seeds,
    col_sd,
    vert_factor,
    h_values,
    block_obs,
    block_col,
    entry_count,
):
    blocks, lev, profiles = innovation.shape
    members = seeds.shape[0]
    chips = n_slab // 2
    halves = n_slab // blocks
    width = profiles // halves
    colblocks = n_obs
    assert halves * blocks == n_slab and width % LANES == 0 and col_sd.shape[0] == 1
    assert chips & (chips - 1) == 0 and n_obs & (n_obs - 1) == 0
    levp = (lev + 1 + 15) // 16 * 16
    assert members <= 16 and members >= PIECES
    rows = (members * (lev + 1) + 15) // 16 * 16
    lanes = colblocks * LANES
    slab_field = (members, levp, lanes)
    slab_rows = (rows, lanes)
    half_rows = [struct((rows, lanes // 2), BF16)] * 2
    wide = rows + levp - lev + 7
    spread = pltpu.VMEM((wide // 8 * 8, lanes), F32)
    some = rows // 32 * 16
    some, rest = rows - some, some
    via = chips == 4
    if via:
        one, two = (0, some), (some, rest)
        plan = [(0, 0, rows), (1, 0, rows), (2, *one), (2, *two), (3, *one), (3, *two)]
        sends = [(3, *one), (2, *two), (3, *two), (1, *one), (1, *two), (0, 0, rows), (2, *one)]
    else:
        sends = plan = [(i, 0, rows) for i in range(chips)]
    pad = ((0, levp - lev), (0, levp - lev))
    high = lax.reduce_precision(vert_factor, 8, 7)
    low = vert_factor - high
    vert, vert_t = [
        jnp.concatenate([jnp.pad(x, pad).astype(BF16) for x in parts], axis=1)
        for parts in ((high, high, low), (high.T, high.T, low.T))
    ]
    h_block = h_values.reshape(h_values.shape[2:])
    innovation = jnp.transpose(innovation, (1, 0, 2))
    obs_precision = jnp.transpose(obs_precision, (1, 0, 2))
    product = n_slab * width * lanes * rows
    small = 12 * rows * levp * LANES
    plane_bits = [1 << k for k in range(n_obs.bit_length() - 1)]

    def along(x, i):
        return lax.ppermute(x, "slab", [(s, s ^ (2 * i)) for s in range(n_slab)])

    def plane(x, i):
        return lax.ppermute(x, "obs", [(o, o ^ i) for o in range(n_obs)])

    def swap(x):
        return lax.ppermute(x, "slab", [(s, s ^ 1) for s in range(n_slab)])

    def plane_sum(halves, staged):
        halves = list(halves)
        moved_halves = [None] * len(halves)
        for step, bit in enumerate(plane_bits):
            bits = [bit, plane_bits[len(plane_bits) - 1 - step]]
            for at in range(0, len(halves), 2):
                if step > 0:
                    one, two = halves[at : at + 2]
                    one_more, two_more = moved_halves[at : at + 2]
                    halves[at : at + 2] = call(
                        functools.partial(add_halves_kernel, members, 0 if staged else 1),
                        [struct(one.shape, BF16)] * 2,
                        [],
                        0,
                        one,
                        one_more,
                        two,
                        two_more,
                    )
                for half in range(2):
                    moved_halves[at + half] = plane(halves[at + half], bits[half])
            if step == 0 and staged:
                halves[:] = call(
                    stage_kernel,
                    [struct(x.shape, BF16) for x in halves],
                    [pltpu.SemaphoreType.DMA((len(halves),))],
                    0,
                    *halves,
                    space=HBM,
                )
        return [x for pair in zip(halves, moved_halves) for x in pair]

    def line_sum(moved, other):
        ys = call(
            functools.partial(forward_kernel, sends, members),
            [
                struct((count, width), F32 if i == 0 or (via and at == 6) else BF16)
                for at, (i, unused, count) in enumerate(sends)
            ],
            [],
            2 * product,
            moved,
            other,
            own,
            partner,
        )
        if not via:
            return [y if i == 0 else along(y, i) for i, y in enumerate(ys)], [(0, rows)] * chips
        passed, far_rest, last_rest, next_some, next_rest, near, far = ys
        passed = along(passed, 1)
        far_rest, last_rest = along(far_rest, 2), along(last_rest, 3)
        next_some, next_rest = along(next_some, 1), along(next_rest, 1)
        (far,) = call(
            functools.partial(add_kernel, members, 0),
            [struct((some, width), BF16)],
            [],
            0,
            far,
            passed,
        )
        ys = [near, far_rest, last_rest, next_some, next_rest, along(far, 2)]
        return ys, [(0, rows), two, two, one, two, one]

    def line_gather(w, *parts):
        if not via:
            return [w if i == 0 else along(w, i) for i in range(chips)]
        some_w, rest_w = parts
        far = along(some_w, 2)
        far_rest, last_rest, next_ = along(rest_w, 2), along(rest_w, 3), along(w, 1)
        return [w, next_, far, far_rest, along(far, 1), last_rest]

    dense = struct((chips, colblocks, LANES, width), BF16)
    own, for_partner, *partials = call(
        functools.partial(start_kernel, (chips, halves)),
        [dense, dense] + half_rows,
        [
            pltpu.SMEM(seeds.shape, jnp.int32),
            pltpu.SMEM(block_obs.shape, jnp.int32),
            pltpu.SMEM(block_col.shape, jnp.int32),
            pltpu.SMEM(entry_count.shape, jnp.int32),
            pltpu.VMEM(col_sd.shape, F32),
            pltpu.VMEM((blocks, lev, profiles), F32),
            pltpu.VMEM((blocks, lev, profiles), F32),
            pltpu.VMEM((n_slab, members, levp, width), F32),
            pltpu.VMEM((2, rows, width), F32),
            pltpu.VMEM((rows, lanes), F32),
            pltpu.SemaphoreType.DMA((5 + 2 * blocks,)),
            pltpu.SemaphoreType.DMA((h_block.shape[0] * halves,)),
        ],
        2 * product,
        seeds,
        block_obs,
        block_col,
        entry_count,
        col_sd,
        innovation,
        obs_precision,
        h_block,
        space=HBM,
        limit=60,
    )
    ps = plane_sum(partials, True)
    partner = swap(for_partner)
    (precision,) = call(
        functools.partial(precision_kernel, halves, members),
        [struct((rows, width), F32)],
        [],
        0,
        obs_precision,
    )
    slab_sd, residual, moved = call(
        functools.partial(first_kernel, lev),
        [struct((1, lanes), F32), struct(slab_field, F32), struct(slab_rows, BF16)],
        [spread, spread],
        small * colblocks,
        *ps,
        vert,
        vert_t,
    )
    direction = total_step = image = state = None
    for sweep in range(ITERS):
        later, last = sweep > 0, sweep == ITERS - 1
        ys, spans = line_sum(moved, swap(moved))
        state, *weighted = call(
            functools.partial(weigh_kernel, later, last, members, lev, spans),
            [struct((members, 8, LANES), F32)]
            + [struct((n, width), BF16) for n in ((rows, some, rest) if via else (rows,))]
            + ([] if last else [struct((rows, width), F32)]),
            [],
            0,
            *ys,
            precision,
            *([image, state] if later else []),
        )
        if not last:
            *weighted, image = weighted
        ws = line_gather(*weighted)
        (theirs,) = call(
            functools.partial(adjoint_kernel, plan, members),
            [struct(slab_rows, BF16)],
            [],
            product,
            *ws,
            partner,
        )
        theirs = swap(theirs)
        (mine,) = call(
            functools.partial(adjoint_kernel, plan, members),
            [struct(slab_rows, F32)],
            [],
            product,
            *ws,
            own,
        )
        known = [vert, vert_t, state, residual]
        if later:
            known += [direction, total_step]
        if last:
            ps = call(
                functools.partial(combine_columns_kernel, members),
                [struct((rows, LANES), BF16)] * n_obs,
                [],
                0,
                mine,
                theirs,
            )
            ps = [ps[0]] + [plane(ps[i], i) for i in reversed(range(1, n_obs))]
            outputs = call(
                functools.partial(last_kernel, len(ps), later, lev),
                [struct((lev, members, LANES), F32)] * 2,
                [pltpu.VMEM((wide // 8 * 8, LANES), F32)],
                small,
                *ps,
                col_sd,
                *known,
            )
            break
        ps = call(
            functools.partial(combine_kernel, members), half_rows, [], 0, mine, theirs
        )
        ps = plane_sum(ps, False)
        outs = [
            struct(slab_field, F32),
            struct((members, levp, LANES), F32),
            struct(slab_rows, BF16),
        ]
        if later:
            outs.append(struct(slab_field, F32))
        r, total_step, moved, *d = call(
            functools.partial(update_kernel, later, lev),
            outs,
            [spread, spread],
            small * colblocks,
            *ps,
            slab_sd,
            *known,
        )
        direction, residual = (d[0] if later else residual), r
    return tuple(jnp.transpose(x, (1, 0, 2))[None] for x in outputs)


def solution(mesh):
    return jax.shard_map(
        functools.partial(per_device, mesh.shape["slab"], mesh.shape["obs"]),
        mesh=mesh,
        in_specs=(
            P("obs", None, None),
            P("obs", None, None),
            P(),
            P(("slab", "obs"), None),
            P(),
            P("slab", "obs", None, None, None),
            P("slab", "obs", None),
            P("slab", "obs", None),
            P("slab", "obs"),
        ),
        out_specs=(P(("slab", "obs"), None, None, None), P(("slab", "obs"), None, None, None)),
        check_vma=False,
    )
```

time: 114 us -> 122 us (1.070); the launches traced: 114 us -> 121 us
  waiting for transfers between devices: 54 us -> 58.4 us
  starting transfers between devices: 42.6 us -> 44.6 us
    ppermute x24 -> x22, waiting for transfers between devices: 28.8 us -> 33.9 us  [along(): return lax.ppermute(x, 'slab', [(s, s ^ 2 * i) for s in range(n_slab)])]
    ppermute x24 -> x22, starting transfers between devices: 28.4 us -> 30.7 us  [along(): return lax.ppermute(x, 'slab', [(s, s ^ 2 * i) for s in range(n_slab)])]
  transfers between devices with their start and end apart: 40 -> 38, of which waited for: 32 -> 26; matrix products, arithmetic and copies ran while one was open for 0% -> 0% of each run, Pallas kernels for 3% -> 2%
where the time goes in v10:
time: 122 us; the launch traced here: 121 us
  waiting for transfers between devices  58.4 us (48%)
  starting transfers between devices  44.6 us (37%)
  Pallas kernels  14.2 us (12%)
  local copies, waits for them, and re-layouts  2.09 us (2%)
  between operations  1.56 us (1%)
    ppermute x22, waiting for transfers between devices, along(): return lax.ppermute(x, 'slab', [(s, s ^ 2 * i) for s in range(n_slab)])  33.9 us
    ppermute x22, starting transfers between devices, along(): return lax.ppermute(x, 'slab', [(s, s ^ 2 * i) for s in range(n_slab)])  30.7 us
    ppermute x11, waiting for transfers between devices, plane(): return lax.ppermute(x, 'obs', [(o, o ^ i) for o in range(n_obs)])  19.2 us
    pallas_call x20, Pallas kernels, call(): pl.pallas_call(kernel, out_shape=outs, in_specs=[space] * len(args), out_...  14.2 us
    ppermute x11, starting transfers between devices, plane(): return lax.ppermute(x, 'obs', [(o, o ^ i) for o in range(n_obs)])  13.1 us
    ppermute x5, waiting for transfers between devices, swap(): return lax.ppermute(x, 'slab', [(s, s ^ 1) for s in range(n_slab)])  5.3 us
  transfers between devices with their start and end apart: 38, of which 26 were waited for; matrix products, arithmetic and copies ran while one was open for 0% of the time, Pallas kernels for 2%

profile of v10, /device:TPU:0, one launch (start us, length us, event | category | flops | bytes accessed | tf_op | source)
XLA Modules:
  0.0 120.9 jit_solution(2639869111894385639)
XLA Ops:
  1.3 5.3 %shard_map.104 = (bf16[4,4,128,256]{3,2,1,0:T(8,128)(2,1)}, bf16[4,4,128,256]{3,2,1,0:T(8,128)(2,1)}, bf16[304,256]{1,0:T(8,128)(2,1)}, bf16[304,256]{1,0:T(8,128)(2,1)}) custom-call(s32[4]{0:T(128)} %seeds_in.1, s32[1,1,32]{2,1,0:T(1,128)} %ids_in.1, s32[1,1,32]{2,1,0:T(1,128)} %cols_in.1, s32[1,1]{1,0:T(1,128)S(6)} %copy.16.count_in, f32[1,128]{1,0:T(1,128)} %refs_4_.1, ...), custom_call_target="tpu_custom_call" | custom-call | flops 637534208 | bytes 5735188 | tf_op jit(solution)/shard_map/pallas_call | solution.py:23
  7.1 2.5 %collective-permute-start = (bf16[304,256]{1,0:T(8,128)(2,1)}, bf16[304,256]{1,0:T(8,128)(2,1)S(1)}, u32[]{:S(2)}, u32[]{:S(2)}) collective-permute-start(bf16[304,256]{1,0:T(8,128)(2,1)} %get-tuple-element.49.refs_0_), channel_id=1, source_target_pairs={{0,1},{1,0},{2,3},{3,2},{4,5},{5,4},{6,7},{7,6},{8,9},{9,8},{10,11... | collective-permute-start | bytes 466952 | tf_op jit(solution)/shard_map/ppermute | solution.py:541
  9.6 1.6 %collective-permute-start.1 = (bf16[304,256]{1,0:T(8,128)(2,1)}, bf16[304,256]{1,0:T(8,128)(2,1)S(1)}, u32[]{:S(2)}, u32[]{:S(2)}) collective-permute-start(bf16[304,256]{1,0:T(8,128)(2,1)} %get-tuple-element.50.refs_1_), channel_id=1, source_target_pairs={{0,2},{1,3},{2,0},{3,1},{4,6},{5,7},{6,4},{7,5},{8,10},{9,11},{10,... | collective-permute-start | bytes 466952 | tf_op jit(solution)/shard_map/ppermute | solution.py:541
  16.0 1.7 %collective-permute-start.2 = (bf16[304,256]{1,0:T(8,128)(2,1)S(1)}, bf16[304,256]{1,0:T(8,128)(2,1)S(1)}, u32[]{:S(2)}, u32[]{:S(2)}) collective-permute-start(bf16[304,256]{1,0:T(8,128)(2,1)S(1)} %get-tuple-element.53.refs_0_), channel_id=1, source_target_pairs={{0,2},{1,3},{2,0},{3,1},{4,6},{5,7},{6,4},{7,5},{8,10},{9,11},{10,... | collective-permute-start | bytes 466952 | tf_op jit(solution)/shard_map/ppermute | solution.py:541
  18.9 2.4 %collective-permute-done.2.refs_1_ = bf16[304,256]{1,0:T(8,128)(2,1)S(1)} collective-permute-done((bf16[304,256]{1,0:T(8,128)(2,1)S(1)}, bf16[304,256]{1,0:T(8,128)(2,1)S(1)}, u32[]{:S(2)}, u32[]{:S(2)}) %collective-permute-start.2) | collective-permute-done | bytes 155680 | tf_op jit(solution)/shard_map/ppermute | solution.py:541
  24.0 1.6 %collective-permute-done.4.other = bf16[304,512]{1,0:T(8,128)(2,1)S(1)} collective-permute-done((bf16[304,512]{1,0:T(8,128)(2,1)S(1)}, bf16[304,512]{1,0:T(8,128)(2,1)S(1)}, u32[]{:S(2)}, u32[]{:S(2)}) %collective-permute-start.4) | collective-permute-done | bytes 311328 | tf_op jit(solution)/shard_map/ppermute | solution.py:544
  26.5 1.7 %collective-permute-start.10 = (bf16[160,256]{1,0:T(8,128)(2,1)S(1)}, bf16[160,256]{1,0:T(8,128)(2,1)S(1)}, u32[]{:S(2)}, u32[]{:S(2)}) collective-permute-start(bf16[160,256]{1,0:T(8,128)(2,1)S(1)} %get-tuple-element.64), channel_id=1, source_target_pairs={{0,8},{4,12},{8,0},{12,4},{16,24},{20,28},{24,16},{28,20},{1,9},{5... | collective-permute-start | bytes 245768 | tf_op jit(solution)/shard_map/ppermute | solution.py:538
  28.6 3.0 %collective-permute-done.10.refs_1_ = bf16[160,256]{1,0:T(8,128)(2,1)S(1)} collective-permute-done((bf16[160,256]{1,0:T(8,128)(2,1)S(1)}, bf16[160,256]{1,0:T(8,128)(2,1)S(1)}, u32[]{:S(2)}, u32[]{:S(2)}) %collective-permute-start.10) | collective-permute-done | bytes 81952 | tf_op jit(solution)/shard_map/ppermute | solution.py:538
  31.6 2.5 %collective-permute-start.11 = (bf16[160,256]{1,0:T(8,128)(2,1)S(1)}, bf16[160,256]{1,0:T(8,128)(2,1)S(1)}, u32[]{:S(2)}, u32[]{:S(2)}) collective-permute-start(bf16[160,256]{1,0:T(8,128)(2,1)S(1)} %shard_map.109), channel_id=1, source_target_pairs={{0,16},{4,20},{8,24},{12,28},{16,0},{20,4},{24,8},{28,12},{1,17},{... | collective-permute-start | bytes 245768 | tf_op jit(solution)/shard_map/ppermute | solution.py:538
  34.6 3.9 %collective-permute-start.7 = (bf16[144,256]{1,0:T(8,128)(2,1)S(1)}, bf16[144,256]{1,0:T(8,128)(2,1)S(1)}, u32[]{:S(2)}, u32[]{:S(2)}) collective-permute-start(bf16[144,256]{1,0:T(8,128)(2,1)S(1)} %get-tuple-element.60), channel_id=1, source_target_pairs={{0,24},{4,28},{8,16},{12,20},{16,8},{20,12},{24,0},{28,4},{1,25},{... | collective-permute-start | bytes 221192 | tf_op jit(solution)/shard_map/ppermute | solution.py:538
  38.7 4.7 %collective-permute-done.6.refs_1_ = bf16[144,256]{1,0:T(8,128)(2,1)S(1)} collective-permute-done((bf16[144,256]{1,0:T(8,128)(2,1)S(1)}, bf16[144,256]{1,0:T(8,128)(2,1)S(1)}, u32[]{:S(2)}, u32[]{:S(2)}) %collective-permute-start.6) | collective-permute-done | bytes 73760 | tf_op jit(solution)/shard_map/ppermute | solution.py:538
  43.8 2.8 %collective-permute-start.13 = (bf16[160,256]{1,0:T(8,128)(2,1)S(1)}, bf16[160,256]{1,0:T(8,128)(2,1)S(1)}, u32[]{:S(2)}, u32[]{:S(2)}) collective-permute-start(bf16[160,256]{1,0:T(8,128)(2,1)S(1)} %get-tuple-element.66), channel_id=1, source_target_pairs={{0,16},{4,20},{8,24},{12,28},{16,0},{20,4},{24,8},{28,12},{1,17},{... | collective-permute-start | bytes 245768 | tf_op jit(solution)/shard_map/ppermute | solution.py:538
  47.2 3.3 %collective-permute-done.13.refs_2_ = bf16[160,256]{1,0:T(8,128)(2,1)S(1)} collective-permute-done((bf16[160,256]{1,0:T(8,128)(2,1)S(1)}, bf16[160,256]{1,0:T(8,128)(2,1)S(1)}, u32[]{:S(2)}, u32[]{:S(2)}) %collective-permute-start.13) | collective-permute-done | bytes 81952 | tf_op jit(solution)/shard_map/ppermute | solution.py:538
  51.2 3.1 %collective-permute-start.16 = (bf16[144,256]{1,0:T(8,128)(2,1)S(1)}, bf16[144,256]{1,0:T(8,128)(2,1)S(1)}, u32[]{:S(2)}, u32[]{:S(2)}) collective-permute-start(bf16[144,256]{1,0:T(8,128)(2,1)S(1)} %get-tuple-element.67), channel_id=1, source_target_pairs={{0,24},{4,28},{8,16},{12,20},{16,8},{20,12},{24,0},{28,4},{1,25},{... | collective-permute-start | bytes 221192 | tf_op jit(solution)/shard_map/ppermute | solution.py:538
  54.3 3.3 %collective-permute-done.16.refs_5_ = bf16[144,256]{1,0:T(8,128)(2,1)S(1)} collective-permute-done((bf16[144,256]{1,0:T(8,128)(2,1)S(1)}, bf16[144,256]{1,0:T(8,128)(2,1)S(1)}, u32[]{:S(2)}, u32[]{:S(2)}) %collective-permute-start.16) | collective-permute-done | bytes 73760 | tf_op jit(solution)/shard_map/ppermute | solution.py:538
  57.6 2.3 %collective-permute-done.14.refs_3_ = bf16[144,256]{1,0:T(8,128)(2,1)S(1)} collective-permute-done((bf16[144,256]{1,0:T(8,128)(2,1)S(1)}, bf16[144,256]{1,0:T(8,128)(2,1)S(1)}, u32[]{:S(2)}, u32[]{:S(2)}) %collective-permute-start.14) | collective-permute-done | bytes 73760 | tf_op jit(solution)/shard_map/ppermute | solution.py:538
  63.1 5.3 %collective-permute-done.18.one_more = bf16[304,256]{1,0:T(8,128)(2,1)S(1)} collective-permute-done((bf16[304,256]{1,0:T(8,128)(2,1)S(1)}, bf16[304,256]{1,0:T(8,128)(2,1)S(1)}, u32[]{:S(2)}, u32[]{:S(2)}) %collective-permute-start.18) | collective-permute-done | bytes 155680 | tf_op jit(solution)/shard_map/ppermute | solution.py:541
  70.6 3.3 %collective-permute-done.20.refs_1_ = bf16[304,256]{1,0:T(8,128)(2,1)S(1)} collective-permute-done((bf16[304,256]{1,0:T(8,128)(2,1)S(1)}, bf16[304,256]{1,0:T(8,128)(2,1)S(1)}, u32[]{:S(2)}, u32[]{:S(2)}) %collective-permute-start.20) | collective-permute-done | bytes 155680 | tf_op jit(solution)/shard_map/ppermute | solution.py:541
  78.1 2.0 %collective-permute-start.25 = (bf16[160,256]{1,0:T(8,128)(2,1)S(1)}, bf16[160,256]{1,0:T(8,128)(2,1)S(1)}, u32[]{:S(2)}, u32[]{:S(2)}) collective-permute-start(bf16[160,256]{1,0:T(8,128)(2,1)S(1)} %get-tuple-element.79), channel_id=1, source_target_pairs={{0,8},{4,12},{8,0},{12,4},{16,24},{20,28},{24,16},{28,20},{1,9},{5... | collective-permute-start | bytes 245768 | tf_op jit(solution)/shard_map/ppermute | solution.py:538
  80.1 3.3 %collective-permute-done.27.refs_1_ = bf16[160,256]{1,0:T(8,128)(2,1)S(1)} collective-permute-done((bf16[160,256]{1,0:T(8,128)(2,1)S(1)}, bf16[160,256]{1,0:T(8,128)(2,1)S(1)}, u32[]{:S(2)}, u32[]{:S(2)}) %collective-permute-start.27) | collective-permute-done | bytes 81952 | tf_op jit(solution)/shard_map/ppermute | solution.py:538
  84.1 2.4 %collective-permute-start.23 = (bf16[144,256]{1,0:T(8,128)(2,1)S(1)}, bf16[144,256]{1,0:T(8,128)(2,1)S(1)}, u32[]{:S(2)}, u32[]{:S(2)}) collective-permute-start(bf16[144,256]{1,0:T(8,128)(2,1)S(1)} %get-tuple-element.77), channel_id=1, source_target_pairs={{0,16},{4,20},{8,24},{12,28},{16,0},{20,4},{24,8},{28,12},{1,17},{... | collective-permute-start | bytes 221192 | tf_op jit(solution)/shard_map/ppermute | solution.py:538
  86.4 2.2 %collective-permute-start.24 = (bf16[144,256]{1,0:T(8,128)(2,1)S(1)}, bf16[144,256]{1,0:T(8,128)(2,1)S(1)}, u32[]{:S(2)}, u32[]{:S(2)}) collective-permute-start(bf16[144,256]{1,0:T(8,128)(2,1)S(1)} %get-tuple-element.78), channel_id=1, source_target_pairs={{0,24},{4,28},{8,16},{12,20},{16,8},{20,12},{24,0},{28,4},{1,25},{... | collective-permute-start | bytes 221192 | tf_op jit(solution)/shard_map/ppermute | solution.py:538
  88.6 5.9 %collective-permute-done.23.refs_1_ = bf16[144,256]{1,0:T(8,128)(2,1)S(1)} collective-permute-done((bf16[144,256]{1,0:T(8,128)(2,1)S(1)}, bf16[144,256]{1,0:T(8,128)(2,1)S(1)}, u32[]{:S(2)}, u32[]{:S(2)}) %collective-permute-start.23) | collective-permute-done | bytes 73760 | tf_op jit(solution)/shard_map/ppermute | solution.py:538
  94.9 2.1 %collective-permute-start.30 = (bf16[160,256]{1,0:T(8,128)(2,1)S(1)}, bf16[160,256]{1,0:T(8,128)(2,1)S(1)}, u32[]{:S(2)}, u32[]{:S(2)}) collective-permute-start(bf16[160,256]{1,0:T(8,128)(2,1)S(1)} %get-tuple-element.85), channel_id=1, source_target_pairs={{0,16},{4,20},{8,24},{12,28},{16,0},{20,4},{24,8},{28,12},{1,17},{... | collective-permute-start | bytes 245768 | tf_op jit(solution)/shard_map/ppermute | solution.py:538
  97.7 2.7 %collective-permute-done.30.refs_2_ = bf16[160,256]{1,0:T(8,128)(2,1)S(1)} collective-permute-done((bf16[160,256]{1,0:T(8,128)(2,1)S(1)}, bf16[160,256]{1,0:T(8,128)(2,1)S(1)}, u32[]{:S(2)}, u32[]{:S(2)}) %collective-permute-start.30) | collective-permute-done | bytes 81952 | tf_op jit(solution)/shard_map/ppermute | solution.py:538
  100.4 1.6 %collective-permute-start.32 = (bf16[160,256]{1,0:T(8,128)(2,1)S(1)}, bf16[160,256]{1,0:T(8,128)(2,1)S(1)}, u32[]{:S(2)}, u32[]{:S(2)}) collective-permute-start(bf16[160,256]{1,0:T(8,128)(2,1)S(1)} %collective-permute-done.30.refs_2_), channel_id=1, source_target_pairs={{0,8},{4,12},{8,0},{12,4},{16,24},{20,28},{24,16},{28,20},{1,9},{5... | collective-permute-start | bytes 245768 | tf_op jit(solution)/shard_map/ppermute | solution.py:538
  102.0 2.8 %collective-permute-start.33 = (bf16[144,256]{1,0:T(8,128)(2,1)S(1)}, bf16[144,256]{1,0:T(8,128)(2,1)S(1)}, u32[]{:S(2)}, u32[]{:S(2)}) collective-permute-start(bf16[144,256]{1,0:T(8,128)(2,1)S(1)} %get-tuple-element.86), channel_id=1, source_target_pairs={{0,24},{4,28},{8,16},{12,20},{16,8},{20,12},{24,0},{28,4},{1,25},{... | collective-permute-start | bytes 221192 | tf_op jit(solution)/shard_map/ppermute | solution.py:538
  104.8 3.4 %collective-permute-done.33.refs_5_ = bf16[144,256]{1,0:T(8,128)(2,1)S(1)} collective-permute-done((bf16[144,256]{1,0:T(8,128)(2,1)S(1)}, bf16[144,256]{1,0:T(8,128)(2,1)S(1)}, u32[]{:S(2)}, u32[]{:S(2)}) %collective-permute-start.33) | collective-permute-done | bytes 73760 | tf_op jit(solution)/shard_map/ppermute | solution.py:538
  108.2 1.9 %collective-permute-done.31.refs_3_ = bf16[144,256]{1,0:T(8,128)(2,1)S(1)} collective-permute-done((bf16[144,256]{1,0:T(8,128)(2,1)S(1)}, bf16[144,256]{1,0:T(8,128)(2,1)S(1)}, u32[]{:S(2)}, u32[]{:S(2)}) %collective-permute-start.31) | collective-permute-done | bytes 73760 | tf_op jit(solution)/shard_map/ppermute | solution.py:538
  112.4 2.8 %collective-permute-start.35 = (bf16[304,128]{1,0:T(8,128)(2,1)S(1)}, bf16[304,128]{1,0:T(8,128)(2,1)S(1)}, u32[]{:S(2)}, u32[]{:S(2)}) collective-permute-start(bf16[304,128]{1,0:T(8,128)(2,1)S(1)} %get-tuple-element.88), channel_id=1, source_target_pairs={{0,3},{1,2},{2,1},{3,0},{4,7},{5,6},{6,5},{7,4},{8,11},{9,10},{10,... | collective-permute-start | bytes 233480 | tf_op jit(solution)/shard_map/ppermute | solution.py:541
  116.0 2.0 %collective-permute-done.35.refs_1_ = bf16[304,128]{1,0:T(8,128)(2,1)S(1)} collective-permute-done((bf16[304,128]{1,0:T(8,128)(2,1)S(1)}, bf16[304,128]{1,0:T(8,128)(2,1)S(1)}, u32[]{:S(2)}, u32[]{:S(2)}) %collective-permute-start.35) | collective-permute-done | bytes 77856 | tf_op jit(solution)/shard_map/ppermute | solution.py:541
  118.0 1.7 %collective-permute-done.36.refs_2_ = bf16[304,128]{1,0:T(8,128)(2,1)S(1)} collective-permute-done((bf16[304,128]{1,0:T(8,128)(2,1)S(1)}, bf16[304,128]{1,0:T(8,128)(2,1)S(1)}, u32[]{:S(2)}, u32[]{:S(2)}) %collective-permute-start.36) | collective-permute-done | bytes 77856 | tf_op jit(solution)/shard_map/ppermute | solution.py:541
  (83 shorter events, 28.5 us)
Async XLA Ops:
  6.6 19.0 %collective-permute-start.5 = (bf16[4,4,128,256]{3,2,1,0:T(8,128)(2,1)}, bf16[4,4,128,256]{3,2,1,0:T(8,128)(2,1)S(1)}, u32[]{:S(2)}, u32[]{:S(2)}) collective-permute-start(bf16[4,4,128,256]{3,2,1,0:T(8,128)(2,1)} %get-tuple-element.57), channel_id=1, source_target_pairs={{0,4},{4,0},{8,12},{12,8},{16,20},{20,16},{24,28},{28,24},{1,5},{5... | collective-permute-start | bytes 3145736 | tf_op jit(solution)/shard_map/ppermute | solution.py:544
  7.1 7.3 %collective-permute-start = (bf16[304,256]{1,0:T(8,128)(2,1)}, bf16[304,256]{1,0:T(8,128)(2,1)S(1)}, u32[]{:S(2)}, u32[]{:S(2)}) collective-permute-start(bf16[304,256]{1,0:T(8,128)(2,1)} %get-tuple-element.49.refs_0_), channel_id=1, source_target_pairs={{0,1},{1,0},{2,3},{3,2},{4,5},{5,4},{6,7},{7,6},{8,9},{9,8},{10,11... | collective-permute-start | bytes 466952 | tf_op jit(solution)/shard_map/ppermute | solution.py:541
  9.6 6.3 %collective-permute-start.1 = (bf16[304,256]{1,0:T(8,128)(2,1)}, bf16[304,256]{1,0:T(8,128)(2,1)S(1)}, u32[]{:S(2)}, u32[]{:S(2)}) collective-permute-start(bf16[304,256]{1,0:T(8,128)(2,1)} %get-tuple-element.50.refs_1_), channel_id=1, source_target_pairs={{0,2},{1,3},{2,0},{3,1},{4,6},{5,7},{6,4},{7,5},{8,10},{9,11},{10,... | collective-permute-start | bytes 466952 | tf_op jit(solution)/shard_map/ppermute | solution.py:541
  16.0 5.3 %collective-permute-start.2 = (bf16[304,256]{1,0:T(8,128)(2,1)S(1)}, bf16[304,256]{1,0:T(8,128)(2,1)S(1)}, u32[]{:S(2)}, u32[]{:S(2)}) collective-permute-start(bf16[304,256]{1,0:T(8,128)(2,1)S(1)} %get-tuple-element.53.refs_0_), channel_id=1, source_target_pairs={{0,2},{1,3},{2,0},{3,1},{4,6},{5,7},{6,4},{7,5},{8,10},{9,11},{10,... | collective-permute-start | bytes 466952 | tf_op jit(solution)/shard_map/ppermute | solution.py:541
  17.7 5.2 %collective-permute-start.3 = (bf16[304,256]{1,0:T(8,128)(2,1)S(1)}, bf16[304,256]{1,0:T(8,128)(2,1)S(1)}, u32[]{:S(2)}, u32[]{:S(2)}) collective-permute-start(bf16[304,256]{1,0:T(8,128)(2,1)S(1)} %get-tuple-element.54.refs_2_), channel_id=1, source_target_pairs={{0,1},{1,0},{2,3},{3,2},{4,5},{5,4},{6,7},{7,6},{8,9},{9,8},{10,11... | collective-permute-start | bytes 466952 | tf_op jit(solution)/shard_map/ppermute | solution.py:541
  26.5 5.1 %collective-permute-start.10 = (bf16[160,256]{1,0:T(8,128)(2,1)S(1)}, bf16[160,256]{1,0:T(8,128)(2,1)S(1)}, u32[]{:S(2)}, u32[]{:S(2)}) collective-permute-start(bf16[160,256]{1,0:T(8,128)(2,1)S(1)} %get-tuple-element.64), channel_id=1, source_target_pairs={{0,8},{4,12},{8,0},{12,4},{16,24},{20,28},{24,16},{28,20},{1,9},{5... | collective-permute-start | bytes 245768 | tf_op jit(solution)/shard_map/ppermute | solution.py:538
  28.1 15.4 %collective-permute-start.8 = (bf16[160,256]{1,0:T(8,128)(2,1)S(1)}, bf16[160,256]{1,0:T(8,128)(2,1)S(1)}, u32[]{:S(2)}, u32[]{:S(2)}) collective-permute-start(bf16[160,256]{1,0:T(8,128)(2,1)S(1)} %get-tuple-element.61), channel_id=1, source_target_pairs={{0,8},{4,12},{8,0},{12,4},{16,24},{20,28},{24,16},{28,20},{1,9},{5... | collective-permute-start | bytes 245768 | tf_op jit(solution)/shard_map/ppermute | solution.py:538
  31.6 12.0 %collective-permute-start.11 = (bf16[160,256]{1,0:T(8,128)(2,1)S(1)}, bf16[160,256]{1,0:T(8,128)(2,1)S(1)}, u32[]{:S(2)}, u32[]{:S(2)}) collective-permute-start(bf16[160,256]{1,0:T(8,128)(2,1)S(1)} %shard_map.109), channel_id=1, source_target_pairs={{0,16},{4,20},{8,24},{12,28},{16,0},{20,4},{24,8},{28,12},{1,17},{... | collective-permute-start | bytes 245768 | tf_op jit(solution)/shard_map/ppermute | solution.py:538
  34.1 9.3 %collective-permute-start.6 = (bf16[144,256]{1,0:T(8,128)(2,1)S(1)}, bf16[144,256]{1,0:T(8,128)(2,1)S(1)}, u32[]{:S(2)}, u32[]{:S(2)}) collective-permute-start(bf16[144,256]{1,0:T(8,128)(2,1)S(1)} %get-tuple-element.59), channel_id=1, source_target_pairs={{0,16},{4,20},{8,24},{12,28},{16,0},{20,4},{24,8},{28,12},{1,17},{... | collective-permute-start | bytes 221192 | tf_op jit(solution)/shard_map/ppermute | solution.py:538
  34.6 8.8 %collective-permute-start.7 = (bf16[144,256]{1,0:T(8,128)(2,1)S(1)}, bf16[144,256]{1,0:T(8,128)(2,1)S(1)}, u32[]{:S(2)}, u32[]{:S(2)}) collective-permute-start(bf16[144,256]{1,0:T(8,128)(2,1)S(1)} %get-tuple-element.60), channel_id=1, source_target_pairs={{0,24},{4,28},{8,16},{12,20},{16,8},{20,12},{24,0},{28,4},{1,25},{... | collective-permute-start | bytes 221192 | tf_op jit(solution)/shard_map/ppermute | solution.py:538
  38.5 5.1 %collective-permute-start.9 = (bf16[144,256]{1,0:T(8,128)(2,1)S(1)}, bf16[144,256]{1,0:T(8,128)(2,1)S(1)}, u32[]{:S(2)}, u32[]{:S(2)}) collective-permute-start(bf16[144,256]{1,0:T(8,128)(2,1)S(1)} %get-tuple-element.62), channel_id=1, source_target_pairs={{0,8},{4,12},{8,0},{12,4},{16,24},{20,28},{24,16},{28,20},{1,9},{5... | collective-permute-start | bytes 221192 | tf_op jit(solution)/shard_map/ppermute | solution.py:538
  43.8 6.7 %collective-permute-start.13 = (bf16[160,256]{1,0:T(8,128)(2,1)S(1)}, bf16[160,256]{1,0:T(8,128)(2,1)S(1)}, u32[]{:S(2)}, u32[]{:S(2)}) collective-permute-start(bf16[160,256]{1,0:T(8,128)(2,1)S(1)} %get-tuple-element.66), channel_id=1, source_target_pairs={{0,16},{4,20},{8,24},{12,28},{16,0},{20,4},{24,8},{28,12},{1,17},{... | collective-permute-start | bytes 245768 | tf_op jit(solution)/shard_map/ppermute | solution.py:538
  46.6 13.3 %collective-permute-start.12 = (bf16[304,256]{1,0:T(8,128)(2,1)S(1)}, bf16[304,256]{1,0:T(8,128)(2,1)S(1)}, u32[]{:S(2)}, u32[]{:S(2)}) collective-permute-start(bf16[304,256]{1,0:T(8,128)(2,1)S(1)} %get-tuple-element.65.refs_0_), channel_id=1, source_target_pairs={{0,8},{4,12},{8,0},{12,4},{16,24},{20,28},{24,16},{28,20},{1,9},{5... | collective-permute-start | bytes 466952 | tf_op jit(solution)/shard_map/ppermute | solution.py:538
  50.5 9.4 %collective-permute-start.15 = (bf16[160,256]{1,0:T(8,128)(2,1)S(1)}, bf16[160,256]{1,0:T(8,128)(2,1)S(1)}, u32[]{:S(2)}, u32[]{:S(2)}) collective-permute-start(bf16[160,256]{1,0:T(8,128)(2,1)S(1)} %collective-permute-done.13.refs_2_), channel_id=1, source_target_pairs={{0,8},{4,12},{8,0},{12,4},{16,24},{20,28},{24,16},{28,20},{1,9},{5... | collective-permute-start | bytes 245768 | tf_op jit(solution)/shard_map/ppermute | solution.py:538
  51.2 6.4 %collective-permute-start.16 = (bf16[144,256]{1,0:T(8,128)(2,1)S(1)}, bf16[144,256]{1,0:T(8,128)(2,1)S(1)}, u32[]{:S(2)}, u32[]{:S(2)}) collective-permute-start(bf16[144,256]{1,0:T(8,128)(2,1)S(1)} %get-tuple-element.67), channel_id=1, source_target_pairs={{0,24},{4,28},{8,16},{12,20},{16,8},{20,12},{24,0},{28,4},{1,25},{... | collective-permute-start | bytes 221192 | tf_op jit(solution)/shard_map/ppermute | solution.py:538
  54.3 5.6 %collective-permute-start.14 = (bf16[144,256]{1,0:T(8,128)(2,1)S(1)}, bf16[144,256]{1,0:T(8,128)(2,1)S(1)}, u32[]{:S(2)}, u32[]{:S(2)}) collective-permute-start(bf16[144,256]{1,0:T(8,128)(2,1)S(1)} %get-tuple-element.67), channel_id=1, source_target_pairs={{0,16},{4,20},{8,24},{12,28},{16,0},{20,4},{24,8},{28,12},{1,17},{... | collective-permute-start | bytes 221192 | tf_op jit(solution)/shard_map/ppermute | solution.py:538
  62.2 6.1 %collective-permute-start.18 = (bf16[304,256]{1,0:T(8,128)(2,1)S(1)}, bf16[304,256]{1,0:T(8,128)(2,1)S(1)}, u32[]{:S(2)}, u32[]{:S(2)}) collective-permute-start(bf16[304,256]{1,0:T(8,128)(2,1)S(1)} %get-tuple-element.68.one), channel_id=1, source_target_pairs={{0,1},{1,0},{2,3},{3,2},{4,5},{5,4},{6,7},{7,6},{8,9},{9,8},{10,11... | collective-permute-start | bytes 466952 | tf_op jit(solution)/shard_map/ppermute | solution.py:541
  62.6 5.9 %collective-permute-start.19 = (bf16[304,256]{1,0:T(8,128)(2,1)S(1)}, bf16[304,256]{1,0:T(8,128)(2,1)S(1)}, u32[]{:S(2)}, u32[]{:S(2)}) collective-permute-start(bf16[304,256]{1,0:T(8,128)(2,1)S(1)} %get-tuple-element.69.two), channel_id=1, source_target_pairs={{0,2},{1,3},{2,0},{3,1},{4,6},{5,7},{6,4},{7,5},{8,10},{9,11},{10,... | collective-permute-start | bytes 466952 | tf_op jit(solution)/shard_map/ppermute | solution.py:541
  68.6 5.3 %collective-permute-start.20 = (bf16[304,256]{1,0:T(8,128)(2,1)S(1)}, bf16[304,256]{1,0:T(8,128)(2,1)S(1)}, u32[]{:S(2)}, u32[]{:S(2)}) collective-permute-start(bf16[304,256]{1,0:T(8,128)(2,1)S(1)} %get-tuple-element.70.refs_0_), channel_id=1, source_target_pairs={{0,2},{1,3},{2,0},{3,1},{4,6},{5,7},{6,4},{7,5},{8,10},{9,11},{10,... | collective-permute-start | bytes 466952 | tf_op jit(solution)/shard_map/ppermute | solution.py:541
  69.0 5.2 %collective-permute-start.21 = (bf16[304,256]{1,0:T(8,128)(2,1)S(1)}, bf16[304,256]{1,0:T(8,128)(2,1)S(1)}, u32[]{:S(2)}, u32[]{:S(2)}) collective-permute-start(bf16[304,256]{1,0:T(8,128)(2,1)S(1)} %get-tuple-element.71.refs_2_), channel_id=1, source_target_pairs={{0,1},{1,0},{2,3},{3,2},{4,5},{5,4},{6,7},{7,6},{8,9},{9,8},{10,11... | collective-permute-start | bytes 466952 | tf_op jit(solution)/shard_map/ppermute | solution.py:541
  78.0 5.4 %collective-permute-start.27 = (bf16[160,256]{1,0:T(8,128)(2,1)S(1)}, bf16[160,256]{1,0:T(8,128)(2,1)S(1)}, u32[]{:S(2)}, u32[]{:S(2)}) collective-permute-start(bf16[160,256]{1,0:T(8,128)(2,1)S(1)} %get-tuple-element.82), channel_id=1, source_target_pairs={{0,8},{4,12},{8,0},{12,4},{16,24},{20,28},{24,16},{28,20},{1,9},{5... | collective-permute-start | bytes 245768 | tf_op jit(solution)/shard_map/ppermute | solution.py:538
  78.1 16.4 %collective-permute-start.25 = (bf16[160,256]{1,0:T(8,128)(2,1)S(1)}, bf16[160,256]{1,0:T(8,128)(2,1)S(1)}, u32[]{:S(2)}, u32[]{:S(2)}) collective-permute-start(bf16[160,256]{1,0:T(8,128)(2,1)S(1)} %get-tuple-element.79), channel_id=1, source_target_pairs={{0,8},{4,12},{8,0},{12,4},{16,24},{20,28},{24,16},{28,20},{1,9},{5... | collective-permute-start | bytes 245768 | tf_op jit(solution)/shard_map/ppermute | solution.py:538
  83.4 11.2 %collective-permute-start.28 = (bf16[160,256]{1,0:T(8,128)(2,1)S(1)}, bf16[160,256]{1,0:T(8,128)(2,1)S(1)}, u32[]{:S(2)}, u32[]{:S(2)}) collective-permute-start(bf16[160,256]{1,0:T(8,128)(2,1)S(1)} %shard_map.118), channel_id=1, source_target_pairs={{0,16},{4,20},{8,24},{12,28},{16,0},{20,4},{24,8},{28,12},{1,17},{... | collective-permute-start | bytes 245768 | tf_op jit(solution)/shard_map/ppermute | solution.py:538
  84.1 10.5 %collective-permute-start.23 = (bf16[144,256]{1,0:T(8,128)(2,1)S(1)}, bf16[144,256]{1,0:T(8,128)(2,1)S(1)}, u32[]{:S(2)}, u32[]{:S(2)}) collective-permute-start(bf16[144,256]{1,0:T(8,128)(2,1)S(1)} %get-tuple-element.77), channel_id=1, source_target_pairs={{0,16},{4,20},{8,24},{12,28},{16,0},{20,4},{24,8},{28,12},{1,17},{... | collective-permute-start | bytes 221192 | tf_op jit(solution)/shard_map/ppermute | solution.py:538
  86.4 8.2 %collective-permute-start.24 = (bf16[144,256]{1,0:T(8,128)(2,1)S(1)}, bf16[144,256]{1,0:T(8,128)(2,1)S(1)}, u32[]{:S(2)}, u32[]{:S(2)}) collective-permute-start(bf16[144,256]{1,0:T(8,128)(2,1)S(1)} %get-tuple-element.78), channel_id=1, source_target_pairs={{0,24},{4,28},{8,16},{12,20},{16,8},{20,12},{24,0},{28,4},{1,25},{... | collective-permute-start | bytes 221192 | tf_op jit(solution)/shard_map/ppermute | solution.py:538
  88.6 5.9 %collective-permute-start.26 = (bf16[144,256]{1,0:T(8,128)(2,1)S(1)}, bf16[144,256]{1,0:T(8,128)(2,1)S(1)}, u32[]{:S(2)}, u32[]{:S(2)}) collective-permute-start(bf16[144,256]{1,0:T(8,128)(2,1)S(1)} %get-tuple-element.80), channel_id=1, source_target_pairs={{0,8},{4,12},{8,0},{12,4},{16,24},{20,28},{24,16},{28,20},{1,9},{5... | collective-permute-start | bytes 221192 | tf_op jit(solution)/shard_map/ppermute | solution.py:538
  94.9 5.5 %collective-permute-start.30 = (bf16[160,256]{1,0:T(8,128)(2,1)S(1)}, bf16[160,256]{1,0:T(8,128)(2,1)S(1)}, u32[]{:S(2)}, u32[]{:S(2)}) collective-permute-start(bf16[160,256]{1,0:T(8,128)(2,1)S(1)} %get-tuple-element.85), channel_id=1, source_target_pairs={{0,16},{4,20},{8,24},{12,28},{16,0},{20,4},{24,8},{28,12},{1,17},{... | collective-permute-start | bytes 245768 | tf_op jit(solution)/shard_map/ppermute | solution.py:538
  97.0 13.0 %collective-permute-start.29 = (bf16[304,256]{1,0:T(8,128)(2,1)S(1)}, bf16[304,256]{1,0:T(8,128)(2,1)S(1)}, u32[]{:S(2)}, u32[]{:S(2)}) collective-permute-start(bf16[304,256]{1,0:T(8,128)(2,1)S(1)} %get-tuple-element.84.refs_0_), channel_id=1, source_target_pairs={{0,8},{4,12},{8,0},{12,4},{16,24},{20,28},{24,16},{28,20},{1,9},{5... | collective-permute-start | bytes 466952 | tf_op jit(solution)/shard_map/ppermute | solution.py:538
  100.4 9.6 %collective-permute-start.32 = (bf16[160,256]{1,0:T(8,128)(2,1)S(1)}, bf16[160,256]{1,0:T(8,128)(2,1)S(1)}, u32[]{:S(2)}, u32[]{:S(2)}) collective-permute-start(bf16[160,256]{1,0:T(8,128)(2,1)S(1)} %collective-permute-done.30.refs_2_), channel_id=1, source_target_pairs={{0,8},{4,12},{8,0},{12,4},{16,24},{20,28},{24,16},{28,20},{1,9},{5... | collective-permute-start | bytes 245768 | tf_op jit(solution)/shard_map/ppermute | solution.py:538
  102.0 6.2 %collective-permute-start.33 = (bf16[144,256]{1,0:T(8,128)(2,1)S(1)}, bf16[144,256]{1,0:T(8,128)(2,1)S(1)}, u32[]{:S(2)}, u32[]{:S(2)}) collective-permute-start(bf16[144,256]{1,0:T(8,128)(2,1)S(1)} %get-tuple-element.86), channel_id=1, source_target_pairs={{0,24},{4,28},{8,16},{12,20},{16,8},{20,12},{24,0},{28,4},{1,25},{... | collective-permute-start | bytes 221192 | tf_op jit(solution)/shard_map/ppermute | solution.py:538
  104.8 5.3 %collective-permute-start.31 = (bf16[144,256]{1,0:T(8,128)(2,1)S(1)}, bf16[144,256]{1,0:T(8,128)(2,1)S(1)}, u32[]{:S(2)}, u32[]{:S(2)}) collective-permute-start(bf16[144,256]{1,0:T(8,128)(2,1)S(1)} %get-tuple-element.86), channel_id=1, source_target_pairs={{0,16},{4,20},{8,24},{12,28},{16,0},{20,4},{24,8},{28,12},{1,17},{... | collective-permute-start | bytes 221192 | tf_op jit(solution)/shard_map/ppermute | solution.py:538
  112.4 5.6 %collective-permute-start.35 = (bf16[304,128]{1,0:T(8,128)(2,1)S(1)}, bf16[304,128]{1,0:T(8,128)(2,1)S(1)}, u32[]{:S(2)}, u32[]{:S(2)}) collective-permute-start(bf16[304,128]{1,0:T(8,128)(2,1)S(1)} %get-tuple-element.88), channel_id=1, source_target_pairs={{0,3},{1,2},{2,1},{3,0},{4,7},{5,6},{6,5},{7,4},{8,11},{9,10},{10,... | collective-permute-start | bytes 233480 | tf_op jit(solution)/shard_map/ppermute | solution.py:541
  (12 other events, 81.0 us)

commit v11 on v10

--- a/solution.py
+++ b/solution.py
@@ -397,7 +397,8 @@
     width = ws[0].shape[1]
     acc = None
     for i in range(tiles.shape[0]):
-        w = [ref[...] for ref, (chip, *span) in zip(ws, plan) if chip == i]
+        w = {first: ref for ref, (chip, first, count) in zip(ws, plan) if chip == i}
+        w = [w[first][...] for first in sorted(w)]
         w = w[0] if len(w) == 1 else jnp.concatenate(w, axis=0)
         part = lax.dot_general(
             w, tiles[z ^ i].reshape(lanes, width), NT, preferred_element_type=F32
@@ -512,11 +513,11 @@
     wide = rows + levp - lev + 7
     spread = pltpu.VMEM((wide // 8 * 8, lanes), F32)
     some = rows // 32 * 16
-    some, rest = rows - some, some
+    rest = rows - some
     via = chips == 4
     if via:
         one, two = (0, some), (some, rest)
-        plan = [(0, 0, rows), (1, 0, rows), (2, *one), (2, *two), (3, *one), (3, *two)]
+        plan = [(0, 0, rows), *((i, *two) for i in (1, 3, 2)), *((i, *one) for i in (1, 2, 3))]
         sends = [(3, *one), (2, *two), (3, *two), (1, *one), (1, *two), (0, 0, rows), (2, *one)]
     else:
         sends = plan = [(i, 0, rows) for i in range(chips)]
@@ -610,9 +611,9 @@
         if not via:
             return [w if i == 0 else along(w, i) for i in range(chips)]
         some_w, rest_w = parts
-        far = along(some_w, 2)
-        far_rest, last_rest, next_ = along(rest_w, 2), along(rest_w, 3), along(w, 1)
-        return [w, next_, far, far_rest, along(far, 1), last_rest]
+        far, next_ = along(some_w, 2), along(some_w, 1)
+        rest_ws = [along(rest_w, i) for i in (1, 3, 2)]
+        return [w, *rest_ws, next_, far, along(far, 1)]
 
     dense = struct((chips, colblocks, LANES, width), BF16)
     own, for_partner, *partials = call(

time: 122 us -> 114 us (0.934)
  waiting for transfers between devices: 58.4 us -> 50 us
    ppermute x22 -> x24, waiting for transfers between devices: 33.9 us -> 25.3 us  [along(): return lax.ppermute(x, 'slab', [(s, s ^ 2 * i) for s in range(n_slab)])]
    ppermute x22 -> x24, starting transfers between devices: 30.7 us -> 31.6 us  [along(): return lax.ppermute(x, 'slab', [(s, s ^ 2 * i) for s in range(n_slab)])]
  transfers between devices with their start and end apart: 38 -> 40, of which waited for: 26 -> 25; matrix products, arithmetic and copies ran while one was open for 0% -> 0% of each run, Pallas kernels for 2% -> 3%
where the time goes in v11:
time: 114 us; the launch traced here: 113 us
  waiting for transfers between devices  50 us (44%)
  starting transfers between devices  45.6 us (40%)
  Pallas kernels  14 us (12%)
  local copies, waits for them, and re-layouts  2.09 us (2%)
  between operations  1.56 us (1%)
    ppermute x24, starting transfers between devices, along(): return lax.ppermute(x, 'slab', [(s, s ^ 2 * i) for s in range(n_slab)])  31.6 us
    ppermute x24, waiting for transfers between devices, along(): return lax.ppermute(x, 'slab', [(s, s ^ 2 * i) for s in range(n_slab)])  25.3 us
    ppermute x11, waiting for transfers between devices, plane(): return lax.ppermute(x, 'obs', [(o, o ^ i) for o in range(n_obs)])  19.4 us
    pallas_call x20, Pallas kernels, call(): pl.pallas_call(kernel, out_shape=outs, in_specs=[space] * len(args), out_...  14 us
    ppermute x11, starting transfers between devices, plane(): return lax.ppermute(x, 'obs', [(o, o ^ i) for o in range(n_obs)])  13.1 us
    ppermute x5, waiting for transfers between devices, swap(): return lax.ppermute(x, 'slab', [(s, s ^ 1) for s in range(n_slab)])  5.29 us
  transfers between devices with their start and end apart: 40, of which 25 were waited for; matrix products, arithmetic and copies ran while one was open for 0% of the time, Pallas kernels for 3%

profile of v11, /device:TPU:0, one launch (start us, length us, event | category | flops | bytes accessed | tf_op | source)
XLA Modules:
  0.0 113.4 jit_solution(9057439966262752725)
XLA Ops:
  1.3 5.2 %shard_map.104 = (bf16[4,4,128,256]{3,2,1,0:T(8,128)(2,1)}, bf16[4,4,128,256]{3,2,1,0:T(8,128)(2,1)}, bf16[304,256]{1,0:T(8,128)(2,1)}, bf16[304,256]{1,0:T(8,128)(2,1)}) custom-call(s32[4]{0:T(128)} %seeds_in.1, s32[1,1,32]{2,1,0:T(1,128)} %ids_in.1, s32[1,1,32]{2,1,0:T(1,128)} %cols_in.1, s32[1,1]{1,0:T(1,128)S(6)} %copy.16.count_in, f32[1,128]{1,0:T(1,128)} %refs_4_.1, ...), custom_call_target="tpu_custom_call" | custom-call | flops 637534208 | bytes 5735188 | tf_op jit(solution)/shard_map/pallas_call | solution.py:23
  7.1 2.8 %collective-permute-start = (bf16[304,256]{1,0:T(8,128)(2,1)}, bf16[304,256]{1,0:T(8,128)(2,1)S(1)}, u32[]{:S(2)}, u32[]{:S(2)}) collective-permute-start(bf16[304,256]{1,0:T(8,128)(2,1)} %get-tuple-element.49.refs_0_), channel_id=1, source_target_pairs={{0,1},{1,0},{2,3},{3,2},{4,5},{5,4},{6,7},{7,6},{8,9},{9,8},{10,11... | collective-permute-start | bytes 466952 | tf_op jit(solution)/shard_map/ppermute | solution.py:542
  14.5 1.5 %collective-permute-done.1.two_more = bf16[304,256]{1,0:T(8,128)(2,1)S(1)} collective-permute-done((bf16[304,256]{1,0:T(8,128)(2,1)}, bf16[304,256]{1,0:T(8,128)(2,1)S(1)}, u32[]{:S(2)}, u32[]{:S(2)}) %collective-permute-start.1) | collective-permute-done | bytes 155680 | tf_op jit(solution)/shard_map/ppermute | solution.py:542
  16.0 1.6 %collective-permute-start.2 = (bf16[304,256]{1,0:T(8,128)(2,1)S(1)}, bf16[304,256]{1,0:T(8,128)(2,1)S(1)}, u32[]{:S(2)}, u32[]{:S(2)}) collective-permute-start(bf16[304,256]{1,0:T(8,128)(2,1)S(1)} %get-tuple-element.53.refs_0_), channel_id=1, source_target_pairs={{0,2},{1,3},{2,0},{3,1},{4,6},{5,7},{6,4},{7,5},{8,10},{9,11},{10,... | collective-permute-start | bytes 466952 | tf_op jit(solution)/shard_map/ppermute | solution.py:542
  18.9 2.4 %collective-permute-done.2.refs_1_ = bf16[304,256]{1,0:T(8,128)(2,1)S(1)} collective-permute-done((bf16[304,256]{1,0:T(8,128)(2,1)S(1)}, bf16[304,256]{1,0:T(8,128)(2,1)S(1)}, u32[]{:S(2)}, u32[]{:S(2)}) %collective-permute-start.2) | collective-permute-done | bytes 155680 | tf_op jit(solution)/shard_map/ppermute | solution.py:542
  21.3 1.6 %collective-permute-done.3.refs_3_ = bf16[304,256]{1,0:T(8,128)(2,1)S(1)} collective-permute-done((bf16[304,256]{1,0:T(8,128)(2,1)S(1)}, bf16[304,256]{1,0:T(8,128)(2,1)S(1)}, u32[]{:S(2)}, u32[]{:S(2)}) %collective-permute-start.3) | collective-permute-done | bytes 155680 | tf_op jit(solution)/shard_map/ppermute | solution.py:542
  24.1 1.6 %collective-permute-done.4.other = bf16[304,512]{1,0:T(8,128)(2,1)S(1)} collective-permute-done((bf16[304,512]{1,0:T(8,128)(2,1)S(1)}, bf16[304,512]{1,0:T(8,128)(2,1)S(1)}, u32[]{:S(2)}, u32[]{:S(2)}) %collective-permute-start.4) | collective-permute-done | bytes 311328 | tf_op jit(solution)/shard_map/ppermute | solution.py:545
  26.5 1.6 %collective-permute-start.10 = (bf16[144,256]{1,0:T(8,128)(2,1)S(1)}, bf16[144,256]{1,0:T(8,128)(2,1)S(1)}, u32[]{:S(2)}, u32[]{:S(2)}) collective-permute-start(bf16[144,256]{1,0:T(8,128)(2,1)S(1)} %get-tuple-element.64), channel_id=1, source_target_pairs={{0,8},{4,12},{8,0},{12,4},{16,24},{20,28},{24,16},{28,20},{1,9},{5... | collective-permute-start | bytes 221192 | tf_op jit(solution)/shard_map/ppermute | solution.py:539
  28.1 3.1 %collective-permute-start.6 = (bf16[160,256]{1,0:T(8,128)(2,1)S(1)}, bf16[160,256]{1,0:T(8,128)(2,1)S(1)}, u32[]{:S(2)}, u32[]{:S(2)}) collective-permute-start(bf16[160,256]{1,0:T(8,128)(2,1)S(1)} %get-tuple-element.59), channel_id=1, source_target_pairs={{0,16},{4,20},{8,24},{12,28},{16,0},{20,4},{24,8},{28,12},{1,17},{... | collective-permute-start | bytes 245768 | tf_op jit(solution)/shard_map/ppermute | solution.py:539
  33.2 2.5 %collective-permute-start.11 = (bf16[144,256]{1,0:T(8,128)(2,1)S(1)}, bf16[144,256]{1,0:T(8,128)(2,1)S(1)}, u32[]{:S(2)}, u32[]{:S(2)}) collective-permute-start(bf16[144,256]{1,0:T(8,128)(2,1)S(1)} %shard_map.109), channel_id=1, source_target_pairs={{0,16},{4,20},{8,24},{12,28},{16,0},{20,4},{24,8},{28,12},{1,17},{... | collective-permute-start | bytes 221192 | tf_op jit(solution)/shard_map/ppermute | solution.py:539
  35.9 3.7 %collective-permute-done.8.refs_3_ = bf16[144,256]{1,0:T(8,128)(2,1)S(1)} collective-permute-done((bf16[144,256]{1,0:T(8,128)(2,1)S(1)}, bf16[144,256]{1,0:T(8,128)(2,1)S(1)}, u32[]{:S(2)}, u32[]{:S(2)}) %collective-permute-start.8) | collective-permute-done | bytes 73760 | tf_op jit(solution)/shard_map/ppermute | solution.py:539
  39.6 2.4 %collective-permute-done.11.refs_5_ = bf16[144,256]{1,0:T(8,128)(2,1)S(1)} collective-permute-done((bf16[144,256]{1,0:T(8,128)(2,1)S(1)}, bf16[144,256]{1,0:T(8,128)(2,1)S(1)}, u32[]{:S(2)}, u32[]{:S(2)}) %collective-permute-start.11) | collective-permute-done | bytes 73760 | tf_op jit(solution)/shard_map/ppermute | solution.py:539
  43.4 1.9 %collective-permute-start.14 = (bf16[160,256]{1,0:T(8,128)(2,1)S(1)}, bf16[160,256]{1,0:T(8,128)(2,1)S(1)}, u32[]{:S(2)}, u32[]{:S(2)}) collective-permute-start(bf16[160,256]{1,0:T(8,128)(2,1)S(1)} %get-tuple-element.66), channel_id=1, source_target_pairs={{0,16},{4,20},{8,24},{12,28},{16,0},{20,4},{24,8},{28,12},{1,17},{... | collective-permute-start | bytes 245768 | tf_op jit(solution)/shard_map/ppermute | solution.py:539
  45.3 2.5 %collective-permute-start.13 = (bf16[160,256]{1,0:T(8,128)(2,1)S(1)}, bf16[160,256]{1,0:T(8,128)(2,1)S(1)}, u32[]{:S(2)}, u32[]{:S(2)}) collective-permute-start(bf16[160,256]{1,0:T(8,128)(2,1)S(1)} %get-tuple-element.66), channel_id=1, source_target_pairs={{0,24},{4,28},{8,16},{12,20},{16,8},{20,12},{24,0},{28,4},{1,25},{... | collective-permute-start | bytes 245768 | tf_op jit(solution)/shard_map/ppermute | solution.py:539
  47.7 2.0 %collective-permute-start.15 = (bf16[144,256]{1,0:T(8,128)(2,1)S(1)}, bf16[144,256]{1,0:T(8,128)(2,1)S(1)}, u32[]{:S(2)}, u32[]{:S(2)}) collective-permute-start(bf16[144,256]{1,0:T(8,128)(2,1)S(1)} %get-tuple-element.67), channel_id=1, source_target_pairs={{0,8},{4,12},{8,0},{12,4},{16,24},{20,28},{24,16},{28,20},{1,9},{5... | collective-permute-start | bytes 221192 | tf_op jit(solution)/shard_map/ppermute | solution.py:539
  49.7 1.9 %collective-permute-done.16.refs_5_ = bf16[144,256]{1,0:T(8,128)(2,1)S(1)} collective-permute-done((bf16[144,256]{1,0:T(8,128)(2,1)S(1)}, bf16[144,256]{1,0:T(8,128)(2,1)S(1)}, u32[]{:S(2)}, u32[]{:S(2)}) %collective-permute-start.16) | collective-permute-done | bytes 73760 | tf_op jit(solution)/shard_map/ppermute | solution.py:539
  51.7 3.6 %collective-permute-done.15.refs_4_ = bf16[144,256]{1,0:T(8,128)(2,1)S(1)} collective-permute-done((bf16[144,256]{1,0:T(8,128)(2,1)S(1)}, bf16[144,256]{1,0:T(8,128)(2,1)S(1)}, u32[]{:S(2)}, u32[]{:S(2)}) %collective-permute-start.15) | collective-permute-done | bytes 73760 | tf_op jit(solution)/shard_map/ppermute | solution.py:539
  59.2 5.4 %collective-permute-done.19.one_more = bf16[304,256]{1,0:T(8,128)(2,1)S(1)} collective-permute-done((bf16[304,256]{1,0:T(8,128)(2,1)S(1)}, bf16[304,256]{1,0:T(8,128)(2,1)S(1)}, u32[]{:S(2)}, u32[]{:S(2)}) %collective-permute-start.19) | collective-permute-done | bytes 155680 | tf_op jit(solution)/shard_map/ppermute | solution.py:542
  65.2 1.6 %collective-permute-start.22 = (bf16[304,256]{1,0:T(8,128)(2,1)S(1)}, bf16[304,256]{1,0:T(8,128)(2,1)S(1)}, u32[]{:S(2)}, u32[]{:S(2)}) collective-permute-start(bf16[304,256]{1,0:T(8,128)(2,1)S(1)} %get-tuple-element.71.refs_2_), channel_id=1, source_target_pairs={{0,1},{1,0},{2,3},{3,2},{4,5},{5,4},{6,7},{7,6},{8,9},{9,8},{10,11... | collective-permute-start | bytes 466952 | tf_op jit(solution)/shard_map/ppermute | solution.py:542
  66.8 3.2 %collective-permute-done.21.refs_1_ = bf16[304,256]{1,0:T(8,128)(2,1)S(1)} collective-permute-done((bf16[304,256]{1,0:T(8,128)(2,1)S(1)}, bf16[304,256]{1,0:T(8,128)(2,1)S(1)}, u32[]{:S(2)}, u32[]{:S(2)}) %collective-permute-start.21) | collective-permute-done | bytes 155680 | tf_op jit(solution)/shard_map/ppermute | solution.py:542
  71.7 1.6 %collective-permute-done.23.other = bf16[304,512]{1,0:T(8,128)(2,1)S(1)} collective-permute-done((bf16[304,512]{1,0:T(8,128)(2,1)S(1)}, bf16[304,512]{1,0:T(8,128)(2,1)S(1)}, u32[]{:S(2)}, u32[]{:S(2)}) %collective-permute-start.23) | collective-permute-done | bytes 311328 | tf_op jit(solution)/shard_map/ppermute | solution.py:545
  74.2 3.0 %collective-permute-start.24 = (bf16[160,256]{1,0:T(8,128)(2,1)S(1)}, bf16[160,256]{1,0:T(8,128)(2,1)S(1)}, u32[]{:S(2)}, u32[]{:S(2)}) collective-permute-start(bf16[160,256]{1,0:T(8,128)(2,1)S(1)} %get-tuple-element.77), channel_id=1, source_target_pairs={{0,16},{4,20},{8,24},{12,28},{16,0},{20,4},{24,8},{28,12},{1,17},{... | collective-permute-start | bytes 245768 | tf_op jit(solution)/shard_map/ppermute | solution.py:539
  78.6 2.0 %collective-permute-start.26 = (bf16[144,256]{1,0:T(8,128)(2,1)S(1)}, bf16[144,256]{1,0:T(8,128)(2,1)S(1)}, u32[]{:S(2)}, u32[]{:S(2)}) collective-permute-start(bf16[144,256]{1,0:T(8,128)(2,1)S(1)} %get-tuple-element.79), channel_id=1, source_target_pairs={{0,8},{4,12},{8,0},{12,4},{16,24},{20,28},{24,16},{28,20},{1,9},{5... | collective-permute-start | bytes 221192 | tf_op jit(solution)/shard_map/ppermute | solution.py:539
  81.7 5.8 %collective-permute-done.26.refs_3_ = bf16[144,256]{1,0:T(8,128)(2,1)S(1)} collective-permute-done((bf16[144,256]{1,0:T(8,128)(2,1)S(1)}, bf16[144,256]{1,0:T(8,128)(2,1)S(1)}, u32[]{:S(2)}, u32[]{:S(2)}) %collective-permute-start.26) | collective-permute-done | bytes 73760 | tf_op jit(solution)/shard_map/ppermute | solution.py:539
  89.7 1.8 %collective-permute-start.32 = (bf16[160,256]{1,0:T(8,128)(2,1)S(1)}, bf16[160,256]{1,0:T(8,128)(2,1)S(1)}, u32[]{:S(2)}, u32[]{:S(2)}) collective-permute-start(bf16[160,256]{1,0:T(8,128)(2,1)S(1)} %get-tuple-element.85), channel_id=1, source_target_pairs={{0,16},{4,20},{8,24},{12,28},{16,0},{20,4},{24,8},{28,12},{1,17},{... | collective-permute-start | bytes 245768 | tf_op jit(solution)/shard_map/ppermute | solution.py:539
  91.5 2.4 %collective-permute-start.31 = (bf16[160,256]{1,0:T(8,128)(2,1)S(1)}, bf16[160,256]{1,0:T(8,128)(2,1)S(1)}, u32[]{:S(2)}, u32[]{:S(2)}) collective-permute-start(bf16[160,256]{1,0:T(8,128)(2,1)S(1)} %get-tuple-element.85), channel_id=1, source_target_pairs={{0,24},{4,28},{8,16},{12,20},{16,8},{20,12},{24,0},{28,4},{1,25},{... | collective-permute-start | bytes 245768 | tf_op jit(solution)/shard_map/ppermute | solution.py:539
  93.9 2.0 %collective-permute-start.33 = (bf16[144,256]{1,0:T(8,128)(2,1)S(1)}, bf16[144,256]{1,0:T(8,128)(2,1)S(1)}, u32[]{:S(2)}, u32[]{:S(2)}) collective-permute-start(bf16[144,256]{1,0:T(8,128)(2,1)S(1)} %get-tuple-element.86), channel_id=1, source_target_pairs={{0,8},{4,12},{8,0},{12,4},{16,24},{20,28},{24,16},{28,20},{1,9},{5... | collective-permute-start | bytes 221192 | tf_op jit(solution)/shard_map/ppermute | solution.py:539
  96.0 1.5 %collective-permute-done.34.refs_5_ = bf16[144,256]{1,0:T(8,128)(2,1)S(1)} collective-permute-done((bf16[144,256]{1,0:T(8,128)(2,1)S(1)}, bf16[144,256]{1,0:T(8,128)(2,1)S(1)}, u32[]{:S(2)}, u32[]{:S(2)}) %collective-permute-start.34) | collective-permute-done | bytes 73760 | tf_op jit(solution)/shard_map/ppermute | solution.py:539
  97.4 4.1 %collective-permute-done.33.refs_4_ = bf16[144,256]{1,0:T(8,128)(2,1)S(1)} collective-permute-done((bf16[144,256]{1,0:T(8,128)(2,1)S(1)}, bf16[144,256]{1,0:T(8,128)(2,1)S(1)}, u32[]{:S(2)}, u32[]{:S(2)}) %collective-permute-start.33) | collective-permute-done | bytes 73760 | tf_op jit(solution)/shard_map/ppermute | solution.py:539
  104.7 2.9 %collective-permute-start.37 = (bf16[304,128]{1,0:T(8,128)(2,1)S(1)}, bf16[304,128]{1,0:T(8,128)(2,1)S(1)}, u32[]{:S(2)}, u32[]{:S(2)}) collective-permute-start(bf16[304,128]{1,0:T(8,128)(2,1)S(1)} %get-tuple-element.88), channel_id=1, source_target_pairs={{0,3},{1,2},{2,1},{3,0},{4,7},{5,6},{6,5},{7,4},{8,11},{9,10},{10,... | collective-permute-start | bytes 233480 | tf_op jit(solution)/shard_map/ppermute | solution.py:542
  108.3 2.0 %collective-permute-done.37.refs_1_ = bf16[304,128]{1,0:T(8,128)(2,1)S(1)} collective-permute-done((bf16[304,128]{1,0:T(8,128)(2,1)S(1)}, bf16[304,128]{1,0:T(8,128)(2,1)S(1)}, u32[]{:S(2)}, u32[]{:S(2)}) %collective-permute-start.37) | collective-permute-done | bytes 77856 | tf_op jit(solution)/shard_map/ppermute | solution.py:542
  110.3 1.7 %collective-permute-done.38.refs_2_ = bf16[304,128]{1,0:T(8,128)(2,1)S(1)} collective-permute-done((bf16[304,128]{1,0:T(8,128)(2,1)S(1)}, bf16[304,128]{1,0:T(8,128)(2,1)S(1)}, u32[]{:S(2)}, u32[]{:S(2)}) %collective-permute-start.38) | collective-permute-done | bytes 77856 | tf_op jit(solution)/shard_map/ppermute | solution.py:542
  (87 shorter events, 28.9 us)
Async XLA Ops:
  6.5 19.1 %collective-permute-start.5 = (bf16[4,4,128,256]{3,2,1,0:T(8,128)(2,1)}, bf16[4,4,128,256]{3,2,1,0:T(8,128)(2,1)S(1)}, u32[]{:S(2)}, u32[]{:S(2)}) collective-permute-start(bf16[4,4,128,256]{3,2,1,0:T(8,128)(2,1)} %get-tuple-element.57), channel_id=1, source_target_pairs={{0,4},{4,0},{8,12},{12,8},{16,20},{20,16},{24,28},{28,24},{1,5},{5... | collective-permute-start | bytes 3145736 | tf_op jit(solution)/shard_map/ppermute | solution.py:545
  7.1 7.4 %collective-permute-start = (bf16[304,256]{1,0:T(8,128)(2,1)}, bf16[304,256]{1,0:T(8,128)(2,1)S(1)}, u32[]{:S(2)}, u32[]{:S(2)}) collective-permute-start(bf16[304,256]{1,0:T(8,128)(2,1)} %get-tuple-element.49.refs_0_), channel_id=1, source_target_pairs={{0,1},{1,0},{2,3},{3,2},{4,5},{5,4},{6,7},{7,6},{8,9},{9,8},{10,11... | collective-permute-start | bytes 466952 | tf_op jit(solution)/shard_map/ppermute | solution.py:542
  9.9 6.0 %collective-permute-start.1 = (bf16[304,256]{1,0:T(8,128)(2,1)}, bf16[304,256]{1,0:T(8,128)(2,1)S(1)}, u32[]{:S(2)}, u32[]{:S(2)}) collective-permute-start(bf16[304,256]{1,0:T(8,128)(2,1)} %get-tuple-element.50.refs_1_), channel_id=1, source_target_pairs={{0,2},{1,3},{2,0},{3,1},{4,6},{5,7},{6,4},{7,5},{8,10},{9,11},{10,... | collective-permute-start | bytes 466952 | tf_op jit(solution)/shard_map/ppermute | solution.py:542
  16.0 5.3 %collective-permute-start.2 = (bf16[304,256]{1,0:T(8,128)(2,1)S(1)}, bf16[304,256]{1,0:T(8,128)(2,1)S(1)}, u32[]{:S(2)}, u32[]{:S(2)}) collective-permute-start(bf16[304,256]{1,0:T(8,128)(2,1)S(1)} %get-tuple-element.53.refs_0_), channel_id=1, source_target_pairs={{0,2},{1,3},{2,0},{3,1},{4,6},{5,7},{6,4},{7,5},{8,10},{9,11},{10,... | collective-permute-start | bytes 466952 | tf_op jit(solution)/shard_map/ppermute | solution.py:542
  17.7 5.2 %collective-permute-start.3 = (bf16[304,256]{1,0:T(8,128)(2,1)S(1)}, bf16[304,256]{1,0:T(8,128)(2,1)S(1)}, u32[]{:S(2)}, u32[]{:S(2)}) collective-permute-start(bf16[304,256]{1,0:T(8,128)(2,1)S(1)} %get-tuple-element.54.refs_2_), channel_id=1, source_target_pairs={{0,1},{1,0},{2,3},{3,2},{4,5},{5,4},{6,7},{7,6},{8,9},{9,8},{10,11... | collective-permute-start | bytes 466952 | tf_op jit(solution)/shard_map/ppermute | solution.py:542
  26.5 6.7 %collective-permute-start.10 = (bf16[144,256]{1,0:T(8,128)(2,1)S(1)}, bf16[144,256]{1,0:T(8,128)(2,1)S(1)}, u32[]{:S(2)}, u32[]{:S(2)}) collective-permute-start(bf16[144,256]{1,0:T(8,128)(2,1)S(1)} %get-tuple-element.64), channel_id=1, source_target_pairs={{0,8},{4,12},{8,0},{12,4},{16,24},{20,28},{24,16},{28,20},{1,9},{5... | collective-permute-start | bytes 221192 | tf_op jit(solution)/shard_map/ppermute | solution.py:539
  28.1 11.5 %collective-permute-start.6 = (bf16[160,256]{1,0:T(8,128)(2,1)S(1)}, bf16[160,256]{1,0:T(8,128)(2,1)S(1)}, u32[]{:S(2)}, u32[]{:S(2)}) collective-permute-start(bf16[160,256]{1,0:T(8,128)(2,1)S(1)} %get-tuple-element.59), channel_id=1, source_target_pairs={{0,16},{4,20},{8,24},{12,28},{16,0},{20,4},{24,8},{28,12},{1,17},{... | collective-permute-start | bytes 245768 | tf_op jit(solution)/shard_map/ppermute | solution.py:539
  31.2 8.4 %collective-permute-start.7 = (bf16[160,256]{1,0:T(8,128)(2,1)S(1)}, bf16[160,256]{1,0:T(8,128)(2,1)S(1)}, u32[]{:S(2)}, u32[]{:S(2)}) collective-permute-start(bf16[160,256]{1,0:T(8,128)(2,1)S(1)} %get-tuple-element.60), channel_id=1, source_target_pairs={{0,24},{4,28},{8,16},{12,20},{16,8},{20,12},{24,0},{28,4},{1,25},{... | collective-permute-start | bytes 245768 | tf_op jit(solution)/shard_map/ppermute | solution.py:539
  31.2 8.4 %collective-permute-start.9 = (bf16[160,256]{1,0:T(8,128)(2,1)S(1)}, bf16[160,256]{1,0:T(8,128)(2,1)S(1)}, u32[]{:S(2)}, u32[]{:S(2)}) collective-permute-start(bf16[160,256]{1,0:T(8,128)(2,1)S(1)} %get-tuple-element.62), channel_id=1, source_target_pairs={{0,8},{4,12},{8,0},{12,4},{16,24},{20,28},{24,16},{28,20},{1,9},{5... | collective-permute-start | bytes 245768 | tf_op jit(solution)/shard_map/ppermute | solution.py:539
  31.7 7.9 %collective-permute-start.8 = (bf16[144,256]{1,0:T(8,128)(2,1)S(1)}, bf16[144,256]{1,0:T(8,128)(2,1)S(1)}, u32[]{:S(2)}, u32[]{:S(2)}) collective-permute-start(bf16[144,256]{1,0:T(8,128)(2,1)S(1)} %get-tuple-element.61), channel_id=1, source_target_pairs={{0,8},{4,12},{8,0},{12,4},{16,24},{20,28},{24,16},{28,20},{1,9},{5... | collective-permute-start | bytes 221192 | tf_op jit(solution)/shard_map/ppermute | solution.py:539
  33.2 8.8 %collective-permute-start.11 = (bf16[144,256]{1,0:T(8,128)(2,1)S(1)}, bf16[144,256]{1,0:T(8,128)(2,1)S(1)}, u32[]{:S(2)}, u32[]{:S(2)}) collective-permute-start(bf16[144,256]{1,0:T(8,128)(2,1)S(1)} %shard_map.109), channel_id=1, source_target_pairs={{0,16},{4,20},{8,24},{12,28},{16,0},{20,4},{24,8},{28,12},{1,17},{... | collective-permute-start | bytes 221192 | tf_op jit(solution)/shard_map/ppermute | solution.py:539
  42.3 9.4 %collective-permute-start.16 = (bf16[144,256]{1,0:T(8,128)(2,1)S(1)}, bf16[144,256]{1,0:T(8,128)(2,1)S(1)}, u32[]{:S(2)}, u32[]{:S(2)}) collective-permute-start(bf16[144,256]{1,0:T(8,128)(2,1)S(1)} %get-tuple-element.67), channel_id=1, source_target_pairs={{0,16},{4,20},{8,24},{12,28},{16,0},{20,4},{24,8},{28,12},{1,17},{... | collective-permute-start | bytes 221192 | tf_op jit(solution)/shard_map/ppermute | solution.py:539
  43.4 12.0 %collective-permute-start.14 = (bf16[160,256]{1,0:T(8,128)(2,1)S(1)}, bf16[160,256]{1,0:T(8,128)(2,1)S(1)}, u32[]{:S(2)}, u32[]{:S(2)}) collective-permute-start(bf16[160,256]{1,0:T(8,128)(2,1)S(1)} %get-tuple-element.66), channel_id=1, source_target_pairs={{0,16},{4,20},{8,24},{12,28},{16,0},{20,4},{24,8},{28,12},{1,17},{... | collective-permute-start | bytes 245768 | tf_op jit(solution)/shard_map/ppermute | solution.py:539
  45.3 10.1 %collective-permute-start.13 = (bf16[160,256]{1,0:T(8,128)(2,1)S(1)}, bf16[160,256]{1,0:T(8,128)(2,1)S(1)}, u32[]{:S(2)}, u32[]{:S(2)}) collective-permute-start(bf16[160,256]{1,0:T(8,128)(2,1)S(1)} %get-tuple-element.66), channel_id=1, source_target_pairs={{0,24},{4,28},{8,16},{12,20},{16,8},{20,12},{24,0},{28,4},{1,25},{... | collective-permute-start | bytes 245768 | tf_op jit(solution)/shard_map/ppermute | solution.py:539
  47.7 7.6 %collective-permute-start.12 = (bf16[160,256]{1,0:T(8,128)(2,1)S(1)}, bf16[160,256]{1,0:T(8,128)(2,1)S(1)}, u32[]{:S(2)}, u32[]{:S(2)}) collective-permute-start(bf16[160,256]{1,0:T(8,128)(2,1)S(1)} %get-tuple-element.66), channel_id=1, source_target_pairs={{0,8},{4,12},{8,0},{12,4},{16,24},{20,28},{24,16},{28,20},{1,9},{5... | collective-permute-start | bytes 245768 | tf_op jit(solution)/shard_map/ppermute | solution.py:539
  47.7 7.6 %collective-permute-start.15 = (bf16[144,256]{1,0:T(8,128)(2,1)S(1)}, bf16[144,256]{1,0:T(8,128)(2,1)S(1)}, u32[]{:S(2)}, u32[]{:S(2)}) collective-permute-start(bf16[144,256]{1,0:T(8,128)(2,1)S(1)} %get-tuple-element.67), channel_id=1, source_target_pairs={{0,8},{4,12},{8,0},{12,4},{16,24},{20,28},{24,16},{28,20},{1,9},{5... | collective-permute-start | bytes 221192 | tf_op jit(solution)/shard_map/ppermute | solution.py:539
  58.4 6.1 %collective-permute-start.19 = (bf16[304,256]{1,0:T(8,128)(2,1)S(1)}, bf16[304,256]{1,0:T(8,128)(2,1)S(1)}, u32[]{:S(2)}, u32[]{:S(2)}) collective-permute-start(bf16[304,256]{1,0:T(8,128)(2,1)S(1)} %get-tuple-element.68.one), channel_id=1, source_target_pairs={{0,1},{1,0},{2,3},{3,2},{4,5},{5,4},{6,7},{7,6},{8,9},{9,8},{10,11... | collective-permute-start | bytes 466952 | tf_op jit(solution)/shard_map/ppermute | solution.py:542
  58.8 5.8 %collective-permute-start.20 = (bf16[304,256]{1,0:T(8,128)(2,1)S(1)}, bf16[304,256]{1,0:T(8,128)(2,1)S(1)}, u32[]{:S(2)}, u32[]{:S(2)}) collective-permute-start(bf16[304,256]{1,0:T(8,128)(2,1)S(1)} %get-tuple-element.69.two), channel_id=1, source_target_pairs={{0,2},{1,3},{2,0},{3,1},{4,6},{5,7},{6,4},{7,5},{8,10},{9,11},{10,... | collective-permute-start | bytes 466952 | tf_op jit(solution)/shard_map/ppermute | solution.py:542
  64.8 5.3 %collective-permute-start.21 = (bf16[304,256]{1,0:T(8,128)(2,1)S(1)}, bf16[304,256]{1,0:T(8,128)(2,1)S(1)}, u32[]{:S(2)}, u32[]{:S(2)}) collective-permute-start(bf16[304,256]{1,0:T(8,128)(2,1)S(1)} %get-tuple-element.70.refs_0_), channel_id=1, source_target_pairs={{0,2},{1,3},{2,0},{3,1},{4,6},{5,7},{6,4},{7,5},{8,10},{9,11},{10,... | collective-permute-start | bytes 466952 | tf_op jit(solution)/shard_map/ppermute | solution.py:542
  65.2 5.2 %collective-permute-start.22 = (bf16[304,256]{1,0:T(8,128)(2,1)S(1)}, bf16[304,256]{1,0:T(8,128)(2,1)S(1)}, u32[]{:S(2)}, u32[]{:S(2)}) collective-permute-start(bf16[304,256]{1,0:T(8,128)(2,1)S(1)} %get-tuple-element.71.refs_2_), channel_id=1, source_target_pairs={{0,1},{1,0},{2,3},{3,2},{4,5},{5,4},{6,7},{7,6},{8,9},{9,8},{10,11... | collective-permute-start | bytes 466952 | tf_op jit(solution)/shard_map/ppermute | solution.py:542
  74.1 6.5 %collective-permute-start.28 = (bf16[144,256]{1,0:T(8,128)(2,1)S(1)}, bf16[144,256]{1,0:T(8,128)(2,1)S(1)}, u32[]{:S(2)}, u32[]{:S(2)}) collective-permute-start(bf16[144,256]{1,0:T(8,128)(2,1)S(1)} %get-tuple-element.82), channel_id=1, source_target_pairs={{0,8},{4,12},{8,0},{12,4},{16,24},{20,28},{24,16},{28,20},{1,9},{5... | collective-permute-start | bytes 221192 | tf_op jit(solution)/shard_map/ppermute | solution.py:539
  74.2 13.3 %collective-permute-start.24 = (bf16[160,256]{1,0:T(8,128)(2,1)S(1)}, bf16[160,256]{1,0:T(8,128)(2,1)S(1)}, u32[]{:S(2)}, u32[]{:S(2)}) collective-permute-start(bf16[160,256]{1,0:T(8,128)(2,1)S(1)} %get-tuple-element.77), channel_id=1, source_target_pairs={{0,16},{4,20},{8,24},{12,28},{16,0},{20,4},{24,8},{28,12},{1,17},{... | collective-permute-start | bytes 245768 | tf_op jit(solution)/shard_map/ppermute | solution.py:539
  77.2 10.3 %collective-permute-start.25 = (bf16[160,256]{1,0:T(8,128)(2,1)S(1)}, bf16[160,256]{1,0:T(8,128)(2,1)S(1)}, u32[]{:S(2)}, u32[]{:S(2)}) collective-permute-start(bf16[160,256]{1,0:T(8,128)(2,1)S(1)} %get-tuple-element.78), channel_id=1, source_target_pairs={{0,24},{4,28},{8,16},{12,20},{16,8},{20,12},{24,0},{28,4},{1,25},{... | collective-permute-start | bytes 245768 | tf_op jit(solution)/shard_map/ppermute | solution.py:539
  78.6 8.9 %collective-permute-start.27 = (bf16[160,256]{1,0:T(8,128)(2,1)S(1)}, bf16[160,256]{1,0:T(8,128)(2,1)S(1)}, u32[]{:S(2)}, u32[]{:S(2)}) collective-permute-start(bf16[160,256]{1,0:T(8,128)(2,1)S(1)} %get-tuple-element.80), channel_id=1, source_target_pairs={{0,8},{4,12},{8,0},{12,4},{16,24},{20,28},{24,16},{28,20},{1,9},{5... | collective-permute-start | bytes 245768 | tf_op jit(solution)/shard_map/ppermute | solution.py:539
  78.6 8.9 %collective-permute-start.26 = (bf16[144,256]{1,0:T(8,128)(2,1)S(1)}, bf16[144,256]{1,0:T(8,128)(2,1)S(1)}, u32[]{:S(2)}, u32[]{:S(2)}) collective-permute-start(bf16[144,256]{1,0:T(8,128)(2,1)S(1)} %get-tuple-element.79), channel_id=1, source_target_pairs={{0,8},{4,12},{8,0},{12,4},{16,24},{20,28},{24,16},{28,20},{1,9},{5... | collective-permute-start | bytes 221192 | tf_op jit(solution)/shard_map/ppermute | solution.py:539
  80.6 7.5 %collective-permute-start.29 = (bf16[144,256]{1,0:T(8,128)(2,1)S(1)}, bf16[144,256]{1,0:T(8,128)(2,1)S(1)}, u32[]{:S(2)}, u32[]{:S(2)}) collective-permute-start(bf16[144,256]{1,0:T(8,128)(2,1)S(1)} %shard_map.118), channel_id=1, source_target_pairs={{0,16},{4,20},{8,24},{12,28},{16,0},{20,4},{24,8},{28,12},{1,17},{... | collective-permute-start | bytes 221192 | tf_op jit(solution)/shard_map/ppermute | solution.py:539
  88.5 8.9 %collective-permute-start.34 = (bf16[144,256]{1,0:T(8,128)(2,1)S(1)}, bf16[144,256]{1,0:T(8,128)(2,1)S(1)}, u32[]{:S(2)}, u32[]{:S(2)}) collective-permute-start(bf16[144,256]{1,0:T(8,128)(2,1)S(1)} %get-tuple-element.86), channel_id=1, source_target_pairs={{0,16},{4,20},{8,24},{12,28},{16,0},{20,4},{24,8},{28,12},{1,17},{... | collective-permute-start | bytes 221192 | tf_op jit(solution)/shard_map/ppermute | solution.py:539
  89.7 11.8 %collective-permute-start.32 = (bf16[160,256]{1,0:T(8,128)(2,1)S(1)}, bf16[160,256]{1,0:T(8,128)(2,1)S(1)}, u32[]{:S(2)}, u32[]{:S(2)}) collective-permute-start(bf16[160,256]{1,0:T(8,128)(2,1)S(1)} %get-tuple-element.85), channel_id=1, source_target_pairs={{0,16},{4,20},{8,24},{12,28},{16,0},{20,4},{24,8},{28,12},{1,17},{... | collective-permute-start | bytes 245768 | tf_op jit(solution)/shard_map/ppermute | solution.py:539
  91.5 10.1 %collective-permute-start.31 = (bf16[160,256]{1,0:T(8,128)(2,1)S(1)}, bf16[160,256]{1,0:T(8,128)(2,1)S(1)}, u32[]{:S(2)}, u32[]{:S(2)}) collective-permute-start(bf16[160,256]{1,0:T(8,128)(2,1)S(1)} %get-tuple-element.85), channel_id=1, source_target_pairs={{0,24},{4,28},{8,16},{12,20},{16,8},{20,12},{24,0},{28,4},{1,25},{... | collective-permute-start | bytes 245768 | tf_op jit(solution)/shard_map/ppermute | solution.py:539
  93.9 7.7 %collective-permute-start.30 = (bf16[160,256]{1,0:T(8,128)(2,1)S(1)}, bf16[160,256]{1,0:T(8,128)(2,1)S(1)}, u32[]{:S(2)}, u32[]{:S(2)}) collective-permute-start(bf16[160,256]{1,0:T(8,128)(2,1)S(1)} %get-tuple-element.85), channel_id=1, source_target_pairs={{0,8},{4,12},{8,0},{12,4},{16,24},{20,28},{24,16},{28,20},{1,9},{5... | collective-permute-start | bytes 245768 | tf_op jit(solution)/shard_map/ppermute | solution.py:539
  93.9 7.6 %collective-permute-start.33 = (bf16[144,256]{1,0:T(8,128)(2,1)S(1)}, bf16[144,256]{1,0:T(8,128)(2,1)S(1)}, u32[]{:S(2)}, u32[]{:S(2)}) collective-permute-start(bf16[144,256]{1,0:T(8,128)(2,1)S(1)} %get-tuple-element.86), channel_id=1, source_target_pairs={{0,8},{4,12},{8,0},{12,4},{16,24},{20,28},{24,16},{28,20},{1,9},{5... | collective-permute-start | bytes 221192 | tf_op jit(solution)/shard_map/ppermute | solution.py:539
  104.7 5.6 %collective-permute-start.37 = (bf16[304,128]{1,0:T(8,128)(2,1)S(1)}, bf16[304,128]{1,0:T(8,128)(2,1)S(1)}, u32[]{:S(2)}, u32[]{:S(2)}) collective-permute-start(bf16[304,128]{1,0:T(8,128)(2,1)S(1)} %get-tuple-element.88), channel_id=1, source_target_pairs={{0,3},{1,2},{2,1},{3,0},{4,7},{5,6},{6,5},{7,4},{8,11},{9,10},{10,... | collective-permute-start | bytes 233480 | tf_op jit(solution)/shard_map/ppermute | solution.py:542
  (14 other events, 87.7 us)

commit v12 on v10

--- a/solution.py
+++ b/solution.py
@@ -325,24 +325,24 @@
         copy.wait()
 
 
-def forward_kernel(sends, members, mine, other, own, partner, *outs):
+def forward_kernel(sends, members, x, tiles, *refs):
     z, core, obs = place()
-    rows, lanes = mine.shape
-    width = own.shape[3]
-    scalars = read_scalars([mine, other], members, 2)
-    for out, (chip, first, count) in zip(outs, sends):
-        zz = z ^ chip
-        y = [
-            jnp.dot(
-                x[first : first + count, :],
-                tiles[zz].reshape(lanes, width),
-                preferred_element_type=F32,
-            )
-            for x, tiles in ((mine, own), (other, partner))
-        ]
-        y = y[0] + y[1]
-        if first + count == rows:
-            y = with_scalars(y, scalars)
+    outs = refs[-len(sends) :]
+    rows, lanes = x.shape
+    width = tiles.shape[3]
+    added = refs[1 : 1 + len(sends)] if len(refs) > len(sends) else [None] * len(sends)
+    if added[0] is not None:
+        scalars = read_scalars([refs[0], x], members, 2)
+    for out, before, (chip, first, count) in zip(outs, added, sends):
+        y = jnp.dot(
+            x[first : first + count, :],
+            tiles[z ^ chip].reshape(lanes, width),
+            preferred_element_type=F32,
+        )
+        if before is not None:
+            y = before[...] + y
+            if first + count == rows:
+                y = with_scalars(y, scalars)
         out[...] = y.astype(out.dtype)
 
 
@@ -397,7 +397,8 @@
     width = ws[0].shape[1]
     acc = None
     for i in range(tiles.shape[0]):
-        w = [ref[...] for ref, (chip, *span) in zip(ws, plan) if chip == i]
+        w = {first: ref for ref, (chip, first, count) in zip(ws, plan) if chip == i}
+        w = [w[first][...] for first in sorted(w)]
         w = w[0] if len(w) == 1 else jnp.concatenate(w, axis=0)
         part = lax.dot_general(
             w, tiles[z ^ i].reshape(lanes, width), NT, preferred_element_type=F32
@@ -512,7 +513,7 @@
     wide = rows + levp - lev + 7
     spread = pltpu.VMEM((wide // 8 * 8, lanes), F32)
     some = rows // 32 * 16
-    some, rest = rows - some, some
+    rest = rows - some
     via = chips == 4
     if via:
         one, two = (0, some), (some, rest)
@@ -576,18 +577,27 @@
         return [x for pair in zip(halves, moved_halves) for x in pair]
 
     def line_sum(moved, other):
+        shapes = [(count, width) for i, unused, count in sends]
+        mine = call(
+            functools.partial(forward_kernel, sends, members),
+            [struct(shape, F32) for shape in shapes],
+            [],
+            product,
+            moved,
+            own,
+        )
         ys = call(
             functools.partial(forward_kernel, sends, members),
             [
-                struct((count, width), F32 if i == 0 or (via and at == 6) else BF16)
-                for at, (i, unused, count) in enumerate(sends)
+                struct(shape, F32 if i == 0 or (via and at == 6) else BF16)
+                for at, ((i, *unused), shape) in enumerate(zip(sends, shapes))
             ],
             [],
-            2 * product,
+            product,
+            other,
+            partner,
             moved,
-            other,
-            own,
-            partner,
+            *mine,
         )
         if not via:
             return [y if i == 0 else along(y, i) for i, y in enumerate(ys)], [(0, rows)] * chips

time: 122 us -> 114 us (0.934)
  waiting for transfers between devices: 58.4 us -> 51.1 us
    ppermute x22, waiting for transfers between devices: 33.9 us -> 27.3 us  [along(): return lax.ppermute(x, 'slab', [(s, s ^ 2 * i) for s in range(n_slab)])]
    pallas_call x20 -> x22, Pallas kernels: 14.2 us -> 14.4 us  [call(): pl.pallas_call(kernel, out_shape=outs, in_specs=[space] * len(args), out_...]
  transfers between devices with their start and end apart: 38 -> 38, of which waited for: 26 -> 27; matrix products, arithmetic and copies ran while one was open for 0% -> 0% of each run, Pallas kernels for 2% -> 3%
where the time goes in v12:
time: 114 us
  waiting for transfers between devices  51.1 us (45%)
  starting transfers between devices  44.9 us (39%)
  Pallas kernels  14.4 us (13%)
  local copies, waits for them, and re-layouts  2.09 us (2%)
  between operations  1.57 us (1%)
    ppermute x22, starting transfers between devices, along(): return lax.ppermute(x, 'slab', [(s, s ^ 2 * i) for s in range(n_slab)])  30.2 us
    ppermute x22, waiting for transfers between devices, along(): return lax.ppermute(x, 'slab', [(s, s ^ 2 * i) for s in range(n_slab)])  27.3 us
    ppermute x11, waiting for transfers between devices, plane(): return lax.ppermute(x, 'obs', [(o, o ^ i) for o in range(n_obs)])  19.6 us
    pallas_call x22, Pallas kernels, call(): pl.pallas_call(kernel, out_shape=outs, in_specs=[space] * len(args), out_...  14.4 us
    ppermute x11, starting transfers between devices, plane(): return lax.ppermute(x, 'obs', [(o, o ^ i) for o in range(n_obs)])  13.8 us
    ppermute x5, waiting for transfers between devices, swap(): return lax.ppermute(x, 'slab', [(s, s ^ 1) for s in range(n_slab)])  4.24 us
  transfers between devices with their start and end apart: 38, of which 27 were waited for; matrix products, arithmetic and copies ran while one was open for 0% of the time, Pallas kernels for 3%

profile of v12, /device:TPU:0, one launch (start us, length us, event | category | flops | bytes accessed | tf_op | source)
XLA Modules:
  0.0 114.1 jit_solution(17313491687076310238)
XLA Ops:
  1.3 5.2 %shard_map.104 = (bf16[4,4,128,256]{3,2,1,0:T(8,128)(2,1)}, bf16[4,4,128,256]{3,2,1,0:T(8,128)(2,1)}, bf16[304,256]{1,0:T(8,128)(2,1)}, bf16[304,256]{1,0:T(8,128)(2,1)}) custom-call(s32[4]{0:T(128)} %seeds_in.1, s32[1,1,32]{2,1,0:T(1,128)} %ids_in.1, s32[1,1,32]{2,1,0:T(1,128)} %cols_in.1, s32[1,1]{1,0:T(1,128)S(6)} %copy.16.count_in, f32[1,128]{1,0:T(1,128)} %refs_4_.1, ...), custom_call_target="tpu_custom_call" | custom-call | flops 637534208 | bytes 5735188 | tf_op jit(solution)/shard_map/pallas_call | solution.py:23
  7.1 2.6 %collective-permute-start = (bf16[304,256]{1,0:T(8,128)(2,1)}, bf16[304,256]{1,0:T(8,128)(2,1)S(1)}, u32[]{:S(2)}, u32[]{:S(2)}) collective-permute-start(bf16[304,256]{1,0:T(8,128)(2,1)} %get-tuple-element.63.refs_0_), channel_id=1, source_target_pairs={{0,1},{1,0},{2,3},{3,2},{4,5},{5,4},{6,7},{7,6},{8,9},{9,8},{10,11... | collective-permute-start | bytes 466952 | tf_op jit(solution)/shard_map/ppermute | solution.py:542
  9.7 2.0 %collective-permute-start.1 = (bf16[304,256]{1,0:T(8,128)(2,1)}, bf16[304,256]{1,0:T(8,128)(2,1)S(1)}, u32[]{:S(2)}, u32[]{:S(2)}) collective-permute-start(bf16[304,256]{1,0:T(8,128)(2,1)} %get-tuple-element.64.refs_1_), channel_id=1, source_target_pairs={{0,2},{1,3},{2,0},{3,1},{4,6},{5,7},{6,4},{7,5},{8,10},{9,11},{10,... | collective-permute-start | bytes 466952 | tf_op jit(solution)/shard_map/ppermute | solution.py:542
  14.5 1.7 %collective-permute-done.1.two_more = bf16[304,256]{1,0:T(8,128)(2,1)S(1)} collective-permute-done((bf16[304,256]{1,0:T(8,128)(2,1)}, bf16[304,256]{1,0:T(8,128)(2,1)S(1)}, u32[]{:S(2)}, u32[]{:S(2)}) %collective-permute-start.1) | collective-permute-done | bytes 155680 | tf_op jit(solution)/shard_map/ppermute | solution.py:542
  16.3 1.8 %collective-permute-start.2 = (bf16[304,256]{1,0:T(8,128)(2,1)S(1)}, bf16[304,256]{1,0:T(8,128)(2,1)S(1)}, u32[]{:S(2)}, u32[]{:S(2)}) collective-permute-start(bf16[304,256]{1,0:T(8,128)(2,1)S(1)} %get-tuple-element.67.refs_0_), channel_id=1, source_target_pairs={{0,2},{1,3},{2,0},{3,1},{4,6},{5,7},{6,4},{7,5},{8,10},{9,11},{10,... | collective-permute-start | bytes 466952 | tf_op jit(solution)/shard_map/ppermute | solution.py:542
  18.9 3.0 %collective-permute-done.2.refs_1_ = bf16[304,256]{1,0:T(8,128)(2,1)S(1)} collective-permute-done((bf16[304,256]{1,0:T(8,128)(2,1)S(1)}, bf16[304,256]{1,0:T(8,128)(2,1)S(1)}, u32[]{:S(2)}, u32[]{:S(2)}) %collective-permute-start.2) | collective-permute-done | bytes 155680 | tf_op jit(solution)/shard_map/ppermute | solution.py:542
  21.9 1.4 %collective-permute-done.3.refs_3_ = bf16[304,256]{1,0:T(8,128)(2,1)S(1)} collective-permute-done((bf16[304,256]{1,0:T(8,128)(2,1)S(1)}, bf16[304,256]{1,0:T(8,128)(2,1)S(1)}, u32[]{:S(2)}, u32[]{:S(2)}) %collective-permute-start.3) | collective-permute-done | bytes 155680 | tf_op jit(solution)/shard_map/ppermute | solution.py:542
  27.8 2.5 %collective-permute-start.6 = (bf16[160,256]{1,0:T(8,128)(2,1)S(1)}, bf16[160,256]{1,0:T(8,128)(2,1)S(1)}, u32[]{:S(2)}, u32[]{:S(2)}) collective-permute-start(bf16[160,256]{1,0:T(8,128)(2,1)S(1)} %get-tuple-element.80), channel_id=1, source_target_pairs={{0,16},{4,20},{8,24},{12,28},{16,0},{20,4},{24,8},{28,12},{1,17},{... | collective-permute-start | bytes 245768 | tf_op jit(solution)/shard_map/ppermute | solution.py:539
  31.3 1.8 %collective-permute-start.8 = (bf16[144,256]{1,0:T(8,128)(2,1)S(1)}, bf16[144,256]{1,0:T(8,128)(2,1)S(1)}, u32[]{:S(2)}, u32[]{:S(2)}) collective-permute-start(bf16[144,256]{1,0:T(8,128)(2,1)S(1)} %get-tuple-element.82), channel_id=1, source_target_pairs={{0,8},{4,12},{8,0},{12,4},{16,24},{20,28},{24,16},{28,20},{1,9},{5... | collective-permute-start | bytes 221192 | tf_op jit(solution)/shard_map/ppermute | solution.py:539
  33.1 1.8 %collective-permute-start.11 = (bf16[144,256]{1,0:T(8,128)(2,1)S(1)}, bf16[144,256]{1,0:T(8,128)(2,1)S(1)}, u32[]{:S(2)}, u32[]{:S(2)}) collective-permute-start(bf16[144,256]{1,0:T(8,128)(2,1)S(1)} %shard_map.110), channel_id=1, source_target_pairs={{0,16},{4,20},{8,24},{12,28},{16,0},{20,4},{24,8},{28,12},{1,17},{... | collective-permute-start | bytes 221192 | tf_op jit(solution)/shard_map/ppermute | solution.py:539
  35.1 4.3 %collective-permute-done.8.refs_3_ = bf16[144,256]{1,0:T(8,128)(2,1)S(1)} collective-permute-done((bf16[144,256]{1,0:T(8,128)(2,1)S(1)}, bf16[144,256]{1,0:T(8,128)(2,1)S(1)}, u32[]{:S(2)}, u32[]{:S(2)}) %collective-permute-start.8) | collective-permute-done | bytes 73760 | tf_op jit(solution)/shard_map/ppermute | solution.py:539
  39.4 1.4 %collective-permute-done.11.refs_5_ = bf16[144,256]{1,0:T(8,128)(2,1)S(1)} collective-permute-done((bf16[144,256]{1,0:T(8,128)(2,1)S(1)}, bf16[144,256]{1,0:T(8,128)(2,1)S(1)}, u32[]{:S(2)}, u32[]{:S(2)}) %collective-permute-start.11) | collective-permute-done | bytes 73760 | tf_op jit(solution)/shard_map/ppermute | solution.py:539
  40.9 1.4 %collective-permute-start.12 = (bf16[304,256]{1,0:T(8,128)(2,1)S(1)}, bf16[304,256]{1,0:T(8,128)(2,1)S(1)}, u32[]{:S(2)}, u32[]{:S(2)}) collective-permute-start(bf16[304,256]{1,0:T(8,128)(2,1)S(1)} %get-tuple-element.86.refs_0_), channel_id=1, source_target_pairs={{0,8},{4,12},{8,0},{12,4},{16,24},{20,28},{24,16},{28,20},{1,9},{5... | collective-permute-start | bytes 466952 | tf_op jit(solution)/shard_map/ppermute | solution.py:539
  42.3 2.8 %collective-permute-start.13 = (bf16[144,256]{1,0:T(8,128)(2,1)S(1)}, bf16[144,256]{1,0:T(8,128)(2,1)S(1)}, u32[]{:S(2)}, u32[]{:S(2)}) collective-permute-start(bf16[144,256]{1,0:T(8,128)(2,1)S(1)} %get-tuple-element.87), channel_id=1, source_target_pairs={{0,16},{4,20},{8,24},{12,28},{16,0},{20,4},{24,8},{28,12},{1,17},{... | collective-permute-start | bytes 221192 | tf_op jit(solution)/shard_map/ppermute | solution.py:539
  46.6 2.9 %collective-permute-done.13.refs_2_ = bf16[144,256]{1,0:T(8,128)(2,1)S(1)} collective-permute-done((bf16[144,256]{1,0:T(8,128)(2,1)S(1)}, bf16[144,256]{1,0:T(8,128)(2,1)S(1)}, u32[]{:S(2)}, u32[]{:S(2)}) %collective-permute-start.13) | collective-permute-done | bytes 73760 | tf_op jit(solution)/shard_map/ppermute | solution.py:539
  49.5 3.2 %collective-permute-start.15 = (bf16[144,256]{1,0:T(8,128)(2,1)S(1)}, bf16[144,256]{1,0:T(8,128)(2,1)S(1)}, u32[]{:S(2)}, u32[]{:S(2)}) collective-permute-start(bf16[144,256]{1,0:T(8,128)(2,1)S(1)} %collective-permute-done.13.refs_2_), channel_id=1, source_target_pairs={{0,8},{4,12},{8,0},{12,4},{16,24},{20,28},{24,16},{28,20},{1,9},{5... | collective-permute-start | bytes 221192 | tf_op jit(solution)/shard_map/ppermute | solution.py:539
  52.8 3.2 %collective-permute-done.14.refs_3_ = bf16[160,256]{1,0:T(8,128)(2,1)S(1)} collective-permute-done((bf16[160,256]{1,0:T(8,128)(2,1)S(1)}, bf16[160,256]{1,0:T(8,128)(2,1)S(1)}, u32[]{:S(2)}, u32[]{:S(2)}) %collective-permute-start.14) | collective-permute-done | bytes 81952 | tf_op jit(solution)/shard_map/ppermute | solution.py:539
  59.8 4.8 %collective-permute-done.18.one_more = bf16[304,256]{1,0:T(8,128)(2,1)S(1)} collective-permute-done((bf16[304,256]{1,0:T(8,128)(2,1)S(1)}, bf16[304,256]{1,0:T(8,128)(2,1)S(1)}, u32[]{:S(2)}, u32[]{:S(2)}) %collective-permute-start.18) | collective-permute-done | bytes 155680 | tf_op jit(solution)/shard_map/ppermute | solution.py:542
  66.8 3.3 %collective-permute-done.20.refs_1_ = bf16[304,256]{1,0:T(8,128)(2,1)S(1)} collective-permute-done((bf16[304,256]{1,0:T(8,128)(2,1)S(1)}, bf16[304,256]{1,0:T(8,128)(2,1)S(1)}, u32[]{:S(2)}, u32[]{:S(2)}) %collective-permute-start.20) | collective-permute-done | bytes 155680 | tf_op jit(solution)/shard_map/ppermute | solution.py:542
  74.8 3.7 %collective-permute-start.23 = (bf16[160,256]{1,0:T(8,128)(2,1)S(1)}, bf16[160,256]{1,0:T(8,128)(2,1)S(1)}, u32[]{:S(2)}, u32[]{:S(2)}) collective-permute-start(bf16[160,256]{1,0:T(8,128)(2,1)S(1)} %get-tuple-element.105), channel_id=1, source_target_pairs={{0,16},{4,20},{8,24},{12,28},{16,0},{20,4},{24,8},{28,12},{1,17},{... | collective-permute-start | bytes 245768 | tf_op jit(solution)/shard_map/ppermute | solution.py:539
  79.0 1.9 %collective-permute-start.25 = (bf16[144,256]{1,0:T(8,128)(2,1)S(1)}, bf16[144,256]{1,0:T(8,128)(2,1)S(1)}, u32[]{:S(2)}, u32[]{:S(2)}) collective-permute-start(bf16[144,256]{1,0:T(8,128)(2,1)S(1)} %get-tuple-element.107), channel_id=1, source_target_pairs={{0,8},{4,12},{8,0},{12,4},{16,24},{20,28},{24,16},{28,20},{1,9},{5... | collective-permute-start | bytes 221192 | tf_op jit(solution)/shard_map/ppermute | solution.py:539
  81.0 2.0 %collective-permute-start.28 = (bf16[144,256]{1,0:T(8,128)(2,1)S(1)}, bf16[144,256]{1,0:T(8,128)(2,1)S(1)}, u32[]{:S(2)}, u32[]{:S(2)}) collective-permute-start(bf16[144,256]{1,0:T(8,128)(2,1)S(1)} %shard_map.120), channel_id=1, source_target_pairs={{0,16},{4,20},{8,24},{12,28},{16,0},{20,4},{24,8},{28,12},{1,17},{... | collective-permute-start | bytes 221192 | tf_op jit(solution)/shard_map/ppermute | solution.py:539
  82.9 4.1 %collective-permute-done.25.refs_3_ = bf16[144,256]{1,0:T(8,128)(2,1)S(1)} collective-permute-done((bf16[144,256]{1,0:T(8,128)(2,1)S(1)}, bf16[144,256]{1,0:T(8,128)(2,1)S(1)}, u32[]{:S(2)}, u32[]{:S(2)}) %collective-permute-start.25) | collective-permute-done | bytes 73760 | tf_op jit(solution)/shard_map/ppermute | solution.py:539
  87.1 2.2 %collective-permute-done.28.refs_5_ = bf16[144,256]{1,0:T(8,128)(2,1)S(1)} collective-permute-done((bf16[144,256]{1,0:T(8,128)(2,1)S(1)}, bf16[144,256]{1,0:T(8,128)(2,1)S(1)}, u32[]{:S(2)}, u32[]{:S(2)}) %collective-permute-start.28) | collective-permute-done | bytes 73760 | tf_op jit(solution)/shard_map/ppermute | solution.py:539
  90.2 2.6 %collective-permute-start.30 = (bf16[144,256]{1,0:T(8,128)(2,1)S(1)}, bf16[144,256]{1,0:T(8,128)(2,1)S(1)}, u32[]{:S(2)}, u32[]{:S(2)}) collective-permute-start(bf16[144,256]{1,0:T(8,128)(2,1)S(1)} %get-tuple-element.113), channel_id=1, source_target_pairs={{0,16},{4,20},{8,24},{12,28},{16,0},{20,4},{24,8},{28,12},{1,17},{... | collective-permute-start | bytes 221192 | tf_op jit(solution)/shard_map/ppermute | solution.py:539
  92.8 1.4 %collective-permute-start.33 = (bf16[160,256]{1,0:T(8,128)(2,1)S(1)}, bf16[160,256]{1,0:T(8,128)(2,1)S(1)}, u32[]{:S(2)}, u32[]{:S(2)}) collective-permute-start(bf16[160,256]{1,0:T(8,128)(2,1)S(1)} %get-tuple-element.114), channel_id=1, source_target_pairs={{0,24},{4,28},{8,16},{12,20},{16,8},{20,12},{24,0},{28,4},{1,25},{... | collective-permute-start | bytes 245768 | tf_op jit(solution)/shard_map/ppermute | solution.py:539
  94.3 4.2 %collective-permute-done.30.refs_2_ = bf16[144,256]{1,0:T(8,128)(2,1)S(1)} collective-permute-done((bf16[144,256]{1,0:T(8,128)(2,1)S(1)}, bf16[144,256]{1,0:T(8,128)(2,1)S(1)}, u32[]{:S(2)}, u32[]{:S(2)}) %collective-permute-start.30) | collective-permute-done | bytes 73760 | tf_op jit(solution)/shard_map/ppermute | solution.py:539
  98.5 1.3 %collective-permute-done.33.refs_5_ = bf16[160,256]{1,0:T(8,128)(2,1)S(1)} collective-permute-done((bf16[160,256]{1,0:T(8,128)(2,1)S(1)}, bf16[160,256]{1,0:T(8,128)(2,1)S(1)}, u32[]{:S(2)}, u32[]{:S(2)}) %collective-permute-start.33) | collective-permute-done | bytes 81952 | tf_op jit(solution)/shard_map/ppermute | solution.py:539
  99.8 2.6 %collective-permute-done.31.refs_3_ = bf16[160,256]{1,0:T(8,128)(2,1)S(1)} collective-permute-done((bf16[160,256]{1,0:T(8,128)(2,1)S(1)}, bf16[160,256]{1,0:T(8,128)(2,1)S(1)}, u32[]{:S(2)}, u32[]{:S(2)}) %collective-permute-start.31) | collective-permute-done | bytes 81952 | tf_op jit(solution)/shard_map/ppermute | solution.py:539
  105.5 2.8 %collective-permute-start.35 = (bf16[304,128]{1,0:T(8,128)(2,1)S(1)}, bf16[304,128]{1,0:T(8,128)(2,1)S(1)}, u32[]{:S(2)}, u32[]{:S(2)}) collective-permute-start(bf16[304,128]{1,0:T(8,128)(2,1)S(1)} %get-tuple-element.116), channel_id=1, source_target_pairs={{0,3},{1,2},{2,1},{3,0},{4,7},{5,6},{6,5},{7,4},{8,11},{9,10},{10,... | collective-permute-start | bytes 233480 | tf_op jit(solution)/shard_map/ppermute | solution.py:542
  109.1 1.9 %collective-permute-done.35.refs_1_ = bf16[304,128]{1,0:T(8,128)(2,1)S(1)} collective-permute-done((bf16[304,128]{1,0:T(8,128)(2,1)S(1)}, bf16[304,128]{1,0:T(8,128)(2,1)S(1)}, u32[]{:S(2)}, u32[]{:S(2)}) %collective-permute-start.35) | collective-permute-done | bytes 77856 | tf_op jit(solution)/shard_map/ppermute | solution.py:542
  111.0 1.7 %collective-permute-done.36.refs_2_ = bf16[304,128]{1,0:T(8,128)(2,1)S(1)} collective-permute-done((bf16[304,128]{1,0:T(8,128)(2,1)S(1)}, bf16[304,128]{1,0:T(8,128)(2,1)S(1)}, u32[]{:S(2)}, u32[]{:S(2)}) %collective-permute-start.36) | collective-permute-done | bytes 77856 | tf_op jit(solution)/shard_map/ppermute | solution.py:542
  (85 shorter events, 29.2 us)
Async XLA Ops:
  6.5 19.6 %collective-permute-start.5 = (bf16[4,4,128,256]{3,2,1,0:T(8,128)(2,1)}, bf16[4,4,128,256]{3,2,1,0:T(8,128)(2,1)S(1)}, u32[]{:S(2)}, u32[]{:S(2)}) collective-permute-start(bf16[4,4,128,256]{3,2,1,0:T(8,128)(2,1)} %get-tuple-element.70), channel_id=1, source_target_pairs={{0,4},{4,0},{8,12},{12,8},{16,20},{20,16},{24,28},{28,24},{1,5},{5... | collective-permute-start | bytes 3145736 | tf_op jit(solution)/shard_map/ppermute | solution.py:545
  7.1 7.4 %collective-permute-start = (bf16[304,256]{1,0:T(8,128)(2,1)}, bf16[304,256]{1,0:T(8,128)(2,1)S(1)}, u32[]{:S(2)}, u32[]{:S(2)}) collective-permute-start(bf16[304,256]{1,0:T(8,128)(2,1)} %get-tuple-element.63.refs_0_), channel_id=1, source_target_pairs={{0,1},{1,0},{2,3},{3,2},{4,5},{5,4},{6,7},{7,6},{8,9},{9,8},{10,11... | collective-permute-start | bytes 466952 | tf_op jit(solution)/shard_map/ppermute | solution.py:542
  9.7 6.6 %collective-permute-start.1 = (bf16[304,256]{1,0:T(8,128)(2,1)}, bf16[304,256]{1,0:T(8,128)(2,1)S(1)}, u32[]{:S(2)}, u32[]{:S(2)}) collective-permute-start(bf16[304,256]{1,0:T(8,128)(2,1)} %get-tuple-element.64.refs_1_), channel_id=1, source_target_pairs={{0,2},{1,3},{2,0},{3,1},{4,6},{5,7},{6,4},{7,5},{8,10},{9,11},{10,... | collective-permute-start | bytes 466952 | tf_op jit(solution)/shard_map/ppermute | solution.py:542
  16.3 5.6 %collective-permute-start.2 = (bf16[304,256]{1,0:T(8,128)(2,1)S(1)}, bf16[304,256]{1,0:T(8,128)(2,1)S(1)}, u32[]{:S(2)}, u32[]{:S(2)}) collective-permute-start(bf16[304,256]{1,0:T(8,128)(2,1)S(1)} %get-tuple-element.67.refs_0_), channel_id=1, source_target_pairs={{0,2},{1,3},{2,0},{3,1},{4,6},{5,7},{6,4},{7,5},{8,10},{9,11},{10,... | collective-permute-start | bytes 466952 | tf_op jit(solution)/shard_map/ppermute | solution.py:542
  18.1 5.2 %collective-permute-start.3 = (bf16[304,256]{1,0:T(8,128)(2,1)S(1)}, bf16[304,256]{1,0:T(8,128)(2,1)S(1)}, u32[]{:S(2)}, u32[]{:S(2)}) collective-permute-start(bf16[304,256]{1,0:T(8,128)(2,1)S(1)} %get-tuple-element.68.refs_2_), channel_id=1, source_target_pairs={{0,1},{1,0},{2,3},{3,2},{4,5},{5,4},{6,7},{7,6},{8,9},{9,8},{10,11... | collective-permute-start | bytes 466952 | tf_op jit(solution)/shard_map/ppermute | solution.py:542
  26.6 6.5 %collective-permute-start.10 = (bf16[144,256]{1,0:T(8,128)(2,1)S(1)}, bf16[144,256]{1,0:T(8,128)(2,1)S(1)}, u32[]{:S(2)}, u32[]{:S(2)}) collective-permute-start(bf16[144,256]{1,0:T(8,128)(2,1)S(1)} %get-tuple-element.85), channel_id=1, source_target_pairs={{0,8},{4,12},{8,0},{12,4},{16,24},{20,28},{24,16},{28,20},{1,9},{5... | collective-permute-start | bytes 221192 | tf_op jit(solution)/shard_map/ppermute | solution.py:539
  27.8 11.6 %collective-permute-start.6 = (bf16[160,256]{1,0:T(8,128)(2,1)S(1)}, bf16[160,256]{1,0:T(8,128)(2,1)S(1)}, u32[]{:S(2)}, u32[]{:S(2)}) collective-permute-start(bf16[160,256]{1,0:T(8,128)(2,1)S(1)} %get-tuple-element.80), channel_id=1, source_target_pairs={{0,16},{4,20},{8,24},{12,28},{16,0},{20,4},{24,8},{28,12},{1,17},{... | collective-permute-start | bytes 245768 | tf_op jit(solution)/shard_map/ppermute | solution.py:539
  30.3 9.1 %collective-permute-start.7 = (bf16[160,256]{1,0:T(8,128)(2,1)S(1)}, bf16[160,256]{1,0:T(8,128)(2,1)S(1)}, u32[]{:S(2)}, u32[]{:S(2)}) collective-permute-start(bf16[160,256]{1,0:T(8,128)(2,1)S(1)} %get-tuple-element.81), channel_id=1, source_target_pairs={{0,24},{4,28},{8,16},{12,20},{16,8},{20,12},{24,0},{28,4},{1,25},{... | collective-permute-start | bytes 245768 | tf_op jit(solution)/shard_map/ppermute | solution.py:539
  31.1 8.3 %collective-permute-start.9 = (bf16[160,256]{1,0:T(8,128)(2,1)S(1)}, bf16[160,256]{1,0:T(8,128)(2,1)S(1)}, u32[]{:S(2)}, u32[]{:S(2)}) collective-permute-start(bf16[160,256]{1,0:T(8,128)(2,1)S(1)} %get-tuple-element.83), channel_id=1, source_target_pairs={{0,8},{4,12},{8,0},{12,4},{16,24},{20,28},{24,16},{28,20},{1,9},{5... | collective-permute-start | bytes 245768 | tf_op jit(solution)/shard_map/ppermute | solution.py:539
  31.3 8.1 %collective-permute-start.8 = (bf16[144,256]{1,0:T(8,128)(2,1)S(1)}, bf16[144,256]{1,0:T(8,128)(2,1)S(1)}, u32[]{:S(2)}, u32[]{:S(2)}) collective-permute-start(bf16[144,256]{1,0:T(8,128)(2,1)S(1)} %get-tuple-element.82), channel_id=1, source_target_pairs={{0,8},{4,12},{8,0},{12,4},{16,24},{20,28},{24,16},{28,20},{1,9},{5... | collective-permute-start | bytes 221192 | tf_op jit(solution)/shard_map/ppermute | solution.py:539
  33.1 7.6 %collective-permute-start.11 = (bf16[144,256]{1,0:T(8,128)(2,1)S(1)}, bf16[144,256]{1,0:T(8,128)(2,1)S(1)}, u32[]{:S(2)}, u32[]{:S(2)}) collective-permute-start(bf16[144,256]{1,0:T(8,128)(2,1)S(1)} %shard_map.110), channel_id=1, source_target_pairs={{0,16},{4,20},{8,24},{12,28},{16,0},{20,4},{24,8},{28,12},{1,17},{... | collective-permute-start | bytes 221192 | tf_op jit(solution)/shard_map/ppermute | solution.py:539
  40.9 15.2 %collective-permute-start.12 = (bf16[304,256]{1,0:T(8,128)(2,1)S(1)}, bf16[304,256]{1,0:T(8,128)(2,1)S(1)}, u32[]{:S(2)}, u32[]{:S(2)}) collective-permute-start(bf16[304,256]{1,0:T(8,128)(2,1)S(1)} %get-tuple-element.86.refs_0_), channel_id=1, source_target_pairs={{0,8},{4,12},{8,0},{12,4},{16,24},{20,28},{24,16},{28,20},{1,9},{5... | collective-permute-start | bytes 466952 | tf_op jit(solution)/shard_map/ppermute | solution.py:539
  42.3 7.2 %collective-permute-start.13 = (bf16[144,256]{1,0:T(8,128)(2,1)S(1)}, bf16[144,256]{1,0:T(8,128)(2,1)S(1)}, u32[]{:S(2)}, u32[]{:S(2)}) collective-permute-start(bf16[144,256]{1,0:T(8,128)(2,1)S(1)} %get-tuple-element.87), channel_id=1, source_target_pairs={{0,16},{4,20},{8,24},{12,28},{16,0},{20,4},{24,8},{28,12},{1,17},{... | collective-permute-start | bytes 221192 | tf_op jit(solution)/shard_map/ppermute | solution.py:539
  45.1 7.7 %collective-permute-start.16 = (bf16[160,256]{1,0:T(8,128)(2,1)S(1)}, bf16[160,256]{1,0:T(8,128)(2,1)S(1)}, u32[]{:S(2)}, u32[]{:S(2)}) collective-permute-start(bf16[160,256]{1,0:T(8,128)(2,1)S(1)} %get-tuple-element.88), channel_id=1, source_target_pairs={{0,24},{4,28},{8,16},{12,20},{16,8},{20,12},{24,0},{28,4},{1,25},{... | collective-permute-start | bytes 245768 | tf_op jit(solution)/shard_map/ppermute | solution.py:539
  45.4 10.6 %collective-permute-start.14 = (bf16[160,256]{1,0:T(8,128)(2,1)S(1)}, bf16[160,256]{1,0:T(8,128)(2,1)S(1)}, u32[]{:S(2)}, u32[]{:S(2)}) collective-permute-start(bf16[160,256]{1,0:T(8,128)(2,1)S(1)} %get-tuple-element.88), channel_id=1, source_target_pairs={{0,16},{4,20},{8,24},{12,28},{16,0},{20,4},{24,8},{28,12},{1,17},{... | collective-permute-start | bytes 245768 | tf_op jit(solution)/shard_map/ppermute | solution.py:539
  49.5 6.6 %collective-permute-start.15 = (bf16[144,256]{1,0:T(8,128)(2,1)S(1)}, bf16[144,256]{1,0:T(8,128)(2,1)S(1)}, u32[]{:S(2)}, u32[]{:S(2)}) collective-permute-start(bf16[144,256]{1,0:T(8,128)(2,1)S(1)} %collective-permute-done.13.refs_2_), channel_id=1, source_target_pairs={{0,8},{4,12},{8,0},{12,4},{16,24},{20,28},{24,16},{28,20},{1,9},{5... | collective-permute-start | bytes 221192 | tf_op jit(solution)/shard_map/ppermute | solution.py:539
  58.5 6.1 %collective-permute-start.18 = (bf16[304,256]{1,0:T(8,128)(2,1)S(1)}, bf16[304,256]{1,0:T(8,128)(2,1)S(1)}, u32[]{:S(2)}, u32[]{:S(2)}) collective-permute-start(bf16[304,256]{1,0:T(8,128)(2,1)S(1)} %get-tuple-element.89.one), channel_id=1, source_target_pairs={{0,1},{1,0},{2,3},{3,2},{4,5},{5,4},{6,7},{7,6},{8,9},{9,8},{10,11... | collective-permute-start | bytes 466952 | tf_op jit(solution)/shard_map/ppermute | solution.py:542
  58.8 5.9 %collective-permute-start.19 = (bf16[304,256]{1,0:T(8,128)(2,1)S(1)}, bf16[304,256]{1,0:T(8,128)(2,1)S(1)}, u32[]{:S(2)}, u32[]{:S(2)}) collective-permute-start(bf16[304,256]{1,0:T(8,128)(2,1)S(1)} %get-tuple-element.90.two), channel_id=1, source_target_pairs={{0,2},{1,3},{2,0},{3,1},{4,6},{5,7},{6,4},{7,5},{8,10},{9,11},{10,... | collective-permute-start | bytes 466952 | tf_op jit(solution)/shard_map/ppermute | solution.py:542
  64.8 5.3 %collective-permute-start.20 = (bf16[304,256]{1,0:T(8,128)(2,1)S(1)}, bf16[304,256]{1,0:T(8,128)(2,1)S(1)}, u32[]{:S(2)}, u32[]{:S(2)}) collective-permute-start(bf16[304,256]{1,0:T(8,128)(2,1)S(1)} %get-tuple-element.91.refs_0_), channel_id=1, source_target_pairs={{0,2},{1,3},{2,0},{3,1},{4,6},{5,7},{6,4},{7,5},{8,10},{9,11},{10,... | collective-permute-start | bytes 466952 | tf_op jit(solution)/shard_map/ppermute | solution.py:542
  65.8 5.2 %collective-permute-start.21 = (bf16[304,256]{1,0:T(8,128)(2,1)S(1)}, bf16[304,256]{1,0:T(8,128)(2,1)S(1)}, u32[]{:S(2)}, u32[]{:S(2)}) collective-permute-start(bf16[304,256]{1,0:T(8,128)(2,1)S(1)} %get-tuple-element.92.refs_2_), channel_id=1, source_target_pairs={{0,1},{1,0},{2,3},{3,2},{4,5},{5,4},{6,7},{7,6},{8,9},{9,8},{10,11... | collective-permute-start | bytes 466952 | tf_op jit(solution)/shard_map/ppermute | solution.py:542
  74.5 6.5 %collective-permute-start.27 = (bf16[144,256]{1,0:T(8,128)(2,1)S(1)}, bf16[144,256]{1,0:T(8,128)(2,1)S(1)}, u32[]{:S(2)}, u32[]{:S(2)}) collective-permute-start(bf16[144,256]{1,0:T(8,128)(2,1)S(1)} %get-tuple-element.110), channel_id=1, source_target_pairs={{0,8},{4,12},{8,0},{12,4},{16,24},{20,28},{24,16},{28,20},{1,9},{5... | collective-permute-start | bytes 221192 | tf_op jit(solution)/shard_map/ppermute | solution.py:539
  74.8 12.3 %collective-permute-start.23 = (bf16[160,256]{1,0:T(8,128)(2,1)S(1)}, bf16[160,256]{1,0:T(8,128)(2,1)S(1)}, u32[]{:S(2)}, u32[]{:S(2)}) collective-permute-start(bf16[160,256]{1,0:T(8,128)(2,1)S(1)} %get-tuple-element.105), channel_id=1, source_target_pairs={{0,16},{4,20},{8,24},{12,28},{16,0},{20,4},{24,8},{28,12},{1,17},{... | collective-permute-start | bytes 245768 | tf_op jit(solution)/shard_map/ppermute | solution.py:539
  78.4 8.7 %collective-permute-start.24 = (bf16[160,256]{1,0:T(8,128)(2,1)S(1)}, bf16[160,256]{1,0:T(8,128)(2,1)S(1)}, u32[]{:S(2)}, u32[]{:S(2)}) collective-permute-start(bf16[160,256]{1,0:T(8,128)(2,1)S(1)} %get-tuple-element.106), channel_id=1, source_target_pairs={{0,24},{4,28},{8,16},{12,20},{16,8},{20,12},{24,0},{28,4},{1,25},{... | collective-permute-start | bytes 245768 | tf_op jit(solution)/shard_map/ppermute | solution.py:539
  78.9 8.2 %collective-permute-start.26 = (bf16[160,256]{1,0:T(8,128)(2,1)S(1)}, bf16[160,256]{1,0:T(8,128)(2,1)S(1)}, u32[]{:S(2)}, u32[]{:S(2)}) collective-permute-start(bf16[160,256]{1,0:T(8,128)(2,1)S(1)} %get-tuple-element.108), channel_id=1, source_target_pairs={{0,8},{4,12},{8,0},{12,4},{16,24},{20,28},{24,16},{28,20},{1,9},{5... | collective-permute-start | bytes 245768 | tf_op jit(solution)/shard_map/ppermute | solution.py:539
  79.0 8.1 %collective-permute-start.25 = (bf16[144,256]{1,0:T(8,128)(2,1)S(1)}, bf16[144,256]{1,0:T(8,128)(2,1)S(1)}, u32[]{:S(2)}, u32[]{:S(2)}) collective-permute-start(bf16[144,256]{1,0:T(8,128)(2,1)S(1)} %get-tuple-element.107), channel_id=1, source_target_pairs={{0,8},{4,12},{8,0},{12,4},{16,24},{20,28},{24,16},{28,20},{1,9},{5... | collective-permute-start | bytes 221192 | tf_op jit(solution)/shard_map/ppermute | solution.py:539
  81.0 8.3 %collective-permute-start.28 = (bf16[144,256]{1,0:T(8,128)(2,1)S(1)}, bf16[144,256]{1,0:T(8,128)(2,1)S(1)}, u32[]{:S(2)}, u32[]{:S(2)}) collective-permute-start(bf16[144,256]{1,0:T(8,128)(2,1)S(1)} %shard_map.120), channel_id=1, source_target_pairs={{0,16},{4,20},{8,24},{12,28},{16,0},{20,4},{24,8},{28,12},{1,17},{... | collective-permute-start | bytes 221192 | tf_op jit(solution)/shard_map/ppermute | solution.py:539
  89.7 13.5 %collective-permute-start.29 = (bf16[304,256]{1,0:T(8,128)(2,1)S(1)}, bf16[304,256]{1,0:T(8,128)(2,1)S(1)}, u32[]{:S(2)}, u32[]{:S(2)}) collective-permute-start(bf16[304,256]{1,0:T(8,128)(2,1)S(1)} %get-tuple-element.112.refs_0_), channel_id=1, source_target_pairs={{0,8},{4,12},{8,0},{12,4},{16,24},{20,28},{24,16},{28,20},{1,9},{5... | collective-permute-start | bytes 466952 | tf_op jit(solution)/shard_map/ppermute | solution.py:539
  90.2 8.3 %collective-permute-start.30 = (bf16[144,256]{1,0:T(8,128)(2,1)S(1)}, bf16[144,256]{1,0:T(8,128)(2,1)S(1)}, u32[]{:S(2)}, u32[]{:S(2)}) collective-permute-start(bf16[144,256]{1,0:T(8,128)(2,1)S(1)} %get-tuple-element.113), channel_id=1, source_target_pairs={{0,16},{4,20},{8,24},{12,28},{16,0},{20,4},{24,8},{28,12},{1,17},{... | collective-permute-start | bytes 221192 | tf_op jit(solution)/shard_map/ppermute | solution.py:539
  92.8 7.0 %collective-permute-start.33 = (bf16[160,256]{1,0:T(8,128)(2,1)S(1)}, bf16[160,256]{1,0:T(8,128)(2,1)S(1)}, u32[]{:S(2)}, u32[]{:S(2)}) collective-permute-start(bf16[160,256]{1,0:T(8,128)(2,1)S(1)} %get-tuple-element.114), channel_id=1, source_target_pairs={{0,24},{4,28},{8,16},{12,20},{16,8},{20,12},{24,0},{28,4},{1,25},{... | collective-permute-start | bytes 245768 | tf_op jit(solution)/shard_map/ppermute | solution.py:539
  94.1 8.3 %collective-permute-start.31 = (bf16[160,256]{1,0:T(8,128)(2,1)S(1)}, bf16[160,256]{1,0:T(8,128)(2,1)S(1)}, u32[]{:S(2)}, u32[]{:S(2)}) collective-permute-start(bf16[160,256]{1,0:T(8,128)(2,1)S(1)} %get-tuple-element.114), channel_id=1, source_target_pairs={{0,16},{4,20},{8,24},{12,28},{16,0},{20,4},{24,8},{28,12},{1,17},{... | collective-permute-start | bytes 245768 | tf_op jit(solution)/shard_map/ppermute | solution.py:539
  98.5 4.7 %collective-permute-start.32 = (bf16[144,256]{1,0:T(8,128)(2,1)S(1)}, bf16[144,256]{1,0:T(8,128)(2,1)S(1)}, u32[]{:S(2)}, u32[]{:S(2)}) collective-permute-start(bf16[144,256]{1,0:T(8,128)(2,1)S(1)} %collective-permute-done.30.refs_2_), channel_id=1, source_target_pairs={{0,8},{4,12},{8,0},{12,4},{16,24},{20,28},{24,16},{28,20},{1,9},{5... | collective-permute-start | bytes 221192 | tf_op jit(solution)/shard_map/ppermute | solution.py:539
  105.5 5.5 %collective-permute-start.35 = (bf16[304,128]{1,0:T(8,128)(2,1)S(1)}, bf16[304,128]{1,0:T(8,128)(2,1)S(1)}, u32[]{:S(2)}, u32[]{:S(2)}) collective-permute-start(bf16[304,128]{1,0:T(8,128)(2,1)S(1)} %get-tuple-element.116), channel_id=1, source_target_pairs={{0,3},{1,2},{2,1},{3,0},{4,7},{5,6},{6,5},{7,4},{8,11},{9,10},{10,... | collective-permute-start | bytes 233480 | tf_op jit(solution)/shard_map/ppermute | solution.py:542
  (12 other events, 68.3 us)

commit v13 on v9

--- a/solution.py
+++ b/solution.py
@@ -302,39 +302,39 @@
         copy.wait()
 
 
-def forward_kernel(sends, mine, other, own, partner, *outs):
+def forward_kernel(sends, x, tiles, *refs):
     z, core, obs = place()
-    members, levp, lanes = mine.shape
-    width = own.shape[3]
-    scalars = [read_scalars([mine.at[m], other.at[m]], 2) for m in range(members)]
-    for out, (chip, first, count) in zip(outs, sends):
-        zz = z ^ chip
-        y = [
-            jnp.dot(
-                x[first : first + count].reshape(count * levp, lanes),
-                tiles[zz].reshape(lanes, width),
-                preferred_element_type=F32,
-            )
-            for x, tiles in ((mine, own), (other, partner))
-        ]
-        y = (y[0] + y[1]).reshape(count, levp, width)
-        for m in range(count):
-            out[m] = with_scalars(y[m], scalars[first + m]).astype(out.dtype)
-
-
-def weigh_kernel(later, last, spans, *refs):
-    ys, refs = refs[: len(spans)], refs[len(spans) :]
-    prec = refs[0]
-    state, *parts = refs[3 if later else 1 :]
-    if not last:
-        *parts, image = parts
+    outs = refs[-len(sends) :]
+    members, levp, lanes = x.shape
+    width = tiles.shape[3]
+    added = refs[1 : 1 + len(sends)] if len(refs) > len(sends) else [None] * len(sends)
+    if added[0] is not None:
+        scalars = [read_scalars([refs[0].at[m], x.at[m]], 2) for m in range(members)]
+    for out, before, (chip, first, count) in zip(outs, added, sends):
+        y = jnp.dot(
+            x[first : first + count].reshape(count * levp, lanes),
+            tiles[z ^ chip].reshape(lanes, width),
+            preferred_element_type=F32,
+        ).reshape(count, levp, width)
+        if before is None:
+            out[...] = y
+        else:
+            for m in range(count):
+                value = with_scalars(before[m] + y[m], scalars[first + m])
+                out[m] = value.astype(out.dtype)
+
+
+def weigh_kernel(later, last, n_ys, *refs):
+    ys, prec, refs = refs[:n_ys], refs[n_ys], refs[n_ys + 1 :]
+    if later:
+        (old_image, old), refs = refs[:2], refs[2:]
+    weighted, state = refs[:2]
     p = prec[...]
     for m in range(state.shape[0]):
-        mine = of_member(ys, spans, m)
+        mine = [y.at[m] for y in ys]
         y = add([x[...] for x in mine])
         norm, cross = read_scalars(mine, 2)
         if later:
-            old_image, old = refs[1:3]
             old_norm, old_square = old[m, 0:1, 0:1], old[m, 1:2, 0:1]
             beta = norm / old_norm
             square = norm + 2.0 * beta * cross + beta * beta * old_square
@@ -344,13 +344,8 @@
             square = norm
         scaled = p * y
         if not last:
-            image[m] = y
-        value = with_scalars(scaled, [total(scaled * y)]).astype(BF16)
-        first = 0
-        for part in parts:
-            if first <= m < first + part.shape[0]:
-                part[m - first] = value
-            first += part.shape[0]
+            refs[2][m] = y
+        weighted[m] = with_scalars(scaled, [total(scaled * y)]).astype(BF16)
         sub = lax.broadcasted_iota(jnp.int32, (8, LANES), 0)
         state[m] = jnp.where(sub == 0, norm, jnp.where(sub == 1, square, beta))
 
@@ -392,9 +387,11 @@
             out[m] = with_scalars(value, energy).astype(BF16)
 
 
-def update_kernel(parts, later, *refs):
+def update_kernel(parts, later, parts_of, *refs):
     pieces, refs = refs[:parts], refs[parts:]
-    sd, vert, vert_t, state, residual = refs[:5]
+    n_states = len(parts_of)
+    sd, vert, vert_t, *states, residual = refs[: 4 + n_states]
+    refs = refs[n_states - 1 :]
     if later:
         old_direction, old_solution, residual_out, solution_out, moved, direction_out = refs[5:]
     else:
@@ -404,7 +401,8 @@
     for m in range(residual.shape[0]):
         t, places = joined(pieces, m)
         (energy,) = read_scalars(places, 1)
-        norm, square, beta = state[m, 0:1, 0:1], state[m, 1:2, 0:1], state[m, 2:3, 0:1]
+        state = of_member(states, parts_of, m)[0]
+        norm, square, beta = state[0:1, 0:1], state[1:2, 0:1], state[2:3, 0:1]
         alpha = norm / (square + energy)
         r = residual[m]
         if later:
@@ -421,16 +419,19 @@
         moved[m] = with_scalars(x, [total(r * r), total(r * d)]).astype(BF16)
 
 
-def last_kernel(parts, later, lev, *refs):
+def last_kernel(parts, later, lev, parts_of, *refs):
     pieces, refs = refs[:parts], refs[parts:]
-    sd, vert, vert_t, state, residual = refs[:5]
+    n_states = len(parts_of)
+    sd, vert, vert_t, *states, residual = refs[: 4 + n_states]
+    refs = refs[n_states - 1 :]
     increment_out, residual_out = refs[-2:]
     obs = lax.axis_index("obs")
     mine = pl.ds(pl.multiple_of(obs * LANES, LANES), LANES)
     for m in range(residual.shape[0]):
         t = add([x[m] for x in pieces])
         (energy,) = read_scalars([x.at[m] for x in pieces], 1)
-        norm, square, beta = state[m, 0:1, 0:1], state[m, 1:2, 0:1], state[m, 2:3, 0:1]
+        state = of_member(states, parts_of, m)[0]
+        norm, square, beta = state[0:1, 0:1], state[1:2, 0:1], state[2:3, 0:1]
         alpha = norm / (square + energy)
         d = r = residual[m, :, mine]
         if later:
@@ -472,16 +473,17 @@
     field = (members, levp, LANES)
     slab_field = (members, levp, lanes)
     panel = (members, levp, width)
-    some, rest = members // 2, members - members // 2
+    some, rest = members // 4, members - members // 4
     half_fields = [struct((members, levp, lanes // 2), BF16)] * 2
     via = chips == 4 and some > 0
     if via:
-        plan = [(i, *span) for i in range(chips) for span in ((0, some), (some, rest))]
-        sends = [plan[6], plan[5], plan[7], *plan[2:4], (0, 0, members), plan[4]]
-        plan = [*plan[0:2], plan[5], plan[7], *plan[2:4], plan[4], plan[6]]
+        one, two = (0, some), (some, rest)
+        parts_of = [(*one, 0), (*two, 0)]
+        plan = [(i, *two) for i in range(chips)] + [(i, *one) for i in range(chips)]
+        sends = [(3, *one), (2, *two), (3, *two), (1, *two), (0, *two), (1, *one), (0, *one), (2, *one)]
     else:
-        plan = [(i, 0, members) for i in range(chips)]
-        sends = plan
+        parts_of = [(0, members, 0)]
+        sends = plan = [(i, 0, members) for i in range(chips)]
     pad = ((0, levp - lev), (0, levp - lev))
     high = lax.reduce_precision(vert_factor, 8, 7)
     low = vert_factor - high
@@ -538,27 +540,34 @@
         return [x for pair in zip(halves, moved_halves) for x in pair]
 
     def line_sum(moved, other):
+        shapes = [(count, levp, width) for i, unused, count in sends]
+        mine = call(
+            functools.partial(forward_kernel, sends),
+            [struct(shape, F32) for shape in shapes],
+            [],
+            product,
+            moved,
+            own,
+        )
         ys = call(
             functools.partial(forward_kernel, sends),
             [
-                struct((count, levp, width), F32 if i == 0 or (via and at == 6) else BF16)
-                for at, (i, unused, count) in enumerate(sends)
+                struct(shape, F32 if i == 0 or (via and at == 7) else BF16)
+                for at, ((i, *unused), shape) in enumerate(zip(sends, shapes))
             ],
             [],
-            2 * product,
+            product,
+            other,
+            partner,
             moved,
-            other,
-            own,
-            partner,
+            *mine,
         )
         if not via:
-            return [y if i == 0 else along(y, i) for i, y in enumerate(ys)], [
-                (0, members, 0) for y in ys
-            ]
-        passed, far_rest, last_rest, next_some, next_rest, near, far = ys
+            return [[y if i == 0 else along(y, i) for i, y in enumerate(ys)]]
+        passed, far_rest, last_rest, next_rest, near_rest, next_some, near_some, far = ys
         passed = along(passed, 1)
-        far_rest, last_rest = along(far_rest, 2), along(last_rest, 3)
-        next_some, next_rest = along(next_some, 1), along(next_rest, 1)
+        rest_ys = [near_rest, along(far_rest, 2), along(last_rest, 3), along(next_rest, 1)]
+        next_some = along(next_some, 1)
         (far,) = call(
             functools.partial(add_kernel, 2),
             [struct((some, levp, width), BF16)],
@@ -567,17 +576,14 @@
             far,
             passed,
         )
-        ys = [near, far_rest, last_rest, next_some, next_rest, along(far, 2)]
-        spans = [(0, members, 0)] + [(some, rest, 0)] * 2 + [(0, some, 0), (some, rest, 0)]
-        return ys, spans + [(0, some, 0)]
+        return [[near_some, next_some, along(far, 2)], rest_ys]
 
     def line_gather(*parts):
         if not via:
             return [parts[0] if i == 0 else along(parts[0], i) for i in range(chips)]
         one, two = parts
         far = along(one, 2)
-        far_rest, last_rest = along(two, 2), along(two, 3)
-        return [one, two, far_rest, last_rest, along(one, 1), along(two, 1), far, along(far, 1)]
+        return [two, *(along(two, i) for i in (1, 2, 3)), one, along(one, 1), far, along(far, 1)]
 
     dense = struct((chips, colblocks, LANES, width), BF16)
     own, for_partner, *partials = call(
@@ -627,23 +633,26 @@
         vert,
         vert_t,
     )
-    direction = total_step = image = state = None
+    direction = total_step = None
+    image, state = [None] * len(parts_of), [None] * len(parts_of)
     for sweep in range(ITERS):
         later, last = sweep > 0, sweep == ITERS - 1
-        ys, spans = line_sum(moved, swap(moved))
-        state, *weighted = call(
-            functools.partial(weigh_kernel, later, last, spans),
-            [struct((members, 8, LANES), F32)]
-            + [struct((n, levp, width), BF16) for n in ((some, rest) if via else (members,))]
-            + ([] if last else [struct(panel, F32)]),
-            [],
-            0,
-            *ys,
-            precision,
-            *([image, state] if later else []),
-        )
-        if not last:
-            *weighted, image = weighted
+        weighted = []
+        for part, ys in reversed(list(enumerate(line_sum(moved, swap(moved))))):
+            count = parts_of[part][1]
+            shape = (count, levp, width)
+            w, state[part], *y = call(
+                functools.partial(weigh_kernel, later, last, len(ys)),
+                [struct(shape, BF16), struct((count, 8, LANES), F32)]
+                + ([] if last else [struct(shape, F32)]),
+                [],
+                0,
+                *ys,
+                precision,
+                *([image[part], state[part]] if later else []),
+            )
+            weighted.insert(0, w)
+            image[part] = None if last else y[0]
         ws = line_gather(*weighted)
         (theirs,) = call(
             functools.partial(adjoint_kernel, plan),
@@ -662,7 +671,7 @@
             *ws,
             own,
         )
-        known = [vert, vert_t, state, residual]
+        known = [vert, vert_t, *state, residual]
         if later:
             known += [direction, total_step]
         if last:
@@ -671,7 +680,7 @@
             )
             ps = [ps[0]] + [plane(ps[i], i) for i in reversed(range(1, n_obs))]
             outputs = call(
-                functools.partial(last_kernel, len(ps), later, lev),
+                functools.partial(last_kernel, len(ps), later, lev, parts_of),
                 [struct((lev, members, LANES), F32)] * 2,
                 [],
                 small,
@@ -686,7 +695,7 @@
         if later:
             outs.append(struct(slab_field, F32))
         r, total_step, moved, *d = call(
-            functools.partial(update_kernel, len(ps), later),
+            functools.partial(update_kernel, len(ps), later, parts_of),
             outs,
             [],
             small * colblocks,

time: 114 us -> 127 us (1.11)
  waiting for transfers between devices: 54 us -> 65 us
    ppermute x24, waiting for transfers between devices: 28.8 us -> 40.5 us  [along(): return lax.ppermute(x, 'slab', [(s, s ^ 2 * i) for s in range(n_slab)])]
    pallas_call x20 -> x24, Pallas kernels: 13.9 us -> 14.8 us  [call(): pl.pallas_call(kernel, out_shape=outs, in_specs=[space] * len(args), out_...]
  transfers between devices with their start and end apart: 40 -> 40, of which waited for: 32 -> 25; matrix products, arithmetic and copies ran while one was open for 0% -> 0% of each run, Pallas kernels for 3% -> 4%
where the time goes in v13:
time: 127 us
  waiting for transfers between devices  65 us (51%)
  starting transfers between devices  43 us (34%)
  Pallas kernels  14.8 us (12%)
  local copies, waits for them, and re-layouts  2.1 us (2%)
  between operations  1.57 us (1%)
    ppermute x24, waiting for transfers between devices, along(): return lax.ppermute(x, 'slab', [(s, s ^ 2 * i) for s in range(n_slab)])  40.5 us
    ppermute x24, starting transfers between devices, along(): return lax.ppermute(x, 'slab', [(s, s ^ 2 * i) for s in range(n_slab)])  28.9 us
    ppermute x11, waiting for transfers between devices, plane(): return lax.ppermute(x, 'obs', [(o, o ^ i) for o in range(n_obs)])  20.4 us
    pallas_call x24, Pallas kernels, call(): pl.pallas_call(kernel, out_shape=outs, in_specs=[space] * len(args), out_...  14.8 us
    ppermute x11, starting transfers between devices, plane(): return lax.ppermute(x, 'obs', [(o, o ^ i) for o in range(n_obs)])  12.7 us
    ppermute x5, waiting for transfers between devices, swap(): return lax.ppermute(x, 'slab', [(s, s ^ 1) for s in range(n_slab)])  4.18 us
  transfers between devices with their start and end apart: 40, of which 25 were waited for; matrix products, arithmetic and copies ran while one was open for 0% of the time, Pallas kernels for 4%

profile of v13, /device:TPU:0, one launch (start us, length us, event | category | flops | bytes accessed | tf_op | source)
XLA Modules:
  0.0 126.5 jit_solution(18063931090768410084)
XLA Ops:
  1.3 5.1 %shard_map.104 = (bf16[4,4,128,256]{3,2,1,0:T(8,128)(2,1)}, bf16[4,4,128,256]{3,2,1,0:T(8,128)(2,1)}, bf16[4,80,256]{2,1,0:T(8,128)(2,1)}, bf16[4,80,256]{2,1,0:T(8,128)(2,1)}) custom-call(s32[4]{0:T(128)} %seeds_in.1, s32[1,1,32]{2,1,0:T(1,128)} %ids_in.1, s32[1,1,32]{2,1,0:T(1,128)} %cols_in.1, s32[1,1]{1,0:T(1,128)S(6)} %copy.16.count_in, ...), custom_call_target="tpu_custom_call" | custom-call | flops 671088640 | bytes 5751572 | tf_op jit(solution)/shard_map/pallas_call | solution.py:23
  7.5 2.1 %collective-permute-start = (bf16[4,80,256]{2,1,0:T(8,128)(2,1)}, bf16[4,80,256]{2,1,0:T(8,128)(2,1)S(1)}, u32[]{:S(2)}, u32[]{:S(2)}) collective-permute-start(bf16[4,80,256]{2,1,0:T(8,128)(2,1)} %get-tuple-element.68.refs_0_), channel_id=1, source_target_pairs={{0,1},{1,0},{2,3},{3,2},{4,5},{5,4},{6,7},{7,6},{8,9},{9,8},{10,11... | collective-permute-start | bytes 491528 | tf_op jit(solution)/shard_map/ppermute | solution.py:505
  9.6 2.0 %collective-permute-start.1 = (bf16[4,80,256]{2,1,0:T(8,128)(2,1)}, bf16[4,80,256]{2,1,0:T(8,128)(2,1)S(1)}, u32[]{:S(2)}, u32[]{:S(2)}) collective-permute-start(bf16[4,80,256]{2,1,0:T(8,128)(2,1)} %get-tuple-element.69.refs_1_), channel_id=1, source_target_pairs={{0,2},{1,3},{2,0},{3,1},{4,6},{5,7},{6,4},{7,5},{8,10},{9,11},{10,... | collective-permute-start | bytes 491528 | tf_op jit(solution)/shard_map/ppermute | solution.py:505
  14.6 1.7 %collective-permute-done.1.two_more = bf16[4,80,256]{2,1,0:T(8,128)(2,1)S(1)} collective-permute-done((bf16[4,80,256]{2,1,0:T(8,128)(2,1)}, bf16[4,80,256]{2,1,0:T(8,128)(2,1)S(1)}, u32[]{:S(2)}, u32[]{:S(2)}) %collective-permute-start.1) | collective-permute-done | bytes 163872 | tf_op jit(solution)/shard_map/ppermute | solution.py:505
  16.4 1.8 %collective-permute-start.2 = (bf16[4,80,256]{2,1,0:T(8,128)(2,1)S(1)}, bf16[4,80,256]{2,1,0:T(8,128)(2,1)S(1)}, u32[]{:S(2)}, u32[]{:S(2)}) collective-permute-start(bf16[4,80,256]{2,1,0:T(8,128)(2,1)S(1)} %get-tuple-element.72.refs_0_), channel_id=1, source_target_pairs={{0,2},{1,3},{2,0},{3,1},{4,6},{5,7},{6,4},{7,5},{8,10},{9,11},{10,... | collective-permute-start | bytes 491528 | tf_op jit(solution)/shard_map/ppermute | solution.py:505
  18.7 3.4 %collective-permute-done.2.refs_1_ = bf16[4,80,256]{2,1,0:T(8,128)(2,1)S(1)} collective-permute-done((bf16[4,80,256]{2,1,0:T(8,128)(2,1)S(1)}, bf16[4,80,256]{2,1,0:T(8,128)(2,1)S(1)}, u32[]{:S(2)}, u32[]{:S(2)}) %collective-permute-start.2) | collective-permute-done | bytes 163872 | tf_op jit(solution)/shard_map/ppermute | solution.py:505
  22.1 1.4 %collective-permute-done.3.refs_3_ = bf16[4,80,256]{2,1,0:T(8,128)(2,1)S(1)} collective-permute-done((bf16[4,80,256]{2,1,0:T(8,128)(2,1)S(1)}, bf16[4,80,256]{2,1,0:T(8,128)(2,1)S(1)}, u32[]{:S(2)}, u32[]{:S(2)}) %collective-permute-start.3) | collective-permute-done | bytes 163872 | tf_op jit(solution)/shard_map/ppermute | solution.py:505
  26.7 2.7 %collective-permute-start.6 = (bf16[3,80,256]{2,1,0:T(8,128)(2,1)S(1)}, bf16[3,80,256]{2,1,0:T(8,128)(2,1)S(1)}, u32[]{:S(2)}, u32[]{:S(2)}) collective-permute-start(bf16[3,80,256]{2,1,0:T(8,128)(2,1)S(1)} %get-tuple-element.86), channel_id=1, source_target_pairs={{0,16},{4,20},{8,24},{12,28},{16,0},{20,4},{24,8},{28,12},{1,17},{... | collective-permute-start | bytes 368648 | tf_op jit(solution)/shard_map/ppermute | solution.py:502
  31.0 1.5 %collective-permute-start.13 = (bf16[1,80,256]{2,1,0:T(8,128)(2,1)S(1)}, bf16[1,80,256]{2,1,0:T(8,128)(2,1)S(1)}, u32[]{:S(2)}, u32[]{:S(2)}) collective-permute-start(bf16[1,80,256]{2,1,0:T(8,128)(2,1)S(1)} %get-tuple-element.93), channel_id=1, source_target_pairs={{0,8},{4,12},{8,0},{12,4},{16,24},{20,28},{24,16},{28,20},{1,9},{5... | collective-permute-start | bytes 122888 | tf_op jit(solution)/shard_map/ppermute | solution.py:502
  33.2 7.8 %collective-permute-done.13.refs_1_ = bf16[1,80,256]{2,1,0:T(8,128)(2,1)S(1)} collective-permute-done((bf16[1,80,256]{2,1,0:T(8,128)(2,1)S(1)}, bf16[1,80,256]{2,1,0:T(8,128)(2,1)S(1)}, u32[]{:S(2)}, u32[]{:S(2)}) %collective-permute-start.13) | collective-permute-done | bytes 40992 | tf_op jit(solution)/shard_map/ppermute | solution.py:502
  41.2 1.5 %collective-permute-start.14 = (bf16[1,80,256]{2,1,0:T(8,128)(2,1)S(1)}, bf16[1,80,256]{2,1,0:T(8,128)(2,1)S(1)}, u32[]{:S(2)}, u32[]{:S(2)}) collective-permute-start(bf16[1,80,256]{2,1,0:T(8,128)(2,1)S(1)} %shard_map.112), channel_id=1, source_target_pairs={{0,16},{4,20},{8,24},{12,28},{16,0},{20,4},{24,8},{28,12},{1,17},{... | collective-permute-start | bytes 122888 | tf_op jit(solution)/shard_map/ppermute | solution.py:502
  42.9 2.0 %collective-permute-start.11 = (bf16[3,80,256]{2,1,0:T(8,128)(2,1)S(1)}, bf16[3,80,256]{2,1,0:T(8,128)(2,1)S(1)}, u32[]{:S(2)}, u32[]{:S(2)}) collective-permute-start(bf16[3,80,256]{2,1,0:T(8,128)(2,1)S(1)} %get-tuple-element.89.refs_0_), channel_id=1, source_target_pairs={{0,24},{4,28},{8,16},{12,20},{16,8},{20,12},{24,0},{28,4},{1,25},{... | collective-permute-start | bytes 368648 | tf_op jit(solution)/shard_map/ppermute | solution.py:502
  44.9 2.0 %collective-permute-start.10 = (bf16[3,80,256]{2,1,0:T(8,128)(2,1)S(1)}, bf16[3,80,256]{2,1,0:T(8,128)(2,1)S(1)}, u32[]{:S(2)}, u32[]{:S(2)}) collective-permute-start(bf16[3,80,256]{2,1,0:T(8,128)(2,1)S(1)} %get-tuple-element.89.refs_0_), channel_id=1, source_target_pairs={{0,16},{4,20},{8,24},{12,28},{16,0},{20,4},{24,8},{28,12},{1,17},{... | collective-permute-start | bytes 368648 | tf_op jit(solution)/shard_map/ppermute | solution.py:502
  47.4 3.1 %collective-permute-done.14.refs_2_ = bf16[1,80,256]{2,1,0:T(8,128)(2,1)S(1)} collective-permute-done((bf16[1,80,256]{2,1,0:T(8,128)(2,1)S(1)}, bf16[1,80,256]{2,1,0:T(8,128)(2,1)S(1)}, u32[]{:S(2)}, u32[]{:S(2)}) %collective-permute-start.14) | collective-permute-done | bytes 40992 | tf_op jit(solution)/shard_map/ppermute | solution.py:502
  50.6 4.0 %collective-permute-start.15 = (bf16[1,80,256]{2,1,0:T(8,128)(2,1)S(1)}, bf16[1,80,256]{2,1,0:T(8,128)(2,1)S(1)}, u32[]{:S(2)}, u32[]{:S(2)}) collective-permute-start(bf16[1,80,256]{2,1,0:T(8,128)(2,1)S(1)} %get-tuple-element.94.refs_4_), channel_id=1, source_target_pairs={{0,8},{4,12},{8,0},{12,4},{16,24},{20,28},{24,16},{28,20},{1,9},{5... | collective-permute-start | bytes 122888 | tf_op jit(solution)/shard_map/ppermute | solution.py:502
  54.6 4.4 %collective-permute-done.16.refs_6_ = bf16[1,80,256]{2,1,0:T(8,128)(2,1)S(1)} collective-permute-done((bf16[1,80,256]{2,1,0:T(8,128)(2,1)S(1)}, bf16[1,80,256]{2,1,0:T(8,128)(2,1)S(1)}, u32[]{:S(2)}, u32[]{:S(2)}) %collective-permute-start.16) | collective-permute-done | bytes 40992 | tf_op jit(solution)/shard_map/ppermute | solution.py:502
  59.3 3.7 %collective-permute-done.17.refs_7_ = bf16[1,80,256]{2,1,0:T(8,128)(2,1)S(1)} collective-permute-done((bf16[1,80,256]{2,1,0:T(8,128)(2,1)S(1)}, bf16[1,80,256]{2,1,0:T(8,128)(2,1)S(1)}, u32[]{:S(2)}, u32[]{:S(2)}) %collective-permute-start.17) | collective-permute-done | bytes 40992 | tf_op jit(solution)/shard_map/ppermute | solution.py:502
  66.2 5.4 %collective-permute-done.19.one_more = bf16[4,80,256]{2,1,0:T(8,128)(2,1)S(1)} collective-permute-done((bf16[4,80,256]{2,1,0:T(8,128)(2,1)S(1)}, bf16[4,80,256]{2,1,0:T(8,128)(2,1)S(1)}, u32[]{:S(2)}, u32[]{:S(2)}) %collective-permute-start.19) | collective-permute-done | bytes 163872 | tf_op jit(solution)/shard_map/ppermute | solution.py:505
  72.4 1.6 %collective-permute-start.22 = (bf16[4,80,256]{2,1,0:T(8,128)(2,1)S(1)}, bf16[4,80,256]{2,1,0:T(8,128)(2,1)S(1)}, u32[]{:S(2)}, u32[]{:S(2)}) collective-permute-start(bf16[4,80,256]{2,1,0:T(8,128)(2,1)S(1)} %get-tuple-element.98.refs_2_), channel_id=1, source_target_pairs={{0,1},{1,0},{2,3},{3,2},{4,5},{5,4},{6,7},{7,6},{8,9},{9,8},{10,11... | collective-permute-start | bytes 491528 | tf_op jit(solution)/shard_map/ppermute | solution.py:505
  73.9 3.4 %collective-permute-done.21.refs_1_ = bf16[4,80,256]{2,1,0:T(8,128)(2,1)S(1)} collective-permute-done((bf16[4,80,256]{2,1,0:T(8,128)(2,1)S(1)}, bf16[4,80,256]{2,1,0:T(8,128)(2,1)S(1)}, u32[]{:S(2)}, u32[]{:S(2)}) %collective-permute-start.21) | collective-permute-done | bytes 163872 | tf_op jit(solution)/shard_map/ppermute | solution.py:505
  81.3 2.2 %collective-permute-start.25 = (bf16[3,80,256]{2,1,0:T(8,128)(2,1)S(1)}, bf16[3,80,256]{2,1,0:T(8,128)(2,1)S(1)}, u32[]{:S(2)}, u32[]{:S(2)}) collective-permute-start(bf16[3,80,256]{2,1,0:T(8,128)(2,1)S(1)} %get-tuple-element.114), channel_id=1, source_target_pairs={{0,24},{4,28},{8,16},{12,20},{16,8},{20,12},{24,0},{28,4},{1,25},{... | collective-permute-start | bytes 368648 | tf_op jit(solution)/shard_map/ppermute | solution.py:502
  83.5 1.1 collective-permute-start.26
  86.7 8.2 %collective-permute-done.31.refs_1_ = bf16[1,80,256]{2,1,0:T(8,128)(2,1)S(1)} collective-permute-done((bf16[1,80,256]{2,1,0:T(8,128)(2,1)S(1)}, bf16[1,80,256]{2,1,0:T(8,128)(2,1)S(1)}, u32[]{:S(2)}, u32[]{:S(2)}) %collective-permute-start.31) | collective-permute-done | bytes 40992 | tf_op jit(solution)/shard_map/ppermute | solution.py:502
  95.3 1.9 %collective-permute-start.29 = (bf16[3,80,256]{2,1,0:T(8,128)(2,1)S(1)}, bf16[3,80,256]{2,1,0:T(8,128)(2,1)S(1)}, u32[]{:S(2)}, u32[]{:S(2)}) collective-permute-start(bf16[3,80,256]{2,1,0:T(8,128)(2,1)S(1)} %get-tuple-element.117.refs_0_), channel_id=1, source_target_pairs={{0,24},{4,28},{8,16},{12,20},{16,8},{20,12},{24,0},{28,4},{1,25},{... | collective-permute-start | bytes 368648 | tf_op jit(solution)/shard_map/ppermute | solution.py:502
  97.2 1.9 %collective-permute-start.28 = (bf16[3,80,256]{2,1,0:T(8,128)(2,1)S(1)}, bf16[3,80,256]{2,1,0:T(8,128)(2,1)S(1)}, u32[]{:S(2)}, u32[]{:S(2)}) collective-permute-start(bf16[3,80,256]{2,1,0:T(8,128)(2,1)S(1)} %get-tuple-element.117.refs_0_), channel_id=1, source_target_pairs={{0,16},{4,20},{8,24},{12,28},{16,0},{20,4},{24,8},{28,12},{1,17},{... | collective-permute-start | bytes 368648 | tf_op jit(solution)/shard_map/ppermute | solution.py:502
  99.7 4.4 %collective-permute-done.32.refs_2_ = bf16[1,80,256]{2,1,0:T(8,128)(2,1)S(1)} collective-permute-done((bf16[1,80,256]{2,1,0:T(8,128)(2,1)S(1)}, bf16[1,80,256]{2,1,0:T(8,128)(2,1)S(1)}, u32[]{:S(2)}, u32[]{:S(2)}) %collective-permute-start.32) | collective-permute-done | bytes 40992 | tf_op jit(solution)/shard_map/ppermute | solution.py:502
  104.4 2.5 %collective-permute-start.33 = (bf16[1,80,256]{2,1,0:T(8,128)(2,1)S(1)}, bf16[1,80,256]{2,1,0:T(8,128)(2,1)S(1)}, u32[]{:S(2)}, u32[]{:S(2)}) collective-permute-start(bf16[1,80,256]{2,1,0:T(8,128)(2,1)S(1)} %get-tuple-element.123.refs_4_), channel_id=1, source_target_pairs={{0,8},{4,12},{8,0},{12,4},{16,24},{20,28},{24,16},{28,20},{1,9},{5... | collective-permute-start | bytes 122888 | tf_op jit(solution)/shard_map/ppermute | solution.py:502
  106.9 4.6 %collective-permute-done.34.refs_6_ = bf16[1,80,256]{2,1,0:T(8,128)(2,1)S(1)} collective-permute-done((bf16[1,80,256]{2,1,0:T(8,128)(2,1)S(1)}, bf16[1,80,256]{2,1,0:T(8,128)(2,1)S(1)}, u32[]{:S(2)}, u32[]{:S(2)}) %collective-permute-start.34) | collective-permute-done | bytes 40992 | tf_op jit(solution)/shard_map/ppermute | solution.py:502
  111.7 3.8 %collective-permute-done.35.refs_7_ = bf16[1,80,256]{2,1,0:T(8,128)(2,1)S(1)} collective-permute-done((bf16[1,80,256]{2,1,0:T(8,128)(2,1)S(1)}, bf16[1,80,256]{2,1,0:T(8,128)(2,1)S(1)}, u32[]{:S(2)}, u32[]{:S(2)}) %collective-permute-start.35) | collective-permute-done | bytes 40992 | tf_op jit(solution)/shard_map/ppermute | solution.py:502
  117.9 2.7 %collective-permute-start.37 = (bf16[4,80,128]{2,1,0:T(8,128)(2,1)S(1)}, bf16[4,80,128]{2,1,0:T(8,128)(2,1)S(1)}, u32[]{:S(2)}, u32[]{:S(2)}) collective-permute-start(bf16[4,80,128]{2,1,0:T(8,128)(2,1)S(1)} %get-tuple-element.125), channel_id=1, source_target_pairs={{0,3},{1,2},{2,1},{3,0},{4,7},{5,6},{6,5},{7,4},{8,11},{9,10},{10,... | collective-permute-start | bytes 245768 | tf_op jit(solution)/shard_map/ppermute | solution.py:505
  121.5 1.9 %collective-permute-done.37.refs_1_ = bf16[4,80,128]{2,1,0:T(8,128)(2,1)S(1)} collective-permute-done((bf16[4,80,128]{2,1,0:T(8,128)(2,1)S(1)}, bf16[4,80,128]{2,1,0:T(8,128)(2,1)S(1)}, u32[]{:S(2)}, u32[]{:S(2)}) %collective-permute-start.37) | collective-permute-done | bytes 81952 | tf_op jit(solution)/shard_map/ppermute | solution.py:505
  123.4 1.7 %collective-permute-done.38.refs_2_ = bf16[4,80,128]{2,1,0:T(8,128)(2,1)S(1)} collective-permute-done((bf16[4,80,128]{2,1,0:T(8,128)(2,1)S(1)}, bf16[4,80,128]{2,1,0:T(8,128)(2,1)S(1)}, u32[]{:S(2)}, u32[]{:S(2)}) %collective-permute-start.38) | collective-permute-done | bytes 81952 | tf_op jit(solution)/shard_map/ppermute | solution.py:505
  (91 shorter events, 27.5 us)
Async XLA Ops:
  6.4 19.8 %collective-permute-start.5 = (bf16[4,4,128,256]{3,2,1,0:T(8,128)(2,1)}, bf16[4,4,128,256]{3,2,1,0:T(8,128)(2,1)S(1)}, u32[]{:S(2)}, u32[]{:S(2)}) collective-permute-start(bf16[4,4,128,256]{3,2,1,0:T(8,128)(2,1)} %get-tuple-element.75), channel_id=1, source_target_pairs={{0,4},{4,0},{8,12},{12,8},{16,20},{20,16},{24,28},{28,24},{1,5},{5... | collective-permute-start | bytes 3145736 | tf_op jit(solution)/shard_map/ppermute | solution.py:508
  7.5 7.1 %collective-permute-start = (bf16[4,80,256]{2,1,0:T(8,128)(2,1)}, bf16[4,80,256]{2,1,0:T(8,128)(2,1)S(1)}, u32[]{:S(2)}, u32[]{:S(2)}) collective-permute-start(bf16[4,80,256]{2,1,0:T(8,128)(2,1)} %get-tuple-element.68.refs_0_), channel_id=1, source_target_pairs={{0,1},{1,0},{2,3},{3,2},{4,5},{5,4},{6,7},{7,6},{8,9},{9,8},{10,11... | collective-permute-start | bytes 491528 | tf_op jit(solution)/shard_map/ppermute | solution.py:505
  9.6 6.7 %collective-permute-start.1 = (bf16[4,80,256]{2,1,0:T(8,128)(2,1)}, bf16[4,80,256]{2,1,0:T(8,128)(2,1)S(1)}, u32[]{:S(2)}, u32[]{:S(2)}) collective-permute-start(bf16[4,80,256]{2,1,0:T(8,128)(2,1)} %get-tuple-element.69.refs_1_), channel_id=1, source_target_pairs={{0,2},{1,3},{2,0},{3,1},{4,6},{5,7},{6,4},{7,5},{8,10},{9,11},{10,... | collective-permute-start | bytes 491528 | tf_op jit(solution)/shard_map/ppermute | solution.py:505
  16.4 5.8 %collective-permute-start.2 = (bf16[4,80,256]{2,1,0:T(8,128)(2,1)S(1)}, bf16[4,80,256]{2,1,0:T(8,128)(2,1)S(1)}, u32[]{:S(2)}, u32[]{:S(2)}) collective-permute-start(bf16[4,80,256]{2,1,0:T(8,128)(2,1)S(1)} %get-tuple-element.72.refs_0_), channel_id=1, source_target_pairs={{0,2},{1,3},{2,0},{3,1},{4,6},{5,7},{6,4},{7,5},{8,10},{9,11},{10,... | collective-permute-start | bytes 491528 | tf_op jit(solution)/shard_map/ppermute | solution.py:505
  18.2 5.3 %collective-permute-start.3 = (bf16[4,80,256]{2,1,0:T(8,128)(2,1)S(1)}, bf16[4,80,256]{2,1,0:T(8,128)(2,1)S(1)}, u32[]{:S(2)}, u32[]{:S(2)}) collective-permute-start(bf16[4,80,256]{2,1,0:T(8,128)(2,1)S(1)} %get-tuple-element.73.refs_2_), channel_id=1, source_target_pairs={{0,1},{1,0},{2,3},{3,2},{4,5},{5,4},{6,7},{7,6},{8,9},{9,8},{10,11... | collective-permute-start | bytes 491528 | tf_op jit(solution)/shard_map/ppermute | solution.py:505
  26.7 16.0 %collective-permute-start.6 = (bf16[3,80,256]{2,1,0:T(8,128)(2,1)S(1)}, bf16[3,80,256]{2,1,0:T(8,128)(2,1)S(1)}, u32[]{:S(2)}, u32[]{:S(2)}) collective-permute-start(bf16[3,80,256]{2,1,0:T(8,128)(2,1)S(1)} %get-tuple-element.86), channel_id=1, source_target_pairs={{0,16},{4,20},{8,24},{12,28},{16,0},{20,4},{24,8},{28,12},{1,17},{... | collective-permute-start | bytes 368648 | tf_op jit(solution)/shard_map/ppermute | solution.py:502
  29.4 13.3 %collective-permute-start.7 = (bf16[3,80,256]{2,1,0:T(8,128)(2,1)S(1)}, bf16[3,80,256]{2,1,0:T(8,128)(2,1)S(1)}, u32[]{:S(2)}, u32[]{:S(2)}) collective-permute-start(bf16[3,80,256]{2,1,0:T(8,128)(2,1)S(1)} %get-tuple-element.87), channel_id=1, source_target_pairs={{0,24},{4,28},{8,16},{12,20},{16,8},{20,12},{24,0},{28,4},{1,25},{... | collective-permute-start | bytes 368648 | tf_op jit(solution)/shard_map/ppermute | solution.py:502
  30.5 12.2 %collective-permute-start.8 = (bf16[3,80,256]{2,1,0:T(8,128)(2,1)S(1)}, bf16[3,80,256]{2,1,0:T(8,128)(2,1)S(1)}, u32[]{:S(2)}, u32[]{:S(2)}) collective-permute-start(bf16[3,80,256]{2,1,0:T(8,128)(2,1)S(1)} %get-tuple-element.88), channel_id=1, source_target_pairs={{0,8},{4,12},{8,0},{12,4},{16,24},{20,28},{24,16},{28,20},{1,9},{5... | collective-permute-start | bytes 368648 | tf_op jit(solution)/shard_map/ppermute | solution.py:502
  31.0 10.1 %collective-permute-start.13 = (bf16[1,80,256]{2,1,0:T(8,128)(2,1)S(1)}, bf16[1,80,256]{2,1,0:T(8,128)(2,1)S(1)}, u32[]{:S(2)}, u32[]{:S(2)}) collective-permute-start(bf16[1,80,256]{2,1,0:T(8,128)(2,1)S(1)} %get-tuple-element.93), channel_id=1, source_target_pairs={{0,8},{4,12},{8,0},{12,4},{16,24},{20,28},{24,16},{28,20},{1,9},{5... | collective-permute-start | bytes 122888 | tf_op jit(solution)/shard_map/ppermute | solution.py:502
  32.7 14.7 %collective-permute-start.12 = (bf16[1,80,256]{2,1,0:T(8,128)(2,1)S(1)}, bf16[1,80,256]{2,1,0:T(8,128)(2,1)S(1)}, u32[]{:S(2)}, u32[]{:S(2)}) collective-permute-start(bf16[1,80,256]{2,1,0:T(8,128)(2,1)S(1)} %get-tuple-element.91), channel_id=1, source_target_pairs={{0,8},{4,12},{8,0},{12,4},{16,24},{20,28},{24,16},{28,20},{1,9},{5... | collective-permute-start | bytes 122888 | tf_op jit(solution)/shard_map/ppermute | solution.py:502
  41.2 9.3 %collective-permute-start.14 = (bf16[1,80,256]{2,1,0:T(8,128)(2,1)S(1)}, bf16[1,80,256]{2,1,0:T(8,128)(2,1)S(1)}, u32[]{:S(2)}, u32[]{:S(2)}) collective-permute-start(bf16[1,80,256]{2,1,0:T(8,128)(2,1)S(1)} %shard_map.112), channel_id=1, source_target_pairs={{0,16},{4,20},{8,24},{12,28},{16,0},{20,4},{24,8},{28,12},{1,17},{... | collective-permute-start | bytes 122888 | tf_op jit(solution)/shard_map/ppermute | solution.py:502
  42.9 20.0 %collective-permute-start.11 = (bf16[3,80,256]{2,1,0:T(8,128)(2,1)S(1)}, bf16[3,80,256]{2,1,0:T(8,128)(2,1)S(1)}, u32[]{:S(2)}, u32[]{:S(2)}) collective-permute-start(bf16[3,80,256]{2,1,0:T(8,128)(2,1)S(1)} %get-tuple-element.89.refs_0_), channel_id=1, source_target_pairs={{0,24},{4,28},{8,16},{12,20},{16,8},{20,12},{24,0},{28,4},{1,25},{... | collective-permute-start | bytes 368648 | tf_op jit(solution)/shard_map/ppermute | solution.py:502
  44.9 18.0 %collective-permute-start.10 = (bf16[3,80,256]{2,1,0:T(8,128)(2,1)S(1)}, bf16[3,80,256]{2,1,0:T(8,128)(2,1)S(1)}, u32[]{:S(2)}, u32[]{:S(2)}) collective-permute-start(bf16[3,80,256]{2,1,0:T(8,128)(2,1)S(1)} %get-tuple-element.89.refs_0_), channel_id=1, source_target_pairs={{0,16},{4,20},{8,24},{12,28},{16,0},{20,4},{24,8},{28,12},{1,17},{... | collective-permute-start | bytes 368648 | tf_op jit(solution)/shard_map/ppermute | solution.py:502
  46.9 16.0 %collective-permute-start.9 = (bf16[3,80,256]{2,1,0:T(8,128)(2,1)S(1)}, bf16[3,80,256]{2,1,0:T(8,128)(2,1)S(1)}, u32[]{:S(2)}, u32[]{:S(2)}) collective-permute-start(bf16[3,80,256]{2,1,0:T(8,128)(2,1)S(1)} %get-tuple-element.89.refs_0_), channel_id=1, source_target_pairs={{0,8},{4,12},{8,0},{12,4},{16,24},{20,28},{24,16},{28,20},{1,9},{5... | collective-permute-start | bytes 368648 | tf_op jit(solution)/shard_map/ppermute | solution.py:502
  50.6 8.4 %collective-permute-start.16 = (bf16[1,80,256]{2,1,0:T(8,128)(2,1)S(1)}, bf16[1,80,256]{2,1,0:T(8,128)(2,1)S(1)}, u32[]{:S(2)}, u32[]{:S(2)}) collective-permute-start(bf16[1,80,256]{2,1,0:T(8,128)(2,1)S(1)} %get-tuple-element.94.refs_4_), channel_id=1, source_target_pairs={{0,16},{4,20},{8,24},{12,28},{16,0},{20,4},{24,8},{28,12},{1,17},{... | collective-permute-start | bytes 122888 | tf_op jit(solution)/shard_map/ppermute | solution.py:502
  50.6 8.7 %collective-permute-start.15 = (bf16[1,80,256]{2,1,0:T(8,128)(2,1)S(1)}, bf16[1,80,256]{2,1,0:T(8,128)(2,1)S(1)}, u32[]{:S(2)}, u32[]{:S(2)}) collective-permute-start(bf16[1,80,256]{2,1,0:T(8,128)(2,1)S(1)} %get-tuple-element.94.refs_4_), channel_id=1, source_target_pairs={{0,8},{4,12},{8,0},{12,4},{16,24},{20,28},{24,16},{28,20},{1,9},{5... | collective-permute-start | bytes 122888 | tf_op jit(solution)/shard_map/ppermute | solution.py:502
  65.3 6.3 %collective-permute-start.19 = (bf16[4,80,256]{2,1,0:T(8,128)(2,1)S(1)}, bf16[4,80,256]{2,1,0:T(8,128)(2,1)S(1)}, u32[]{:S(2)}, u32[]{:S(2)}) collective-permute-start(bf16[4,80,256]{2,1,0:T(8,128)(2,1)S(1)} %get-tuple-element.95.one), channel_id=1, source_target_pairs={{0,1},{1,0},{2,3},{3,2},{4,5},{5,4},{6,7},{7,6},{8,9},{9,8},{10,11... | collective-permute-start | bytes 491528 | tf_op jit(solution)/shard_map/ppermute | solution.py:505
  65.8 6.0 %collective-permute-start.20 = (bf16[4,80,256]{2,1,0:T(8,128)(2,1)S(1)}, bf16[4,80,256]{2,1,0:T(8,128)(2,1)S(1)}, u32[]{:S(2)}, u32[]{:S(2)}) collective-permute-start(bf16[4,80,256]{2,1,0:T(8,128)(2,1)S(1)} %get-tuple-element.96.two), channel_id=1, source_target_pairs={{0,2},{1,3},{2,0},{3,1},{4,6},{5,7},{6,4},{7,5},{8,10},{9,11},{10,... | collective-permute-start | bytes 491528 | tf_op jit(solution)/shard_map/ppermute | solution.py:505
  71.9 5.4 %collective-permute-start.21 = (bf16[4,80,256]{2,1,0:T(8,128)(2,1)S(1)}, bf16[4,80,256]{2,1,0:T(8,128)(2,1)S(1)}, u32[]{:S(2)}, u32[]{:S(2)}) collective-permute-start(bf16[4,80,256]{2,1,0:T(8,128)(2,1)S(1)} %get-tuple-element.97.refs_0_), channel_id=1, source_target_pairs={{0,2},{1,3},{2,0},{3,1},{4,6},{5,7},{6,4},{7,5},{8,10},{9,11},{10,... | collective-permute-start | bytes 491528 | tf_op jit(solution)/shard_map/ppermute | solution.py:505
  72.4 5.3 %collective-permute-start.22 = (bf16[4,80,256]{2,1,0:T(8,128)(2,1)S(1)}, bf16[4,80,256]{2,1,0:T(8,128)(2,1)S(1)}, u32[]{:S(2)}, u32[]{:S(2)}) collective-permute-start(bf16[4,80,256]{2,1,0:T(8,128)(2,1)S(1)} %get-tuple-element.98.refs_2_), channel_id=1, source_target_pairs={{0,1},{1,0},{2,3},{3,2},{4,5},{5,4},{6,7},{7,6},{8,9},{9,8},{10,11... | collective-permute-start | bytes 491528 | tf_op jit(solution)/shard_map/ppermute | solution.py:505
  81.1 13.9 %collective-permute-start.24 = (bf16[3,80,256]{2,1,0:T(8,128)(2,1)S(1)}, bf16[3,80,256]{2,1,0:T(8,128)(2,1)S(1)}, u32[]{:S(2)}, u32[]{:S(2)}) collective-permute-start(bf16[3,80,256]{2,1,0:T(8,128)(2,1)S(1)} %get-tuple-element.113), channel_id=1, source_target_pairs={{0,16},{4,20},{8,24},{12,28},{16,0},{20,4},{24,8},{28,12},{1,17},{... | collective-permute-start | bytes 368648 | tf_op jit(solution)/shard_map/ppermute | solution.py:502
  81.3 13.7 %collective-permute-start.25 = (bf16[3,80,256]{2,1,0:T(8,128)(2,1)S(1)}, bf16[3,80,256]{2,1,0:T(8,128)(2,1)S(1)}, u32[]{:S(2)}, u32[]{:S(2)}) collective-permute-start(bf16[3,80,256]{2,1,0:T(8,128)(2,1)S(1)} %get-tuple-element.114), channel_id=1, source_target_pairs={{0,24},{4,28},{8,16},{12,20},{16,8},{20,12},{24,0},{28,4},{1,25},{... | collective-permute-start | bytes 368648 | tf_op jit(solution)/shard_map/ppermute | solution.py:502
  83.5 11.5 %collective-permute-start.26 = (bf16[3,80,256]{2,1,0:T(8,128)(2,1)S(1)}, bf16[3,80,256]{2,1,0:T(8,128)(2,1)S(1)}, u32[]{:S(2)}, u32[]{:S(2)}) collective-permute-start(bf16[3,80,256]{2,1,0:T(8,128)(2,1)S(1)} %get-tuple-element.115), channel_id=1, source_target_pairs={{0,8},{4,12},{8,0},{12,4},{16,24},{20,28},{24,16},{28,20},{1,9},{5... | collective-permute-start | bytes 368648 | tf_op jit(solution)/shard_map/ppermute | solution.py:502
  84.6 10.2 %collective-permute-start.31 = (bf16[1,80,256]{2,1,0:T(8,128)(2,1)S(1)}, bf16[1,80,256]{2,1,0:T(8,128)(2,1)S(1)}, u32[]{:S(2)}, u32[]{:S(2)}) collective-permute-start(bf16[1,80,256]{2,1,0:T(8,128)(2,1)S(1)} %get-tuple-element.121), channel_id=1, source_target_pairs={{0,8},{4,12},{8,0},{12,4},{16,24},{20,28},{24,16},{28,20},{1,9},{5... | collective-permute-start | bytes 122888 | tf_op jit(solution)/shard_map/ppermute | solution.py:502
  85.5 14.2 %collective-permute-start.30 = (bf16[1,80,256]{2,1,0:T(8,128)(2,1)S(1)}, bf16[1,80,256]{2,1,0:T(8,128)(2,1)S(1)}, u32[]{:S(2)}, u32[]{:S(2)}) collective-permute-start(bf16[1,80,256]{2,1,0:T(8,128)(2,1)S(1)} %get-tuple-element.119), channel_id=1, source_target_pairs={{0,8},{4,12},{8,0},{12,4},{16,24},{20,28},{24,16},{28,20},{1,9},{5... | collective-permute-start | bytes 122888 | tf_op jit(solution)/shard_map/ppermute | solution.py:502
  94.9 9.2 %collective-permute-start.32 = (bf16[1,80,256]{2,1,0:T(8,128)(2,1)S(1)}, bf16[1,80,256]{2,1,0:T(8,128)(2,1)S(1)}, u32[]{:S(2)}, u32[]{:S(2)}) collective-permute-start(bf16[1,80,256]{2,1,0:T(8,128)(2,1)S(1)} %shard_map.122), channel_id=1, source_target_pairs={{0,16},{4,20},{8,24},{12,28},{16,0},{20,4},{24,8},{28,12},{1,17},{... | collective-permute-start | bytes 122888 | tf_op jit(solution)/shard_map/ppermute | solution.py:502
  95.3 20.2 %collective-permute-start.29 = (bf16[3,80,256]{2,1,0:T(8,128)(2,1)S(1)}, bf16[3,80,256]{2,1,0:T(8,128)(2,1)S(1)}, u32[]{:S(2)}, u32[]{:S(2)}) collective-permute-start(bf16[3,80,256]{2,1,0:T(8,128)(2,1)S(1)} %get-tuple-element.117.refs_0_), channel_id=1, source_target_pairs={{0,24},{4,28},{8,16},{12,20},{16,8},{20,12},{24,0},{28,4},{1,25},{... | collective-permute-start | bytes 368648 | tf_op jit(solution)/shard_map/ppermute | solution.py:502
  97.2 18.3 %collective-permute-start.28 = (bf16[3,80,256]{2,1,0:T(8,128)(2,1)S(1)}, bf16[3,80,256]{2,1,0:T(8,128)(2,1)S(1)}, u32[]{:S(2)}, u32[]{:S(2)}) collective-permute-start(bf16[3,80,256]{2,1,0:T(8,128)(2,1)S(1)} %get-tuple-element.117.refs_0_), channel_id=1, source_target_pairs={{0,16},{4,20},{8,24},{12,28},{16,0},{20,4},{24,8},{28,12},{1,17},{... | collective-permute-start | bytes 368648 | tf_op jit(solution)/shard_map/ppermute | solution.py:502
  99.1 16.4 %collective-permute-start.27 = (bf16[3,80,256]{2,1,0:T(8,128)(2,1)S(1)}, bf16[3,80,256]{2,1,0:T(8,128)(2,1)S(1)}, u32[]{:S(2)}, u32[]{:S(2)}) collective-permute-start(bf16[3,80,256]{2,1,0:T(8,128)(2,1)S(1)} %get-tuple-element.117.refs_0_), channel_id=1, source_target_pairs={{0,8},{4,12},{8,0},{12,4},{16,24},{20,28},{24,16},{28,20},{1,9},{5... | collective-permute-start | bytes 368648 | tf_op jit(solution)/shard_map/ppermute | solution.py:502
  104.4 7.1 %collective-permute-start.34 = (bf16[1,80,256]{2,1,0:T(8,128)(2,1)S(1)}, bf16[1,80,256]{2,1,0:T(8,128)(2,1)S(1)}, u32[]{:S(2)}, u32[]{:S(2)}) collective-permute-start(bf16[1,80,256]{2,1,0:T(8,128)(2,1)S(1)} %get-tuple-element.123.refs_4_), channel_id=1, source_target_pairs={{0,16},{4,20},{8,24},{12,28},{16,0},{20,4},{24,8},{28,12},{1,17},{... | collective-permute-start | bytes 122888 | tf_op jit(solution)/shard_map/ppermute | solution.py:502
  104.4 7.4 %collective-permute-start.33 = (bf16[1,80,256]{2,1,0:T(8,128)(2,1)S(1)}, bf16[1,80,256]{2,1,0:T(8,128)(2,1)S(1)}, u32[]{:S(2)}, u32[]{:S(2)}) collective-permute-start(bf16[1,80,256]{2,1,0:T(8,128)(2,1)S(1)} %get-tuple-element.123.refs_4_), channel_id=1, source_target_pairs={{0,8},{4,12},{8,0},{12,4},{16,24},{20,28},{24,16},{28,20},{1,9},{5... | collective-permute-start | bytes 122888 | tf_op jit(solution)/shard_map/ppermute | solution.py:502
  117.9 5.5 %collective-permute-start.37 = (bf16[4,80,128]{2,1,0:T(8,128)(2,1)S(1)}, bf16[4,80,128]{2,1,0:T(8,128)(2,1)S(1)}, u32[]{:S(2)}, u32[]{:S(2)}) collective-permute-start(bf16[4,80,128]{2,1,0:T(8,128)(2,1)S(1)} %get-tuple-element.125), channel_id=1, source_target_pairs={{0,3},{1,2},{2,1},{3,0},{4,7},{5,6},{6,5},{7,4},{8,11},{9,10},{10,... | collective-permute-start | bytes 245768 | tf_op jit(solution)/shard_map/ppermute | solution.py:505
  (14 other events, 74.3 us)

commit v14 on v13

--- a/solution.py
+++ b/solution.py
@@ -473,7 +473,7 @@
     field = (members, levp, LANES)
     slab_field = (members, levp, lanes)
     panel = (members, levp, width)
-    some, rest = members // 4, members - members // 4
+    some, rest = members // 2, members - members // 2
     half_fields = [struct((members, levp, lanes // 2), BF16)] * 2
     via = chips == 4 and some > 0
     if via:

time: 127 us -> 120 us (0.945)
  waiting for transfers between devices: 65 us -> 55.1 us
  starting transfers between devices: 43 us -> 46.6 us
    ppermute x24, waiting for transfers between devices: 40.5 us -> 30.5 us  [along(): return lax.ppermute(x, 'slab', [(s, s ^ 2 * i) for s in range(n_slab)])]
    ppermute x24, starting transfers between devices: 28.9 us -> 31.9 us  [along(): return lax.ppermute(x, 'slab', [(s, s ^ 2 * i) for s in range(n_slab)])]
  transfers between devices with their start and end apart: 40 -> 40, of which waited for: 25 -> 31; matrix products, arithmetic and copies ran while one was open for 0% -> 0% of each run, Pallas kernels for 4% -> 4%
where the time goes in v14:
time: 120 us
  waiting for transfers between devices  55.1 us (46%)
  starting transfers between devices  46.6 us (39%)
  Pallas kernels  14.6 us (12%)
  local copies, waits for them, and re-layouts  2.1 us (2%)
  between operations  1.56 us (1%)
    ppermute x24, starting transfers between devices, along(): return lax.ppermute(x, 'slab', [(s, s ^ 2 * i) for s in range(n_slab)])  31.9 us
    ppermute x24, waiting for transfers between devices, along(): return lax.ppermute(x, 'slab', [(s, s ^ 2 * i) for s in range(n_slab)])  30.5 us
    ppermute x11, waiting for transfers between devices, plane(): return lax.ppermute(x, 'obs', [(o, o ^ i) for o in range(n_obs)])  20.3 us
    pallas_call x24, Pallas kernels, call(): pl.pallas_call(kernel, out_shape=outs, in_specs=[space] * len(args), out_...  14.6 us
    ppermute x11, starting transfers between devices, plane(): return lax.ppermute(x, 'obs', [(o, o ^ i) for o in range(n_obs)])  13.9 us
    ppermute x5, waiting for transfers between devices, swap(): return lax.ppermute(x, 'slab', [(s, s ^ 1) for s in range(n_slab)])  4.27 us
  transfers between devices with their start and end apart: 40, of which 31 were waited for; matrix products, arithmetic and copies ran while one was open for 0% of the time, Pallas kernels for 4%

profile of v14, /device:TPU:0, one launch (start us, length us, event | category | flops | bytes accessed | tf_op | source)
XLA Modules:
  0.0 120.0 jit_solution(15585118498780243367)
XLA Ops:
  1.3 5.1 %shard_map.104 = (bf16[4,4,128,256]{3,2,1,0:T(8,128)(2,1)}, bf16[4,4,128,256]{3,2,1,0:T(8,128)(2,1)}, bf16[4,80,256]{2,1,0:T(8,128)(2,1)}, bf16[4,80,256]{2,1,0:T(8,128)(2,1)}) custom-call(s32[4]{0:T(128)} %seeds_in.1, s32[1,1,32]{2,1,0:T(1,128)} %ids_in.1, s32[1,1,32]{2,1,0:T(1,128)} %cols_in.1, s32[1,1]{1,0:T(1,128)S(6)} %copy.16.count_in, ...), custom_call_target="tpu_custom_call" | custom-call | flops 671088640 | bytes 5751572 | tf_op jit(solution)/shard_map/pallas_call | solution.py:23
  6.9 3.1 %collective-permute-start = (bf16[4,80,256]{2,1,0:T(8,128)(2,1)}, bf16[4,80,256]{2,1,0:T(8,128)(2,1)S(1)}, u32[]{:S(2)}, u32[]{:S(2)}) collective-permute-start(bf16[4,80,256]{2,1,0:T(8,128)(2,1)} %get-tuple-element.68.refs_0_), channel_id=1, source_target_pairs={{0,1},{1,0},{2,3},{3,2},{4,5},{5,4},{6,7},{7,6},{8,9},{9,8},{10,11... | collective-permute-start | bytes 491528 | tf_op jit(solution)/shard_map/ppermute | solution.py:505
  13.5 1.5 %collective-permute-done.one_more = bf16[4,80,256]{2,1,0:T(8,128)(2,1)S(1)} collective-permute-done((bf16[4,80,256]{2,1,0:T(8,128)(2,1)}, bf16[4,80,256]{2,1,0:T(8,128)(2,1)S(1)}, u32[]{:S(2)}, u32[]{:S(2)}) %collective-permute-start) | collective-permute-done | bytes 163872 | tf_op jit(solution)/shard_map/ppermute | solution.py:505
  15.0 1.5 %collective-permute-done.1.two_more = bf16[4,80,256]{2,1,0:T(8,128)(2,1)S(1)} collective-permute-done((bf16[4,80,256]{2,1,0:T(8,128)(2,1)}, bf16[4,80,256]{2,1,0:T(8,128)(2,1)S(1)}, u32[]{:S(2)}, u32[]{:S(2)}) %collective-permute-start.1) | collective-permute-done | bytes 163872 | tf_op jit(solution)/shard_map/ppermute | solution.py:505
  18.5 3.7 %collective-permute-done.2.refs_1_ = bf16[4,80,256]{2,1,0:T(8,128)(2,1)S(1)} collective-permute-done((bf16[4,80,256]{2,1,0:T(8,128)(2,1)S(1)}, bf16[4,80,256]{2,1,0:T(8,128)(2,1)S(1)}, u32[]{:S(2)}, u32[]{:S(2)}) %collective-permute-start.2) | collective-permute-done | bytes 163872 | tf_op jit(solution)/shard_map/ppermute | solution.py:505
  26.2 2.1 %collective-permute-start.13 = (bf16[2,80,256]{2,1,0:T(8,128)(2,1)S(1)}, bf16[2,80,256]{2,1,0:T(8,128)(2,1)S(1)}, u32[]{:S(2)}, u32[]{:S(2)}) collective-permute-start(bf16[2,80,256]{2,1,0:T(8,128)(2,1)S(1)} %get-tuple-element.93), channel_id=1, source_target_pairs={{0,8},{4,12},{8,0},{12,4},{16,24},{20,28},{24,16},{28,20},{1,9},{5... | collective-permute-start | bytes 245768 | tf_op jit(solution)/shard_map/ppermute | solution.py:502
  28.4 3.0 %collective-permute-done.13.refs_1_ = bf16[2,80,256]{2,1,0:T(8,128)(2,1)S(1)} collective-permute-done((bf16[2,80,256]{2,1,0:T(8,128)(2,1)S(1)}, bf16[2,80,256]{2,1,0:T(8,128)(2,1)S(1)}, u32[]{:S(2)}, u32[]{:S(2)}) %collective-permute-start.13) | collective-permute-done | bytes 81952 | tf_op jit(solution)/shard_map/ppermute | solution.py:502
  31.5 2.5 %collective-permute-start.14 = (bf16[2,80,256]{2,1,0:T(8,128)(2,1)S(1)}, bf16[2,80,256]{2,1,0:T(8,128)(2,1)S(1)}, u32[]{:S(2)}, u32[]{:S(2)}) collective-permute-start(bf16[2,80,256]{2,1,0:T(8,128)(2,1)S(1)} %shard_map.112), channel_id=1, source_target_pairs={{0,16},{4,20},{8,24},{12,28},{16,0},{20,4},{24,8},{28,12},{1,17},{... | collective-permute-start | bytes 245768 | tf_op jit(solution)/shard_map/ppermute | solution.py:502
  34.5 3.8 %collective-permute-start.7 = (bf16[2,80,256]{2,1,0:T(8,128)(2,1)S(1)}, bf16[2,80,256]{2,1,0:T(8,128)(2,1)S(1)}, u32[]{:S(2)}, u32[]{:S(2)}) collective-permute-start(bf16[2,80,256]{2,1,0:T(8,128)(2,1)S(1)} %get-tuple-element.87), channel_id=1, source_target_pairs={{0,24},{4,28},{8,16},{12,20},{16,8},{20,12},{24,0},{28,4},{1,25},{... | collective-permute-start | bytes 245768 | tf_op jit(solution)/shard_map/ppermute | solution.py:502
  38.5 2.7 %collective-permute-done.14.refs_2_ = bf16[2,80,256]{2,1,0:T(8,128)(2,1)S(1)} collective-permute-done((bf16[2,80,256]{2,1,0:T(8,128)(2,1)S(1)}, bf16[2,80,256]{2,1,0:T(8,128)(2,1)S(1)}, u32[]{:S(2)}, u32[]{:S(2)}) %collective-permute-start.14) | collective-permute-done | bytes 81952 | tf_op jit(solution)/shard_map/ppermute | solution.py:502
  41.4 2.7 %collective-permute-done.6.refs_1_ = bf16[2,80,256]{2,1,0:T(8,128)(2,1)S(1)} collective-permute-done((bf16[2,80,256]{2,1,0:T(8,128)(2,1)S(1)}, bf16[2,80,256]{2,1,0:T(8,128)(2,1)S(1)}, u32[]{:S(2)}, u32[]{:S(2)}) %collective-permute-start.6) | collective-permute-done | bytes 81952 | tf_op jit(solution)/shard_map/ppermute | solution.py:502
  44.3 4.1 %collective-permute-start.11 = (bf16[2,80,256]{2,1,0:T(8,128)(2,1)S(1)}, bf16[2,80,256]{2,1,0:T(8,128)(2,1)S(1)}, u32[]{:S(2)}, u32[]{:S(2)}) collective-permute-start(bf16[2,80,256]{2,1,0:T(8,128)(2,1)S(1)} %get-tuple-element.89.refs_0_), channel_id=1, source_target_pairs={{0,24},{4,28},{8,16},{12,20},{16,8},{20,12},{24,0},{28,4},{1,25},{... | collective-permute-start | bytes 245768 | tf_op jit(solution)/shard_map/ppermute | solution.py:502
  49.8 1.5 %collective-permute-start.15 = (bf16[2,80,256]{2,1,0:T(8,128)(2,1)S(1)}, bf16[2,80,256]{2,1,0:T(8,128)(2,1)S(1)}, u32[]{:S(2)}, u32[]{:S(2)}) collective-permute-start(bf16[2,80,256]{2,1,0:T(8,128)(2,1)S(1)} %get-tuple-element.94.refs_4_), channel_id=1, source_target_pairs={{0,8},{4,12},{8,0},{12,4},{16,24},{20,28},{24,16},{28,20},{1,9},{5... | collective-permute-start | bytes 245768 | tf_op jit(solution)/shard_map/ppermute | solution.py:502
  51.8 3.5 %collective-permute-done.10.refs_2_ = bf16[2,80,256]{2,1,0:T(8,128)(2,1)S(1)} collective-permute-done((bf16[2,80,256]{2,1,0:T(8,128)(2,1)S(1)}, bf16[2,80,256]{2,1,0:T(8,128)(2,1)S(1)}, u32[]{:S(2)}, u32[]{:S(2)}) %collective-permute-start.10) | collective-permute-done | bytes 81952 | tf_op jit(solution)/shard_map/ppermute | solution.py:502
  62.0 4.5 %collective-permute-done.19.one_more = bf16[4,80,256]{2,1,0:T(8,128)(2,1)S(1)} collective-permute-done((bf16[4,80,256]{2,1,0:T(8,128)(2,1)S(1)}, bf16[4,80,256]{2,1,0:T(8,128)(2,1)S(1)}, u32[]{:S(2)}, u32[]{:S(2)}) %collective-permute-start.19) | collective-permute-done | bytes 163872 | tf_op jit(solution)/shard_map/ppermute | solution.py:505
  68.2 1.7 %collective-permute-start.22 = (bf16[4,80,256]{2,1,0:T(8,128)(2,1)S(1)}, bf16[4,80,256]{2,1,0:T(8,128)(2,1)S(1)}, u32[]{:S(2)}, u32[]{:S(2)}) collective-permute-start(bf16[4,80,256]{2,1,0:T(8,128)(2,1)S(1)} %get-tuple-element.98.refs_2_), channel_id=1, source_target_pairs={{0,1},{1,0},{2,3},{3,2},{4,5},{5,4},{6,7},{7,6},{8,9},{9,8},{10,11... | collective-permute-start | bytes 491528 | tf_op jit(solution)/shard_map/ppermute | solution.py:505
  69.9 2.6 %collective-permute-done.21.refs_1_ = bf16[4,80,256]{2,1,0:T(8,128)(2,1)S(1)} collective-permute-done((bf16[4,80,256]{2,1,0:T(8,128)(2,1)S(1)}, bf16[4,80,256]{2,1,0:T(8,128)(2,1)S(1)}, u32[]{:S(2)}, u32[]{:S(2)}) %collective-permute-start.21) | collective-permute-done | bytes 163872 | tf_op jit(solution)/shard_map/ppermute | solution.py:505
  79.0 3.3 %collective-permute-done.31.refs_1_ = bf16[2,80,256]{2,1,0:T(8,128)(2,1)S(1)} collective-permute-done((bf16[2,80,256]{2,1,0:T(8,128)(2,1)S(1)}, bf16[2,80,256]{2,1,0:T(8,128)(2,1)S(1)}, u32[]{:S(2)}, u32[]{:S(2)}) %collective-permute-start.31) | collective-permute-done | bytes 81952 | tf_op jit(solution)/shard_map/ppermute | solution.py:502
  82.4 1.7 %collective-permute-start.32 = (bf16[2,80,256]{2,1,0:T(8,128)(2,1)S(1)}, bf16[2,80,256]{2,1,0:T(8,128)(2,1)S(1)}, u32[]{:S(2)}, u32[]{:S(2)}) collective-permute-start(bf16[2,80,256]{2,1,0:T(8,128)(2,1)S(1)} %shard_map.122), channel_id=1, source_target_pairs={{0,16},{4,20},{8,24},{12,28},{16,0},{20,4},{24,8},{28,12},{1,17},{... | collective-permute-start | bytes 245768 | tf_op jit(solution)/shard_map/ppermute | solution.py:502
  84.1 1.3 %collective-permute-start.24 = (bf16[2,80,256]{2,1,0:T(8,128)(2,1)S(1)}, bf16[2,80,256]{2,1,0:T(8,128)(2,1)S(1)}, u32[]{:S(2)}, u32[]{:S(2)}) collective-permute-start(bf16[2,80,256]{2,1,0:T(8,128)(2,1)S(1)} %get-tuple-element.113), channel_id=1, source_target_pairs={{0,16},{4,20},{8,24},{12,28},{16,0},{20,4},{24,8},{28,12},{1,17},{... | collective-permute-start | bytes 245768 | tf_op jit(solution)/shard_map/ppermute | solution.py:502
  85.4 3.3 %collective-permute-start.25 = (bf16[2,80,256]{2,1,0:T(8,128)(2,1)S(1)}, bf16[2,80,256]{2,1,0:T(8,128)(2,1)S(1)}, u32[]{:S(2)}, u32[]{:S(2)}) collective-permute-start(bf16[2,80,256]{2,1,0:T(8,128)(2,1)S(1)} %get-tuple-element.114), channel_id=1, source_target_pairs={{0,24},{4,28},{8,16},{12,20},{16,8},{20,12},{24,0},{28,4},{1,25},{... | collective-permute-start | bytes 245768 | tf_op jit(solution)/shard_map/ppermute | solution.py:502
  88.7 4.4 %collective-permute-done.32.refs_2_ = bf16[2,80,256]{2,1,0:T(8,128)(2,1)S(1)} collective-permute-done((bf16[2,80,256]{2,1,0:T(8,128)(2,1)S(1)}, bf16[2,80,256]{2,1,0:T(8,128)(2,1)S(1)}, u32[]{:S(2)}, u32[]{:S(2)}) %collective-permute-start.32) | collective-permute-done | bytes 81952 | tf_op jit(solution)/shard_map/ppermute | solution.py:502
  93.4 1.5 %collective-permute-done.24.refs_1_ = bf16[2,80,256]{2,1,0:T(8,128)(2,1)S(1)} collective-permute-done((bf16[2,80,256]{2,1,0:T(8,128)(2,1)S(1)}, bf16[2,80,256]{2,1,0:T(8,128)(2,1)S(1)}, u32[]{:S(2)}, u32[]{:S(2)}) %collective-permute-start.24) | collective-permute-done | bytes 81952 | tf_op jit(solution)/shard_map/ppermute | solution.py:502
  95.4 2.5 %collective-permute-start.29 = (bf16[2,80,256]{2,1,0:T(8,128)(2,1)S(1)}, bf16[2,80,256]{2,1,0:T(8,128)(2,1)S(1)}, u32[]{:S(2)}, u32[]{:S(2)}) collective-permute-start(bf16[2,80,256]{2,1,0:T(8,128)(2,1)S(1)} %get-tuple-element.117.refs_0_), channel_id=1, source_target_pairs={{0,24},{4,28},{8,16},{12,20},{16,8},{20,12},{24,0},{28,4},{1,25},{... | collective-permute-start | bytes 245768 | tf_op jit(solution)/shard_map/ppermute | solution.py:502
  97.9 1.8 %collective-permute-start.28 = (bf16[2,80,256]{2,1,0:T(8,128)(2,1)S(1)}, bf16[2,80,256]{2,1,0:T(8,128)(2,1)S(1)}, u32[]{:S(2)}, u32[]{:S(2)}) collective-permute-start(bf16[2,80,256]{2,1,0:T(8,128)(2,1)S(1)} %get-tuple-element.117.refs_0_), channel_id=1, source_target_pairs={{0,16},{4,20},{8,24},{12,28},{16,0},{20,4},{24,8},{28,12},{1,17},{... | collective-permute-start | bytes 245768 | tf_op jit(solution)/shard_map/ppermute | solution.py:502
  100.2 1.5 %collective-permute-start.33 = (bf16[2,80,256]{2,1,0:T(8,128)(2,1)S(1)}, bf16[2,80,256]{2,1,0:T(8,128)(2,1)S(1)}, u32[]{:S(2)}, u32[]{:S(2)}) collective-permute-start(bf16[2,80,256]{2,1,0:T(8,128)(2,1)S(1)} %get-tuple-element.123.refs_4_), channel_id=1, source_target_pairs={{0,8},{4,12},{8,0},{12,4},{16,24},{20,28},{24,16},{28,20},{1,9},{5... | collective-permute-start | bytes 245768 | tf_op jit(solution)/shard_map/ppermute | solution.py:502
  102.2 4.4 %collective-permute-done.28.refs_2_ = bf16[2,80,256]{2,1,0:T(8,128)(2,1)S(1)} collective-permute-done((bf16[2,80,256]{2,1,0:T(8,128)(2,1)S(1)}, bf16[2,80,256]{2,1,0:T(8,128)(2,1)S(1)}, u32[]{:S(2)}, u32[]{:S(2)}) %collective-permute-start.28) | collective-permute-done | bytes 81952 | tf_op jit(solution)/shard_map/ppermute | solution.py:502
  106.6 1.4 %collective-permute-done.33.refs_5_ = bf16[2,80,256]{2,1,0:T(8,128)(2,1)S(1)} collective-permute-done((bf16[2,80,256]{2,1,0:T(8,128)(2,1)S(1)}, bf16[2,80,256]{2,1,0:T(8,128)(2,1)S(1)}, u32[]{:S(2)}, u32[]{:S(2)}) %collective-permute-start.33) | collective-permute-done | bytes 81952 | tf_op jit(solution)/shard_map/ppermute | solution.py:502
  111.2 1.8 %collective-permute-start.37 = (bf16[4,80,128]{2,1,0:T(8,128)(2,1)S(1)}, bf16[4,80,128]{2,1,0:T(8,128)(2,1)S(1)}, u32[]{:S(2)}, u32[]{:S(2)}) collective-permute-start(bf16[4,80,128]{2,1,0:T(8,128)(2,1)S(1)} %get-tuple-element.125), channel_id=1, source_target_pairs={{0,3},{1,2},{2,1},{3,0},{4,7},{5,6},{6,5},{7,4},{8,11},{9,10},{10,... | collective-permute-start | bytes 245768 | tf_op jit(solution)/shard_map/ppermute | solution.py:505
  113.1 1.4 %collective-permute-start.38 = (bf16[4,80,128]{2,1,0:T(8,128)(2,1)S(1)}, bf16[4,80,128]{2,1,0:T(8,128)(2,1)S(1)}, u32[]{:S(2)}, u32[]{:S(2)}) collective-permute-start(bf16[4,80,128]{2,1,0:T(8,128)(2,1)S(1)} %get-tuple-element.126), channel_id=1, source_target_pairs={{0,2},{1,3},{2,0},{3,1},{4,6},{5,7},{6,4},{7,5},{8,10},{9,11},{10,... | collective-permute-start | bytes 245768 | tf_op jit(solution)/shard_map/ppermute | solution.py:505
  114.8 2.0 %collective-permute-done.37.refs_1_ = bf16[4,80,128]{2,1,0:T(8,128)(2,1)S(1)} collective-permute-done((bf16[4,80,128]{2,1,0:T(8,128)(2,1)S(1)}, bf16[4,80,128]{2,1,0:T(8,128)(2,1)S(1)}, u32[]{:S(2)}, u32[]{:S(2)}) %collective-permute-start.37) | collective-permute-done | bytes 81952 | tf_op jit(solution)/shard_map/ppermute | solution.py:505
  116.8 1.7 %collective-permute-done.38.refs_2_ = bf16[4,80,128]{2,1,0:T(8,128)(2,1)S(1)} collective-permute-done((bf16[4,80,128]{2,1,0:T(8,128)(2,1)S(1)}, bf16[4,80,128]{2,1,0:T(8,128)(2,1)S(1)}, u32[]{:S(2)}, u32[]{:S(2)}) %collective-permute-start.38) | collective-permute-done | bytes 81952 | tf_op jit(solution)/shard_map/ppermute | solution.py:505
  (91 shorter events, 35.1 us)
Async XLA Ops:
  6.4 19.3 %collective-permute-start.5 = (bf16[4,4,128,256]{3,2,1,0:T(8,128)(2,1)}, bf16[4,4,128,256]{3,2,1,0:T(8,128)(2,1)S(1)}, u32[]{:S(2)}, u32[]{:S(2)}) collective-permute-start(bf16[4,4,128,256]{3,2,1,0:T(8,128)(2,1)} %get-tuple-element.75), channel_id=1, source_target_pairs={{0,4},{4,0},{8,12},{12,8},{16,20},{20,16},{24,28},{28,24},{1,5},{5... | collective-permute-start | bytes 3145736 | tf_op jit(solution)/shard_map/ppermute | solution.py:508
  6.9 8.1 %collective-permute-start = (bf16[4,80,256]{2,1,0:T(8,128)(2,1)}, bf16[4,80,256]{2,1,0:T(8,128)(2,1)S(1)}, u32[]{:S(2)}, u32[]{:S(2)}) collective-permute-start(bf16[4,80,256]{2,1,0:T(8,128)(2,1)} %get-tuple-element.68.refs_0_), channel_id=1, source_target_pairs={{0,1},{1,0},{2,3},{3,2},{4,5},{5,4},{6,7},{7,6},{8,9},{9,8},{10,11... | collective-permute-start | bytes 491528 | tf_op jit(solution)/shard_map/ppermute | solution.py:505
  10.0 6.5 %collective-permute-start.1 = (bf16[4,80,256]{2,1,0:T(8,128)(2,1)}, bf16[4,80,256]{2,1,0:T(8,128)(2,1)S(1)}, u32[]{:S(2)}, u32[]{:S(2)}) collective-permute-start(bf16[4,80,256]{2,1,0:T(8,128)(2,1)} %get-tuple-element.69.refs_1_), channel_id=1, source_target_pairs={{0,2},{1,3},{2,0},{3,1},{4,6},{5,7},{6,4},{7,5},{8,10},{9,11},{10,... | collective-permute-start | bytes 491528 | tf_op jit(solution)/shard_map/ppermute | solution.py:505
  16.6 5.5 %collective-permute-start.2 = (bf16[4,80,256]{2,1,0:T(8,128)(2,1)S(1)}, bf16[4,80,256]{2,1,0:T(8,128)(2,1)S(1)}, u32[]{:S(2)}, u32[]{:S(2)}) collective-permute-start(bf16[4,80,256]{2,1,0:T(8,128)(2,1)S(1)} %get-tuple-element.72.refs_0_), channel_id=1, source_target_pairs={{0,2},{1,3},{2,0},{3,1},{4,6},{5,7},{6,4},{7,5},{8,10},{9,11},{10,... | collective-permute-start | bytes 491528 | tf_op jit(solution)/shard_map/ppermute | solution.py:505
  28.4 10.1 %collective-permute-start.12 = (bf16[2,80,256]{2,1,0:T(8,128)(2,1)S(1)}, bf16[2,80,256]{2,1,0:T(8,128)(2,1)S(1)}, u32[]{:S(2)}, u32[]{:S(2)}) collective-permute-start(bf16[2,80,256]{2,1,0:T(8,128)(2,1)S(1)} %get-tuple-element.91), channel_id=1, source_target_pairs={{0,8},{4,12},{8,0},{12,4},{16,24},{20,28},{24,16},{28,20},{1,9},{5... | collective-permute-start | bytes 245768 | tf_op jit(solution)/shard_map/ppermute | solution.py:502
  31.5 9.6 %collective-permute-start.14 = (bf16[2,80,256]{2,1,0:T(8,128)(2,1)S(1)}, bf16[2,80,256]{2,1,0:T(8,128)(2,1)S(1)}, u32[]{:S(2)}, u32[]{:S(2)}) collective-permute-start(bf16[2,80,256]{2,1,0:T(8,128)(2,1)S(1)} %shard_map.112), channel_id=1, source_target_pairs={{0,16},{4,20},{8,24},{12,28},{16,0},{20,4},{24,8},{28,12},{1,17},{... | collective-permute-start | bytes 245768 | tf_op jit(solution)/shard_map/ppermute | solution.py:502
  34.0 10.1 %collective-permute-start.6 = (bf16[2,80,256]{2,1,0:T(8,128)(2,1)S(1)}, bf16[2,80,256]{2,1,0:T(8,128)(2,1)S(1)}, u32[]{:S(2)}, u32[]{:S(2)}) collective-permute-start(bf16[2,80,256]{2,1,0:T(8,128)(2,1)S(1)} %get-tuple-element.86), channel_id=1, source_target_pairs={{0,16},{4,20},{8,24},{12,28},{16,0},{20,4},{24,8},{28,12},{1,17},{... | collective-permute-start | bytes 245768 | tf_op jit(solution)/shard_map/ppermute | solution.py:502
  34.5 9.5 %collective-permute-start.7 = (bf16[2,80,256]{2,1,0:T(8,128)(2,1)S(1)}, bf16[2,80,256]{2,1,0:T(8,128)(2,1)S(1)}, u32[]{:S(2)}, u32[]{:S(2)}) collective-permute-start(bf16[2,80,256]{2,1,0:T(8,128)(2,1)S(1)} %get-tuple-element.87), channel_id=1, source_target_pairs={{0,24},{4,28},{8,16},{12,20},{16,8},{20,12},{24,0},{28,4},{1,25},{... | collective-permute-start | bytes 245768 | tf_op jit(solution)/shard_map/ppermute | solution.py:502
  38.3 5.8 %collective-permute-start.8 = (bf16[2,80,256]{2,1,0:T(8,128)(2,1)S(1)}, bf16[2,80,256]{2,1,0:T(8,128)(2,1)S(1)}, u32[]{:S(2)}, u32[]{:S(2)}) collective-permute-start(bf16[2,80,256]{2,1,0:T(8,128)(2,1)S(1)} %get-tuple-element.88), channel_id=1, source_target_pairs={{0,8},{4,12},{8,0},{12,4},{16,24},{20,28},{24,16},{28,20},{1,9},{5... | collective-permute-start | bytes 245768 | tf_op jit(solution)/shard_map/ppermute | solution.py:502
  41.3 10.1 %collective-permute-start.16 = (bf16[2,80,256]{2,1,0:T(8,128)(2,1)S(1)}, bf16[2,80,256]{2,1,0:T(8,128)(2,1)S(1)}, u32[]{:S(2)}, u32[]{:S(2)}) collective-permute-start(bf16[2,80,256]{2,1,0:T(8,128)(2,1)S(1)} %get-tuple-element.94.refs_4_), channel_id=1, source_target_pairs={{0,16},{4,20},{8,24},{12,28},{16,0},{20,4},{24,8},{28,12},{1,17},{... | collective-permute-start | bytes 245768 | tf_op jit(solution)/shard_map/ppermute | solution.py:502
  44.3 7.6 %collective-permute-start.11 = (bf16[2,80,256]{2,1,0:T(8,128)(2,1)S(1)}, bf16[2,80,256]{2,1,0:T(8,128)(2,1)S(1)}, u32[]{:S(2)}, u32[]{:S(2)}) collective-permute-start(bf16[2,80,256]{2,1,0:T(8,128)(2,1)S(1)} %get-tuple-element.89.refs_0_), channel_id=1, source_target_pairs={{0,24},{4,28},{8,16},{12,20},{16,8},{20,12},{24,0},{28,4},{1,25},{... | collective-permute-start | bytes 245768 | tf_op jit(solution)/shard_map/ppermute | solution.py:502
  48.4 7.0 %collective-permute-start.10 = (bf16[2,80,256]{2,1,0:T(8,128)(2,1)S(1)}, bf16[2,80,256]{2,1,0:T(8,128)(2,1)S(1)}, u32[]{:S(2)}, u32[]{:S(2)}) collective-permute-start(bf16[2,80,256]{2,1,0:T(8,128)(2,1)S(1)} %get-tuple-element.89.refs_0_), channel_id=1, source_target_pairs={{0,16},{4,20},{8,24},{12,28},{16,0},{20,4},{24,8},{28,12},{1,17},{... | collective-permute-start | bytes 245768 | tf_op jit(solution)/shard_map/ppermute | solution.py:502
  49.3 6.7 %collective-permute-start.9 = (bf16[2,80,256]{2,1,0:T(8,128)(2,1)S(1)}, bf16[2,80,256]{2,1,0:T(8,128)(2,1)S(1)}, u32[]{:S(2)}, u32[]{:S(2)}) collective-permute-start(bf16[2,80,256]{2,1,0:T(8,128)(2,1)S(1)} %get-tuple-element.89.refs_0_), channel_id=1, source_target_pairs={{0,8},{4,12},{8,0},{12,4},{16,24},{20,28},{24,16},{28,20},{1,9},{5... | collective-permute-start | bytes 245768 | tf_op jit(solution)/shard_map/ppermute | solution.py:502
  49.8 7.2 %collective-permute-start.15 = (bf16[2,80,256]{2,1,0:T(8,128)(2,1)S(1)}, bf16[2,80,256]{2,1,0:T(8,128)(2,1)S(1)}, u32[]{:S(2)}, u32[]{:S(2)}) collective-permute-start(bf16[2,80,256]{2,1,0:T(8,128)(2,1)S(1)} %get-tuple-element.94.refs_4_), channel_id=1, source_target_pairs={{0,8},{4,12},{8,0},{12,4},{16,24},{20,28},{24,16},{28,20},{1,9},{5... | collective-permute-start | bytes 245768 | tf_op jit(solution)/shard_map/ppermute | solution.py:502
  51.4 6.6 %collective-permute-start.17 = (bf16[2,80,256]{2,1,0:T(8,128)(2,1)S(1)}, bf16[2,80,256]{2,1,0:T(8,128)(2,1)S(1)}, u32[]{:S(2)}, u32[]{:S(2)}) collective-permute-start(bf16[2,80,256]{2,1,0:T(8,128)(2,1)S(1)} %collective-permute-done.16.refs_6_), channel_id=1, source_target_pairs={{0,8},{4,12},{8,0},{12,4},{16,24},{20,28},{24,16},{28,20},{1,9},{5... | collective-permute-start | bytes 245768 | tf_op jit(solution)/shard_map/ppermute | solution.py:502
  60.3 6.3 %collective-permute-start.19 = (bf16[4,80,256]{2,1,0:T(8,128)(2,1)S(1)}, bf16[4,80,256]{2,1,0:T(8,128)(2,1)S(1)}, u32[]{:S(2)}, u32[]{:S(2)}) collective-permute-start(bf16[4,80,256]{2,1,0:T(8,128)(2,1)S(1)} %get-tuple-element.95.one), channel_id=1, source_target_pairs={{0,1},{1,0},{2,3},{3,2},{4,5},{5,4},{6,7},{7,6},{8,9},{9,8},{10,11... | collective-permute-start | bytes 491528 | tf_op jit(solution)/shard_map/ppermute | solution.py:505
  61.0 6.0 %collective-permute-start.20 = (bf16[4,80,256]{2,1,0:T(8,128)(2,1)S(1)}, bf16[4,80,256]{2,1,0:T(8,128)(2,1)S(1)}, u32[]{:S(2)}, u32[]{:S(2)}) collective-permute-start(bf16[4,80,256]{2,1,0:T(8,128)(2,1)S(1)} %get-tuple-element.96.two), channel_id=1, source_target_pairs={{0,2},{1,3},{2,0},{3,1},{4,6},{5,7},{6,4},{7,5},{8,10},{9,11},{10,... | collective-permute-start | bytes 491528 | tf_op jit(solution)/shard_map/ppermute | solution.py:505
  67.1 5.4 %collective-permute-start.21 = (bf16[4,80,256]{2,1,0:T(8,128)(2,1)S(1)}, bf16[4,80,256]{2,1,0:T(8,128)(2,1)S(1)}, u32[]{:S(2)}, u32[]{:S(2)}) collective-permute-start(bf16[4,80,256]{2,1,0:T(8,128)(2,1)S(1)} %get-tuple-element.97.refs_0_), channel_id=1, source_target_pairs={{0,2},{1,3},{2,0},{3,1},{4,6},{5,7},{6,4},{7,5},{8,10},{9,11},{10,... | collective-permute-start | bytes 491528 | tf_op jit(solution)/shard_map/ppermute | solution.py:505
  76.9 5.4 %collective-permute-start.31 = (bf16[2,80,256]{2,1,0:T(8,128)(2,1)S(1)}, bf16[2,80,256]{2,1,0:T(8,128)(2,1)S(1)}, u32[]{:S(2)}, u32[]{:S(2)}) collective-permute-start(bf16[2,80,256]{2,1,0:T(8,128)(2,1)S(1)} %get-tuple-element.121), channel_id=1, source_target_pairs={{0,8},{4,12},{8,0},{12,4},{16,24},{20,28},{24,16},{28,20},{1,9},{5... | collective-permute-start | bytes 245768 | tf_op jit(solution)/shard_map/ppermute | solution.py:502
  78.1 10.6 %collective-permute-start.30 = (bf16[2,80,256]{2,1,0:T(8,128)(2,1)S(1)}, bf16[2,80,256]{2,1,0:T(8,128)(2,1)S(1)}, u32[]{:S(2)}, u32[]{:S(2)}) collective-permute-start(bf16[2,80,256]{2,1,0:T(8,128)(2,1)S(1)} %get-tuple-element.119), channel_id=1, source_target_pairs={{0,8},{4,12},{8,0},{12,4},{16,24},{20,28},{24,16},{28,20},{1,9},{5... | collective-permute-start | bytes 245768 | tf_op jit(solution)/shard_map/ppermute | solution.py:502
  82.4 10.7 %collective-permute-start.32 = (bf16[2,80,256]{2,1,0:T(8,128)(2,1)S(1)}, bf16[2,80,256]{2,1,0:T(8,128)(2,1)S(1)}, u32[]{:S(2)}, u32[]{:S(2)}) collective-permute-start(bf16[2,80,256]{2,1,0:T(8,128)(2,1)S(1)} %shard_map.122), channel_id=1, source_target_pairs={{0,16},{4,20},{8,24},{12,28},{16,0},{20,4},{24,8},{28,12},{1,17},{... | collective-permute-start | bytes 245768 | tf_op jit(solution)/shard_map/ppermute | solution.py:502
  84.1 10.8 %collective-permute-start.24 = (bf16[2,80,256]{2,1,0:T(8,128)(2,1)S(1)}, bf16[2,80,256]{2,1,0:T(8,128)(2,1)S(1)}, u32[]{:S(2)}, u32[]{:S(2)}) collective-permute-start(bf16[2,80,256]{2,1,0:T(8,128)(2,1)S(1)} %get-tuple-element.113), channel_id=1, source_target_pairs={{0,16},{4,20},{8,24},{12,28},{16,0},{20,4},{24,8},{28,12},{1,17},{... | collective-permute-start | bytes 245768 | tf_op jit(solution)/shard_map/ppermute | solution.py:502
  85.4 9.5 %collective-permute-start.25 = (bf16[2,80,256]{2,1,0:T(8,128)(2,1)S(1)}, bf16[2,80,256]{2,1,0:T(8,128)(2,1)S(1)}, u32[]{:S(2)}, u32[]{:S(2)}) collective-permute-start(bf16[2,80,256]{2,1,0:T(8,128)(2,1)S(1)} %get-tuple-element.114), channel_id=1, source_target_pairs={{0,24},{4,28},{8,16},{12,20},{16,8},{20,12},{24,0},{28,4},{1,25},{... | collective-permute-start | bytes 245768 | tf_op jit(solution)/shard_map/ppermute | solution.py:502
  88.7 6.4 %collective-permute-start.26 = (bf16[2,80,256]{2,1,0:T(8,128)(2,1)S(1)}, bf16[2,80,256]{2,1,0:T(8,128)(2,1)S(1)}, u32[]{:S(2)}, u32[]{:S(2)}) collective-permute-start(bf16[2,80,256]{2,1,0:T(8,128)(2,1)S(1)} %get-tuple-element.115), channel_id=1, source_target_pairs={{0,8},{4,12},{8,0},{12,4},{16,24},{20,28},{24,16},{28,20},{1,9},{5... | collective-permute-start | bytes 245768 | tf_op jit(solution)/shard_map/ppermute | solution.py:502
  93.3 8.4 %collective-permute-start.34 = (bf16[2,80,256]{2,1,0:T(8,128)(2,1)S(1)}, bf16[2,80,256]{2,1,0:T(8,128)(2,1)S(1)}, u32[]{:S(2)}, u32[]{:S(2)}) collective-permute-start(bf16[2,80,256]{2,1,0:T(8,128)(2,1)S(1)} %get-tuple-element.123.refs_4_), channel_id=1, source_target_pairs={{0,16},{4,20},{8,24},{12,28},{16,0},{20,4},{24,8},{28,12},{1,17},{... | collective-permute-start | bytes 245768 | tf_op jit(solution)/shard_map/ppermute | solution.py:502
  95.4 6.8 %collective-permute-start.29 = (bf16[2,80,256]{2,1,0:T(8,128)(2,1)S(1)}, bf16[2,80,256]{2,1,0:T(8,128)(2,1)S(1)}, u32[]{:S(2)}, u32[]{:S(2)}) collective-permute-start(bf16[2,80,256]{2,1,0:T(8,128)(2,1)S(1)} %get-tuple-element.117.refs_0_), channel_id=1, source_target_pairs={{0,24},{4,28},{8,16},{12,20},{16,8},{20,12},{24,0},{28,4},{1,25},{... | collective-permute-start | bytes 245768 | tf_op jit(solution)/shard_map/ppermute | solution.py:502
  97.9 8.7 %collective-permute-start.28 = (bf16[2,80,256]{2,1,0:T(8,128)(2,1)S(1)}, bf16[2,80,256]{2,1,0:T(8,128)(2,1)S(1)}, u32[]{:S(2)}, u32[]{:S(2)}) collective-permute-start(bf16[2,80,256]{2,1,0:T(8,128)(2,1)S(1)} %get-tuple-element.117.refs_0_), channel_id=1, source_target_pairs={{0,16},{4,20},{8,24},{12,28},{16,0},{20,4},{24,8},{28,12},{1,17},{... | collective-permute-start | bytes 245768 | tf_op jit(solution)/shard_map/ppermute | solution.py:502
  99.7 6.9 %collective-permute-start.27 = (bf16[2,80,256]{2,1,0:T(8,128)(2,1)S(1)}, bf16[2,80,256]{2,1,0:T(8,128)(2,1)S(1)}, u32[]{:S(2)}, u32[]{:S(2)}) collective-permute-start(bf16[2,80,256]{2,1,0:T(8,128)(2,1)S(1)} %get-tuple-element.117.refs_0_), channel_id=1, source_target_pairs={{0,8},{4,12},{8,0},{12,4},{16,24},{20,28},{24,16},{28,20},{1,9},{5... | collective-permute-start | bytes 245768 | tf_op jit(solution)/shard_map/ppermute | solution.py:502
  100.2 7.8 %collective-permute-start.33 = (bf16[2,80,256]{2,1,0:T(8,128)(2,1)S(1)}, bf16[2,80,256]{2,1,0:T(8,128)(2,1)S(1)}, u32[]{:S(2)}, u32[]{:S(2)}) collective-permute-start(bf16[2,80,256]{2,1,0:T(8,128)(2,1)S(1)} %get-tuple-element.123.refs_4_), channel_id=1, source_target_pairs={{0,8},{4,12},{8,0},{12,4},{16,24},{20,28},{24,16},{28,20},{1,9},{5... | collective-permute-start | bytes 245768 | tf_op jit(solution)/shard_map/ppermute | solution.py:502
  101.7 7.1 %collective-permute-start.35 = (bf16[2,80,256]{2,1,0:T(8,128)(2,1)S(1)}, bf16[2,80,256]{2,1,0:T(8,128)(2,1)S(1)}, u32[]{:S(2)}, u32[]{:S(2)}) collective-permute-start(bf16[2,80,256]{2,1,0:T(8,128)(2,1)S(1)} %collective-permute-done.34.refs_6_), channel_id=1, source_target_pairs={{0,8},{4,12},{8,0},{12,4},{16,24},{20,28},{24,16},{28,20},{1,9},{5... | collective-permute-start | bytes 245768 | tf_op jit(solution)/shard_map/ppermute | solution.py:502
  111.2 5.6 %collective-permute-start.37 = (bf16[4,80,128]{2,1,0:T(8,128)(2,1)S(1)}, bf16[4,80,128]{2,1,0:T(8,128)(2,1)S(1)}, u32[]{:S(2)}, u32[]{:S(2)}) collective-permute-start(bf16[4,80,128]{2,1,0:T(8,128)(2,1)S(1)} %get-tuple-element.125), channel_id=1, source_target_pairs={{0,3},{1,2},{2,1},{3,0},{4,7},{5,6},{6,5},{7,4},{8,11},{9,10},{10,... | collective-permute-start | bytes 245768 | tf_op jit(solution)/shard_map/ppermute | solution.py:505
  113.1 5.4 %collective-permute-start.38 = (bf16[4,80,128]{2,1,0:T(8,128)(2,1)S(1)}, bf16[4,80,128]{2,1,0:T(8,128)(2,1)S(1)}, u32[]{:S(2)}, u32[]{:S(2)}) collective-permute-start(bf16[4,80,128]{2,1,0:T(8,128)(2,1)S(1)} %get-tuple-element.126), channel_id=1, source_target_pairs={{0,2},{1,3},{2,0},{3,1},{4,6},{5,7},{6,4},{7,5},{8,10},{9,11},{10,... | collective-permute-start | bytes 245768 | tf_op jit(solution)/shard_map/ppermute | solution.py:505
  (14 other events, 83.0 us)

commit v15 on v12

--- a/solution.py
+++ b/solution.py
@@ -518,7 +518,10 @@
     if via:
         one, two = (0, some), (some, rest)
         plan = [(0, 0, rows), (1, 0, rows), (2, *one), (2, *two), (3, *one), (3, *two)]
-        sends = [(3, *one), (2, *two), (3, *two), (1, *one), (1, *two), (0, 0, rows), (2, *one)]
+        third = rows // 48 * 16
+        near_cuts = [(0, rows - 2 * third), (rows - 2 * third, third), (rows - third, third)]
+        sends = [(3, *one), (2, *two), (3, *two), (0, 0, rows), (2, *one)]
+        sends += [(1, *cut) for cut in near_cuts]
     else:
         sends = plan = [(i, 0, rows) for i in range(chips)]
     pad = ((0, levp - lev), (0, levp - lev))
@@ -589,7 +592,7 @@
         ys = call(
             functools.partial(forward_kernel, sends, members),
             [
-                struct(shape, F32 if i == 0 or (via and at == 6) else BF16)
+                struct(shape, F32 if i == 0 or (via and at == 4) else BF16)
                 for at, ((i, *unused), shape) in enumerate(zip(sends, shapes))
             ],
             [],
@@ -601,10 +604,10 @@
         )
         if not via:
             return [y if i == 0 else along(y, i) for i, y in enumerate(ys)], [(0, rows)] * chips
-        passed, far_rest, last_rest, next_some, next_rest, near, far = ys
+        passed, far_rest, last_rest, near, far, *nexts = ys
         passed = along(passed, 1)
         far_rest, last_rest = along(far_rest, 2), along(last_rest, 3)
-        next_some, next_rest = along(next_some, 1), along(next_rest, 1)
+        nexts = [along(x, 1) for x in nexts]
         (far,) = call(
             functools.partial(add_kernel, members, 0),
             [struct((some, width), BF16)],
@@ -613,8 +616,8 @@
             far,
             passed,
         )
-        ys = [near, far_rest, last_rest, next_some, next_rest, along(far, 2)]
-        return ys, [(0, rows), two, two, one, two, one]
+        ys = [near, far_rest, last_rest, along(far, 2), *nexts]
+        return ys, [(0, rows), two, two, one, *near_cuts]
 
     def line_gather(w, *parts):
         if not via:

time: 114 us -> 118 us (1.035)
  starting transfers between devices: 44.9 us -> 52.8 us
  waiting for transfers between devices: 51.1 us -> 46.5 us
    ppermute x22 -> x24, starting transfers between devices: 30.2 us -> 38.2 us  [along(): return lax.ppermute(x, 'slab', [(s, s ^ 2 * i) for s in range(n_slab)])]
    ppermute x22 -> x24, waiting for transfers between devices: 27.3 us -> 23 us  [along(): return lax.ppermute(x, 'slab', [(s, s ^ 2 * i) for s in range(n_slab)])]
  transfers between devices with their start and end apart: 38 -> 40, of which waited for: 27 -> 25; matrix products, arithmetic and copies ran while one was open for 0% -> 0% of each run, Pallas kernels for 3% -> 3%
where the time goes in v15:
time: 118 us; the launch traced here: 117 us
  starting transfers between devices  52.8 us (45%)
  waiting for transfers between devices  46.5 us (39%)
  Pallas kernels  14.4 us (12%)
  local copies, waits for them, and re-layouts  2.09 us (2%)
  between operations  1.55 us (1%)
    ppermute x24, starting transfers between devices, along(): return lax.ppermute(x, 'slab', [(s, s ^ 2 * i) for s in range(n_slab)])  38.2 us
    ppermute x24, waiting for transfers between devices, along(): return lax.ppermute(x, 'slab', [(s, s ^ 2 * i) for s in range(n_slab)])  23 us
    ppermute x11, waiting for transfers between devices, plane(): return lax.ppermute(x, 'obs', [(o, o ^ i) for o in range(n_obs)])  19.2 us
    pallas_call x22, Pallas kernels, call(): pl.pallas_call(kernel, out_shape=outs, in_specs=[space] * len(args), out_...  14.4 us
    ppermute x11, starting transfers between devices, plane(): return lax.ppermute(x, 'obs', [(o, o ^ i) for o in range(n_obs)])  13.3 us
    ppermute x5, waiting for transfers between devices, swap(): return lax.ppermute(x, 'slab', [(s, s ^ 1) for s in range(n_slab)])  4.21 us
  transfers between devices with their start and end apart: 40, of which 25 were waited for; matrix products, arithmetic and copies ran while one was open for 0% of the time, Pallas kernels for 3%

profile of v15, /device:TPU:0, one launch (start us, length us, event | category | flops | bytes accessed | tf_op | source)
XLA Modules:
  0.0 117.5 jit_solution(9316253401249892735)
XLA Ops:
  1.3 5.2 %shard_map.104 = (bf16[4,4,128,256]{3,2,1,0:T(8,128)(2,1)}, bf16[4,4,128,256]{3,2,1,0:T(8,128)(2,1)}, bf16[304,256]{1,0:T(8,128)(2,1)}, bf16[304,256]{1,0:T(8,128)(2,1)}) custom-call(s32[4]{0:T(128)} %seeds_in.1, s32[1,1,32]{2,1,0:T(1,128)} %ids_in.1, s32[1,1,32]{2,1,0:T(1,128)} %cols_in.1, s32[1,1]{1,0:T(1,128)S(6)} %copy.16.count_in, f32[1,128]{1,0:T(1,128)} %refs_4_.1, ...), custom_call_target="tpu_custom_call" | custom-call | flops 637534208 | bytes 5735188 | tf_op jit(solution)/shard_map/pallas_call | solution.py:23
  7.6 2.3 %collective-permute-start = (bf16[304,256]{1,0:T(8,128)(2,1)}, bf16[304,256]{1,0:T(8,128)(2,1)S(1)}, u32[]{:S(2)}, u32[]{:S(2)}) collective-permute-start(bf16[304,256]{1,0:T(8,128)(2,1)} %get-tuple-element.67.refs_0_), channel_id=1, source_target_pairs={{0,1},{1,0},{2,3},{3,2},{4,5},{5,4},{6,7},{7,6},{8,9},{9,8},{10,11... | collective-permute-start | bytes 466952 | tf_op jit(solution)/shard_map/ppermute | solution.py:545
  14.5 1.5 %collective-permute-done.1.two_more = bf16[304,256]{1,0:T(8,128)(2,1)S(1)} collective-permute-done((bf16[304,256]{1,0:T(8,128)(2,1)}, bf16[304,256]{1,0:T(8,128)(2,1)S(1)}, u32[]{:S(2)}, u32[]{:S(2)}) %collective-permute-start.1) | collective-permute-done | bytes 155680 | tf_op jit(solution)/shard_map/ppermute | solution.py:545
  16.0 1.6 %collective-permute-start.2 = (bf16[304,256]{1,0:T(8,128)(2,1)S(1)}, bf16[304,256]{1,0:T(8,128)(2,1)S(1)}, u32[]{:S(2)}, u32[]{:S(2)}) collective-permute-start(bf16[304,256]{1,0:T(8,128)(2,1)S(1)} %get-tuple-element.71.refs_0_), channel_id=1, source_target_pairs={{0,2},{1,3},{2,0},{3,1},{4,6},{5,7},{6,4},{7,5},{8,10},{9,11},{10,... | collective-permute-start | bytes 466952 | tf_op jit(solution)/shard_map/ppermute | solution.py:545
  18.3 3.0 %collective-permute-done.2.refs_1_ = bf16[304,256]{1,0:T(8,128)(2,1)S(1)} collective-permute-done((bf16[304,256]{1,0:T(8,128)(2,1)S(1)}, bf16[304,256]{1,0:T(8,128)(2,1)S(1)}, u32[]{:S(2)}, u32[]{:S(2)}) %collective-permute-start.2) | collective-permute-done | bytes 155680 | tf_op jit(solution)/shard_map/ppermute | solution.py:545
  21.3 1.5 %collective-permute-done.3.refs_3_ = bf16[304,256]{1,0:T(8,128)(2,1)S(1)} collective-permute-done((bf16[304,256]{1,0:T(8,128)(2,1)S(1)}, bf16[304,256]{1,0:T(8,128)(2,1)S(1)}, u32[]{:S(2)}, u32[]{:S(2)}) %collective-permute-start.3) | collective-permute-done | bytes 155680 | tf_op jit(solution)/shard_map/ppermute | solution.py:545
  26.0 1.7 %collective-permute-start.8 = (bf16[144,256]{1,0:T(8,128)(2,1)S(1)}, bf16[144,256]{1,0:T(8,128)(2,1)S(1)}, u32[]{:S(2)}, u32[]{:S(2)}) collective-permute-start(bf16[144,256]{1,0:T(8,128)(2,1)S(1)} %get-tuple-element.88), channel_id=1, source_target_pairs={{0,8},{4,12},{8,0},{12,4},{16,24},{20,28},{24,16},{28,20},{1,9},{5... | collective-permute-start | bytes 221192 | tf_op jit(solution)/shard_map/ppermute | solution.py:542
  28.1 3.1 %collective-permute-start.6 = (bf16[160,256]{1,0:T(8,128)(2,1)S(1)}, bf16[160,256]{1,0:T(8,128)(2,1)S(1)}, u32[]{:S(2)}, u32[]{:S(2)}) collective-permute-start(bf16[160,256]{1,0:T(8,128)(2,1)S(1)} %get-tuple-element.85), channel_id=1, source_target_pairs={{0,16},{4,20},{8,24},{12,28},{16,0},{20,4},{24,8},{28,12},{1,17},{... | collective-permute-start | bytes 245768 | tf_op jit(solution)/shard_map/ppermute | solution.py:542
  32.2 2.3 %collective-permute-start.9 = (bf16[144,256]{1,0:T(8,128)(2,1)S(1)}, bf16[144,256]{1,0:T(8,128)(2,1)S(1)}, u32[]{:S(2)}, u32[]{:S(2)}) collective-permute-start(bf16[144,256]{1,0:T(8,128)(2,1)S(1)} %shard_map.110), channel_id=1, source_target_pairs={{0,16},{4,20},{8,24},{12,28},{16,0},{20,4},{24,8},{28,12},{1,17},{... | collective-permute-start | bytes 221192 | tf_op jit(solution)/shard_map/ppermute | solution.py:542
  34.4 1.3 %collective-permute-start.10 = (bf16[112,256]{1,0:T(8,128)(2,1)S(1)}, bf16[112,256]{1,0:T(8,128)(2,1)S(1)}, u32[]{:S(2)}, u32[]{:S(2)}) collective-permute-start(bf16[112,256]{1,0:T(8,128)(2,1)S(1)} %get-tuple-element.89), channel_id=1, source_target_pairs={{0,8},{4,12},{8,0},{12,4},{16,24},{20,28},{24,16},{28,20},{1,9},{5... | collective-permute-start | bytes 172040 | tf_op jit(solution)/shard_map/ppermute | solution.py:542
  36.7 3.1 %collective-permute-done.12.refs_6_ = bf16[96,256]{1,0:T(8,128)(2,1)S(1)} collective-permute-done((bf16[96,256]{1,0:T(8,128)(2,1)S(1)}, bf16[96,256]{1,0:T(8,128)(2,1)S(1)}, u32[]{:S(2)}, u32[]{:S(2)}) %collective-permute-start.12) | collective-permute-done | bytes 49184 | tf_op jit(solution)/shard_map/ppermute | solution.py:542
  39.8 2.3 %collective-permute-done.9.refs_3_ = bf16[144,256]{1,0:T(8,128)(2,1)S(1)} collective-permute-done((bf16[144,256]{1,0:T(8,128)(2,1)S(1)}, bf16[144,256]{1,0:T(8,128)(2,1)S(1)}, u32[]{:S(2)}, u32[]{:S(2)}) %collective-permute-start.9) | collective-permute-done | bytes 73760 | tf_op jit(solution)/shard_map/ppermute | solution.py:542
  42.5 3.4 %collective-permute-start.14 = (bf16[144,256]{1,0:T(8,128)(2,1)S(1)}, bf16[144,256]{1,0:T(8,128)(2,1)S(1)}, u32[]{:S(2)}, u32[]{:S(2)}) collective-permute-start(bf16[144,256]{1,0:T(8,128)(2,1)S(1)} %get-tuple-element.93), channel_id=1, source_target_pairs={{0,16},{4,20},{8,24},{12,28},{16,0},{20,4},{24,8},{28,12},{1,17},{... | collective-permute-start | bytes 221192 | tf_op jit(solution)/shard_map/ppermute | solution.py:542
  47.4 2.7 %collective-permute-done.14.refs_2_ = bf16[144,256]{1,0:T(8,128)(2,1)S(1)} collective-permute-done((bf16[144,256]{1,0:T(8,128)(2,1)S(1)}, bf16[144,256]{1,0:T(8,128)(2,1)S(1)}, u32[]{:S(2)}, u32[]{:S(2)}) %collective-permute-start.14) | collective-permute-done | bytes 73760 | tf_op jit(solution)/shard_map/ppermute | solution.py:542
  50.1 3.4 %collective-permute-start.16 = (bf16[144,256]{1,0:T(8,128)(2,1)S(1)}, bf16[144,256]{1,0:T(8,128)(2,1)S(1)}, u32[]{:S(2)}, u32[]{:S(2)}) collective-permute-start(bf16[144,256]{1,0:T(8,128)(2,1)S(1)} %collective-permute-done.14.refs_2_), channel_id=1, source_target_pairs={{0,8},{4,12},{8,0},{12,4},{16,24},{20,28},{24,16},{28,20},{1,9},{5... | collective-permute-start | bytes 221192 | tf_op jit(solution)/shard_map/ppermute | solution.py:542
  53.6 3.1 %collective-permute-done.15.refs_3_ = bf16[160,256]{1,0:T(8,128)(2,1)S(1)} collective-permute-done((bf16[160,256]{1,0:T(8,128)(2,1)S(1)}, bf16[160,256]{1,0:T(8,128)(2,1)S(1)}, u32[]{:S(2)}, u32[]{:S(2)}) %collective-permute-start.15) | collective-permute-done | bytes 81952 | tf_op jit(solution)/shard_map/ppermute | solution.py:542
  61.2 4.2 %collective-permute-done.19.one_more = bf16[304,256]{1,0:T(8,128)(2,1)S(1)} collective-permute-done((bf16[304,256]{1,0:T(8,128)(2,1)S(1)}, bf16[304,256]{1,0:T(8,128)(2,1)S(1)}, u32[]{:S(2)}, u32[]{:S(2)}) %collective-permute-start.19) | collective-permute-done | bytes 155680 | tf_op jit(solution)/shard_map/ppermute | solution.py:545
  68.2 3.1 %collective-permute-done.21.refs_1_ = bf16[304,256]{1,0:T(8,128)(2,1)S(1)} collective-permute-done((bf16[304,256]{1,0:T(8,128)(2,1)S(1)}, bf16[304,256]{1,0:T(8,128)(2,1)S(1)}, u32[]{:S(2)}, u32[]{:S(2)}) %collective-permute-start.21) | collective-permute-done | bytes 155680 | tf_op jit(solution)/shard_map/ppermute | solution.py:545
  76.6 1.3 %collective-permute-start.29 = (bf16[96,256]{1,0:T(8,128)(2,1)S(1)}, bf16[96,256]{1,0:T(8,128)(2,1)S(1)}, u32[]{:S(2)}, u32[]{:S(2)}) collective-permute-start(bf16[96,256]{1,0:T(8,128)(2,1)S(1)} %get-tuple-element.117), channel_id=1, source_target_pairs={{0,8},{4,12},{8,0},{12,4},{16,24},{20,28},{24,16},{28,20},{1,9},{5... | collective-permute-start | bytes 147464 | tf_op jit(solution)/shard_map/ppermute | solution.py:542
  77.9 2.1 %collective-permute-start.24 = (bf16[160,256]{1,0:T(8,128)(2,1)S(1)}, bf16[160,256]{1,0:T(8,128)(2,1)S(1)}, u32[]{:S(2)}, u32[]{:S(2)}) collective-permute-start(bf16[160,256]{1,0:T(8,128)(2,1)S(1)} %get-tuple-element.112), channel_id=1, source_target_pairs={{0,16},{4,20},{8,24},{12,28},{16,0},{20,4},{24,8},{28,12},{1,17},{... | collective-permute-start | bytes 245768 | tf_op jit(solution)/shard_map/ppermute | solution.py:542
  80.0 1.4 %collective-permute-start.25 = (bf16[160,256]{1,0:T(8,128)(2,1)S(1)}, bf16[160,256]{1,0:T(8,128)(2,1)S(1)}, u32[]{:S(2)}, u32[]{:S(2)}) collective-permute-start(bf16[160,256]{1,0:T(8,128)(2,1)S(1)} %get-tuple-element.113), channel_id=1, source_target_pairs={{0,24},{4,28},{8,16},{12,20},{16,8},{20,12},{24,0},{28,4},{1,25},{... | collective-permute-start | bytes 245768 | tf_op jit(solution)/shard_map/ppermute | solution.py:542
  81.5 2.1 %collective-permute-start.27 = (bf16[144,256]{1,0:T(8,128)(2,1)S(1)}, bf16[144,256]{1,0:T(8,128)(2,1)S(1)}, u32[]{:S(2)}, u32[]{:S(2)}) collective-permute-start(bf16[144,256]{1,0:T(8,128)(2,1)S(1)} %shard_map.120), channel_id=1, source_target_pairs={{0,16},{4,20},{8,24},{12,28},{16,0},{20,4},{24,8},{28,12},{1,17},{... | collective-permute-start | bytes 221192 | tf_op jit(solution)/shard_map/ppermute | solution.py:542
  83.6 1.3 %collective-permute-start.28 = (bf16[112,256]{1,0:T(8,128)(2,1)S(1)}, bf16[112,256]{1,0:T(8,128)(2,1)S(1)}, u32[]{:S(2)}, u32[]{:S(2)}) collective-permute-start(bf16[112,256]{1,0:T(8,128)(2,1)S(1)} %get-tuple-element.116), channel_id=1, source_target_pairs={{0,8},{4,12},{8,0},{12,4},{16,24},{20,28},{24,16},{28,20},{1,9},{5... | collective-permute-start | bytes 172040 | tf_op jit(solution)/shard_map/ppermute | solution.py:542
  85.6 3.6 %collective-permute-done.30.refs_6_ = bf16[96,256]{1,0:T(8,128)(2,1)S(1)} collective-permute-done((bf16[96,256]{1,0:T(8,128)(2,1)S(1)}, bf16[96,256]{1,0:T(8,128)(2,1)S(1)}, u32[]{:S(2)}, u32[]{:S(2)}) %collective-permute-start.30) | collective-permute-done | bytes 49184 | tf_op jit(solution)/shard_map/ppermute | solution.py:542
  89.2 2.5 %collective-permute-done.27.refs_3_ = bf16[144,256]{1,0:T(8,128)(2,1)S(1)} collective-permute-done((bf16[144,256]{1,0:T(8,128)(2,1)S(1)}, bf16[144,256]{1,0:T(8,128)(2,1)S(1)}, u32[]{:S(2)}, u32[]{:S(2)}) %collective-permute-start.27) | collective-permute-done | bytes 73760 | tf_op jit(solution)/shard_map/ppermute | solution.py:542
  92.1 3.3 %collective-permute-start.32 = (bf16[144,256]{1,0:T(8,128)(2,1)S(1)}, bf16[144,256]{1,0:T(8,128)(2,1)S(1)}, u32[]{:S(2)}, u32[]{:S(2)}) collective-permute-start(bf16[144,256]{1,0:T(8,128)(2,1)S(1)} %get-tuple-element.121), channel_id=1, source_target_pairs={{0,16},{4,20},{8,24},{12,28},{16,0},{20,4},{24,8},{28,12},{1,17},{... | collective-permute-start | bytes 221192 | tf_op jit(solution)/shard_map/ppermute | solution.py:542
  97.0 1.6 %collective-permute-done.32.refs_2_ = bf16[144,256]{1,0:T(8,128)(2,1)S(1)} collective-permute-done((bf16[144,256]{1,0:T(8,128)(2,1)S(1)}, bf16[144,256]{1,0:T(8,128)(2,1)S(1)}, u32[]{:S(2)}, u32[]{:S(2)}) %collective-permute-start.32) | collective-permute-done | bytes 73760 | tf_op jit(solution)/shard_map/ppermute | solution.py:542
  98.6 4.7 %collective-permute-start.34 = (bf16[144,256]{1,0:T(8,128)(2,1)S(1)}, bf16[144,256]{1,0:T(8,128)(2,1)S(1)}, u32[]{:S(2)}, u32[]{:S(2)}) collective-permute-start(bf16[144,256]{1,0:T(8,128)(2,1)S(1)} %collective-permute-done.32.refs_2_), channel_id=1, source_target_pairs={{0,8},{4,12},{8,0},{12,4},{16,24},{20,28},{24,16},{28,20},{1,9},{5... | collective-permute-start | bytes 221192 | tf_op jit(solution)/shard_map/ppermute | solution.py:542
  103.3 3.1 %collective-permute-done.33.refs_3_ = bf16[160,256]{1,0:T(8,128)(2,1)S(1)} collective-permute-done((bf16[160,256]{1,0:T(8,128)(2,1)S(1)}, bf16[160,256]{1,0:T(8,128)(2,1)S(1)}, u32[]{:S(2)}, u32[]{:S(2)}) %collective-permute-start.33) | collective-permute-done | bytes 81952 | tf_op jit(solution)/shard_map/ppermute | solution.py:542
  109.3 2.0 %collective-permute-start.37 = (bf16[304,128]{1,0:T(8,128)(2,1)S(1)}, bf16[304,128]{1,0:T(8,128)(2,1)S(1)}, u32[]{:S(2)}, u32[]{:S(2)}) collective-permute-start(bf16[304,128]{1,0:T(8,128)(2,1)S(1)} %get-tuple-element.124), channel_id=1, source_target_pairs={{0,3},{1,2},{2,1},{3,0},{4,7},{5,6},{6,5},{7,4},{8,11},{9,10},{10,... | collective-permute-start | bytes 233480 | tf_op jit(solution)/shard_map/ppermute | solution.py:545
  112.9 1.9 %collective-permute-done.37.refs_1_ = bf16[304,128]{1,0:T(8,128)(2,1)S(1)} collective-permute-done((bf16[304,128]{1,0:T(8,128)(2,1)S(1)}, bf16[304,128]{1,0:T(8,128)(2,1)S(1)}, u32[]{:S(2)}, u32[]{:S(2)}) %collective-permute-start.37) | collective-permute-done | bytes 77856 | tf_op jit(solution)/shard_map/ppermute | solution.py:545
  114.8 1.6 %collective-permute-done.38.refs_2_ = bf16[304,128]{1,0:T(8,128)(2,1)S(1)} collective-permute-done((bf16[304,128]{1,0:T(8,128)(2,1)S(1)}, bf16[304,128]{1,0:T(8,128)(2,1)S(1)}, u32[]{:S(2)}, u32[]{:S(2)}) %collective-permute-start.38) | collective-permute-done | bytes 77856 | tf_op jit(solution)/shard_map/ppermute | solution.py:545
  (89 shorter events, 34.5 us)
Async XLA Ops:
  6.5 19.0 %collective-permute-start.5 = (bf16[4,4,128,256]{3,2,1,0:T(8,128)(2,1)}, bf16[4,4,128,256]{3,2,1,0:T(8,128)(2,1)S(1)}, u32[]{:S(2)}, u32[]{:S(2)}) collective-permute-start(bf16[4,4,128,256]{3,2,1,0:T(8,128)(2,1)} %get-tuple-element.74), channel_id=1, source_target_pairs={{0,4},{4,0},{8,12},{12,8},{16,20},{20,16},{24,28},{28,24},{1,5},{5... | collective-permute-start | bytes 3145736 | tf_op jit(solution)/shard_map/ppermute | solution.py:548
  7.6 6.9 %collective-permute-start = (bf16[304,256]{1,0:T(8,128)(2,1)}, bf16[304,256]{1,0:T(8,128)(2,1)S(1)}, u32[]{:S(2)}, u32[]{:S(2)}) collective-permute-start(bf16[304,256]{1,0:T(8,128)(2,1)} %get-tuple-element.67.refs_0_), channel_id=1, source_target_pairs={{0,1},{1,0},{2,3},{3,2},{4,5},{5,4},{6,7},{7,6},{8,9},{9,8},{10,11... | collective-permute-start | bytes 466952 | tf_op jit(solution)/shard_map/ppermute | solution.py:545
  9.9 6.0 %collective-permute-start.1 = (bf16[304,256]{1,0:T(8,128)(2,1)}, bf16[304,256]{1,0:T(8,128)(2,1)S(1)}, u32[]{:S(2)}, u32[]{:S(2)}) collective-permute-start(bf16[304,256]{1,0:T(8,128)(2,1)} %get-tuple-element.68.refs_1_), channel_id=1, source_target_pairs={{0,2},{1,3},{2,0},{3,1},{4,6},{5,7},{6,4},{7,5},{8,10},{9,11},{10,... | collective-permute-start | bytes 466952 | tf_op jit(solution)/shard_map/ppermute | solution.py:545
  16.0 5.3 %collective-permute-start.2 = (bf16[304,256]{1,0:T(8,128)(2,1)S(1)}, bf16[304,256]{1,0:T(8,128)(2,1)S(1)}, u32[]{:S(2)}, u32[]{:S(2)}) collective-permute-start(bf16[304,256]{1,0:T(8,128)(2,1)S(1)} %get-tuple-element.71.refs_0_), channel_id=1, source_target_pairs={{0,2},{1,3},{2,0},{3,1},{4,6},{5,7},{6,4},{7,5},{8,10},{9,11},{10,... | collective-permute-start | bytes 466952 | tf_op jit(solution)/shard_map/ppermute | solution.py:545
  17.6 5.2 %collective-permute-start.3 = (bf16[304,256]{1,0:T(8,128)(2,1)S(1)}, bf16[304,256]{1,0:T(8,128)(2,1)S(1)}, u32[]{:S(2)}, u32[]{:S(2)}) collective-permute-start(bf16[304,256]{1,0:T(8,128)(2,1)S(1)} %get-tuple-element.72.refs_2_), channel_id=1, source_target_pairs={{0,1},{1,0},{2,3},{3,2},{4,5},{5,4},{6,7},{7,6},{8,9},{9,8},{10,11... | collective-permute-start | bytes 466952 | tf_op jit(solution)/shard_map/ppermute | solution.py:545
  26.0 6.1 %collective-permute-start.8 = (bf16[144,256]{1,0:T(8,128)(2,1)S(1)}, bf16[144,256]{1,0:T(8,128)(2,1)S(1)}, u32[]{:S(2)}, u32[]{:S(2)}) collective-permute-start(bf16[144,256]{1,0:T(8,128)(2,1)S(1)} %get-tuple-element.88), channel_id=1, source_target_pairs={{0,8},{4,12},{8,0},{12,4},{16,24},{20,28},{24,16},{28,20},{1,9},{5... | collective-permute-start | bytes 221192 | tf_op jit(solution)/shard_map/ppermute | solution.py:542
  27.7 8.0 %collective-permute-start.11 = (bf16[96,256]{1,0:T(8,128)(2,1)S(1)}, bf16[96,256]{1,0:T(8,128)(2,1)S(1)}, u32[]{:S(2)}, u32[]{:S(2)}) collective-permute-start(bf16[96,256]{1,0:T(8,128)(2,1)S(1)} %get-tuple-element.90), channel_id=1, source_target_pairs={{0,8},{4,12},{8,0},{12,4},{16,24},{20,28},{24,16},{28,20},{1,9},{5... | collective-permute-start | bytes 147464 | tf_op jit(solution)/shard_map/ppermute | solution.py:542
  28.1 11.7 %collective-permute-start.6 = (bf16[160,256]{1,0:T(8,128)(2,1)S(1)}, bf16[160,256]{1,0:T(8,128)(2,1)S(1)}, u32[]{:S(2)}, u32[]{:S(2)}) collective-permute-start(bf16[160,256]{1,0:T(8,128)(2,1)S(1)} %get-tuple-element.85), channel_id=1, source_target_pairs={{0,16},{4,20},{8,24},{12,28},{16,0},{20,4},{24,8},{28,12},{1,17},{... | collective-permute-start | bytes 245768 | tf_op jit(solution)/shard_map/ppermute | solution.py:542
  31.2 8.6 %collective-permute-start.7 = (bf16[160,256]{1,0:T(8,128)(2,1)S(1)}, bf16[160,256]{1,0:T(8,128)(2,1)S(1)}, u32[]{:S(2)}, u32[]{:S(2)}) collective-permute-start(bf16[160,256]{1,0:T(8,128)(2,1)S(1)} %get-tuple-element.86), channel_id=1, source_target_pairs={{0,24},{4,28},{8,16},{12,20},{16,8},{20,12},{24,0},{28,4},{1,25},{... | collective-permute-start | bytes 245768 | tf_op jit(solution)/shard_map/ppermute | solution.py:542
  32.2 9.9 %collective-permute-start.9 = (bf16[144,256]{1,0:T(8,128)(2,1)S(1)}, bf16[144,256]{1,0:T(8,128)(2,1)S(1)}, u32[]{:S(2)}, u32[]{:S(2)}) collective-permute-start(bf16[144,256]{1,0:T(8,128)(2,1)S(1)} %shard_map.110), channel_id=1, source_target_pairs={{0,16},{4,20},{8,24},{12,28},{16,0},{20,4},{24,8},{28,12},{1,17},{... | collective-permute-start | bytes 221192 | tf_op jit(solution)/shard_map/ppermute | solution.py:542
  34.4 5.4 %collective-permute-start.10 = (bf16[112,256]{1,0:T(8,128)(2,1)S(1)}, bf16[112,256]{1,0:T(8,128)(2,1)S(1)}, u32[]{:S(2)}, u32[]{:S(2)}) collective-permute-start(bf16[112,256]{1,0:T(8,128)(2,1)S(1)} %get-tuple-element.89), channel_id=1, source_target_pairs={{0,8},{4,12},{8,0},{12,4},{16,24},{20,28},{24,16},{28,20},{1,9},{5... | collective-permute-start | bytes 172040 | tf_op jit(solution)/shard_map/ppermute | solution.py:542
  42.3 14.7 %collective-permute-start.13 = (bf16[304,256]{1,0:T(8,128)(2,1)S(1)}, bf16[304,256]{1,0:T(8,128)(2,1)S(1)}, u32[]{:S(2)}, u32[]{:S(2)}) collective-permute-start(bf16[304,256]{1,0:T(8,128)(2,1)S(1)} %get-tuple-element.92.refs_0_), channel_id=1, source_target_pairs={{0,8},{4,12},{8,0},{12,4},{16,24},{20,28},{24,16},{28,20},{1,9},{5... | collective-permute-start | bytes 466952 | tf_op jit(solution)/shard_map/ppermute | solution.py:542
  42.5 7.6 %collective-permute-start.14 = (bf16[144,256]{1,0:T(8,128)(2,1)S(1)}, bf16[144,256]{1,0:T(8,128)(2,1)S(1)}, u32[]{:S(2)}, u32[]{:S(2)}) collective-permute-start(bf16[144,256]{1,0:T(8,128)(2,1)S(1)} %get-tuple-element.93), channel_id=1, source_target_pairs={{0,16},{4,20},{8,24},{12,28},{16,0},{20,4},{24,8},{28,12},{1,17},{... | collective-permute-start | bytes 221192 | tf_op jit(solution)/shard_map/ppermute | solution.py:542
  45.8 7.7 %collective-permute-start.17 = (bf16[160,256]{1,0:T(8,128)(2,1)S(1)}, bf16[160,256]{1,0:T(8,128)(2,1)S(1)}, u32[]{:S(2)}, u32[]{:S(2)}) collective-permute-start(bf16[160,256]{1,0:T(8,128)(2,1)S(1)} %get-tuple-element.94), channel_id=1, source_target_pairs={{0,24},{4,28},{8,16},{12,20},{16,8},{20,12},{24,0},{28,4},{1,25},{... | collective-permute-start | bytes 245768 | tf_op jit(solution)/shard_map/ppermute | solution.py:542
  46.7 10.0 %collective-permute-start.15 = (bf16[160,256]{1,0:T(8,128)(2,1)S(1)}, bf16[160,256]{1,0:T(8,128)(2,1)S(1)}, u32[]{:S(2)}, u32[]{:S(2)}) collective-permute-start(bf16[160,256]{1,0:T(8,128)(2,1)S(1)} %get-tuple-element.94), channel_id=1, source_target_pairs={{0,16},{4,20},{8,24},{12,28},{16,0},{20,4},{24,8},{28,12},{1,17},{... | collective-permute-start | bytes 245768 | tf_op jit(solution)/shard_map/ppermute | solution.py:542
  50.1 6.9 %collective-permute-start.16 = (bf16[144,256]{1,0:T(8,128)(2,1)S(1)}, bf16[144,256]{1,0:T(8,128)(2,1)S(1)}, u32[]{:S(2)}, u32[]{:S(2)}) collective-permute-start(bf16[144,256]{1,0:T(8,128)(2,1)S(1)} %collective-permute-done.14.refs_2_), channel_id=1, source_target_pairs={{0,8},{4,12},{8,0},{12,4},{16,24},{20,28},{24,16},{28,20},{1,9},{5... | collective-permute-start | bytes 221192 | tf_op jit(solution)/shard_map/ppermute | solution.py:542
  59.3 6.1 %collective-permute-start.19 = (bf16[304,256]{1,0:T(8,128)(2,1)S(1)}, bf16[304,256]{1,0:T(8,128)(2,1)S(1)}, u32[]{:S(2)}, u32[]{:S(2)}) collective-permute-start(bf16[304,256]{1,0:T(8,128)(2,1)S(1)} %get-tuple-element.95.one), channel_id=1, source_target_pairs={{0,1},{1,0},{2,3},{3,2},{4,5},{5,4},{6,7},{7,6},{8,9},{9,8},{10,11... | collective-permute-start | bytes 466952 | tf_op jit(solution)/shard_map/ppermute | solution.py:545
  60.1 5.8 %collective-permute-start.20 = (bf16[304,256]{1,0:T(8,128)(2,1)S(1)}, bf16[304,256]{1,0:T(8,128)(2,1)S(1)}, u32[]{:S(2)}, u32[]{:S(2)}) collective-permute-start(bf16[304,256]{1,0:T(8,128)(2,1)S(1)} %get-tuple-element.96.two), channel_id=1, source_target_pairs={{0,2},{1,3},{2,0},{3,1},{4,6},{5,7},{6,4},{7,5},{8,10},{9,11},{10,... | collective-permute-start | bytes 466952 | tf_op jit(solution)/shard_map/ppermute | solution.py:545
  66.0 5.3 %collective-permute-start.21 = (bf16[304,256]{1,0:T(8,128)(2,1)S(1)}, bf16[304,256]{1,0:T(8,128)(2,1)S(1)}, u32[]{:S(2)}, u32[]{:S(2)}) collective-permute-start(bf16[304,256]{1,0:T(8,128)(2,1)S(1)} %get-tuple-element.97.refs_0_), channel_id=1, source_target_pairs={{0,2},{1,3},{2,0},{3,1},{4,6},{5,7},{6,4},{7,5},{8,10},{9,11},{10,... | collective-permute-start | bytes 466952 | tf_op jit(solution)/shard_map/ppermute | solution.py:545
  67.2 5.2 %collective-permute-start.22 = (bf16[304,256]{1,0:T(8,128)(2,1)S(1)}, bf16[304,256]{1,0:T(8,128)(2,1)S(1)}, u32[]{:S(2)}, u32[]{:S(2)}) collective-permute-start(bf16[304,256]{1,0:T(8,128)(2,1)S(1)} %get-tuple-element.98.refs_2_), channel_id=1, source_target_pairs={{0,1},{1,0},{2,3},{3,2},{4,5},{5,4},{6,7},{7,6},{8,9},{9,8},{10,11... | collective-permute-start | bytes 466952 | tf_op jit(solution)/shard_map/ppermute | solution.py:545
  75.8 5.6 %collective-permute-start.26 = (bf16[144,256]{1,0:T(8,128)(2,1)S(1)}, bf16[144,256]{1,0:T(8,128)(2,1)S(1)}, u32[]{:S(2)}, u32[]{:S(2)}) collective-permute-start(bf16[144,256]{1,0:T(8,128)(2,1)S(1)} %get-tuple-element.115), channel_id=1, source_target_pairs={{0,8},{4,12},{8,0},{12,4},{16,24},{20,28},{24,16},{28,20},{1,9},{5... | collective-permute-start | bytes 221192 | tf_op jit(solution)/shard_map/ppermute | solution.py:542
  76.6 8.3 %collective-permute-start.29 = (bf16[96,256]{1,0:T(8,128)(2,1)S(1)}, bf16[96,256]{1,0:T(8,128)(2,1)S(1)}, u32[]{:S(2)}, u32[]{:S(2)}) collective-permute-start(bf16[96,256]{1,0:T(8,128)(2,1)S(1)} %get-tuple-element.117), channel_id=1, source_target_pairs={{0,8},{4,12},{8,0},{12,4},{16,24},{20,28},{24,16},{28,20},{1,9},{5... | collective-permute-start | bytes 147464 | tf_op jit(solution)/shard_map/ppermute | solution.py:542
  77.9 11.2 %collective-permute-start.24 = (bf16[160,256]{1,0:T(8,128)(2,1)S(1)}, bf16[160,256]{1,0:T(8,128)(2,1)S(1)}, u32[]{:S(2)}, u32[]{:S(2)}) collective-permute-start(bf16[160,256]{1,0:T(8,128)(2,1)S(1)} %get-tuple-element.112), channel_id=1, source_target_pairs={{0,16},{4,20},{8,24},{12,28},{16,0},{20,4},{24,8},{28,12},{1,17},{... | collective-permute-start | bytes 245768 | tf_op jit(solution)/shard_map/ppermute | solution.py:542
  80.0 9.1 %collective-permute-start.25 = (bf16[160,256]{1,0:T(8,128)(2,1)S(1)}, bf16[160,256]{1,0:T(8,128)(2,1)S(1)}, u32[]{:S(2)}, u32[]{:S(2)}) collective-permute-start(bf16[160,256]{1,0:T(8,128)(2,1)S(1)} %get-tuple-element.113), channel_id=1, source_target_pairs={{0,24},{4,28},{8,16},{12,20},{16,8},{20,12},{24,0},{28,4},{1,25},{... | collective-permute-start | bytes 245768 | tf_op jit(solution)/shard_map/ppermute | solution.py:542
  81.5 10.2 %collective-permute-start.27 = (bf16[144,256]{1,0:T(8,128)(2,1)S(1)}, bf16[144,256]{1,0:T(8,128)(2,1)S(1)}, u32[]{:S(2)}, u32[]{:S(2)}) collective-permute-start(bf16[144,256]{1,0:T(8,128)(2,1)S(1)} %shard_map.120), channel_id=1, source_target_pairs={{0,16},{4,20},{8,24},{12,28},{16,0},{20,4},{24,8},{28,12},{1,17},{... | collective-permute-start | bytes 221192 | tf_op jit(solution)/shard_map/ppermute | solution.py:542
  83.6 5.6 %collective-permute-start.28 = (bf16[112,256]{1,0:T(8,128)(2,1)S(1)}, bf16[112,256]{1,0:T(8,128)(2,1)S(1)}, u32[]{:S(2)}, u32[]{:S(2)}) collective-permute-start(bf16[112,256]{1,0:T(8,128)(2,1)S(1)} %get-tuple-element.116), channel_id=1, source_target_pairs={{0,8},{4,12},{8,0},{12,4},{16,24},{20,28},{24,16},{28,20},{1,9},{5... | collective-permute-start | bytes 172040 | tf_op jit(solution)/shard_map/ppermute | solution.py:542
  92.1 14.9 %collective-permute-start.31 = (bf16[304,256]{1,0:T(8,128)(2,1)S(1)}, bf16[304,256]{1,0:T(8,128)(2,1)S(1)}, u32[]{:S(2)}, u32[]{:S(2)}) collective-permute-start(bf16[304,256]{1,0:T(8,128)(2,1)S(1)} %get-tuple-element.120.refs_0_), channel_id=1, source_target_pairs={{0,8},{4,12},{8,0},{12,4},{16,24},{20,28},{24,16},{28,20},{1,9},{5... | collective-permute-start | bytes 466952 | tf_op jit(solution)/shard_map/ppermute | solution.py:542
  92.1 6.5 %collective-permute-start.32 = (bf16[144,256]{1,0:T(8,128)(2,1)S(1)}, bf16[144,256]{1,0:T(8,128)(2,1)S(1)}, u32[]{:S(2)}, u32[]{:S(2)}) collective-permute-start(bf16[144,256]{1,0:T(8,128)(2,1)S(1)} %get-tuple-element.121), channel_id=1, source_target_pairs={{0,16},{4,20},{8,24},{12,28},{16,0},{20,4},{24,8},{28,12},{1,17},{... | collective-permute-start | bytes 221192 | tf_op jit(solution)/shard_map/ppermute | solution.py:542
  95.5 7.8 %collective-permute-start.35 = (bf16[160,256]{1,0:T(8,128)(2,1)S(1)}, bf16[160,256]{1,0:T(8,128)(2,1)S(1)}, u32[]{:S(2)}, u32[]{:S(2)}) collective-permute-start(bf16[160,256]{1,0:T(8,128)(2,1)S(1)} %get-tuple-element.122), channel_id=1, source_target_pairs={{0,24},{4,28},{8,16},{12,20},{16,8},{20,12},{24,0},{28,4},{1,25},{... | collective-permute-start | bytes 245768 | tf_op jit(solution)/shard_map/ppermute | solution.py:542
  96.5 9.9 %collective-permute-start.33 = (bf16[160,256]{1,0:T(8,128)(2,1)S(1)}, bf16[160,256]{1,0:T(8,128)(2,1)S(1)}, u32[]{:S(2)}, u32[]{:S(2)}) collective-permute-start(bf16[160,256]{1,0:T(8,128)(2,1)S(1)} %get-tuple-element.122), channel_id=1, source_target_pairs={{0,16},{4,20},{8,24},{12,28},{16,0},{20,4},{24,8},{28,12},{1,17},{... | collective-permute-start | bytes 245768 | tf_op jit(solution)/shard_map/ppermute | solution.py:542
  98.6 8.4 %collective-permute-start.34 = (bf16[144,256]{1,0:T(8,128)(2,1)S(1)}, bf16[144,256]{1,0:T(8,128)(2,1)S(1)}, u32[]{:S(2)}, u32[]{:S(2)}) collective-permute-start(bf16[144,256]{1,0:T(8,128)(2,1)S(1)} %collective-permute-done.32.refs_2_), channel_id=1, source_target_pairs={{0,8},{4,12},{8,0},{12,4},{16,24},{20,28},{24,16},{28,20},{1,9},{5... | collective-permute-start | bytes 221192 | tf_op jit(solution)/shard_map/ppermute | solution.py:542
  109.3 5.5 %collective-permute-start.37 = (bf16[304,128]{1,0:T(8,128)(2,1)S(1)}, bf16[304,128]{1,0:T(8,128)(2,1)S(1)}, u32[]{:S(2)}, u32[]{:S(2)}) collective-permute-start(bf16[304,128]{1,0:T(8,128)(2,1)S(1)} %get-tuple-element.124), channel_id=1, source_target_pairs={{0,3},{1,2},{2,1},{3,0},{4,7},{5,6},{6,5},{7,4},{8,11},{9,10},{10,... | collective-permute-start | bytes 233480 | tf_op jit(solution)/shard_map/ppermute | solution.py:545
  (14 other events, 77.9 us)

commit v16 on v12

--- a/solution.py
+++ b/solution.py
@@ -120,8 +120,8 @@
     dims, seeds_in, ids_in, cols_in, count_in, sd_in, innov_in, prec_in, h, own, partner, *rest
 ):
     chips, halves = dims
-    outs = rest[:-12]
-    seeds, ids, cols, count, sd, innov, prec, hashed, scratch, acc, sems, h_sems = rest[-12:]
+    outs = rest[:-13]
+    seeds, ids, cols, count, sd, innov, prec, bases, hashed, scratch, acc, sems, h_sems = rest[-13:]
     z, core, obs = place()
     blocks, lev, profiles = innov.shape
     colblocks, width = own.shape[1], own.shape[3]
@@ -142,52 +142,66 @@
     own[...] = jnp.zeros_like(own)
     partner[...] = jnp.zeros_like(partner)
     scratch[...] = jnp.zeros_like(scratch)
-    for copy in small:
-        copy.wait()
-
-    def tile_copy(n, half, target):
-        lanes = pl.ds(half * width, width)
-        return pltpu.make_async_copy(h.at[n, :, lanes], target, h_sems.at[n * halves + half])
-
-    def put(n, carry):
-        for half in range(halves):
-            piece, k = ids[0, 0, n] * halves + half, cols[0, 0, n]
-
-            @pl.when(piece % 2 == core)
-            def _():
-                tile_copy(n, half, own.at[piece // 2, k]).start()
-
-            @pl.when(piece % 2 != core)
-            def _():
-                tile_copy(n, half, partner.at[piece // 2, k]).start()
-
-        return carry
-
-    lax.fori_loop(0, count[0, 0], put, 0)
-
-    starts = [lax.rem(seeds[m], PRIME) - PRIME for m in range(members)]
     order = [(source, zz) for source in range(2) for zz in range(chips)]
     shape = (levp, width)
     spot = lax.broadcasted_iota(jnp.int32, shape, 0) * profiles
     spot = spot + lax.broadcasted_iota(jnp.int32, shape, 1)
-    low = (1.0 - 2.0**-21) / PRIME
 
     def piece_at(at):
         source, zz = order[at]
         return 2 * zz + (core if source == 0 else 1 - core)
 
-    def draw(at):
+    for at in range(len(order)):
         piece = piece_at(at)
         first = (obs * blocks + piece // halves) * (lev * profiles) + (piece % halves) * width
-        base = remainder(7919 * remainder(spot + first, 1.0 / PRIME), 1.0 / PRIME)
+        bases[at] = remainder(7919 * remainder(spot + first, 1.0 / PRIME), 1.0 / PRIME)
+    for copy in small:
+        copy.wait()
+
+    def tile_copy(n, half, target):
+        lanes = pl.ds(half * width, width)
+        return pltpu.make_async_copy(h.at[n, :, lanes], target, h_sems.at[n * halves + half])
+
+    def put(n, carry):
+        for half in range(halves):
+            piece, k = ids[0, 0, n] * halves + half, cols[0, 0, n]
+
+            @pl.when(piece % 2 == core)
+            def _():
+                tile_copy(n, half, own.at[piece // 2, k]).start()
+
+            @pl.when(piece % 2 != core)
+            def _():
+                tile_copy(n, half, partner.at[piece // 2, k]).start()
+
+        return carry
+
+    lax.fori_loop(0, count[0, 0], put, 0)
+
+    starts = [lax.rem(seeds[m], PRIME) - PRIME for m in range(members)]
+    low = (1.0 - 2.0**-21) / PRIME
+
+    def draw(at, m):
+        k0 = bases[at] + starts[m]
+        k1 = remainder(k0 * k0 + 12345, 1.0 / PRIME)
+        k2 = remainder(k1 * k1 + 2719, low)
+        return jnp.where(k2 >= PRIME, k2 - PRIME, k2).astype(F32)
+
+    early = len(order) // 2
+    for at in range(early):
         for m in range(members):
-            k0 = base + starts[m]
-            k1 = remainder(k0 * k0 + 12345, 1.0 / PRIME)
-            k2 = remainder(k1 * k1 + 2719, low)
-            k2 = jnp.where(k2 >= PRIME, k2 - PRIME, k2)
-            hashed[at, m] = k2.astype(F32)
-
-    def adjoint(at):
+            hashed[at, m] = draw(at, m)
+    for copy in large:
+        copy.wait()
+
+    def arrive(n, carry):
+        for half in range(halves):
+            tile_copy(n, half, own.at[0, 0]).wait()
+        return carry
+
+    lax.fori_loop(0, count[0, 0], arrive, 0)
+
+    for at in range(len(order)):
         source, zz = order[at]
         piece = piece_at(at)
         b = piece // halves
@@ -199,34 +213,26 @@
         gain = 3.4 * p * lax.rsqrt(p)
         offset = p * d - 0.5 * gain
         gain = gain * (1.0 / PRIME)
+        slot, side = at // 2 % 2, at % 2
         for m in range(members):
-            w = offset + gain * hashed[at, m, 0:lev, :]
-            scratch[at % 2, m * lev : (m + 1) * lev, :] = w
-        w = scratch[at % 2].astype(BF16)
-        tiles = (own if source == 0 else partner)[zz].reshape(colblocks * LANES, width)
-        part = lax.dot_general(w, tiles, NT, preferred_element_type=F32)
-        if at == 0:
+            k2 = hashed[at, m, 0:lev, :] if at < early else draw(at, m)[0:lev]
+            scratch[slot, m * lev : (m + 1) * lev, side * width : (side + 1) * width] = (
+                offset + gain * k2
+            )
+        if side == 0:
+            continue
+        tiles = own if source == 0 else partner
+        tiles = [tiles[i].reshape(colblocks * LANES, width) for i in (zz - 1, zz)]
+        part = lax.dot_general(
+            scratch[slot].astype(BF16),
+            jnp.concatenate(tiles, axis=1),
+            NT,
+            preferred_element_type=F32,
+        )
+        if at == 1:
             acc[...] = part
         else:
             acc[...] += part
-
-    early = len(order) // 2
-    for at in range(early):
-        draw(at)
-    for copy in large:
-        copy.wait()
-
-    def arrive(n, carry):
-        for half in range(halves):
-            tile_copy(n, half, own.at[0, 0]).wait()
-        return carry
-
-    lax.fori_loop(0, count[0, 0], arrive, 0)
-
-    for at in range(len(order)):
-        if at + early < len(order):
-            draw(at + early)
-        adjoint(at)
 
     line = jnp.concatenate([sd[...]] * colblocks, axis=1)
     put_halves(outs, with_columns(acc[...], line, obs, members))
@@ -456,10 +462,25 @@
     moved[...] = with_scalars(packed[0 : moved.shape[0], :], scalars).astype(BF16)
 
 
-def last_kernel(parts, later, lev, *refs):
+def increment_kernel(later, sd, vert, state, residual, *refs):
+    before, direction, moved = refs[-3:]
+    obs = lax.axis_index("obs")
+    mine = pl.ds(pl.multiple_of(obs * LANES, LANES), LANES)
+    for m in range(residual.shape[0]):
+        d = residual[m, :, mine]
+        if later:
+            d = d + state[m, 2:3, 0:1] * refs[0][m, :, mine]
+            before[m] = sd[...] * dot(vert[...], refs[1][m])
+        else:
+            before[m] = jnp.zeros_like(d)
+        direction[m] = d
+        moved[m] = sd[...] * dot(vert[...], d)
+
+
+def last_kernel(parts, lev, *refs):
     pieces, refs = refs[:parts], refs[parts:]
-    sd, vert, vert_t, state, residual = refs[:5]
-    increment_out, residual_out, spread = refs[-3:]
+    sd, vert_t, state, residual, before, direction, moved = refs[:7]
+    increment_out, residual_out, spread = refs[7:]
     members, levp, unused = residual.shape
     obs = lax.axis_index("obs")
     mine = pl.ds(pl.multiple_of(obs * LANES, LANES), LANES)
@@ -467,18 +488,9 @@
     energies = read_scalars(pieces, members, 1)
     for m in range(members):
         t = spread[m * lev : m * lev + levp, :]
-        norm, square, beta = state[m, 0:1, 0:1], state[m, 1:2, 0:1], state[m, 2:3, 0:1]
-        alpha = norm / (square + energies[m][0])
-        d = r = residual[m, :, mine]
-        if later:
-            old_direction, old_solution = refs[5:7]
-            d = r + beta * old_direction[m, :, mine]
-        solution = alpha * d
-        if later:
-            solution = old_solution[m] + solution
-        r = r - alpha * (d + dot(vert_t[...], sd[...] * t))
-        increment = sd[...] * dot(vert[...], solution)
-        increment_out[:, m, :] = increment[0:lev]
+        alpha = state[m, 0:1, 0:1] / (state[m, 1:2, 0:1] + energies[m][0])
+        increment_out[:, m, :] = (before[m] + alpha * moved[m])[0:lev]
+        r = residual[m, :, mine] - alpha * (direction[m] + dot(vert_t[...], sd[...] * t))
         residual_out[:, m, :] = r[0:lev]
 
 
@@ -636,8 +648,9 @@
             pltpu.VMEM(col_sd.shape, F32),
             pltpu.VMEM((blocks, lev, profiles), F32),
             pltpu.VMEM((blocks, lev, profiles), F32),
-            pltpu.VMEM((n_slab, members, levp, width), F32),
-            pltpu.VMEM((2, rows, width), F32),
+            pltpu.VMEM((n_slab, levp, width), jnp.int32),
+            pltpu.VMEM((n_slab // 2, members, levp, width), F32),
+            pltpu.VMEM((2, rows, 2 * width), F32),
             pltpu.VMEM((rows, lanes), F32),
             pltpu.SemaphoreType.DMA((5 + 2 * blocks,)),
             pltpu.SemaphoreType.DMA((h_block.shape[0] * halves,)),
@@ -720,14 +733,31 @@
                 theirs,
             )
             ps = [ps[0]] + [plane(ps[i], i) for i in reversed(range(1, n_obs))]
+            own_field = struct((members, levp, LANES), F32)
+            before, d, u_d = call(
+                functools.partial(increment_kernel, later),
+                [own_field] * 3,
+                [],
+                small,
+                col_sd,
+                vert,
+                state,
+                residual,
+                *([direction, total_step] if later else []),
+            )
             outputs = call(
-                functools.partial(last_kernel, len(ps), later, lev),
+                functools.partial(last_kernel, len(ps), lev),
                 [struct((lev, members, LANES), F32)] * 2,
                 [pltpu.VMEM((wide // 8 * 8, LANES), F32)],
                 small,
                 *ps,
                 col_sd,
-                *known,
+                vert_t,
+                state,
+                residual,
+                before,
+                d,
+                u_d,
             )
             break
         ps = call(

time: 114 us -> 113 us (level); the launches traced: 114 us -> 112 us
  starting transfers between devices: 44.9 us -> 38.9 us
  waiting for transfers between devices: 51.1 us -> 54.7 us
    ppermute x22, starting transfers between devices: 30.2 us -> 25 us  [along(): return lax.ppermute(x, 'slab', [(s, s ^ 2 * i) for s in range(n_slab)])]
    ppermute x22, waiting for transfers between devices: 27.3 us -> 30.8 us  [along(): return lax.ppermute(x, 'slab', [(s, s ^ 2 * i) for s in range(n_slab)])]
    ppermute x11, starting transfers between devices: 13.8 us -> 12.6 us  [plane(): return lax.ppermute(x, 'obs', [(o, o ^ i) for o in range(n_obs)])]
    pallas_call x22 -> x23, Pallas kernels: 14.4 us -> 14.5 us  [call(): pl.pallas_call(kernel, out_shape=outs, in_specs=[space] * len(args), out_...]
  transfers between devices with their start and end apart: 38 -> 38, of which waited for: 27 -> 27; matrix products, arithmetic and copies ran while one was open for 0% -> 0% of each run, Pallas kernels for 3% -> 4%
where the time goes in v16:
time: 113 us; the launch traced here: 112 us
  waiting for transfers between devices  54.7 us (48%)
  starting transfers between devices  38.9 us (34%)
  Pallas kernels  14.5 us (13%)
  local copies, waits for them, and re-layouts  2.09 us (2%)
  between operations  1.58 us (1%)
    ppermute x22, waiting for transfers between devices, along(): return lax.ppermute(x, 'slab', [(s, s ^ 2 * i) for s in range(n_slab)])  30.8 us
    ppermute x22, starting transfers between devices, along(): return lax.ppermute(x, 'slab', [(s, s ^ 2 * i) for s in range(n_slab)])  25 us
    ppermute x11, waiting for transfers between devices, plane(): return lax.ppermute(x, 'obs', [(o, o ^ i) for o in range(n_obs)])  19.7 us
    pallas_call x23, Pallas kernels, call(): pl.pallas_call(kernel, out_shape=outs, in_specs=[space] * len(args), out_...  14.5 us
    ppermute x11, starting transfers between devices, plane(): return lax.ppermute(x, 'obs', [(o, o ^ i) for o in range(n_obs)])  12.6 us
    ppermute x5, waiting for transfers between devices, swap(): return lax.ppermute(x, 'slab', [(s, s ^ 1) for s in range(n_slab)])  4.24 us
  transfers between devices with their start and end apart: 38, of which 27 were waited for; matrix products, arithmetic and copies ran while one was open for 0% of the time, Pallas kernels for 4%

profile of v16, /device:TPU:0, one launch (start us, length us, event | category | flops | bytes accessed | tf_op | source)
XLA Modules:
  0.0 111.9 jit_solution(3031336425273457215)
XLA Ops:
  1.3 5.1 %shard_map.104 = (bf16[4,4,128,256]{3,2,1,0:T(8,128)(2,1)}, bf16[4,4,128,256]{3,2,1,0:T(8,128)(2,1)}, bf16[304,256]{1,0:T(8,128)(2,1)}, bf16[304,256]{1,0:T(8,128)(2,1)}) custom-call(s32[4]{0:T(128)} %seeds_in.1, s32[1,1,32]{2,1,0:T(1,128)} %ids_in.1, s32[1,1,32]{2,1,0:T(1,128)} %cols_in.1, s32[1,1]{1,0:T(1,128)S(6)} %copy.16.count_in, f32[1,128]{1,0:T(1,128)} %refs_4_.1, ...), custom_call_target="tpu_custom_call" | custom-call | flops 637534208 | bytes 5735188 | tf_op jit(solution)/shard_map/pallas_call | solution.py:23
  7.4 2.6 %collective-permute-start = (bf16[304,256]{1,0:T(8,128)(2,1)}, bf16[304,256]{1,0:T(8,128)(2,1)S(1)}, u32[]{:S(2)}, u32[]{:S(2)}) collective-permute-start(bf16[304,256]{1,0:T(8,128)(2,1)} %get-tuple-element.66.refs_0_), channel_id=1, source_target_pairs={{0,1},{1,0},{2,3},{3,2},{4,5},{5,4},{6,7},{7,6},{8,9},{9,8},{10,11... | collective-permute-start | bytes 466952 | tf_op jit(solution)/shard_map/ppermute | solution.py:554
  10.0 1.5 %collective-permute-start.1 = (bf16[304,256]{1,0:T(8,128)(2,1)}, bf16[304,256]{1,0:T(8,128)(2,1)S(1)}, u32[]{:S(2)}, u32[]{:S(2)}) collective-permute-start(bf16[304,256]{1,0:T(8,128)(2,1)} %get-tuple-element.67.refs_1_), channel_id=1, source_target_pairs={{0,2},{1,3},{2,0},{3,1},{4,6},{5,7},{6,4},{7,5},{8,10},{9,11},{10,... | collective-permute-start | bytes 466952 | tf_op jit(solution)/shard_map/ppermute | solution.py:554
  14.8 1.5 %collective-permute-done.1.two_more = bf16[304,256]{1,0:T(8,128)(2,1)S(1)} collective-permute-done((bf16[304,256]{1,0:T(8,128)(2,1)}, bf16[304,256]{1,0:T(8,128)(2,1)S(1)}, u32[]{:S(2)}, u32[]{:S(2)}) %collective-permute-start.1) | collective-permute-done | bytes 155680 | tf_op jit(solution)/shard_map/ppermute | solution.py:554
  16.4 1.6 %collective-permute-start.2 = (bf16[304,256]{1,0:T(8,128)(2,1)S(1)}, bf16[304,256]{1,0:T(8,128)(2,1)S(1)}, u32[]{:S(2)}, u32[]{:S(2)}) collective-permute-start(bf16[304,256]{1,0:T(8,128)(2,1)S(1)} %get-tuple-element.70.refs_0_), channel_id=1, source_target_pairs={{0,2},{1,3},{2,0},{3,1},{4,6},{5,7},{6,4},{7,5},{8,10},{9,11},{10,... | collective-permute-start | bytes 466952 | tf_op jit(solution)/shard_map/ppermute | solution.py:554
  18.5 3.2 %collective-permute-done.2.refs_1_ = bf16[304,256]{1,0:T(8,128)(2,1)S(1)} collective-permute-done((bf16[304,256]{1,0:T(8,128)(2,1)S(1)}, bf16[304,256]{1,0:T(8,128)(2,1)S(1)}, u32[]{:S(2)}, u32[]{:S(2)}) %collective-permute-start.2) | collective-permute-done | bytes 155680 | tf_op jit(solution)/shard_map/ppermute | solution.py:554
  21.7 1.5 %collective-permute-done.3.refs_3_ = bf16[304,256]{1,0:T(8,128)(2,1)S(1)} collective-permute-done((bf16[304,256]{1,0:T(8,128)(2,1)S(1)}, bf16[304,256]{1,0:T(8,128)(2,1)S(1)}, u32[]{:S(2)}, u32[]{:S(2)}) %collective-permute-start.3) | collective-permute-done | bytes 155680 | tf_op jit(solution)/shard_map/ppermute | solution.py:554
  27.5 3.1 %collective-permute-start.6 = (bf16[160,256]{1,0:T(8,128)(2,1)S(1)}, bf16[160,256]{1,0:T(8,128)(2,1)S(1)}, u32[]{:S(2)}, u32[]{:S(2)}) collective-permute-start(bf16[160,256]{1,0:T(8,128)(2,1)S(1)} %get-tuple-element.83), channel_id=1, source_target_pairs={{0,16},{4,20},{8,24},{12,28},{16,0},{20,4},{24,8},{28,12},{1,17},{... | collective-permute-start | bytes 245768 | tf_op jit(solution)/shard_map/ppermute | solution.py:551
  31.2 1.7 %collective-permute-start.8 = (bf16[144,256]{1,0:T(8,128)(2,1)S(1)}, bf16[144,256]{1,0:T(8,128)(2,1)S(1)}, u32[]{:S(2)}, u32[]{:S(2)}) collective-permute-start(bf16[144,256]{1,0:T(8,128)(2,1)S(1)} %get-tuple-element.85), channel_id=1, source_target_pairs={{0,8},{4,12},{8,0},{12,4},{16,24},{20,28},{24,16},{28,20},{1,9},{5... | collective-permute-start | bytes 221192 | tf_op jit(solution)/shard_map/ppermute | solution.py:551
  32.9 2.2 %collective-permute-start.11 = (bf16[144,256]{1,0:T(8,128)(2,1)S(1)}, bf16[144,256]{1,0:T(8,128)(2,1)S(1)}, u32[]{:S(2)}, u32[]{:S(2)}) collective-permute-start(bf16[144,256]{1,0:T(8,128)(2,1)S(1)} %shard_map.110), channel_id=1, source_target_pairs={{0,16},{4,20},{8,24},{12,28},{16,0},{20,4},{24,8},{28,12},{1,17},{... | collective-permute-start | bytes 221192 | tf_op jit(solution)/shard_map/ppermute | solution.py:551
  35.4 3.7 %collective-permute-done.8.refs_3_ = bf16[144,256]{1,0:T(8,128)(2,1)S(1)} collective-permute-done((bf16[144,256]{1,0:T(8,128)(2,1)S(1)}, bf16[144,256]{1,0:T(8,128)(2,1)S(1)}, u32[]{:S(2)}, u32[]{:S(2)}) %collective-permute-start.8) | collective-permute-done | bytes 73760 | tf_op jit(solution)/shard_map/ppermute | solution.py:551
  39.1 2.4 %collective-permute-done.11.refs_5_ = bf16[144,256]{1,0:T(8,128)(2,1)S(1)} collective-permute-done((bf16[144,256]{1,0:T(8,128)(2,1)S(1)}, bf16[144,256]{1,0:T(8,128)(2,1)S(1)}, u32[]{:S(2)}, u32[]{:S(2)}) %collective-permute-start.11) | collective-permute-done | bytes 73760 | tf_op jit(solution)/shard_map/ppermute | solution.py:551
  42.2 2.6 %collective-permute-start.13 = (bf16[144,256]{1,0:T(8,128)(2,1)S(1)}, bf16[144,256]{1,0:T(8,128)(2,1)S(1)}, u32[]{:S(2)}, u32[]{:S(2)}) collective-permute-start(bf16[144,256]{1,0:T(8,128)(2,1)S(1)} %get-tuple-element.90), channel_id=1, source_target_pairs={{0,16},{4,20},{8,24},{12,28},{16,0},{20,4},{24,8},{28,12},{1,17},{... | collective-permute-start | bytes 221192 | tf_op jit(solution)/shard_map/ppermute | solution.py:551
  44.8 1.4 %collective-permute-start.16 = (bf16[160,256]{1,0:T(8,128)(2,1)S(1)}, bf16[160,256]{1,0:T(8,128)(2,1)S(1)}, u32[]{:S(2)}, u32[]{:S(2)}) collective-permute-start(bf16[160,256]{1,0:T(8,128)(2,1)S(1)} %get-tuple-element.91), channel_id=1, source_target_pairs={{0,24},{4,28},{8,16},{12,20},{16,8},{20,12},{24,0},{28,4},{1,25},{... | collective-permute-start | bytes 245768 | tf_op jit(solution)/shard_map/ppermute | solution.py:551
  46.3 4.2 %collective-permute-done.13.refs_2_ = bf16[144,256]{1,0:T(8,128)(2,1)S(1)} collective-permute-done((bf16[144,256]{1,0:T(8,128)(2,1)S(1)}, bf16[144,256]{1,0:T(8,128)(2,1)S(1)}, u32[]{:S(2)}, u32[]{:S(2)}) %collective-permute-start.13) | collective-permute-done | bytes 73760 | tf_op jit(solution)/shard_map/ppermute | solution.py:551
  50.5 1.3 %collective-permute-done.16.refs_5_ = bf16[160,256]{1,0:T(8,128)(2,1)S(1)} collective-permute-done((bf16[160,256]{1,0:T(8,128)(2,1)S(1)}, bf16[160,256]{1,0:T(8,128)(2,1)S(1)}, u32[]{:S(2)}, u32[]{:S(2)}) %collective-permute-start.16) | collective-permute-done | bytes 81952 | tf_op jit(solution)/shard_map/ppermute | solution.py:551
  51.8 2.6 %collective-permute-done.14.refs_3_ = bf16[160,256]{1,0:T(8,128)(2,1)S(1)} collective-permute-done((bf16[160,256]{1,0:T(8,128)(2,1)S(1)}, bf16[160,256]{1,0:T(8,128)(2,1)S(1)}, u32[]{:S(2)}, u32[]{:S(2)}) %collective-permute-start.14) | collective-permute-done | bytes 81952 | tf_op jit(solution)/shard_map/ppermute | solution.py:551
  58.6 5.0 %collective-permute-done.18.one_more = bf16[304,256]{1,0:T(8,128)(2,1)S(1)} collective-permute-done((bf16[304,256]{1,0:T(8,128)(2,1)S(1)}, bf16[304,256]{1,0:T(8,128)(2,1)S(1)}, u32[]{:S(2)}, u32[]{:S(2)}) %collective-permute-start.18) | collective-permute-done | bytes 155680 | tf_op jit(solution)/shard_map/ppermute | solution.py:554
  64.6 1.3 %collective-permute-start.21 = (bf16[304,256]{1,0:T(8,128)(2,1)S(1)}, bf16[304,256]{1,0:T(8,128)(2,1)S(1)}, u32[]{:S(2)}, u32[]{:S(2)}) collective-permute-start(bf16[304,256]{1,0:T(8,128)(2,1)S(1)} %get-tuple-element.95.refs_2_), channel_id=1, source_target_pairs={{0,1},{1,0},{2,3},{3,2},{4,5},{5,4},{6,7},{7,6},{8,9},{9,8},{10,11... | collective-permute-start | bytes 466952 | tf_op jit(solution)/shard_map/ppermute | solution.py:554
  65.9 3.3 %collective-permute-done.20.refs_1_ = bf16[304,256]{1,0:T(8,128)(2,1)S(1)} collective-permute-done((bf16[304,256]{1,0:T(8,128)(2,1)S(1)}, bf16[304,256]{1,0:T(8,128)(2,1)S(1)}, u32[]{:S(2)}, u32[]{:S(2)}) %collective-permute-start.20) | collective-permute-done | bytes 155680 | tf_op jit(solution)/shard_map/ppermute | solution.py:554
  69.8 1.2 %shard_map.117 = (f32[4,80,512]{2,1,0:T(8,128)S(1)}, f32[4,80,128]{2,1,0:T(8,128)S(1)}, bf16[304,512]{1,0:T(8,128)(2,1)S(1)}) custom-call(bf16[304,256]{1,0:T(8,128)(2,1)S(1)} %get-tuple-element.94.refs_0_, bf16[304,256]{1,0:T(8,128)(2,1)S(1)} %collective-permute-done.20.refs_1_, bf16[304,256]{1,0:T(8,128)(2,1)S(1)} %get-tuple-element.95.refs_2_, ...), custom_call_target="tpu_custom_call" | custom-call | flops 149422080 | bytes 2503680 | tf_op jit(solution)/shard_map/pallas_call | solution.py:23
  73.4 2.6 %collective-permute-start.23 = (bf16[160,256]{1,0:T(8,128)(2,1)S(1)}, bf16[160,256]{1,0:T(8,128)(2,1)S(1)}, u32[]{:S(2)}, u32[]{:S(2)}) collective-permute-start(bf16[160,256]{1,0:T(8,128)(2,1)S(1)} %get-tuple-element.108), channel_id=1, source_target_pairs={{0,16},{4,20},{8,24},{12,28},{16,0},{20,4},{24,8},{28,12},{1,17},{... | collective-permute-start | bytes 245768 | tf_op jit(solution)/shard_map/ppermute | solution.py:551
  76.0 1.7 %collective-permute-start.24 = (bf16[160,256]{1,0:T(8,128)(2,1)S(1)}, bf16[160,256]{1,0:T(8,128)(2,1)S(1)}, u32[]{:S(2)}, u32[]{:S(2)}) collective-permute-start(bf16[160,256]{1,0:T(8,128)(2,1)S(1)} %get-tuple-element.109), channel_id=1, source_target_pairs={{0,24},{4,28},{8,16},{12,20},{16,8},{20,12},{24,0},{28,4},{1,25},{... | collective-permute-start | bytes 245768 | tf_op jit(solution)/shard_map/ppermute | solution.py:551
  77.7 2.0 %collective-permute-start.25 = (bf16[144,256]{1,0:T(8,128)(2,1)S(1)}, bf16[144,256]{1,0:T(8,128)(2,1)S(1)}, u32[]{:S(2)}, u32[]{:S(2)}) collective-permute-start(bf16[144,256]{1,0:T(8,128)(2,1)S(1)} %get-tuple-element.110), channel_id=1, source_target_pairs={{0,8},{4,12},{8,0},{12,4},{16,24},{20,28},{24,16},{28,20},{1,9},{5... | collective-permute-start | bytes 221192 | tf_op jit(solution)/shard_map/ppermute | solution.py:551
  80.5 6.1 %collective-permute-done.25.refs_3_ = bf16[144,256]{1,0:T(8,128)(2,1)S(1)} collective-permute-done((bf16[144,256]{1,0:T(8,128)(2,1)S(1)}, bf16[144,256]{1,0:T(8,128)(2,1)S(1)}, u32[]{:S(2)}, u32[]{:S(2)}) %collective-permute-start.25) | collective-permute-done | bytes 73760 | tf_op jit(solution)/shard_map/ppermute | solution.py:551
  87.9 2.4 %collective-permute-start.30 = (bf16[144,256]{1,0:T(8,128)(2,1)S(1)}, bf16[144,256]{1,0:T(8,128)(2,1)S(1)}, u32[]{:S(2)}, u32[]{:S(2)}) collective-permute-start(bf16[144,256]{1,0:T(8,128)(2,1)S(1)} %get-tuple-element.116), channel_id=1, source_target_pairs={{0,16},{4,20},{8,24},{12,28},{16,0},{20,4},{24,8},{28,12},{1,17},{... | collective-permute-start | bytes 221192 | tf_op jit(solution)/shard_map/ppermute | solution.py:551
  90.3 1.7 %collective-permute-start.33 = (bf16[160,256]{1,0:T(8,128)(2,1)S(1)}, bf16[160,256]{1,0:T(8,128)(2,1)S(1)}, u32[]{:S(2)}, u32[]{:S(2)}) collective-permute-start(bf16[160,256]{1,0:T(8,128)(2,1)S(1)} %get-tuple-element.117), channel_id=1, source_target_pairs={{0,24},{4,28},{8,16},{12,20},{16,8},{20,12},{24,0},{28,4},{1,25},{... | collective-permute-start | bytes 245768 | tf_op jit(solution)/shard_map/ppermute | solution.py:551
  92.1 4.7 %collective-permute-done.30.refs_2_ = bf16[144,256]{1,0:T(8,128)(2,1)S(1)} collective-permute-done((bf16[144,256]{1,0:T(8,128)(2,1)S(1)}, bf16[144,256]{1,0:T(8,128)(2,1)S(1)}, u32[]{:S(2)}, u32[]{:S(2)}) %collective-permute-start.30) | collective-permute-done | bytes 73760 | tf_op jit(solution)/shard_map/ppermute | solution.py:551
  97.7 2.5 %collective-permute-done.31.refs_3_ = bf16[160,256]{1,0:T(8,128)(2,1)S(1)} collective-permute-done((bf16[160,256]{1,0:T(8,128)(2,1)S(1)}, bf16[160,256]{1,0:T(8,128)(2,1)S(1)}, u32[]{:S(2)}, u32[]{:S(2)}) %collective-permute-start.31) | collective-permute-done | bytes 81952 | tf_op jit(solution)/shard_map/ppermute | solution.py:551
  103.5 2.4 %collective-permute-start.35 = (bf16[304,128]{1,0:T(8,128)(2,1)S(1)}, bf16[304,128]{1,0:T(8,128)(2,1)S(1)}, u32[]{:S(2)}, u32[]{:S(2)}) collective-permute-start(bf16[304,128]{1,0:T(8,128)(2,1)S(1)} %get-tuple-element.119), channel_id=1, source_target_pairs={{0,3},{1,2},{2,1},{3,0},{4,7},{5,6},{6,5},{7,4},{8,11},{9,10},{10,... | collective-permute-start | bytes 233480 | tf_op jit(solution)/shard_map/ppermute | solution.py:554
  107.3 1.5 %collective-permute-done.35.refs_1_ = bf16[304,128]{1,0:T(8,128)(2,1)S(1)} collective-permute-done((bf16[304,128]{1,0:T(8,128)(2,1)S(1)}, bf16[304,128]{1,0:T(8,128)(2,1)S(1)}, u32[]{:S(2)}, u32[]{:S(2)}) %collective-permute-start.35) | collective-permute-done | bytes 77856 | tf_op jit(solution)/shard_map/ppermute | solution.py:554
  108.9 1.6 %collective-permute-done.36.refs_2_ = bf16[304,128]{1,0:T(8,128)(2,1)S(1)} collective-permute-done((bf16[304,128]{1,0:T(8,128)(2,1)S(1)}, bf16[304,128]{1,0:T(8,128)(2,1)S(1)}, u32[]{:S(2)}, u32[]{:S(2)}) %collective-permute-start.36) | collective-permute-done | bytes 77856 | tf_op jit(solution)/shard_map/ppermute | solution.py:554
  (86 shorter events, 28.0 us)
Async XLA Ops:
  6.4 19.5 %collective-permute-start.5 = (bf16[4,4,128,256]{3,2,1,0:T(8,128)(2,1)}, bf16[4,4,128,256]{3,2,1,0:T(8,128)(2,1)S(1)}, u32[]{:S(2)}, u32[]{:S(2)}) collective-permute-start(bf16[4,4,128,256]{3,2,1,0:T(8,128)(2,1)} %get-tuple-element.73), channel_id=1, source_target_pairs={{0,4},{4,0},{8,12},{12,8},{16,20},{20,16},{24,28},{28,24},{1,5},{5... | collective-permute-start | bytes 3145736 | tf_op jit(solution)/shard_map/ppermute | solution.py:557
  7.4 7.4 %collective-permute-start = (bf16[304,256]{1,0:T(8,128)(2,1)}, bf16[304,256]{1,0:T(8,128)(2,1)S(1)}, u32[]{:S(2)}, u32[]{:S(2)}) collective-permute-start(bf16[304,256]{1,0:T(8,128)(2,1)} %get-tuple-element.66.refs_0_), channel_id=1, source_target_pairs={{0,1},{1,0},{2,3},{3,2},{4,5},{5,4},{6,7},{7,6},{8,9},{9,8},{10,11... | collective-permute-start | bytes 466952 | tf_op jit(solution)/shard_map/ppermute | solution.py:554
  10.0 6.3 %collective-permute-start.1 = (bf16[304,256]{1,0:T(8,128)(2,1)}, bf16[304,256]{1,0:T(8,128)(2,1)S(1)}, u32[]{:S(2)}, u32[]{:S(2)}) collective-permute-start(bf16[304,256]{1,0:T(8,128)(2,1)} %get-tuple-element.67.refs_1_), channel_id=1, source_target_pairs={{0,2},{1,3},{2,0},{3,1},{4,6},{5,7},{6,4},{7,5},{8,10},{9,11},{10,... | collective-permute-start | bytes 466952 | tf_op jit(solution)/shard_map/ppermute | solution.py:554
  16.4 5.3 %collective-permute-start.2 = (bf16[304,256]{1,0:T(8,128)(2,1)S(1)}, bf16[304,256]{1,0:T(8,128)(2,1)S(1)}, u32[]{:S(2)}, u32[]{:S(2)}) collective-permute-start(bf16[304,256]{1,0:T(8,128)(2,1)S(1)} %get-tuple-element.70.refs_0_), channel_id=1, source_target_pairs={{0,2},{1,3},{2,0},{3,1},{4,6},{5,7},{6,4},{7,5},{8,10},{9,11},{10,... | collective-permute-start | bytes 466952 | tf_op jit(solution)/shard_map/ppermute | solution.py:554
  17.9 5.2 %collective-permute-start.3 = (bf16[304,256]{1,0:T(8,128)(2,1)S(1)}, bf16[304,256]{1,0:T(8,128)(2,1)S(1)}, u32[]{:S(2)}, u32[]{:S(2)}) collective-permute-start(bf16[304,256]{1,0:T(8,128)(2,1)S(1)} %get-tuple-element.71.refs_2_), channel_id=1, source_target_pairs={{0,1},{1,0},{2,3},{3,2},{4,5},{5,4},{6,7},{7,6},{8,9},{9,8},{10,11... | collective-permute-start | bytes 466952 | tf_op jit(solution)/shard_map/ppermute | solution.py:554
  26.4 6.5 %collective-permute-start.10 = (bf16[144,256]{1,0:T(8,128)(2,1)S(1)}, bf16[144,256]{1,0:T(8,128)(2,1)S(1)}, u32[]{:S(2)}, u32[]{:S(2)}) collective-permute-start(bf16[144,256]{1,0:T(8,128)(2,1)S(1)} %get-tuple-element.88), channel_id=1, source_target_pairs={{0,8},{4,12},{8,0},{12,4},{16,24},{20,28},{24,16},{28,20},{1,9},{5... | collective-permute-start | bytes 221192 | tf_op jit(solution)/shard_map/ppermute | solution.py:551
  27.5 11.5 %collective-permute-start.6 = (bf16[160,256]{1,0:T(8,128)(2,1)S(1)}, bf16[160,256]{1,0:T(8,128)(2,1)S(1)}, u32[]{:S(2)}, u32[]{:S(2)}) collective-permute-start(bf16[160,256]{1,0:T(8,128)(2,1)S(1)} %get-tuple-element.83), channel_id=1, source_target_pairs={{0,16},{4,20},{8,24},{12,28},{16,0},{20,4},{24,8},{28,12},{1,17},{... | collective-permute-start | bytes 245768 | tf_op jit(solution)/shard_map/ppermute | solution.py:551
  30.6 8.4 %collective-permute-start.7 = (bf16[160,256]{1,0:T(8,128)(2,1)S(1)}, bf16[160,256]{1,0:T(8,128)(2,1)S(1)}, u32[]{:S(2)}, u32[]{:S(2)}) collective-permute-start(bf16[160,256]{1,0:T(8,128)(2,1)S(1)} %get-tuple-element.84), channel_id=1, source_target_pairs={{0,24},{4,28},{8,16},{12,20},{16,8},{20,12},{24,0},{28,4},{1,25},{... | collective-permute-start | bytes 245768 | tf_op jit(solution)/shard_map/ppermute | solution.py:551
  30.9 8.2 %collective-permute-start.9 = (bf16[160,256]{1,0:T(8,128)(2,1)S(1)}, bf16[160,256]{1,0:T(8,128)(2,1)S(1)}, u32[]{:S(2)}, u32[]{:S(2)}) collective-permute-start(bf16[160,256]{1,0:T(8,128)(2,1)S(1)} %get-tuple-element.86), channel_id=1, source_target_pairs={{0,8},{4,12},{8,0},{12,4},{16,24},{20,28},{24,16},{28,20},{1,9},{5... | collective-permute-start | bytes 245768 | tf_op jit(solution)/shard_map/ppermute | solution.py:551
  31.2 7.9 %collective-permute-start.8 = (bf16[144,256]{1,0:T(8,128)(2,1)S(1)}, bf16[144,256]{1,0:T(8,128)(2,1)S(1)}, u32[]{:S(2)}, u32[]{:S(2)}) collective-permute-start(bf16[144,256]{1,0:T(8,128)(2,1)S(1)} %get-tuple-element.85), channel_id=1, source_target_pairs={{0,8},{4,12},{8,0},{12,4},{16,24},{20,28},{24,16},{28,20},{1,9},{5... | collective-permute-start | bytes 221192 | tf_op jit(solution)/shard_map/ppermute | solution.py:551
  32.9 8.6 %collective-permute-start.11 = (bf16[144,256]{1,0:T(8,128)(2,1)S(1)}, bf16[144,256]{1,0:T(8,128)(2,1)S(1)}, u32[]{:S(2)}, u32[]{:S(2)}) collective-permute-start(bf16[144,256]{1,0:T(8,128)(2,1)S(1)} %shard_map.110), channel_id=1, source_target_pairs={{0,16},{4,20},{8,24},{12,28},{16,0},{20,4},{24,8},{28,12},{1,17},{... | collective-permute-start | bytes 221192 | tf_op jit(solution)/shard_map/ppermute | solution.py:551
  41.7 13.5 %collective-permute-start.12 = (bf16[304,256]{1,0:T(8,128)(2,1)S(1)}, bf16[304,256]{1,0:T(8,128)(2,1)S(1)}, u32[]{:S(2)}, u32[]{:S(2)}) collective-permute-start(bf16[304,256]{1,0:T(8,128)(2,1)S(1)} %get-tuple-element.89.refs_0_), channel_id=1, source_target_pairs={{0,8},{4,12},{8,0},{12,4},{16,24},{20,28},{24,16},{28,20},{1,9},{5... | collective-permute-start | bytes 466952 | tf_op jit(solution)/shard_map/ppermute | solution.py:551
  42.2 8.3 %collective-permute-start.13 = (bf16[144,256]{1,0:T(8,128)(2,1)S(1)}, bf16[144,256]{1,0:T(8,128)(2,1)S(1)}, u32[]{:S(2)}, u32[]{:S(2)}) collective-permute-start(bf16[144,256]{1,0:T(8,128)(2,1)S(1)} %get-tuple-element.90), channel_id=1, source_target_pairs={{0,16},{4,20},{8,24},{12,28},{16,0},{20,4},{24,8},{28,12},{1,17},{... | collective-permute-start | bytes 221192 | tf_op jit(solution)/shard_map/ppermute | solution.py:551
  44.8 7.0 %collective-permute-start.16 = (bf16[160,256]{1,0:T(8,128)(2,1)S(1)}, bf16[160,256]{1,0:T(8,128)(2,1)S(1)}, u32[]{:S(2)}, u32[]{:S(2)}) collective-permute-start(bf16[160,256]{1,0:T(8,128)(2,1)S(1)} %get-tuple-element.91), channel_id=1, source_target_pairs={{0,24},{4,28},{8,16},{12,20},{16,8},{20,12},{24,0},{28,4},{1,25},{... | collective-permute-start | bytes 245768 | tf_op jit(solution)/shard_map/ppermute | solution.py:551
  46.2 8.3 %collective-permute-start.14 = (bf16[160,256]{1,0:T(8,128)(2,1)S(1)}, bf16[160,256]{1,0:T(8,128)(2,1)S(1)}, u32[]{:S(2)}, u32[]{:S(2)}) collective-permute-start(bf16[160,256]{1,0:T(8,128)(2,1)S(1)} %get-tuple-element.91), channel_id=1, source_target_pairs={{0,16},{4,20},{8,24},{12,28},{16,0},{20,4},{24,8},{28,12},{1,17},{... | collective-permute-start | bytes 245768 | tf_op jit(solution)/shard_map/ppermute | solution.py:551
  50.5 4.7 %collective-permute-start.15 = (bf16[144,256]{1,0:T(8,128)(2,1)S(1)}, bf16[144,256]{1,0:T(8,128)(2,1)S(1)}, u32[]{:S(2)}, u32[]{:S(2)}) collective-permute-start(bf16[144,256]{1,0:T(8,128)(2,1)S(1)} %collective-permute-done.13.refs_2_), channel_id=1, source_target_pairs={{0,8},{4,12},{8,0},{12,4},{16,24},{20,28},{24,16},{28,20},{1,9},{5... | collective-permute-start | bytes 221192 | tf_op jit(solution)/shard_map/ppermute | solution.py:551
  57.5 6.1 %collective-permute-start.18 = (bf16[304,256]{1,0:T(8,128)(2,1)S(1)}, bf16[304,256]{1,0:T(8,128)(2,1)S(1)}, u32[]{:S(2)}, u32[]{:S(2)}) collective-permute-start(bf16[304,256]{1,0:T(8,128)(2,1)S(1)} %get-tuple-element.92.one), channel_id=1, source_target_pairs={{0,1},{1,0},{2,3},{3,2},{4,5},{5,4},{6,7},{7,6},{8,9},{9,8},{10,11... | collective-permute-start | bytes 466952 | tf_op jit(solution)/shard_map/ppermute | solution.py:554
  58.0 5.8 %collective-permute-start.19 = (bf16[304,256]{1,0:T(8,128)(2,1)S(1)}, bf16[304,256]{1,0:T(8,128)(2,1)S(1)}, u32[]{:S(2)}, u32[]{:S(2)}) collective-permute-start(bf16[304,256]{1,0:T(8,128)(2,1)S(1)} %get-tuple-element.93.two), channel_id=1, source_target_pairs={{0,2},{1,3},{2,0},{3,1},{4,6},{5,7},{6,4},{7,5},{8,10},{9,11},{10,... | collective-permute-start | bytes 466952 | tf_op jit(solution)/shard_map/ppermute | solution.py:554
  63.9 5.3 %collective-permute-start.20 = (bf16[304,256]{1,0:T(8,128)(2,1)S(1)}, bf16[304,256]{1,0:T(8,128)(2,1)S(1)}, u32[]{:S(2)}, u32[]{:S(2)}) collective-permute-start(bf16[304,256]{1,0:T(8,128)(2,1)S(1)} %get-tuple-element.94.refs_0_), channel_id=1, source_target_pairs={{0,2},{1,3},{2,0},{3,1},{4,6},{5,7},{6,4},{7,5},{8,10},{9,11},{10,... | collective-permute-start | bytes 466952 | tf_op jit(solution)/shard_map/ppermute | solution.py:554
  64.6 5.2 %collective-permute-start.21 = (bf16[304,256]{1,0:T(8,128)(2,1)S(1)}, bf16[304,256]{1,0:T(8,128)(2,1)S(1)}, u32[]{:S(2)}, u32[]{:S(2)}) collective-permute-start(bf16[304,256]{1,0:T(8,128)(2,1)S(1)} %get-tuple-element.95.refs_2_), channel_id=1, source_target_pairs={{0,1},{1,0},{2,3},{3,2},{4,5},{5,4},{6,7},{7,6},{8,9},{9,8},{10,11... | collective-permute-start | bytes 466952 | tf_op jit(solution)/shard_map/ppermute | solution.py:554
  73.3 6.5 %collective-permute-start.27 = (bf16[144,256]{1,0:T(8,128)(2,1)S(1)}, bf16[144,256]{1,0:T(8,128)(2,1)S(1)}, u32[]{:S(2)}, u32[]{:S(2)}) collective-permute-start(bf16[144,256]{1,0:T(8,128)(2,1)S(1)} %get-tuple-element.113), channel_id=1, source_target_pairs={{0,8},{4,12},{8,0},{12,4},{16,24},{20,28},{24,16},{28,20},{1,9},{5... | collective-permute-start | bytes 221192 | tf_op jit(solution)/shard_map/ppermute | solution.py:551
  73.4 13.2 %collective-permute-start.23 = (bf16[160,256]{1,0:T(8,128)(2,1)S(1)}, bf16[160,256]{1,0:T(8,128)(2,1)S(1)}, u32[]{:S(2)}, u32[]{:S(2)}) collective-permute-start(bf16[160,256]{1,0:T(8,128)(2,1)S(1)} %get-tuple-element.108), channel_id=1, source_target_pairs={{0,16},{4,20},{8,24},{12,28},{16,0},{20,4},{24,8},{28,12},{1,17},{... | collective-permute-start | bytes 245768 | tf_op jit(solution)/shard_map/ppermute | solution.py:551
  76.0 10.6 %collective-permute-start.24 = (bf16[160,256]{1,0:T(8,128)(2,1)S(1)}, bf16[160,256]{1,0:T(8,128)(2,1)S(1)}, u32[]{:S(2)}, u32[]{:S(2)}) collective-permute-start(bf16[160,256]{1,0:T(8,128)(2,1)S(1)} %get-tuple-element.109), channel_id=1, source_target_pairs={{0,24},{4,28},{8,16},{12,20},{16,8},{20,12},{24,0},{28,4},{1,25},{... | collective-permute-start | bytes 245768 | tf_op jit(solution)/shard_map/ppermute | solution.py:551
  77.7 8.9 %collective-permute-start.26 = (bf16[160,256]{1,0:T(8,128)(2,1)S(1)}, bf16[160,256]{1,0:T(8,128)(2,1)S(1)}, u32[]{:S(2)}, u32[]{:S(2)}) collective-permute-start(bf16[160,256]{1,0:T(8,128)(2,1)S(1)} %get-tuple-element.111), channel_id=1, source_target_pairs={{0,8},{4,12},{8,0},{12,4},{16,24},{20,28},{24,16},{28,20},{1,9},{5... | collective-permute-start | bytes 245768 | tf_op jit(solution)/shard_map/ppermute | solution.py:551
  77.7 8.8 %collective-permute-start.25 = (bf16[144,256]{1,0:T(8,128)(2,1)S(1)}, bf16[144,256]{1,0:T(8,128)(2,1)S(1)}, u32[]{:S(2)}, u32[]{:S(2)}) collective-permute-start(bf16[144,256]{1,0:T(8,128)(2,1)S(1)} %get-tuple-element.110), channel_id=1, source_target_pairs={{0,8},{4,12},{8,0},{12,4},{16,24},{20,28},{24,16},{28,20},{1,9},{5... | collective-permute-start | bytes 221192 | tf_op jit(solution)/shard_map/ppermute | solution.py:551
  79.8 7.5 %collective-permute-start.28 = (bf16[144,256]{1,0:T(8,128)(2,1)S(1)}, bf16[144,256]{1,0:T(8,128)(2,1)S(1)}, u32[]{:S(2)}, u32[]{:S(2)}) collective-permute-start(bf16[144,256]{1,0:T(8,128)(2,1)S(1)} %shard_map.120), channel_id=1, source_target_pairs={{0,16},{4,20},{8,24},{12,28},{16,0},{20,4},{24,8},{28,12},{1,17},{... | collective-permute-start | bytes 221192 | tf_op jit(solution)/shard_map/ppermute | solution.py:551
  87.6 13.5 %collective-permute-start.29 = (bf16[304,256]{1,0:T(8,128)(2,1)S(1)}, bf16[304,256]{1,0:T(8,128)(2,1)S(1)}, u32[]{:S(2)}, u32[]{:S(2)}) collective-permute-start(bf16[304,256]{1,0:T(8,128)(2,1)S(1)} %get-tuple-element.115.refs_0_), channel_id=1, source_target_pairs={{0,8},{4,12},{8,0},{12,4},{16,24},{20,28},{24,16},{28,20},{1,9},{5... | collective-permute-start | bytes 466952 | tf_op jit(solution)/shard_map/ppermute | solution.py:551
  87.9 8.8 %collective-permute-start.30 = (bf16[144,256]{1,0:T(8,128)(2,1)S(1)}, bf16[144,256]{1,0:T(8,128)(2,1)S(1)}, u32[]{:S(2)}, u32[]{:S(2)}) collective-permute-start(bf16[144,256]{1,0:T(8,128)(2,1)S(1)} %get-tuple-element.116), channel_id=1, source_target_pairs={{0,16},{4,20},{8,24},{12,28},{16,0},{20,4},{24,8},{28,12},{1,17},{... | collective-permute-start | bytes 221192 | tf_op jit(solution)/shard_map/ppermute | solution.py:551
  90.3 7.4 %collective-permute-start.33 = (bf16[160,256]{1,0:T(8,128)(2,1)S(1)}, bf16[160,256]{1,0:T(8,128)(2,1)S(1)}, u32[]{:S(2)}, u32[]{:S(2)}) collective-permute-start(bf16[160,256]{1,0:T(8,128)(2,1)S(1)} %get-tuple-element.117), channel_id=1, source_target_pairs={{0,24},{4,28},{8,16},{12,20},{16,8},{20,12},{24,0},{28,4},{1,25},{... | collective-permute-start | bytes 245768 | tf_op jit(solution)/shard_map/ppermute | solution.py:551
  92.1 8.2 %collective-permute-start.31 = (bf16[160,256]{1,0:T(8,128)(2,1)S(1)}, bf16[160,256]{1,0:T(8,128)(2,1)S(1)}, u32[]{:S(2)}, u32[]{:S(2)}) collective-permute-start(bf16[160,256]{1,0:T(8,128)(2,1)S(1)} %get-tuple-element.117), channel_id=1, source_target_pairs={{0,16},{4,20},{8,24},{12,28},{16,0},{20,4},{24,8},{28,12},{1,17},{... | collective-permute-start | bytes 245768 | tf_op jit(solution)/shard_map/ppermute | solution.py:551
  103.5 5.4 %collective-permute-start.35 = (bf16[304,128]{1,0:T(8,128)(2,1)S(1)}, bf16[304,128]{1,0:T(8,128)(2,1)S(1)}, u32[]{:S(2)}, u32[]{:S(2)}) collective-permute-start(bf16[304,128]{1,0:T(8,128)(2,1)S(1)} %get-tuple-element.119), channel_id=1, source_target_pairs={{0,3},{1,2},{2,1},{3,0},{4,7},{5,6},{6,5},{7,4},{8,11},{9,10},{10,... | collective-permute-start | bytes 233480 | tf_op jit(solution)/shard_map/ppermute | solution.py:554
  105.9 4.6 %collective-permute-start.36 = (bf16[304,128]{1,0:T(8,128)(2,1)S(1)}, bf16[304,128]{1,0:T(8,128)(2,1)S(1)}, u32[]{:S(2)}, u32[]{:S(2)}) collective-permute-start(bf16[304,128]{1,0:T(8,128)(2,1)S(1)} %get-tuple-element.120), channel_id=1, source_target_pairs={{0,2},{1,3},{2,0},{3,1},{4,6},{5,7},{6,4},{7,5},{8,10},{9,11},{10,... | collective-permute-start | bytes 233480 | tf_op jit(solution)/shard_map/ppermute | solution.py:554
  (12 other events, 64.6 us)

commit v17 on v16

--- a/solution.py
+++ b/solution.py
@@ -119,11 +119,12 @@
 def start_kernel(
     dims, seeds_in, ids_in, cols_in, count_in, sd_in, innov_in, prec_in, h, own, partner, *rest
 ):
-    chips, halves = dims
+    chips, halves, blocks, lev = dims
     outs = rest[:-13]
     seeds, ids, cols, count, sd, innov, prec, bases, hashed, scratch, acc, sems, h_sems = rest[-13:]
     z, core, obs = place()
-    blocks, lev, profiles = innov.shape
+    strips = innov.shape[0]
+    profiles = strips * LANES
     colblocks, width = own.shape[1], own.shape[3]
     members, levp = hashed.shape[1], hashed.shape[2]
     rows = acc.shape[0]
@@ -133,10 +134,14 @@
     for copy in small:
         copy.start()
     large = []
-    for b in range(blocks):
-        at = len(pairs) + 2 * b
-        large.append(pltpu.make_async_copy(innov_in.at[:, b, :], innov.at[b], sems.at[at]))
-        large.append(pltpu.make_async_copy(prec_in.at[:, b, :], prec.at[b], sems.at[at + 1]))
+    for x, y in ((innov_in, innov), (prec_in, prec)):
+        for t in range(strips):
+            at = len(pairs) + len(large)
+            large.append(
+                pltpu.make_async_copy(
+                    x.at[:, t * LANES : (t + 1) * LANES], y.at[t, 0 : lev * blocks, :], sems.at[at]
+                )
+            )
     for copy in large:
         copy.start()
     own[...] = jnp.zeros_like(own)
@@ -205,11 +210,17 @@
         source, zz = order[at]
         piece = piece_at(at)
         b = piece // halves
-        if halves == 1:
-            p, d = prec[b], innov[b]
-        else:
-            lanes = pl.ds(pl.multiple_of((piece % halves) * width, LANES), width)
-            p, d = prec[b, :, lanes], innov[b, :, lanes]
+        strip = (piece % halves) * (width // LANES)
+        p, d = [
+            jnp.concatenate(
+                [
+                    x[strip + t, pl.ds(b, lev, stride=blocks), :]
+                    for t in range(width // LANES)
+                ],
+                axis=1,
+            )
+            for x in (prec, innov)
+        ]
         gain = 3.4 * p * lax.rsqrt(p)
         offset = p * d - 0.5 * gain
         gain = gain * (1.0 / PRIME)
@@ -638,7 +649,7 @@
 
     dense = struct((chips, colblocks, LANES, width), BF16)
     own, for_partner, *partials = call(
-        functools.partial(start_kernel, (chips, halves)),
+        functools.partial(start_kernel, (chips, halves, blocks, lev)),
         [dense, dense] + half_rows,
         [
             pltpu.SMEM(seeds.shape, jnp.int32),
@@ -646,13 +657,13 @@
             pltpu.SMEM(block_col.shape, jnp.int32),
             pltpu.SMEM(entry_count.shape, jnp.int32),
             pltpu.VMEM(col_sd.shape, F32),
-            pltpu.VMEM((blocks, lev, profiles), F32),
-            pltpu.VMEM((blocks, lev, profiles), F32),
+            pltpu.VMEM((profiles // LANES, levp * blocks, LANES), F32),
+            pltpu.VMEM((profiles // LANES, levp * blocks, LANES), F32),
             pltpu.VMEM((n_slab, levp, width), jnp.int32),
             pltpu.VMEM((n_slab // 2, members, levp, width), F32),
             pltpu.VMEM((2, rows, 2 * width), F32),
             pltpu.VMEM((rows, lanes), F32),
-            pltpu.SemaphoreType.DMA((5 + 2 * blocks,)),
+            pltpu.SemaphoreType.DMA((5 + 2 * (profiles // LANES),)),
             pltpu.SemaphoreType.DMA((h_block.shape[0] * halves,)),
         ],
         2 * product,
@@ -661,8 +672,8 @@
         block_col,
         entry_count,
         col_sd,
-        innovation,
-        obs_precision,
+        innovation.reshape(lev * blocks, profiles),
+        obs_precision.reshape(lev * blocks, profiles),
         h_block,
         space=HBM,
         limit=60,

time: 113 us -> 113 us (level)
    ppermute x22, starting transfers between devices: 25 us -> 26.8 us  [along(): return lax.ppermute(x, 'slab', [(s, s ^ 2 * i) for s in range(n_slab)])]
where the time goes in v17:
time: 113 us; the launch traced here: 112 us
  waiting for transfers between devices  53.7 us (48%)
  starting transfers between devices  39.5 us (35%)
  Pallas kernels  14.9 us (13%)
  local copies, waits for them, and re-layouts  2.09 us (2%)
  between operations  1.58 us (1%)
    ppermute x22, waiting for transfers between devices, along(): return lax.ppermute(x, 'slab', [(s, s ^ 2 * i) for s in range(n_slab)])  29.7 us
    ppermute x22, starting transfers between devices, along(): return lax.ppermute(x, 'slab', [(s, s ^ 2 * i) for s in range(n_slab)])  26.8 us
    ppermute x11, waiting for transfers between devices, plane(): return lax.ppermute(x, 'obs', [(o, o ^ i) for o in range(n_obs)])  19.7 us
    pallas_call x23, Pallas kernels, call(): pl.pallas_call(kernel, out_shape=outs, in_specs=[space] * len(args), out_...  14.9 us
    ppermute x11, starting transfers between devices, plane(): return lax.ppermute(x, 'obs', [(o, o ^ i) for o in range(n_obs)])  11.9 us
    ppermute x5, waiting for transfers between devices, swap(): return lax.ppermute(x, 'slab', [(s, s ^ 1) for s in range(n_slab)])  4.24 us
  transfers between devices with their start and end apart: 38, of which 27 were waited for; matrix products, arithmetic and copies ran while one was open for 0% of the time, Pallas kernels for 4%

profile of v17, /device:TPU:0, one launch (start us, length us, event | category | flops | bytes accessed | tf_op | source)
XLA Modules:
  0.0 111.9 jit_solution(15585873579967014878)
XLA Ops:
  1.3 5.5 %shard_map.104 = (bf16[4,4,128,256]{3,2,1,0:T(8,128)(2,1)}, bf16[4,4,128,256]{3,2,1,0:T(8,128)(2,1)}, bf16[304,256]{1,0:T(8,128)(2,1)}, bf16[304,256]{1,0:T(8,128)(2,1)}) custom-call(s32[4]{0:T(128)} %seeds_in.1, s32[1,1,32]{2,1,0:T(1,128)} %ids_in.1, s32[1,1,32]{2,1,0:T(1,128)} %cols_in.1, s32[1,1]{1,0:T(1,128)S(6)} %copy.16.count_in, f32[1,128]{1,0:T(1,128)} %refs_4_.1, ...), custom_call_target="tpu_custom_call" | custom-call | flops 637534208 | bytes 5735188 | tf_op jit(solution)/shard_map/pallas_call | solution.py:23
  7.3 2.1 %collective-permute-start = (bf16[304,256]{1,0:T(8,128)(2,1)}, bf16[304,256]{1,0:T(8,128)(2,1)S(1)}, u32[]{:S(2)}, u32[]{:S(2)}) collective-permute-start(bf16[304,256]{1,0:T(8,128)(2,1)} %get-tuple-element.66.refs_0_), channel_id=1, source_target_pairs={{0,1},{1,0},{2,3},{3,2},{4,5},{5,4},{6,7},{7,6},{8,9},{9,8},{10,11... | collective-permute-start | bytes 466952 | tf_op jit(solution)/shard_map/ppermute | solution.py:565
  9.4 1.5 %collective-permute-start.1 = (bf16[304,256]{1,0:T(8,128)(2,1)}, bf16[304,256]{1,0:T(8,128)(2,1)S(1)}, u32[]{:S(2)}, u32[]{:S(2)}) collective-permute-start(bf16[304,256]{1,0:T(8,128)(2,1)} %get-tuple-element.67.refs_1_), channel_id=1, source_target_pairs={{0,2},{1,3},{2,0},{3,1},{4,6},{5,7},{6,4},{7,5},{8,10},{9,11},{10,... | collective-permute-start | bytes 466952 | tf_op jit(solution)/shard_map/ppermute | solution.py:565
  14.2 1.5 %collective-permute-done.1.two_more = bf16[304,256]{1,0:T(8,128)(2,1)S(1)} collective-permute-done((bf16[304,256]{1,0:T(8,128)(2,1)}, bf16[304,256]{1,0:T(8,128)(2,1)S(1)}, u32[]{:S(2)}, u32[]{:S(2)}) %collective-permute-start.1) | collective-permute-done | bytes 155680 | tf_op jit(solution)/shard_map/ppermute | solution.py:565
  15.8 1.6 %collective-permute-start.2 = (bf16[304,256]{1,0:T(8,128)(2,1)S(1)}, bf16[304,256]{1,0:T(8,128)(2,1)S(1)}, u32[]{:S(2)}, u32[]{:S(2)}) collective-permute-start(bf16[304,256]{1,0:T(8,128)(2,1)S(1)} %get-tuple-element.70.refs_0_), channel_id=1, source_target_pairs={{0,2},{1,3},{2,0},{3,1},{4,6},{5,7},{6,4},{7,5},{8,10},{9,11},{10,... | collective-permute-start | bytes 466952 | tf_op jit(solution)/shard_map/ppermute | solution.py:565
  18.1 3.0 %collective-permute-done.2.refs_1_ = bf16[304,256]{1,0:T(8,128)(2,1)S(1)} collective-permute-done((bf16[304,256]{1,0:T(8,128)(2,1)S(1)}, bf16[304,256]{1,0:T(8,128)(2,1)S(1)}, u32[]{:S(2)}, u32[]{:S(2)}) %collective-permute-start.2) | collective-permute-done | bytes 155680 | tf_op jit(solution)/shard_map/ppermute | solution.py:565
  21.1 1.5 %collective-permute-done.3.refs_3_ = bf16[304,256]{1,0:T(8,128)(2,1)S(1)} collective-permute-done((bf16[304,256]{1,0:T(8,128)(2,1)S(1)}, bf16[304,256]{1,0:T(8,128)(2,1)S(1)}, u32[]{:S(2)}, u32[]{:S(2)}) %collective-permute-start.3) | collective-permute-done | bytes 155680 | tf_op jit(solution)/shard_map/ppermute | solution.py:565
  25.8 1.6 %collective-permute-start.10 = (bf16[144,256]{1,0:T(8,128)(2,1)S(1)}, bf16[144,256]{1,0:T(8,128)(2,1)S(1)}, u32[]{:S(2)}, u32[]{:S(2)}) collective-permute-start(bf16[144,256]{1,0:T(8,128)(2,1)S(1)} %get-tuple-element.88), channel_id=1, source_target_pairs={{0,8},{4,12},{8,0},{12,4},{16,24},{20,28},{24,16},{28,20},{1,9},{5... | collective-permute-start | bytes 221192 | tf_op jit(solution)/shard_map/ppermute | solution.py:562
  27.4 3.1 %collective-permute-start.6 = (bf16[160,256]{1,0:T(8,128)(2,1)S(1)}, bf16[160,256]{1,0:T(8,128)(2,1)S(1)}, u32[]{:S(2)}, u32[]{:S(2)}) collective-permute-start(bf16[160,256]{1,0:T(8,128)(2,1)S(1)} %get-tuple-element.83), channel_id=1, source_target_pairs={{0,16},{4,20},{8,24},{12,28},{16,0},{20,4},{24,8},{28,12},{1,17},{... | collective-permute-start | bytes 245768 | tf_op jit(solution)/shard_map/ppermute | solution.py:562
  31.1 1.5 %collective-permute-start.8 = (bf16[144,256]{1,0:T(8,128)(2,1)S(1)}, bf16[144,256]{1,0:T(8,128)(2,1)S(1)}, u32[]{:S(2)}, u32[]{:S(2)}) collective-permute-start(bf16[144,256]{1,0:T(8,128)(2,1)S(1)} %get-tuple-element.85), channel_id=1, source_target_pairs={{0,8},{4,12},{8,0},{12,4},{16,24},{20,28},{24,16},{28,20},{1,9},{5... | collective-permute-start | bytes 221192 | tf_op jit(solution)/shard_map/ppermute | solution.py:562
  32.6 2.5 %collective-permute-start.11 = (bf16[144,256]{1,0:T(8,128)(2,1)S(1)}, bf16[144,256]{1,0:T(8,128)(2,1)S(1)}, u32[]{:S(2)}, u32[]{:S(2)}) collective-permute-start(bf16[144,256]{1,0:T(8,128)(2,1)S(1)} %shard_map.110), channel_id=1, source_target_pairs={{0,16},{4,20},{8,24},{12,28},{16,0},{20,4},{24,8},{28,12},{1,17},{... | collective-permute-start | bytes 221192 | tf_op jit(solution)/shard_map/ppermute | solution.py:562
  35.3 3.7 %collective-permute-done.8.refs_3_ = bf16[144,256]{1,0:T(8,128)(2,1)S(1)} collective-permute-done((bf16[144,256]{1,0:T(8,128)(2,1)S(1)}, bf16[144,256]{1,0:T(8,128)(2,1)S(1)}, u32[]{:S(2)}, u32[]{:S(2)}) %collective-permute-start.8) | collective-permute-done | bytes 73760 | tf_op jit(solution)/shard_map/ppermute | solution.py:562
  39.0 2.4 %collective-permute-done.11.refs_5_ = bf16[144,256]{1,0:T(8,128)(2,1)S(1)} collective-permute-done((bf16[144,256]{1,0:T(8,128)(2,1)S(1)}, bf16[144,256]{1,0:T(8,128)(2,1)S(1)}, u32[]{:S(2)}, u32[]{:S(2)}) %collective-permute-start.11) | collective-permute-done | bytes 73760 | tf_op jit(solution)/shard_map/ppermute | solution.py:562
  42.1 2.6 %collective-permute-start.13 = (bf16[144,256]{1,0:T(8,128)(2,1)S(1)}, bf16[144,256]{1,0:T(8,128)(2,1)S(1)}, u32[]{:S(2)}, u32[]{:S(2)}) collective-permute-start(bf16[144,256]{1,0:T(8,128)(2,1)S(1)} %get-tuple-element.90), channel_id=1, source_target_pairs={{0,16},{4,20},{8,24},{12,28},{16,0},{20,4},{24,8},{28,12},{1,17},{... | collective-permute-start | bytes 221192 | tf_op jit(solution)/shard_map/ppermute | solution.py:562
  44.7 1.4 %collective-permute-start.16 = (bf16[160,256]{1,0:T(8,128)(2,1)S(1)}, bf16[160,256]{1,0:T(8,128)(2,1)S(1)}, u32[]{:S(2)}, u32[]{:S(2)}) collective-permute-start(bf16[160,256]{1,0:T(8,128)(2,1)S(1)} %get-tuple-element.91), channel_id=1, source_target_pairs={{0,24},{4,28},{8,16},{12,20},{16,8},{20,12},{24,0},{28,4},{1,25},{... | collective-permute-start | bytes 245768 | tf_op jit(solution)/shard_map/ppermute | solution.py:562
  46.2 4.2 %collective-permute-done.13.refs_2_ = bf16[144,256]{1,0:T(8,128)(2,1)S(1)} collective-permute-done((bf16[144,256]{1,0:T(8,128)(2,1)S(1)}, bf16[144,256]{1,0:T(8,128)(2,1)S(1)}, u32[]{:S(2)}, u32[]{:S(2)}) %collective-permute-start.13) | collective-permute-done | bytes 73760 | tf_op jit(solution)/shard_map/ppermute | solution.py:562
  50.4 1.3 %collective-permute-done.16.refs_5_ = bf16[160,256]{1,0:T(8,128)(2,1)S(1)} collective-permute-done((bf16[160,256]{1,0:T(8,128)(2,1)S(1)}, bf16[160,256]{1,0:T(8,128)(2,1)S(1)}, u32[]{:S(2)}, u32[]{:S(2)}) %collective-permute-start.16) | collective-permute-done | bytes 81952 | tf_op jit(solution)/shard_map/ppermute | solution.py:562
  51.7 2.6 %collective-permute-done.14.refs_3_ = bf16[160,256]{1,0:T(8,128)(2,1)S(1)} collective-permute-done((bf16[160,256]{1,0:T(8,128)(2,1)S(1)}, bf16[160,256]{1,0:T(8,128)(2,1)S(1)}, u32[]{:S(2)}, u32[]{:S(2)}) %collective-permute-start.14) | collective-permute-done | bytes 81952 | tf_op jit(solution)/shard_map/ppermute | solution.py:562
  58.2 5.3 %collective-permute-done.18.one_more = bf16[304,256]{1,0:T(8,128)(2,1)S(1)} collective-permute-done((bf16[304,256]{1,0:T(8,128)(2,1)S(1)}, bf16[304,256]{1,0:T(8,128)(2,1)S(1)}, u32[]{:S(2)}, u32[]{:S(2)}) %collective-permute-start.18) | collective-permute-done | bytes 155680 | tf_op jit(solution)/shard_map/ppermute | solution.py:565
  64.3 1.5 %collective-permute-start.21 = (bf16[304,256]{1,0:T(8,128)(2,1)S(1)}, bf16[304,256]{1,0:T(8,128)(2,1)S(1)}, u32[]{:S(2)}, u32[]{:S(2)}) collective-permute-start(bf16[304,256]{1,0:T(8,128)(2,1)S(1)} %get-tuple-element.95.refs_2_), channel_id=1, source_target_pairs={{0,1},{1,0},{2,3},{3,2},{4,5},{5,4},{6,7},{7,6},{8,9},{9,8},{10,11... | collective-permute-start | bytes 466952 | tf_op jit(solution)/shard_map/ppermute | solution.py:565
  65.8 3.4 %collective-permute-done.20.refs_1_ = bf16[304,256]{1,0:T(8,128)(2,1)S(1)} collective-permute-done((bf16[304,256]{1,0:T(8,128)(2,1)S(1)}, bf16[304,256]{1,0:T(8,128)(2,1)S(1)}, u32[]{:S(2)}, u32[]{:S(2)}) %collective-permute-start.20) | collective-permute-done | bytes 155680 | tf_op jit(solution)/shard_map/ppermute | solution.py:565
  73.0 2.9 %collective-permute-start.23 = (bf16[160,256]{1,0:T(8,128)(2,1)S(1)}, bf16[160,256]{1,0:T(8,128)(2,1)S(1)}, u32[]{:S(2)}, u32[]{:S(2)}) collective-permute-start(bf16[160,256]{1,0:T(8,128)(2,1)S(1)} %get-tuple-element.108), channel_id=1, source_target_pairs={{0,16},{4,20},{8,24},{12,28},{16,0},{20,4},{24,8},{28,12},{1,17},{... | collective-permute-start | bytes 245768 | tf_op jit(solution)/shard_map/ppermute | solution.py:562
  75.9 1.4 %collective-permute-start.24 = (bf16[160,256]{1,0:T(8,128)(2,1)S(1)}, bf16[160,256]{1,0:T(8,128)(2,1)S(1)}, u32[]{:S(2)}, u32[]{:S(2)}) collective-permute-start(bf16[160,256]{1,0:T(8,128)(2,1)S(1)} %get-tuple-element.109), channel_id=1, source_target_pairs={{0,24},{4,28},{8,16},{12,20},{16,8},{20,12},{24,0},{28,4},{1,25},{... | collective-permute-start | bytes 245768 | tf_op jit(solution)/shard_map/ppermute | solution.py:562
  77.4 2.0 %collective-permute-start.25 = (bf16[144,256]{1,0:T(8,128)(2,1)S(1)}, bf16[144,256]{1,0:T(8,128)(2,1)S(1)}, u32[]{:S(2)}, u32[]{:S(2)}) collective-permute-start(bf16[144,256]{1,0:T(8,128)(2,1)S(1)} %get-tuple-element.110), channel_id=1, source_target_pairs={{0,8},{4,12},{8,0},{12,4},{16,24},{20,28},{24,16},{28,20},{1,9},{5... | collective-permute-start | bytes 221192 | tf_op jit(solution)/shard_map/ppermute | solution.py:562
  80.5 5.8 %collective-permute-done.25.refs_3_ = bf16[144,256]{1,0:T(8,128)(2,1)S(1)} collective-permute-done((bf16[144,256]{1,0:T(8,128)(2,1)S(1)}, bf16[144,256]{1,0:T(8,128)(2,1)S(1)}, u32[]{:S(2)}, u32[]{:S(2)}) %collective-permute-start.25) | collective-permute-done | bytes 73760 | tf_op jit(solution)/shard_map/ppermute | solution.py:562
  87.7 2.6 %collective-permute-start.30 = (bf16[144,256]{1,0:T(8,128)(2,1)S(1)}, bf16[144,256]{1,0:T(8,128)(2,1)S(1)}, u32[]{:S(2)}, u32[]{:S(2)}) collective-permute-start(bf16[144,256]{1,0:T(8,128)(2,1)S(1)} %get-tuple-element.116), channel_id=1, source_target_pairs={{0,16},{4,20},{8,24},{12,28},{16,0},{20,4},{24,8},{28,12},{1,17},{... | collective-permute-start | bytes 221192 | tf_op jit(solution)/shard_map/ppermute | solution.py:562
  90.3 1.5 %collective-permute-start.33 = (bf16[160,256]{1,0:T(8,128)(2,1)S(1)}, bf16[160,256]{1,0:T(8,128)(2,1)S(1)}, u32[]{:S(2)}, u32[]{:S(2)}) collective-permute-start(bf16[160,256]{1,0:T(8,128)(2,1)S(1)} %get-tuple-element.117), channel_id=1, source_target_pairs={{0,24},{4,28},{8,16},{12,20},{16,8},{20,12},{24,0},{28,4},{1,25},{... | collective-permute-start | bytes 245768 | tf_op jit(solution)/shard_map/ppermute | solution.py:562
  92.0 4.2 %collective-permute-done.30.refs_2_ = bf16[144,256]{1,0:T(8,128)(2,1)S(1)} collective-permute-done((bf16[144,256]{1,0:T(8,128)(2,1)S(1)}, bf16[144,256]{1,0:T(8,128)(2,1)S(1)}, u32[]{:S(2)}, u32[]{:S(2)}) %collective-permute-start.30) | collective-permute-done | bytes 73760 | tf_op jit(solution)/shard_map/ppermute | solution.py:562
  97.8 2.6 %collective-permute-done.31.refs_3_ = bf16[160,256]{1,0:T(8,128)(2,1)S(1)} collective-permute-done((bf16[160,256]{1,0:T(8,128)(2,1)S(1)}, bf16[160,256]{1,0:T(8,128)(2,1)S(1)}, u32[]{:S(2)}, u32[]{:S(2)}) %collective-permute-start.31) | collective-permute-done | bytes 81952 | tf_op jit(solution)/shard_map/ppermute | solution.py:562
  103.4 2.4 %collective-permute-start.35 = (bf16[304,128]{1,0:T(8,128)(2,1)S(1)}, bf16[304,128]{1,0:T(8,128)(2,1)S(1)}, u32[]{:S(2)}, u32[]{:S(2)}) collective-permute-start(bf16[304,128]{1,0:T(8,128)(2,1)S(1)} %get-tuple-element.119), channel_id=1, source_target_pairs={{0,3},{1,2},{2,1},{3,0},{4,7},{5,6},{6,5},{7,4},{8,11},{9,10},{10,... | collective-permute-start | bytes 233480 | tf_op jit(solution)/shard_map/ppermute | solution.py:565
  107.3 1.5 %collective-permute-done.35.refs_1_ = bf16[304,128]{1,0:T(8,128)(2,1)S(1)} collective-permute-done((bf16[304,128]{1,0:T(8,128)(2,1)S(1)}, bf16[304,128]{1,0:T(8,128)(2,1)S(1)}, u32[]{:S(2)}, u32[]{:S(2)}) %collective-permute-start.35) | collective-permute-done | bytes 77856 | tf_op jit(solution)/shard_map/ppermute | solution.py:565
  108.8 1.6 %collective-permute-done.36.refs_2_ = bf16[304,128]{1,0:T(8,128)(2,1)S(1)} collective-permute-done((bf16[304,128]{1,0:T(8,128)(2,1)S(1)}, bf16[304,128]{1,0:T(8,128)(2,1)S(1)}, u32[]{:S(2)}, u32[]{:S(2)}) %collective-permute-start.36) | collective-permute-done | bytes 77856 | tf_op jit(solution)/shard_map/ppermute | solution.py:565
  (86 shorter events, 28.0 us)
Async XLA Ops:
  6.8 18.5 %collective-permute-start.5 = (bf16[4,4,128,256]{3,2,1,0:T(8,128)(2,1)}, bf16[4,4,128,256]{3,2,1,0:T(8,128)(2,1)S(1)}, u32[]{:S(2)}, u32[]{:S(2)}) collective-permute-start(bf16[4,4,128,256]{3,2,1,0:T(8,128)(2,1)} %get-tuple-element.73), channel_id=1, source_target_pairs={{0,4},{4,0},{8,12},{12,8},{16,20},{20,16},{24,28},{28,24},{1,5},{5... | collective-permute-start | bytes 3145736 | tf_op jit(solution)/shard_map/ppermute | solution.py:568
  7.3 6.9 %collective-permute-start = (bf16[304,256]{1,0:T(8,128)(2,1)}, bf16[304,256]{1,0:T(8,128)(2,1)S(1)}, u32[]{:S(2)}, u32[]{:S(2)}) collective-permute-start(bf16[304,256]{1,0:T(8,128)(2,1)} %get-tuple-element.66.refs_0_), channel_id=1, source_target_pairs={{0,1},{1,0},{2,3},{3,2},{4,5},{5,4},{6,7},{7,6},{8,9},{9,8},{10,11... | collective-permute-start | bytes 466952 | tf_op jit(solution)/shard_map/ppermute | solution.py:565
  9.4 6.3 %collective-permute-start.1 = (bf16[304,256]{1,0:T(8,128)(2,1)}, bf16[304,256]{1,0:T(8,128)(2,1)S(1)}, u32[]{:S(2)}, u32[]{:S(2)}) collective-permute-start(bf16[304,256]{1,0:T(8,128)(2,1)} %get-tuple-element.67.refs_1_), channel_id=1, source_target_pairs={{0,2},{1,3},{2,0},{3,1},{4,6},{5,7},{6,4},{7,5},{8,10},{9,11},{10,... | collective-permute-start | bytes 466952 | tf_op jit(solution)/shard_map/ppermute | solution.py:565
  15.8 5.3 %collective-permute-start.2 = (bf16[304,256]{1,0:T(8,128)(2,1)S(1)}, bf16[304,256]{1,0:T(8,128)(2,1)S(1)}, u32[]{:S(2)}, u32[]{:S(2)}) collective-permute-start(bf16[304,256]{1,0:T(8,128)(2,1)S(1)} %get-tuple-element.70.refs_0_), channel_id=1, source_target_pairs={{0,2},{1,3},{2,0},{3,1},{4,6},{5,7},{6,4},{7,5},{8,10},{9,11},{10,... | collective-permute-start | bytes 466952 | tf_op jit(solution)/shard_map/ppermute | solution.py:565
  17.4 5.2 %collective-permute-start.3 = (bf16[304,256]{1,0:T(8,128)(2,1)S(1)}, bf16[304,256]{1,0:T(8,128)(2,1)S(1)}, u32[]{:S(2)}, u32[]{:S(2)}) collective-permute-start(bf16[304,256]{1,0:T(8,128)(2,1)S(1)} %get-tuple-element.71.refs_2_), channel_id=1, source_target_pairs={{0,1},{1,0},{2,3},{3,2},{4,5},{5,4},{6,7},{7,6},{8,9},{9,8},{10,11... | collective-permute-start | bytes 466952 | tf_op jit(solution)/shard_map/ppermute | solution.py:565
  25.8 6.7 %collective-permute-start.10 = (bf16[144,256]{1,0:T(8,128)(2,1)S(1)}, bf16[144,256]{1,0:T(8,128)(2,1)S(1)}, u32[]{:S(2)}, u32[]{:S(2)}) collective-permute-start(bf16[144,256]{1,0:T(8,128)(2,1)S(1)} %get-tuple-element.88), channel_id=1, source_target_pairs={{0,8},{4,12},{8,0},{12,4},{16,24},{20,28},{24,16},{28,20},{1,9},{5... | collective-permute-start | bytes 221192 | tf_op jit(solution)/shard_map/ppermute | solution.py:562
  27.4 11.6 %collective-permute-start.6 = (bf16[160,256]{1,0:T(8,128)(2,1)S(1)}, bf16[160,256]{1,0:T(8,128)(2,1)S(1)}, u32[]{:S(2)}, u32[]{:S(2)}) collective-permute-start(bf16[160,256]{1,0:T(8,128)(2,1)S(1)} %get-tuple-element.83), channel_id=1, source_target_pairs={{0,16},{4,20},{8,24},{12,28},{16,0},{20,4},{24,8},{28,12},{1,17},{... | collective-permute-start | bytes 245768 | tf_op jit(solution)/shard_map/ppermute | solution.py:562
  30.5 8.4 %collective-permute-start.7 = (bf16[160,256]{1,0:T(8,128)(2,1)S(1)}, bf16[160,256]{1,0:T(8,128)(2,1)S(1)}, u32[]{:S(2)}, u32[]{:S(2)}) collective-permute-start(bf16[160,256]{1,0:T(8,128)(2,1)S(1)} %get-tuple-element.84), channel_id=1, source_target_pairs={{0,24},{4,28},{8,16},{12,20},{16,8},{20,12},{24,0},{28,4},{1,25},{... | collective-permute-start | bytes 245768 | tf_op jit(solution)/shard_map/ppermute | solution.py:562
  30.5 8.4 %collective-permute-start.9 = (bf16[160,256]{1,0:T(8,128)(2,1)S(1)}, bf16[160,256]{1,0:T(8,128)(2,1)S(1)}, u32[]{:S(2)}, u32[]{:S(2)}) collective-permute-start(bf16[160,256]{1,0:T(8,128)(2,1)S(1)} %get-tuple-element.86), channel_id=1, source_target_pairs={{0,8},{4,12},{8,0},{12,4},{16,24},{20,28},{24,16},{28,20},{1,9},{5... | collective-permute-start | bytes 245768 | tf_op jit(solution)/shard_map/ppermute | solution.py:562
  31.1 7.9 %collective-permute-start.8 = (bf16[144,256]{1,0:T(8,128)(2,1)S(1)}, bf16[144,256]{1,0:T(8,128)(2,1)S(1)}, u32[]{:S(2)}, u32[]{:S(2)}) collective-permute-start(bf16[144,256]{1,0:T(8,128)(2,1)S(1)} %get-tuple-element.85), channel_id=1, source_target_pairs={{0,8},{4,12},{8,0},{12,4},{16,24},{20,28},{24,16},{28,20},{1,9},{5... | collective-permute-start | bytes 221192 | tf_op jit(solution)/shard_map/ppermute | solution.py:562
  32.6 8.8 %collective-permute-start.11 = (bf16[144,256]{1,0:T(8,128)(2,1)S(1)}, bf16[144,256]{1,0:T(8,128)(2,1)S(1)}, u32[]{:S(2)}, u32[]{:S(2)}) collective-permute-start(bf16[144,256]{1,0:T(8,128)(2,1)S(1)} %shard_map.110), channel_id=1, source_target_pairs={{0,16},{4,20},{8,24},{12,28},{16,0},{20,4},{24,8},{28,12},{1,17},{... | collective-permute-start | bytes 221192 | tf_op jit(solution)/shard_map/ppermute | solution.py:562
  41.6 13.5 %collective-permute-start.12 = (bf16[304,256]{1,0:T(8,128)(2,1)S(1)}, bf16[304,256]{1,0:T(8,128)(2,1)S(1)}, u32[]{:S(2)}, u32[]{:S(2)}) collective-permute-start(bf16[304,256]{1,0:T(8,128)(2,1)S(1)} %get-tuple-element.89.refs_0_), channel_id=1, source_target_pairs={{0,8},{4,12},{8,0},{12,4},{16,24},{20,28},{24,16},{28,20},{1,9},{5... | collective-permute-start | bytes 466952 | tf_op jit(solution)/shard_map/ppermute | solution.py:562
  42.1 8.3 %collective-permute-start.13 = (bf16[144,256]{1,0:T(8,128)(2,1)S(1)}, bf16[144,256]{1,0:T(8,128)(2,1)S(1)}, u32[]{:S(2)}, u32[]{:S(2)}) collective-permute-start(bf16[144,256]{1,0:T(8,128)(2,1)S(1)} %get-tuple-element.90), channel_id=1, source_target_pairs={{0,16},{4,20},{8,24},{12,28},{16,0},{20,4},{24,8},{28,12},{1,17},{... | collective-permute-start | bytes 221192 | tf_op jit(solution)/shard_map/ppermute | solution.py:562
  44.7 7.0 %collective-permute-start.16 = (bf16[160,256]{1,0:T(8,128)(2,1)S(1)}, bf16[160,256]{1,0:T(8,128)(2,1)S(1)}, u32[]{:S(2)}, u32[]{:S(2)}) collective-permute-start(bf16[160,256]{1,0:T(8,128)(2,1)S(1)} %get-tuple-element.91), channel_id=1, source_target_pairs={{0,24},{4,28},{8,16},{12,20},{16,8},{20,12},{24,0},{28,4},{1,25},{... | collective-permute-start | bytes 245768 | tf_op jit(solution)/shard_map/ppermute | solution.py:562
  46.1 8.3 %collective-permute-start.14 = (bf16[160,256]{1,0:T(8,128)(2,1)S(1)}, bf16[160,256]{1,0:T(8,128)(2,1)S(1)}, u32[]{:S(2)}, u32[]{:S(2)}) collective-permute-start(bf16[160,256]{1,0:T(8,128)(2,1)S(1)} %get-tuple-element.91), channel_id=1, source_target_pairs={{0,16},{4,20},{8,24},{12,28},{16,0},{20,4},{24,8},{28,12},{1,17},{... | collective-permute-start | bytes 245768 | tf_op jit(solution)/shard_map/ppermute | solution.py:562
  50.4 4.7 %collective-permute-start.15 = (bf16[144,256]{1,0:T(8,128)(2,1)S(1)}, bf16[144,256]{1,0:T(8,128)(2,1)S(1)}, u32[]{:S(2)}, u32[]{:S(2)}) collective-permute-start(bf16[144,256]{1,0:T(8,128)(2,1)S(1)} %collective-permute-done.13.refs_2_), channel_id=1, source_target_pairs={{0,8},{4,12},{8,0},{12,4},{16,24},{20,28},{24,16},{28,20},{1,9},{5... | collective-permute-start | bytes 221192 | tf_op jit(solution)/shard_map/ppermute | solution.py:562
  57.4 6.1 %collective-permute-start.18 = (bf16[304,256]{1,0:T(8,128)(2,1)S(1)}, bf16[304,256]{1,0:T(8,128)(2,1)S(1)}, u32[]{:S(2)}, u32[]{:S(2)}) collective-permute-start(bf16[304,256]{1,0:T(8,128)(2,1)S(1)} %get-tuple-element.92.one), channel_id=1, source_target_pairs={{0,1},{1,0},{2,3},{3,2},{4,5},{5,4},{6,7},{7,6},{8,9},{9,8},{10,11... | collective-permute-start | bytes 466952 | tf_op jit(solution)/shard_map/ppermute | solution.py:565
  58.0 5.8 %collective-permute-start.19 = (bf16[304,256]{1,0:T(8,128)(2,1)S(1)}, bf16[304,256]{1,0:T(8,128)(2,1)S(1)}, u32[]{:S(2)}, u32[]{:S(2)}) collective-permute-start(bf16[304,256]{1,0:T(8,128)(2,1)S(1)} %get-tuple-element.93.two), channel_id=1, source_target_pairs={{0,2},{1,3},{2,0},{3,1},{4,6},{5,7},{6,4},{7,5},{8,10},{9,11},{10,... | collective-permute-start | bytes 466952 | tf_op jit(solution)/shard_map/ppermute | solution.py:565
  63.9 5.3 %collective-permute-start.20 = (bf16[304,256]{1,0:T(8,128)(2,1)S(1)}, bf16[304,256]{1,0:T(8,128)(2,1)S(1)}, u32[]{:S(2)}, u32[]{:S(2)}) collective-permute-start(bf16[304,256]{1,0:T(8,128)(2,1)S(1)} %get-tuple-element.94.refs_0_), channel_id=1, source_target_pairs={{0,2},{1,3},{2,0},{3,1},{4,6},{5,7},{6,4},{7,5},{8,10},{9,11},{10,... | collective-permute-start | bytes 466952 | tf_op jit(solution)/shard_map/ppermute | solution.py:565
  64.3 5.2 %collective-permute-start.21 = (bf16[304,256]{1,0:T(8,128)(2,1)S(1)}, bf16[304,256]{1,0:T(8,128)(2,1)S(1)}, u32[]{:S(2)}, u32[]{:S(2)}) collective-permute-start(bf16[304,256]{1,0:T(8,128)(2,1)S(1)} %get-tuple-element.95.refs_2_), channel_id=1, source_target_pairs={{0,1},{1,0},{2,3},{3,2},{4,5},{5,4},{6,7},{7,6},{8,9},{9,8},{10,11... | collective-permute-start | bytes 466952 | tf_op jit(solution)/shard_map/ppermute | solution.py:565
  72.9 6.5 %collective-permute-start.27 = (bf16[144,256]{1,0:T(8,128)(2,1)S(1)}, bf16[144,256]{1,0:T(8,128)(2,1)S(1)}, u32[]{:S(2)}, u32[]{:S(2)}) collective-permute-start(bf16[144,256]{1,0:T(8,128)(2,1)S(1)} %get-tuple-element.113), channel_id=1, source_target_pairs={{0,8},{4,12},{8,0},{12,4},{16,24},{20,28},{24,16},{28,20},{1,9},{5... | collective-permute-start | bytes 221192 | tf_op jit(solution)/shard_map/ppermute | solution.py:562
  73.0 13.2 %collective-permute-start.23 = (bf16[160,256]{1,0:T(8,128)(2,1)S(1)}, bf16[160,256]{1,0:T(8,128)(2,1)S(1)}, u32[]{:S(2)}, u32[]{:S(2)}) collective-permute-start(bf16[160,256]{1,0:T(8,128)(2,1)S(1)} %get-tuple-element.108), channel_id=1, source_target_pairs={{0,16},{4,20},{8,24},{12,28},{16,0},{20,4},{24,8},{28,12},{1,17},{... | collective-permute-start | bytes 245768 | tf_op jit(solution)/shard_map/ppermute | solution.py:562
  75.9 10.3 %collective-permute-start.24 = (bf16[160,256]{1,0:T(8,128)(2,1)S(1)}, bf16[160,256]{1,0:T(8,128)(2,1)S(1)}, u32[]{:S(2)}, u32[]{:S(2)}) collective-permute-start(bf16[160,256]{1,0:T(8,128)(2,1)S(1)} %get-tuple-element.109), channel_id=1, source_target_pairs={{0,24},{4,28},{8,16},{12,20},{16,8},{20,12},{24,0},{28,4},{1,25},{... | collective-permute-start | bytes 245768 | tf_op jit(solution)/shard_map/ppermute | solution.py:562
  77.4 8.8 %collective-permute-start.26 = (bf16[160,256]{1,0:T(8,128)(2,1)S(1)}, bf16[160,256]{1,0:T(8,128)(2,1)S(1)}, u32[]{:S(2)}, u32[]{:S(2)}) collective-permute-start(bf16[160,256]{1,0:T(8,128)(2,1)S(1)} %get-tuple-element.111), channel_id=1, source_target_pairs={{0,8},{4,12},{8,0},{12,4},{16,24},{20,28},{24,16},{28,20},{1,9},{5... | collective-permute-start | bytes 245768 | tf_op jit(solution)/shard_map/ppermute | solution.py:562
  77.4 8.8 %collective-permute-start.25 = (bf16[144,256]{1,0:T(8,128)(2,1)S(1)}, bf16[144,256]{1,0:T(8,128)(2,1)S(1)}, u32[]{:S(2)}, u32[]{:S(2)}) collective-permute-start(bf16[144,256]{1,0:T(8,128)(2,1)S(1)} %get-tuple-element.110), channel_id=1, source_target_pairs={{0,8},{4,12},{8,0},{12,4},{16,24},{20,28},{24,16},{28,20},{1,9},{5... | collective-permute-start | bytes 221192 | tf_op jit(solution)/shard_map/ppermute | solution.py:562
  79.4 7.5 %collective-permute-start.28 = (bf16[144,256]{1,0:T(8,128)(2,1)S(1)}, bf16[144,256]{1,0:T(8,128)(2,1)S(1)}, u32[]{:S(2)}, u32[]{:S(2)}) collective-permute-start(bf16[144,256]{1,0:T(8,128)(2,1)S(1)} %shard_map.120), channel_id=1, source_target_pairs={{0,16},{4,20},{8,24},{12,28},{16,0},{20,4},{24,8},{28,12},{1,17},{... | collective-permute-start | bytes 221192 | tf_op jit(solution)/shard_map/ppermute | solution.py:562
  87.3 13.8 %collective-permute-start.29 = (bf16[304,256]{1,0:T(8,128)(2,1)S(1)}, bf16[304,256]{1,0:T(8,128)(2,1)S(1)}, u32[]{:S(2)}, u32[]{:S(2)}) collective-permute-start(bf16[304,256]{1,0:T(8,128)(2,1)S(1)} %get-tuple-element.115.refs_0_), channel_id=1, source_target_pairs={{0,8},{4,12},{8,0},{12,4},{16,24},{20,28},{24,16},{28,20},{1,9},{5... | collective-permute-start | bytes 466952 | tf_op jit(solution)/shard_map/ppermute | solution.py:562
  87.7 8.5 %collective-permute-start.30 = (bf16[144,256]{1,0:T(8,128)(2,1)S(1)}, bf16[144,256]{1,0:T(8,128)(2,1)S(1)}, u32[]{:S(2)}, u32[]{:S(2)}) collective-permute-start(bf16[144,256]{1,0:T(8,128)(2,1)S(1)} %get-tuple-element.116), channel_id=1, source_target_pairs={{0,16},{4,20},{8,24},{12,28},{16,0},{20,4},{24,8},{28,12},{1,17},{... | collective-permute-start | bytes 221192 | tf_op jit(solution)/shard_map/ppermute | solution.py:562
  90.3 7.5 %collective-permute-start.33 = (bf16[160,256]{1,0:T(8,128)(2,1)S(1)}, bf16[160,256]{1,0:T(8,128)(2,1)S(1)}, u32[]{:S(2)}, u32[]{:S(2)}) collective-permute-start(bf16[160,256]{1,0:T(8,128)(2,1)S(1)} %get-tuple-element.117), channel_id=1, source_target_pairs={{0,24},{4,28},{8,16},{12,20},{16,8},{20,12},{24,0},{28,4},{1,25},{... | collective-permute-start | bytes 245768 | tf_op jit(solution)/shard_map/ppermute | solution.py:562
  91.8 8.6 %collective-permute-start.31 = (bf16[160,256]{1,0:T(8,128)(2,1)S(1)}, bf16[160,256]{1,0:T(8,128)(2,1)S(1)}, u32[]{:S(2)}, u32[]{:S(2)}) collective-permute-start(bf16[160,256]{1,0:T(8,128)(2,1)S(1)} %get-tuple-element.117), channel_id=1, source_target_pairs={{0,16},{4,20},{8,24},{12,28},{16,0},{20,4},{24,8},{28,12},{1,17},{... | collective-permute-start | bytes 245768 | tf_op jit(solution)/shard_map/ppermute | solution.py:562
  96.2 4.9 %collective-permute-start.32 = (bf16[144,256]{1,0:T(8,128)(2,1)S(1)}, bf16[144,256]{1,0:T(8,128)(2,1)S(1)}, u32[]{:S(2)}, u32[]{:S(2)}) collective-permute-start(bf16[144,256]{1,0:T(8,128)(2,1)S(1)} %collective-permute-done.30.refs_2_), channel_id=1, source_target_pairs={{0,8},{4,12},{8,0},{12,4},{16,24},{20,28},{24,16},{28,20},{1,9},{5... | collective-permute-start | bytes 221192 | tf_op jit(solution)/shard_map/ppermute | solution.py:562
  103.4 5.4 %collective-permute-start.35 = (bf16[304,128]{1,0:T(8,128)(2,1)S(1)}, bf16[304,128]{1,0:T(8,128)(2,1)S(1)}, u32[]{:S(2)}, u32[]{:S(2)}) collective-permute-start(bf16[304,128]{1,0:T(8,128)(2,1)S(1)} %get-tuple-element.119), channel_id=1, source_target_pairs={{0,3},{1,2},{2,1},{3,0},{4,7},{5,6},{6,5},{7,4},{8,11},{9,10},{10,... | collective-permute-start | bytes 233480 | tf_op jit(solution)/shard_map/ppermute | solution.py:565
  (12 other events, 63.8 us)

commit v18 on v17

--- a/solution.py
+++ b/solution.py
@@ -18,13 +18,13 @@
 NT = (((1,), (1,)), ((), ()))
 
 
-def call(kernel, outs, scratch, flops, *args, space=VMEM, limit=24):
+def call(kernel, outs, scratch, flops, *args, space=VMEM, limit=24, stored=0):
     nbytes = sum(a.size * a.dtype.itemsize for a in (*args, *outs))
     return pl.pallas_call(
         kernel,
         out_shape=outs,
         in_specs=[space] * len(args),
-        out_specs=[VMEM] * len(outs),
+        out_specs=[HBM] * stored + [VMEM] * (len(outs) - stored),
         scratch_shapes=scratch,
         compiler_params=pltpu.CompilerParams(vmem_limit_bytes=limit * 1024 * 1024),
         cost_estimate=pl.CostEstimate(flops=flops, bytes_accessed=nbytes, transcendentals=0),
@@ -117,11 +117,12 @@
 
 
 def start_kernel(
-    dims, seeds_in, ids_in, cols_in, count_in, sd_in, innov_in, prec_in, h, own, partner, *rest
+    dims, seeds_in, ids_in, cols_in, count_in, sd_in, innov_in, prec_in, h, own_out, partner_out, *rest
 ):
     chips, halves, blocks, lev = dims
-    outs = rest[:-13]
-    seeds, ids, cols, count, sd, innov, prec, bases, hashed, scratch, acc, sems, h_sems = rest[-13:]
+    outs = rest[:-15]
+    seeds, ids, cols, count, sd, innov, prec, bases, hashed, scratch, acc = rest[-15:-4]
+    own, partner, sems, h_sems = rest[-4:]
     z, core, obs = place()
     strips = innov.shape[0]
     profiles = strips * LANES
@@ -205,6 +206,12 @@
         return carry
 
     lax.fori_loop(0, count[0, 0], arrive, 0)
+    kept = [
+        pltpu.make_async_copy(x, y, sems.at[len(pairs) + len(large) + i])
+        for i, (x, y) in enumerate(((partner, partner_out), (own, own_out)))
+    ]
+    for copy in kept:
+        copy.start()
 
     for at in range(len(order)):
         source, zz = order[at]
@@ -247,6 +254,8 @@
 
     line = jnp.concatenate([sd[...]] * colblocks, axis=1)
     put_halves(outs, with_columns(acc[...], line, obs, members))
+    for copy in kept:
+        copy.wait()
 
 
 def put_halves(outs, value):
@@ -663,7 +672,9 @@
             pltpu.VMEM((n_slab // 2, members, levp, width), F32),
             pltpu.VMEM((2, rows, 2 * width), F32),
             pltpu.VMEM((rows, lanes), F32),
-            pltpu.SemaphoreType.DMA((5 + 2 * (profiles // LANES),)),
+            pltpu.VMEM(dense.shape, BF16),
+            pltpu.VMEM(dense.shape, BF16),
+            pltpu.SemaphoreType.DMA((7 + 2 * (profiles // LANES),)),
             pltpu.SemaphoreType.DMA((h_block.shape[0] * halves,)),
         ],
         2 * product,
@@ -677,6 +688,7 @@
         h_block,
         space=HBM,
         limit=60,
+        stored=2,
     )
     ps = plane_sum(partials, True)
     partner = swap(for_partner)

time: 113 us -> 114 us (level)
  waiting for transfers between devices: 53.7 us -> 56.7 us
  starting transfers between devices: 39.5 us -> 38.2 us
    ppermute x22, waiting for transfers between devices: 29.7 us -> 33.1 us  [along(): return lax.ppermute(x, 'slab', [(s, s ^ 2 * i) for s in range(n_slab)])]
    ppermute x22, starting transfers between devices: 26.8 us -> 24 us  [along(): return lax.ppermute(x, 'slab', [(s, s ^ 2 * i) for s in range(n_slab)])]
    ppermute x11, starting transfers between devices: 11.9 us -> 13.4 us  [plane(): return lax.ppermute(x, 'obs', [(o, o ^ i) for o in range(n_obs)])]
  transfers between devices with their start and end apart: 38 -> 38, of which waited for: 27 -> 25; matrix products, arithmetic and copies ran while one was open for 0% -> 0% of each run, Pallas kernels for 4% -> 4%
where the time goes in v18:
time: 114 us; the launch traced here: 113 us
  waiting for transfers between devices  56.7 us (50%)
  starting transfers between devices  38.2 us (34%)
  Pallas kernels  14.4 us (13%)
  local copies, waits for them, and re-layouts  2.09 us (2%)
  between operations  1.6 us (1%)
    ppermute x22, waiting for transfers between devices, along(): return lax.ppermute(x, 'slab', [(s, s ^ 2 * i) for s in range(n_slab)])  33.1 us
    ppermute x22, starting transfers between devices, along(): return lax.ppermute(x, 'slab', [(s, s ^ 2 * i) for s in range(n_slab)])  24 us
    ppermute x11, waiting for transfers between devices, plane(): return lax.ppermute(x, 'obs', [(o, o ^ i) for o in range(n_obs)])  19.3 us
    pallas_call x23, Pallas kernels, call(): pl.pallas_call(kernel, out_shape=outs, in_specs=[space] * len(args), out_...  14.4 us
    ppermute x11, starting transfers between devices, plane(): return lax.ppermute(x, 'obs', [(o, o ^ i) for o in range(n_obs)])  13.4 us
    ppermute x5, waiting for transfers between devices, swap(): return lax.ppermute(x, 'slab', [(s, s ^ 1) for s in range(n_slab)])  4.24 us
  transfers between devices with their start and end apart: 38, of which 25 were waited for; matrix products, arithmetic and copies ran while one was open for 0% of the time, Pallas kernels for 4%

profile of v18, /device:TPU:0, one launch (start us, length us, event | category | flops | bytes accessed | tf_op | source)
XLA Modules:
  0.0 113.1 jit_solution(12242244152373477461)
XLA Ops:
  1.3 5.0 %shard_map.104 = (bf16[4,4,128,256]{3,2,1,0:T(8,128)(2,1)}, bf16[4,4,128,256]{3,2,1,0:T(8,128)(2,1)}, bf16[304,256]{1,0:T(8,128)(2,1)}, bf16[304,256]{1,0:T(8,128)(2,1)}) custom-call(s32[4]{0:T(128)} %seeds_in.1, s32[1,1,32]{2,1,0:T(1,128)} %ids_in.1, s32[1,1,32]{2,1,0:T(1,128)} %cols_in.1, s32[1,1]{1,0:T(1,128)S(6)} %copy.16.count_in, f32[1,128]{1,0:T(1,128)} %refs_4_.1, ...), custom_call_target="tpu_custom_call" | custom-call | flops 637534208 | bytes 5735188 | tf_op jit(solution)/shard_map/pallas_call | solution.py:23
  6.8 3.1 %collective-permute-start = (bf16[304,256]{1,0:T(8,128)(2,1)}, bf16[304,256]{1,0:T(8,128)(2,1)S(1)}, u32[]{:S(2)}, u32[]{:S(2)}) collective-permute-start(bf16[304,256]{1,0:T(8,128)(2,1)} %get-tuple-element.66.refs_0_), channel_id=1, source_target_pairs={{0,1},{1,0},{2,3},{3,2},{4,5},{5,4},{6,7},{7,6},{8,9},{9,8},{10,11... | collective-permute-start | bytes 466952 | tf_op jit(solution)/shard_map/ppermute | solution.py:574
  9.9 1.5 %collective-permute-start.1 = (bf16[304,256]{1,0:T(8,128)(2,1)}, bf16[304,256]{1,0:T(8,128)(2,1)S(1)}, u32[]{:S(2)}, u32[]{:S(2)}) collective-permute-start(bf16[304,256]{1,0:T(8,128)(2,1)} %get-tuple-element.67.refs_1_), channel_id=1, source_target_pairs={{0,2},{1,3},{2,0},{3,1},{4,6},{5,7},{6,4},{7,5},{8,10},{9,11},{10,... | collective-permute-start | bytes 466952 | tf_op jit(solution)/shard_map/ppermute | solution.py:574
  14.7 1.5 %collective-permute-done.1.two_more = bf16[304,256]{1,0:T(8,128)(2,1)S(1)} collective-permute-done((bf16[304,256]{1,0:T(8,128)(2,1)}, bf16[304,256]{1,0:T(8,128)(2,1)S(1)}, u32[]{:S(2)}, u32[]{:S(2)}) %collective-permute-start.1) | collective-permute-done | bytes 155680 | tf_op jit(solution)/shard_map/ppermute | solution.py:574
  16.3 1.6 %collective-permute-start.2 = (bf16[304,256]{1,0:T(8,128)(2,1)S(1)}, bf16[304,256]{1,0:T(8,128)(2,1)S(1)}, u32[]{:S(2)}, u32[]{:S(2)}) collective-permute-start(bf16[304,256]{1,0:T(8,128)(2,1)S(1)} %get-tuple-element.70.refs_0_), channel_id=1, source_target_pairs={{0,2},{1,3},{2,0},{3,1},{4,6},{5,7},{6,4},{7,5},{8,10},{9,11},{10,... | collective-permute-start | bytes 466952 | tf_op jit(solution)/shard_map/ppermute | solution.py:574
  18.4 3.2 %collective-permute-done.2.refs_1_ = bf16[304,256]{1,0:T(8,128)(2,1)S(1)} collective-permute-done((bf16[304,256]{1,0:T(8,128)(2,1)S(1)}, bf16[304,256]{1,0:T(8,128)(2,1)S(1)}, u32[]{:S(2)}, u32[]{:S(2)}) %collective-permute-start.2) | collective-permute-done | bytes 155680 | tf_op jit(solution)/shard_map/ppermute | solution.py:574
  21.6 1.5 %collective-permute-done.3.refs_3_ = bf16[304,256]{1,0:T(8,128)(2,1)S(1)} collective-permute-done((bf16[304,256]{1,0:T(8,128)(2,1)S(1)}, bf16[304,256]{1,0:T(8,128)(2,1)S(1)}, u32[]{:S(2)}, u32[]{:S(2)}) %collective-permute-start.3) | collective-permute-done | bytes 155680 | tf_op jit(solution)/shard_map/ppermute | solution.py:574
  26.3 1.6 %collective-permute-start.10 = (bf16[144,256]{1,0:T(8,128)(2,1)S(1)}, bf16[144,256]{1,0:T(8,128)(2,1)S(1)}, u32[]{:S(2)}, u32[]{:S(2)}) collective-permute-start(bf16[144,256]{1,0:T(8,128)(2,1)S(1)} %get-tuple-element.88), channel_id=1, source_target_pairs={{0,8},{4,12},{8,0},{12,4},{16,24},{20,28},{24,16},{28,20},{1,9},{5... | collective-permute-start | bytes 221192 | tf_op jit(solution)/shard_map/ppermute | solution.py:571
  28.0 2.1 %collective-permute-start.6 = (bf16[160,256]{1,0:T(8,128)(2,1)S(1)}, bf16[160,256]{1,0:T(8,128)(2,1)S(1)}, u32[]{:S(2)}, u32[]{:S(2)}) collective-permute-start(bf16[160,256]{1,0:T(8,128)(2,1)S(1)} %get-tuple-element.83), channel_id=1, source_target_pairs={{0,16},{4,20},{8,24},{12,28},{16,0},{20,4},{24,8},{28,12},{1,17},{... | collective-permute-start | bytes 245768 | tf_op jit(solution)/shard_map/ppermute | solution.py:571
  31.5 1.3 %collective-permute-start.8 = (bf16[144,256]{1,0:T(8,128)(2,1)S(1)}, bf16[144,256]{1,0:T(8,128)(2,1)S(1)}, u32[]{:S(2)}, u32[]{:S(2)}) collective-permute-start(bf16[144,256]{1,0:T(8,128)(2,1)S(1)} %get-tuple-element.85), channel_id=1, source_target_pairs={{0,8},{4,12},{8,0},{12,4},{16,24},{20,28},{24,16},{28,20},{1,9},{5... | collective-permute-start | bytes 221192 | tf_op jit(solution)/shard_map/ppermute | solution.py:571
  32.8 1.7 %collective-permute-start.11 = (bf16[144,256]{1,0:T(8,128)(2,1)S(1)}, bf16[144,256]{1,0:T(8,128)(2,1)S(1)}, u32[]{:S(2)}, u32[]{:S(2)}) collective-permute-start(bf16[144,256]{1,0:T(8,128)(2,1)S(1)} %shard_map.110), channel_id=1, source_target_pairs={{0,16},{4,20},{8,24},{12,28},{16,0},{20,4},{24,8},{28,12},{1,17},{... | collective-permute-start | bytes 221192 | tf_op jit(solution)/shard_map/ppermute | solution.py:571
  34.8 4.3 %collective-permute-done.8.refs_3_ = bf16[144,256]{1,0:T(8,128)(2,1)S(1)} collective-permute-done((bf16[144,256]{1,0:T(8,128)(2,1)S(1)}, bf16[144,256]{1,0:T(8,128)(2,1)S(1)}, u32[]{:S(2)}, u32[]{:S(2)}) %collective-permute-start.8) | collective-permute-done | bytes 73760 | tf_op jit(solution)/shard_map/ppermute | solution.py:571
  39.1 2.4 %collective-permute-done.11.refs_5_ = bf16[144,256]{1,0:T(8,128)(2,1)S(1)} collective-permute-done((bf16[144,256]{1,0:T(8,128)(2,1)S(1)}, bf16[144,256]{1,0:T(8,128)(2,1)S(1)}, u32[]{:S(2)}, u32[]{:S(2)}) %collective-permute-start.11) | collective-permute-done | bytes 73760 | tf_op jit(solution)/shard_map/ppermute | solution.py:571
  41.8 2.5 %collective-permute-start.13 = (bf16[144,256]{1,0:T(8,128)(2,1)S(1)}, bf16[144,256]{1,0:T(8,128)(2,1)S(1)}, u32[]{:S(2)}, u32[]{:S(2)}) collective-permute-start(bf16[144,256]{1,0:T(8,128)(2,1)S(1)} %get-tuple-element.90), channel_id=1, source_target_pairs={{0,16},{4,20},{8,24},{12,28},{16,0},{20,4},{24,8},{28,12},{1,17},{... | collective-permute-start | bytes 221192 | tf_op jit(solution)/shard_map/ppermute | solution.py:571
  44.4 1.8 %collective-permute-start.16 = (bf16[160,256]{1,0:T(8,128)(2,1)S(1)}, bf16[160,256]{1,0:T(8,128)(2,1)S(1)}, u32[]{:S(2)}, u32[]{:S(2)}) collective-permute-start(bf16[160,256]{1,0:T(8,128)(2,1)S(1)} %get-tuple-element.91), channel_id=1, source_target_pairs={{0,24},{4,28},{8,16},{12,20},{16,8},{20,12},{24,0},{28,4},{1,25},{... | collective-permute-start | bytes 245768 | tf_op jit(solution)/shard_map/ppermute | solution.py:571
  46.2 5.7 %collective-permute-done.13.refs_2_ = bf16[144,256]{1,0:T(8,128)(2,1)S(1)} collective-permute-done((bf16[144,256]{1,0:T(8,128)(2,1)S(1)}, bf16[144,256]{1,0:T(8,128)(2,1)S(1)}, u32[]{:S(2)}, u32[]{:S(2)}) %collective-permute-start.13) | collective-permute-done | bytes 73760 | tf_op jit(solution)/shard_map/ppermute | solution.py:571
  51.9 3.1 %collective-permute-done.14.refs_3_ = bf16[160,256]{1,0:T(8,128)(2,1)S(1)} collective-permute-done((bf16[160,256]{1,0:T(8,128)(2,1)S(1)}, bf16[160,256]{1,0:T(8,128)(2,1)S(1)}, u32[]{:S(2)}, u32[]{:S(2)}) %collective-permute-start.14) | collective-permute-done | bytes 81952 | tf_op jit(solution)/shard_map/ppermute | solution.py:571
  58.7 1.3 %collective-permute-start.19 = (bf16[304,256]{1,0:T(8,128)(2,1)S(1)}, bf16[304,256]{1,0:T(8,128)(2,1)S(1)}, u32[]{:S(2)}, u32[]{:S(2)}) collective-permute-start(bf16[304,256]{1,0:T(8,128)(2,1)S(1)} %get-tuple-element.93.two), channel_id=1, source_target_pairs={{0,2},{1,3},{2,0},{3,1},{4,6},{5,7},{6,4},{7,5},{8,10},{9,11},{10,... | collective-permute-start | bytes 466952 | tf_op jit(solution)/shard_map/ppermute | solution.py:574
  60.0 4.7 %collective-permute-done.18.one_more = bf16[304,256]{1,0:T(8,128)(2,1)S(1)} collective-permute-done((bf16[304,256]{1,0:T(8,128)(2,1)S(1)}, bf16[304,256]{1,0:T(8,128)(2,1)S(1)}, u32[]{:S(2)}, u32[]{:S(2)}) %collective-permute-start.18) | collective-permute-done | bytes 155680 | tf_op jit(solution)/shard_map/ppermute | solution.py:574
  66.9 3.3 %collective-permute-done.20.refs_1_ = bf16[304,256]{1,0:T(8,128)(2,1)S(1)} collective-permute-done((bf16[304,256]{1,0:T(8,128)(2,1)S(1)}, bf16[304,256]{1,0:T(8,128)(2,1)S(1)}, u32[]{:S(2)}, u32[]{:S(2)}) %collective-permute-start.20) | collective-permute-done | bytes 155680 | tf_op jit(solution)/shard_map/ppermute | solution.py:574
  74.7 2.3 %collective-permute-start.23 = (bf16[160,256]{1,0:T(8,128)(2,1)S(1)}, bf16[160,256]{1,0:T(8,128)(2,1)S(1)}, u32[]{:S(2)}, u32[]{:S(2)}) collective-permute-start(bf16[160,256]{1,0:T(8,128)(2,1)S(1)} %get-tuple-element.108), channel_id=1, source_target_pairs={{0,16},{4,20},{8,24},{12,28},{16,0},{20,4},{24,8},{28,12},{1,17},{... | collective-permute-start | bytes 245768 | tf_op jit(solution)/shard_map/ppermute | solution.py:571
  77.0 2.1 %collective-permute-start.24 = (bf16[160,256]{1,0:T(8,128)(2,1)S(1)}, bf16[160,256]{1,0:T(8,128)(2,1)S(1)}, u32[]{:S(2)}, u32[]{:S(2)}) collective-permute-start(bf16[160,256]{1,0:T(8,128)(2,1)S(1)} %get-tuple-element.109), channel_id=1, source_target_pairs={{0,24},{4,28},{8,16},{12,20},{16,8},{20,12},{24,0},{28,4},{1,25},{... | collective-permute-start | bytes 245768 | tf_op jit(solution)/shard_map/ppermute | solution.py:571
  79.1 2.0 %collective-permute-start.25 = (bf16[144,256]{1,0:T(8,128)(2,1)S(1)}, bf16[144,256]{1,0:T(8,128)(2,1)S(1)}, u32[]{:S(2)}, u32[]{:S(2)}) collective-permute-start(bf16[144,256]{1,0:T(8,128)(2,1)S(1)} %get-tuple-element.110), channel_id=1, source_target_pairs={{0,8},{4,12},{8,0},{12,4},{16,24},{20,28},{24,16},{28,20},{1,9},{5... | collective-permute-start | bytes 221192 | tf_op jit(solution)/shard_map/ppermute | solution.py:571
  81.5 6.4 %collective-permute-done.25.refs_3_ = bf16[144,256]{1,0:T(8,128)(2,1)S(1)} collective-permute-done((bf16[144,256]{1,0:T(8,128)(2,1)S(1)}, bf16[144,256]{1,0:T(8,128)(2,1)S(1)}, u32[]{:S(2)}, u32[]{:S(2)}) %collective-permute-start.25) | collective-permute-done | bytes 73760 | tf_op jit(solution)/shard_map/ppermute | solution.py:571
  89.2 2.1 %collective-permute-start.30 = (bf16[144,256]{1,0:T(8,128)(2,1)S(1)}, bf16[144,256]{1,0:T(8,128)(2,1)S(1)}, u32[]{:S(2)}, u32[]{:S(2)}) collective-permute-start(bf16[144,256]{1,0:T(8,128)(2,1)S(1)} %get-tuple-element.116), channel_id=1, source_target_pairs={{0,16},{4,20},{8,24},{12,28},{16,0},{20,4},{24,8},{28,12},{1,17},{... | collective-permute-start | bytes 221192 | tf_op jit(solution)/shard_map/ppermute | solution.py:571
  91.3 2.1 %collective-permute-start.33 = (bf16[160,256]{1,0:T(8,128)(2,1)S(1)}, bf16[160,256]{1,0:T(8,128)(2,1)S(1)}, u32[]{:S(2)}, u32[]{:S(2)}) collective-permute-start(bf16[160,256]{1,0:T(8,128)(2,1)S(1)} %get-tuple-element.117), channel_id=1, source_target_pairs={{0,24},{4,28},{8,16},{12,20},{16,8},{20,12},{24,0},{28,4},{1,25},{... | collective-permute-start | bytes 245768 | tf_op jit(solution)/shard_map/ppermute | solution.py:571
  93.4 4.9 %collective-permute-done.30.refs_2_ = bf16[144,256]{1,0:T(8,128)(2,1)S(1)} collective-permute-done((bf16[144,256]{1,0:T(8,128)(2,1)S(1)}, bf16[144,256]{1,0:T(8,128)(2,1)S(1)}, u32[]{:S(2)}, u32[]{:S(2)}) %collective-permute-start.30) | collective-permute-done | bytes 73760 | tf_op jit(solution)/shard_map/ppermute | solution.py:571
  98.7 2.8 %collective-permute-done.31.refs_3_ = bf16[160,256]{1,0:T(8,128)(2,1)S(1)} collective-permute-done((bf16[160,256]{1,0:T(8,128)(2,1)S(1)}, bf16[160,256]{1,0:T(8,128)(2,1)S(1)}, u32[]{:S(2)}, u32[]{:S(2)}) %collective-permute-start.31) | collective-permute-done | bytes 81952 | tf_op jit(solution)/shard_map/ppermute | solution.py:571
  105.0 2.0 %collective-permute-start.35 = (bf16[304,128]{1,0:T(8,128)(2,1)S(1)}, bf16[304,128]{1,0:T(8,128)(2,1)S(1)}, u32[]{:S(2)}, u32[]{:S(2)}) collective-permute-start(bf16[304,128]{1,0:T(8,128)(2,1)S(1)} %get-tuple-element.119), channel_id=1, source_target_pairs={{0,3},{1,2},{2,1},{3,0},{4,7},{5,6},{6,5},{7,4},{8,11},{9,10},{10,... | collective-permute-start | bytes 233480 | tf_op jit(solution)/shard_map/ppermute | solution.py:574
  107.3 1.3 %collective-permute-start.37 = (bf16[304,128]{1,0:T(8,128)(2,1)S(1)}, bf16[304,128]{1,0:T(8,128)(2,1)S(1)}, u32[]{:S(2)}, u32[]{:S(2)}) collective-permute-start(bf16[304,128]{1,0:T(8,128)(2,1)S(1)} %get-tuple-element.121), channel_id=1, source_target_pairs={{0,1},{1,0},{2,3},{3,2},{4,5},{5,4},{6,7},{7,6},{8,9},{9,8},{10,11... | collective-permute-start | bytes 233480 | tf_op jit(solution)/shard_map/ppermute | solution.py:574
  108.9 1.6 %collective-permute-done.35.refs_1_ = bf16[304,128]{1,0:T(8,128)(2,1)S(1)} collective-permute-done((bf16[304,128]{1,0:T(8,128)(2,1)S(1)}, bf16[304,128]{1,0:T(8,128)(2,1)S(1)}, u32[]{:S(2)}, u32[]{:S(2)}) %collective-permute-start.35) | collective-permute-done | bytes 77856 | tf_op jit(solution)/shard_map/ppermute | solution.py:574
  110.5 1.6 %collective-permute-done.36.refs_2_ = bf16[304,128]{1,0:T(8,128)(2,1)S(1)} collective-permute-done((bf16[304,128]{1,0:T(8,128)(2,1)S(1)}, bf16[304,128]{1,0:T(8,128)(2,1)S(1)}, u32[]{:S(2)}, u32[]{:S(2)}) %collective-permute-start.36) | collective-permute-done | bytes 77856 | tf_op jit(solution)/shard_map/ppermute | solution.py:574
  (86 shorter events, 27.0 us)
Async XLA Ops:
  6.3 19.5 %collective-permute-start.5 = (bf16[4,4,128,256]{3,2,1,0:T(8,128)(2,1)}, bf16[4,4,128,256]{3,2,1,0:T(8,128)(2,1)S(1)}, u32[]{:S(2)}, u32[]{:S(2)}) collective-permute-start(bf16[4,4,128,256]{3,2,1,0:T(8,128)(2,1)} %get-tuple-element.73), channel_id=1, source_target_pairs={{0,4},{4,0},{8,12},{12,8},{16,20},{20,16},{24,28},{28,24},{1,5},{5... | collective-permute-start | bytes 3145736 | tf_op jit(solution)/shard_map/ppermute | solution.py:577
  6.8 7.9 %collective-permute-start = (bf16[304,256]{1,0:T(8,128)(2,1)}, bf16[304,256]{1,0:T(8,128)(2,1)S(1)}, u32[]{:S(2)}, u32[]{:S(2)}) collective-permute-start(bf16[304,256]{1,0:T(8,128)(2,1)} %get-tuple-element.66.refs_0_), channel_id=1, source_target_pairs={{0,1},{1,0},{2,3},{3,2},{4,5},{5,4},{6,7},{7,6},{8,9},{9,8},{10,11... | collective-permute-start | bytes 466952 | tf_op jit(solution)/shard_map/ppermute | solution.py:574
  9.9 6.3 %collective-permute-start.1 = (bf16[304,256]{1,0:T(8,128)(2,1)}, bf16[304,256]{1,0:T(8,128)(2,1)S(1)}, u32[]{:S(2)}, u32[]{:S(2)}) collective-permute-start(bf16[304,256]{1,0:T(8,128)(2,1)} %get-tuple-element.67.refs_1_), channel_id=1, source_target_pairs={{0,2},{1,3},{2,0},{3,1},{4,6},{5,7},{6,4},{7,5},{8,10},{9,11},{10,... | collective-permute-start | bytes 466952 | tf_op jit(solution)/shard_map/ppermute | solution.py:574
  16.3 5.3 %collective-permute-start.2 = (bf16[304,256]{1,0:T(8,128)(2,1)S(1)}, bf16[304,256]{1,0:T(8,128)(2,1)S(1)}, u32[]{:S(2)}, u32[]{:S(2)}) collective-permute-start(bf16[304,256]{1,0:T(8,128)(2,1)S(1)} %get-tuple-element.70.refs_0_), channel_id=1, source_target_pairs={{0,2},{1,3},{2,0},{3,1},{4,6},{5,7},{6,4},{7,5},{8,10},{9,11},{10,... | collective-permute-start | bytes 466952 | tf_op jit(solution)/shard_map/ppermute | solution.py:574
  17.9 5.2 %collective-permute-start.3 = (bf16[304,256]{1,0:T(8,128)(2,1)S(1)}, bf16[304,256]{1,0:T(8,128)(2,1)S(1)}, u32[]{:S(2)}, u32[]{:S(2)}) collective-permute-start(bf16[304,256]{1,0:T(8,128)(2,1)S(1)} %get-tuple-element.71.refs_2_), channel_id=1, source_target_pairs={{0,1},{1,0},{2,3},{3,2},{4,5},{5,4},{6,7},{7,6},{8,9},{9,8},{10,11... | collective-permute-start | bytes 466952 | tf_op jit(solution)/shard_map/ppermute | solution.py:574
  26.3 6.5 %collective-permute-start.10 = (bf16[144,256]{1,0:T(8,128)(2,1)S(1)}, bf16[144,256]{1,0:T(8,128)(2,1)S(1)}, u32[]{:S(2)}, u32[]{:S(2)}) collective-permute-start(bf16[144,256]{1,0:T(8,128)(2,1)S(1)} %get-tuple-element.88), channel_id=1, source_target_pairs={{0,8},{4,12},{8,0},{12,4},{16,24},{20,28},{24,16},{28,20},{1,9},{5... | collective-permute-start | bytes 221192 | tf_op jit(solution)/shard_map/ppermute | solution.py:571
  28.0 11.1 %collective-permute-start.6 = (bf16[160,256]{1,0:T(8,128)(2,1)S(1)}, bf16[160,256]{1,0:T(8,128)(2,1)S(1)}, u32[]{:S(2)}, u32[]{:S(2)}) collective-permute-start(bf16[160,256]{1,0:T(8,128)(2,1)S(1)} %get-tuple-element.83), channel_id=1, source_target_pairs={{0,16},{4,20},{8,24},{12,28},{16,0},{20,4},{24,8},{28,12},{1,17},{... | collective-permute-start | bytes 245768 | tf_op jit(solution)/shard_map/ppermute | solution.py:571
  30.1 9.0 %collective-permute-start.7 = (bf16[160,256]{1,0:T(8,128)(2,1)S(1)}, bf16[160,256]{1,0:T(8,128)(2,1)S(1)}, u32[]{:S(2)}, u32[]{:S(2)}) collective-permute-start(bf16[160,256]{1,0:T(8,128)(2,1)S(1)} %get-tuple-element.84), channel_id=1, source_target_pairs={{0,24},{4,28},{8,16},{12,20},{16,8},{20,12},{24,0},{28,4},{1,25},{... | collective-permute-start | bytes 245768 | tf_op jit(solution)/shard_map/ppermute | solution.py:571
  30.8 8.3 %collective-permute-start.9 = (bf16[160,256]{1,0:T(8,128)(2,1)S(1)}, bf16[160,256]{1,0:T(8,128)(2,1)S(1)}, u32[]{:S(2)}, u32[]{:S(2)}) collective-permute-start(bf16[160,256]{1,0:T(8,128)(2,1)S(1)} %get-tuple-element.86), channel_id=1, source_target_pairs={{0,8},{4,12},{8,0},{12,4},{16,24},{20,28},{24,16},{28,20},{1,9},{5... | collective-permute-start | bytes 245768 | tf_op jit(solution)/shard_map/ppermute | solution.py:571
  31.5 7.6 %collective-permute-start.8 = (bf16[144,256]{1,0:T(8,128)(2,1)S(1)}, bf16[144,256]{1,0:T(8,128)(2,1)S(1)}, u32[]{:S(2)}, u32[]{:S(2)}) collective-permute-start(bf16[144,256]{1,0:T(8,128)(2,1)S(1)} %get-tuple-element.85), channel_id=1, source_target_pairs={{0,8},{4,12},{8,0},{12,4},{16,24},{20,28},{24,16},{28,20},{1,9},{5... | collective-permute-start | bytes 221192 | tf_op jit(solution)/shard_map/ppermute | solution.py:571
  32.8 8.7 %collective-permute-start.11 = (bf16[144,256]{1,0:T(8,128)(2,1)S(1)}, bf16[144,256]{1,0:T(8,128)(2,1)S(1)}, u32[]{:S(2)}, u32[]{:S(2)}) collective-permute-start(bf16[144,256]{1,0:T(8,128)(2,1)S(1)} %shard_map.110), channel_id=1, source_target_pairs={{0,16},{4,20},{8,24},{12,28},{16,0},{20,4},{24,8},{28,12},{1,17},{... | collective-permute-start | bytes 221192 | tf_op jit(solution)/shard_map/ppermute | solution.py:571
  41.7 14.5 %collective-permute-start.12 = (bf16[304,256]{1,0:T(8,128)(2,1)S(1)}, bf16[304,256]{1,0:T(8,128)(2,1)S(1)}, u32[]{:S(2)}, u32[]{:S(2)}) collective-permute-start(bf16[304,256]{1,0:T(8,128)(2,1)S(1)} %get-tuple-element.89.refs_0_), channel_id=1, source_target_pairs={{0,8},{4,12},{8,0},{12,4},{16,24},{20,28},{24,16},{28,20},{1,9},{5... | collective-permute-start | bytes 466952 | tf_op jit(solution)/shard_map/ppermute | solution.py:571
  41.8 10.1 %collective-permute-start.13 = (bf16[144,256]{1,0:T(8,128)(2,1)S(1)}, bf16[144,256]{1,0:T(8,128)(2,1)S(1)}, u32[]{:S(2)}, u32[]{:S(2)}) collective-permute-start(bf16[144,256]{1,0:T(8,128)(2,1)S(1)} %get-tuple-element.90), channel_id=1, source_target_pairs={{0,16},{4,20},{8,24},{12,28},{16,0},{20,4},{24,8},{28,12},{1,17},{... | collective-permute-start | bytes 221192 | tf_op jit(solution)/shard_map/ppermute | solution.py:571
  44.4 7.6 %collective-permute-start.16 = (bf16[160,256]{1,0:T(8,128)(2,1)S(1)}, bf16[160,256]{1,0:T(8,128)(2,1)S(1)}, u32[]{:S(2)}, u32[]{:S(2)}) collective-permute-start(bf16[160,256]{1,0:T(8,128)(2,1)S(1)} %get-tuple-element.91), channel_id=1, source_target_pairs={{0,24},{4,28},{8,16},{12,20},{16,8},{20,12},{24,0},{28,4},{1,25},{... | collective-permute-start | bytes 245768 | tf_op jit(solution)/shard_map/ppermute | solution.py:571
  46.2 8.8 %collective-permute-start.14 = (bf16[160,256]{1,0:T(8,128)(2,1)S(1)}, bf16[160,256]{1,0:T(8,128)(2,1)S(1)}, u32[]{:S(2)}, u32[]{:S(2)}) collective-permute-start(bf16[160,256]{1,0:T(8,128)(2,1)S(1)} %get-tuple-element.91), channel_id=1, source_target_pairs={{0,16},{4,20},{8,24},{12,28},{16,0},{20,4},{24,8},{28,12},{1,17},{... | collective-permute-start | bytes 245768 | tf_op jit(solution)/shard_map/ppermute | solution.py:571
  58.6 6.1 %collective-permute-start.18 = (bf16[304,256]{1,0:T(8,128)(2,1)S(1)}, bf16[304,256]{1,0:T(8,128)(2,1)S(1)}, u32[]{:S(2)}, u32[]{:S(2)}) collective-permute-start(bf16[304,256]{1,0:T(8,128)(2,1)S(1)} %get-tuple-element.92.one), channel_id=1, source_target_pairs={{0,1},{1,0},{2,3},{3,2},{4,5},{5,4},{6,7},{7,6},{8,9},{9,8},{10,11... | collective-permute-start | bytes 466952 | tf_op jit(solution)/shard_map/ppermute | solution.py:574
  58.7 6.1 %collective-permute-start.19 = (bf16[304,256]{1,0:T(8,128)(2,1)S(1)}, bf16[304,256]{1,0:T(8,128)(2,1)S(1)}, u32[]{:S(2)}, u32[]{:S(2)}) collective-permute-start(bf16[304,256]{1,0:T(8,128)(2,1)S(1)} %get-tuple-element.93.two), channel_id=1, source_target_pairs={{0,2},{1,3},{2,0},{3,1},{4,6},{5,7},{6,4},{7,5},{8,10},{9,11},{10,... | collective-permute-start | bytes 466952 | tf_op jit(solution)/shard_map/ppermute | solution.py:574
  64.9 5.3 %collective-permute-start.20 = (bf16[304,256]{1,0:T(8,128)(2,1)S(1)}, bf16[304,256]{1,0:T(8,128)(2,1)S(1)}, u32[]{:S(2)}, u32[]{:S(2)}) collective-permute-start(bf16[304,256]{1,0:T(8,128)(2,1)S(1)} %get-tuple-element.94.refs_0_), channel_id=1, source_target_pairs={{0,2},{1,3},{2,0},{3,1},{4,6},{5,7},{6,4},{7,5},{8,10},{9,11},{10,... | collective-permute-start | bytes 466952 | tf_op jit(solution)/shard_map/ppermute | solution.py:574
  65.9 5.2 %collective-permute-start.21 = (bf16[304,256]{1,0:T(8,128)(2,1)S(1)}, bf16[304,256]{1,0:T(8,128)(2,1)S(1)}, u32[]{:S(2)}, u32[]{:S(2)}) collective-permute-start(bf16[304,256]{1,0:T(8,128)(2,1)S(1)} %get-tuple-element.95.refs_2_), channel_id=1, source_target_pairs={{0,1},{1,0},{2,3},{3,2},{4,5},{5,4},{6,7},{7,6},{8,9},{9,8},{10,11... | collective-permute-start | bytes 466952 | tf_op jit(solution)/shard_map/ppermute | solution.py:574
  74.6 6.5 %collective-permute-start.27 = (bf16[144,256]{1,0:T(8,128)(2,1)S(1)}, bf16[144,256]{1,0:T(8,128)(2,1)S(1)}, u32[]{:S(2)}, u32[]{:S(2)}) collective-permute-start(bf16[144,256]{1,0:T(8,128)(2,1)S(1)} %get-tuple-element.113), channel_id=1, source_target_pairs={{0,8},{4,12},{8,0},{12,4},{16,24},{20,28},{24,16},{28,20},{1,9},{5... | collective-permute-start | bytes 221192 | tf_op jit(solution)/shard_map/ppermute | solution.py:571
  74.7 13.2 %collective-permute-start.23 = (bf16[160,256]{1,0:T(8,128)(2,1)S(1)}, bf16[160,256]{1,0:T(8,128)(2,1)S(1)}, u32[]{:S(2)}, u32[]{:S(2)}) collective-permute-start(bf16[160,256]{1,0:T(8,128)(2,1)S(1)} %get-tuple-element.108), channel_id=1, source_target_pairs={{0,16},{4,20},{8,24},{12,28},{16,0},{20,4},{24,8},{28,12},{1,17},{... | collective-permute-start | bytes 245768 | tf_op jit(solution)/shard_map/ppermute | solution.py:571
  77.0 10.9 %collective-permute-start.24 = (bf16[160,256]{1,0:T(8,128)(2,1)S(1)}, bf16[160,256]{1,0:T(8,128)(2,1)S(1)}, u32[]{:S(2)}, u32[]{:S(2)}) collective-permute-start(bf16[160,256]{1,0:T(8,128)(2,1)S(1)} %get-tuple-element.109), channel_id=1, source_target_pairs={{0,24},{4,28},{8,16},{12,20},{16,8},{20,12},{24,0},{28,4},{1,25},{... | collective-permute-start | bytes 245768 | tf_op jit(solution)/shard_map/ppermute | solution.py:571
  79.1 8.8 %collective-permute-start.26 = (bf16[160,256]{1,0:T(8,128)(2,1)S(1)}, bf16[160,256]{1,0:T(8,128)(2,1)S(1)}, u32[]{:S(2)}, u32[]{:S(2)}) collective-permute-start(bf16[160,256]{1,0:T(8,128)(2,1)S(1)} %get-tuple-element.111), channel_id=1, source_target_pairs={{0,8},{4,12},{8,0},{12,4},{16,24},{20,28},{24,16},{28,20},{1,9},{5... | collective-permute-start | bytes 245768 | tf_op jit(solution)/shard_map/ppermute | solution.py:571
  79.1 8.8 %collective-permute-start.25 = (bf16[144,256]{1,0:T(8,128)(2,1)S(1)}, bf16[144,256]{1,0:T(8,128)(2,1)S(1)}, u32[]{:S(2)}, u32[]{:S(2)}) collective-permute-start(bf16[144,256]{1,0:T(8,128)(2,1)S(1)} %get-tuple-element.110), channel_id=1, source_target_pairs={{0,8},{4,12},{8,0},{12,4},{16,24},{20,28},{24,16},{28,20},{1,9},{5... | collective-permute-start | bytes 221192 | tf_op jit(solution)/shard_map/ppermute | solution.py:571
  81.1 7.5 %collective-permute-start.28 = (bf16[144,256]{1,0:T(8,128)(2,1)S(1)}, bf16[144,256]{1,0:T(8,128)(2,1)S(1)}, u32[]{:S(2)}, u32[]{:S(2)}) collective-permute-start(bf16[144,256]{1,0:T(8,128)(2,1)S(1)} %shard_map.120), channel_id=1, source_target_pairs={{0,16},{4,20},{8,24},{12,28},{16,0},{20,4},{24,8},{28,12},{1,17},{... | collective-permute-start | bytes 221192 | tf_op jit(solution)/shard_map/ppermute | solution.py:571
  89.0 13.7 %collective-permute-start.29 = (bf16[304,256]{1,0:T(8,128)(2,1)S(1)}, bf16[304,256]{1,0:T(8,128)(2,1)S(1)}, u32[]{:S(2)}, u32[]{:S(2)}) collective-permute-start(bf16[304,256]{1,0:T(8,128)(2,1)S(1)} %get-tuple-element.115.refs_0_), channel_id=1, source_target_pairs={{0,8},{4,12},{8,0},{12,4},{16,24},{20,28},{24,16},{28,20},{1,9},{5... | collective-permute-start | bytes 466952 | tf_op jit(solution)/shard_map/ppermute | solution.py:571
  89.2 9.1 %collective-permute-start.30 = (bf16[144,256]{1,0:T(8,128)(2,1)S(1)}, bf16[144,256]{1,0:T(8,128)(2,1)S(1)}, u32[]{:S(2)}, u32[]{:S(2)}) collective-permute-start(bf16[144,256]{1,0:T(8,128)(2,1)S(1)} %get-tuple-element.116), channel_id=1, source_target_pairs={{0,16},{4,20},{8,24},{12,28},{16,0},{20,4},{24,8},{28,12},{1,17},{... | collective-permute-start | bytes 221192 | tf_op jit(solution)/shard_map/ppermute | solution.py:571
  91.3 7.3 %collective-permute-start.33 = (bf16[160,256]{1,0:T(8,128)(2,1)S(1)}, bf16[160,256]{1,0:T(8,128)(2,1)S(1)}, u32[]{:S(2)}, u32[]{:S(2)}) collective-permute-start(bf16[160,256]{1,0:T(8,128)(2,1)S(1)} %get-tuple-element.117), channel_id=1, source_target_pairs={{0,24},{4,28},{8,16},{12,20},{16,8},{20,12},{24,0},{28,4},{1,25},{... | collective-permute-start | bytes 245768 | tf_op jit(solution)/shard_map/ppermute | solution.py:571
  93.4 8.0 %collective-permute-start.31 = (bf16[160,256]{1,0:T(8,128)(2,1)S(1)}, bf16[160,256]{1,0:T(8,128)(2,1)S(1)}, u32[]{:S(2)}, u32[]{:S(2)}) collective-permute-start(bf16[160,256]{1,0:T(8,128)(2,1)S(1)} %get-tuple-element.117), channel_id=1, source_target_pairs={{0,16},{4,20},{8,24},{12,28},{16,0},{20,4},{24,8},{28,12},{1,17},{... | collective-permute-start | bytes 245768 | tf_op jit(solution)/shard_map/ppermute | solution.py:571
  105.0 5.5 %collective-permute-start.35 = (bf16[304,128]{1,0:T(8,128)(2,1)S(1)}, bf16[304,128]{1,0:T(8,128)(2,1)S(1)}, u32[]{:S(2)}, u32[]{:S(2)}) collective-permute-start(bf16[304,128]{1,0:T(8,128)(2,1)S(1)} %get-tuple-element.119), channel_id=1, source_target_pairs={{0,3},{1,2},{2,1},{3,0},{4,7},{5,6},{6,5},{7,4},{8,11},{9,10},{10,... | collective-permute-start | bytes 233480 | tf_op jit(solution)/shard_map/ppermute | solution.py:574
  107.0 5.0 %collective-permute-start.36 = (bf16[304,128]{1,0:T(8,128)(2,1)S(1)}, bf16[304,128]{1,0:T(8,128)(2,1)S(1)}, u32[]{:S(2)}, u32[]{:S(2)}) collective-permute-start(bf16[304,128]{1,0:T(8,128)(2,1)S(1)} %get-tuple-element.120), channel_id=1, source_target_pairs={{0,2},{1,3},{2,0},{3,1},{4,6},{5,7},{6,4},{7,5},{8,10},{9,11},{10,... | collective-permute-start | bytes 233480 | tf_op jit(solution)/shard_map/ppermute | solution.py:574
  107.3 4.7 %collective-permute-start.37 = (bf16[304,128]{1,0:T(8,128)(2,1)S(1)}, bf16[304,128]{1,0:T(8,128)(2,1)S(1)}, u32[]{:S(2)}, u32[]{:S(2)}) collective-permute-start(bf16[304,128]{1,0:T(8,128)(2,1)S(1)} %get-tuple-element.121), channel_id=1, source_target_pairs={{0,1},{1,0},{2,3},{3,2},{4,5},{5,4},{6,7},{7,6},{8,9},{9,8},{10,11... | collective-permute-start | bytes 233480 | tf_op jit(solution)/shard_map/ppermute | solution.py:574
  (12 other events, 64.0 us)

commit v19 on v18

--- a/solution.py
+++ b/solution.py
@@ -410,10 +410,9 @@
     energies = [[x] for x in member_sums(scaled * y, members, lev)]
     weighted = with_scalars(scaled, energies).astype(BF16)
     first = 0
-    outs[0][...] = weighted
-    for out in outs[1:]:
+    for out in outs:
         out[...] = weighted[first : first + out.shape[0]]
-        first += out.shape[0]
+        first = (first + out.shape[0]) % rows
 
 
 def adjoint_kernel(plan, members, *refs):
@@ -549,7 +548,10 @@
     via = chips == 4
     if via:
         one, two = (0, some), (some, rest)
-        plan = [(0, 0, rows), (1, 0, rows), (2, *one), (2, *two), (3, *one), (3, *two)]
+        most = rows - 32
+        near_parts = [(0, most), (most, rows - most)]
+        plan = [(0, 0, rows), *((1, *part) for part in near_parts)]
+        plan += [(2, *one), (2, *two), (3, *one), (3, *two)]
         sends = [(3, *one), (2, *two), (3, *two), (1, *one), (1, *two), (0, 0, rows), (2, *one)]
     else:
         sends = plan = [(i, 0, rows) for i in range(chips)]
@@ -651,10 +653,10 @@
     def line_gather(w, *parts):
         if not via:
             return [w if i == 0 else along(w, i) for i in range(chips)]
-        some_w, rest_w = parts
+        some_w, rest_w, *near = parts
         far = along(some_w, 2)
-        far_rest, last_rest, next_ = along(rest_w, 2), along(rest_w, 3), along(w, 1)
-        return [w, next_, far, far_rest, along(far, 1), last_rest]
+        far_rest, last_rest = along(rest_w, 2), along(rest_w, 3)
+        return [w, *(along(x, 1) for x in near), far, far_rest, along(far, 1), last_rest]
 
     dense = struct((chips, colblocks, LANES, width), BF16)
     own, for_partner, *partials = call(
@@ -715,7 +717,7 @@
         state, *weighted = call(
             functools.partial(weigh_kernel, later, last, members, lev, spans),
             [struct((members, 8, LANES), F32)]
-            + [struct((n, width), BF16) for n in ((rows, some, rest) if via else (rows,))]
+            + [struct((n, width), BF16) for n in ((rows, some, rest, most, rows - most) if via else (rows,))]
             + ([] if last else [struct((rows, width), F32)]),
             [],
             0,

time: 114 us -> 112 us (0.982)
  waiting for transfers between devices: 56.7 us -> 50.2 us
  starting transfers between devices: 38.2 us -> 42.2 us
    ppermute x22 -> x24, waiting for transfers between devices: 33.1 us -> 26.1 us  [along(): return lax.ppermute(x, 'slab', [(s, s ^ 2 * i) for s in range(n_slab)])]
    ppermute x22 -> x24, starting transfers between devices: 24 us -> 29.3 us  [along(): return lax.ppermute(x, 'slab', [(s, s ^ 2 * i) for s in range(n_slab)])]
  transfers between devices with their start and end apart: 38 -> 40, of which waited for: 25 -> 25; matrix products, arithmetic and copies ran while one was open for 0% -> 0% of each run, Pallas kernels for 4% -> 4%
where the time goes in v19:
time: 112 us; the launch traced here: 111 us
  waiting for transfers between devices  50.2 us (45%)
  starting transfers between devices  42.2 us (38%)
  Pallas kernels  14.9 us (13%)
  local copies, waits for them, and re-layouts  2.09 us (2%)
  between operations  1.58 us (1%)
    ppermute x24, starting transfers between devices, along(): return lax.ppermute(x, 'slab', [(s, s ^ 2 * i) for s in range(n_slab)])  29.3 us
    ppermute x24, waiting for transfers between devices, along(): return lax.ppermute(x, 'slab', [(s, s ^ 2 * i) for s in range(n_slab)])  26.1 us
    ppermute x11, waiting for transfers between devices, plane(): return lax.ppermute(x, 'obs', [(o, o ^ i) for o in range(n_obs)])  19.8 us
    pallas_call x23, Pallas kernels, call(): pl.pallas_call(kernel, out_shape=outs, in_specs=[space] * len(args), out_...  14.9 us
    ppermute x11, starting transfers between devices, plane(): return lax.ppermute(x, 'obs', [(o, o ^ i) for o in range(n_obs)])  12.6 us
    ppermute x5, waiting for transfers between devices, swap(): return lax.ppermute(x, 'slab', [(s, s ^ 1) for s in range(n_slab)])  4.24 us
  transfers between devices with their start and end apart: 40, of which 25 were waited for; matrix products, arithmetic and copies ran while one was open for 0% of the time, Pallas kernels for 4%

profile of v19, /device:TPU:0, one launch (start us, length us, event | category | flops | bytes accessed | tf_op | source)
XLA Modules:
  0.0 111.1 jit_solution(5099109179125437170)
XLA Ops:
  1.3 5.5 %shard_map.104 = (bf16[4,4,128,256]{3,2,1,0:T(8,128)(2,1)}, bf16[4,4,128,256]{3,2,1,0:T(8,128)(2,1)}, bf16[304,256]{1,0:T(8,128)(2,1)}, bf16[304,256]{1,0:T(8,128)(2,1)}) custom-call(s32[4]{0:T(128)} %seeds_in.1, s32[1,1,32]{2,1,0:T(1,128)} %ids_in.1, s32[1,1,32]{2,1,0:T(1,128)} %cols_in.1, s32[1,1]{1,0:T(1,128)S(6)} %copy.16.count_in, f32[1,128]{1,0:T(1,128)} %refs_4_.1, ...), custom_call_target="tpu_custom_call" | custom-call | flops 637534208 | bytes 5735188 | tf_op jit(solution)/shard_map/pallas_call | solution.py:23
  6.9 2.5 %collective-permute-start = (bf16[304,256]{1,0:T(8,128)(2,1)}, bf16[304,256]{1,0:T(8,128)(2,1)S(1)}, u32[]{:S(2)}, u32[]{:S(2)}) collective-permute-start(bf16[304,256]{1,0:T(8,128)(2,1)} %get-tuple-element.70.refs_0_), channel_id=1, source_target_pairs={{0,1},{1,0},{2,3},{3,2},{4,5},{5,4},{6,7},{7,6},{8,9},{9,8},{10,11... | collective-permute-start | bytes 466952 | tf_op jit(solution)/shard_map/ppermute | solution.py:576
  9.4 2.0 %collective-permute-start.1 = (bf16[304,256]{1,0:T(8,128)(2,1)}, bf16[304,256]{1,0:T(8,128)(2,1)S(1)}, u32[]{:S(2)}, u32[]{:S(2)}) collective-permute-start(bf16[304,256]{1,0:T(8,128)(2,1)} %get-tuple-element.71.refs_1_), channel_id=1, source_target_pairs={{0,2},{1,3},{2,0},{3,1},{4,6},{5,7},{6,4},{7,5},{8,10},{9,11},{10,... | collective-permute-start | bytes 466952 | tf_op jit(solution)/shard_map/ppermute | solution.py:576
  14.2 1.7 %collective-permute-done.1.two_more = bf16[304,256]{1,0:T(8,128)(2,1)S(1)} collective-permute-done((bf16[304,256]{1,0:T(8,128)(2,1)}, bf16[304,256]{1,0:T(8,128)(2,1)S(1)}, u32[]{:S(2)}, u32[]{:S(2)}) %collective-permute-start.1) | collective-permute-done | bytes 155680 | tf_op jit(solution)/shard_map/ppermute | solution.py:576
  16.0 1.8 %collective-permute-start.2 = (bf16[304,256]{1,0:T(8,128)(2,1)S(1)}, bf16[304,256]{1,0:T(8,128)(2,1)S(1)}, u32[]{:S(2)}, u32[]{:S(2)}) collective-permute-start(bf16[304,256]{1,0:T(8,128)(2,1)S(1)} %get-tuple-element.74.refs_0_), channel_id=1, source_target_pairs={{0,2},{1,3},{2,0},{3,1},{4,6},{5,7},{6,4},{7,5},{8,10},{9,11},{10,... | collective-permute-start | bytes 466952 | tf_op jit(solution)/shard_map/ppermute | solution.py:576
  18.4 3.3 %collective-permute-done.2.refs_1_ = bf16[304,256]{1,0:T(8,128)(2,1)S(1)} collective-permute-done((bf16[304,256]{1,0:T(8,128)(2,1)S(1)}, bf16[304,256]{1,0:T(8,128)(2,1)S(1)}, u32[]{:S(2)}, u32[]{:S(2)}) %collective-permute-start.2) | collective-permute-done | bytes 155680 | tf_op jit(solution)/shard_map/ppermute | solution.py:576
  21.7 1.4 %collective-permute-done.3.refs_3_ = bf16[304,256]{1,0:T(8,128)(2,1)S(1)} collective-permute-done((bf16[304,256]{1,0:T(8,128)(2,1)S(1)}, bf16[304,256]{1,0:T(8,128)(2,1)S(1)}, u32[]{:S(2)}, u32[]{:S(2)}) %collective-permute-start.3) | collective-permute-done | bytes 155680 | tf_op jit(solution)/shard_map/ppermute | solution.py:576
  26.3 1.6 %collective-permute-start.10 = (bf16[144,256]{1,0:T(8,128)(2,1)S(1)}, bf16[144,256]{1,0:T(8,128)(2,1)S(1)}, u32[]{:S(2)}, u32[]{:S(2)}) collective-permute-start(bf16[144,256]{1,0:T(8,128)(2,1)S(1)} %get-tuple-element.92), channel_id=1, source_target_pairs={{0,8},{4,12},{8,0},{12,4},{16,24},{20,28},{24,16},{28,20},{1,9},{5... | collective-permute-start | bytes 221192 | tf_op jit(solution)/shard_map/ppermute | solution.py:573
  28.0 2.0 %collective-permute-start.6 = (bf16[160,256]{1,0:T(8,128)(2,1)S(1)}, bf16[160,256]{1,0:T(8,128)(2,1)S(1)}, u32[]{:S(2)}, u32[]{:S(2)}) collective-permute-start(bf16[160,256]{1,0:T(8,128)(2,1)S(1)} %get-tuple-element.87), channel_id=1, source_target_pairs={{0,16},{4,20},{8,24},{12,28},{16,0},{20,4},{24,8},{28,12},{1,17},{... | collective-permute-start | bytes 245768 | tf_op jit(solution)/shard_map/ppermute | solution.py:573
  31.5 1.3 %collective-permute-start.8 = (bf16[144,256]{1,0:T(8,128)(2,1)S(1)}, bf16[144,256]{1,0:T(8,128)(2,1)S(1)}, u32[]{:S(2)}, u32[]{:S(2)}) collective-permute-start(bf16[144,256]{1,0:T(8,128)(2,1)S(1)} %get-tuple-element.89), channel_id=1, source_target_pairs={{0,8},{4,12},{8,0},{12,4},{16,24},{20,28},{24,16},{28,20},{1,9},{5... | collective-permute-start | bytes 221192 | tf_op jit(solution)/shard_map/ppermute | solution.py:573
  32.8 1.8 %collective-permute-start.11 = (bf16[144,256]{1,0:T(8,128)(2,1)S(1)}, bf16[144,256]{1,0:T(8,128)(2,1)S(1)}, u32[]{:S(2)}, u32[]{:S(2)}) collective-permute-start(bf16[144,256]{1,0:T(8,128)(2,1)S(1)} %shard_map.110), channel_id=1, source_target_pairs={{0,16},{4,20},{8,24},{12,28},{16,0},{20,4},{24,8},{28,12},{1,17},{... | collective-permute-start | bytes 221192 | tf_op jit(solution)/shard_map/ppermute | solution.py:573
  34.8 4.4 %collective-permute-done.8.refs_3_ = bf16[144,256]{1,0:T(8,128)(2,1)S(1)} collective-permute-done((bf16[144,256]{1,0:T(8,128)(2,1)S(1)}, bf16[144,256]{1,0:T(8,128)(2,1)S(1)}, u32[]{:S(2)}, u32[]{:S(2)}) %collective-permute-start.8) | collective-permute-done | bytes 73760 | tf_op jit(solution)/shard_map/ppermute | solution.py:573
  39.3 2.2 %collective-permute-done.11.refs_5_ = bf16[144,256]{1,0:T(8,128)(2,1)S(1)} collective-permute-done((bf16[144,256]{1,0:T(8,128)(2,1)S(1)}, bf16[144,256]{1,0:T(8,128)(2,1)S(1)}, u32[]{:S(2)}, u32[]{:S(2)}) %collective-permute-start.11) | collective-permute-done | bytes 73760 | tf_op jit(solution)/shard_map/ppermute | solution.py:573
  42.3 2.5 %collective-permute-start.12 = (bf16[272,256]{1,0:T(8,128)(2,1)S(1)}, bf16[272,256]{1,0:T(8,128)(2,1)S(1)}, u32[]{:S(2)}, u32[]{:S(2)}) collective-permute-start(bf16[272,256]{1,0:T(8,128)(2,1)S(1)} %get-tuple-element.94), channel_id=1, source_target_pairs={{0,8},{4,12},{8,0},{12,4},{16,24},{20,28},{24,16},{28,20},{1,9},{5... | collective-permute-start | bytes 417800 | tf_op jit(solution)/shard_map/ppermute | solution.py:573
  44.8 1.3 %collective-permute-start.17 = (bf16[160,256]{1,0:T(8,128)(2,1)S(1)}, bf16[160,256]{1,0:T(8,128)(2,1)S(1)}, u32[]{:S(2)}, u32[]{:S(2)}) collective-permute-start(bf16[160,256]{1,0:T(8,128)(2,1)S(1)} %get-tuple-element.97), channel_id=1, source_target_pairs={{0,24},{4,28},{8,16},{12,20},{16,8},{20,12},{24,0},{28,4},{1,25},{... | collective-permute-start | bytes 245768 | tf_op jit(solution)/shard_map/ppermute | solution.py:573
  46.3 2.5 %collective-permute-done.14.refs_3_ = bf16[144,256]{1,0:T(8,128)(2,1)S(1)} collective-permute-done((bf16[144,256]{1,0:T(8,128)(2,1)S(1)}, bf16[144,256]{1,0:T(8,128)(2,1)S(1)}, u32[]{:S(2)}, u32[]{:S(2)}) %collective-permute-start.14) | collective-permute-done | bytes 73760 | tf_op jit(solution)/shard_map/ppermute | solution.py:573
  49.2 1.6 %collective-permute-start.13 = (bf16[32,256]{1,0:T(8,128)(2,1)S(1)}, bf16[32,256]{1,0:T(8,128)(2,1)S(1)}, u32[]{:S(2)}, u32[]{:S(2)}) collective-permute-start(bf16[32,256]{1,0:T(8,128)(2,1)S(1)} %get-tuple-element.95), channel_id=1, source_target_pairs={{0,8},{4,12},{8,0},{12,4},{16,24},{20,28},{24,16},{28,20},{1,9},{5... | collective-permute-start | bytes 49160 | tf_op jit(solution)/shard_map/ppermute | solution.py:573
  50.8 2.8 %collective-permute-done.13.refs_2_ = bf16[32,256]{1,0:T(8,128)(2,1)S(1)} collective-permute-done((bf16[32,256]{1,0:T(8,128)(2,1)S(1)}, bf16[32,256]{1,0:T(8,128)(2,1)S(1)}, u32[]{:S(2)}, u32[]{:S(2)}) %collective-permute-start.13) | collective-permute-done | bytes 16416 | tf_op jit(solution)/shard_map/ppermute | solution.py:573
  57.4 5.8 %collective-permute-done.19.one_more = bf16[304,256]{1,0:T(8,128)(2,1)S(1)} collective-permute-done((bf16[304,256]{1,0:T(8,128)(2,1)S(1)}, bf16[304,256]{1,0:T(8,128)(2,1)S(1)}, u32[]{:S(2)}, u32[]{:S(2)}) %collective-permute-start.19) | collective-permute-done | bytes 155680 | tf_op jit(solution)/shard_map/ppermute | solution.py:576
  63.7 1.7 %collective-permute-start.22 = (bf16[304,256]{1,0:T(8,128)(2,1)S(1)}, bf16[304,256]{1,0:T(8,128)(2,1)S(1)}, u32[]{:S(2)}, u32[]{:S(2)}) collective-permute-start(bf16[304,256]{1,0:T(8,128)(2,1)S(1)} %get-tuple-element.101.refs_2_), channel_id=1, source_target_pairs={{0,1},{1,0},{2,3},{3,2},{4,5},{5,4},{6,7},{7,6},{8,9},{9,8},{10,11... | collective-permute-start | bytes 466952 | tf_op jit(solution)/shard_map/ppermute | solution.py:576
  65.3 3.3 %collective-permute-done.21.refs_1_ = bf16[304,256]{1,0:T(8,128)(2,1)S(1)} collective-permute-done((bf16[304,256]{1,0:T(8,128)(2,1)S(1)}, bf16[304,256]{1,0:T(8,128)(2,1)S(1)}, u32[]{:S(2)}, u32[]{:S(2)}) %collective-permute-start.21) | collective-permute-done | bytes 155680 | tf_op jit(solution)/shard_map/ppermute | solution.py:576
  73.0 2.3 %collective-permute-start.24 = (bf16[160,256]{1,0:T(8,128)(2,1)S(1)}, bf16[160,256]{1,0:T(8,128)(2,1)S(1)}, u32[]{:S(2)}, u32[]{:S(2)}) collective-permute-start(bf16[160,256]{1,0:T(8,128)(2,1)S(1)} %get-tuple-element.114), channel_id=1, source_target_pairs={{0,16},{4,20},{8,24},{12,28},{16,0},{20,4},{24,8},{28,12},{1,17},{... | collective-permute-start | bytes 245768 | tf_op jit(solution)/shard_map/ppermute | solution.py:573
  75.4 1.4 %collective-permute-start.25 = (bf16[160,256]{1,0:T(8,128)(2,1)S(1)}, bf16[160,256]{1,0:T(8,128)(2,1)S(1)}, u32[]{:S(2)}, u32[]{:S(2)}) collective-permute-start(bf16[160,256]{1,0:T(8,128)(2,1)S(1)} %get-tuple-element.115), channel_id=1, source_target_pairs={{0,24},{4,28},{8,16},{12,20},{16,8},{20,12},{24,0},{28,4},{1,25},{... | collective-permute-start | bytes 245768 | tf_op jit(solution)/shard_map/ppermute | solution.py:573
  76.8 2.0 %collective-permute-start.26 = (bf16[144,256]{1,0:T(8,128)(2,1)S(1)}, bf16[144,256]{1,0:T(8,128)(2,1)S(1)}, u32[]{:S(2)}, u32[]{:S(2)}) collective-permute-start(bf16[144,256]{1,0:T(8,128)(2,1)S(1)} %get-tuple-element.116), channel_id=1, source_target_pairs={{0,8},{4,12},{8,0},{12,4},{16,24},{20,28},{24,16},{28,20},{1,9},{5... | collective-permute-start | bytes 221192 | tf_op jit(solution)/shard_map/ppermute | solution.py:573
  80.0 5.5 %collective-permute-done.26.refs_3_ = bf16[144,256]{1,0:T(8,128)(2,1)S(1)} collective-permute-done((bf16[144,256]{1,0:T(8,128)(2,1)S(1)}, bf16[144,256]{1,0:T(8,128)(2,1)S(1)}, u32[]{:S(2)}, u32[]{:S(2)}) %collective-permute-start.26) | collective-permute-done | bytes 73760 | tf_op jit(solution)/shard_map/ppermute | solution.py:573
  87.9 2.5 %collective-permute-start.30 = (bf16[272,256]{1,0:T(8,128)(2,1)S(1)}, bf16[272,256]{1,0:T(8,128)(2,1)S(1)}, u32[]{:S(2)}, u32[]{:S(2)}) collective-permute-start(bf16[272,256]{1,0:T(8,128)(2,1)S(1)} %get-tuple-element.122), channel_id=1, source_target_pairs={{0,8},{4,12},{8,0},{12,4},{16,24},{20,28},{24,16},{28,20},{1,9},{5... | collective-permute-start | bytes 417800 | tf_op jit(solution)/shard_map/ppermute | solution.py:573
  91.9 2.1 %collective-permute-done.32.refs_3_ = bf16[144,256]{1,0:T(8,128)(2,1)S(1)} collective-permute-done((bf16[144,256]{1,0:T(8,128)(2,1)S(1)}, bf16[144,256]{1,0:T(8,128)(2,1)S(1)}, u32[]{:S(2)}, u32[]{:S(2)}) %collective-permute-start.32) | collective-permute-done | bytes 73760 | tf_op jit(solution)/shard_map/ppermute | solution.py:573
  96.0 2.9 %collective-permute-done.31.refs_2_ = bf16[32,256]{1,0:T(8,128)(2,1)S(1)} collective-permute-done((bf16[32,256]{1,0:T(8,128)(2,1)S(1)}, bf16[32,256]{1,0:T(8,128)(2,1)S(1)}, u32[]{:S(2)}, u32[]{:S(2)}) %collective-permute-start.31) | collective-permute-done | bytes 16416 | tf_op jit(solution)/shard_map/ppermute | solution.py:573
  98.9 1.4 %collective-permute-done.33.refs_4_ = bf16[160,256]{1,0:T(8,128)(2,1)S(1)} collective-permute-done((bf16[160,256]{1,0:T(8,128)(2,1)S(1)}, bf16[160,256]{1,0:T(8,128)(2,1)S(1)}, u32[]{:S(2)}, u32[]{:S(2)}) %collective-permute-start.33) | collective-permute-done | bytes 81952 | tf_op jit(solution)/shard_map/ppermute | solution.py:573
  102.6 2.5 %collective-permute-start.37 = (bf16[304,128]{1,0:T(8,128)(2,1)S(1)}, bf16[304,128]{1,0:T(8,128)(2,1)S(1)}, u32[]{:S(2)}, u32[]{:S(2)}) collective-permute-start(bf16[304,128]{1,0:T(8,128)(2,1)S(1)} %get-tuple-element.127), channel_id=1, source_target_pairs={{0,3},{1,2},{2,1},{3,0},{4,7},{5,6},{6,5},{7,4},{8,11},{9,10},{10,... | collective-permute-start | bytes 233480 | tf_op jit(solution)/shard_map/ppermute | solution.py:576
  106.5 1.5 %collective-permute-done.37.refs_1_ = bf16[304,128]{1,0:T(8,128)(2,1)S(1)} collective-permute-done((bf16[304,128]{1,0:T(8,128)(2,1)S(1)}, bf16[304,128]{1,0:T(8,128)(2,1)S(1)}, u32[]{:S(2)}, u32[]{:S(2)}) %collective-permute-start.37) | collective-permute-done | bytes 77856 | tf_op jit(solution)/shard_map/ppermute | solution.py:576
  108.0 1.6 %collective-permute-done.38.refs_2_ = bf16[304,128]{1,0:T(8,128)(2,1)S(1)} collective-permute-done((bf16[304,128]{1,0:T(8,128)(2,1)S(1)}, bf16[304,128]{1,0:T(8,128)(2,1)S(1)}, u32[]{:S(2)}, u32[]{:S(2)}) %collective-permute-start.38) | collective-permute-done | bytes 77856 | tf_op jit(solution)/shard_map/ppermute | solution.py:576
  (90 shorter events, 30.7 us)
Async XLA Ops:
  6.8 19.0 %collective-permute-start.5 = (bf16[4,4,128,256]{3,2,1,0:T(8,128)(2,1)}, bf16[4,4,128,256]{3,2,1,0:T(8,128)(2,1)S(1)}, u32[]{:S(2)}, u32[]{:S(2)}) collective-permute-start(bf16[4,4,128,256]{3,2,1,0:T(8,128)(2,1)} %get-tuple-element.77), channel_id=1, source_target_pairs={{0,4},{4,0},{8,12},{12,8},{16,20},{20,16},{24,28},{28,24},{1,5},{5... | collective-permute-start | bytes 3145736 | tf_op jit(solution)/shard_map/ppermute | solution.py:579
  6.9 7.3 %collective-permute-start = (bf16[304,256]{1,0:T(8,128)(2,1)}, bf16[304,256]{1,0:T(8,128)(2,1)S(1)}, u32[]{:S(2)}, u32[]{:S(2)}) collective-permute-start(bf16[304,256]{1,0:T(8,128)(2,1)} %get-tuple-element.70.refs_0_), channel_id=1, source_target_pairs={{0,1},{1,0},{2,3},{3,2},{4,5},{5,4},{6,7},{7,6},{8,9},{9,8},{10,11... | collective-permute-start | bytes 466952 | tf_op jit(solution)/shard_map/ppermute | solution.py:576
  9.4 6.6 %collective-permute-start.1 = (bf16[304,256]{1,0:T(8,128)(2,1)}, bf16[304,256]{1,0:T(8,128)(2,1)S(1)}, u32[]{:S(2)}, u32[]{:S(2)}) collective-permute-start(bf16[304,256]{1,0:T(8,128)(2,1)} %get-tuple-element.71.refs_1_), channel_id=1, source_target_pairs={{0,2},{1,3},{2,0},{3,1},{4,6},{5,7},{6,4},{7,5},{8,10},{9,11},{10,... | collective-permute-start | bytes 466952 | tf_op jit(solution)/shard_map/ppermute | solution.py:576
  16.0 5.6 %collective-permute-start.2 = (bf16[304,256]{1,0:T(8,128)(2,1)S(1)}, bf16[304,256]{1,0:T(8,128)(2,1)S(1)}, u32[]{:S(2)}, u32[]{:S(2)}) collective-permute-start(bf16[304,256]{1,0:T(8,128)(2,1)S(1)} %get-tuple-element.74.refs_0_), channel_id=1, source_target_pairs={{0,2},{1,3},{2,0},{3,1},{4,6},{5,7},{6,4},{7,5},{8,10},{9,11},{10,... | collective-permute-start | bytes 466952 | tf_op jit(solution)/shard_map/ppermute | solution.py:576
  17.8 5.2 %collective-permute-start.3 = (bf16[304,256]{1,0:T(8,128)(2,1)S(1)}, bf16[304,256]{1,0:T(8,128)(2,1)S(1)}, u32[]{:S(2)}, u32[]{:S(2)}) collective-permute-start(bf16[304,256]{1,0:T(8,128)(2,1)S(1)} %get-tuple-element.75.refs_2_), channel_id=1, source_target_pairs={{0,1},{1,0},{2,3},{3,2},{4,5},{5,4},{6,7},{7,6},{8,9},{9,8},{10,11... | collective-permute-start | bytes 466952 | tf_op jit(solution)/shard_map/ppermute | solution.py:576
  26.3 6.5 %collective-permute-start.10 = (bf16[144,256]{1,0:T(8,128)(2,1)S(1)}, bf16[144,256]{1,0:T(8,128)(2,1)S(1)}, u32[]{:S(2)}, u32[]{:S(2)}) collective-permute-start(bf16[144,256]{1,0:T(8,128)(2,1)S(1)} %get-tuple-element.92), channel_id=1, source_target_pairs={{0,8},{4,12},{8,0},{12,4},{16,24},{20,28},{24,16},{28,20},{1,9},{5... | collective-permute-start | bytes 221192 | tf_op jit(solution)/shard_map/ppermute | solution.py:573
  28.0 11.3 %collective-permute-start.6 = (bf16[160,256]{1,0:T(8,128)(2,1)S(1)}, bf16[160,256]{1,0:T(8,128)(2,1)S(1)}, u32[]{:S(2)}, u32[]{:S(2)}) collective-permute-start(bf16[160,256]{1,0:T(8,128)(2,1)S(1)} %get-tuple-element.87), channel_id=1, source_target_pairs={{0,16},{4,20},{8,24},{12,28},{16,0},{20,4},{24,8},{28,12},{1,17},{... | collective-permute-start | bytes 245768 | tf_op jit(solution)/shard_map/ppermute | solution.py:573
  30.0 9.3 %collective-permute-start.7 = (bf16[160,256]{1,0:T(8,128)(2,1)S(1)}, bf16[160,256]{1,0:T(8,128)(2,1)S(1)}, u32[]{:S(2)}, u32[]{:S(2)}) collective-permute-start(bf16[160,256]{1,0:T(8,128)(2,1)S(1)} %get-tuple-element.88), channel_id=1, source_target_pairs={{0,24},{4,28},{8,16},{12,20},{16,8},{20,12},{24,0},{28,4},{1,25},{... | collective-permute-start | bytes 245768 | tf_op jit(solution)/shard_map/ppermute | solution.py:573
  30.8 8.5 %collective-permute-start.9 = (bf16[160,256]{1,0:T(8,128)(2,1)S(1)}, bf16[160,256]{1,0:T(8,128)(2,1)S(1)}, u32[]{:S(2)}, u32[]{:S(2)}) collective-permute-start(bf16[160,256]{1,0:T(8,128)(2,1)S(1)} %get-tuple-element.90), channel_id=1, source_target_pairs={{0,8},{4,12},{8,0},{12,4},{16,24},{20,28},{24,16},{28,20},{1,9},{5... | collective-permute-start | bytes 245768 | tf_op jit(solution)/shard_map/ppermute | solution.py:573
  31.5 7.8 %collective-permute-start.8 = (bf16[144,256]{1,0:T(8,128)(2,1)S(1)}, bf16[144,256]{1,0:T(8,128)(2,1)S(1)}, u32[]{:S(2)}, u32[]{:S(2)}) collective-permute-start(bf16[144,256]{1,0:T(8,128)(2,1)S(1)} %get-tuple-element.89), channel_id=1, source_target_pairs={{0,8},{4,12},{8,0},{12,4},{16,24},{20,28},{24,16},{28,20},{1,9},{5... | collective-permute-start | bytes 221192 | tf_op jit(solution)/shard_map/ppermute | solution.py:573
  32.8 8.7 %collective-permute-start.11 = (bf16[144,256]{1,0:T(8,128)(2,1)S(1)}, bf16[144,256]{1,0:T(8,128)(2,1)S(1)}, u32[]{:S(2)}, u32[]{:S(2)}) collective-permute-start(bf16[144,256]{1,0:T(8,128)(2,1)S(1)} %shard_map.110), channel_id=1, source_target_pairs={{0,16},{4,20},{8,24},{12,28},{16,0},{20,4},{24,8},{28,12},{1,17},{... | collective-permute-start | bytes 221192 | tf_op jit(solution)/shard_map/ppermute | solution.py:573
  41.7 7.1 %collective-permute-start.14 = (bf16[144,256]{1,0:T(8,128)(2,1)S(1)}, bf16[144,256]{1,0:T(8,128)(2,1)S(1)}, u32[]{:S(2)}, u32[]{:S(2)}) collective-permute-start(bf16[144,256]{1,0:T(8,128)(2,1)S(1)} %get-tuple-element.96), channel_id=1, source_target_pairs={{0,16},{4,20},{8,24},{12,28},{16,0},{20,4},{24,8},{28,12},{1,17},{... | collective-permute-start | bytes 221192 | tf_op jit(solution)/shard_map/ppermute | solution.py:573
  42.3 12.3 %collective-permute-start.12 = (bf16[272,256]{1,0:T(8,128)(2,1)S(1)}, bf16[272,256]{1,0:T(8,128)(2,1)S(1)}, u32[]{:S(2)}, u32[]{:S(2)}) collective-permute-start(bf16[272,256]{1,0:T(8,128)(2,1)S(1)} %get-tuple-element.94), channel_id=1, source_target_pairs={{0,8},{4,12},{8,0},{12,4},{16,24},{20,28},{24,16},{28,20},{1,9},{5... | collective-permute-start | bytes 417800 | tf_op jit(solution)/shard_map/ppermute | solution.py:573
  44.8 8.8 %collective-permute-start.17 = (bf16[160,256]{1,0:T(8,128)(2,1)S(1)}, bf16[160,256]{1,0:T(8,128)(2,1)S(1)}, u32[]{:S(2)}, u32[]{:S(2)}) collective-permute-start(bf16[160,256]{1,0:T(8,128)(2,1)S(1)} %get-tuple-element.97), channel_id=1, source_target_pairs={{0,24},{4,28},{8,16},{12,20},{16,8},{20,12},{24,0},{28,4},{1,25},{... | collective-permute-start | bytes 245768 | tf_op jit(solution)/shard_map/ppermute | solution.py:573
  46.1 8.5 %collective-permute-start.15 = (bf16[160,256]{1,0:T(8,128)(2,1)S(1)}, bf16[160,256]{1,0:T(8,128)(2,1)S(1)}, u32[]{:S(2)}, u32[]{:S(2)}) collective-permute-start(bf16[160,256]{1,0:T(8,128)(2,1)S(1)} %get-tuple-element.97), channel_id=1, source_target_pairs={{0,16},{4,20},{8,24},{12,28},{16,0},{20,4},{24,8},{28,12},{1,17},{... | collective-permute-start | bytes 245768 | tf_op jit(solution)/shard_map/ppermute | solution.py:573
  48.8 5.9 %collective-permute-start.16 = (bf16[144,256]{1,0:T(8,128)(2,1)S(1)}, bf16[144,256]{1,0:T(8,128)(2,1)S(1)}, u32[]{:S(2)}, u32[]{:S(2)}) collective-permute-start(bf16[144,256]{1,0:T(8,128)(2,1)S(1)} %collective-permute-done.14.refs_3_), channel_id=1, source_target_pairs={{0,8},{4,12},{8,0},{12,4},{16,24},{20,28},{24,16},{28,20},{1,9},{5... | collective-permute-start | bytes 221192 | tf_op jit(solution)/shard_map/ppermute | solution.py:573
  57.0 6.1 %collective-permute-start.19 = (bf16[304,256]{1,0:T(8,128)(2,1)S(1)}, bf16[304,256]{1,0:T(8,128)(2,1)S(1)}, u32[]{:S(2)}, u32[]{:S(2)}) collective-permute-start(bf16[304,256]{1,0:T(8,128)(2,1)S(1)} %get-tuple-element.98.one), channel_id=1, source_target_pairs={{0,1},{1,0},{2,3},{3,2},{4,5},{5,4},{6,7},{7,6},{8,9},{9,8},{10,11... | collective-permute-start | bytes 466952 | tf_op jit(solution)/shard_map/ppermute | solution.py:576
  57.4 5.8 %collective-permute-start.20 = (bf16[304,256]{1,0:T(8,128)(2,1)S(1)}, bf16[304,256]{1,0:T(8,128)(2,1)S(1)}, u32[]{:S(2)}, u32[]{:S(2)}) collective-permute-start(bf16[304,256]{1,0:T(8,128)(2,1)S(1)} %get-tuple-element.99.two), channel_id=1, source_target_pairs={{0,2},{1,3},{2,0},{3,1},{4,6},{5,7},{6,4},{7,5},{8,10},{9,11},{10,... | collective-permute-start | bytes 466952 | tf_op jit(solution)/shard_map/ppermute | solution.py:576
  63.3 5.3 %collective-permute-start.21 = (bf16[304,256]{1,0:T(8,128)(2,1)S(1)}, bf16[304,256]{1,0:T(8,128)(2,1)S(1)}, u32[]{:S(2)}, u32[]{:S(2)}) collective-permute-start(bf16[304,256]{1,0:T(8,128)(2,1)S(1)} %get-tuple-element.100.refs_0_), channel_id=1, source_target_pairs={{0,2},{1,3},{2,0},{3,1},{4,6},{5,7},{6,4},{7,5},{8,10},{9,11},{10,... | collective-permute-start | bytes 466952 | tf_op jit(solution)/shard_map/ppermute | solution.py:576
  63.7 5.2 %collective-permute-start.22 = (bf16[304,256]{1,0:T(8,128)(2,1)S(1)}, bf16[304,256]{1,0:T(8,128)(2,1)S(1)}, u32[]{:S(2)}, u32[]{:S(2)}) collective-permute-start(bf16[304,256]{1,0:T(8,128)(2,1)S(1)} %get-tuple-element.101.refs_2_), channel_id=1, source_target_pairs={{0,1},{1,0},{2,3},{3,2},{4,5},{5,4},{6,7},{7,6},{8,9},{9,8},{10,11... | collective-permute-start | bytes 466952 | tf_op jit(solution)/shard_map/ppermute | solution.py:576
  72.3 6.5 %collective-permute-start.28 = (bf16[144,256]{1,0:T(8,128)(2,1)S(1)}, bf16[144,256]{1,0:T(8,128)(2,1)S(1)}, u32[]{:S(2)}, u32[]{:S(2)}) collective-permute-start(bf16[144,256]{1,0:T(8,128)(2,1)S(1)} %get-tuple-element.119), channel_id=1, source_target_pairs={{0,8},{4,12},{8,0},{12,4},{16,24},{20,28},{24,16},{28,20},{1,9},{5... | collective-permute-start | bytes 221192 | tf_op jit(solution)/shard_map/ppermute | solution.py:573
  73.0 12.4 %collective-permute-start.24 = (bf16[160,256]{1,0:T(8,128)(2,1)S(1)}, bf16[160,256]{1,0:T(8,128)(2,1)S(1)}, u32[]{:S(2)}, u32[]{:S(2)}) collective-permute-start(bf16[160,256]{1,0:T(8,128)(2,1)S(1)} %get-tuple-element.114), channel_id=1, source_target_pairs={{0,16},{4,20},{8,24},{12,28},{16,0},{20,4},{24,8},{28,12},{1,17},{... | collective-permute-start | bytes 245768 | tf_op jit(solution)/shard_map/ppermute | solution.py:573
  75.4 10.1 %collective-permute-start.25 = (bf16[160,256]{1,0:T(8,128)(2,1)S(1)}, bf16[160,256]{1,0:T(8,128)(2,1)S(1)}, u32[]{:S(2)}, u32[]{:S(2)}) collective-permute-start(bf16[160,256]{1,0:T(8,128)(2,1)S(1)} %get-tuple-element.115), channel_id=1, source_target_pairs={{0,24},{4,28},{8,16},{12,20},{16,8},{20,12},{24,0},{28,4},{1,25},{... | collective-permute-start | bytes 245768 | tf_op jit(solution)/shard_map/ppermute | solution.py:573
  76.8 8.7 %collective-permute-start.27 = (bf16[160,256]{1,0:T(8,128)(2,1)S(1)}, bf16[160,256]{1,0:T(8,128)(2,1)S(1)}, u32[]{:S(2)}, u32[]{:S(2)}) collective-permute-start(bf16[160,256]{1,0:T(8,128)(2,1)S(1)} %get-tuple-element.117), channel_id=1, source_target_pairs={{0,8},{4,12},{8,0},{12,4},{16,24},{20,28},{24,16},{28,20},{1,9},{5... | collective-permute-start | bytes 245768 | tf_op jit(solution)/shard_map/ppermute | solution.py:573
  76.8 8.7 %collective-permute-start.26 = (bf16[144,256]{1,0:T(8,128)(2,1)S(1)}, bf16[144,256]{1,0:T(8,128)(2,1)S(1)}, u32[]{:S(2)}, u32[]{:S(2)}) collective-permute-start(bf16[144,256]{1,0:T(8,128)(2,1)S(1)} %get-tuple-element.116), channel_id=1, source_target_pairs={{0,8},{4,12},{8,0},{12,4},{16,24},{20,28},{24,16},{28,20},{1,9},{5... | collective-permute-start | bytes 221192 | tf_op jit(solution)/shard_map/ppermute | solution.py:573
  78.8 7.9 %collective-permute-start.29 = (bf16[144,256]{1,0:T(8,128)(2,1)S(1)}, bf16[144,256]{1,0:T(8,128)(2,1)S(1)}, u32[]{:S(2)}, u32[]{:S(2)}) collective-permute-start(bf16[144,256]{1,0:T(8,128)(2,1)S(1)} %shard_map.120), channel_id=1, source_target_pairs={{0,16},{4,20},{8,24},{12,28},{16,0},{20,4},{24,8},{28,12},{1,17},{... | collective-permute-start | bytes 221192 | tf_op jit(solution)/shard_map/ppermute | solution.py:573
  87.1 6.9 %collective-permute-start.32 = (bf16[144,256]{1,0:T(8,128)(2,1)S(1)}, bf16[144,256]{1,0:T(8,128)(2,1)S(1)}, u32[]{:S(2)}, u32[]{:S(2)}) collective-permute-start(bf16[144,256]{1,0:T(8,128)(2,1)S(1)} %get-tuple-element.124), channel_id=1, source_target_pairs={{0,16},{4,20},{8,24},{12,28},{16,0},{20,4},{24,8},{28,12},{1,17},{... | collective-permute-start | bytes 221192 | tf_op jit(solution)/shard_map/ppermute | solution.py:573
  87.9 12.3 %collective-permute-start.30 = (bf16[272,256]{1,0:T(8,128)(2,1)S(1)}, bf16[272,256]{1,0:T(8,128)(2,1)S(1)}, u32[]{:S(2)}, u32[]{:S(2)}) collective-permute-start(bf16[272,256]{1,0:T(8,128)(2,1)S(1)} %get-tuple-element.122), channel_id=1, source_target_pairs={{0,8},{4,12},{8,0},{12,4},{16,24},{20,28},{24,16},{28,20},{1,9},{5... | collective-permute-start | bytes 417800 | tf_op jit(solution)/shard_map/ppermute | solution.py:573
  90.4 8.4 %collective-permute-start.35 = (bf16[160,256]{1,0:T(8,128)(2,1)S(1)}, bf16[160,256]{1,0:T(8,128)(2,1)S(1)}, u32[]{:S(2)}, u32[]{:S(2)}) collective-permute-start(bf16[160,256]{1,0:T(8,128)(2,1)S(1)} %get-tuple-element.125), channel_id=1, source_target_pairs={{0,24},{4,28},{8,16},{12,20},{16,8},{20,12},{24,0},{28,4},{1,25},{... | collective-permute-start | bytes 245768 | tf_op jit(solution)/shard_map/ppermute | solution.py:573
  91.5 8.7 %collective-permute-start.33 = (bf16[160,256]{1,0:T(8,128)(2,1)S(1)}, bf16[160,256]{1,0:T(8,128)(2,1)S(1)}, u32[]{:S(2)}, u32[]{:S(2)}) collective-permute-start(bf16[160,256]{1,0:T(8,128)(2,1)S(1)} %get-tuple-element.125), channel_id=1, source_target_pairs={{0,16},{4,20},{8,24},{12,28},{16,0},{20,4},{24,8},{28,12},{1,17},{... | collective-permute-start | bytes 245768 | tf_op jit(solution)/shard_map/ppermute | solution.py:573
  94.0 6.3 %collective-permute-start.34 = (bf16[144,256]{1,0:T(8,128)(2,1)S(1)}, bf16[144,256]{1,0:T(8,128)(2,1)S(1)}, u32[]{:S(2)}, u32[]{:S(2)}) collective-permute-start(bf16[144,256]{1,0:T(8,128)(2,1)S(1)} %collective-permute-done.32.refs_3_), channel_id=1, source_target_pairs={{0,8},{4,12},{8,0},{12,4},{16,24},{20,28},{24,16},{28,20},{1,9},{5... | collective-permute-start | bytes 221192 | tf_op jit(solution)/shard_map/ppermute | solution.py:573
  102.6 5.4 %collective-permute-start.37 = (bf16[304,128]{1,0:T(8,128)(2,1)S(1)}, bf16[304,128]{1,0:T(8,128)(2,1)S(1)}, u32[]{:S(2)}, u32[]{:S(2)}) collective-permute-start(bf16[304,128]{1,0:T(8,128)(2,1)S(1)} %get-tuple-element.127), channel_id=1, source_target_pairs={{0,3},{1,2},{2,1},{3,0},{4,7},{5,6},{6,5},{7,4},{8,11},{9,10},{10,... | collective-permute-start | bytes 233480 | tf_op jit(solution)/shard_map/ppermute | solution.py:576
  (14 other events, 72.2 us)

commit v20 on v19

--- a/solution.py
+++ b/solution.py
@@ -552,7 +552,8 @@
         near_parts = [(0, most), (most, rows - most)]
         plan = [(0, 0, rows), *((1, *part) for part in near_parts)]
         plan += [(2, *one), (2, *two), (3, *one), (3, *two)]
-        sends = [(3, *one), (2, *two), (3, *two), (1, *one), (1, *two), (0, 0, rows), (2, *one)]
+        sends = [(3, *one), (2, *two), (3, *two), *((1, *part) for part in near_parts)]
+        sends += [(0, 0, rows), (2, *one)]
     else:
         sends = plan = [(i, 0, rows) for i in range(chips)]
     pad = ((0, levp - lev), (0, levp - lev))
@@ -635,10 +636,10 @@
         )
         if not via:
             return [y if i == 0 else along(y, i) for i, y in enumerate(ys)], [(0, rows)] * chips
-        passed, far_rest, last_rest, next_some, next_rest, near, far = ys
+        passed, far_rest, last_rest, next_most, next_rest, near, far = ys
         passed = along(passed, 1)
         far_rest, last_rest = along(far_rest, 2), along(last_rest, 3)
-        next_some, next_rest = along(next_some, 1), along(next_rest, 1)
+        next_most, next_rest = along(next_most, 1), along(next_rest, 1)
         (far,) = call(
             functools.partial(add_kernel, members, 0),
             [struct((some, width), BF16)],
@@ -647,8 +648,8 @@
             far,
             passed,
         )
-        ys = [near, far_rest, last_rest, next_some, next_rest, along(far, 2)]
-        return ys, [(0, rows), two, two, one, two, one]
+        ys = [near, far_rest, last_rest, next_most, next_rest, along(far, 2)]
+        return ys, [(0, rows), two, two, *near_parts, one]
 
     def line_gather(w, *parts):
         if not via:

time: 112 us -> 112 us (level)
  starting transfers between devices: 42.2 us -> 43.9 us
  waiting for transfers between devices: 50.2 us -> 48.7 us
  transfers between devices with their start and end apart: 40 -> 40, of which waited for: 25 -> 26; matrix products, arithmetic and copies ran while one was open for 0% -> 0% of each run, Pallas kernels for 4% -> 4%
where the time goes in v20:
time: 112 us; the launch traced here: 111 us
  waiting for transfers between devices  48.7 us (43%)
  starting transfers between devices  43.9 us (39%)
  Pallas kernels  15.1 us (13%)
  local copies, waits for them, and re-layouts  2.09 us (2%)
  between operations  1.58 us (1%)
    ppermute x24, starting transfers between devices, along(): return lax.ppermute(x, 'slab', [(s, s ^ 2 * i) for s in range(n_slab)])  30.3 us
    ppermute x24, waiting for transfers between devices, along(): return lax.ppermute(x, 'slab', [(s, s ^ 2 * i) for s in range(n_slab)])  25.3 us
    ppermute x11, waiting for transfers between devices, plane(): return lax.ppermute(x, 'obs', [(o, o ^ i) for o in range(n_obs)])  19.2 us
    pallas_call x23, Pallas kernels, call(): pl.pallas_call(kernel, out_shape=outs, in_specs=[space] * len(args), out_...  15.1 us
    ppermute x11, starting transfers between devices, plane(): return lax.ppermute(x, 'obs', [(o, o ^ i) for o in range(n_obs)])  13.3 us
    ppermute x5, waiting for transfers between devices, swap(): return lax.ppermute(x, 'slab', [(s, s ^ 1) for s in range(n_slab)])  4.18 us
  transfers between devices with their start and end apart: 40, of which 26 were waited for; matrix products, arithmetic and copies ran while one was open for 0% of the time, Pallas kernels for 4%

profile of v20, /device:TPU:0, one launch (start us, length us, event | category | flops | bytes accessed | tf_op | source)
XLA Modules:
  0.0 111.5 jit_solution(11754124098925425470)
XLA Ops:
  1.3 5.5 %shard_map.104 = (bf16[4,4,128,256]{3,2,1,0:T(8,128)(2,1)}, bf16[4,4,128,256]{3,2,1,0:T(8,128)(2,1)}, bf16[304,256]{1,0:T(8,128)(2,1)}, bf16[304,256]{1,0:T(8,128)(2,1)}) custom-call(s32[4]{0:T(128)} %seeds_in.1, s32[1,1,32]{2,1,0:T(1,128)} %ids_in.1, s32[1,1,32]{2,1,0:T(1,128)} %cols_in.1, s32[1,1]{1,0:T(1,128)S(6)} %copy.16.count_in, f32[1,128]{1,0:T(1,128)} %refs_4_.1, ...), custom_call_target="tpu_custom_call" | custom-call | flops 637534208 | bytes 5735188 | tf_op jit(solution)/shard_map/pallas_call | solution.py:23
  6.9 2.5 %collective-permute-start = (bf16[304,256]{1,0:T(8,128)(2,1)}, bf16[304,256]{1,0:T(8,128)(2,1)S(1)}, u32[]{:S(2)}, u32[]{:S(2)}) collective-permute-start(bf16[304,256]{1,0:T(8,128)(2,1)} %get-tuple-element.70.refs_0_), channel_id=1, source_target_pairs={{0,1},{1,0},{2,3},{3,2},{4,5},{5,4},{6,7},{7,6},{8,9},{9,8},{10,11... | collective-permute-start | bytes 466952 | tf_op jit(solution)/shard_map/ppermute | solution.py:577
  9.4 2.0 %collective-permute-start.1 = (bf16[304,256]{1,0:T(8,128)(2,1)}, bf16[304,256]{1,0:T(8,128)(2,1)S(1)}, u32[]{:S(2)}, u32[]{:S(2)}) collective-permute-start(bf16[304,256]{1,0:T(8,128)(2,1)} %get-tuple-element.71.refs_1_), channel_id=1, source_target_pairs={{0,2},{1,3},{2,0},{3,1},{4,6},{5,7},{6,4},{7,5},{8,10},{9,11},{10,... | collective-permute-start | bytes 466952 | tf_op jit(solution)/shard_map/ppermute | solution.py:577
  14.2 1.7 %collective-permute-done.1.two_more = bf16[304,256]{1,0:T(8,128)(2,1)S(1)} collective-permute-done((bf16[304,256]{1,0:T(8,128)(2,1)}, bf16[304,256]{1,0:T(8,128)(2,1)S(1)}, u32[]{:S(2)}, u32[]{:S(2)}) %collective-permute-start.1) | collective-permute-done | bytes 155680 | tf_op jit(solution)/shard_map/ppermute | solution.py:577
  16.0 1.8 %collective-permute-start.2 = (bf16[304,256]{1,0:T(8,128)(2,1)S(1)}, bf16[304,256]{1,0:T(8,128)(2,1)S(1)}, u32[]{:S(2)}, u32[]{:S(2)}) collective-permute-start(bf16[304,256]{1,0:T(8,128)(2,1)S(1)} %get-tuple-element.74.refs_0_), channel_id=1, source_target_pairs={{0,2},{1,3},{2,0},{3,1},{4,6},{5,7},{6,4},{7,5},{8,10},{9,11},{10,... | collective-permute-start | bytes 466952 | tf_op jit(solution)/shard_map/ppermute | solution.py:577
  18.4 3.3 %collective-permute-done.2.refs_1_ = bf16[304,256]{1,0:T(8,128)(2,1)S(1)} collective-permute-done((bf16[304,256]{1,0:T(8,128)(2,1)S(1)}, bf16[304,256]{1,0:T(8,128)(2,1)S(1)}, u32[]{:S(2)}, u32[]{:S(2)}) %collective-permute-start.2) | collective-permute-done | bytes 155680 | tf_op jit(solution)/shard_map/ppermute | solution.py:577
  21.7 1.4 %collective-permute-done.3.refs_3_ = bf16[304,256]{1,0:T(8,128)(2,1)S(1)} collective-permute-done((bf16[304,256]{1,0:T(8,128)(2,1)S(1)}, bf16[304,256]{1,0:T(8,128)(2,1)S(1)}, u32[]{:S(2)}, u32[]{:S(2)}) %collective-permute-start.3) | collective-permute-done | bytes 155680 | tf_op jit(solution)/shard_map/ppermute | solution.py:577
  26.3 1.6 %collective-permute-start.10 = (bf16[144,256]{1,0:T(8,128)(2,1)S(1)}, bf16[144,256]{1,0:T(8,128)(2,1)S(1)}, u32[]{:S(2)}, u32[]{:S(2)}) collective-permute-start(bf16[144,256]{1,0:T(8,128)(2,1)S(1)} %get-tuple-element.92), channel_id=1, source_target_pairs={{0,8},{4,12},{8,0},{12,4},{16,24},{20,28},{24,16},{28,20},{1,9},{5... | collective-permute-start | bytes 221192 | tf_op jit(solution)/shard_map/ppermute | solution.py:574
  28.4 2.6 %collective-permute-start.6 = (bf16[160,256]{1,0:T(8,128)(2,1)S(1)}, bf16[160,256]{1,0:T(8,128)(2,1)S(1)}, u32[]{:S(2)}, u32[]{:S(2)}) collective-permute-start(bf16[160,256]{1,0:T(8,128)(2,1)S(1)} %get-tuple-element.87), channel_id=1, source_target_pairs={{0,16},{4,20},{8,24},{12,28},{16,0},{20,4},{24,8},{28,12},{1,17},{... | collective-permute-start | bytes 245768 | tf_op jit(solution)/shard_map/ppermute | solution.py:574
  32.4 1.8 %collective-permute-start.11 = (bf16[144,256]{1,0:T(8,128)(2,1)S(1)}, bf16[144,256]{1,0:T(8,128)(2,1)S(1)}, u32[]{:S(2)}, u32[]{:S(2)}) collective-permute-start(bf16[144,256]{1,0:T(8,128)(2,1)S(1)} %shard_map.110), channel_id=1, source_target_pairs={{0,16},{4,20},{8,24},{12,28},{16,0},{20,4},{24,8},{28,12},{1,17},{... | collective-permute-start | bytes 221192 | tf_op jit(solution)/shard_map/ppermute | solution.py:574
  35.7 2.5 %collective-permute-done.9.refs_4_ = bf16[32,256]{1,0:T(8,128)(2,1)S(1)} collective-permute-done((bf16[32,256]{1,0:T(8,128)(2,1)S(1)}, bf16[32,256]{1,0:T(8,128)(2,1)S(1)}, u32[]{:S(2)}, u32[]{:S(2)}) %collective-permute-start.9) | collective-permute-done | bytes 16416 | tf_op jit(solution)/shard_map/ppermute | solution.py:574
  38.3 1.8 %collective-permute-done.7.refs_2_ = bf16[160,256]{1,0:T(8,128)(2,1)S(1)} collective-permute-done((bf16[160,256]{1,0:T(8,128)(2,1)S(1)}, bf16[160,256]{1,0:T(8,128)(2,1)S(1)}, u32[]{:S(2)}, u32[]{:S(2)}) %collective-permute-start.7) | collective-permute-done | bytes 81952 | tf_op jit(solution)/shard_map/ppermute | solution.py:574
  40.1 2.4 %collective-permute-done.11.refs_5_ = bf16[144,256]{1,0:T(8,128)(2,1)S(1)} collective-permute-done((bf16[144,256]{1,0:T(8,128)(2,1)S(1)}, bf16[144,256]{1,0:T(8,128)(2,1)S(1)}, u32[]{:S(2)}, u32[]{:S(2)}) %collective-permute-start.11) | collective-permute-done | bytes 73760 | tf_op jit(solution)/shard_map/ppermute | solution.py:574
  43.3 2.2 %collective-permute-start.12 = (bf16[272,256]{1,0:T(8,128)(2,1)S(1)}, bf16[272,256]{1,0:T(8,128)(2,1)S(1)}, u32[]{:S(2)}, u32[]{:S(2)}) collective-permute-start(bf16[272,256]{1,0:T(8,128)(2,1)S(1)} %get-tuple-element.94), channel_id=1, source_target_pairs={{0,8},{4,12},{8,0},{12,4},{16,24},{20,28},{24,16},{28,20},{1,9},{5... | collective-permute-start | bytes 417800 | tf_op jit(solution)/shard_map/ppermute | solution.py:574
  45.6 1.6 %collective-permute-start.17 = (bf16[160,256]{1,0:T(8,128)(2,1)S(1)}, bf16[160,256]{1,0:T(8,128)(2,1)S(1)}, u32[]{:S(2)}, u32[]{:S(2)}) collective-permute-start(bf16[160,256]{1,0:T(8,128)(2,1)S(1)} %get-tuple-element.97), channel_id=1, source_target_pairs={{0,24},{4,28},{8,16},{12,20},{16,8},{20,12},{24,0},{28,4},{1,25},{... | collective-permute-start | bytes 245768 | tf_op jit(solution)/shard_map/ppermute | solution.py:574
  47.1 1.5 %collective-permute-done.14.refs_3_ = bf16[144,256]{1,0:T(8,128)(2,1)S(1)} collective-permute-done((bf16[144,256]{1,0:T(8,128)(2,1)S(1)}, bf16[144,256]{1,0:T(8,128)(2,1)S(1)}, u32[]{:S(2)}, u32[]{:S(2)}) %collective-permute-start.14) | collective-permute-done | bytes 73760 | tf_op jit(solution)/shard_map/ppermute | solution.py:574
  50.7 4.2 %collective-permute-done.13.refs_2_ = bf16[32,256]{1,0:T(8,128)(2,1)S(1)} collective-permute-done((bf16[32,256]{1,0:T(8,128)(2,1)S(1)}, bf16[32,256]{1,0:T(8,128)(2,1)S(1)}, u32[]{:S(2)}, u32[]{:S(2)}) %collective-permute-start.13) | collective-permute-done | bytes 16416 | tf_op jit(solution)/shard_map/ppermute | solution.py:574
  58.3 5.0 %collective-permute-done.19.one_more = bf16[304,256]{1,0:T(8,128)(2,1)S(1)} collective-permute-done((bf16[304,256]{1,0:T(8,128)(2,1)S(1)}, bf16[304,256]{1,0:T(8,128)(2,1)S(1)}, u32[]{:S(2)}, u32[]{:S(2)}) %collective-permute-start.19) | collective-permute-done | bytes 155680 | tf_op jit(solution)/shard_map/ppermute | solution.py:577
  64.3 1.5 %collective-permute-start.22 = (bf16[304,256]{1,0:T(8,128)(2,1)S(1)}, bf16[304,256]{1,0:T(8,128)(2,1)S(1)}, u32[]{:S(2)}, u32[]{:S(2)}) collective-permute-start(bf16[304,256]{1,0:T(8,128)(2,1)S(1)} %get-tuple-element.101.refs_2_), channel_id=1, source_target_pairs={{0,1},{1,0},{2,3},{3,2},{4,5},{5,4},{6,7},{7,6},{8,9},{9,8},{10,11... | collective-permute-start | bytes 466952 | tf_op jit(solution)/shard_map/ppermute | solution.py:577
  65.8 3.3 %collective-permute-done.21.refs_1_ = bf16[304,256]{1,0:T(8,128)(2,1)S(1)} collective-permute-done((bf16[304,256]{1,0:T(8,128)(2,1)S(1)}, bf16[304,256]{1,0:T(8,128)(2,1)S(1)}, u32[]{:S(2)}, u32[]{:S(2)}) %collective-permute-start.21) | collective-permute-done | bytes 155680 | tf_op jit(solution)/shard_map/ppermute | solution.py:577
  75.1 1.7 %collective-permute-start.24 = (bf16[160,256]{1,0:T(8,128)(2,1)S(1)}, bf16[160,256]{1,0:T(8,128)(2,1)S(1)}, u32[]{:S(2)}, u32[]{:S(2)}) collective-permute-start(bf16[160,256]{1,0:T(8,128)(2,1)S(1)} %get-tuple-element.114), channel_id=1, source_target_pairs={{0,16},{4,20},{8,24},{12,28},{16,0},{20,4},{24,8},{28,12},{1,17},{... | collective-permute-start | bytes 245768 | tf_op jit(solution)/shard_map/ppermute | solution.py:574
  76.7 1.4 %collective-permute-start.25 = (bf16[160,256]{1,0:T(8,128)(2,1)S(1)}, bf16[160,256]{1,0:T(8,128)(2,1)S(1)}, u32[]{:S(2)}, u32[]{:S(2)}) collective-permute-start(bf16[160,256]{1,0:T(8,128)(2,1)S(1)} %get-tuple-element.115), channel_id=1, source_target_pairs={{0,24},{4,28},{8,16},{12,20},{16,8},{20,12},{24,0},{28,4},{1,25},{... | collective-permute-start | bytes 245768 | tf_op jit(solution)/shard_map/ppermute | solution.py:574
  78.2 1.6 %collective-permute-start.29 = (bf16[144,256]{1,0:T(8,128)(2,1)S(1)}, bf16[144,256]{1,0:T(8,128)(2,1)S(1)}, u32[]{:S(2)}, u32[]{:S(2)}) collective-permute-start(bf16[144,256]{1,0:T(8,128)(2,1)S(1)} %shard_map.120), channel_id=1, source_target_pairs={{0,16},{4,20},{8,24},{12,28},{16,0},{20,4},{24,8},{28,12},{1,17},{... | collective-permute-start | bytes 221192 | tf_op jit(solution)/shard_map/ppermute | solution.py:574
  81.2 2.9 %collective-permute-done.27.refs_4_ = bf16[32,256]{1,0:T(8,128)(2,1)S(1)} collective-permute-done((bf16[32,256]{1,0:T(8,128)(2,1)S(1)}, bf16[32,256]{1,0:T(8,128)(2,1)S(1)}, u32[]{:S(2)}, u32[]{:S(2)}) %collective-permute-start.27) | collective-permute-done | bytes 16416 | tf_op jit(solution)/shard_map/ppermute | solution.py:574
  84.1 1.7 %collective-permute-done.25.refs_2_ = bf16[160,256]{1,0:T(8,128)(2,1)S(1)} collective-permute-done((bf16[160,256]{1,0:T(8,128)(2,1)S(1)}, bf16[160,256]{1,0:T(8,128)(2,1)S(1)}, u32[]{:S(2)}, u32[]{:S(2)}) %collective-permute-start.25) | collective-permute-done | bytes 81952 | tf_op jit(solution)/shard_map/ppermute | solution.py:574
  85.8 2.8 %collective-permute-done.29.refs_5_ = bf16[144,256]{1,0:T(8,128)(2,1)S(1)} collective-permute-done((bf16[144,256]{1,0:T(8,128)(2,1)S(1)}, bf16[144,256]{1,0:T(8,128)(2,1)S(1)}, u32[]{:S(2)}, u32[]{:S(2)}) %collective-permute-start.29) | collective-permute-done | bytes 73760 | tf_op jit(solution)/shard_map/ppermute | solution.py:574
  89.4 2.2 %collective-permute-start.30 = (bf16[272,256]{1,0:T(8,128)(2,1)S(1)}, bf16[272,256]{1,0:T(8,128)(2,1)S(1)}, u32[]{:S(2)}, u32[]{:S(2)}) collective-permute-start(bf16[272,256]{1,0:T(8,128)(2,1)S(1)} %get-tuple-element.122), channel_id=1, source_target_pairs={{0,8},{4,12},{8,0},{12,4},{16,24},{20,28},{24,16},{28,20},{1,9},{5... | collective-permute-start | bytes 417800 | tf_op jit(solution)/shard_map/ppermute | solution.py:574
  91.6 1.8 %collective-permute-start.35 = (bf16[160,256]{1,0:T(8,128)(2,1)S(1)}, bf16[160,256]{1,0:T(8,128)(2,1)S(1)}, u32[]{:S(2)}, u32[]{:S(2)}) collective-permute-start(bf16[160,256]{1,0:T(8,128)(2,1)S(1)} %get-tuple-element.125), channel_id=1, source_target_pairs={{0,24},{4,28},{8,16},{12,20},{16,8},{20,12},{24,0},{28,4},{1,25},{... | collective-permute-start | bytes 245768 | tf_op jit(solution)/shard_map/ppermute | solution.py:574
  96.8 3.9 %collective-permute-done.31.refs_2_ = bf16[32,256]{1,0:T(8,128)(2,1)S(1)} collective-permute-done((bf16[32,256]{1,0:T(8,128)(2,1)S(1)}, bf16[32,256]{1,0:T(8,128)(2,1)S(1)}, u32[]{:S(2)}, u32[]{:S(2)}) %collective-permute-start.31) | collective-permute-done | bytes 16416 | tf_op jit(solution)/shard_map/ppermute | solution.py:574
  103.3 2.3 %collective-permute-start.37 = (bf16[304,128]{1,0:T(8,128)(2,1)S(1)}, bf16[304,128]{1,0:T(8,128)(2,1)S(1)}, u32[]{:S(2)}, u32[]{:S(2)}) collective-permute-start(bf16[304,128]{1,0:T(8,128)(2,1)S(1)} %get-tuple-element.127), channel_id=1, source_target_pairs={{0,3},{1,2},{2,1},{3,0},{4,7},{5,6},{6,5},{7,4},{8,11},{9,10},{10,... | collective-permute-start | bytes 233480 | tf_op jit(solution)/shard_map/ppermute | solution.py:577
  107.2 1.5 %collective-permute-done.37.refs_1_ = bf16[304,128]{1,0:T(8,128)(2,1)S(1)} collective-permute-done((bf16[304,128]{1,0:T(8,128)(2,1)S(1)}, bf16[304,128]{1,0:T(8,128)(2,1)S(1)}, u32[]{:S(2)}, u32[]{:S(2)}) %collective-permute-start.37) | collective-permute-done | bytes 77856 | tf_op jit(solution)/shard_map/ppermute | solution.py:577
  108.7 1.6 %collective-permute-done.38.refs_2_ = bf16[304,128]{1,0:T(8,128)(2,1)S(1)} collective-permute-done((bf16[304,128]{1,0:T(8,128)(2,1)S(1)}, bf16[304,128]{1,0:T(8,128)(2,1)S(1)}, u32[]{:S(2)}, u32[]{:S(2)}) %collective-permute-start.38) | collective-permute-done | bytes 77856 | tf_op jit(solution)/shard_map/ppermute | solution.py:577
  (90 shorter events, 34.1 us)
Async XLA Ops:
  6.8 19.0 %collective-permute-start.5 = (bf16[4,4,128,256]{3,2,1,0:T(8,128)(2,1)}, bf16[4,4,128,256]{3,2,1,0:T(8,128)(2,1)S(1)}, u32[]{:S(2)}, u32[]{:S(2)}) collective-permute-start(bf16[4,4,128,256]{3,2,1,0:T(8,128)(2,1)} %get-tuple-element.77), channel_id=1, source_target_pairs={{0,4},{4,0},{8,12},{12,8},{16,20},{20,16},{24,28},{28,24},{1,5},{5... | collective-permute-start | bytes 3145736 | tf_op jit(solution)/shard_map/ppermute | solution.py:580
  6.9 7.4 %collective-permute-start = (bf16[304,256]{1,0:T(8,128)(2,1)}, bf16[304,256]{1,0:T(8,128)(2,1)S(1)}, u32[]{:S(2)}, u32[]{:S(2)}) collective-permute-start(bf16[304,256]{1,0:T(8,128)(2,1)} %get-tuple-element.70.refs_0_), channel_id=1, source_target_pairs={{0,1},{1,0},{2,3},{3,2},{4,5},{5,4},{6,7},{7,6},{8,9},{9,8},{10,11... | collective-permute-start | bytes 466952 | tf_op jit(solution)/shard_map/ppermute | solution.py:577
  9.4 6.6 %collective-permute-start.1 = (bf16[304,256]{1,0:T(8,128)(2,1)}, bf16[304,256]{1,0:T(8,128)(2,1)S(1)}, u32[]{:S(2)}, u32[]{:S(2)}) collective-permute-start(bf16[304,256]{1,0:T(8,128)(2,1)} %get-tuple-element.71.refs_1_), channel_id=1, source_target_pairs={{0,2},{1,3},{2,0},{3,1},{4,6},{5,7},{6,4},{7,5},{8,10},{9,11},{10,... | collective-permute-start | bytes 466952 | tf_op jit(solution)/shard_map/ppermute | solution.py:577
  16.0 5.6 %collective-permute-start.2 = (bf16[304,256]{1,0:T(8,128)(2,1)S(1)}, bf16[304,256]{1,0:T(8,128)(2,1)S(1)}, u32[]{:S(2)}, u32[]{:S(2)}) collective-permute-start(bf16[304,256]{1,0:T(8,128)(2,1)S(1)} %get-tuple-element.74.refs_0_), channel_id=1, source_target_pairs={{0,2},{1,3},{2,0},{3,1},{4,6},{5,7},{6,4},{7,5},{8,10},{9,11},{10,... | collective-permute-start | bytes 466952 | tf_op jit(solution)/shard_map/ppermute | solution.py:577
  17.8 5.2 %collective-permute-start.3 = (bf16[304,256]{1,0:T(8,128)(2,1)S(1)}, bf16[304,256]{1,0:T(8,128)(2,1)S(1)}, u32[]{:S(2)}, u32[]{:S(2)}) collective-permute-start(bf16[304,256]{1,0:T(8,128)(2,1)S(1)} %get-tuple-element.75.refs_2_), channel_id=1, source_target_pairs={{0,1},{1,0},{2,3},{3,2},{4,5},{5,4},{6,7},{7,6},{8,9},{9,8},{10,11... | collective-permute-start | bytes 466952 | tf_op jit(solution)/shard_map/ppermute | solution.py:577
  26.3 6.0 %collective-permute-start.10 = (bf16[144,256]{1,0:T(8,128)(2,1)S(1)}, bf16[144,256]{1,0:T(8,128)(2,1)S(1)}, u32[]{:S(2)}, u32[]{:S(2)}) collective-permute-start(bf16[144,256]{1,0:T(8,128)(2,1)S(1)} %get-tuple-element.92), channel_id=1, source_target_pairs={{0,8},{4,12},{8,0},{12,4},{16,24},{20,28},{24,16},{28,20},{1,9},{5... | collective-permute-start | bytes 221192 | tf_op jit(solution)/shard_map/ppermute | solution.py:574
  28.0 12.1 %collective-permute-start.8 = (bf16[272,256]{1,0:T(8,128)(2,1)S(1)}, bf16[272,256]{1,0:T(8,128)(2,1)S(1)}, u32[]{:S(2)}, u32[]{:S(2)}) collective-permute-start(bf16[272,256]{1,0:T(8,128)(2,1)S(1)} %get-tuple-element.89), channel_id=1, source_target_pairs={{0,8},{4,12},{8,0},{12,4},{16,24},{20,28},{24,16},{28,20},{1,9},{5... | collective-permute-start | bytes 417800 | tf_op jit(solution)/shard_map/ppermute | solution.py:574
  28.4 9.9 %collective-permute-start.6 = (bf16[160,256]{1,0:T(8,128)(2,1)S(1)}, bf16[160,256]{1,0:T(8,128)(2,1)S(1)}, u32[]{:S(2)}, u32[]{:S(2)}) collective-permute-start(bf16[160,256]{1,0:T(8,128)(2,1)S(1)} %get-tuple-element.87), channel_id=1, source_target_pairs={{0,16},{4,20},{8,24},{12,28},{16,0},{20,4},{24,8},{28,12},{1,17},{... | collective-permute-start | bytes 245768 | tf_op jit(solution)/shard_map/ppermute | solution.py:574
  31.0 9.1 %collective-permute-start.7 = (bf16[160,256]{1,0:T(8,128)(2,1)S(1)}, bf16[160,256]{1,0:T(8,128)(2,1)S(1)}, u32[]{:S(2)}, u32[]{:S(2)}) collective-permute-start(bf16[160,256]{1,0:T(8,128)(2,1)S(1)} %get-tuple-element.88), channel_id=1, source_target_pairs={{0,24},{4,28},{8,16},{12,20},{16,8},{20,12},{24,0},{28,4},{1,25},{... | collective-permute-start | bytes 245768 | tf_op jit(solution)/shard_map/ppermute | solution.py:574
  32.4 10.1 %collective-permute-start.11 = (bf16[144,256]{1,0:T(8,128)(2,1)S(1)}, bf16[144,256]{1,0:T(8,128)(2,1)S(1)}, u32[]{:S(2)}, u32[]{:S(2)}) collective-permute-start(bf16[144,256]{1,0:T(8,128)(2,1)S(1)} %shard_map.110), channel_id=1, source_target_pairs={{0,16},{4,20},{8,24},{12,28},{16,0},{20,4},{24,8},{28,12},{1,17},{... | collective-permute-start | bytes 221192 | tf_op jit(solution)/shard_map/ppermute | solution.py:574
  42.7 6.0 %collective-permute-start.14 = (bf16[144,256]{1,0:T(8,128)(2,1)S(1)}, bf16[144,256]{1,0:T(8,128)(2,1)S(1)}, u32[]{:S(2)}, u32[]{:S(2)}) collective-permute-start(bf16[144,256]{1,0:T(8,128)(2,1)S(1)} %get-tuple-element.96), channel_id=1, source_target_pairs={{0,16},{4,20},{8,24},{12,28},{16,0},{20,4},{24,8},{28,12},{1,17},{... | collective-permute-start | bytes 221192 | tf_op jit(solution)/shard_map/ppermute | solution.py:574
  43.3 11.5 %collective-permute-start.12 = (bf16[272,256]{1,0:T(8,128)(2,1)S(1)}, bf16[272,256]{1,0:T(8,128)(2,1)S(1)}, u32[]{:S(2)}, u32[]{:S(2)}) collective-permute-start(bf16[272,256]{1,0:T(8,128)(2,1)S(1)} %get-tuple-element.94), channel_id=1, source_target_pairs={{0,8},{4,12},{8,0},{12,4},{16,24},{20,28},{24,16},{28,20},{1,9},{5... | collective-permute-start | bytes 417800 | tf_op jit(solution)/shard_map/ppermute | solution.py:574
  45.6 9.3 %collective-permute-start.17 = (bf16[160,256]{1,0:T(8,128)(2,1)S(1)}, bf16[160,256]{1,0:T(8,128)(2,1)S(1)}, u32[]{:S(2)}, u32[]{:S(2)}) collective-permute-start(bf16[160,256]{1,0:T(8,128)(2,1)S(1)} %get-tuple-element.97), channel_id=1, source_target_pairs={{0,24},{4,28},{8,16},{12,20},{16,8},{20,12},{24,0},{28,4},{1,25},{... | collective-permute-start | bytes 245768 | tf_op jit(solution)/shard_map/ppermute | solution.py:574
  47.1 7.7 %collective-permute-start.15 = (bf16[160,256]{1,0:T(8,128)(2,1)S(1)}, bf16[160,256]{1,0:T(8,128)(2,1)S(1)}, u32[]{:S(2)}, u32[]{:S(2)}) collective-permute-start(bf16[160,256]{1,0:T(8,128)(2,1)S(1)} %get-tuple-element.97), channel_id=1, source_target_pairs={{0,16},{4,20},{8,24},{12,28},{16,0},{20,4},{24,8},{28,12},{1,17},{... | collective-permute-start | bytes 245768 | tf_op jit(solution)/shard_map/ppermute | solution.py:574
  48.7 6.2 %collective-permute-start.16 = (bf16[144,256]{1,0:T(8,128)(2,1)S(1)}, bf16[144,256]{1,0:T(8,128)(2,1)S(1)}, u32[]{:S(2)}, u32[]{:S(2)}) collective-permute-start(bf16[144,256]{1,0:T(8,128)(2,1)S(1)} %collective-permute-done.14.refs_3_), channel_id=1, source_target_pairs={{0,8},{4,12},{8,0},{12,4},{16,24},{20,28},{24,16},{28,20},{1,9},{5... | collective-permute-start | bytes 221192 | tf_op jit(solution)/shard_map/ppermute | solution.py:574
  50.0 4.9 %collective-permute-start.13 = (bf16[32,256]{1,0:T(8,128)(2,1)S(1)}, bf16[32,256]{1,0:T(8,128)(2,1)S(1)}, u32[]{:S(2)}, u32[]{:S(2)}) collective-permute-start(bf16[32,256]{1,0:T(8,128)(2,1)S(1)} %get-tuple-element.95), channel_id=1, source_target_pairs={{0,8},{4,12},{8,0},{12,4},{16,24},{20,28},{24,16},{28,20},{1,9},{5... | collective-permute-start | bytes 49160 | tf_op jit(solution)/shard_map/ppermute | solution.py:574
  57.2 6.1 %collective-permute-start.19 = (bf16[304,256]{1,0:T(8,128)(2,1)S(1)}, bf16[304,256]{1,0:T(8,128)(2,1)S(1)}, u32[]{:S(2)}, u32[]{:S(2)}) collective-permute-start(bf16[304,256]{1,0:T(8,128)(2,1)S(1)} %get-tuple-element.98.one), channel_id=1, source_target_pairs={{0,1},{1,0},{2,3},{3,2},{4,5},{5,4},{6,7},{7,6},{8,9},{9,8},{10,11... | collective-permute-start | bytes 466952 | tf_op jit(solution)/shard_map/ppermute | solution.py:577
  57.9 5.8 %collective-permute-start.20 = (bf16[304,256]{1,0:T(8,128)(2,1)S(1)}, bf16[304,256]{1,0:T(8,128)(2,1)S(1)}, u32[]{:S(2)}, u32[]{:S(2)}) collective-permute-start(bf16[304,256]{1,0:T(8,128)(2,1)S(1)} %get-tuple-element.99.two), channel_id=1, source_target_pairs={{0,2},{1,3},{2,0},{3,1},{4,6},{5,7},{6,4},{7,5},{8,10},{9,11},{10,... | collective-permute-start | bytes 466952 | tf_op jit(solution)/shard_map/ppermute | solution.py:577
  63.8 5.3 %collective-permute-start.21 = (bf16[304,256]{1,0:T(8,128)(2,1)S(1)}, bf16[304,256]{1,0:T(8,128)(2,1)S(1)}, u32[]{:S(2)}, u32[]{:S(2)}) collective-permute-start(bf16[304,256]{1,0:T(8,128)(2,1)S(1)} %get-tuple-element.100.refs_0_), channel_id=1, source_target_pairs={{0,2},{1,3},{2,0},{3,1},{4,6},{5,7},{6,4},{7,5},{8,10},{9,11},{10,... | collective-permute-start | bytes 466952 | tf_op jit(solution)/shard_map/ppermute | solution.py:577
  64.3 5.2 %collective-permute-start.22 = (bf16[304,256]{1,0:T(8,128)(2,1)S(1)}, bf16[304,256]{1,0:T(8,128)(2,1)S(1)}, u32[]{:S(2)}, u32[]{:S(2)}) collective-permute-start(bf16[304,256]{1,0:T(8,128)(2,1)S(1)} %get-tuple-element.101.refs_2_), channel_id=1, source_target_pairs={{0,1},{1,0},{2,3},{3,2},{4,5},{5,4},{6,7},{7,6},{8,9},{9,8},{10,11... | collective-permute-start | bytes 466952 | tf_op jit(solution)/shard_map/ppermute | solution.py:577
  73.0 5.2 %collective-permute-start.28 = (bf16[144,256]{1,0:T(8,128)(2,1)S(1)}, bf16[144,256]{1,0:T(8,128)(2,1)S(1)}, u32[]{:S(2)}, u32[]{:S(2)}) collective-permute-start(bf16[144,256]{1,0:T(8,128)(2,1)S(1)} %get-tuple-element.119), channel_id=1, source_target_pairs={{0,8},{4,12},{8,0},{12,4},{16,24},{20,28},{24,16},{28,20},{1,9},{5... | collective-permute-start | bytes 221192 | tf_op jit(solution)/shard_map/ppermute | solution.py:574
  73.8 12.0 %collective-permute-start.26 = (bf16[272,256]{1,0:T(8,128)(2,1)S(1)}, bf16[272,256]{1,0:T(8,128)(2,1)S(1)}, u32[]{:S(2)}, u32[]{:S(2)}) collective-permute-start(bf16[272,256]{1,0:T(8,128)(2,1)S(1)} %get-tuple-element.116), channel_id=1, source_target_pairs={{0,8},{4,12},{8,0},{12,4},{16,24},{20,28},{24,16},{28,20},{1,9},{5... | collective-permute-start | bytes 417800 | tf_op jit(solution)/shard_map/ppermute | solution.py:574
  75.1 9.0 %collective-permute-start.24 = (bf16[160,256]{1,0:T(8,128)(2,1)S(1)}, bf16[160,256]{1,0:T(8,128)(2,1)S(1)}, u32[]{:S(2)}, u32[]{:S(2)}) collective-permute-start(bf16[160,256]{1,0:T(8,128)(2,1)S(1)} %get-tuple-element.114), channel_id=1, source_target_pairs={{0,16},{4,20},{8,24},{12,28},{16,0},{20,4},{24,8},{28,12},{1,17},{... | collective-permute-start | bytes 245768 | tf_op jit(solution)/shard_map/ppermute | solution.py:574
  76.7 9.0 %collective-permute-start.25 = (bf16[160,256]{1,0:T(8,128)(2,1)S(1)}, bf16[160,256]{1,0:T(8,128)(2,1)S(1)}, u32[]{:S(2)}, u32[]{:S(2)}) collective-permute-start(bf16[160,256]{1,0:T(8,128)(2,1)S(1)} %get-tuple-element.115), channel_id=1, source_target_pairs={{0,24},{4,28},{8,16},{12,20},{16,8},{20,12},{24,0},{28,4},{1,25},{... | collective-permute-start | bytes 245768 | tf_op jit(solution)/shard_map/ppermute | solution.py:574
  78.2 10.4 %collective-permute-start.29 = (bf16[144,256]{1,0:T(8,128)(2,1)S(1)}, bf16[144,256]{1,0:T(8,128)(2,1)S(1)}, u32[]{:S(2)}, u32[]{:S(2)}) collective-permute-start(bf16[144,256]{1,0:T(8,128)(2,1)S(1)} %shard_map.120), channel_id=1, source_target_pairs={{0,16},{4,20},{8,24},{12,28},{16,0},{20,4},{24,8},{28,12},{1,17},{... | collective-permute-start | bytes 221192 | tf_op jit(solution)/shard_map/ppermute | solution.py:574
  89.0 5.8 %collective-permute-start.32 = (bf16[144,256]{1,0:T(8,128)(2,1)S(1)}, bf16[144,256]{1,0:T(8,128)(2,1)S(1)}, u32[]{:S(2)}, u32[]{:S(2)}) collective-permute-start(bf16[144,256]{1,0:T(8,128)(2,1)S(1)} %get-tuple-element.124), channel_id=1, source_target_pairs={{0,16},{4,20},{8,24},{12,28},{16,0},{20,4},{24,8},{28,12},{1,17},{... | collective-permute-start | bytes 221192 | tf_op jit(solution)/shard_map/ppermute | solution.py:574
  89.4 11.5 %collective-permute-start.30 = (bf16[272,256]{1,0:T(8,128)(2,1)S(1)}, bf16[272,256]{1,0:T(8,128)(2,1)S(1)}, u32[]{:S(2)}, u32[]{:S(2)}) collective-permute-start(bf16[272,256]{1,0:T(8,128)(2,1)S(1)} %get-tuple-element.122), channel_id=1, source_target_pairs={{0,8},{4,12},{8,0},{12,4},{16,24},{20,28},{24,16},{28,20},{1,9},{5... | collective-permute-start | bytes 417800 | tf_op jit(solution)/shard_map/ppermute | solution.py:574
  91.6 9.1 %collective-permute-start.35 = (bf16[160,256]{1,0:T(8,128)(2,1)S(1)}, bf16[160,256]{1,0:T(8,128)(2,1)S(1)}, u32[]{:S(2)}, u32[]{:S(2)}) collective-permute-start(bf16[160,256]{1,0:T(8,128)(2,1)S(1)} %get-tuple-element.125), channel_id=1, source_target_pairs={{0,24},{4,28},{8,16},{12,20},{16,8},{20,12},{24,0},{28,4},{1,25},{... | collective-permute-start | bytes 245768 | tf_op jit(solution)/shard_map/ppermute | solution.py:574
  93.4 7.5 %collective-permute-start.33 = (bf16[160,256]{1,0:T(8,128)(2,1)S(1)}, bf16[160,256]{1,0:T(8,128)(2,1)S(1)}, u32[]{:S(2)}, u32[]{:S(2)}) collective-permute-start(bf16[160,256]{1,0:T(8,128)(2,1)S(1)} %get-tuple-element.125), channel_id=1, source_target_pairs={{0,16},{4,20},{8,24},{12,28},{16,0},{20,4},{24,8},{28,12},{1,17},{... | collective-permute-start | bytes 245768 | tf_op jit(solution)/shard_map/ppermute | solution.py:574
  94.8 6.1 %collective-permute-start.34 = (bf16[144,256]{1,0:T(8,128)(2,1)S(1)}, bf16[144,256]{1,0:T(8,128)(2,1)S(1)}, u32[]{:S(2)}, u32[]{:S(2)}) collective-permute-start(bf16[144,256]{1,0:T(8,128)(2,1)S(1)} %collective-permute-done.32.refs_3_), channel_id=1, source_target_pairs={{0,8},{4,12},{8,0},{12,4},{16,24},{20,28},{24,16},{28,20},{1,9},{5... | collective-permute-start | bytes 221192 | tf_op jit(solution)/shard_map/ppermute | solution.py:574
  103.3 5.4 %collective-permute-start.37 = (bf16[304,128]{1,0:T(8,128)(2,1)S(1)}, bf16[304,128]{1,0:T(8,128)(2,1)S(1)}, u32[]{:S(2)}, u32[]{:S(2)}) collective-permute-start(bf16[304,128]{1,0:T(8,128)(2,1)S(1)} %get-tuple-element.127), channel_id=1, source_target_pairs={{0,3},{1,2},{2,1},{3,0},{4,7},{5,6},{6,5},{7,4},{8,11},{9,10},{10,... | collective-permute-start | bytes 233480 | tf_op jit(solution)/shard_map/ppermute | solution.py:577
  105.6 4.8 %collective-permute-start.38 = (bf16[304,128]{1,0:T(8,128)(2,1)S(1)}, bf16[304,128]{1,0:T(8,128)(2,1)S(1)}, u32[]{:S(2)}, u32[]{:S(2)}) collective-permute-start(bf16[304,128]{1,0:T(8,128)(2,1)S(1)} %get-tuple-element.128), channel_id=1, source_target_pairs={{0,2},{1,3},{2,0},{3,1},{4,6},{5,7},{6,4},{7,5},{8,10},{9,11},{10,... | collective-permute-start | bytes 233480 | tf_op jit(solution)/shard_map/ppermute | solution.py:577
  (14 other events, 73.1 us)

commit v21 on v19

--- a/solution.py
+++ b/solution.py
@@ -310,7 +310,7 @@
 
 
 def first_kernel(lev, *refs):
-    vert, vert_t, sd_out, residual, moved, spread, packed = refs[4:]
+    vert, vert_t, sd_out, residual, *moved, spread, packed = refs[4:]
     members, levp, unused = residual.shape
     t = joined(refs[:4])
     sd = read_columns(t)
@@ -323,7 +323,7 @@
         residual[m] = r
         packed[at, :] = sd * dot(vert[...], r)
         scalars.append([total(r * r)])
-    moved[...] = with_scalars(packed[0 : moved.shape[0], :], scalars).astype(BF16)
+    put_halves(moved, with_scalars(packed[0 : moved[0].shape[0], :], scalars))
 
 
 def add_kernel(members, scalars, *refs):
@@ -351,20 +351,24 @@
         copy.wait()
 
 
-def forward_kernel(sends, members, x, tiles, *refs):
+def forward_kernel(sends, members, left, right, tiles, *refs):
     z, core, obs = place()
     outs = refs[-len(sends) :]
-    rows, lanes = x.shape
-    width = tiles.shape[3]
+    rows, lanes = left.shape
+    half, width = tiles.shape[1] // 2, tiles.shape[3]
     added = refs[1 : 1 + len(sends)] if len(refs) > len(sends) else [None] * len(sends)
     if added[0] is not None:
-        scalars = read_scalars([refs[0], x], members, 2)
+        scalars = read_scalars([refs[0], left], members, 2)
     for out, before, (chip, first, count) in zip(outs, added, sends):
-        y = jnp.dot(
-            x[first : first + count, :],
-            tiles[z ^ chip].reshape(lanes, width),
-            preferred_element_type=F32,
-        )
+        y = [
+            jnp.dot(
+                x[first : first + count, :],
+                tiles[z ^ chip, at : at + half].reshape(lanes, width),
+                preferred_element_type=F32,
+            )
+            for x, at in ((left, 0), (right, half))
+        ]
+        y = y[0] + y[1]
         if before is not None:
             y = before[...] + y
             if first + count == rows:
@@ -417,8 +421,8 @@
 
 def adjoint_kernel(plan, members, *refs):
     z, core, obs = place()
-    ws, tiles, out = refs[: len(plan)], refs[len(plan)], refs[len(plan) + 1]
-    rows, lanes = out.shape
+    ws, tiles, outs = refs[: len(plan)], refs[len(plan)], refs[len(plan) + 1 :]
+    rows, lanes = outs[0].shape[0], tiles.shape[1] * LANES
     width = ws[0].shape[1]
     acc = None
     for i in range(tiles.shape[0]):
@@ -430,21 +434,30 @@
         )
         acc = part if i == 0 else acc + part
     ends = [ref for ref, (chip, first, count) in zip(ws, plan) if first + count == rows]
-    out[...] = with_scalars(acc, read_scalars(ends, members, 1)).astype(out.dtype)
-
-
-def combine_kernel(members, mine, theirs, *outs):
-    value = mine[...] + theirs[...].astype(F32)
-    put_halves(outs, with_scalars(value, read_scalars([mine, theirs], members, 1)))
-
-
-def combine_columns_kernel(members, mine, theirs, *outs):
+    acc = with_scalars(acc, read_scalars(ends, members, 1))
+    if len(outs) == 2:
+        put_halves(outs, acc)
+    else:
+        outs[0][...] = acc
+
+
+def both_cores(members, mine, left, right):
+    value = mine[...] + jnp.concatenate([left[...], right[...]], axis=1).astype(F32)
+    return with_scalars(value, read_scalars([mine, left], members, 1))
+
+
+def combine_kernel(members, mine, left, right, *outs):
+    put_halves(outs, both_cores(members, mine, left, right))
+
+
+def combine_columns_kernel(members, mine, left, right, *refs):
+    outs, scratch = refs[:-1], refs[-1]
     obs = lax.axis_index("obs")
-    energies = read_scalars([mine, theirs], members, 1)
+    scratch[...] = both_cores(members, mine, left, right)
+    energies = read_scalars([mine, left], members, 1)
     for i, out in enumerate(outs):
         lane = pl.ds(pl.multiple_of((obs ^ i) * LANES, LANES), LANES)
-        value = mine[:, lane] + theirs[:, lane].astype(F32)
-        out[...] = with_scalars(value, energies).astype(BF16)
+        out[...] = with_scalars(scratch[:, lane], energies).astype(BF16)
 
 
 def update_kernel(later, lev, *refs):
@@ -452,9 +465,9 @@
     sd, vert, vert_t, state, residual = refs[:5]
     spread, packed = refs[-2:]
     if later:
-        old_direction, old_solution, residual_out, solution_out, moved, direction_out = refs[5:-2]
+        old_direction, old_solution, residual_out, solution_out, *moved, direction_out = refs[5:-2]
     else:
-        residual_out, solution_out, moved = refs[5:-2]
+        residual_out, solution_out, *moved = refs[5:-2]
     members, levp, unused = residual.shape
     obs = lax.axis_index("obs")
     mine = pl.ds(pl.multiple_of(obs * LANES, LANES), LANES)
@@ -478,7 +491,7 @@
         residual_out[m] = r
         packed[at, :] = sd[...] * dot(vert[...], r)
         scalars.append([total(r * r), total(r * d)])
-    moved[...] = with_scalars(packed[0 : moved.shape[0], :], scalars).astype(BF16)
+    put_halves(moved, with_scalars(packed[0 : moved[0].shape[0], :], scalars))
 
 
 def increment_kernel(later, sd, vert, state, residual, *refs):
@@ -610,14 +623,15 @@
                 )
         return [x for pair in zip(halves, moved_halves) for x in pair]
 
-    def line_sum(moved, other):
+    def line_sum(moved):
+        other = [swap(x) for x in moved]
         shapes = [(count, width) for i, unused, count in sends]
         mine = call(
             functools.partial(forward_kernel, sends, members),
             [struct(shape, F32) for shape in shapes],
             [],
             product,
-            moved,
+            *moved,
             own,
         )
         ys = call(
@@ -628,9 +642,9 @@
             ],
             [],
             product,
-            other,
+            *other,
             partner,
-            moved,
+            moved[0],
             *mine,
         )
         if not via:
@@ -701,9 +715,9 @@
         0,
         obs_precision,
     )
-    slab_sd, residual, moved = call(
+    slab_sd, residual, *moved = call(
         functools.partial(first_kernel, lev),
-        [struct((1, lanes), F32), struct(slab_field, F32), struct(slab_rows, BF16)],
+        [struct((1, lanes), F32), struct(slab_field, F32), *half_rows],
         [spread, spread],
         small * colblocks,
         *ps,
@@ -713,7 +727,7 @@
     direction = total_step = image = state = None
     for sweep in range(ITERS):
         later, last = sweep > 0, sweep == ITERS - 1
-        ys, spans = line_sum(moved, swap(moved))
+        ys, spans = line_sum(moved)
         state, *weighted = call(
             functools.partial(weigh_kernel, later, last, members, lev, spans),
             [struct((members, 8, LANES), F32)]
@@ -728,15 +742,15 @@
         if not last:
             *weighted, image = weighted
         ws = line_gather(*weighted)
-        (theirs,) = call(
+        theirs = call(
             functools.partial(adjoint_kernel, plan, members),
-            [struct(slab_rows, BF16)],
+            half_rows,
             [],
             product,
             *ws,
             partner,
         )
-        theirs = swap(theirs)
+        theirs = [swap(x) for x in theirs]
         (mine,) = call(
             functools.partial(adjoint_kernel, plan, members),
             [struct(slab_rows, F32)],
@@ -752,10 +766,10 @@
             ps = call(
                 functools.partial(combine_columns_kernel, members),
                 [struct((rows, LANES), BF16)] * n_obs,
-                [],
+                [pltpu.VMEM(slab_rows, F32)],
                 0,
                 mine,
-                theirs,
+                *theirs,
             )
             ps = [ps[0]] + [plane(ps[i], i) for i in reversed(range(1, n_obs))]
             own_field = struct((members, levp, LANES), F32)
@@ -786,17 +800,17 @@
             )
             break
         ps = call(
-            functools.partial(combine_kernel, members), half_rows, [], 0, mine, theirs
+            functools.partial(combine_kernel, members), half_rows, [], 0, mine, *theirs
         )
         ps = plane_sum(ps, False)
         outs = [
             struct(slab_field, F32),
             struct((members, levp, LANES), F32),
-            struct(slab_rows, BF16),
+            *half_rows,
         ]
         if later:
             outs.append(struct(slab_field, F32))
-        r, total_step, moved, *d = call(
+        r, total_step, *moved = call(
             functools.partial(update_kernel, later, lev),
             outs,
             [spread, spread],
@@ -805,7 +819,7 @@
             slab_sd,
             *known,
         )
-        direction, residual = (d[0] if later else residual), r
+        direction, residual = (moved.pop() if later else residual), r
     return tuple(jnp.transpose(x, (1, 0, 2))[None] for x in outputs)
 
 

time: 112 us -> 112 us (level)
  starting transfers between devices: 42.2 us -> 46.9 us
  waiting for transfers between devices: 50.2 us -> 46.2 us
    ppermute x5 -> x9, starting transfers between devices: 0.35 us -> 2.9 us  [swap(): return lax.ppermute(x, 'slab', [(s, s ^ 1) for s in range(n_slab)])]
    ppermute x5 -> x9, waiting for transfers between devices: 4.24 us -> 2.32 us  [swap(): return lax.ppermute(x, 'slab', [(s, s ^ 1) for s in range(n_slab)])]
    ppermute x24, starting transfers between devices: 29.3 us -> 31.1 us  [along(): return lax.ppermute(x, 'slab', [(s, s ^ 2 * i) for s in range(n_slab)])]
    ppermute x24, waiting for transfers between devices: 26.1 us -> 24.3 us  [along(): return lax.ppermute(x, 'slab', [(s, s ^ 2 * i) for s in range(n_slab)])]
  transfers between devices with their start and end apart: 40 -> 44, of which waited for: 25 -> 27; matrix products, arithmetic and copies ran while one was open for 0% -> 0% of each run, Pallas kernels for 4% -> 4%
where the time goes in v21:
time: 112 us; the launch traced here: 111 us
  starting transfers between devices  46.9 us (42%)
  waiting for transfers between devices  46.2 us (41%)
  Pallas kernels  14.4 us (13%)
  local copies, waits for them, and re-layouts  2.09 us (2%)
  between operations  1.57 us (1%)
    ppermute x24, starting transfers between devices, along(): return lax.ppermute(x, 'slab', [(s, s ^ 2 * i) for s in range(n_slab)])  31.1 us
    ppermute x24, waiting for transfers between devices, along(): return lax.ppermute(x, 'slab', [(s, s ^ 2 * i) for s in range(n_slab)])  24.3 us
    ppermute x11, waiting for transfers between devices, plane(): return lax.ppermute(x, 'obs', [(o, o ^ i) for o in range(n_obs)])  19.7 us
    pallas_call x23, Pallas kernels, call(): pl.pallas_call(kernel, out_shape=outs, in_specs=[space] * len(args), out_...  14.4 us
    ppermute x11, starting transfers between devices, plane(): return lax.ppermute(x, 'obs', [(o, o ^ i) for o in range(n_obs)])  12.9 us
    ppermute x9, starting transfers between devices, swap(): return lax.ppermute(x, 'slab', [(s, s ^ 1) for s in range(n_slab)])  2.9 us
    ppermute x9, waiting for transfers between devices, swap(): return lax.ppermute(x, 'slab', [(s, s ^ 1) for s in range(n_slab)])  2.32 us
  transfers between devices with their start and end apart: 44, of which 27 were waited for; matrix products, arithmetic and copies ran while one was open for 0% of the time, Pallas kernels for 4%

profile of v21, /device:TPU:0, one launch (start us, length us, event | category | flops | bytes accessed | tf_op | source)
XLA Modules:
  0.0 111.4 jit_solution(1527075806003396491)
XLA Ops:
  1.3 4.9 %shard_map.104 = (bf16[4,4,128,256]{3,2,1,0:T(8,128)(2,1)}, bf16[4,4,128,256]{3,2,1,0:T(8,128)(2,1)}, bf16[304,256]{1,0:T(8,128)(2,1)}, bf16[304,256]{1,0:T(8,128)(2,1)}) custom-call(s32[4]{0:T(128)} %seeds_in.1, s32[1,1,32]{2,1,0:T(1,128)} %ids_in.1, s32[1,1,32]{2,1,0:T(1,128)} %cols_in.1, s32[1,1]{1,0:T(1,128)S(6)} %copy.16.count_in, f32[1,128]{1,0:T(1,128)} %refs_4_.1, ...), custom_call_target="tpu_custom_call" | custom-call | flops 637534208 | bytes 5735188 | tf_op jit(solution)/shard_map/pallas_call | solution.py:23
  6.9 2.8 %collective-permute-start = (bf16[304,256]{1,0:T(8,128)(2,1)}, bf16[304,256]{1,0:T(8,128)(2,1)S(1)}, u32[]{:S(2)}, u32[]{:S(2)}) collective-permute-start(bf16[304,256]{1,0:T(8,128)(2,1)} %get-tuple-element.76.refs_0_), channel_id=1, source_target_pairs={{0,1},{1,0},{2,3},{3,2},{4,5},{5,4},{6,7},{7,6},{8,9},{9,8},{10,11... | collective-permute-start | bytes 466952 | tf_op jit(solution)/shard_map/ppermute | solution.py:589
  9.6 1.5 %collective-permute-start.1 = (bf16[304,256]{1,0:T(8,128)(2,1)}, bf16[304,256]{1,0:T(8,128)(2,1)S(1)}, u32[]{:S(2)}, u32[]{:S(2)}) collective-permute-start(bf16[304,256]{1,0:T(8,128)(2,1)} %get-tuple-element.77.refs_1_), channel_id=1, source_target_pairs={{0,2},{1,3},{2,0},{3,1},{4,6},{5,7},{6,4},{7,5},{8,10},{9,11},{10,... | collective-permute-start | bytes 466952 | tf_op jit(solution)/shard_map/ppermute | solution.py:589
  14.2 1.5 %collective-permute-done.1.two_more = bf16[304,256]{1,0:T(8,128)(2,1)S(1)} collective-permute-done((bf16[304,256]{1,0:T(8,128)(2,1)}, bf16[304,256]{1,0:T(8,128)(2,1)S(1)}, u32[]{:S(2)}, u32[]{:S(2)}) %collective-permute-start.1) | collective-permute-done | bytes 155680 | tf_op jit(solution)/shard_map/ppermute | solution.py:589
  15.8 1.6 %collective-permute-start.2 = (bf16[304,256]{1,0:T(8,128)(2,1)S(1)}, bf16[304,256]{1,0:T(8,128)(2,1)S(1)}, u32[]{:S(2)}, u32[]{:S(2)}) collective-permute-start(bf16[304,256]{1,0:T(8,128)(2,1)S(1)} %get-tuple-element.80.refs_0_), channel_id=1, source_target_pairs={{0,2},{1,3},{2,0},{3,1},{4,6},{5,7},{6,4},{7,5},{8,10},{9,11},{10,... | collective-permute-start | bytes 466952 | tf_op jit(solution)/shard_map/ppermute | solution.py:589
  18.6 2.5 %collective-permute-done.2.refs_1_ = bf16[304,256]{1,0:T(8,128)(2,1)S(1)} collective-permute-done((bf16[304,256]{1,0:T(8,128)(2,1)S(1)}, bf16[304,256]{1,0:T(8,128)(2,1)S(1)}, u32[]{:S(2)}, u32[]{:S(2)}) %collective-permute-start.2) | collective-permute-done | bytes 155680 | tf_op jit(solution)/shard_map/ppermute | solution.py:589
  21.1 1.5 %collective-permute-done.3.refs_3_ = bf16[304,256]{1,0:T(8,128)(2,1)S(1)} collective-permute-done((bf16[304,256]{1,0:T(8,128)(2,1)S(1)}, bf16[304,256]{1,0:T(8,128)(2,1)S(1)}, u32[]{:S(2)}, u32[]{:S(2)}) %collective-permute-start.3) | collective-permute-done | bytes 155680 | tf_op jit(solution)/shard_map/ppermute | solution.py:589
  25.9 1.6 %collective-permute-start.11 = (bf16[144,256]{1,0:T(8,128)(2,1)S(1)}, bf16[144,256]{1,0:T(8,128)(2,1)S(1)}, u32[]{:S(2)}, u32[]{:S(2)}) collective-permute-start(bf16[144,256]{1,0:T(8,128)(2,1)S(1)} %get-tuple-element.99), channel_id=1, source_target_pairs={{0,8},{4,12},{8,0},{12,4},{16,24},{20,28},{24,16},{28,20},{1,9},{5... | collective-permute-start | bytes 221192 | tf_op jit(solution)/shard_map/ppermute | solution.py:586
  27.5 2.6 %collective-permute-start.7 = (bf16[160,256]{1,0:T(8,128)(2,1)S(1)}, bf16[160,256]{1,0:T(8,128)(2,1)S(1)}, u32[]{:S(2)}, u32[]{:S(2)}) collective-permute-start(bf16[160,256]{1,0:T(8,128)(2,1)S(1)} %get-tuple-element.94), channel_id=1, source_target_pairs={{0,16},{4,20},{8,24},{12,28},{16,0},{20,4},{24,8},{28,12},{1,17},{... | collective-permute-start | bytes 245768 | tf_op jit(solution)/shard_map/ppermute | solution.py:586
  31.0 1.5 %collective-permute-start.9 = (bf16[144,256]{1,0:T(8,128)(2,1)S(1)}, bf16[144,256]{1,0:T(8,128)(2,1)S(1)}, u32[]{:S(2)}, u32[]{:S(2)}) collective-permute-start(bf16[144,256]{1,0:T(8,128)(2,1)S(1)} %get-tuple-element.96), channel_id=1, source_target_pairs={{0,8},{4,12},{8,0},{12,4},{16,24},{20,28},{24,16},{28,20},{1,9},{5... | collective-permute-start | bytes 221192 | tf_op jit(solution)/shard_map/ppermute | solution.py:586
  32.5 2.1 %collective-permute-start.12 = (bf16[144,256]{1,0:T(8,128)(2,1)S(1)}, bf16[144,256]{1,0:T(8,128)(2,1)S(1)}, u32[]{:S(2)}, u32[]{:S(2)}) collective-permute-start(bf16[144,256]{1,0:T(8,128)(2,1)S(1)} %shard_map.110), channel_id=1, source_target_pairs={{0,16},{4,20},{8,24},{12,28},{16,0},{20,4},{24,8},{28,12},{1,17},{... | collective-permute-start | bytes 221192 | tf_op jit(solution)/shard_map/ppermute | solution.py:586
  34.8 3.7 %collective-permute-done.9.refs_3_ = bf16[144,256]{1,0:T(8,128)(2,1)S(1)} collective-permute-done((bf16[144,256]{1,0:T(8,128)(2,1)S(1)}, bf16[144,256]{1,0:T(8,128)(2,1)S(1)}, u32[]{:S(2)}, u32[]{:S(2)}) %collective-permute-start.9) | collective-permute-done | bytes 73760 | tf_op jit(solution)/shard_map/ppermute | solution.py:586
  38.5 1.8 %collective-permute-done.12.refs_5_ = bf16[144,256]{1,0:T(8,128)(2,1)S(1)} collective-permute-done((bf16[144,256]{1,0:T(8,128)(2,1)S(1)}, bf16[144,256]{1,0:T(8,128)(2,1)S(1)}, u32[]{:S(2)}, u32[]{:S(2)}) %collective-permute-start.12) | collective-permute-done | bytes 73760 | tf_op jit(solution)/shard_map/ppermute | solution.py:586
  40.5 2.0 %collective-permute-start.15 = (bf16[144,256]{1,0:T(8,128)(2,1)S(1)}, bf16[144,256]{1,0:T(8,128)(2,1)S(1)}, u32[]{:S(2)}, u32[]{:S(2)}) collective-permute-start(bf16[144,256]{1,0:T(8,128)(2,1)S(1)} %get-tuple-element.103), channel_id=1, source_target_pairs={{0,16},{4,20},{8,24},{12,28},{16,0},{20,4},{24,8},{28,12},{1,17},{... | collective-permute-start | bytes 221192 | tf_op jit(solution)/shard_map/ppermute | solution.py:586
  42.6 2.4 %collective-permute-start.13 = (bf16[272,256]{1,0:T(8,128)(2,1)S(1)}, bf16[272,256]{1,0:T(8,128)(2,1)S(1)}, u32[]{:S(2)}, u32[]{:S(2)}) collective-permute-start(bf16[272,256]{1,0:T(8,128)(2,1)S(1)} %get-tuple-element.101), channel_id=1, source_target_pairs={{0,8},{4,12},{8,0},{12,4},{16,24},{20,28},{24,16},{28,20},{1,9},{5... | collective-permute-start | bytes 417800 | tf_op jit(solution)/shard_map/ppermute | solution.py:586
  45.0 1.5 %collective-permute-start.16 = (bf16[160,256]{1,0:T(8,128)(2,1)S(1)}, bf16[160,256]{1,0:T(8,128)(2,1)S(1)}, u32[]{:S(2)}, u32[]{:S(2)}) collective-permute-start(bf16[160,256]{1,0:T(8,128)(2,1)S(1)} %get-tuple-element.104), channel_id=1, source_target_pairs={{0,16},{4,20},{8,24},{12,28},{16,0},{20,4},{24,8},{28,12},{1,17},{... | collective-permute-start | bytes 245768 | tf_op jit(solution)/shard_map/ppermute | solution.py:586
  46.9 2.5 %collective-permute-start.17 = (bf16[144,256]{1,0:T(8,128)(2,1)S(1)}, bf16[144,256]{1,0:T(8,128)(2,1)S(1)}, u32[]{:S(2)}, u32[]{:S(2)}) collective-permute-start(bf16[144,256]{1,0:T(8,128)(2,1)S(1)} %collective-permute-done.15.refs_3_), channel_id=1, source_target_pairs={{0,8},{4,12},{8,0},{12,4},{16,24},{20,28},{24,16},{28,20},{1,9},{5... | collective-permute-start | bytes 221192 | tf_op jit(solution)/shard_map/ppermute | solution.py:586
  49.4 4.9 %collective-permute-done.14.refs_2_ = bf16[32,256]{1,0:T(8,128)(2,1)S(1)} collective-permute-done((bf16[32,256]{1,0:T(8,128)(2,1)S(1)}, bf16[32,256]{1,0:T(8,128)(2,1)S(1)}, u32[]{:S(2)}, u32[]{:S(2)}) %collective-permute-start.14) | collective-permute-done | bytes 16416 | tf_op jit(solution)/shard_map/ppermute | solution.py:586
  57.8 5.1 %collective-permute-done.21.one_more = bf16[304,256]{1,0:T(8,128)(2,1)S(1)} collective-permute-done((bf16[304,256]{1,0:T(8,128)(2,1)S(1)}, bf16[304,256]{1,0:T(8,128)(2,1)S(1)}, u32[]{:S(2)}, u32[]{:S(2)}) %collective-permute-start.21) | collective-permute-done | bytes 155680 | tf_op jit(solution)/shard_map/ppermute | solution.py:589
  65.2 4.0 %collective-permute-done.23.refs_1_ = bf16[304,256]{1,0:T(8,128)(2,1)S(1)} collective-permute-done((bf16[304,256]{1,0:T(8,128)(2,1)S(1)}, bf16[304,256]{1,0:T(8,128)(2,1)S(1)}, u32[]{:S(2)}, u32[]{:S(2)}) %collective-permute-start.23) | collective-permute-done | bytes 155680 | tf_op jit(solution)/shard_map/ppermute | solution.py:589
  73.6 2.1 %collective-permute-start.27 = (bf16[160,256]{1,0:T(8,128)(2,1)S(1)}, bf16[160,256]{1,0:T(8,128)(2,1)S(1)}, u32[]{:S(2)}, u32[]{:S(2)}) collective-permute-start(bf16[160,256]{1,0:T(8,128)(2,1)S(1)} %get-tuple-element.124), channel_id=1, source_target_pairs={{0,16},{4,20},{8,24},{12,28},{16,0},{20,4},{24,8},{28,12},{1,17},{... | collective-permute-start | bytes 245768 | tf_op jit(solution)/shard_map/ppermute | solution.py:586
  75.7 1.6 %collective-permute-start.28 = (bf16[160,256]{1,0:T(8,128)(2,1)S(1)}, bf16[160,256]{1,0:T(8,128)(2,1)S(1)}, u32[]{:S(2)}, u32[]{:S(2)}) collective-permute-start(bf16[160,256]{1,0:T(8,128)(2,1)S(1)} %get-tuple-element.125), channel_id=1, source_target_pairs={{0,24},{4,28},{8,16},{12,20},{16,8},{20,12},{24,0},{28,4},{1,25},{... | collective-permute-start | bytes 245768 | tf_op jit(solution)/shard_map/ppermute | solution.py:586
  77.4 2.0 %collective-permute-start.29 = (bf16[144,256]{1,0:T(8,128)(2,1)S(1)}, bf16[144,256]{1,0:T(8,128)(2,1)S(1)}, u32[]{:S(2)}, u32[]{:S(2)}) collective-permute-start(bf16[144,256]{1,0:T(8,128)(2,1)S(1)} %get-tuple-element.126), channel_id=1, source_target_pairs={{0,8},{4,12},{8,0},{12,4},{16,24},{20,28},{24,16},{28,20},{1,9},{5... | collective-permute-start | bytes 221192 | tf_op jit(solution)/shard_map/ppermute | solution.py:586
  80.3 6.1 %collective-permute-done.29.refs_3_ = bf16[144,256]{1,0:T(8,128)(2,1)S(1)} collective-permute-done((bf16[144,256]{1,0:T(8,128)(2,1)S(1)}, bf16[144,256]{1,0:T(8,128)(2,1)S(1)}, u32[]{:S(2)}, u32[]{:S(2)}) %collective-permute-start.29) | collective-permute-done | bytes 73760 | tf_op jit(solution)/shard_map/ppermute | solution.py:586
  88.4 2.5 %collective-permute-start.33 = (bf16[272,256]{1,0:T(8,128)(2,1)S(1)}, bf16[272,256]{1,0:T(8,128)(2,1)S(1)}, u32[]{:S(2)}, u32[]{:S(2)}) collective-permute-start(bf16[272,256]{1,0:T(8,128)(2,1)S(1)} %get-tuple-element.132), channel_id=1, source_target_pairs={{0,8},{4,12},{8,0},{12,4},{16,24},{20,28},{24,16},{28,20},{1,9},{5... | collective-permute-start | bytes 417800 | tf_op jit(solution)/shard_map/ppermute | solution.py:586
  90.8 1.3 %collective-permute-start.38 = (bf16[160,256]{1,0:T(8,128)(2,1)S(1)}, bf16[160,256]{1,0:T(8,128)(2,1)S(1)}, u32[]{:S(2)}, u32[]{:S(2)}) collective-permute-start(bf16[160,256]{1,0:T(8,128)(2,1)S(1)} %get-tuple-element.135), channel_id=1, source_target_pairs={{0,24},{4,28},{8,16},{12,20},{16,8},{20,12},{24,0},{28,4},{1,25},{... | collective-permute-start | bytes 245768 | tf_op jit(solution)/shard_map/ppermute | solution.py:586
  92.3 2.5 %collective-permute-done.35.refs_3_ = bf16[144,256]{1,0:T(8,128)(2,1)S(1)} collective-permute-done((bf16[144,256]{1,0:T(8,128)(2,1)S(1)}, bf16[144,256]{1,0:T(8,128)(2,1)S(1)}, u32[]{:S(2)}, u32[]{:S(2)}) %collective-permute-start.35) | collective-permute-done | bytes 73760 | tf_op jit(solution)/shard_map/ppermute | solution.py:586
  95.2 1.6 %collective-permute-start.34 = (bf16[32,256]{1,0:T(8,128)(2,1)S(1)}, bf16[32,256]{1,0:T(8,128)(2,1)S(1)}, u32[]{:S(2)}, u32[]{:S(2)}) collective-permute-start(bf16[32,256]{1,0:T(8,128)(2,1)S(1)} %get-tuple-element.133), channel_id=1, source_target_pairs={{0,8},{4,12},{8,0},{12,4},{16,24},{20,28},{24,16},{28,20},{1,9},{5... | collective-permute-start | bytes 49160 | tf_op jit(solution)/shard_map/ppermute | solution.py:586
  96.8 2.8 %collective-permute-done.34.refs_2_ = bf16[32,256]{1,0:T(8,128)(2,1)S(1)} collective-permute-done((bf16[32,256]{1,0:T(8,128)(2,1)S(1)}, bf16[32,256]{1,0:T(8,128)(2,1)S(1)}, u32[]{:S(2)}, u32[]{:S(2)}) %collective-permute-start.34) | collective-permute-done | bytes 16416 | tf_op jit(solution)/shard_map/ppermute | solution.py:586
  103.1 2.0 %collective-permute-start.41 = (bf16[304,128]{1,0:T(8,128)(2,1)S(1)}, bf16[304,128]{1,0:T(8,128)(2,1)S(1)}, u32[]{:S(2)}, u32[]{:S(2)}) collective-permute-start(bf16[304,128]{1,0:T(8,128)(2,1)S(1)} %get-tuple-element.139), channel_id=1, source_target_pairs={{0,3},{1,2},{2,1},{3,0},{4,7},{5,6},{6,5},{7,4},{8,11},{9,10},{10,... | collective-permute-start | bytes 233480 | tf_op jit(solution)/shard_map/ppermute | solution.py:589
  107.0 1.7 %collective-permute-done.41.refs_1_ = bf16[304,128]{1,0:T(8,128)(2,1)S(1)} collective-permute-done((bf16[304,128]{1,0:T(8,128)(2,1)S(1)}, bf16[304,128]{1,0:T(8,128)(2,1)S(1)}, u32[]{:S(2)}, u32[]{:S(2)}) %collective-permute-start.41) | collective-permute-done | bytes 77856 | tf_op jit(solution)/shard_map/ppermute | solution.py:589
  108.7 1.6 %collective-permute-done.42.refs_2_ = bf16[304,128]{1,0:T(8,128)(2,1)S(1)} collective-permute-done((bf16[304,128]{1,0:T(8,128)(2,1)S(1)}, bf16[304,128]{1,0:T(8,128)(2,1)S(1)}, u32[]{:S(2)}, u32[]{:S(2)}) %collective-permute-start.42) | collective-permute-done | bytes 77856 | tf_op jit(solution)/shard_map/ppermute | solution.py:589
  (98 shorter events, 30.2 us)
Async XLA Ops:
  6.2 19.1 %collective-permute-start.6 = (bf16[4,4,128,256]{3,2,1,0:T(8,128)(2,1)}, bf16[4,4,128,256]{3,2,1,0:T(8,128)(2,1)S(1)}, u32[]{:S(2)}, u32[]{:S(2)}) collective-permute-start(bf16[4,4,128,256]{3,2,1,0:T(8,128)(2,1)} %get-tuple-element.84), channel_id=1, source_target_pairs={{0,4},{4,0},{8,12},{12,8},{16,20},{20,16},{24,28},{28,24},{1,5},{5... | collective-permute-start | bytes 3145736 | tf_op jit(solution)/shard_map/ppermute | solution.py:592
  6.9 7.4 %collective-permute-start = (bf16[304,256]{1,0:T(8,128)(2,1)}, bf16[304,256]{1,0:T(8,128)(2,1)S(1)}, u32[]{:S(2)}, u32[]{:S(2)}) collective-permute-start(bf16[304,256]{1,0:T(8,128)(2,1)} %get-tuple-element.76.refs_0_), channel_id=1, source_target_pairs={{0,1},{1,0},{2,3},{3,2},{4,5},{5,4},{6,7},{7,6},{8,9},{9,8},{10,11... | collective-permute-start | bytes 466952 | tf_op jit(solution)/shard_map/ppermute | solution.py:589
  9.6 6.1 %collective-permute-start.1 = (bf16[304,256]{1,0:T(8,128)(2,1)}, bf16[304,256]{1,0:T(8,128)(2,1)S(1)}, u32[]{:S(2)}, u32[]{:S(2)}) collective-permute-start(bf16[304,256]{1,0:T(8,128)(2,1)} %get-tuple-element.77.refs_1_), channel_id=1, source_target_pairs={{0,2},{1,3},{2,0},{3,1},{4,6},{5,7},{6,4},{7,5},{8,10},{9,11},{10,... | collective-permute-start | bytes 466952 | tf_op jit(solution)/shard_map/ppermute | solution.py:589
  15.8 5.3 %collective-permute-start.2 = (bf16[304,256]{1,0:T(8,128)(2,1)S(1)}, bf16[304,256]{1,0:T(8,128)(2,1)S(1)}, u32[]{:S(2)}, u32[]{:S(2)}) collective-permute-start(bf16[304,256]{1,0:T(8,128)(2,1)S(1)} %get-tuple-element.80.refs_0_), channel_id=1, source_target_pairs={{0,2},{1,3},{2,0},{3,1},{4,6},{5,7},{6,4},{7,5},{8,10},{9,11},{10,... | collective-permute-start | bytes 466952 | tf_op jit(solution)/shard_map/ppermute | solution.py:589
  17.3 5.2 %collective-permute-start.3 = (bf16[304,256]{1,0:T(8,128)(2,1)S(1)}, bf16[304,256]{1,0:T(8,128)(2,1)S(1)}, u32[]{:S(2)}, u32[]{:S(2)}) collective-permute-start(bf16[304,256]{1,0:T(8,128)(2,1)S(1)} %get-tuple-element.81.refs_2_), channel_id=1, source_target_pairs={{0,1},{1,0},{2,3},{3,2},{4,5},{5,4},{6,7},{7,6},{8,9},{9,8},{10,11... | collective-permute-start | bytes 466952 | tf_op jit(solution)/shard_map/ppermute | solution.py:589
  25.9 6.6 %collective-permute-start.11 = (bf16[144,256]{1,0:T(8,128)(2,1)S(1)}, bf16[144,256]{1,0:T(8,128)(2,1)S(1)}, u32[]{:S(2)}, u32[]{:S(2)}) collective-permute-start(bf16[144,256]{1,0:T(8,128)(2,1)S(1)} %get-tuple-element.99), channel_id=1, source_target_pairs={{0,8},{4,12},{8,0},{12,4},{16,24},{20,28},{24,16},{28,20},{1,9},{5... | collective-permute-start | bytes 221192 | tf_op jit(solution)/shard_map/ppermute | solution.py:586
  27.5 11.0 %collective-permute-start.7 = (bf16[160,256]{1,0:T(8,128)(2,1)S(1)}, bf16[160,256]{1,0:T(8,128)(2,1)S(1)}, u32[]{:S(2)}, u32[]{:S(2)}) collective-permute-start(bf16[160,256]{1,0:T(8,128)(2,1)S(1)} %get-tuple-element.94), channel_id=1, source_target_pairs={{0,16},{4,20},{8,24},{12,28},{16,0},{20,4},{24,8},{28,12},{1,17},{... | collective-permute-start | bytes 245768 | tf_op jit(solution)/shard_map/ppermute | solution.py:586
  30.1 8.5 %collective-permute-start.8 = (bf16[160,256]{1,0:T(8,128)(2,1)S(1)}, bf16[160,256]{1,0:T(8,128)(2,1)S(1)}, u32[]{:S(2)}, u32[]{:S(2)}) collective-permute-start(bf16[160,256]{1,0:T(8,128)(2,1)S(1)} %get-tuple-element.95), channel_id=1, source_target_pairs={{0,24},{4,28},{8,16},{12,20},{16,8},{20,12},{24,0},{28,4},{1,25},{... | collective-permute-start | bytes 245768 | tf_op jit(solution)/shard_map/ppermute | solution.py:586
  30.5 8.1 %collective-permute-start.10 = (bf16[160,256]{1,0:T(8,128)(2,1)S(1)}, bf16[160,256]{1,0:T(8,128)(2,1)S(1)}, u32[]{:S(2)}, u32[]{:S(2)}) collective-permute-start(bf16[160,256]{1,0:T(8,128)(2,1)S(1)} %get-tuple-element.97), channel_id=1, source_target_pairs={{0,8},{4,12},{8,0},{12,4},{16,24},{20,28},{24,16},{28,20},{1,9},{5... | collective-permute-start | bytes 245768 | tf_op jit(solution)/shard_map/ppermute | solution.py:586
  31.0 7.5 %collective-permute-start.9 = (bf16[144,256]{1,0:T(8,128)(2,1)S(1)}, bf16[144,256]{1,0:T(8,128)(2,1)S(1)}, u32[]{:S(2)}, u32[]{:S(2)}) collective-permute-start(bf16[144,256]{1,0:T(8,128)(2,1)S(1)} %get-tuple-element.96), channel_id=1, source_target_pairs={{0,8},{4,12},{8,0},{12,4},{16,24},{20,28},{24,16},{28,20},{1,9},{5... | collective-permute-start | bytes 221192 | tf_op jit(solution)/shard_map/ppermute | solution.py:586
  32.5 7.8 %collective-permute-start.12 = (bf16[144,256]{1,0:T(8,128)(2,1)S(1)}, bf16[144,256]{1,0:T(8,128)(2,1)S(1)}, u32[]{:S(2)}, u32[]{:S(2)}) collective-permute-start(bf16[144,256]{1,0:T(8,128)(2,1)S(1)} %shard_map.110), channel_id=1, source_target_pairs={{0,16},{4,20},{8,24},{12,28},{16,0},{20,4},{24,8},{28,12},{1,17},{... | collective-permute-start | bytes 221192 | tf_op jit(solution)/shard_map/ppermute | solution.py:586
  40.5 6.4 %collective-permute-start.15 = (bf16[144,256]{1,0:T(8,128)(2,1)S(1)}, bf16[144,256]{1,0:T(8,128)(2,1)S(1)}, u32[]{:S(2)}, u32[]{:S(2)}) collective-permute-start(bf16[144,256]{1,0:T(8,128)(2,1)S(1)} %get-tuple-element.103), channel_id=1, source_target_pairs={{0,16},{4,20},{8,24},{12,28},{16,0},{20,4},{24,8},{28,12},{1,17},{... | collective-permute-start | bytes 221192 | tf_op jit(solution)/shard_map/ppermute | solution.py:586
  42.6 11.7 %collective-permute-start.13 = (bf16[272,256]{1,0:T(8,128)(2,1)S(1)}, bf16[272,256]{1,0:T(8,128)(2,1)S(1)}, u32[]{:S(2)}, u32[]{:S(2)}) collective-permute-start(bf16[272,256]{1,0:T(8,128)(2,1)S(1)} %get-tuple-element.101), channel_id=1, source_target_pairs={{0,8},{4,12},{8,0},{12,4},{16,24},{20,28},{24,16},{28,20},{1,9},{5... | collective-permute-start | bytes 417800 | tf_op jit(solution)/shard_map/ppermute | solution.py:586
  45.0 9.3 %collective-permute-start.18 = (bf16[160,256]{1,0:T(8,128)(2,1)S(1)}, bf16[160,256]{1,0:T(8,128)(2,1)S(1)}, u32[]{:S(2)}, u32[]{:S(2)}) collective-permute-start(bf16[160,256]{1,0:T(8,128)(2,1)S(1)} %get-tuple-element.104), channel_id=1, source_target_pairs={{0,24},{4,28},{8,16},{12,20},{16,8},{20,12},{24,0},{28,4},{1,25},{... | collective-permute-start | bytes 245768 | tf_op jit(solution)/shard_map/ppermute | solution.py:586
  45.0 9.3 %collective-permute-start.16 = (bf16[160,256]{1,0:T(8,128)(2,1)S(1)}, bf16[160,256]{1,0:T(8,128)(2,1)S(1)}, u32[]{:S(2)}, u32[]{:S(2)}) collective-permute-start(bf16[160,256]{1,0:T(8,128)(2,1)S(1)} %get-tuple-element.104), channel_id=1, source_target_pairs={{0,16},{4,20},{8,24},{12,28},{16,0},{20,4},{24,8},{28,12},{1,17},{... | collective-permute-start | bytes 245768 | tf_op jit(solution)/shard_map/ppermute | solution.py:586
  46.9 7.4 %collective-permute-start.17 = (bf16[144,256]{1,0:T(8,128)(2,1)S(1)}, bf16[144,256]{1,0:T(8,128)(2,1)S(1)}, u32[]{:S(2)}, u32[]{:S(2)}) collective-permute-start(bf16[144,256]{1,0:T(8,128)(2,1)S(1)} %collective-permute-done.15.refs_3_), channel_id=1, source_target_pairs={{0,8},{4,12},{8,0},{12,4},{16,24},{20,28},{24,16},{28,20},{1,9},{5... | collective-permute-start | bytes 221192 | tf_op jit(solution)/shard_map/ppermute | solution.py:586
  56.6 6.3 %collective-permute-start.21 = (bf16[304,256]{1,0:T(8,128)(2,1)S(1)}, bf16[304,256]{1,0:T(8,128)(2,1)S(1)}, u32[]{:S(2)}, u32[]{:S(2)}) collective-permute-start(bf16[304,256]{1,0:T(8,128)(2,1)S(1)} %get-tuple-element.107.one), channel_id=1, source_target_pairs={{0,1},{1,0},{2,3},{3,2},{4,5},{5,4},{6,7},{7,6},{8,9},{9,8},{10,11... | collective-permute-start | bytes 466952 | tf_op jit(solution)/shard_map/ppermute | solution.py:589
  57.8 5.9 %collective-permute-start.22 = (bf16[304,256]{1,0:T(8,128)(2,1)S(1)}, bf16[304,256]{1,0:T(8,128)(2,1)S(1)}, u32[]{:S(2)}, u32[]{:S(2)}) collective-permute-start(bf16[304,256]{1,0:T(8,128)(2,1)S(1)} %get-tuple-element.108.two), channel_id=1, source_target_pairs={{0,2},{1,3},{2,0},{3,1},{4,6},{5,7},{6,4},{7,5},{8,10},{9,11},{10,... | collective-permute-start | bytes 466952 | tf_op jit(solution)/shard_map/ppermute | solution.py:589
  63.9 5.3 %collective-permute-start.23 = (bf16[304,256]{1,0:T(8,128)(2,1)S(1)}, bf16[304,256]{1,0:T(8,128)(2,1)S(1)}, u32[]{:S(2)}, u32[]{:S(2)}) collective-permute-start(bf16[304,256]{1,0:T(8,128)(2,1)S(1)} %get-tuple-element.109.refs_0_), channel_id=1, source_target_pairs={{0,2},{1,3},{2,0},{3,1},{4,6},{5,7},{6,4},{7,5},{8,10},{9,11},{10,... | collective-permute-start | bytes 466952 | tf_op jit(solution)/shard_map/ppermute | solution.py:589
  64.2 5.2 %collective-permute-start.24 = (bf16[304,256]{1,0:T(8,128)(2,1)S(1)}, bf16[304,256]{1,0:T(8,128)(2,1)S(1)}, u32[]{:S(2)}, u32[]{:S(2)}) collective-permute-start(bf16[304,256]{1,0:T(8,128)(2,1)S(1)} %get-tuple-element.110.refs_2_), channel_id=1, source_target_pairs={{0,1},{1,0},{2,3},{3,2},{4,5},{5,4},{6,7},{7,6},{8,9},{9,8},{10,11... | collective-permute-start | bytes 466952 | tf_op jit(solution)/shard_map/ppermute | solution.py:589
  72.9 6.5 %collective-permute-start.31 = (bf16[144,256]{1,0:T(8,128)(2,1)S(1)}, bf16[144,256]{1,0:T(8,128)(2,1)S(1)}, u32[]{:S(2)}, u32[]{:S(2)}) collective-permute-start(bf16[144,256]{1,0:T(8,128)(2,1)S(1)} %get-tuple-element.129), channel_id=1, source_target_pairs={{0,8},{4,12},{8,0},{12,4},{16,24},{20,28},{24,16},{28,20},{1,9},{5... | collective-permute-start | bytes 221192 | tf_op jit(solution)/shard_map/ppermute | solution.py:586
  73.6 12.7 %collective-permute-start.27 = (bf16[160,256]{1,0:T(8,128)(2,1)S(1)}, bf16[160,256]{1,0:T(8,128)(2,1)S(1)}, u32[]{:S(2)}, u32[]{:S(2)}) collective-permute-start(bf16[160,256]{1,0:T(8,128)(2,1)S(1)} %get-tuple-element.124), channel_id=1, source_target_pairs={{0,16},{4,20},{8,24},{12,28},{16,0},{20,4},{24,8},{28,12},{1,17},{... | collective-permute-start | bytes 245768 | tf_op jit(solution)/shard_map/ppermute | solution.py:586
  75.7 10.6 %collective-permute-start.28 = (bf16[160,256]{1,0:T(8,128)(2,1)S(1)}, bf16[160,256]{1,0:T(8,128)(2,1)S(1)}, u32[]{:S(2)}, u32[]{:S(2)}) collective-permute-start(bf16[160,256]{1,0:T(8,128)(2,1)S(1)} %get-tuple-element.125), channel_id=1, source_target_pairs={{0,24},{4,28},{8,16},{12,20},{16,8},{20,12},{24,0},{28,4},{1,25},{... | collective-permute-start | bytes 245768 | tf_op jit(solution)/shard_map/ppermute | solution.py:586
  77.4 9.0 %collective-permute-start.30 = (bf16[160,256]{1,0:T(8,128)(2,1)S(1)}, bf16[160,256]{1,0:T(8,128)(2,1)S(1)}, u32[]{:S(2)}, u32[]{:S(2)}) collective-permute-start(bf16[160,256]{1,0:T(8,128)(2,1)S(1)} %get-tuple-element.127), channel_id=1, source_target_pairs={{0,8},{4,12},{8,0},{12,4},{16,24},{20,28},{24,16},{28,20},{1,9},{5... | collective-permute-start | bytes 245768 | tf_op jit(solution)/shard_map/ppermute | solution.py:586
  77.4 9.0 %collective-permute-start.29 = (bf16[144,256]{1,0:T(8,128)(2,1)S(1)}, bf16[144,256]{1,0:T(8,128)(2,1)S(1)}, u32[]{:S(2)}, u32[]{:S(2)}) collective-permute-start(bf16[144,256]{1,0:T(8,128)(2,1)S(1)} %get-tuple-element.126), channel_id=1, source_target_pairs={{0,8},{4,12},{8,0},{12,4},{16,24},{20,28},{24,16},{28,20},{1,9},{5... | collective-permute-start | bytes 221192 | tf_op jit(solution)/shard_map/ppermute | solution.py:586
  79.4 7.9 %collective-permute-start.32 = (bf16[144,256]{1,0:T(8,128)(2,1)S(1)}, bf16[144,256]{1,0:T(8,128)(2,1)S(1)}, u32[]{:S(2)}, u32[]{:S(2)}) collective-permute-start(bf16[144,256]{1,0:T(8,128)(2,1)S(1)} %shard_map.120), channel_id=1, source_target_pairs={{0,16},{4,20},{8,24},{12,28},{16,0},{20,4},{24,8},{28,12},{1,17},{... | collective-permute-start | bytes 221192 | tf_op jit(solution)/shard_map/ppermute | solution.py:586
  87.7 7.1 %collective-permute-start.35 = (bf16[144,256]{1,0:T(8,128)(2,1)S(1)}, bf16[144,256]{1,0:T(8,128)(2,1)S(1)}, u32[]{:S(2)}, u32[]{:S(2)}) collective-permute-start(bf16[144,256]{1,0:T(8,128)(2,1)S(1)} %get-tuple-element.134), channel_id=1, source_target_pairs={{0,16},{4,20},{8,24},{12,28},{16,0},{20,4},{24,8},{28,12},{1,17},{... | collective-permute-start | bytes 221192 | tf_op jit(solution)/shard_map/ppermute | solution.py:586
  88.4 12.4 %collective-permute-start.33 = (bf16[272,256]{1,0:T(8,128)(2,1)S(1)}, bf16[272,256]{1,0:T(8,128)(2,1)S(1)}, u32[]{:S(2)}, u32[]{:S(2)}) collective-permute-start(bf16[272,256]{1,0:T(8,128)(2,1)S(1)} %get-tuple-element.132), channel_id=1, source_target_pairs={{0,8},{4,12},{8,0},{12,4},{16,24},{20,28},{24,16},{28,20},{1,9},{5... | collective-permute-start | bytes 417800 | tf_op jit(solution)/shard_map/ppermute | solution.py:586
  90.8 8.8 %collective-permute-start.38 = (bf16[160,256]{1,0:T(8,128)(2,1)S(1)}, bf16[160,256]{1,0:T(8,128)(2,1)S(1)}, u32[]{:S(2)}, u32[]{:S(2)}) collective-permute-start(bf16[160,256]{1,0:T(8,128)(2,1)S(1)} %get-tuple-element.135), channel_id=1, source_target_pairs={{0,24},{4,28},{8,16},{12,20},{16,8},{20,12},{24,0},{28,4},{1,25},{... | collective-permute-start | bytes 245768 | tf_op jit(solution)/shard_map/ppermute | solution.py:586
  92.1 8.6 %collective-permute-start.36 = (bf16[160,256]{1,0:T(8,128)(2,1)S(1)}, bf16[160,256]{1,0:T(8,128)(2,1)S(1)}, u32[]{:S(2)}, u32[]{:S(2)}) collective-permute-start(bf16[160,256]{1,0:T(8,128)(2,1)S(1)} %get-tuple-element.135), channel_id=1, source_target_pairs={{0,16},{4,20},{8,24},{12,28},{16,0},{20,4},{24,8},{28,12},{1,17},{... | collective-permute-start | bytes 245768 | tf_op jit(solution)/shard_map/ppermute | solution.py:586
  94.8 6.0 %collective-permute-start.37 = (bf16[144,256]{1,0:T(8,128)(2,1)S(1)}, bf16[144,256]{1,0:T(8,128)(2,1)S(1)}, u32[]{:S(2)}, u32[]{:S(2)}) collective-permute-start(bf16[144,256]{1,0:T(8,128)(2,1)S(1)} %collective-permute-done.35.refs_3_), channel_id=1, source_target_pairs={{0,8},{4,12},{8,0},{12,4},{16,24},{20,28},{24,16},{28,20},{1,9},{5... | collective-permute-start | bytes 221192 | tf_op jit(solution)/shard_map/ppermute | solution.py:586
  103.1 5.6 %collective-permute-start.41 = (bf16[304,128]{1,0:T(8,128)(2,1)S(1)}, bf16[304,128]{1,0:T(8,128)(2,1)S(1)}, u32[]{:S(2)}, u32[]{:S(2)}) collective-permute-start(bf16[304,128]{1,0:T(8,128)(2,1)S(1)} %get-tuple-element.139), channel_id=1, source_target_pairs={{0,3},{1,2},{2,1},{3,0},{4,7},{5,6},{6,5},{7,4},{8,11},{9,10},{10,... | collective-permute-start | bytes 233480 | tf_op jit(solution)/shard_map/ppermute | solution.py:589
  (18 other events, 80.3 us)

commit v22 on v19

--- a/solution.py
+++ b/solution.py
@@ -543,12 +543,12 @@
     half_rows = [struct((rows, lanes // 2), BF16)] * 2
     wide = rows + levp - lev + 7
     spread = pltpu.VMEM((wide // 8 * 8, lanes), F32)
-    some = rows // 32 * 16
+    some = rows // 38 * 16
     rest = rows - some
     via = chips == 4
     if via:
         one, two = (0, some), (some, rest)
-        most = rows - 32
+        most = rows - 64
         near_parts = [(0, most), (most, rows - most)]
         plan = [(0, 0, rows), *((1, *part) for part in near_parts)]
         plan += [(2, *one), (2, *two), (3, *one), (3, *two)]

time: 112 us -> 112 us (level)
    ppermute x24, waiting for transfers between devices: 26.1 us -> 27.9 us  [along(): return lax.ppermute(x, 'slab', [(s, s ^ 2 * i) for s in range(n_slab)])]
    ppermute x11, waiting for transfers between devices: 19.8 us -> 18.6 us  [plane(): return lax.ppermute(x, 'obs', [(o, o ^ i) for o in range(n_obs)])]
  transfers between devices with their start and end apart: 40 -> 40, of which waited for: 25 -> 22; matrix products, arithmetic and copies ran while one was open for 0% -> 0% of each run, Pallas kernels for 4% -> 4%
where the time goes in v22:
time: 112 us
  waiting for transfers between devices  50.7 us (45%)
  starting transfers between devices  43.3 us (39%)
  Pallas kernels  14.4 us (13%)
  local copies, waits for them, and re-layouts  2.09 us (2%)
  between operations  1.6 us (1%)
    ppermute x24, starting transfers between devices, along(): return lax.ppermute(x, 'slab', [(s, s ^ 2 * i) for s in range(n_slab)])  28.8 us
    ppermute x24, waiting for transfers between devices, along(): return lax.ppermute(x, 'slab', [(s, s ^ 2 * i) for s in range(n_slab)])  27.9 us
    ppermute x11, waiting for transfers between devices, plane(): return lax.ppermute(x, 'obs', [(o, o ^ i) for o in range(n_obs)])  18.6 us
    pallas_call x23, Pallas kernels, call(): pl.pallas_call(kernel, out_shape=outs, in_specs=[space] * len(args), out_...  14.4 us
    ppermute x11, starting transfers between devices, plane(): return lax.ppermute(x, 'obs', [(o, o ^ i) for o in range(n_obs)])  13.6 us
    ppermute x5, waiting for transfers between devices, swap(): return lax.ppermute(x, 'slab', [(s, s ^ 1) for s in range(n_slab)])  4.24 us
  transfers between devices with their start and end apart: 40, of which 22 were waited for; matrix products, arithmetic and copies ran while one was open for 0% of the time, Pallas kernels for 4%

profile of v22, /device:TPU:0, one launch (start us, length us, event | category | flops | bytes accessed | tf_op | source)
XLA Modules:
  0.0 112.2 jit_solution(9565684762961108396)
XLA Ops:
  1.3 4.9 %shard_map.104 = (bf16[4,4,128,256]{3,2,1,0:T(8,128)(2,1)}, bf16[4,4,128,256]{3,2,1,0:T(8,128)(2,1)}, bf16[304,256]{1,0:T(8,128)(2,1)}, bf16[304,256]{1,0:T(8,128)(2,1)}) custom-call(s32[4]{0:T(128)} %seeds_in.1, s32[1,1,32]{2,1,0:T(1,128)} %ids_in.1, s32[1,1,32]{2,1,0:T(1,128)} %cols_in.1, s32[1,1]{1,0:T(1,128)S(6)} %copy.16.count_in, f32[1,128]{1,0:T(1,128)} %refs_4_.1, ...), custom_call_target="tpu_custom_call" | custom-call | flops 637534208 | bytes 5735188 | tf_op jit(solution)/shard_map/pallas_call | solution.py:23
  6.8 2.6 %collective-permute-start = (bf16[304,256]{1,0:T(8,128)(2,1)}, bf16[304,256]{1,0:T(8,128)(2,1)S(1)}, u32[]{:S(2)}, u32[]{:S(2)}) collective-permute-start(bf16[304,256]{1,0:T(8,128)(2,1)} %get-tuple-element.70.refs_0_), channel_id=1, source_target_pairs={{0,1},{1,0},{2,3},{3,2},{4,5},{5,4},{6,7},{7,6},{8,9},{9,8},{10,11... | collective-permute-start | bytes 466952 | tf_op jit(solution)/shard_map/ppermute | solution.py:576
  9.4 1.5 %collective-permute-start.1 = (bf16[304,256]{1,0:T(8,128)(2,1)}, bf16[304,256]{1,0:T(8,128)(2,1)S(1)}, u32[]{:S(2)}, u32[]{:S(2)}) collective-permute-start(bf16[304,256]{1,0:T(8,128)(2,1)} %get-tuple-element.71.refs_1_), channel_id=1, source_target_pairs={{0,2},{1,3},{2,0},{3,1},{4,6},{5,7},{6,4},{7,5},{8,10},{9,11},{10,... | collective-permute-start | bytes 466952 | tf_op jit(solution)/shard_map/ppermute | solution.py:576
  14.3 1.5 %collective-permute-done.1.two_more = bf16[304,256]{1,0:T(8,128)(2,1)S(1)} collective-permute-done((bf16[304,256]{1,0:T(8,128)(2,1)}, bf16[304,256]{1,0:T(8,128)(2,1)S(1)}, u32[]{:S(2)}, u32[]{:S(2)}) %collective-permute-start.1) | collective-permute-done | bytes 155680 | tf_op jit(solution)/shard_map/ppermute | solution.py:576
  15.8 1.6 %collective-permute-start.2 = (bf16[304,256]{1,0:T(8,128)(2,1)S(1)}, bf16[304,256]{1,0:T(8,128)(2,1)S(1)}, u32[]{:S(2)}, u32[]{:S(2)}) collective-permute-start(bf16[304,256]{1,0:T(8,128)(2,1)S(1)} %get-tuple-element.74.refs_0_), channel_id=1, source_target_pairs={{0,2},{1,3},{2,0},{3,1},{4,6},{5,7},{6,4},{7,5},{8,10},{9,11},{10,... | collective-permute-start | bytes 466952 | tf_op jit(solution)/shard_map/ppermute | solution.py:576
  18.6 2.5 %collective-permute-done.2.refs_1_ = bf16[304,256]{1,0:T(8,128)(2,1)S(1)} collective-permute-done((bf16[304,256]{1,0:T(8,128)(2,1)S(1)}, bf16[304,256]{1,0:T(8,128)(2,1)S(1)}, u32[]{:S(2)}, u32[]{:S(2)}) %collective-permute-start.2) | collective-permute-done | bytes 155680 | tf_op jit(solution)/shard_map/ppermute | solution.py:576
  21.2 1.5 %collective-permute-done.3.refs_3_ = bf16[304,256]{1,0:T(8,128)(2,1)S(1)} collective-permute-done((bf16[304,256]{1,0:T(8,128)(2,1)S(1)}, bf16[304,256]{1,0:T(8,128)(2,1)S(1)}, u32[]{:S(2)}, u32[]{:S(2)}) %collective-permute-start.3) | collective-permute-done | bytes 155680 | tf_op jit(solution)/shard_map/ppermute | solution.py:576
  25.9 1.7 %collective-permute-start.10 = (bf16[128,256]{1,0:T(8,128)(2,1)S(1)}, bf16[128,256]{1,0:T(8,128)(2,1)S(1)}, u32[]{:S(2)}, u32[]{:S(2)}) collective-permute-start(bf16[128,256]{1,0:T(8,128)(2,1)S(1)} %get-tuple-element.92), channel_id=1, source_target_pairs={{0,8},{4,12},{8,0},{12,4},{16,24},{20,28},{24,16},{28,20},{1,9},{5... | collective-permute-start | bytes 196616 | tf_op jit(solution)/shard_map/ppermute | solution.py:573
  27.5 2.5 %collective-permute-start.6 = (bf16[176,256]{1,0:T(8,128)(2,1)S(1)}, bf16[176,256]{1,0:T(8,128)(2,1)S(1)}, u32[]{:S(2)}, u32[]{:S(2)}) collective-permute-start(bf16[176,256]{1,0:T(8,128)(2,1)S(1)} %get-tuple-element.87), channel_id=1, source_target_pairs={{0,16},{4,20},{8,24},{12,28},{16,0},{20,4},{24,8},{28,12},{1,17},{... | collective-permute-start | bytes 270344 | tf_op jit(solution)/shard_map/ppermute | solution.py:573
  31.0 1.3 %collective-permute-start.8 = (bf16[128,256]{1,0:T(8,128)(2,1)S(1)}, bf16[128,256]{1,0:T(8,128)(2,1)S(1)}, u32[]{:S(2)}, u32[]{:S(2)}) collective-permute-start(bf16[128,256]{1,0:T(8,128)(2,1)S(1)} %get-tuple-element.89), channel_id=1, source_target_pairs={{0,8},{4,12},{8,0},{12,4},{16,24},{20,28},{24,16},{28,20},{1,9},{5... | collective-permute-start | bytes 196616 | tf_op jit(solution)/shard_map/ppermute | solution.py:573
  32.4 2.2 %collective-permute-start.11 = (bf16[128,256]{1,0:T(8,128)(2,1)S(1)}, bf16[128,256]{1,0:T(8,128)(2,1)S(1)}, u32[]{:S(2)}, u32[]{:S(2)}) collective-permute-start(bf16[128,256]{1,0:T(8,128)(2,1)S(1)} %shard_map.110), channel_id=1, source_target_pairs={{0,16},{4,20},{8,24},{12,28},{16,0},{20,4},{24,8},{28,12},{1,17},{... | collective-permute-start | bytes 196616 | tf_op jit(solution)/shard_map/ppermute | solution.py:573
  34.7 4.0 %collective-permute-done.8.refs_3_ = bf16[128,256]{1,0:T(8,128)(2,1)S(1)} collective-permute-done((bf16[128,256]{1,0:T(8,128)(2,1)S(1)}, bf16[128,256]{1,0:T(8,128)(2,1)S(1)}, u32[]{:S(2)}, u32[]{:S(2)}) %collective-permute-start.8) | collective-permute-done | bytes 65568 | tf_op jit(solution)/shard_map/ppermute | solution.py:573
  38.8 2.7 %collective-permute-done.11.refs_5_ = bf16[128,256]{1,0:T(8,128)(2,1)S(1)} collective-permute-done((bf16[128,256]{1,0:T(8,128)(2,1)S(1)}, bf16[128,256]{1,0:T(8,128)(2,1)S(1)}, u32[]{:S(2)}, u32[]{:S(2)}) %collective-permute-start.11) | collective-permute-done | bytes 65568 | tf_op jit(solution)/shard_map/ppermute | solution.py:573
  42.5 2.2 %collective-permute-start.12 = (bf16[240,256]{1,0:T(8,128)(2,1)S(1)}, bf16[240,256]{1,0:T(8,128)(2,1)S(1)}, u32[]{:S(2)}, u32[]{:S(2)}) collective-permute-start(bf16[240,256]{1,0:T(8,128)(2,1)S(1)} %get-tuple-element.94), channel_id=1, source_target_pairs={{0,8},{4,12},{8,0},{12,4},{16,24},{20,28},{24,16},{28,20},{1,9},{5... | collective-permute-start | bytes 368648 | tf_op jit(solution)/shard_map/ppermute | solution.py:573
  44.6 1.4 %collective-permute-start.17 = (bf16[176,256]{1,0:T(8,128)(2,1)S(1)}, bf16[176,256]{1,0:T(8,128)(2,1)S(1)}, u32[]{:S(2)}, u32[]{:S(2)}) collective-permute-start(bf16[176,256]{1,0:T(8,128)(2,1)S(1)} %get-tuple-element.97), channel_id=1, source_target_pairs={{0,24},{4,28},{8,16},{12,20},{16,8},{20,12},{24,0},{28,4},{1,25},{... | collective-permute-start | bytes 270344 | tf_op jit(solution)/shard_map/ppermute | solution.py:573
  46.1 3.3 %collective-permute-done.14.refs_3_ = bf16[128,256]{1,0:T(8,128)(2,1)S(1)} collective-permute-done((bf16[128,256]{1,0:T(8,128)(2,1)S(1)}, bf16[128,256]{1,0:T(8,128)(2,1)S(1)}, u32[]{:S(2)}, u32[]{:S(2)}) %collective-permute-start.14) | collective-permute-done | bytes 65568 | tf_op jit(solution)/shard_map/ppermute | solution.py:573
  49.4 2.0 %collective-permute-start.13 = (bf16[64,256]{1,0:T(8,128)(2,1)S(1)}, bf16[64,256]{1,0:T(8,128)(2,1)S(1)}, u32[]{:S(2)}, u32[]{:S(2)}) collective-permute-start(bf16[64,256]{1,0:T(8,128)(2,1)S(1)} %get-tuple-element.95), channel_id=1, source_target_pairs={{0,8},{4,12},{8,0},{12,4},{16,24},{20,28},{24,16},{28,20},{1,9},{5... | collective-permute-start | bytes 98312 | tf_op jit(solution)/shard_map/ppermute | solution.py:573
  51.5 3.6 %collective-permute-done.13.refs_2_ = bf16[64,256]{1,0:T(8,128)(2,1)S(1)} collective-permute-done((bf16[64,256]{1,0:T(8,128)(2,1)S(1)}, bf16[64,256]{1,0:T(8,128)(2,1)S(1)}, u32[]{:S(2)}, u32[]{:S(2)}) %collective-permute-start.13) | collective-permute-done | bytes 32800 | tf_op jit(solution)/shard_map/ppermute | solution.py:573
  58.7 4.8 %collective-permute-done.19.one_more = bf16[304,256]{1,0:T(8,128)(2,1)S(1)} collective-permute-done((bf16[304,256]{1,0:T(8,128)(2,1)S(1)}, bf16[304,256]{1,0:T(8,128)(2,1)S(1)}, u32[]{:S(2)}, u32[]{:S(2)}) %collective-permute-start.19) | collective-permute-done | bytes 155680 | tf_op jit(solution)/shard_map/ppermute | solution.py:576
  66.0 3.2 %collective-permute-done.21.refs_1_ = bf16[304,256]{1,0:T(8,128)(2,1)S(1)} collective-permute-done((bf16[304,256]{1,0:T(8,128)(2,1)S(1)}, bf16[304,256]{1,0:T(8,128)(2,1)S(1)}, u32[]{:S(2)}, u32[]{:S(2)}) %collective-permute-start.21) | collective-permute-done | bytes 155680 | tf_op jit(solution)/shard_map/ppermute | solution.py:576
  74.0 2.0 %collective-permute-start.24 = (bf16[176,256]{1,0:T(8,128)(2,1)S(1)}, bf16[176,256]{1,0:T(8,128)(2,1)S(1)}, u32[]{:S(2)}, u32[]{:S(2)}) collective-permute-start(bf16[176,256]{1,0:T(8,128)(2,1)S(1)} %get-tuple-element.114), channel_id=1, source_target_pairs={{0,16},{4,20},{8,24},{12,28},{16,0},{20,4},{24,8},{28,12},{1,17},{... | collective-permute-start | bytes 270344 | tf_op jit(solution)/shard_map/ppermute | solution.py:573
  76.1 1.7 %collective-permute-start.25 = (bf16[176,256]{1,0:T(8,128)(2,1)S(1)}, bf16[176,256]{1,0:T(8,128)(2,1)S(1)}, u32[]{:S(2)}, u32[]{:S(2)}) collective-permute-start(bf16[176,256]{1,0:T(8,128)(2,1)S(1)} %get-tuple-element.115), channel_id=1, source_target_pairs={{0,24},{4,28},{8,16},{12,20},{16,8},{20,12},{24,0},{28,4},{1,25},{... | collective-permute-start | bytes 270344 | tf_op jit(solution)/shard_map/ppermute | solution.py:573
  77.8 2.0 %collective-permute-start.26 = (bf16[128,256]{1,0:T(8,128)(2,1)S(1)}, bf16[128,256]{1,0:T(8,128)(2,1)S(1)}, u32[]{:S(2)}, u32[]{:S(2)}) collective-permute-start(bf16[128,256]{1,0:T(8,128)(2,1)S(1)} %get-tuple-element.116), channel_id=1, source_target_pairs={{0,8},{4,12},{8,0},{12,4},{16,24},{20,28},{24,16},{28,20},{1,9},{5... | collective-permute-start | bytes 196616 | tf_op jit(solution)/shard_map/ppermute | solution.py:573
  80.6 6.0 %collective-permute-done.26.refs_3_ = bf16[128,256]{1,0:T(8,128)(2,1)S(1)} collective-permute-done((bf16[128,256]{1,0:T(8,128)(2,1)S(1)}, bf16[128,256]{1,0:T(8,128)(2,1)S(1)}, u32[]{:S(2)}, u32[]{:S(2)}) %collective-permute-start.26) | collective-permute-done | bytes 65568 | tf_op jit(solution)/shard_map/ppermute | solution.py:573
  88.8 2.2 %collective-permute-start.30 = (bf16[240,256]{1,0:T(8,128)(2,1)S(1)}, bf16[240,256]{1,0:T(8,128)(2,1)S(1)}, u32[]{:S(2)}, u32[]{:S(2)}) collective-permute-start(bf16[240,256]{1,0:T(8,128)(2,1)S(1)} %get-tuple-element.122), channel_id=1, source_target_pairs={{0,8},{4,12},{8,0},{12,4},{16,24},{20,28},{24,16},{28,20},{1,9},{5... | collective-permute-start | bytes 368648 | tf_op jit(solution)/shard_map/ppermute | solution.py:573
  90.9 1.8 %collective-permute-start.35 = (bf16[176,256]{1,0:T(8,128)(2,1)S(1)}, bf16[176,256]{1,0:T(8,128)(2,1)S(1)}, u32[]{:S(2)}, u32[]{:S(2)}) collective-permute-start(bf16[176,256]{1,0:T(8,128)(2,1)S(1)} %get-tuple-element.125), channel_id=1, source_target_pairs={{0,24},{4,28},{8,16},{12,20},{16,8},{20,12},{24,0},{28,4},{1,25},{... | collective-permute-start | bytes 270344 | tf_op jit(solution)/shard_map/ppermute | solution.py:573
  92.8 3.6 %collective-permute-done.32.refs_3_ = bf16[128,256]{1,0:T(8,128)(2,1)S(1)} collective-permute-done((bf16[128,256]{1,0:T(8,128)(2,1)S(1)}, bf16[128,256]{1,0:T(8,128)(2,1)S(1)}, u32[]{:S(2)}, u32[]{:S(2)}) %collective-permute-start.32) | collective-permute-done | bytes 65568 | tf_op jit(solution)/shard_map/ppermute | solution.py:573
  96.3 2.0 %collective-permute-start.31 = (bf16[64,256]{1,0:T(8,128)(2,1)S(1)}, bf16[64,256]{1,0:T(8,128)(2,1)S(1)}, u32[]{:S(2)}, u32[]{:S(2)}) collective-permute-start(bf16[64,256]{1,0:T(8,128)(2,1)S(1)} %get-tuple-element.123), channel_id=1, source_target_pairs={{0,8},{4,12},{8,0},{12,4},{16,24},{20,28},{24,16},{28,20},{1,9},{5... | collective-permute-start | bytes 98312 | tf_op jit(solution)/shard_map/ppermute | solution.py:573
  98.4 3.3 %collective-permute-done.31.refs_2_ = bf16[64,256]{1,0:T(8,128)(2,1)S(1)} collective-permute-done((bf16[64,256]{1,0:T(8,128)(2,1)S(1)}, bf16[64,256]{1,0:T(8,128)(2,1)S(1)}, u32[]{:S(2)}, u32[]{:S(2)}) %collective-permute-start.31) | collective-permute-done | bytes 32800 | tf_op jit(solution)/shard_map/ppermute | solution.py:573
  104.1 1.8 %collective-permute-start.37 = (bf16[304,128]{1,0:T(8,128)(2,1)S(1)}, bf16[304,128]{1,0:T(8,128)(2,1)S(1)}, u32[]{:S(2)}, u32[]{:S(2)}) collective-permute-start(bf16[304,128]{1,0:T(8,128)(2,1)S(1)} %get-tuple-element.127), channel_id=1, source_target_pairs={{0,3},{1,2},{2,1},{3,0},{4,7},{5,6},{6,5},{7,4},{8,11},{9,10},{10,... | collective-permute-start | bytes 233480 | tf_op jit(solution)/shard_map/ppermute | solution.py:576
  108.0 1.6 %collective-permute-done.37.refs_1_ = bf16[304,128]{1,0:T(8,128)(2,1)S(1)} collective-permute-done((bf16[304,128]{1,0:T(8,128)(2,1)S(1)}, bf16[304,128]{1,0:T(8,128)(2,1)S(1)}, u32[]{:S(2)}, u32[]{:S(2)}) %collective-permute-start.37) | collective-permute-done | bytes 77856 | tf_op jit(solution)/shard_map/ppermute | solution.py:576
  109.6 1.6 %collective-permute-done.38.refs_2_ = bf16[304,128]{1,0:T(8,128)(2,1)S(1)} collective-permute-done((bf16[304,128]{1,0:T(8,128)(2,1)S(1)}, bf16[304,128]{1,0:T(8,128)(2,1)S(1)}, u32[]{:S(2)}, u32[]{:S(2)}) %collective-permute-start.38) | collective-permute-done | bytes 77856 | tf_op jit(solution)/shard_map/ppermute | solution.py:576
  (90 shorter events, 30.0 us)
Async XLA Ops:
  6.3 19.1 %collective-permute-start.5 = (bf16[4,4,128,256]{3,2,1,0:T(8,128)(2,1)}, bf16[4,4,128,256]{3,2,1,0:T(8,128)(2,1)S(1)}, u32[]{:S(2)}, u32[]{:S(2)}) collective-permute-start(bf16[4,4,128,256]{3,2,1,0:T(8,128)(2,1)} %get-tuple-element.77), channel_id=1, source_target_pairs={{0,4},{4,0},{8,12},{12,8},{16,20},{20,16},{24,28},{28,24},{1,5},{5... | collective-permute-start | bytes 3145736 | tf_op jit(solution)/shard_map/ppermute | solution.py:579
  6.8 7.4 %collective-permute-start = (bf16[304,256]{1,0:T(8,128)(2,1)}, bf16[304,256]{1,0:T(8,128)(2,1)S(1)}, u32[]{:S(2)}, u32[]{:S(2)}) collective-permute-start(bf16[304,256]{1,0:T(8,128)(2,1)} %get-tuple-element.70.refs_0_), channel_id=1, source_target_pairs={{0,1},{1,0},{2,3},{3,2},{4,5},{5,4},{6,7},{7,6},{8,9},{9,8},{10,11... | collective-permute-start | bytes 466952 | tf_op jit(solution)/shard_map/ppermute | solution.py:576
  9.4 6.3 %collective-permute-start.1 = (bf16[304,256]{1,0:T(8,128)(2,1)}, bf16[304,256]{1,0:T(8,128)(2,1)S(1)}, u32[]{:S(2)}, u32[]{:S(2)}) collective-permute-start(bf16[304,256]{1,0:T(8,128)(2,1)} %get-tuple-element.71.refs_1_), channel_id=1, source_target_pairs={{0,2},{1,3},{2,0},{3,1},{4,6},{5,7},{6,4},{7,5},{8,10},{9,11},{10,... | collective-permute-start | bytes 466952 | tf_op jit(solution)/shard_map/ppermute | solution.py:576
  15.8 5.3 %collective-permute-start.2 = (bf16[304,256]{1,0:T(8,128)(2,1)S(1)}, bf16[304,256]{1,0:T(8,128)(2,1)S(1)}, u32[]{:S(2)}, u32[]{:S(2)}) collective-permute-start(bf16[304,256]{1,0:T(8,128)(2,1)S(1)} %get-tuple-element.74.refs_0_), channel_id=1, source_target_pairs={{0,2},{1,3},{2,0},{3,1},{4,6},{5,7},{6,4},{7,5},{8,10},{9,11},{10,... | collective-permute-start | bytes 466952 | tf_op jit(solution)/shard_map/ppermute | solution.py:576
  25.9 6.5 %collective-permute-start.10 = (bf16[128,256]{1,0:T(8,128)(2,1)S(1)}, bf16[128,256]{1,0:T(8,128)(2,1)S(1)}, u32[]{:S(2)}, u32[]{:S(2)}) collective-permute-start(bf16[128,256]{1,0:T(8,128)(2,1)S(1)} %get-tuple-element.92), channel_id=1, source_target_pairs={{0,8},{4,12},{8,0},{12,4},{16,24},{20,28},{24,16},{28,20},{1,9},{5... | collective-permute-start | bytes 196616 | tf_op jit(solution)/shard_map/ppermute | solution.py:573
  27.5 11.2 %collective-permute-start.6 = (bf16[176,256]{1,0:T(8,128)(2,1)S(1)}, bf16[176,256]{1,0:T(8,128)(2,1)S(1)}, u32[]{:S(2)}, u32[]{:S(2)}) collective-permute-start(bf16[176,256]{1,0:T(8,128)(2,1)S(1)} %get-tuple-element.87), channel_id=1, source_target_pairs={{0,16},{4,20},{8,24},{12,28},{16,0},{20,4},{24,8},{28,12},{1,17},{... | collective-permute-start | bytes 270344 | tf_op jit(solution)/shard_map/ppermute | solution.py:573
  30.0 8.7 %collective-permute-start.7 = (bf16[176,256]{1,0:T(8,128)(2,1)S(1)}, bf16[176,256]{1,0:T(8,128)(2,1)S(1)}, u32[]{:S(2)}, u32[]{:S(2)}) collective-permute-start(bf16[176,256]{1,0:T(8,128)(2,1)S(1)} %get-tuple-element.88), channel_id=1, source_target_pairs={{0,24},{4,28},{8,16},{12,20},{16,8},{20,12},{24,0},{28,4},{1,25},{... | collective-permute-start | bytes 270344 | tf_op jit(solution)/shard_map/ppermute | solution.py:573
  30.3 8.4 %collective-permute-start.9 = (bf16[176,256]{1,0:T(8,128)(2,1)S(1)}, bf16[176,256]{1,0:T(8,128)(2,1)S(1)}, u32[]{:S(2)}, u32[]{:S(2)}) collective-permute-start(bf16[176,256]{1,0:T(8,128)(2,1)S(1)} %get-tuple-element.90), channel_id=1, source_target_pairs={{0,8},{4,12},{8,0},{12,4},{16,24},{20,28},{24,16},{28,20},{1,9},{5... | collective-permute-start | bytes 270344 | tf_op jit(solution)/shard_map/ppermute | solution.py:573
  31.0 7.7 %collective-permute-start.8 = (bf16[128,256]{1,0:T(8,128)(2,1)S(1)}, bf16[128,256]{1,0:T(8,128)(2,1)S(1)}, u32[]{:S(2)}, u32[]{:S(2)}) collective-permute-start(bf16[128,256]{1,0:T(8,128)(2,1)S(1)} %get-tuple-element.89), channel_id=1, source_target_pairs={{0,8},{4,12},{8,0},{12,4},{16,24},{20,28},{24,16},{28,20},{1,9},{5... | collective-permute-start | bytes 196616 | tf_op jit(solution)/shard_map/ppermute | solution.py:573
  32.4 9.1 %collective-permute-start.11 = (bf16[128,256]{1,0:T(8,128)(2,1)S(1)}, bf16[128,256]{1,0:T(8,128)(2,1)S(1)}, u32[]{:S(2)}, u32[]{:S(2)}) collective-permute-start(bf16[128,256]{1,0:T(8,128)(2,1)S(1)} %shard_map.110), channel_id=1, source_target_pairs={{0,16},{4,20},{8,24},{12,28},{16,0},{20,4},{24,8},{28,12},{1,17},{... | collective-permute-start | bytes 196616 | tf_op jit(solution)/shard_map/ppermute | solution.py:573
  41.6 7.8 %collective-permute-start.14 = (bf16[128,256]{1,0:T(8,128)(2,1)S(1)}, bf16[128,256]{1,0:T(8,128)(2,1)S(1)}, u32[]{:S(2)}, u32[]{:S(2)}) collective-permute-start(bf16[128,256]{1,0:T(8,128)(2,1)S(1)} %get-tuple-element.96), channel_id=1, source_target_pairs={{0,16},{4,20},{8,24},{12,28},{16,0},{20,4},{24,8},{28,12},{1,17},{... | collective-permute-start | bytes 196616 | tf_op jit(solution)/shard_map/ppermute | solution.py:573
  42.5 12.6 %collective-permute-start.12 = (bf16[240,256]{1,0:T(8,128)(2,1)S(1)}, bf16[240,256]{1,0:T(8,128)(2,1)S(1)}, u32[]{:S(2)}, u32[]{:S(2)}) collective-permute-start(bf16[240,256]{1,0:T(8,128)(2,1)S(1)} %get-tuple-element.94), channel_id=1, source_target_pairs={{0,8},{4,12},{8,0},{12,4},{16,24},{20,28},{24,16},{28,20},{1,9},{5... | collective-permute-start | bytes 368648 | tf_op jit(solution)/shard_map/ppermute | solution.py:573
  44.6 10.4 %collective-permute-start.17 = (bf16[176,256]{1,0:T(8,128)(2,1)S(1)}, bf16[176,256]{1,0:T(8,128)(2,1)S(1)}, u32[]{:S(2)}, u32[]{:S(2)}) collective-permute-start(bf16[176,256]{1,0:T(8,128)(2,1)S(1)} %get-tuple-element.97), channel_id=1, source_target_pairs={{0,24},{4,28},{8,16},{12,20},{16,8},{20,12},{24,0},{28,4},{1,25},{... | collective-permute-start | bytes 270344 | tf_op jit(solution)/shard_map/ppermute | solution.py:573
  46.1 9.0 %collective-permute-start.15 = (bf16[176,256]{1,0:T(8,128)(2,1)S(1)}, bf16[176,256]{1,0:T(8,128)(2,1)S(1)}, u32[]{:S(2)}, u32[]{:S(2)}) collective-permute-start(bf16[176,256]{1,0:T(8,128)(2,1)S(1)} %get-tuple-element.97), channel_id=1, source_target_pairs={{0,16},{4,20},{8,24},{12,28},{16,0},{20,4},{24,8},{28,12},{1,17},{... | collective-permute-start | bytes 270344 | tf_op jit(solution)/shard_map/ppermute | solution.py:573
  49.4 5.6 %collective-permute-start.16 = (bf16[128,256]{1,0:T(8,128)(2,1)S(1)}, bf16[128,256]{1,0:T(8,128)(2,1)S(1)}, u32[]{:S(2)}, u32[]{:S(2)}) collective-permute-start(bf16[128,256]{1,0:T(8,128)(2,1)S(1)} %collective-permute-done.14.refs_3_), channel_id=1, source_target_pairs={{0,8},{4,12},{8,0},{12,4},{16,24},{20,28},{24,16},{28,20},{1,9},{5... | collective-permute-start | bytes 196616 | tf_op jit(solution)/shard_map/ppermute | solution.py:573
  49.4 5.6 %collective-permute-start.13 = (bf16[64,256]{1,0:T(8,128)(2,1)S(1)}, bf16[64,256]{1,0:T(8,128)(2,1)S(1)}, u32[]{:S(2)}, u32[]{:S(2)}) collective-permute-start(bf16[64,256]{1,0:T(8,128)(2,1)S(1)} %get-tuple-element.95), channel_id=1, source_target_pairs={{0,8},{4,12},{8,0},{12,4},{16,24},{20,28},{24,16},{28,20},{1,9},{5... | collective-permute-start | bytes 98312 | tf_op jit(solution)/shard_map/ppermute | solution.py:573
  57.4 6.1 %collective-permute-start.19 = (bf16[304,256]{1,0:T(8,128)(2,1)S(1)}, bf16[304,256]{1,0:T(8,128)(2,1)S(1)}, u32[]{:S(2)}, u32[]{:S(2)}) collective-permute-start(bf16[304,256]{1,0:T(8,128)(2,1)S(1)} %get-tuple-element.98.one), channel_id=1, source_target_pairs={{0,1},{1,0},{2,3},{3,2},{4,5},{5,4},{6,7},{7,6},{8,9},{9,8},{10,11... | collective-permute-start | bytes 466952 | tf_op jit(solution)/shard_map/ppermute | solution.py:576
  58.0 5.8 %collective-permute-start.20 = (bf16[304,256]{1,0:T(8,128)(2,1)S(1)}, bf16[304,256]{1,0:T(8,128)(2,1)S(1)}, u32[]{:S(2)}, u32[]{:S(2)}) collective-permute-start(bf16[304,256]{1,0:T(8,128)(2,1)S(1)} %get-tuple-element.99.two), channel_id=1, source_target_pairs={{0,2},{1,3},{2,0},{3,1},{4,6},{5,7},{6,4},{7,5},{8,10},{9,11},{10,... | collective-permute-start | bytes 466952 | tf_op jit(solution)/shard_map/ppermute | solution.py:576
  63.9 5.3 %collective-permute-start.21 = (bf16[304,256]{1,0:T(8,128)(2,1)S(1)}, bf16[304,256]{1,0:T(8,128)(2,1)S(1)}, u32[]{:S(2)}, u32[]{:S(2)}) collective-permute-start(bf16[304,256]{1,0:T(8,128)(2,1)S(1)} %get-tuple-element.100.refs_0_), channel_id=1, source_target_pairs={{0,2},{1,3},{2,0},{3,1},{4,6},{5,7},{6,4},{7,5},{8,10},{9,11},{10,... | collective-permute-start | bytes 466952 | tf_op jit(solution)/shard_map/ppermute | solution.py:576
  73.3 6.5 %collective-permute-start.28 = (bf16[128,256]{1,0:T(8,128)(2,1)S(1)}, bf16[128,256]{1,0:T(8,128)(2,1)S(1)}, u32[]{:S(2)}, u32[]{:S(2)}) collective-permute-start(bf16[128,256]{1,0:T(8,128)(2,1)S(1)} %get-tuple-element.119), channel_id=1, source_target_pairs={{0,8},{4,12},{8,0},{12,4},{16,24},{20,28},{24,16},{28,20},{1,9},{5... | collective-permute-start | bytes 196616 | tf_op jit(solution)/shard_map/ppermute | solution.py:573
  74.0 12.6 %collective-permute-start.24 = (bf16[176,256]{1,0:T(8,128)(2,1)S(1)}, bf16[176,256]{1,0:T(8,128)(2,1)S(1)}, u32[]{:S(2)}, u32[]{:S(2)}) collective-permute-start(bf16[176,256]{1,0:T(8,128)(2,1)S(1)} %get-tuple-element.114), channel_id=1, source_target_pairs={{0,16},{4,20},{8,24},{12,28},{16,0},{20,4},{24,8},{28,12},{1,17},{... | collective-permute-start | bytes 270344 | tf_op jit(solution)/shard_map/ppermute | solution.py:573
  76.1 10.6 %collective-permute-start.25 = (bf16[176,256]{1,0:T(8,128)(2,1)S(1)}, bf16[176,256]{1,0:T(8,128)(2,1)S(1)}, u32[]{:S(2)}, u32[]{:S(2)}) collective-permute-start(bf16[176,256]{1,0:T(8,128)(2,1)S(1)} %get-tuple-element.115), channel_id=1, source_target_pairs={{0,24},{4,28},{8,16},{12,20},{16,8},{20,12},{24,0},{28,4},{1,25},{... | collective-permute-start | bytes 270344 | tf_op jit(solution)/shard_map/ppermute | solution.py:573
  77.8 8.8 %collective-permute-start.27 = (bf16[176,256]{1,0:T(8,128)(2,1)S(1)}, bf16[176,256]{1,0:T(8,128)(2,1)S(1)}, u32[]{:S(2)}, u32[]{:S(2)}) collective-permute-start(bf16[176,256]{1,0:T(8,128)(2,1)S(1)} %get-tuple-element.117), channel_id=1, source_target_pairs={{0,8},{4,12},{8,0},{12,4},{16,24},{20,28},{24,16},{28,20},{1,9},{5... | collective-permute-start | bytes 270344 | tf_op jit(solution)/shard_map/ppermute | solution.py:573
  77.8 8.8 %collective-permute-start.26 = (bf16[128,256]{1,0:T(8,128)(2,1)S(1)}, bf16[128,256]{1,0:T(8,128)(2,1)S(1)}, u32[]{:S(2)}, u32[]{:S(2)}) collective-permute-start(bf16[128,256]{1,0:T(8,128)(2,1)S(1)} %get-tuple-element.116), channel_id=1, source_target_pairs={{0,8},{4,12},{8,0},{12,4},{16,24},{20,28},{24,16},{28,20},{1,9},{5... | collective-permute-start | bytes 196616 | tf_op jit(solution)/shard_map/ppermute | solution.py:573
  79.8 8.1 %collective-permute-start.29 = (bf16[128,256]{1,0:T(8,128)(2,1)S(1)}, bf16[128,256]{1,0:T(8,128)(2,1)S(1)}, u32[]{:S(2)}, u32[]{:S(2)}) collective-permute-start(bf16[128,256]{1,0:T(8,128)(2,1)S(1)} %shard_map.120), channel_id=1, source_target_pairs={{0,16},{4,20},{8,24},{12,28},{16,0},{20,4},{24,8},{28,12},{1,17},{... | collective-permute-start | bytes 196616 | tf_op jit(solution)/shard_map/ppermute | solution.py:573
  88.3 8.0 %collective-permute-start.32 = (bf16[128,256]{1,0:T(8,128)(2,1)S(1)}, bf16[128,256]{1,0:T(8,128)(2,1)S(1)}, u32[]{:S(2)}, u32[]{:S(2)}) collective-permute-start(bf16[128,256]{1,0:T(8,128)(2,1)S(1)} %get-tuple-element.124), channel_id=1, source_target_pairs={{0,16},{4,20},{8,24},{12,28},{16,0},{20,4},{24,8},{28,12},{1,17},{... | collective-permute-start | bytes 196616 | tf_op jit(solution)/shard_map/ppermute | solution.py:573
  88.8 12.9 %collective-permute-start.30 = (bf16[240,256]{1,0:T(8,128)(2,1)S(1)}, bf16[240,256]{1,0:T(8,128)(2,1)S(1)}, u32[]{:S(2)}, u32[]{:S(2)}) collective-permute-start(bf16[240,256]{1,0:T(8,128)(2,1)S(1)} %get-tuple-element.122), channel_id=1, source_target_pairs={{0,8},{4,12},{8,0},{12,4},{16,24},{20,28},{24,16},{28,20},{1,9},{5... | collective-permute-start | bytes 368648 | tf_op jit(solution)/shard_map/ppermute | solution.py:573
  90.9 10.8 %collective-permute-start.35 = (bf16[176,256]{1,0:T(8,128)(2,1)S(1)}, bf16[176,256]{1,0:T(8,128)(2,1)S(1)}, u32[]{:S(2)}, u32[]{:S(2)}) collective-permute-start(bf16[176,256]{1,0:T(8,128)(2,1)S(1)} %get-tuple-element.125), channel_id=1, source_target_pairs={{0,24},{4,28},{8,16},{12,20},{16,8},{20,12},{24,0},{28,4},{1,25},{... | collective-permute-start | bytes 270344 | tf_op jit(solution)/shard_map/ppermute | solution.py:573
  92.7 8.9 %collective-permute-start.33 = (bf16[176,256]{1,0:T(8,128)(2,1)S(1)}, bf16[176,256]{1,0:T(8,128)(2,1)S(1)}, u32[]{:S(2)}, u32[]{:S(2)}) collective-permute-start(bf16[176,256]{1,0:T(8,128)(2,1)S(1)} %get-tuple-element.125), channel_id=1, source_target_pairs={{0,16},{4,20},{8,24},{12,28},{16,0},{20,4},{24,8},{28,12},{1,17},{... | collective-permute-start | bytes 270344 | tf_op jit(solution)/shard_map/ppermute | solution.py:573
  96.3 5.4 %collective-permute-start.34 = (bf16[128,256]{1,0:T(8,128)(2,1)S(1)}, bf16[128,256]{1,0:T(8,128)(2,1)S(1)}, u32[]{:S(2)}, u32[]{:S(2)}) collective-permute-start(bf16[128,256]{1,0:T(8,128)(2,1)S(1)} %collective-permute-done.32.refs_3_), channel_id=1, source_target_pairs={{0,8},{4,12},{8,0},{12,4},{16,24},{20,28},{24,16},{28,20},{1,9},{5... | collective-permute-start | bytes 196616 | tf_op jit(solution)/shard_map/ppermute | solution.py:573
  96.3 5.3 %collective-permute-start.31 = (bf16[64,256]{1,0:T(8,128)(2,1)S(1)}, bf16[64,256]{1,0:T(8,128)(2,1)S(1)}, u32[]{:S(2)}, u32[]{:S(2)}) collective-permute-start(bf16[64,256]{1,0:T(8,128)(2,1)S(1)} %get-tuple-element.123), channel_id=1, source_target_pairs={{0,8},{4,12},{8,0},{12,4},{16,24},{20,28},{24,16},{28,20},{1,9},{5... | collective-permute-start | bytes 98312 | tf_op jit(solution)/shard_map/ppermute | solution.py:573
  104.1 5.5 %collective-permute-start.37 = (bf16[304,128]{1,0:T(8,128)(2,1)S(1)}, bf16[304,128]{1,0:T(8,128)(2,1)S(1)}, u32[]{:S(2)}, u32[]{:S(2)}) collective-permute-start(bf16[304,128]{1,0:T(8,128)(2,1)S(1)} %get-tuple-element.127), channel_id=1, source_target_pairs={{0,3},{1,2},{2,1},{3,0},{4,7},{5,6},{6,5},{7,4},{8,11},{9,10},{10,... | collective-permute-start | bytes 233480 | tf_op jit(solution)/shard_map/ppermute | solution.py:576
  (14 other events, 75.2 us)

commit v23 on v19

--- a/solution.py
+++ b/solution.py
@@ -120,9 +120,10 @@
     dims, seeds_in, ids_in, cols_in, count_in, sd_in, innov_in, prec_in, h, own_out, partner_out, *rest
 ):
     chips, halves, blocks, lev = dims
-    outs = rest[:-15]
-    seeds, ids, cols, count, sd, innov, prec, bases, hashed, scratch, acc = rest[-15:-4]
-    own, partner, sems, h_sems = rest[-4:]
+    outs = rest[:-14]
+    seeds, ids, cols, count, sd, innov, prec, bases, hashed, scratch, acc = rest[-14:-3]
+    both, sems, h_sems = rest[-3:]
+    own, partner = both.at[0], both.at[1]
     z, core, obs = place()
     strips = innov.shape[0]
     profiles = strips * LANES
@@ -145,8 +146,7 @@
             )
     for copy in large:
         copy.start()
-    own[...] = jnp.zeros_like(own)
-    partner[...] = jnp.zeros_like(partner)
+    both[...] = jnp.zeros_like(both)
     scratch[...] = jnp.zeros_like(scratch)
     order = [(source, zz) for source in range(2) for zz in range(chips)]
     shape = (levp, width)
@@ -171,15 +171,8 @@
     def put(n, carry):
         for half in range(halves):
             piece, k = ids[0, 0, n] * halves + half, cols[0, 0, n]
-
-            @pl.when(piece % 2 == core)
-            def _():
-                tile_copy(n, half, own.at[piece // 2, k]).start()
-
-            @pl.when(piece % 2 != core)
-            def _():
-                tile_copy(n, half, partner.at[piece // 2, k]).start()
-
+            share = (piece % 2) ^ core
+            tile_copy(n, half, both.at[share, piece // 2, k]).start()
         return carry
 
     lax.fori_loop(0, count[0, 0], put, 0)
@@ -674,8 +667,7 @@
             pltpu.VMEM((n_slab // 2, members, levp, width), F32),
             pltpu.VMEM((2, rows, 2 * width), F32),
             pltpu.VMEM((rows, lanes), F32),
-            pltpu.VMEM(dense.shape, BF16),
-            pltpu.VMEM(dense.shape, BF16),
+            pltpu.VMEM((2, *dense.shape), BF16),
             pltpu.SemaphoreType.DMA((7 + 2 * (profiles // LANES),)),
             pltpu.SemaphoreType.DMA((h_block.shape[0] * halves,)),
         ],

time: 112 us -> 111 us (level)
  transfers between devices with their start and end apart: 40 -> 40, of which waited for: 25 -> 24; matrix products, arithmetic and copies ran while one was open for 0% -> 0% of each run, Pallas kernels for 4% -> 4%
where the time goes in v23:
time: 111 us
  waiting for transfers between devices  50.3 us (45%)
  starting transfers between devices  42.5 us (38%)
  Pallas kernels  14.4 us (13%)
  local copies, waits for them, and re-layouts  2.09 us (2%)
  between operations  1.59 us (1%)
    ppermute x24, starting transfers between devices, along(): return lax.ppermute(x, 'slab', [(s, s ^ 2 * i) for s in range(n_slab)])  29.4 us
    ppermute x24, waiting for transfers between devices, along(): return lax.ppermute(x, 'slab', [(s, s ^ 2 * i) for s in range(n_slab)])  26.1 us
    ppermute x11, waiting for transfers between devices, plane(): return lax.ppermute(x, 'obs', [(o, o ^ i) for o in range(n_obs)])  19.9 us
    pallas_call x23, Pallas kernels, call(): pl.pallas_call(kernel, out_shape=outs, in_specs=[space] * len(args), out_...  14.4 us
    ppermute x11, starting transfers between devices, plane(): return lax.ppermute(x, 'obs', [(o, o ^ i) for o in range(n_obs)])  12.3 us
    ppermute x5, waiting for transfers between devices, swap(): return lax.ppermute(x, 'slab', [(s, s ^ 1) for s in range(n_slab)])  4.23 us
  transfers between devices with their start and end apart: 40, of which 24 were waited for; matrix products, arithmetic and copies ran while one was open for 0% of the time, Pallas kernels for 4%

profile of v23, /device:TPU:0, one launch (start us, length us, event | category | flops | bytes accessed | tf_op | source)
XLA Modules:
  0.0 111.0 jit_solution(18083418304786422404)
XLA Ops:
  1.3 4.9 %shard_map.104 = (bf16[4,4,128,256]{3,2,1,0:T(8,128)(2,1)}, bf16[4,4,128,256]{3,2,1,0:T(8,128)(2,1)}, bf16[304,256]{1,0:T(8,128)(2,1)}, bf16[304,256]{1,0:T(8,128)(2,1)}) custom-call(s32[4]{0:T(128)} %seeds_in.1, s32[1,1,32]{2,1,0:T(1,128)} %ids_in.1, s32[1,1,32]{2,1,0:T(1,128)} %cols_in.1, s32[1,1]{1,0:T(1,128)S(6)} %copy.16.count_in, f32[1,128]{1,0:T(1,128)} %refs_4_.1, ...), custom_call_target="tpu_custom_call" | custom-call | flops 637534208 | bytes 5735188 | tf_op jit(solution)/shard_map/pallas_call | solution.py:23
  6.8 3.1 %collective-permute-start = (bf16[304,256]{1,0:T(8,128)(2,1)}, bf16[304,256]{1,0:T(8,128)(2,1)S(1)}, u32[]{:S(2)}, u32[]{:S(2)}) collective-permute-start(bf16[304,256]{1,0:T(8,128)(2,1)} %get-tuple-element.70.refs_0_), channel_id=1, source_target_pairs={{0,1},{1,0},{2,3},{3,2},{4,5},{5,4},{6,7},{7,6},{8,9},{9,8},{10,11... | collective-permute-start | bytes 466952 | tf_op jit(solution)/shard_map/ppermute | solution.py:569
  13.2 1.5 %collective-permute-done.one_more = bf16[304,256]{1,0:T(8,128)(2,1)S(1)} collective-permute-done((bf16[304,256]{1,0:T(8,128)(2,1)}, bf16[304,256]{1,0:T(8,128)(2,1)S(1)}, u32[]{:S(2)}, u32[]{:S(2)}) %collective-permute-start) | collective-permute-done | bytes 155680 | tf_op jit(solution)/shard_map/ppermute | solution.py:569
  14.7 1.5 %collective-permute-done.1.two_more = bf16[304,256]{1,0:T(8,128)(2,1)S(1)} collective-permute-done((bf16[304,256]{1,0:T(8,128)(2,1)}, bf16[304,256]{1,0:T(8,128)(2,1)S(1)}, u32[]{:S(2)}, u32[]{:S(2)}) %collective-permute-start.1) | collective-permute-done | bytes 155680 | tf_op jit(solution)/shard_map/ppermute | solution.py:569
  18.2 3.4 %collective-permute-done.2.refs_1_ = bf16[304,256]{1,0:T(8,128)(2,1)S(1)} collective-permute-done((bf16[304,256]{1,0:T(8,128)(2,1)S(1)}, bf16[304,256]{1,0:T(8,128)(2,1)S(1)}, u32[]{:S(2)}, u32[]{:S(2)}) %collective-permute-start.2) | collective-permute-done | bytes 155680 | tf_op jit(solution)/shard_map/ppermute | solution.py:569
  25.8 1.7 %collective-permute-start.10 = (bf16[144,256]{1,0:T(8,128)(2,1)S(1)}, bf16[144,256]{1,0:T(8,128)(2,1)S(1)}, u32[]{:S(2)}, u32[]{:S(2)}) collective-permute-start(bf16[144,256]{1,0:T(8,128)(2,1)S(1)} %get-tuple-element.92), channel_id=1, source_target_pairs={{0,8},{4,12},{8,0},{12,4},{16,24},{20,28},{24,16},{28,20},{1,9},{5... | collective-permute-start | bytes 221192 | tf_op jit(solution)/shard_map/ppermute | solution.py:566
  27.5 2.6 %collective-permute-start.6 = (bf16[160,256]{1,0:T(8,128)(2,1)S(1)}, bf16[160,256]{1,0:T(8,128)(2,1)S(1)}, u32[]{:S(2)}, u32[]{:S(2)}) collective-permute-start(bf16[160,256]{1,0:T(8,128)(2,1)S(1)} %get-tuple-element.87), channel_id=1, source_target_pairs={{0,16},{4,20},{8,24},{12,28},{16,0},{20,4},{24,8},{28,12},{1,17},{... | collective-permute-start | bytes 245768 | tf_op jit(solution)/shard_map/ppermute | solution.py:566
  31.0 1.3 %collective-permute-start.8 = (bf16[144,256]{1,0:T(8,128)(2,1)S(1)}, bf16[144,256]{1,0:T(8,128)(2,1)S(1)}, u32[]{:S(2)}, u32[]{:S(2)}) collective-permute-start(bf16[144,256]{1,0:T(8,128)(2,1)S(1)} %get-tuple-element.89), channel_id=1, source_target_pairs={{0,8},{4,12},{8,0},{12,4},{16,24},{20,28},{24,16},{28,20},{1,9},{5... | collective-permute-start | bytes 221192 | tf_op jit(solution)/shard_map/ppermute | solution.py:566
  32.3 2.3 %collective-permute-start.11 = (bf16[144,256]{1,0:T(8,128)(2,1)S(1)}, bf16[144,256]{1,0:T(8,128)(2,1)S(1)}, u32[]{:S(2)}, u32[]{:S(2)}) collective-permute-start(bf16[144,256]{1,0:T(8,128)(2,1)S(1)} %shard_map.110), channel_id=1, source_target_pairs={{0,16},{4,20},{8,24},{12,28},{16,0},{20,4},{24,8},{28,12},{1,17},{... | collective-permute-start | bytes 221192 | tf_op jit(solution)/shard_map/ppermute | solution.py:566
  34.8 3.9 %collective-permute-done.8.refs_3_ = bf16[144,256]{1,0:T(8,128)(2,1)S(1)} collective-permute-done((bf16[144,256]{1,0:T(8,128)(2,1)S(1)}, bf16[144,256]{1,0:T(8,128)(2,1)S(1)}, u32[]{:S(2)}, u32[]{:S(2)}) %collective-permute-start.8) | collective-permute-done | bytes 73760 | tf_op jit(solution)/shard_map/ppermute | solution.py:566
  38.8 2.3 %collective-permute-done.11.refs_5_ = bf16[144,256]{1,0:T(8,128)(2,1)S(1)} collective-permute-done((bf16[144,256]{1,0:T(8,128)(2,1)S(1)}, bf16[144,256]{1,0:T(8,128)(2,1)S(1)}, u32[]{:S(2)}, u32[]{:S(2)}) %collective-permute-start.11) | collective-permute-done | bytes 73760 | tf_op jit(solution)/shard_map/ppermute | solution.py:566
  42.3 2.0 %collective-permute-start.12 = (bf16[272,256]{1,0:T(8,128)(2,1)S(1)}, bf16[272,256]{1,0:T(8,128)(2,1)S(1)}, u32[]{:S(2)}, u32[]{:S(2)}) collective-permute-start(bf16[272,256]{1,0:T(8,128)(2,1)S(1)} %get-tuple-element.94), channel_id=1, source_target_pairs={{0,8},{4,12},{8,0},{12,4},{16,24},{20,28},{24,16},{28,20},{1,9},{5... | collective-permute-start | bytes 417800 | tf_op jit(solution)/shard_map/ppermute | solution.py:566
  44.2 1.4 %collective-permute-start.17 = (bf16[160,256]{1,0:T(8,128)(2,1)S(1)}, bf16[160,256]{1,0:T(8,128)(2,1)S(1)}, u32[]{:S(2)}, u32[]{:S(2)}) collective-permute-start(bf16[160,256]{1,0:T(8,128)(2,1)S(1)} %get-tuple-element.97), channel_id=1, source_target_pairs={{0,24},{4,28},{8,16},{12,20},{16,8},{20,12},{24,0},{28,4},{1,25},{... | collective-permute-start | bytes 245768 | tf_op jit(solution)/shard_map/ppermute | solution.py:566
  45.7 4.0 %collective-permute-done.14.refs_3_ = bf16[144,256]{1,0:T(8,128)(2,1)S(1)} collective-permute-done((bf16[144,256]{1,0:T(8,128)(2,1)S(1)}, bf16[144,256]{1,0:T(8,128)(2,1)S(1)}, u32[]{:S(2)}, u32[]{:S(2)}) %collective-permute-start.14) | collective-permute-done | bytes 73760 | tf_op jit(solution)/shard_map/ppermute | solution.py:566
  49.7 2.0 %collective-permute-start.13 = (bf16[32,256]{1,0:T(8,128)(2,1)S(1)}, bf16[32,256]{1,0:T(8,128)(2,1)S(1)}, u32[]{:S(2)}, u32[]{:S(2)}) collective-permute-start(bf16[32,256]{1,0:T(8,128)(2,1)S(1)} %get-tuple-element.95), channel_id=1, source_target_pairs={{0,8},{4,12},{8,0},{12,4},{16,24},{20,28},{24,16},{28,20},{1,9},{5... | collective-permute-start | bytes 49160 | tf_op jit(solution)/shard_map/ppermute | solution.py:566
  51.8 2.6 %collective-permute-done.13.refs_2_ = bf16[32,256]{1,0:T(8,128)(2,1)S(1)} collective-permute-done((bf16[32,256]{1,0:T(8,128)(2,1)S(1)}, bf16[32,256]{1,0:T(8,128)(2,1)S(1)}, u32[]{:S(2)}, u32[]{:S(2)}) %collective-permute-start.13) | collective-permute-done | bytes 16416 | tf_op jit(solution)/shard_map/ppermute | solution.py:566
  57.7 5.1 %collective-permute-done.19.one_more = bf16[304,256]{1,0:T(8,128)(2,1)S(1)} collective-permute-done((bf16[304,256]{1,0:T(8,128)(2,1)S(1)}, bf16[304,256]{1,0:T(8,128)(2,1)S(1)}, u32[]{:S(2)}, u32[]{:S(2)}) %collective-permute-start.19) | collective-permute-done | bytes 155680 | tf_op jit(solution)/shard_map/ppermute | solution.py:569
  63.7 1.5 %collective-permute-start.22 = (bf16[304,256]{1,0:T(8,128)(2,1)S(1)}, bf16[304,256]{1,0:T(8,128)(2,1)S(1)}, u32[]{:S(2)}, u32[]{:S(2)}) collective-permute-start(bf16[304,256]{1,0:T(8,128)(2,1)S(1)} %get-tuple-element.101.refs_2_), channel_id=1, source_target_pairs={{0,1},{1,0},{2,3},{3,2},{4,5},{5,4},{6,7},{7,6},{8,9},{9,8},{10,11... | collective-permute-start | bytes 466952 | tf_op jit(solution)/shard_map/ppermute | solution.py:569
  65.2 3.3 %collective-permute-done.21.refs_1_ = bf16[304,256]{1,0:T(8,128)(2,1)S(1)} collective-permute-done((bf16[304,256]{1,0:T(8,128)(2,1)S(1)}, bf16[304,256]{1,0:T(8,128)(2,1)S(1)}, u32[]{:S(2)}, u32[]{:S(2)}) %collective-permute-start.21) | collective-permute-done | bytes 155680 | tf_op jit(solution)/shard_map/ppermute | solution.py:569
  73.6 1.5 %collective-permute-start.24 = (bf16[160,256]{1,0:T(8,128)(2,1)S(1)}, bf16[160,256]{1,0:T(8,128)(2,1)S(1)}, u32[]{:S(2)}, u32[]{:S(2)}) collective-permute-start(bf16[160,256]{1,0:T(8,128)(2,1)S(1)} %get-tuple-element.114), channel_id=1, source_target_pairs={{0,16},{4,20},{8,24},{12,28},{16,0},{20,4},{24,8},{28,12},{1,17},{... | collective-permute-start | bytes 245768 | tf_op jit(solution)/shard_map/ppermute | solution.py:566
  75.1 1.7 %collective-permute-start.25 = (bf16[160,256]{1,0:T(8,128)(2,1)S(1)}, bf16[160,256]{1,0:T(8,128)(2,1)S(1)}, u32[]{:S(2)}, u32[]{:S(2)}) collective-permute-start(bf16[160,256]{1,0:T(8,128)(2,1)S(1)} %get-tuple-element.115), channel_id=1, source_target_pairs={{0,24},{4,28},{8,16},{12,20},{16,8},{20,12},{24,0},{28,4},{1,25},{... | collective-permute-start | bytes 245768 | tf_op jit(solution)/shard_map/ppermute | solution.py:566
  77.1 1.7 %collective-permute-start.26 = (bf16[144,256]{1,0:T(8,128)(2,1)S(1)}, bf16[144,256]{1,0:T(8,128)(2,1)S(1)}, u32[]{:S(2)}, u32[]{:S(2)}) collective-permute-start(bf16[144,256]{1,0:T(8,128)(2,1)S(1)} %get-tuple-element.116), channel_id=1, source_target_pairs={{0,8},{4,12},{8,0},{12,4},{16,24},{20,28},{24,16},{28,20},{1,9},{5... | collective-permute-start | bytes 221192 | tf_op jit(solution)/shard_map/ppermute | solution.py:566
  79.9 5.4 %collective-permute-done.26.refs_3_ = bf16[144,256]{1,0:T(8,128)(2,1)S(1)} collective-permute-done((bf16[144,256]{1,0:T(8,128)(2,1)S(1)}, bf16[144,256]{1,0:T(8,128)(2,1)S(1)}, u32[]{:S(2)}, u32[]{:S(2)}) %collective-permute-start.26) | collective-permute-done | bytes 73760 | tf_op jit(solution)/shard_map/ppermute | solution.py:566
  85.3 1.9 %collective-permute-done.29.refs_5_ = bf16[144,256]{1,0:T(8,128)(2,1)S(1)} collective-permute-done((bf16[144,256]{1,0:T(8,128)(2,1)S(1)}, bf16[144,256]{1,0:T(8,128)(2,1)S(1)}, u32[]{:S(2)}, u32[]{:S(2)}) %collective-permute-start.29) | collective-permute-done | bytes 73760 | tf_op jit(solution)/shard_map/ppermute | solution.py:566
  88.0 2.4 %collective-permute-start.30 = (bf16[272,256]{1,0:T(8,128)(2,1)S(1)}, bf16[272,256]{1,0:T(8,128)(2,1)S(1)}, u32[]{:S(2)}, u32[]{:S(2)}) collective-permute-start(bf16[272,256]{1,0:T(8,128)(2,1)S(1)} %get-tuple-element.122), channel_id=1, source_target_pairs={{0,8},{4,12},{8,0},{12,4},{16,24},{20,28},{24,16},{28,20},{1,9},{5... | collective-permute-start | bytes 417800 | tf_op jit(solution)/shard_map/ppermute | solution.py:566
  90.3 1.6 %collective-permute-start.35 = (bf16[160,256]{1,0:T(8,128)(2,1)S(1)}, bf16[160,256]{1,0:T(8,128)(2,1)S(1)}, u32[]{:S(2)}, u32[]{:S(2)}) collective-permute-start(bf16[160,256]{1,0:T(8,128)(2,1)S(1)} %get-tuple-element.125), channel_id=1, source_target_pairs={{0,24},{4,28},{8,16},{12,20},{16,8},{20,12},{24,0},{28,4},{1,25},{... | collective-permute-start | bytes 245768 | tf_op jit(solution)/shard_map/ppermute | solution.py:566
  92.0 2.7 %collective-permute-done.32.refs_3_ = bf16[144,256]{1,0:T(8,128)(2,1)S(1)} collective-permute-done((bf16[144,256]{1,0:T(8,128)(2,1)S(1)}, bf16[144,256]{1,0:T(8,128)(2,1)S(1)}, u32[]{:S(2)}, u32[]{:S(2)}) %collective-permute-start.32) | collective-permute-done | bytes 73760 | tf_op jit(solution)/shard_map/ppermute | solution.py:566
  94.7 2.0 %collective-permute-start.31 = (bf16[32,256]{1,0:T(8,128)(2,1)S(1)}, bf16[32,256]{1,0:T(8,128)(2,1)S(1)}, u32[]{:S(2)}, u32[]{:S(2)}) collective-permute-start(bf16[32,256]{1,0:T(8,128)(2,1)S(1)} %get-tuple-element.123), channel_id=1, source_target_pairs={{0,8},{4,12},{8,0},{12,4},{16,24},{20,28},{24,16},{28,20},{1,9},{5... | collective-permute-start | bytes 49160 | tf_op jit(solution)/shard_map/ppermute | solution.py:566
  96.7 2.7 %collective-permute-done.31.refs_2_ = bf16[32,256]{1,0:T(8,128)(2,1)S(1)} collective-permute-done((bf16[32,256]{1,0:T(8,128)(2,1)S(1)}, bf16[32,256]{1,0:T(8,128)(2,1)S(1)}, u32[]{:S(2)}, u32[]{:S(2)}) %collective-permute-start.31) | collective-permute-done | bytes 16416 | tf_op jit(solution)/shard_map/ppermute | solution.py:566
  102.5 2.6 %collective-permute-start.37 = (bf16[304,128]{1,0:T(8,128)(2,1)S(1)}, bf16[304,128]{1,0:T(8,128)(2,1)S(1)}, u32[]{:S(2)}, u32[]{:S(2)}) collective-permute-start(bf16[304,128]{1,0:T(8,128)(2,1)S(1)} %get-tuple-element.127), channel_id=1, source_target_pairs={{0,3},{1,2},{2,1},{3,0},{4,7},{5,6},{6,5},{7,4},{8,11},{9,10},{10,... | collective-permute-start | bytes 233480 | tf_op jit(solution)/shard_map/ppermute | solution.py:569
  106.4 1.5 %collective-permute-done.37.refs_1_ = bf16[304,128]{1,0:T(8,128)(2,1)S(1)} collective-permute-done((bf16[304,128]{1,0:T(8,128)(2,1)S(1)}, bf16[304,128]{1,0:T(8,128)(2,1)S(1)}, u32[]{:S(2)}, u32[]{:S(2)}) %collective-permute-start.37) | collective-permute-done | bytes 77856 | tf_op jit(solution)/shard_map/ppermute | solution.py:569
  107.9 1.6 %collective-permute-done.38.refs_2_ = bf16[304,128]{1,0:T(8,128)(2,1)S(1)} collective-permute-done((bf16[304,128]{1,0:T(8,128)(2,1)S(1)}, bf16[304,128]{1,0:T(8,128)(2,1)S(1)}, u32[]{:S(2)}, u32[]{:S(2)}) %collective-permute-start.38) | collective-permute-done | bytes 77856 | tf_op jit(solution)/shard_map/ppermute | solution.py:569
  (90 shorter events, 29.8 us)
Async XLA Ops:
  6.3 19.0 %collective-permute-start.5 = (bf16[4,4,128,256]{3,2,1,0:T(8,128)(2,1)}, bf16[4,4,128,256]{3,2,1,0:T(8,128)(2,1)S(1)}, u32[]{:S(2)}, u32[]{:S(2)}) collective-permute-start(bf16[4,4,128,256]{3,2,1,0:T(8,128)(2,1)} %get-tuple-element.77), channel_id=1, source_target_pairs={{0,4},{4,0},{8,12},{12,8},{16,20},{20,16},{24,28},{28,24},{1,5},{5... | collective-permute-start | bytes 3145736 | tf_op jit(solution)/shard_map/ppermute | solution.py:572
  6.8 7.9 %collective-permute-start = (bf16[304,256]{1,0:T(8,128)(2,1)}, bf16[304,256]{1,0:T(8,128)(2,1)S(1)}, u32[]{:S(2)}, u32[]{:S(2)}) collective-permute-start(bf16[304,256]{1,0:T(8,128)(2,1)} %get-tuple-element.70.refs_0_), channel_id=1, source_target_pairs={{0,1},{1,0},{2,3},{3,2},{4,5},{5,4},{6,7},{7,6},{8,9},{9,8},{10,11... | collective-permute-start | bytes 466952 | tf_op jit(solution)/shard_map/ppermute | solution.py:569
  9.9 6.3 %collective-permute-start.1 = (bf16[304,256]{1,0:T(8,128)(2,1)}, bf16[304,256]{1,0:T(8,128)(2,1)S(1)}, u32[]{:S(2)}, u32[]{:S(2)}) collective-permute-start(bf16[304,256]{1,0:T(8,128)(2,1)} %get-tuple-element.71.refs_1_), channel_id=1, source_target_pairs={{0,2},{1,3},{2,0},{3,1},{4,6},{5,7},{6,4},{7,5},{8,10},{9,11},{10,... | collective-permute-start | bytes 466952 | tf_op jit(solution)/shard_map/ppermute | solution.py:569
  16.3 5.3 %collective-permute-start.2 = (bf16[304,256]{1,0:T(8,128)(2,1)S(1)}, bf16[304,256]{1,0:T(8,128)(2,1)S(1)}, u32[]{:S(2)}, u32[]{:S(2)}) collective-permute-start(bf16[304,256]{1,0:T(8,128)(2,1)S(1)} %get-tuple-element.74.refs_0_), channel_id=1, source_target_pairs={{0,2},{1,3},{2,0},{3,1},{4,6},{5,7},{6,4},{7,5},{8,10},{9,11},{10,... | collective-permute-start | bytes 466952 | tf_op jit(solution)/shard_map/ppermute | solution.py:569
  17.3 5.2 %collective-permute-start.3 = (bf16[304,256]{1,0:T(8,128)(2,1)S(1)}, bf16[304,256]{1,0:T(8,128)(2,1)S(1)}, u32[]{:S(2)}, u32[]{:S(2)}) collective-permute-start(bf16[304,256]{1,0:T(8,128)(2,1)S(1)} %get-tuple-element.75.refs_2_), channel_id=1, source_target_pairs={{0,1},{1,0},{2,3},{3,2},{4,5},{5,4},{6,7},{7,6},{8,9},{9,8},{10,11... | collective-permute-start | bytes 466952 | tf_op jit(solution)/shard_map/ppermute | solution.py:569
  25.8 6.5 %collective-permute-start.10 = (bf16[144,256]{1,0:T(8,128)(2,1)S(1)}, bf16[144,256]{1,0:T(8,128)(2,1)S(1)}, u32[]{:S(2)}, u32[]{:S(2)}) collective-permute-start(bf16[144,256]{1,0:T(8,128)(2,1)S(1)} %get-tuple-element.92), channel_id=1, source_target_pairs={{0,8},{4,12},{8,0},{12,4},{16,24},{20,28},{24,16},{28,20},{1,9},{5... | collective-permute-start | bytes 221192 | tf_op jit(solution)/shard_map/ppermute | solution.py:566
  27.5 11.3 %collective-permute-start.6 = (bf16[160,256]{1,0:T(8,128)(2,1)S(1)}, bf16[160,256]{1,0:T(8,128)(2,1)S(1)}, u32[]{:S(2)}, u32[]{:S(2)}) collective-permute-start(bf16[160,256]{1,0:T(8,128)(2,1)S(1)} %get-tuple-element.87), channel_id=1, source_target_pairs={{0,16},{4,20},{8,24},{12,28},{16,0},{20,4},{24,8},{28,12},{1,17},{... | collective-permute-start | bytes 245768 | tf_op jit(solution)/shard_map/ppermute | solution.py:566
  30.1 8.7 %collective-permute-start.7 = (bf16[160,256]{1,0:T(8,128)(2,1)S(1)}, bf16[160,256]{1,0:T(8,128)(2,1)S(1)}, u32[]{:S(2)}, u32[]{:S(2)}) collective-permute-start(bf16[160,256]{1,0:T(8,128)(2,1)S(1)} %get-tuple-element.88), channel_id=1, source_target_pairs={{0,24},{4,28},{8,16},{12,20},{16,8},{20,12},{24,0},{28,4},{1,25},{... | collective-permute-start | bytes 245768 | tf_op jit(solution)/shard_map/ppermute | solution.py:566
  30.2 8.5 %collective-permute-start.9 = (bf16[160,256]{1,0:T(8,128)(2,1)S(1)}, bf16[160,256]{1,0:T(8,128)(2,1)S(1)}, u32[]{:S(2)}, u32[]{:S(2)}) collective-permute-start(bf16[160,256]{1,0:T(8,128)(2,1)S(1)} %get-tuple-element.90), channel_id=1, source_target_pairs={{0,8},{4,12},{8,0},{12,4},{16,24},{20,28},{24,16},{28,20},{1,9},{5... | collective-permute-start | bytes 245768 | tf_op jit(solution)/shard_map/ppermute | solution.py:566
  31.0 7.8 %collective-permute-start.8 = (bf16[144,256]{1,0:T(8,128)(2,1)S(1)}, bf16[144,256]{1,0:T(8,128)(2,1)S(1)}, u32[]{:S(2)}, u32[]{:S(2)}) collective-permute-start(bf16[144,256]{1,0:T(8,128)(2,1)S(1)} %get-tuple-element.89), channel_id=1, source_target_pairs={{0,8},{4,12},{8,0},{12,4},{16,24},{20,28},{24,16},{28,20},{1,9},{5... | collective-permute-start | bytes 221192 | tf_op jit(solution)/shard_map/ppermute | solution.py:566
  32.3 8.7 %collective-permute-start.11 = (bf16[144,256]{1,0:T(8,128)(2,1)S(1)}, bf16[144,256]{1,0:T(8,128)(2,1)S(1)}, u32[]{:S(2)}, u32[]{:S(2)}) collective-permute-start(bf16[144,256]{1,0:T(8,128)(2,1)S(1)} %shard_map.110), channel_id=1, source_target_pairs={{0,16},{4,20},{8,24},{12,28},{16,0},{20,4},{24,8},{28,12},{1,17},{... | collective-permute-start | bytes 221192 | tf_op jit(solution)/shard_map/ppermute | solution.py:566
  41.2 8.5 %collective-permute-start.14 = (bf16[144,256]{1,0:T(8,128)(2,1)S(1)}, bf16[144,256]{1,0:T(8,128)(2,1)S(1)}, u32[]{:S(2)}, u32[]{:S(2)}) collective-permute-start(bf16[144,256]{1,0:T(8,128)(2,1)S(1)} %get-tuple-element.96), channel_id=1, source_target_pairs={{0,16},{4,20},{8,24},{12,28},{16,0},{20,4},{24,8},{28,12},{1,17},{... | collective-permute-start | bytes 221192 | tf_op jit(solution)/shard_map/ppermute | solution.py:566
  42.3 12.1 %collective-permute-start.12 = (bf16[272,256]{1,0:T(8,128)(2,1)S(1)}, bf16[272,256]{1,0:T(8,128)(2,1)S(1)}, u32[]{:S(2)}, u32[]{:S(2)}) collective-permute-start(bf16[272,256]{1,0:T(8,128)(2,1)S(1)} %get-tuple-element.94), channel_id=1, source_target_pairs={{0,8},{4,12},{8,0},{12,4},{16,24},{20,28},{24,16},{28,20},{1,9},{5... | collective-permute-start | bytes 417800 | tf_op jit(solution)/shard_map/ppermute | solution.py:566
  44.2 10.1 %collective-permute-start.17 = (bf16[160,256]{1,0:T(8,128)(2,1)S(1)}, bf16[160,256]{1,0:T(8,128)(2,1)S(1)}, u32[]{:S(2)}, u32[]{:S(2)}) collective-permute-start(bf16[160,256]{1,0:T(8,128)(2,1)S(1)} %get-tuple-element.97), channel_id=1, source_target_pairs={{0,24},{4,28},{8,16},{12,20},{16,8},{20,12},{24,0},{28,4},{1,25},{... | collective-permute-start | bytes 245768 | tf_op jit(solution)/shard_map/ppermute | solution.py:566
  45.7 8.7 %collective-permute-start.15 = (bf16[160,256]{1,0:T(8,128)(2,1)S(1)}, bf16[160,256]{1,0:T(8,128)(2,1)S(1)}, u32[]{:S(2)}, u32[]{:S(2)}) collective-permute-start(bf16[160,256]{1,0:T(8,128)(2,1)S(1)} %get-tuple-element.97), channel_id=1, source_target_pairs={{0,16},{4,20},{8,24},{12,28},{16,0},{20,4},{24,8},{28,12},{1,17},{... | collective-permute-start | bytes 245768 | tf_op jit(solution)/shard_map/ppermute | solution.py:566
  56.7 6.1 %collective-permute-start.19 = (bf16[304,256]{1,0:T(8,128)(2,1)S(1)}, bf16[304,256]{1,0:T(8,128)(2,1)S(1)}, u32[]{:S(2)}, u32[]{:S(2)}) collective-permute-start(bf16[304,256]{1,0:T(8,128)(2,1)S(1)} %get-tuple-element.98.one), channel_id=1, source_target_pairs={{0,1},{1,0},{2,3},{3,2},{4,5},{5,4},{6,7},{7,6},{8,9},{9,8},{10,11... | collective-permute-start | bytes 466952 | tf_op jit(solution)/shard_map/ppermute | solution.py:569
  57.3 5.8 %collective-permute-start.20 = (bf16[304,256]{1,0:T(8,128)(2,1)S(1)}, bf16[304,256]{1,0:T(8,128)(2,1)S(1)}, u32[]{:S(2)}, u32[]{:S(2)}) collective-permute-start(bf16[304,256]{1,0:T(8,128)(2,1)S(1)} %get-tuple-element.99.two), channel_id=1, source_target_pairs={{0,2},{1,3},{2,0},{3,1},{4,6},{5,7},{6,4},{7,5},{8,10},{9,11},{10,... | collective-permute-start | bytes 466952 | tf_op jit(solution)/shard_map/ppermute | solution.py:569
  63.2 5.3 %collective-permute-start.21 = (bf16[304,256]{1,0:T(8,128)(2,1)S(1)}, bf16[304,256]{1,0:T(8,128)(2,1)S(1)}, u32[]{:S(2)}, u32[]{:S(2)}) collective-permute-start(bf16[304,256]{1,0:T(8,128)(2,1)S(1)} %get-tuple-element.100.refs_0_), channel_id=1, source_target_pairs={{0,2},{1,3},{2,0},{3,1},{4,6},{5,7},{6,4},{7,5},{8,10},{9,11},{10,... | collective-permute-start | bytes 466952 | tf_op jit(solution)/shard_map/ppermute | solution.py:569
  63.7 5.2 %collective-permute-start.22 = (bf16[304,256]{1,0:T(8,128)(2,1)S(1)}, bf16[304,256]{1,0:T(8,128)(2,1)S(1)}, u32[]{:S(2)}, u32[]{:S(2)}) collective-permute-start(bf16[304,256]{1,0:T(8,128)(2,1)S(1)} %get-tuple-element.101.refs_2_), channel_id=1, source_target_pairs={{0,1},{1,0},{2,3},{3,2},{4,5},{5,4},{6,7},{7,6},{8,9},{9,8},{10,11... | collective-permute-start | bytes 466952 | tf_op jit(solution)/shard_map/ppermute | solution.py:569
  72.4 6.5 %collective-permute-start.28 = (bf16[144,256]{1,0:T(8,128)(2,1)S(1)}, bf16[144,256]{1,0:T(8,128)(2,1)S(1)}, u32[]{:S(2)}, u32[]{:S(2)}) collective-permute-start(bf16[144,256]{1,0:T(8,128)(2,1)S(1)} %get-tuple-element.119), channel_id=1, source_target_pairs={{0,8},{4,12},{8,0},{12,4},{16,24},{20,28},{24,16},{28,20},{1,9},{5... | collective-permute-start | bytes 221192 | tf_op jit(solution)/shard_map/ppermute | solution.py:566
  73.6 11.7 %collective-permute-start.24 = (bf16[160,256]{1,0:T(8,128)(2,1)S(1)}, bf16[160,256]{1,0:T(8,128)(2,1)S(1)}, u32[]{:S(2)}, u32[]{:S(2)}) collective-permute-start(bf16[160,256]{1,0:T(8,128)(2,1)S(1)} %get-tuple-element.114), channel_id=1, source_target_pairs={{0,16},{4,20},{8,24},{12,28},{16,0},{20,4},{24,8},{28,12},{1,17},{... | collective-permute-start | bytes 245768 | tf_op jit(solution)/shard_map/ppermute | solution.py:566
  75.1 10.2 %collective-permute-start.25 = (bf16[160,256]{1,0:T(8,128)(2,1)S(1)}, bf16[160,256]{1,0:T(8,128)(2,1)S(1)}, u32[]{:S(2)}, u32[]{:S(2)}) collective-permute-start(bf16[160,256]{1,0:T(8,128)(2,1)S(1)} %get-tuple-element.115), channel_id=1, source_target_pairs={{0,24},{4,28},{8,16},{12,20},{16,8},{20,12},{24,0},{28,4},{1,25},{... | collective-permute-start | bytes 245768 | tf_op jit(solution)/shard_map/ppermute | solution.py:566
  76.8 8.5 %collective-permute-start.27 = (bf16[160,256]{1,0:T(8,128)(2,1)S(1)}, bf16[160,256]{1,0:T(8,128)(2,1)S(1)}, u32[]{:S(2)}, u32[]{:S(2)}) collective-permute-start(bf16[160,256]{1,0:T(8,128)(2,1)S(1)} %get-tuple-element.117), channel_id=1, source_target_pairs={{0,8},{4,12},{8,0},{12,4},{16,24},{20,28},{24,16},{28,20},{1,9},{5... | collective-permute-start | bytes 245768 | tf_op jit(solution)/shard_map/ppermute | solution.py:566
  77.1 8.2 %collective-permute-start.26 = (bf16[144,256]{1,0:T(8,128)(2,1)S(1)}, bf16[144,256]{1,0:T(8,128)(2,1)S(1)}, u32[]{:S(2)}, u32[]{:S(2)}) collective-permute-start(bf16[144,256]{1,0:T(8,128)(2,1)S(1)} %get-tuple-element.116), channel_id=1, source_target_pairs={{0,8},{4,12},{8,0},{12,4},{16,24},{20,28},{24,16},{28,20},{1,9},{5... | collective-permute-start | bytes 221192 | tf_op jit(solution)/shard_map/ppermute | solution.py:566
  78.9 8.3 %collective-permute-start.29 = (bf16[144,256]{1,0:T(8,128)(2,1)S(1)}, bf16[144,256]{1,0:T(8,128)(2,1)S(1)}, u32[]{:S(2)}, u32[]{:S(2)}) collective-permute-start(bf16[144,256]{1,0:T(8,128)(2,1)S(1)} %shard_map.120), channel_id=1, source_target_pairs={{0,16},{4,20},{8,24},{12,28},{16,0},{20,4},{24,8},{28,12},{1,17},{... | collective-permute-start | bytes 221192 | tf_op jit(solution)/shard_map/ppermute | solution.py:566
  87.5 7.2 %collective-permute-start.32 = (bf16[144,256]{1,0:T(8,128)(2,1)S(1)}, bf16[144,256]{1,0:T(8,128)(2,1)S(1)}, u32[]{:S(2)}, u32[]{:S(2)}) collective-permute-start(bf16[144,256]{1,0:T(8,128)(2,1)S(1)} %get-tuple-element.124), channel_id=1, source_target_pairs={{0,16},{4,20},{8,24},{12,28},{16,0},{20,4},{24,8},{28,12},{1,17},{... | collective-permute-start | bytes 221192 | tf_op jit(solution)/shard_map/ppermute | solution.py:566
  88.0 12.2 %collective-permute-start.30 = (bf16[272,256]{1,0:T(8,128)(2,1)S(1)}, bf16[272,256]{1,0:T(8,128)(2,1)S(1)}, u32[]{:S(2)}, u32[]{:S(2)}) collective-permute-start(bf16[272,256]{1,0:T(8,128)(2,1)S(1)} %get-tuple-element.122), channel_id=1, source_target_pairs={{0,8},{4,12},{8,0},{12,4},{16,24},{20,28},{24,16},{28,20},{1,9},{5... | collective-permute-start | bytes 417800 | tf_op jit(solution)/shard_map/ppermute | solution.py:566
  90.3 9.1 %collective-permute-start.35 = (bf16[160,256]{1,0:T(8,128)(2,1)S(1)}, bf16[160,256]{1,0:T(8,128)(2,1)S(1)}, u32[]{:S(2)}, u32[]{:S(2)}) collective-permute-start(bf16[160,256]{1,0:T(8,128)(2,1)S(1)} %get-tuple-element.125), channel_id=1, source_target_pairs={{0,24},{4,28},{8,16},{12,20},{16,8},{20,12},{24,0},{28,4},{1,25},{... | collective-permute-start | bytes 245768 | tf_op jit(solution)/shard_map/ppermute | solution.py:566
  92.0 8.2 %collective-permute-start.33 = (bf16[160,256]{1,0:T(8,128)(2,1)S(1)}, bf16[160,256]{1,0:T(8,128)(2,1)S(1)}, u32[]{:S(2)}, u32[]{:S(2)}) collective-permute-start(bf16[160,256]{1,0:T(8,128)(2,1)S(1)} %get-tuple-element.125), channel_id=1, source_target_pairs={{0,16},{4,20},{8,24},{12,28},{16,0},{20,4},{24,8},{28,12},{1,17},{... | collective-permute-start | bytes 245768 | tf_op jit(solution)/shard_map/ppermute | solution.py:566
  94.7 5.4 %collective-permute-start.34 = (bf16[144,256]{1,0:T(8,128)(2,1)S(1)}, bf16[144,256]{1,0:T(8,128)(2,1)S(1)}, u32[]{:S(2)}, u32[]{:S(2)}) collective-permute-start(bf16[144,256]{1,0:T(8,128)(2,1)S(1)} %collective-permute-done.32.refs_3_), channel_id=1, source_target_pairs={{0,8},{4,12},{8,0},{12,4},{16,24},{20,28},{24,16},{28,20},{1,9},{5... | collective-permute-start | bytes 221192 | tf_op jit(solution)/shard_map/ppermute | solution.py:566
  94.7 4.7 %collective-permute-start.31 = (bf16[32,256]{1,0:T(8,128)(2,1)S(1)}, bf16[32,256]{1,0:T(8,128)(2,1)S(1)}, u32[]{:S(2)}, u32[]{:S(2)}) collective-permute-start(bf16[32,256]{1,0:T(8,128)(2,1)S(1)} %get-tuple-element.123), channel_id=1, source_target_pairs={{0,8},{4,12},{8,0},{12,4},{16,24},{20,28},{24,16},{28,20},{1,9},{5... | collective-permute-start | bytes 49160 | tf_op jit(solution)/shard_map/ppermute | solution.py:566
  102.5 5.4 %collective-permute-start.37 = (bf16[304,128]{1,0:T(8,128)(2,1)S(1)}, bf16[304,128]{1,0:T(8,128)(2,1)S(1)}, u32[]{:S(2)}, u32[]{:S(2)}) collective-permute-start(bf16[304,128]{1,0:T(8,128)(2,1)S(1)} %get-tuple-element.127), channel_id=1, source_target_pairs={{0,3},{1,2},{2,1},{3,0},{4,7},{5,6},{6,5},{7,4},{8,11},{9,10},{10,... | collective-permute-start | bytes 233480 | tf_op jit(solution)/shard_map/ppermute | solution.py:569
  (14 other events, 72.8 us)

commit v24 on v23

--- a/solution.py
+++ b/solution.py
@@ -541,7 +541,7 @@
     via = chips == 4
     if via:
         one, two = (0, some), (some, rest)
-        most = rows - 32
+        most = rows - 64
         near_parts = [(0, most), (most, rows - most)]
         plan = [(0, 0, rows), *((1, *part) for part in near_parts)]
         plan += [(2, *one), (2, *two), (3, *one), (3, *two)]

time: 111 us -> 112 us (level)
  starting transfers between devices: 42.5 us -> 45.8 us
  waiting for transfers between devices: 50.3 us -> 47.1 us
    ppermute x24, waiting for transfers between devices: 26.1 us -> 23.7 us  [along(): return lax.ppermute(x, 'slab', [(s, s ^ 2 * i) for s in range(n_slab)])]
    ppermute x24, starting transfers between devices: 29.4 us -> 31.4 us  [along(): return lax.ppermute(x, 'slab', [(s, s ^ 2 * i) for s in range(n_slab)])]
    ppermute x11, starting transfers between devices: 12.3 us -> 14 us  [plane(): return lax.ppermute(x, 'obs', [(o, o ^ i) for o in range(n_obs)])]
where the time goes in v24:
time: 112 us
  waiting for transfers between devices  47.1 us (42%)
  starting transfers between devices  45.8 us (41%)
  Pallas kernels  14.9 us (13%)
  local copies, waits for them, and re-layouts  2.09 us (2%)
  between operations  1.6 us (1%)
    ppermute x24, starting transfers between devices, along(): return lax.ppermute(x, 'slab', [(s, s ^ 2 * i) for s in range(n_slab)])  31.4 us
    ppermute x24, waiting for transfers between devices, along(): return lax.ppermute(x, 'slab', [(s, s ^ 2 * i) for s in range(n_slab)])  23.7 us
    ppermute x11, waiting for transfers between devices, plane(): return lax.ppermute(x, 'obs', [(o, o ^ i) for o in range(n_obs)])  19.1 us
    pallas_call x23, Pallas kernels, call(): pl.pallas_call(kernel, out_shape=outs, in_specs=[space] * len(args), out_...  14.9 us
    ppermute x11, starting transfers between devices, plane(): return lax.ppermute(x, 'obs', [(o, o ^ i) for o in range(n_obs)])  14 us
    ppermute x5, waiting for transfers between devices, swap(): return lax.ppermute(x, 'slab', [(s, s ^ 1) for s in range(n_slab)])  4.24 us
  transfers between devices with their start and end apart: 40, of which 24 were waited for; matrix products, arithmetic and copies ran while one was open for 0% of the time, Pallas kernels for 4%

profile of v24, /device:TPU:0, one launch (start us, length us, event | category | flops | bytes accessed | tf_op | source)
XLA Modules:
  0.0 111.6 jit_solution(3464486683318672749)
XLA Ops:
  1.3 5.5 %shard_map.104 = (bf16[4,4,128,256]{3,2,1,0:T(8,128)(2,1)}, bf16[4,4,128,256]{3,2,1,0:T(8,128)(2,1)}, bf16[304,256]{1,0:T(8,128)(2,1)}, bf16[304,256]{1,0:T(8,128)(2,1)}) custom-call(s32[4]{0:T(128)} %seeds_in.1, s32[1,1,32]{2,1,0:T(1,128)} %ids_in.1, s32[1,1,32]{2,1,0:T(1,128)} %cols_in.1, s32[1,1]{1,0:T(1,128)S(6)} %copy.16.count_in, f32[1,128]{1,0:T(1,128)} %refs_4_.1, ...), custom_call_target="tpu_custom_call" | custom-call | flops 637534208 | bytes 5735188 | tf_op jit(solution)/shard_map/pallas_call | solution.py:23
  6.9 2.5 %collective-permute-start = (bf16[304,256]{1,0:T(8,128)(2,1)}, bf16[304,256]{1,0:T(8,128)(2,1)S(1)}, u32[]{:S(2)}, u32[]{:S(2)}) collective-permute-start(bf16[304,256]{1,0:T(8,128)(2,1)} %get-tuple-element.70.refs_0_), channel_id=1, source_target_pairs={{0,1},{1,0},{2,3},{3,2},{4,5},{5,4},{6,7},{7,6},{8,9},{9,8},{10,11... | collective-permute-start | bytes 466952 | tf_op jit(solution)/shard_map/ppermute | solution.py:569
  9.4 1.7 %collective-permute-start.1 = (bf16[304,256]{1,0:T(8,128)(2,1)}, bf16[304,256]{1,0:T(8,128)(2,1)S(1)}, u32[]{:S(2)}, u32[]{:S(2)}) collective-permute-start(bf16[304,256]{1,0:T(8,128)(2,1)} %get-tuple-element.71.refs_1_), channel_id=1, source_target_pairs={{0,2},{1,3},{2,0},{3,1},{4,6},{5,7},{6,4},{7,5},{8,10},{9,11},{10,... | collective-permute-start | bytes 466952 | tf_op jit(solution)/shard_map/ppermute | solution.py:569
  14.2 1.5 %collective-permute-done.1.two_more = bf16[304,256]{1,0:T(8,128)(2,1)S(1)} collective-permute-done((bf16[304,256]{1,0:T(8,128)(2,1)}, bf16[304,256]{1,0:T(8,128)(2,1)S(1)}, u32[]{:S(2)}, u32[]{:S(2)}) %collective-permute-start.1) | collective-permute-done | bytes 155680 | tf_op jit(solution)/shard_map/ppermute | solution.py:569
  15.8 1.5 %collective-permute-start.2 = (bf16[304,256]{1,0:T(8,128)(2,1)S(1)}, bf16[304,256]{1,0:T(8,128)(2,1)S(1)}, u32[]{:S(2)}, u32[]{:S(2)}) collective-permute-start(bf16[304,256]{1,0:T(8,128)(2,1)S(1)} %get-tuple-element.74.refs_0_), channel_id=1, source_target_pairs={{0,2},{1,3},{2,0},{3,1},{4,6},{5,7},{6,4},{7,5},{8,10},{9,11},{10,... | collective-permute-start | bytes 466952 | tf_op jit(solution)/shard_map/ppermute | solution.py:569
  18.1 3.0 %collective-permute-done.2.refs_1_ = bf16[304,256]{1,0:T(8,128)(2,1)S(1)} collective-permute-done((bf16[304,256]{1,0:T(8,128)(2,1)S(1)}, bf16[304,256]{1,0:T(8,128)(2,1)S(1)}, u32[]{:S(2)}, u32[]{:S(2)}) %collective-permute-start.2) | collective-permute-done | bytes 155680 | tf_op jit(solution)/shard_map/ppermute | solution.py:569
  21.1 1.4 %collective-permute-done.3.refs_3_ = bf16[304,256]{1,0:T(8,128)(2,1)S(1)} collective-permute-done((bf16[304,256]{1,0:T(8,128)(2,1)S(1)}, bf16[304,256]{1,0:T(8,128)(2,1)S(1)}, u32[]{:S(2)}, u32[]{:S(2)}) %collective-permute-start.3) | collective-permute-done | bytes 155680 | tf_op jit(solution)/shard_map/ppermute | solution.py:569
  25.8 1.7 %collective-permute-start.10 = (bf16[144,256]{1,0:T(8,128)(2,1)S(1)}, bf16[144,256]{1,0:T(8,128)(2,1)S(1)}, u32[]{:S(2)}, u32[]{:S(2)}) collective-permute-start(bf16[144,256]{1,0:T(8,128)(2,1)S(1)} %get-tuple-element.92), channel_id=1, source_target_pairs={{0,8},{4,12},{8,0},{12,4},{16,24},{20,28},{24,16},{28,20},{1,9},{5... | collective-permute-start | bytes 221192 | tf_op jit(solution)/shard_map/ppermute | solution.py:566
  27.5 2.6 %collective-permute-start.6 = (bf16[160,256]{1,0:T(8,128)(2,1)S(1)}, bf16[160,256]{1,0:T(8,128)(2,1)S(1)}, u32[]{:S(2)}, u32[]{:S(2)}) collective-permute-start(bf16[160,256]{1,0:T(8,128)(2,1)S(1)} %get-tuple-element.87), channel_id=1, source_target_pairs={{0,16},{4,20},{8,24},{12,28},{16,0},{20,4},{24,8},{28,12},{1,17},{... | collective-permute-start | bytes 245768 | tf_op jit(solution)/shard_map/ppermute | solution.py:566
  31.0 1.5 %collective-permute-start.8 = (bf16[144,256]{1,0:T(8,128)(2,1)S(1)}, bf16[144,256]{1,0:T(8,128)(2,1)S(1)}, u32[]{:S(2)}, u32[]{:S(2)}) collective-permute-start(bf16[144,256]{1,0:T(8,128)(2,1)S(1)} %get-tuple-element.89), channel_id=1, source_target_pairs={{0,8},{4,12},{8,0},{12,4},{16,24},{20,28},{24,16},{28,20},{1,9},{5... | collective-permute-start | bytes 221192 | tf_op jit(solution)/shard_map/ppermute | solution.py:566
  32.5 2.1 %collective-permute-start.11 = (bf16[144,256]{1,0:T(8,128)(2,1)S(1)}, bf16[144,256]{1,0:T(8,128)(2,1)S(1)}, u32[]{:S(2)}, u32[]{:S(2)}) collective-permute-start(bf16[144,256]{1,0:T(8,128)(2,1)S(1)} %shard_map.110), channel_id=1, source_target_pairs={{0,16},{4,20},{8,24},{12,28},{16,0},{20,4},{24,8},{28,12},{1,17},{... | collective-permute-start | bytes 221192 | tf_op jit(solution)/shard_map/ppermute | solution.py:566
  34.9 4.0 %collective-permute-done.8.refs_3_ = bf16[144,256]{1,0:T(8,128)(2,1)S(1)} collective-permute-done((bf16[144,256]{1,0:T(8,128)(2,1)S(1)}, bf16[144,256]{1,0:T(8,128)(2,1)S(1)}, u32[]{:S(2)}, u32[]{:S(2)}) %collective-permute-start.8) | collective-permute-done | bytes 73760 | tf_op jit(solution)/shard_map/ppermute | solution.py:566
  38.9 1.6 %collective-permute-done.11.refs_5_ = bf16[144,256]{1,0:T(8,128)(2,1)S(1)} collective-permute-done((bf16[144,256]{1,0:T(8,128)(2,1)S(1)}, bf16[144,256]{1,0:T(8,128)(2,1)S(1)}, u32[]{:S(2)}, u32[]{:S(2)}) %collective-permute-start.11) | collective-permute-done | bytes 73760 | tf_op jit(solution)/shard_map/ppermute | solution.py:566
  40.6 1.8 %collective-permute-start.14 = (bf16[144,256]{1,0:T(8,128)(2,1)S(1)}, bf16[144,256]{1,0:T(8,128)(2,1)S(1)}, u32[]{:S(2)}, u32[]{:S(2)}) collective-permute-start(bf16[144,256]{1,0:T(8,128)(2,1)S(1)} %get-tuple-element.96), channel_id=1, source_target_pairs={{0,16},{4,20},{8,24},{12,28},{16,0},{20,4},{24,8},{28,12},{1,17},{... | collective-permute-start | bytes 221192 | tf_op jit(solution)/shard_map/ppermute | solution.py:566
  42.4 2.3 %collective-permute-start.12 = (bf16[240,256]{1,0:T(8,128)(2,1)S(1)}, bf16[240,256]{1,0:T(8,128)(2,1)S(1)}, u32[]{:S(2)}, u32[]{:S(2)}) collective-permute-start(bf16[240,256]{1,0:T(8,128)(2,1)S(1)} %get-tuple-element.94), channel_id=1, source_target_pairs={{0,8},{4,12},{8,0},{12,4},{16,24},{20,28},{24,16},{28,20},{1,9},{5... | collective-permute-start | bytes 368648 | tf_op jit(solution)/shard_map/ppermute | solution.py:566
  46.4 2.7 %collective-permute-start.16 = (bf16[144,256]{1,0:T(8,128)(2,1)S(1)}, bf16[144,256]{1,0:T(8,128)(2,1)S(1)}, u32[]{:S(2)}, u32[]{:S(2)}) collective-permute-start(bf16[144,256]{1,0:T(8,128)(2,1)S(1)} %collective-permute-done.14.refs_3_), channel_id=1, source_target_pairs={{0,8},{4,12},{8,0},{12,4},{16,24},{20,28},{24,16},{28,20},{1,9},{5... | collective-permute-start | bytes 221192 | tf_op jit(solution)/shard_map/ppermute | solution.py:566
  49.2 4.8 %collective-permute-done.13.refs_2_ = bf16[64,256]{1,0:T(8,128)(2,1)S(1)} collective-permute-done((bf16[64,256]{1,0:T(8,128)(2,1)S(1)}, bf16[64,256]{1,0:T(8,128)(2,1)S(1)}, u32[]{:S(2)}, u32[]{:S(2)}) %collective-permute-start.13) | collective-permute-done | bytes 32800 | tf_op jit(solution)/shard_map/ppermute | solution.py:566
  58.0 4.4 %collective-permute-done.19.one_more = bf16[304,256]{1,0:T(8,128)(2,1)S(1)} collective-permute-done((bf16[304,256]{1,0:T(8,128)(2,1)S(1)}, bf16[304,256]{1,0:T(8,128)(2,1)S(1)}, u32[]{:S(2)}, u32[]{:S(2)}) %collective-permute-start.19) | collective-permute-done | bytes 155680 | tf_op jit(solution)/shard_map/ppermute | solution.py:569
  64.1 1.7 %collective-permute-start.22 = (bf16[304,256]{1,0:T(8,128)(2,1)S(1)}, bf16[304,256]{1,0:T(8,128)(2,1)S(1)}, u32[]{:S(2)}, u32[]{:S(2)}) collective-permute-start(bf16[304,256]{1,0:T(8,128)(2,1)S(1)} %get-tuple-element.101.refs_2_), channel_id=1, source_target_pairs={{0,1},{1,0},{2,3},{3,2},{4,5},{5,4},{6,7},{7,6},{8,9},{9,8},{10,11... | collective-permute-start | bytes 466952 | tf_op jit(solution)/shard_map/ppermute | solution.py:569
  65.8 2.9 %collective-permute-done.21.refs_1_ = bf16[304,256]{1,0:T(8,128)(2,1)S(1)} collective-permute-done((bf16[304,256]{1,0:T(8,128)(2,1)S(1)}, bf16[304,256]{1,0:T(8,128)(2,1)S(1)}, u32[]{:S(2)}, u32[]{:S(2)}) %collective-permute-start.21) | collective-permute-done | bytes 155680 | tf_op jit(solution)/shard_map/ppermute | solution.py:569
  69.4 1.2 %shard_map.117 = (f32[4,80,512]{2,1,0:T(8,128)S(1)}, f32[4,80,128]{2,1,0:T(8,128)S(1)}, bf16[304,512]{1,0:T(8,128)(2,1)S(1)}) custom-call(bf16[304,256]{1,0:T(8,128)(2,1)S(1)} %get-tuple-element.100.refs_0_, bf16[304,256]{1,0:T(8,128)(2,1)S(1)} %collective-permute-done.21.refs_1_, bf16[304,256]{1,0:T(8,128)(2,1)S(1)} %get-tuple-element.101.refs_2_, ...), custom_call_target="tpu_custom_call" | custom-call | flops 149422080 | bytes 2503680 | tf_op jit(solution)/shard_map/pallas_call | solution.py:23
  73.4 2.1 %collective-permute-start.24 = (bf16[160,256]{1,0:T(8,128)(2,1)S(1)}, bf16[160,256]{1,0:T(8,128)(2,1)S(1)}, u32[]{:S(2)}, u32[]{:S(2)}) collective-permute-start(bf16[160,256]{1,0:T(8,128)(2,1)S(1)} %get-tuple-element.114), channel_id=1, source_target_pairs={{0,16},{4,20},{8,24},{12,28},{16,0},{20,4},{24,8},{28,12},{1,17},{... | collective-permute-start | bytes 245768 | tf_op jit(solution)/shard_map/ppermute | solution.py:566
  75.5 1.7 %collective-permute-start.25 = (bf16[160,256]{1,0:T(8,128)(2,1)S(1)}, bf16[160,256]{1,0:T(8,128)(2,1)S(1)}, u32[]{:S(2)}, u32[]{:S(2)}) collective-permute-start(bf16[160,256]{1,0:T(8,128)(2,1)S(1)} %get-tuple-element.115), channel_id=1, source_target_pairs={{0,24},{4,28},{8,16},{12,20},{16,8},{20,12},{24,0},{28,4},{1,25},{... | collective-permute-start | bytes 245768 | tf_op jit(solution)/shard_map/ppermute | solution.py:566
  77.3 2.0 %collective-permute-start.26 = (bf16[144,256]{1,0:T(8,128)(2,1)S(1)}, bf16[144,256]{1,0:T(8,128)(2,1)S(1)}, u32[]{:S(2)}, u32[]{:S(2)}) collective-permute-start(bf16[144,256]{1,0:T(8,128)(2,1)S(1)} %get-tuple-element.116), channel_id=1, source_target_pairs={{0,8},{4,12},{8,0},{12,4},{16,24},{20,28},{24,16},{28,20},{1,9},{5... | collective-permute-start | bytes 221192 | tf_op jit(solution)/shard_map/ppermute | solution.py:566
  80.3 5.9 %collective-permute-done.26.refs_3_ = bf16[144,256]{1,0:T(8,128)(2,1)S(1)} collective-permute-done((bf16[144,256]{1,0:T(8,128)(2,1)S(1)}, bf16[144,256]{1,0:T(8,128)(2,1)S(1)}, u32[]{:S(2)}, u32[]{:S(2)}) %collective-permute-start.26) | collective-permute-done | bytes 73760 | tf_op jit(solution)/shard_map/ppermute | solution.py:566
  88.1 2.6 %collective-permute-start.30 = (bf16[240,256]{1,0:T(8,128)(2,1)S(1)}, bf16[240,256]{1,0:T(8,128)(2,1)S(1)}, u32[]{:S(2)}, u32[]{:S(2)}) collective-permute-start(bf16[240,256]{1,0:T(8,128)(2,1)S(1)} %get-tuple-element.122), channel_id=1, source_target_pairs={{0,8},{4,12},{8,0},{12,4},{16,24},{20,28},{24,16},{28,20},{1,9},{5... | collective-permute-start | bytes 368648 | tf_op jit(solution)/shard_map/ppermute | solution.py:566
  92.2 2.1 %collective-permute-done.32.refs_3_ = bf16[144,256]{1,0:T(8,128)(2,1)S(1)} collective-permute-done((bf16[144,256]{1,0:T(8,128)(2,1)S(1)}, bf16[144,256]{1,0:T(8,128)(2,1)S(1)}, u32[]{:S(2)}, u32[]{:S(2)}) %collective-permute-start.32) | collective-permute-done | bytes 73760 | tf_op jit(solution)/shard_map/ppermute | solution.py:566
  96.3 3.2 %collective-permute-done.31.refs_2_ = bf16[64,256]{1,0:T(8,128)(2,1)S(1)} collective-permute-done((bf16[64,256]{1,0:T(8,128)(2,1)S(1)}, bf16[64,256]{1,0:T(8,128)(2,1)S(1)}, u32[]{:S(2)}, u32[]{:S(2)}) %collective-permute-start.31) | collective-permute-done | bytes 32800 | tf_op jit(solution)/shard_map/ppermute | solution.py:566
  102.9 1.6 %collective-permute-start.37 = (bf16[304,128]{1,0:T(8,128)(2,1)S(1)}, bf16[304,128]{1,0:T(8,128)(2,1)S(1)}, u32[]{:S(2)}, u32[]{:S(2)}) collective-permute-start(bf16[304,128]{1,0:T(8,128)(2,1)S(1)} %get-tuple-element.127), channel_id=1, source_target_pairs={{0,3},{1,2},{2,1},{3,0},{4,7},{5,6},{6,5},{7,4},{8,11},{9,10},{10,... | collective-permute-start | bytes 233480 | tf_op jit(solution)/shard_map/ppermute | solution.py:569
  104.6 1.6 %collective-permute-start.38 = (bf16[304,128]{1,0:T(8,128)(2,1)S(1)}, bf16[304,128]{1,0:T(8,128)(2,1)S(1)}, u32[]{:S(2)}, u32[]{:S(2)}) collective-permute-start(bf16[304,128]{1,0:T(8,128)(2,1)S(1)} %get-tuple-element.128), channel_id=1, source_target_pairs={{0,2},{1,3},{2,0},{3,1},{4,6},{5,7},{6,4},{7,5},{8,10},{9,11},{10,... | collective-permute-start | bytes 233480 | tf_op jit(solution)/shard_map/ppermute | solution.py:569
  106.8 1.6 %collective-permute-done.37.refs_1_ = bf16[304,128]{1,0:T(8,128)(2,1)S(1)} collective-permute-done((bf16[304,128]{1,0:T(8,128)(2,1)S(1)}, bf16[304,128]{1,0:T(8,128)(2,1)S(1)}, u32[]{:S(2)}, u32[]{:S(2)}) %collective-permute-start.37) | collective-permute-done | bytes 77856 | tf_op jit(solution)/shard_map/ppermute | solution.py:569
  108.5 1.5 %collective-permute-done.38.refs_2_ = bf16[304,128]{1,0:T(8,128)(2,1)S(1)} collective-permute-done((bf16[304,128]{1,0:T(8,128)(2,1)S(1)}, bf16[304,128]{1,0:T(8,128)(2,1)S(1)}, u32[]{:S(2)}, u32[]{:S(2)}) %collective-permute-start.38) | collective-permute-done | bytes 77856 | tf_op jit(solution)/shard_map/ppermute | solution.py:569
  (90 shorter events, 31.4 us)
Async XLA Ops:
  6.8 18.5 %collective-permute-start.5 = (bf16[4,4,128,256]{3,2,1,0:T(8,128)(2,1)}, bf16[4,4,128,256]{3,2,1,0:T(8,128)(2,1)S(1)}, u32[]{:S(2)}, u32[]{:S(2)}) collective-permute-start(bf16[4,4,128,256]{3,2,1,0:T(8,128)(2,1)} %get-tuple-element.77), channel_id=1, source_target_pairs={{0,4},{4,0},{8,12},{12,8},{16,20},{20,16},{24,28},{28,24},{1,5},{5... | collective-permute-start | bytes 3145736 | tf_op jit(solution)/shard_map/ppermute | solution.py:572
  6.9 7.4 %collective-permute-start = (bf16[304,256]{1,0:T(8,128)(2,1)}, bf16[304,256]{1,0:T(8,128)(2,1)S(1)}, u32[]{:S(2)}, u32[]{:S(2)}) collective-permute-start(bf16[304,256]{1,0:T(8,128)(2,1)} %get-tuple-element.70.refs_0_), channel_id=1, source_target_pairs={{0,1},{1,0},{2,3},{3,2},{4,5},{5,4},{6,7},{7,6},{8,9},{9,8},{10,11... | collective-permute-start | bytes 466952 | tf_op jit(solution)/shard_map/ppermute | solution.py:569
  9.4 6.3 %collective-permute-start.1 = (bf16[304,256]{1,0:T(8,128)(2,1)}, bf16[304,256]{1,0:T(8,128)(2,1)S(1)}, u32[]{:S(2)}, u32[]{:S(2)}) collective-permute-start(bf16[304,256]{1,0:T(8,128)(2,1)} %get-tuple-element.71.refs_1_), channel_id=1, source_target_pairs={{0,2},{1,3},{2,0},{3,1},{4,6},{5,7},{6,4},{7,5},{8,10},{9,11},{10,... | collective-permute-start | bytes 466952 | tf_op jit(solution)/shard_map/ppermute | solution.py:569
  15.8 5.3 %collective-permute-start.2 = (bf16[304,256]{1,0:T(8,128)(2,1)S(1)}, bf16[304,256]{1,0:T(8,128)(2,1)S(1)}, u32[]{:S(2)}, u32[]{:S(2)}) collective-permute-start(bf16[304,256]{1,0:T(8,128)(2,1)S(1)} %get-tuple-element.74.refs_0_), channel_id=1, source_target_pairs={{0,2},{1,3},{2,0},{3,1},{4,6},{5,7},{6,4},{7,5},{8,10},{9,11},{10,... | collective-permute-start | bytes 466952 | tf_op jit(solution)/shard_map/ppermute | solution.py:569
  17.3 5.2 %collective-permute-start.3 = (bf16[304,256]{1,0:T(8,128)(2,1)S(1)}, bf16[304,256]{1,0:T(8,128)(2,1)S(1)}, u32[]{:S(2)}, u32[]{:S(2)}) collective-permute-start(bf16[304,256]{1,0:T(8,128)(2,1)S(1)} %get-tuple-element.75.refs_2_), channel_id=1, source_target_pairs={{0,1},{1,0},{2,3},{3,2},{4,5},{5,4},{6,7},{7,6},{8,9},{9,8},{10,11... | collective-permute-start | bytes 466952 | tf_op jit(solution)/shard_map/ppermute | solution.py:569
  25.8 6.7 %collective-permute-start.10 = (bf16[144,256]{1,0:T(8,128)(2,1)S(1)}, bf16[144,256]{1,0:T(8,128)(2,1)S(1)}, u32[]{:S(2)}, u32[]{:S(2)}) collective-permute-start(bf16[144,256]{1,0:T(8,128)(2,1)S(1)} %get-tuple-element.92), channel_id=1, source_target_pairs={{0,8},{4,12},{8,0},{12,4},{16,24},{20,28},{24,16},{28,20},{1,9},{5... | collective-permute-start | bytes 221192 | tf_op jit(solution)/shard_map/ppermute | solution.py:566
  27.5 11.4 %collective-permute-start.6 = (bf16[160,256]{1,0:T(8,128)(2,1)S(1)}, bf16[160,256]{1,0:T(8,128)(2,1)S(1)}, u32[]{:S(2)}, u32[]{:S(2)}) collective-permute-start(bf16[160,256]{1,0:T(8,128)(2,1)S(1)} %get-tuple-element.87), channel_id=1, source_target_pairs={{0,16},{4,20},{8,24},{12,28},{16,0},{20,4},{24,8},{28,12},{1,17},{... | collective-permute-start | bytes 245768 | tf_op jit(solution)/shard_map/ppermute | solution.py:566
  30.1 8.7 %collective-permute-start.7 = (bf16[160,256]{1,0:T(8,128)(2,1)S(1)}, bf16[160,256]{1,0:T(8,128)(2,1)S(1)}, u32[]{:S(2)}, u32[]{:S(2)}) collective-permute-start(bf16[160,256]{1,0:T(8,128)(2,1)S(1)} %get-tuple-element.88), channel_id=1, source_target_pairs={{0,24},{4,28},{8,16},{12,20},{16,8},{20,12},{24,0},{28,4},{1,25},{... | collective-permute-start | bytes 245768 | tf_op jit(solution)/shard_map/ppermute | solution.py:566
  30.4 8.4 %collective-permute-start.9 = (bf16[160,256]{1,0:T(8,128)(2,1)S(1)}, bf16[160,256]{1,0:T(8,128)(2,1)S(1)}, u32[]{:S(2)}, u32[]{:S(2)}) collective-permute-start(bf16[160,256]{1,0:T(8,128)(2,1)S(1)} %get-tuple-element.90), channel_id=1, source_target_pairs={{0,8},{4,12},{8,0},{12,4},{16,24},{20,28},{24,16},{28,20},{1,9},{5... | collective-permute-start | bytes 245768 | tf_op jit(solution)/shard_map/ppermute | solution.py:566
  31.0 7.8 %collective-permute-start.8 = (bf16[144,256]{1,0:T(8,128)(2,1)S(1)}, bf16[144,256]{1,0:T(8,128)(2,1)S(1)}, u32[]{:S(2)}, u32[]{:S(2)}) collective-permute-start(bf16[144,256]{1,0:T(8,128)(2,1)S(1)} %get-tuple-element.89), channel_id=1, source_target_pairs={{0,8},{4,12},{8,0},{12,4},{16,24},{20,28},{24,16},{28,20},{1,9},{5... | collective-permute-start | bytes 221192 | tf_op jit(solution)/shard_map/ppermute | solution.py:566
  32.5 8.0 %collective-permute-start.11 = (bf16[144,256]{1,0:T(8,128)(2,1)S(1)}, bf16[144,256]{1,0:T(8,128)(2,1)S(1)}, u32[]{:S(2)}, u32[]{:S(2)}) collective-permute-start(bf16[144,256]{1,0:T(8,128)(2,1)S(1)} %shard_map.110), channel_id=1, source_target_pairs={{0,16},{4,20},{8,24},{12,28},{16,0},{20,4},{24,8},{28,12},{1,17},{... | collective-permute-start | bytes 221192 | tf_op jit(solution)/shard_map/ppermute | solution.py:566
  40.6 5.8 %collective-permute-start.14 = (bf16[144,256]{1,0:T(8,128)(2,1)S(1)}, bf16[144,256]{1,0:T(8,128)(2,1)S(1)}, u32[]{:S(2)}, u32[]{:S(2)}) collective-permute-start(bf16[144,256]{1,0:T(8,128)(2,1)S(1)} %get-tuple-element.96), channel_id=1, source_target_pairs={{0,16},{4,20},{8,24},{12,28},{16,0},{20,4},{24,8},{28,12},{1,17},{... | collective-permute-start | bytes 221192 | tf_op jit(solution)/shard_map/ppermute | solution.py:566
  42.4 11.6 %collective-permute-start.12 = (bf16[240,256]{1,0:T(8,128)(2,1)S(1)}, bf16[240,256]{1,0:T(8,128)(2,1)S(1)}, u32[]{:S(2)}, u32[]{:S(2)}) collective-permute-start(bf16[240,256]{1,0:T(8,128)(2,1)S(1)} %get-tuple-element.94), channel_id=1, source_target_pairs={{0,8},{4,12},{8,0},{12,4},{16,24},{20,28},{24,16},{28,20},{1,9},{5... | collective-permute-start | bytes 368648 | tf_op jit(solution)/shard_map/ppermute | solution.py:566
  44.8 9.2 %collective-permute-start.17 = (bf16[160,256]{1,0:T(8,128)(2,1)S(1)}, bf16[160,256]{1,0:T(8,128)(2,1)S(1)}, u32[]{:S(2)}, u32[]{:S(2)}) collective-permute-start(bf16[160,256]{1,0:T(8,128)(2,1)S(1)} %get-tuple-element.97), channel_id=1, source_target_pairs={{0,24},{4,28},{8,16},{12,20},{16,8},{20,12},{24,0},{28,4},{1,25},{... | collective-permute-start | bytes 245768 | tf_op jit(solution)/shard_map/ppermute | solution.py:566
  45.1 8.9 %collective-permute-start.15 = (bf16[160,256]{1,0:T(8,128)(2,1)S(1)}, bf16[160,256]{1,0:T(8,128)(2,1)S(1)}, u32[]{:S(2)}, u32[]{:S(2)}) collective-permute-start(bf16[160,256]{1,0:T(8,128)(2,1)S(1)} %get-tuple-element.97), channel_id=1, source_target_pairs={{0,16},{4,20},{8,24},{12,28},{16,0},{20,4},{24,8},{28,12},{1,17},{... | collective-permute-start | bytes 245768 | tf_op jit(solution)/shard_map/ppermute | solution.py:566
  46.4 7.6 %collective-permute-start.16 = (bf16[144,256]{1,0:T(8,128)(2,1)S(1)}, bf16[144,256]{1,0:T(8,128)(2,1)S(1)}, u32[]{:S(2)}, u32[]{:S(2)}) collective-permute-start(bf16[144,256]{1,0:T(8,128)(2,1)S(1)} %collective-permute-done.14.refs_3_), channel_id=1, source_target_pairs={{0,8},{4,12},{8,0},{12,4},{16,24},{20,28},{24,16},{28,20},{1,9},{5... | collective-permute-start | bytes 221192 | tf_op jit(solution)/shard_map/ppermute | solution.py:566
  56.3 6.1 %collective-permute-start.19 = (bf16[304,256]{1,0:T(8,128)(2,1)S(1)}, bf16[304,256]{1,0:T(8,128)(2,1)S(1)}, u32[]{:S(2)}, u32[]{:S(2)}) collective-permute-start(bf16[304,256]{1,0:T(8,128)(2,1)S(1)} %get-tuple-element.98.one), channel_id=1, source_target_pairs={{0,1},{1,0},{2,3},{3,2},{4,5},{5,4},{6,7},{7,6},{8,9},{9,8},{10,11... | collective-permute-start | bytes 466952 | tf_op jit(solution)/shard_map/ppermute | solution.py:569
  57.5 5.8 %collective-permute-start.20 = (bf16[304,256]{1,0:T(8,128)(2,1)S(1)}, bf16[304,256]{1,0:T(8,128)(2,1)S(1)}, u32[]{:S(2)}, u32[]{:S(2)}) collective-permute-start(bf16[304,256]{1,0:T(8,128)(2,1)S(1)} %get-tuple-element.99.two), channel_id=1, source_target_pairs={{0,2},{1,3},{2,0},{3,1},{4,6},{5,7},{6,4},{7,5},{8,10},{9,11},{10,... | collective-permute-start | bytes 466952 | tf_op jit(solution)/shard_map/ppermute | solution.py:569
  63.4 5.3 %collective-permute-start.21 = (bf16[304,256]{1,0:T(8,128)(2,1)S(1)}, bf16[304,256]{1,0:T(8,128)(2,1)S(1)}, u32[]{:S(2)}, u32[]{:S(2)}) collective-permute-start(bf16[304,256]{1,0:T(8,128)(2,1)S(1)} %get-tuple-element.100.refs_0_), channel_id=1, source_target_pairs={{0,2},{1,3},{2,0},{3,1},{4,6},{5,7},{6,4},{7,5},{8,10},{9,11},{10,... | collective-permute-start | bytes 466952 | tf_op jit(solution)/shard_map/ppermute | solution.py:569
  72.8 6.5 %collective-permute-start.28 = (bf16[144,256]{1,0:T(8,128)(2,1)S(1)}, bf16[144,256]{1,0:T(8,128)(2,1)S(1)}, u32[]{:S(2)}, u32[]{:S(2)}) collective-permute-start(bf16[144,256]{1,0:T(8,128)(2,1)S(1)} %get-tuple-element.119), channel_id=1, source_target_pairs={{0,8},{4,12},{8,0},{12,4},{16,24},{20,28},{24,16},{28,20},{1,9},{5... | collective-permute-start | bytes 221192 | tf_op jit(solution)/shard_map/ppermute | solution.py:566
  73.4 12.8 %collective-permute-start.24 = (bf16[160,256]{1,0:T(8,128)(2,1)S(1)}, bf16[160,256]{1,0:T(8,128)(2,1)S(1)}, u32[]{:S(2)}, u32[]{:S(2)}) collective-permute-start(bf16[160,256]{1,0:T(8,128)(2,1)S(1)} %get-tuple-element.114), channel_id=1, source_target_pairs={{0,16},{4,20},{8,24},{12,28},{16,0},{20,4},{24,8},{28,12},{1,17},{... | collective-permute-start | bytes 245768 | tf_op jit(solution)/shard_map/ppermute | solution.py:566
  75.5 10.7 %collective-permute-start.25 = (bf16[160,256]{1,0:T(8,128)(2,1)S(1)}, bf16[160,256]{1,0:T(8,128)(2,1)S(1)}, u32[]{:S(2)}, u32[]{:S(2)}) collective-permute-start(bf16[160,256]{1,0:T(8,128)(2,1)S(1)} %get-tuple-element.115), channel_id=1, source_target_pairs={{0,24},{4,28},{8,16},{12,20},{16,8},{20,12},{24,0},{28,4},{1,25},{... | collective-permute-start | bytes 245768 | tf_op jit(solution)/shard_map/ppermute | solution.py:566
  77.3 9.0 %collective-permute-start.27 = (bf16[160,256]{1,0:T(8,128)(2,1)S(1)}, bf16[160,256]{1,0:T(8,128)(2,1)S(1)}, u32[]{:S(2)}, u32[]{:S(2)}) collective-permute-start(bf16[160,256]{1,0:T(8,128)(2,1)S(1)} %get-tuple-element.117), channel_id=1, source_target_pairs={{0,8},{4,12},{8,0},{12,4},{16,24},{20,28},{24,16},{28,20},{1,9},{5... | collective-permute-start | bytes 245768 | tf_op jit(solution)/shard_map/ppermute | solution.py:566
  77.3 9.0 %collective-permute-start.26 = (bf16[144,256]{1,0:T(8,128)(2,1)S(1)}, bf16[144,256]{1,0:T(8,128)(2,1)S(1)}, u32[]{:S(2)}, u32[]{:S(2)}) collective-permute-start(bf16[144,256]{1,0:T(8,128)(2,1)S(1)} %get-tuple-element.116), channel_id=1, source_target_pairs={{0,8},{4,12},{8,0},{12,4},{16,24},{20,28},{24,16},{28,20},{1,9},{5... | collective-permute-start | bytes 221192 | tf_op jit(solution)/shard_map/ppermute | solution.py:566
  79.3 7.8 %collective-permute-start.29 = (bf16[144,256]{1,0:T(8,128)(2,1)S(1)}, bf16[144,256]{1,0:T(8,128)(2,1)S(1)}, u32[]{:S(2)}, u32[]{:S(2)}) collective-permute-start(bf16[144,256]{1,0:T(8,128)(2,1)S(1)} %shard_map.120), channel_id=1, source_target_pairs={{0,16},{4,20},{8,24},{12,28},{16,0},{20,4},{24,8},{28,12},{1,17},{... | collective-permute-start | bytes 221192 | tf_op jit(solution)/shard_map/ppermute | solution.py:566
  87.5 6.8 %collective-permute-start.32 = (bf16[144,256]{1,0:T(8,128)(2,1)S(1)}, bf16[144,256]{1,0:T(8,128)(2,1)S(1)}, u32[]{:S(2)}, u32[]{:S(2)}) collective-permute-start(bf16[144,256]{1,0:T(8,128)(2,1)S(1)} %get-tuple-element.124), channel_id=1, source_target_pairs={{0,16},{4,20},{8,24},{12,28},{16,0},{20,4},{24,8},{28,12},{1,17},{... | collective-permute-start | bytes 221192 | tf_op jit(solution)/shard_map/ppermute | solution.py:566
  88.1 12.5 %collective-permute-start.30 = (bf16[240,256]{1,0:T(8,128)(2,1)S(1)}, bf16[240,256]{1,0:T(8,128)(2,1)S(1)}, u32[]{:S(2)}, u32[]{:S(2)}) collective-permute-start(bf16[240,256]{1,0:T(8,128)(2,1)S(1)} %get-tuple-element.122), channel_id=1, source_target_pairs={{0,8},{4,12},{8,0},{12,4},{16,24},{20,28},{24,16},{28,20},{1,9},{5... | collective-permute-start | bytes 368648 | tf_op jit(solution)/shard_map/ppermute | solution.py:566
  90.7 8.7 %collective-permute-start.35 = (bf16[160,256]{1,0:T(8,128)(2,1)S(1)}, bf16[160,256]{1,0:T(8,128)(2,1)S(1)}, u32[]{:S(2)}, u32[]{:S(2)}) collective-permute-start(bf16[160,256]{1,0:T(8,128)(2,1)S(1)} %get-tuple-element.125), channel_id=1, source_target_pairs={{0,24},{4,28},{8,16},{12,20},{16,8},{20,12},{24,0},{28,4},{1,25},{... | collective-permute-start | bytes 245768 | tf_op jit(solution)/shard_map/ppermute | solution.py:566
  91.9 8.7 %collective-permute-start.33 = (bf16[160,256]{1,0:T(8,128)(2,1)S(1)}, bf16[160,256]{1,0:T(8,128)(2,1)S(1)}, u32[]{:S(2)}, u32[]{:S(2)}) collective-permute-start(bf16[160,256]{1,0:T(8,128)(2,1)S(1)} %get-tuple-element.125), channel_id=1, source_target_pairs={{0,16},{4,20},{8,24},{12,28},{16,0},{20,4},{24,8},{28,12},{1,17},{... | collective-permute-start | bytes 245768 | tf_op jit(solution)/shard_map/ppermute | solution.py:566
  94.2 6.3 %collective-permute-start.34 = (bf16[144,256]{1,0:T(8,128)(2,1)S(1)}, bf16[144,256]{1,0:T(8,128)(2,1)S(1)}, u32[]{:S(2)}, u32[]{:S(2)}) collective-permute-start(bf16[144,256]{1,0:T(8,128)(2,1)S(1)} %collective-permute-done.32.refs_3_), channel_id=1, source_target_pairs={{0,8},{4,12},{8,0},{12,4},{16,24},{20,28},{24,16},{28,20},{1,9},{5... | collective-permute-start | bytes 221192 | tf_op jit(solution)/shard_map/ppermute | solution.py:566
  102.9 5.5 %collective-permute-start.37 = (bf16[304,128]{1,0:T(8,128)(2,1)S(1)}, bf16[304,128]{1,0:T(8,128)(2,1)S(1)}, u32[]{:S(2)}, u32[]{:S(2)}) collective-permute-start(bf16[304,128]{1,0:T(8,128)(2,1)S(1)} %get-tuple-element.127), channel_id=1, source_target_pairs={{0,3},{1,2},{2,1},{3,0},{4,7},{5,6},{6,5},{7,4},{8,11},{9,10},{10,... | collective-permute-start | bytes 233480 | tf_op jit(solution)/shard_map/ppermute | solution.py:569
  104.6 5.4 %collective-permute-start.38 = (bf16[304,128]{1,0:T(8,128)(2,1)S(1)}, bf16[304,128]{1,0:T(8,128)(2,1)S(1)}, u32[]{:S(2)}, u32[]{:S(2)}) collective-permute-start(bf16[304,128]{1,0:T(8,128)(2,1)S(1)} %get-tuple-element.128), channel_id=1, source_target_pairs={{0,2},{1,3},{2,0},{3,1},{4,6},{5,7},{6,4},{7,5},{8,10},{9,11},{10,... | collective-permute-start | bytes 233480 | tf_op jit(solution)/shard_map/ppermute | solution.py:569
  (14 other events, 73.3 us)
